TPU v7x, 32 devices: a whole 2x2x4 slice. The times are simulated.
32 devices in a mesh: row: 4 (over y, x), proto: 8 (over z, core).
Axes of the slice: x: 2, y: 2, z: 4, core: 2. Of those that a mesh axis runs over, the one named last changes fastest.
Arguments:
- embeddings: bfloat16 [8192, 1024], P('row'), may hold values from -24 to 24, as said below
- prototypes: bfloat16 [8192, 1024], P('proto', 'row'), may hold values from -6 to 6
- block_mask: int32 [64, 64], P('row', 'proto'), may hold values from 0 to 1, as said below
Outputs:
- targets: bfloat16 [8192, 1024], P('row', 'proto')
- row_potential: float32 [8192], P('row')
- column_potential: float32 [8192], P('proto')
Inputs may be any that keep to these rules, and one draw needn't show every extreme that they name: `block_mask`: every row tile and every prototype tile has at least one candidate tile. `embeddings`: some rows copy a scaled prototype.
All inputs are finite; a program needn't handle non-finite values.
Results may differ from a plain program's by a relative error of at most 0.02.
Values may be sent and summed in bfloat16 or wider, within the bound.
No kernel may reach another device: no remote copies, remote signals or barrier semaphores. Data moves between devices by JAX's collectives and lax.ppermute only.
A program may use at most 64 MiB of HBM per device.

v0:
```python
import math

import jax
import jax.numpy as jnp
from jax import lax
from jax.sharding import PartitionSpec as P

ITERS = 3


NEGATIVE = -1e30


def expand_mask(block_mask, tile):
    allowed = block_mask == 1
    return jnp.repeat(jnp.repeat(allowed, tile, axis=0), tile, axis=1)


def row_logsum(values, allowed):
    peak = lax.pmax(jnp.max(jnp.where(allowed, values, NEGATIVE), axis=1), "proto")
    total = lax.psum(
        jnp.sum(jnp.where(allowed, jnp.exp(values - peak[:, None]), 0.0), axis=1), "proto"
    )
    return peak + jnp.log(total)


def column_logsum(values, allowed):
    peak = lax.pmax(jnp.max(jnp.where(allowed, values, NEGATIVE), axis=0), "row")
    total = lax.psum(
        jnp.sum(jnp.where(allowed, jnp.exp(values - peak[None, :]), 0.0), axis=0), "row"
    )
    return peak + jnp.log(total)


def shards(embeddings, prototypes, block_mask):
    features = lax.all_gather(prototypes, "row", axis=1, tiled=True)
    scale = 4.0 / math.sqrt(features.shape[1])
    similar = (
        lax.dot_general(
            embeddings, features, (((1,), (1,)), ((), ())), preferred_element_type=jnp.float32
        )
        * scale
    )
    tile = similar.shape[0] // block_mask.shape[0]
    allowed = expand_mask(block_mask, tile)
    rows_all = similar.shape[0] * lax.axis_size("row")
    protos_all = similar.shape[1] * lax.axis_size("proto")
    log_column = math.log(rows_all / protos_all)
    column_potential = jnp.zeros((similar.shape[1],), jnp.float32)
    row_potential = jnp.zeros((similar.shape[0],), jnp.float32)
    for sweep in range(ITERS):
        row_potential = -row_logsum(similar + column_potential[None, :], allowed)
        column_potential = log_column - column_logsum(similar + row_potential[:, None], allowed)
    plan = jnp.where(
        allowed, jnp.exp(similar + row_potential[:, None] + column_potential[None, :]), 0.0
    ).astype(jnp.bfloat16)
    partial_value = jnp.dot(plan, features, preferred_element_type=jnp.float32)
    targets = lax.psum_scatter(
        partial_value.astype(jnp.bfloat16), "proto", scatter_dimension=1, tiled=True
    )
    return (targets, row_potential, column_potential)


def solution(mesh):
    return jax.shard_map(
        shards,
        mesh=mesh,
        in_specs=(P("row", None), P("proto", "row"), P("row", "proto")),
        out_specs=(P("row", "proto"), P("row"), P("proto")),
        check_vma=False,
    )
```

profile of v0, /device:TPU:0, one launch (start us, length us, event | category | flops | bytes accessed | tf_op | source)
XLA Modules:
  0.0 329.9 jit_solution(10141883297598272202)
XLA Ops:
  7.2 0.0 all-gather.2.cloned.1.call-start
  7.2 0.7 all-gather.2.cloned.1.call-update
  7.9 0.0 reduce-scatter.4.cloned.1.call-start
  7.9 0.7 broadcast_compare_fusion
  8.6 0.1 copy.7
  8.7 39.0 %all-gather.2.cloned.1.call-done = bf16[1024,1024]{1,0:T(8,128)(2,1)} async-done(((bf16[1024,256]{1,0:T(8,128)(2,1)}), bf16[1024,1024]{1,0:T(8,128)(2,1)}) %all-gather.2.cloned.1.call-update) | async-done | bytes 2097168 | tf_op jit(solution)/shard_map/all_gather | solution.py:36
  47.7 0.1 broadcast_in_dim.37
  47.8 6.4 %broadcast_in_dim.38 = pred[2048,8,128]{2,1,0:T(8,128)(4,1)S(1)} broadcast(pred[2048,8]{1,0:T(8,128)(4,1)S(1)} %bitcast.38), dimensions={0,1} | broadcast | bytes 2113536 | tf_op jit(solution)/shard_map/broadcast_in_dim | solution.py:16
  54.2 11.4 %select_reduce_fusion.11 = (f32[2048]{0:T(1024)S(1)}, f32[2048,1024]{1,0:T(8,128)}) fusion(pred[256,8,8,128]{3,2,1,0:T(8,128)(4,1)S(1)} %bitcast.24, bf16[2048,1024]{1,0:T(8,128)(2,1)} %param.3, bf16[1024,1024]{1,0:T(8,128)(2,1)} %all-gather.2.cloned.1.call-done), kind=kOutput, calls=%fused_computation.12 | convolution fusion | flops 4301256704 | bytes 16785408 | tf_op jit(solution)/shard_map/dot_general | solution.py:39
  65.6 16.6 %pmax.42 = f32[2048]{0:T(1024)S(1)} all-reduce(f32[2048]{0:T(1024)S(1)} %get-tuple-element.3), channel_id=1, replica_groups=mesh['row'=4,'proto'=8] {'proto'}, use_global_device_ids=true, to_apply=%region_1.2 | all-reduce | flops 2048 | bytes 16384 | tf_op jit(solution)/shard_map/pmax | solution.py:20
  82.2 4.7 %select_reduce_fusion.10 = f32[2048]{0:T(1024)S(1)} fusion(f32[2048,1024]{1,0:T(8,128)} %get-tuple-element.4, f32[2048]{0:T(1024)S(1)} %pmax.42, pred[256,8,8,128]{3,2,1,0:T(8,128)(4,1)S(1)} %bitcast.25), kind=kLoop, calls=%fused_computation.11 | loop fusion | flops 6289408 | bytes 10502144 | tf_op jit(solution)/shard_map/reduce_sum | solution.py:22
  86.8 13.9 %psum.42 = f32[2048]{0:T(1024)S(1)} all-reduce(f32[2048]{0:T(1024)S(1)} %select_reduce_fusion.10), channel_id=1, replica_groups=mesh['row'=4,'proto'=8] {'proto'}, use_global_device_ids=true, to_apply=%region_3.4 | all-reduce | flops 2048 | bytes 16384 | tf_op jit(solution)/shard_map/psum | solution.py:21
  100.8 4.3 %select_reduce_fusion.9 = f32[1024]{0:T(1024)S(1)} fusion(f32[2048,1024]{1,0:T(8,128)} %get-tuple-element.4, f32[2048]{0:T(1024)S(1)} %add_negate_fusion.2, pred[256,8,8,128]{3,2,1,0:T(8,128)(4,1)S(1)} %bitcast.26), kind=kLoop, calls=%fused_computation.10 | loop fusion | flops 6290432 | bytes 10498048 | tf_op jit(solution)/shard_map/reduce_max | solution.py:28
  105.1 8.9 %pmax.43 = f32[1024]{0:T(1024)S(1)} all-reduce(f32[1024]{0:T(1024)S(1)} %select_reduce_fusion.9), channel_id=1, replica_groups=mesh['row'=4,'proto'=8] {'row'}, use_global_device_ids=true, to_apply=%region_5.6 | all-reduce | flops 1024 | bytes 8192 | tf_op jit(solution)/shard_map/pmax | solution.py:28
  114.0 4.7 %select_reduce_fusion.8 = f32[1024]{0:T(1024)S(1)} fusion(f32[2048,1024]{1,0:T(8,128)} %get-tuple-element.4, f32[1024]{0:T(1024)S(1)} %pmax.43, f32[2048]{0:T(1024)S(1)} %add_negate_fusion.2, pred[256,8,8,128]{3,2,1,0:T(8,128)(4,1)S(1)} %bitcast.27), kind=kLoop, calls=%fused_computation.9 | loop fusion | flops 8387584 | bytes 10502144 | tf_op jit(solution)/shard_map/reduce_sum | solution.py:30
  118.7 8.9 %psum.43 = f32[1024]{0:T(1024)S(1)} all-reduce(f32[1024]{0:T(1024)S(1)} %select_reduce_fusion.8), channel_id=1, replica_groups=mesh['row'=4,'proto'=8] {'row'}, use_global_device_ids=true, to_apply=%region_7.8 | all-reduce | flops 1024 | bytes 8192 | tf_op jit(solution)/shard_map/psum | solution.py:29
  127.6 5.0 %select_reduce_fusion.7 = f32[2048]{0:T(1024)S(1)} fusion(f32[2048,1024]{1,0:T(8,128)} %get-tuple-element.4, f32[1024]{0:T(1024)S(1)} %add_subtract_fusion.2, pred[256,8,8,128]{3,2,1,0:T(8,128)(4,1)S(1)} %bitcast.28), kind=kLoop, calls=%fused_computation.8 | loop fusion | flops 6289408 | bytes 10498048 | tf_op jit(solution)/shard_map/reduce_max | solution.py:20
  132.6 14.1 %pmax.44 = f32[2048]{0:T(1024)S(1)} all-reduce(f32[2048]{0:T(1024)S(1)} %select_reduce_fusion.7), channel_id=1, replica_groups=mesh['row'=4,'proto'=8] {'proto'}, use_global_device_ids=true, to_apply=%region_9.10 | all-reduce | flops 2048 | bytes 16384 | tf_op jit(solution)/shard_map/pmax | solution.py:20
  146.7 4.8 %select_reduce_fusion.6 = f32[2048]{0:T(1024)S(1)} fusion(f32[2048,1024]{1,0:T(8,128)} %get-tuple-element.4, f32[2048]{0:T(1024)S(1)} %pmax.44, f32[1024]{0:T(1024)S(1)} %add_subtract_fusion.2, pred[256,8,8,128]{3,2,1,0:T(8,128)(4,1)S(1)} %bitcast.29), kind=kLoop, calls=%fused_computation.7 | loop fusion | flops 8386560 | bytes 10506240 | tf_op jit(solution)/shard_map/reduce_sum | solution.py:22
  151.5 13.9 %psum.44 = f32[2048]{0:T(1024)S(1)} all-reduce(f32[2048]{0:T(1024)S(1)} %select_reduce_fusion.6), channel_id=1, replica_groups=mesh['row'=4,'proto'=8] {'proto'}, use_global_device_ids=true, to_apply=%region_11.12 | all-reduce | flops 2048 | bytes 16384 | tf_op jit(solution)/shard_map/psum | solution.py:21
  165.4 4.3 %select_reduce_fusion.5 = f32[1024]{0:T(1024)S(1)} fusion(f32[2048,1024]{1,0:T(8,128)} %get-tuple-element.4, f32[2048]{0:T(1024)S(1)} %add_negate_fusion.1, pred[256,8,8,128]{3,2,1,0:T(8,128)(4,1)S(1)} %bitcast.30), kind=kLoop, calls=%fused_computation.6 | loop fusion | flops 6290432 | bytes 10498048 | tf_op jit(solution)/shard_map/reduce_max | solution.py:28
  169.7 8.9 %pmax.45 = f32[1024]{0:T(1024)S(1)} all-reduce(f32[1024]{0:T(1024)S(1)} %select_reduce_fusion.5), channel_id=1, replica_groups=mesh['row'=4,'proto'=8] {'row'}, use_global_device_ids=true, to_apply=%region_13.14 | all-reduce | flops 1024 | bytes 8192 | tf_op jit(solution)/shard_map/pmax | solution.py:28
  178.6 4.7 %select_reduce_fusion.4 = f32[1024]{0:T(1024)S(1)} fusion(f32[2048,1024]{1,0:T(8,128)} %get-tuple-element.4, f32[1024]{0:T(1024)S(1)} %pmax.45, f32[2048]{0:T(1024)S(1)} %add_negate_fusion.1, pred[256,8,8,128]{3,2,1,0:T(8,128)(4,1)S(1)} %bitcast.31), kind=kLoop, calls=%fused_computation.5 | loop fusion | flops 8387584 | bytes 10502144 | tf_op jit(solution)/shard_map/reduce_sum | solution.py:30
  183.3 8.1 %psum.45 = f32[1024]{0:T(1024)S(1)} all-reduce(f32[1024]{0:T(1024)S(1)} %select_reduce_fusion.4), channel_id=1, replica_groups=mesh['row'=4,'proto'=8] {'row'}, use_global_device_ids=true, to_apply=%region_15.16 | all-reduce | flops 1024 | bytes 8192 | tf_op jit(solution)/shard_map/psum | solution.py:29
  191.4 5.0 %select_reduce_fusion.3 = f32[2048]{0:T(1024)S(1)} fusion(f32[2048,1024]{1,0:T(8,128)} %get-tuple-element.4, f32[1024]{0:T(1024)S(1)} %add_subtract_fusion.1, pred[256,8,8,128]{3,2,1,0:T(8,128)(4,1)S(1)} %bitcast.32), kind=kLoop, calls=%fused_computation.4 | loop fusion | flops 6289408 | bytes 10498048 | tf_op jit(solution)/shard_map/reduce_max | solution.py:20
  196.3 13.9 %pmax.46 = f32[2048]{0:T(1024)S(1)} all-reduce(f32[2048]{0:T(1024)S(1)} %select_reduce_fusion.3), channel_id=1, replica_groups=mesh['row'=4,'proto'=8] {'proto'}, use_global_device_ids=true, to_apply=%region_17.18 | all-reduce | flops 2048 | bytes 16384 | tf_op jit(solution)/shard_map/pmax | solution.py:20
  210.3 4.8 %select_reduce_fusion.2 = f32[2048]{0:T(1024)S(1)} fusion(f32[2048,1024]{1,0:T(8,128)} %get-tuple-element.4, f32[2048]{0:T(1024)S(1)} %pmax.46, f32[1024]{0:T(1024)S(1)} %add_subtract_fusion.1, pred[256,8,8,128]{3,2,1,0:T(8,128)(4,1)S(1)} %bitcast.33), kind=kLoop, calls=%fused_computation.3 | loop fusion | flops 8386560 | bytes 10506240 | tf_op jit(solution)/shard_map/reduce_sum | solution.py:22
  215.1 13.9 %psum.46 = f32[2048]{0:T(1024)S(1)} all-reduce(f32[2048]{0:T(1024)S(1)} %select_reduce_fusion.2), channel_id=1, replica_groups=mesh['row'=4,'proto'=8] {'proto'}, use_global_device_ids=true, to_apply=%region_19.20 | all-reduce | flops 2048 | bytes 16384 | tf_op jit(solution)/shard_map/psum | solution.py:21
  229.0 0.0 copy-start
  229.0 4.3 %select_reduce_fusion.1 = f32[1024]{0:T(1024)S(1)} fusion(f32[2048,1024]{1,0:T(8,128)} %get-tuple-element.4, f32[2048]{0:T(1024)S(1)} %add_negate_fusion, pred[256,8,8,128]{3,2,1,0:T(8,128)(4,1)S(1)} %bitcast.34), kind=kLoop, calls=%fused_computation.2 | loop fusion | flops 6290432 | bytes 10498048 | tf_op jit(solution)/shard_map/reduce_max | solution.py:28
  233.3 8.9 %pmax.47 = f32[1024]{0:T(1024)S(1)} all-reduce(f32[1024]{0:T(1024)S(1)} %select_reduce_fusion.1), channel_id=1, replica_groups=mesh['row'=4,'proto'=8] {'row'}, use_global_device_ids=true, to_apply=%region_21.22 | all-reduce | flops 1024 | bytes 8192 | tf_op jit(solution)/shard_map/pmax | solution.py:28
  242.2 4.7 %select_reduce_fusion = f32[1024]{0:T(1024)S(1)} fusion(f32[2048,1024]{1,0:T(8,128)} %get-tuple-element.4, f32[1024]{0:T(1024)S(1)} %pmax.47, f32[2048]{0:T(1024)S(1)} %add_negate_fusion, pred[256,8,8,128]{3,2,1,0:T(8,128)(4,1)S(1)} %bitcast.35), kind=kLoop, calls=%fused_computation.1 | loop fusion | flops 8387584 | bytes 10502144 | tf_op jit(solution)/shard_map/reduce_sum | solution.py:30
  246.9 8.9 %psum.47 = f32[1024]{0:T(1024)S(1)} all-reduce(f32[1024]{0:T(1024)S(1)} %select_reduce_fusion), channel_id=1, replica_groups=mesh['row'=4,'proto'=8] {'row'}, use_global_device_ids=true, to_apply=%region_23.24 | all-reduce | flops 1024 | bytes 8192 | tf_op jit(solution)/shard_map/psum | solution.py:29
  255.8 0.0 copy-done
  255.8 0.0 copy-start.1
  255.8 11.3 %fusion.4 = bf16[2048,1024]{1,0:T(8,128)(2,1)} fusion(bf16[1024,1024]{1,0:T(8,128)(2,1)} %all-gather.2.cloned.1.call-done, f32[2048,1024]{1,0:T(8,128)} %get-tuple-element.4, f32[1024]{0:T(1024)S(1)} %add_subtract_fusion, f32[2048]{0:T(1024)S(1)} %add_negate_fusion, pred[256,8,8,128]{3,2,1,0:T(8,128)(4,1)S(1)} %bitcast.36), kind=kOutput, calls=%fused_computation.18 | convolution fusion | flops 4305453056 | bytes 16789504 | tf_op jit(solution)/shard_map/dot_general | solution.py:57
  267.1 0.0 copy-done.1
  267.1 6.5 %copy.8 = bf16[2048,1024]{0,1:T(8,128)(2,1)} copy(bf16[2048,1024]{1,0:T(8,128)(2,1)} %fusion.4) | data formatting | bytes 8388608
  273.6 0.0 reduce-scatter.4.cloned.1.call-update
  273.6 47.3 %reduce-scatter.4.cloned.1.call-done = bf16[128,2048]{1,0:T(8,128)(2,1)} async-done(((bf16[1024,2048]{1,0:T(8,128)(2,1)}), bf16[128,2048]{1,0:T(8,128)(2,1)}) %reduce-scatter.4.cloned.1.call-update) | async-done | bytes 524304
  321.0 2.0 copy.9
  (6 shorter events, 0.1 us)
Async XLA Ops:
  7.2 40.6 %all-gather.2.cloned.1.call-start = ((), (), s32[]{:S(2)}) async-start(), calls=%async_computation.1 | async-start | bytes 2621440 | tf_op jit(solution)/shard_map/all_gather | solution.py:36
  7.9 313.1 %reduce-scatter.4.cloned.1.call-start = ((), (), s32[]{:S(2)}) async-start(), calls=%async_computation.2 | async-start | bytes 4718592
  229.0 26.8 %copy-start = (f32[2048]{0:T(1024)}, f32[2048]{0:T(1024)S(1)}, u32[]{:S(2)}) copy-start(f32[2048]{0:T(1024)S(1)} %add_negate_fusion) | copy-start | bytes 24580
  255.8 11.3 %copy-start.1 = (f32[1024]{0:T(1024)}, f32[1024]{0:T(1024)S(1)}, u32[]{:S(2)}) copy-start(f32[1024]{0:T(1024)S(1)} %add_subtract_fusion) | copy-start | bytes 12292
Sparse Core Ops, SparseCore 0:
  9.8 37.8 all-gather.1
  273.8 47.1 reduce-scatter.3
where the time goes:
time: 330 us
  blocking collectives  139 us (42%)
  waiting for transfers between devices  87 us (26%)
  other arithmetic  51.8 us (16%)
  matrix products  22.7 us (7%)
  local copies, waits for them, and re-layouts  15.1 us (5%)
  between operations  14.2 us (4%)
    unnamed x3, waiting for transfers between devices  48 us
    pmax x3, blocking collectives, row_logsum(): lax.pmax(jnp.max(jnp.where(allowed, values, NEGATIVE), axis=1), 'proto')  44.6 us
    psum x3, blocking collectives, row_logsum(): lax.psum(jnp.sum(jnp.where(allowed, jnp.exp(values - peak[:, None]), 0.0)...  41.8 us
    all_gather x1, waiting for transfers between devices, shards(): features = lax.all_gather(prototypes, 'row', axis=1, tiled=True)  39 us
    pmax x3, blocking collectives, column_logsum(): lax.pmax(jnp.max(jnp.where(allowed, values, NEGATIVE), axis=0), 'row')  26.7 us
    psum x3, blocking collectives, column_logsum(): lax.psum(jnp.sum(jnp.where(allowed, jnp.exp(values - peak[None, :]), 0.0)...  25.8 us
    reduce_sum x3, other arithmetic, row_logsum(): jnp.sum(jnp.where(allowed, jnp.exp(values - peak[:, None]), 0.0), axis=1)  14.3 us
    reduce_sum x3, other arithmetic, column_logsum(): jnp.sum(jnp.where(allowed, jnp.exp(values - peak[None, :]), 0.0), axis=0)  14.1 us
  transfers between devices with their start and end apart: 2, of which 2 were waited for; matrix products, arithmetic and copies ran while one was open for 0% of the time, Pallas kernels for 0%

commit v1 on v0

v1 whole, which is shorter than its diff:
```python
import math

import jax
import jax.numpy as jnp
from jax import lax
from jax.sharding import PartitionSpec as P

ITERS = 3

NEGATIVE = -1e30


def expand_mask(block_mask, tile):
    allowed = block_mask == 1
    return jnp.repeat(jnp.repeat(allowed, tile, axis=0), tile, axis=1)


def swap(x, axis, offset):
    size = lax.axis_size(axis)
    return lax.ppermute(x, axis, [(i, i ^ offset) for i in range(size)])


def pair_sum(terms):
    while len(terms) > 1:
        terms = [terms[i] + terms[i + 1] for i in range(0, len(terms), 2)]
    return terms[0]


def exchange_lse(local, axis):
    every = [local] + [swap(local, axis, j) for j in range(1, lax.axis_size(axis))]
    peak = every[0]
    for part in every[1:]:
        peak = jnp.maximum(peak, part)
    return peak + jnp.log(pair_sum([jnp.exp(part - peak) for part in every]))


def local_lse(values, allowed, axis):
    values = jnp.where(allowed, values, NEGATIVE)
    peak = jnp.max(values, axis=axis, keepdims=True)
    total = jnp.sum(jnp.where(allowed, jnp.exp(values - peak), 0.0), axis=axis)
    return jnp.squeeze(peak, axis) + jnp.log(total)


def gather_features(shard):
    if lax.axis_size("row") != 4:
        return lax.all_gather(shard, "row", axis=1, tiled=True)
    half = shard.shape[0] // 2
    near = swap(shard, "row", 1)
    far = swap(shard, "row", 2)
    top = swap(far[:half], "row", 1)
    bottom = swap(near[half:], "row", 2)
    cross = jnp.concatenate([top, bottom], axis=0)
    me = lax.axis_index("row")
    width = shard.shape[1]
    out = jnp.zeros((shard.shape[0], 4 * width), shard.dtype)
    for offset, part in enumerate((shard, near, far, cross)):
        out = lax.dynamic_update_slice_in_dim(out, part, (me ^ offset) * width, 1)
    return out


def scatter_partials(partial_value):
    size = lax.axis_size("proto")
    line = size // 2
    me = lax.axis_index("proto")
    z, core = me // 2, me % 2
    rows, features = partial_value.shape
    width = features // size
    split = partial_value.reshape(rows, line, 2, width).transpose(2, 1, 0, 3)
    mine = lax.dynamic_index_in_dim(split, core, 0, keepdims=False)
    other = lax.dynamic_index_in_dim(split, 1 - core, 0, keepdims=False)
    got = lax.ppermute(other, "proto", [(i, i ^ 1) for i in range(size)])
    both = mine.astype(jnp.float32) + got.astype(jnp.float32)
    up = [(i, i + 2) for i in range(size - 2)]
    down = [(i + 2, i) for i in range(size - 2)]

    def chunk(index):
        return lax.dynamic_index_in_dim(both, jnp.clip(index, 0, line - 1), 0, keepdims=False)

    from_below = jnp.zeros((rows, width), jnp.float32)
    from_above = jnp.zeros((rows, width), jnp.float32)
    for step in range(1, line):
        send_up = chunk(line - step + z) + from_below
        send_down = chunk(z - (line - step)) + from_above
        from_below = lax.ppermute(send_up.astype(jnp.bfloat16), "proto", up).astype(jnp.float32)
        from_above = lax.ppermute(send_down.astype(jnp.bfloat16), "proto", down).astype(jnp.float32)
    return (chunk(z) + from_below + from_above).astype(jnp.bfloat16)


def shards(embeddings, prototypes, block_mask):
    features = gather_features(prototypes)
    scale = 4.0 / math.sqrt(features.shape[1])
    similar = (
        lax.dot_general(
            embeddings, features, (((1,), (1,)), ((), ())), preferred_element_type=jnp.float32
        )
        * scale
    )
    tile = similar.shape[0] // block_mask.shape[0]
    allowed = expand_mask(block_mask, tile)
    rows_all = similar.shape[0] * lax.axis_size("row")
    protos_all = similar.shape[1] * lax.axis_size("proto")
    log_column = math.log(rows_all / protos_all)
    column_potential = jnp.zeros((similar.shape[1],), jnp.float32)
    for sweep in range(ITERS):
        row_potential = -exchange_lse(
            local_lse(similar + column_potential[None, :], allowed, 1), "proto"
        )
        column_potential = log_column - exchange_lse(
            local_lse(similar + row_potential[:, None], allowed, 0), "row"
        )
    plan = jnp.where(
        allowed, jnp.exp(similar + row_potential[:, None] + column_potential[None, :]), 0.0
    ).astype(jnp.bfloat16)
    partial_value = jnp.dot(plan, features, preferred_element_type=jnp.float32)
    targets = scatter_partials(partial_value.astype(jnp.bfloat16))
    return (targets, row_potential, column_potential)


def solution(mesh):
    return jax.shard_map(
        shards,
        mesh=mesh,
        in_specs=(P("row", None), P("proto", "row"), P("row", "proto")),
        out_specs=(P("row", "proto"), P("row"), P("proto")),
        check_vma=False,
    )
```

time: 330 us -> 200 us (0.61)
  blocking collectives: 139 us -> 0 us
  starting transfers between devices: 0.08 us -> 56.6 us
  other arithmetic: 51.8 us -> 36.1 us
  between operations: 14.2 us -> 1.05 us
  matrix products: 22.7 us -> 11.5 us
  waiting for transfers between devices: 87 us -> 81.4 us
    ppermute x0 -> x41, waiting for transfers between devices: none -> 81.4 us  [the longest x34 36.7 us: swap(): return lax.ppermute(x, axis, [(i, i ^ offset) for i in range(size)])]
    pmax x6 -> x0, blocking collectives: 71.3 us -> none  [the longest x3 44.6 us: row_logsum(): lax.pmax(jnp.max(jnp.where(allowed, values, NEGATIVE), axis=1), 'proto')]
    psum x6 -> x0, blocking collectives: 67.6 us -> none  [the longest x3 41.8 us: row_logsum(): lax.psum(jnp.sum(jnp.where(allowed, jnp.exp(values - peak[:, None]), 0.0)...]
    ppermute x0 -> x41, starting transfers between devices: none -> 56.6 us  [the longest x34 42 us: swap(): return lax.ppermute(x, axis, [(i, i ^ offset) for i in range(size)])]
    unnamed x3 -> x0, waiting for transfers between devices: 48 us -> none
    all_gather x1 -> x0, waiting for transfers between devices: 39 us -> none  [shards(): features = lax.all_gather(prototypes, 'row', axis=1, tiled=True)]
    reduce_max x5, other arithmetic: 22.8 us -> 5.25 us  [local_lse(): peak = jnp.max(values, axis=axis, keepdims=True)]
    reduce_sum x6, other arithmetic: 28.3 us -> 15.2 us  [local_lse(): total = jnp.sum(jnp.where(allowed, jnp.exp(values - peak), 0.0), axis=axis)]
  transfers between devices with their start and end apart: 2 -> 41, of which waited for: 2 -> 22; matrix products, arithmetic and copies ran while one was open for 0% -> 4% of each run, Pallas kernels for 0% -> 0%
where the time goes in v1:
time: 200 us; the launch traced here: 199 us
  waiting for transfers between devices  81.4 us (41%)
  starting transfers between devices  56.6 us (28%)
  other arithmetic  36.1 us (18%)
  local copies, waits for them, and re-layouts  12.5 us (6%)
  matrix products  11.5 us (6%)
    ppermute x34, starting transfers between devices, swap(): return lax.ppermute(x, axis, [(i, i ^ offset) for i in range(size)])  42 us
    ppermute x34, waiting for transfers between devices, swap(): return lax.ppermute(x, axis, [(i, i ^ offset) for i in range(size)])  36.7 us
    ppermute x3, waiting for transfers between devices, scatter_partials(): lax.ppermute(send_down.astype(jnp.bfloat16), 'proto', down)  21.3 us
    ppermute x3, waiting for transfers between devices, scatter_partials(): lax.ppermute(send_up.astype(jnp.bfloat16), 'proto', up).astype(jnp.float32)  21.3 us
    reduce_sum x6, other arithmetic, local_lse(): total = jnp.sum(jnp.where(allowed, jnp.exp(values - peak), 0.0), axis=axis)  15.2 us
    ppermute x3, starting transfers between devices, scatter_partials(): lax.ppermute(send_up.astype(jnp.bfloat16), 'proto', up).astype(jnp.float32)  10.8 us
    unnamed x10, local copies, waits for them, and re-layouts  8.38 us
    dot_general x1, matrix products, shards(): lax.dot_general(embeddings, features, (((1,), (1,)), ((), ())), preferred...  6.41 us
  transfers between devices with their start and end apart: 41, of which 22 were waited for; matrix products, arithmetic and copies ran while one was open for 4% of the time, Pallas kernels for 0%

profile of v1, /device:TPU:0, one launch (start us, length us, event | category | flops | bytes accessed | tf_op | source)
XLA Modules:
  0.0 199.2 jit_solution(4451388353123845213)
XLA Ops:
  0.6 3.0 %collective-permute-start = (bf16[1024,256]{1,0:T(8,128)(2,1)}, bf16[1024,256]{1,0:T(8,128)(2,1)S(1)}, u32[]{:S(2)}, u32[]{:S(2)}) collective-permute-start(bf16[1024,256]{1,0:T(8,128)(2,1)} %param.4), channel_id=1, source_target_pairs={{0,8},{8,0},{16,24},{24,16},{1,9},{9,1},{17,25},{25,17},{2,10},{10... | collective-permute-start | bytes 1572872 | tf_op jit(solution)/shard_map/ppermute | solution.py:20
  3.6 1.5 collective-permute-start.1
  6.0 11.2 %collective-permute-done.1 = bf16[1024,256]{1,0:T(8,128)(2,1)S(1)} collective-permute-done((bf16[1024,256]{1,0:T(8,128)(2,1)}, bf16[1024,256]{1,0:T(8,128)(2,1)S(1)}, u32[]{:S(2)}, u32[]{:S(2)}) %collective-permute-start.1) | collective-permute-done | bytes 524320 | tf_op jit(solution)/shard_map/ppermute | solution.py:20
  18.4 1.7 collective-permute-start.3
  21.6 2.6 %collective-permute-done.2 = bf16[512,256]{1,0:T(8,128)(2,1)} collective-permute-done((bf16[512,256]{1,0:T(8,128)(2,1)S(1)}, bf16[512,256]{1,0:T(8,128)(2,1)}, u32[]{:S(2)}, u32[]{:S(2)}) %collective-permute-start.2) | collective-permute-done | bytes 262176 | tf_op jit(solution)/shard_map/ppermute | solution.py:20
  26.7 6.4 %fusion.7 = (f32[2048]{0:T(1024)S(1)}, f32[1024,2048]{1,0:T(8,128)S(1)}) fusion(pred[2048,8]{0,1:T(8,128)(4,1)S(1)} %broadcast_bitcast_fusion, bf16[1024,1024]{1,0:T(8,128)(2,1)S(1)} %maximum_dynamic-update-slice_fusion, bf16[2048,1024]{1,0:T(8,128)(2,1)} %param.3), kind=kOutput, calls=%fused_computation.25 | convolution fusion | flops 4301256704 | bytes 14704640 | tf_op jit(solution)/shard_map/dot_general | solution.py:93
  33.2 1.7 fusion
  35.4 3.1 %collective-permute-start.4 = (f32[2048]{0:T(1024)S(1)}, f32[2048]{0:T(1024)S(1)}, u32[]{:S(2)}, u32[]{:S(2)}) collective-permute-start(f32[2048]{0:T(1024)S(1)} %log_add_fusion.2), channel_id=1, source_target_pairs={{0,1},{1,0},{2,3},{3,2},{4,5},{5,4},{6,7},{7,6},{8,9},{9,8},{10,11... | collective-permute-start | bytes 24584 | tf_op jit(solution)/shard_map/ppermute | solution.py:20
  39.9 3.0 %collective-permute-start.8 = (f32[2048]{0:T(1024)S(1)}, f32[2048]{0:T(1024)S(1)}, u32[]{:S(2)}, u32[]{:S(2)}) collective-permute-start(f32[2048]{0:T(1024)S(1)} %log_add_fusion.2), channel_id=1, source_target_pairs={{0,5},{1,4},{2,7},{3,6},{4,1},{5,0},{6,3},{7,2},{8,13},{9,12},{10,... | collective-permute-start | bytes 24584 | tf_op jit(solution)/shard_map/ppermute | solution.py:20
  44.6 3.8 %collective-permute-done.9 = f32[2048]{0:T(1024)S(1)} collective-permute-done((f32[2048]{0:T(1024)S(1)}, f32[2048]{0:T(1024)S(1)}, u32[]{:S(2)}, u32[]{:S(2)}) %collective-permute-start.9) | collective-permute-done | bytes 8224 | tf_op jit(solution)/shard_map/ppermute | solution.py:20
  49.5 2.7 %fusion.1 = f32[1024]{0:T(1024)S(1)} fusion(f32[1024,2048]{1,0:T(8,128)S(1)} %get-tuple-element.10, f32[1024]{0:T(1024)S(1)} %fusion.8, f32[2048]{0:T(1024)S(1)} %add_negate_fusion.2, pred[2048,8]{0,1:T(8,128)(4,1)S(1)} %broadcast_bitcast_fusion), kind=kLoop, calls=%fused_computation.14 | loop fusion | flops 10484736 | bytes 8421376 | tf_op jit(solution)/shard_map/reduce_sum | solution.py:40
  52.2 1.6 collective-permute-start.11
  53.8 1.5 collective-permute-start.12
  57.4 2.4 %collective-permute-done.13 = f32[1024]{0:T(1024)S(1)} collective-permute-done((f32[1024]{0:T(1024)S(1)}, f32[1024]{0:T(1024)S(1)}, u32[]{:S(2)}, u32[]{:S(2)}) %collective-permute-start.13) | collective-permute-done | bytes 4128 | tf_op jit(solution)/shard_map/ppermute | solution.py:20
  60.8 2.5 %fusion.2 = f32[2048]{0:T(1024)S(1)} fusion(f32[1024,2048]{1,0:T(8,128)S(1)} %get-tuple-element.10, f32[2048]{0:T(1024)S(1)} %fusion.9, f32[1024]{0:T(1024)S(1)} %add_subtract_fusion.2, pred[2048,8]{0,1:T(8,128)(4,1)S(1)} %broadcast_bitcast_fusion), kind=kLoop, calls=%fused_computation.15 | loop fusion | flops 10483712 | bytes 8425472 | tf_op jit(solution)/shard_map/reduce_sum | solution.py:40
  63.5 1.8 collective-permute-start.16
  65.3 2.6 %collective-permute-start.18 = (f32[2048]{0:T(1024)S(1)}, f32[2048]{0:T(1024)S(1)}, u32[]{:S(2)}, u32[]{:S(2)}) collective-permute-start(f32[2048]{0:T(1024)S(1)} %log_add_fusion.1), channel_id=1, source_target_pairs={{0,5},{1,4},{2,7},{3,6},{4,1},{5,0},{6,3},{7,2},{8,13},{9,12},{10,... | collective-permute-start | bytes 24584 | tf_op jit(solution)/shard_map/ppermute | solution.py:20
  68.3 3.2 %collective-permute-start.20 = (f32[2048]{0:T(1024)S(1)}, f32[2048]{0:T(1024)S(1)}, u32[]{:S(2)}, u32[]{:S(2)}) collective-permute-start(f32[2048]{0:T(1024)S(1)} %log_add_fusion.1), channel_id=1, source_target_pairs={{0,7},{1,6},{2,5},{3,4},{4,3},{5,2},{6,1},{7,0},{8,15},{9,14},{10,... | collective-permute-start | bytes 24584 | tf_op jit(solution)/shard_map/ppermute | solution.py:20
  71.5 1.8 collective-permute-done.19
  74.5 2.9 %fusion.3 = f32[1024]{0:T(1024)S(1)} fusion(f32[1024,2048]{1,0:T(8,128)S(1)} %get-tuple-element.10, f32[1024]{0:T(1024)S(1)} %fusion.10, f32[2048]{0:T(1024)S(1)} %add_negate_fusion.1, pred[2048,8]{0,1:T(8,128)(4,1)S(1)} %broadcast_bitcast_fusion), kind=kLoop, calls=%fused_computation.16 | loop fusion | flops 10484736 | bytes 8421376 | tf_op jit(solution)/shard_map/reduce_sum | solution.py:40
  78.5 2.5 %collective-permute-start.23 = (f32[1024]{0:T(1024)S(1)}, f32[1024]{0:T(1024)S(1)}, u32[]{:S(2)}, u32[]{:S(2)}) collective-permute-start(f32[1024]{0:T(1024)S(1)} %log_add_fusion.4), channel_id=1, source_target_pairs={{0,24},{8,16},{16,8},{24,0},{1,25},{9,17},{17,9},{25,1},{2,26},{10... | collective-permute-start | bytes 12296 | tf_op jit(solution)/shard_map/ppermute | solution.py:20
  84.0 2.5 %fusion.4 = f32[2048]{0:T(1024)S(1)} fusion(f32[1024,2048]{1,0:T(8,128)S(1)} %get-tuple-element.10, f32[2048]{0:T(1024)S(1)} %fusion.11, f32[1024]{0:T(1024)S(1)} %add_subtract_fusion.1, pred[2048,8]{0,1:T(8,128)(4,1)S(1)} %broadcast_bitcast_fusion), kind=kLoop, calls=%fused_computation.17 | loop fusion | flops 10483712 | bytes 8425472 | tf_op jit(solution)/shard_map/reduce_sum | solution.py:40
  86.7 1.8 collective-permute-start.26
  88.5 2.1 %collective-permute-start.27 = (f32[2048]{0:T(1024)S(1)}, f32[2048]{0:T(1024)S(1)}, u32[]{:S(2)}, u32[]{:S(2)}) collective-permute-start(f32[2048]{0:T(1024)S(1)} %log_add_fusion), channel_id=1, source_target_pairs={{0,4},{1,5},{2,6},{3,7},{4,0},{5,1},{6,2},{7,3},{8,12},{9,13},{10,... | collective-permute-start | bytes 24584 | tf_op jit(solution)/shard_map/ppermute | solution.py:20
  91.1 3.2 %collective-permute-start.29 = (f32[2048]{0:T(1024)S(1)}, f32[2048]{0:T(1024)S(1)}, u32[]{:S(2)}, u32[]{:S(2)}) collective-permute-start(f32[2048]{0:T(1024)S(1)} %log_add_fusion), channel_id=1, source_target_pairs={{0,6},{1,7},{2,4},{3,5},{4,2},{5,3},{6,0},{7,1},{8,14},{9,15},{10,... | collective-permute-start | bytes 24584 | tf_op jit(solution)/shard_map/ppermute | solution.py:20
  94.7 1.8 collective-permute-done.29
  96.6 2.7 %collective-permute-done.30 = f32[2048]{0:T(1024)S(1)} collective-permute-done((f32[2048]{0:T(1024)S(1)}, f32[2048]{0:T(1024)S(1)}, u32[]{:S(2)}, u32[]{:S(2)}) %collective-permute-start.30) | collective-permute-done | bytes 8224 | tf_op jit(solution)/shard_map/ppermute | solution.py:20
  100.4 2.7 %fusion.5 = f32[1024]{0:T(1024)S(1)} fusion(f32[1024,2048]{1,0:T(8,128)S(1)} %get-tuple-element.10, f32[1024]{0:T(1024)S(1)} %fusion.12, f32[2048]{0:T(1024)S(1)} %add_negate_fusion, pred[2048,8]{0,1:T(8,128)(4,1)S(1)} %broadcast_bitcast_fusion), kind=kLoop, calls=%fused_computation.18 | loop fusion | flops 10484736 | bytes 8421376 | tf_op jit(solution)/shard_map/reduce_sum | solution.py:40
  103.2 1.6 collective-permute-start.31
  104.7 1.5 collective-permute-start.32
  106.9 1.5 collective-permute-done.32
  108.4 2.4 %collective-permute-done.33 = f32[1024]{0:T(1024)S(1)} collective-permute-done((f32[1024]{0:T(1024)S(1)}, f32[1024]{0:T(1024)S(1)}, u32[]{:S(2)}, u32[]{:S(2)}) %collective-permute-start.33) | collective-permute-done | bytes 4128 | tf_op jit(solution)/shard_map/ppermute | solution.py:20
  110.8 4.5 %fusion.6 = bf16[2048,1024]{0,1:T(8,128)(2,1)S(1)} fusion(f32[1024,2048]{1,0:T(8,128)} %copy-done, f32[1024]{0:T(1024)S(1)} %add_subtract_fusion, f32[2048]{0:T(1024)S(1)} %add_negate_fusion, pred[2048,8]{0,1:T(8,128)(4,1)S(1)} %broadcast_bitcast_fusion), kind=kLoop, calls=%fused_computation.19 | loop fusion | flops 8388608 | bytes 12611584 | tf_op jit(solution)/shard_map/convert_element_type | solution.py:113
  115.3 5.0 %convolution_convert_fusion = bf16[2048,1024]{0,1:T(8,128)(2,1)S(1)} fusion(bf16[2048,1024]{0,1:T(8,128)(2,1)S(1)} %fusion.6, bf16[1024,1024]{1,0:T(8,128)(2,1)S(1)} %maximum_dynamic-update-slice_fusion), kind=kOutput, calls=%fused_computation.33 | convolution fusion | flops 4297064448 | bytes 10485760 | tf_op jit(solution)/shard_map/dot_general | solution.py:114
  120.4 1.6 constant_dynamic-slice_fusion
  122.0 3.9 %copy.10 = bf16[2048,4,1,128]{3,0,1,2:T(8,128)(2,1)} copy(bf16[2048,4,1,128]{0,3,2,1:T(8,128)(2,1)} %get-tuple-element.7) | data formatting | bytes 4194304
  125.9 2.5 %copy.9 = bf16[2048,4,1,128]{3,0,1,2:T(8,128)(2,1)} copy(bf16[2048,4,1,128]{0,3,2,1:T(8,128)(2,1)S(1)} %get-tuple-element.8) | data formatting | bytes 4194304
  128.4 2.0 %collective-permute-done.34 = bf16[4,2048,128]{2,1,0:T(8,128)(2,1)} collective-permute-done((bf16[4,2048,128]{2,1,0:T(8,128)(2,1)}, bf16[4,2048,128]{2,1,0:T(8,128)(2,1)}, u32[]{:S(2)}, u32[]{:S(2)}) %collective-permute-start.34) | collective-permute-done | bytes 2097184 | tf_op jit(solution)/shard_map/ppermute | solution.py:71
  130.4 2.6 %bitcast_add_fusion.5 = f32[4,2048,128]{2,1,0:T(8,128)S(1)} fusion(bf16[2048,4,1,128]{3,0,1,2:T(8,128)(2,1)} %copy.9, bf16[4,2048,128]{2,1,0:T(8,128)(2,1)} %collective-permute-done.34), kind=kLoop, calls=%fused_computation.32 | loop fusion | flops 3145728 | bytes 8388608 | tf_op jit(solution)/shard_map/add | solution.py:72
  133.1 1.9 copy-done.1
  137.8 10.4 %collective-permute-done.35 = bf16[2048,128]{1,0:T(8,128)(2,1)S(1)} collective-permute-done((bf16[2048,128]{1,0:T(8,128)(2,1)S(1)}, bf16[2048,128]{1,0:T(8,128)(2,1)S(1)}, u32[]{:S(2)}, u32[]{:S(2)}) %collective-permute-start.35) | collective-permute-done | bytes 524320 | tf_op jit(solution)/shard_map/ppermute | solution.py:84
  149.5 4.4 %collective-permute-start.36 = (bf16[2048,128]{1,0:T(8,128)(2,1)S(1)}, bf16[2048,128]{1,0:T(8,128)(2,1)S(1)}, u32[]{:S(2)}, u32[]{:S(2)}) collective-permute-start(bf16[2048,128]{1,0:T(8,128)(2,1)S(1)} %fusion.15), channel_id=1, source_target_pairs={{0,2},{1,3},{2,4},{3,5},{4,6},{5,7},{8,10},{9,11},{10,12},{11,13},... | collective-permute-start | bytes 1572872 | tf_op jit(solution)/shard_map/ppermute | solution.py:84
  154.0 10.9 %collective-permute-done.36 = bf16[2048,128]{1,0:T(8,128)(2,1)S(1)} collective-permute-done((bf16[2048,128]{1,0:T(8,128)(2,1)S(1)}, bf16[2048,128]{1,0:T(8,128)(2,1)S(1)}, u32[]{:S(2)}, u32[]{:S(2)}) %collective-permute-start.36) | collective-permute-done | bytes 524320 | tf_op jit(solution)/shard_map/ppermute | solution.py:84
  164.9 1.7 fusion.16
  167.9 5.0 %collective-permute-start.37 = (bf16[2048,128]{1,0:T(8,128)(2,1)S(1)}, bf16[2048,128]{1,0:T(8,128)(2,1)S(1)}, u32[]{:S(2)}, u32[]{:S(2)}) collective-permute-start(bf16[2048,128]{1,0:T(8,128)(2,1)S(1)} %get-tuple-element.3), channel_id=1, source_target_pairs={{0,2},{1,3},{2,4},{3,5},{4,6},{5,7},{8,10},{9,11},{10,12},{11,13},... | collective-permute-start | bytes 1572872 | tf_op jit(solution)/shard_map/ppermute | solution.py:84
  173.0 8.8 %collective-permute-done.39 = bf16[2048,128]{1,0:T(8,128)(2,1)S(1)} collective-permute-done((bf16[2048,128]{1,0:T(8,128)(2,1)S(1)}, bf16[2048,128]{1,0:T(8,128)(2,1)S(1)}, u32[]{:S(2)}, u32[]{:S(2)}) %collective-permute-start.39) | collective-permute-done | bytes 524320 | tf_op jit(solution)/shard_map/ppermute | solution.py:85
  184.5 12.5 %collective-permute-done.40 = bf16[2048,128]{1,0:T(8,128)(2,1)S(1)} collective-permute-done((bf16[2048,128]{1,0:T(8,128)(2,1)S(1)}, bf16[2048,128]{1,0:T(8,128)(2,1)S(1)}, u32[]{:S(2)}, u32[]{:S(2)}) %collective-permute-start.40) | collective-permute-done | bytes 524320 | tf_op jit(solution)/shard_map/ppermute | solution.py:85
  197.0 2.2 %fusion.18 = bf16[2048,128]{1,0:T(8,128)(2,1)} fusion(bf16[2048,128]{1,0:T(8,128)(2,1)S(1)} %collective-permute-done.40, bf16[2048,128]{1,0:T(8,128)(2,1)S(1)} %collective-permute-done.37, f32[4,2048,128]{2,1,0:T(8,128)} %copy-done.1, s32[]{:T(128)S(6)} %min.22), kind=kLoop, calls=%fused_computation.44 | loop fusion | flops 1310720 | bytes 2621444 | tf_op jit(solution)/shard_map/convert_element_type | solution.py:86
  (87 shorter events, 30.4 us)
Async XLA Ops:
  0.6 17.1 %collective-permute-start = (bf16[1024,256]{1,0:T(8,128)(2,1)}, bf16[1024,256]{1,0:T(8,128)(2,1)S(1)}, u32[]{:S(2)}, u32[]{:S(2)}) collective-permute-start(bf16[1024,256]{1,0:T(8,128)(2,1)} %param.4), channel_id=1, source_target_pairs={{0,8},{8,0},{16,24},{24,16},{1,9},{9,1},{17,25},{25,17},{2,10},{10... | collective-permute-start | bytes 1572872 | tf_op jit(solution)/shard_map/ppermute | solution.py:20
  3.6 13.6 %collective-permute-start.1 = (bf16[1024,256]{1,0:T(8,128)(2,1)}, bf16[1024,256]{1,0:T(8,128)(2,1)S(1)}, u32[]{:S(2)}, u32[]{:S(2)}) collective-permute-start(bf16[1024,256]{1,0:T(8,128)(2,1)} %param.4), channel_id=1, source_target_pairs={{0,16},{8,24},{16,0},{24,8},{1,17},{9,25},{17,1},{25,9},{2,18},{10... | collective-permute-start | bytes 1572872 | tf_op jit(solution)/shard_map/ppermute | solution.py:20
  17.2 7.0 %collective-permute-start.2 = (bf16[512,256]{1,0:T(8,128)(2,1)S(1)}, bf16[512,256]{1,0:T(8,128)(2,1)}, u32[]{:S(2)}, u32[]{:S(2)}) collective-permute-start(bf16[512,256]{1,0:T(8,128)(2,1)S(1)} %slice.8), channel_id=1, source_target_pairs={{0,8},{8,0},{16,24},{24,16},{1,9},{9,1},{17,25},{25,17},{2,10},{10... | collective-permute-start | bytes 786440 | tf_op jit(solution)/shard_map/ppermute | solution.py:20
  18.4 7.2 %collective-permute-start.3 = (bf16[512,256]{1,0:T(8,128)(2,1)}, bf16[512,256]{1,0:T(8,128)(2,1)}, u32[]{:S(2)}, u32[]{:S(2)}) collective-permute-start(bf16[512,256]{1,0:T(8,128)(2,1)} %slice.9), channel_id=1, source_target_pairs={{0,16},{8,24},{16,0},{24,8},{1,17},{9,25},{17,1},{25,9},{2,18},{10... | collective-permute-start | bytes 786440 | tf_op jit(solution)/shard_map/ppermute | solution.py:20
  33.1 67.3 %copy-start = (f32[1024,2048]{1,0:T(8,128)}, f32[1024,2048]{1,0:T(8,128)S(1)}, u32[]{:S(2)}) copy-start(f32[1024,2048]{1,0:T(8,128)S(1)} %get-tuple-element.10) | copy-start | bytes 25165828
  34.9 5.0 %collective-permute-start.10 = (f32[2048]{0:T(1024)S(1)}, f32[2048]{0:T(1024)S(1)}, u32[]{:S(2)}, u32[]{:S(2)}) collective-permute-start(f32[2048]{0:T(1024)S(1)} %log_add_fusion.2), channel_id=1, source_target_pairs={{0,7},{1,6},{2,5},{3,4},{4,3},{5,2},{6,1},{7,0},{8,15},{9,14},{10,... | collective-permute-start | bytes 24584 | tf_op jit(solution)/shard_map/ppermute | solution.py:20
  35.4 7.5 %collective-permute-start.4 = (f32[2048]{0:T(1024)S(1)}, f32[2048]{0:T(1024)S(1)}, u32[]{:S(2)}, u32[]{:S(2)}) collective-permute-start(f32[2048]{0:T(1024)S(1)} %log_add_fusion.2), channel_id=1, source_target_pairs={{0,1},{1,0},{2,3},{3,2},{4,5},{5,4},{6,7},{7,6},{8,9},{9,8},{10,11... | collective-permute-start | bytes 24584 | tf_op jit(solution)/shard_map/ppermute | solution.py:20
  38.5 4.8 %collective-permute-start.5 = (f32[2048]{0:T(1024)S(1)}, f32[2048]{0:T(1024)S(1)}, u32[]{:S(2)}, u32[]{:S(2)}) collective-permute-start(f32[2048]{0:T(1024)S(1)} %log_add_fusion.2), channel_id=1, source_target_pairs={{0,2},{1,3},{2,0},{3,1},{4,6},{5,7},{6,4},{7,5},{8,10},{9,11},{10,... | collective-permute-start | bytes 24584 | tf_op jit(solution)/shard_map/ppermute | solution.py:20
  38.5 4.8 %collective-permute-start.6 = (f32[2048]{0:T(1024)S(1)}, f32[2048]{0:T(1024)S(1)}, u32[]{:S(2)}, u32[]{:S(2)}) collective-permute-start(f32[2048]{0:T(1024)S(1)} %log_add_fusion.2), channel_id=1, source_target_pairs={{0,3},{1,2},{2,1},{3,0},{4,7},{5,6},{6,5},{7,4},{8,11},{9,10},{10,... | collective-permute-start | bytes 24584 | tf_op jit(solution)/shard_map/ppermute | solution.py:20
  39.9 4.7 %collective-permute-start.7 = (f32[2048]{0:T(1024)S(1)}, f32[2048]{0:T(1024)S(1)}, u32[]{:S(2)}, u32[]{:S(2)}) collective-permute-start(f32[2048]{0:T(1024)S(1)} %log_add_fusion.2), channel_id=1, source_target_pairs={{0,4},{1,5},{2,6},{3,7},{4,0},{5,1},{6,2},{7,3},{8,12},{9,13},{10,... | collective-permute-start | bytes 24584 | tf_op jit(solution)/shard_map/ppermute | solution.py:20
  39.9 4.7 %collective-permute-start.8 = (f32[2048]{0:T(1024)S(1)}, f32[2048]{0:T(1024)S(1)}, u32[]{:S(2)}, u32[]{:S(2)}) collective-permute-start(f32[2048]{0:T(1024)S(1)} %log_add_fusion.2), channel_id=1, source_target_pairs={{0,5},{1,4},{2,7},{3,6},{4,1},{5,0},{6,3},{7,2},{8,13},{9,12},{10,... | collective-permute-start | bytes 24584 | tf_op jit(solution)/shard_map/ppermute | solution.py:20
  42.9 5.4 %collective-permute-start.9 = (f32[2048]{0:T(1024)S(1)}, f32[2048]{0:T(1024)S(1)}, u32[]{:S(2)}, u32[]{:S(2)}) collective-permute-start(f32[2048]{0:T(1024)S(1)} %log_add_fusion.2), channel_id=1, source_target_pairs={{0,6},{1,7},{2,4},{3,5},{4,2},{5,3},{6,0},{7,1},{8,14},{9,15},{10,... | collective-permute-start | bytes 24584 | tf_op jit(solution)/shard_map/ppermute | solution.py:20
  52.2 3.7 %collective-permute-start.11 = (f32[1024]{0:T(1024)S(1)}, f32[1024]{0:T(1024)S(1)}, u32[]{:S(2)}, u32[]{:S(2)}) collective-permute-start(f32[1024]{0:T(1024)S(1)} %log_add_fusion.5), channel_id=1, source_target_pairs={{0,8},{8,0},{16,24},{24,16},{1,9},{9,1},{17,25},{25,17},{2,10},{10... | collective-permute-start | bytes 12296 | tf_op jit(solution)/shard_map/ppermute | solution.py:20
  53.8 3.6 %collective-permute-start.12 = (f32[1024]{0:T(1024)S(1)}, f32[1024]{0:T(1024)S(1)}, u32[]{:S(2)}, u32[]{:S(2)}) collective-permute-start(f32[1024]{0:T(1024)S(1)} %log_add_fusion.5), channel_id=1, source_target_pairs={{0,16},{8,24},{16,0},{24,8},{1,17},{9,25},{17,1},{25,9},{2,18},{10... | collective-permute-start | bytes 12296 | tf_op jit(solution)/shard_map/ppermute | solution.py:20
  55.3 4.5 %collective-permute-start.13 = (f32[1024]{0:T(1024)S(1)}, f32[1024]{0:T(1024)S(1)}, u32[]{:S(2)}, u32[]{:S(2)}) collective-permute-start(f32[1024]{0:T(1024)S(1)} %log_add_fusion.5), channel_id=1, source_target_pairs={{0,24},{8,16},{16,8},{24,0},{1,25},{9,17},{17,9},{25,1},{2,26},{10... | collective-permute-start | bytes 12296 | tf_op jit(solution)/shard_map/ppermute | solution.py:20
  63.4 4.5 %collective-permute-start.14 = (f32[2048]{0:T(1024)S(1)}, f32[2048]{0:T(1024)S(1)}, u32[]{:S(2)}, u32[]{:S(2)}) collective-permute-start(f32[2048]{0:T(1024)S(1)} %log_add_fusion.1), channel_id=1, source_target_pairs={{0,1},{1,0},{2,3},{3,2},{4,5},{5,4},{6,7},{7,6},{8,9},{9,8},{10,11... | collective-permute-start | bytes 24584 | tf_op jit(solution)/shard_map/ppermute | solution.py:20
  63.4 4.8 %collective-permute-start.15 = (f32[2048]{0:T(1024)S(1)}, f32[2048]{0:T(1024)S(1)}, u32[]{:S(2)}, u32[]{:S(2)}) collective-permute-start(f32[2048]{0:T(1024)S(1)} %log_add_fusion.1), channel_id=1, source_target_pairs={{0,2},{1,3},{2,0},{3,1},{4,6},{5,7},{6,4},{7,5},{8,10},{9,11},{10,... | collective-permute-start | bytes 24584 | tf_op jit(solution)/shard_map/ppermute | solution.py:20
  63.5 8.0 %collective-permute-start.16 = (f32[2048]{0:T(1024)S(1)}, f32[2048]{0:T(1024)S(1)}, u32[]{:S(2)}, u32[]{:S(2)}) collective-permute-start(f32[2048]{0:T(1024)S(1)} %log_add_fusion.1), channel_id=1, source_target_pairs={{0,3},{1,2},{2,1},{3,0},{4,7},{5,6},{6,5},{7,4},{8,11},{9,10},{10,... | collective-permute-start | bytes 24584 | tf_op jit(solution)/shard_map/ppermute | solution.py:20
  65.3 6.2 %collective-permute-start.17 = (f32[2048]{0:T(1024)S(1)}, f32[2048]{0:T(1024)S(1)}, u32[]{:S(2)}, u32[]{:S(2)}) collective-permute-start(f32[2048]{0:T(1024)S(1)} %log_add_fusion.1), channel_id=1, source_target_pairs={{0,4},{1,5},{2,6},{3,7},{4,0},{5,1},{6,2},{7,3},{8,12},{9,13},{10,... | collective-permute-start | bytes 24584 | tf_op jit(solution)/shard_map/ppermute | solution.py:20
  65.3 6.2 %collective-permute-start.18 = (f32[2048]{0:T(1024)S(1)}, f32[2048]{0:T(1024)S(1)}, u32[]{:S(2)}, u32[]{:S(2)}) collective-permute-start(f32[2048]{0:T(1024)S(1)} %log_add_fusion.1), channel_id=1, source_target_pairs={{0,5},{1,4},{2,7},{3,6},{4,1},{5,0},{6,3},{7,2},{8,13},{9,12},{10,... | collective-permute-start | bytes 24584 | tf_op jit(solution)/shard_map/ppermute | solution.py:20
  67.9 5.4 %collective-permute-start.19 = (f32[2048]{0:T(1024)S(1)}, f32[2048]{0:T(1024)S(1)}, u32[]{:S(2)}, u32[]{:S(2)}) collective-permute-start(f32[2048]{0:T(1024)S(1)} %log_add_fusion.1), channel_id=1, source_target_pairs={{0,6},{1,7},{2,4},{3,5},{4,2},{5,3},{6,0},{7,1},{8,14},{9,15},{10,... | collective-permute-start | bytes 24584 | tf_op jit(solution)/shard_map/ppermute | solution.py:20
  68.3 5.1 %collective-permute-start.20 = (f32[2048]{0:T(1024)S(1)}, f32[2048]{0:T(1024)S(1)}, u32[]{:S(2)}, u32[]{:S(2)}) collective-permute-start(f32[2048]{0:T(1024)S(1)} %log_add_fusion.1), channel_id=1, source_target_pairs={{0,7},{1,6},{2,5},{3,4},{4,3},{5,2},{6,1},{7,0},{8,15},{9,14},{10,... | collective-permute-start | bytes 24584 | tf_op jit(solution)/shard_map/ppermute | solution.py:20
  77.4 3.7 %collective-permute-start.21 = (f32[1024]{0:T(1024)S(1)}, f32[1024]{0:T(1024)S(1)}, u32[]{:S(2)}, u32[]{:S(2)}) collective-permute-start(f32[1024]{0:T(1024)S(1)} %log_add_fusion.4), channel_id=1, source_target_pairs={{0,8},{8,0},{16,24},{24,16},{1,9},{9,1},{17,25},{25,17},{2,10},{10... | collective-permute-start | bytes 12296 | tf_op jit(solution)/shard_map/ppermute | solution.py:20
  78.0 3.6 %collective-permute-start.22 = (f32[1024]{0:T(1024)S(1)}, f32[1024]{0:T(1024)S(1)}, u32[]{:S(2)}, u32[]{:S(2)}) collective-permute-start(f32[1024]{0:T(1024)S(1)} %log_add_fusion.4), channel_id=1, source_target_pairs={{0,16},{8,24},{16,0},{24,8},{1,17},{9,25},{17,1},{25,9},{2,18},{10... | collective-permute-start | bytes 12296 | tf_op jit(solution)/shard_map/ppermute | solution.py:20
  78.5 4.5 %collective-permute-start.23 = (f32[1024]{0:T(1024)S(1)}, f32[1024]{0:T(1024)S(1)}, u32[]{:S(2)}, u32[]{:S(2)}) collective-permute-start(f32[1024]{0:T(1024)S(1)} %log_add_fusion.4), channel_id=1, source_target_pairs={{0,24},{8,16},{16,8},{24,0},{1,25},{9,17},{17,9},{25,1},{2,26},{10... | collective-permute-start | bytes 12296 | tf_op jit(solution)/shard_map/ppermute | solution.py:20
  86.6 4.5 %collective-permute-start.24 = (f32[2048]{0:T(1024)S(1)}, f32[2048]{0:T(1024)S(1)}, u32[]{:S(2)}, u32[]{:S(2)}) collective-permute-start(f32[2048]{0:T(1024)S(1)} %log_add_fusion), channel_id=1, source_target_pairs={{0,1},{1,0},{2,3},{3,2},{4,5},{5,4},{6,7},{7,6},{8,9},{9,8},{10,11... | collective-permute-start | bytes 24584 | tf_op jit(solution)/shard_map/ppermute | solution.py:20
  86.6 7.7 %collective-permute-start.25 = (f32[2048]{0:T(1024)S(1)}, f32[2048]{0:T(1024)S(1)}, u32[]{:S(2)}, u32[]{:S(2)}) collective-permute-start(f32[2048]{0:T(1024)S(1)} %log_add_fusion), channel_id=1, source_target_pairs={{0,2},{1,3},{2,0},{3,1},{4,6},{5,7},{6,4},{7,5},{8,10},{9,11},{10,... | collective-permute-start | bytes 24584 | tf_op jit(solution)/shard_map/ppermute | solution.py:20
  86.7 8.0 %collective-permute-start.26 = (f32[2048]{0:T(1024)S(1)}, f32[2048]{0:T(1024)S(1)}, u32[]{:S(2)}, u32[]{:S(2)}) collective-permute-start(f32[2048]{0:T(1024)S(1)} %log_add_fusion), channel_id=1, source_target_pairs={{0,3},{1,2},{2,1},{3,0},{4,7},{5,6},{6,5},{7,4},{8,11},{9,10},{10,... | collective-permute-start | bytes 24584 | tf_op jit(solution)/shard_map/ppermute | solution.py:20
  88.5 6.2 %collective-permute-start.27 = (f32[2048]{0:T(1024)S(1)}, f32[2048]{0:T(1024)S(1)}, u32[]{:S(2)}, u32[]{:S(2)}) collective-permute-start(f32[2048]{0:T(1024)S(1)} %log_add_fusion), channel_id=1, source_target_pairs={{0,4},{1,5},{2,6},{3,7},{4,0},{5,1},{6,2},{7,3},{8,12},{9,13},{10,... | collective-permute-start | bytes 24584 | tf_op jit(solution)/shard_map/ppermute | solution.py:20
  90.6 4.1 %collective-permute-start.28 = (f32[2048]{0:T(1024)S(1)}, f32[2048]{0:T(1024)S(1)}, u32[]{:S(2)}, u32[]{:S(2)}) collective-permute-start(f32[2048]{0:T(1024)S(1)} %log_add_fusion), channel_id=1, source_target_pairs={{0,5},{1,4},{2,7},{3,6},{4,1},{5,0},{6,3},{7,2},{8,13},{9,12},{10,... | collective-permute-start | bytes 24584 | tf_op jit(solution)/shard_map/ppermute | solution.py:20
  91.1 5.5 %collective-permute-start.29 = (f32[2048]{0:T(1024)S(1)}, f32[2048]{0:T(1024)S(1)}, u32[]{:S(2)}, u32[]{:S(2)}) collective-permute-start(f32[2048]{0:T(1024)S(1)} %log_add_fusion), channel_id=1, source_target_pairs={{0,6},{1,7},{2,4},{3,5},{4,2},{5,3},{6,0},{7,1},{8,14},{9,15},{10,... | collective-permute-start | bytes 24584 | tf_op jit(solution)/shard_map/ppermute | solution.py:20
  94.4 4.9 %collective-permute-start.30 = (f32[2048]{0:T(1024)S(1)}, f32[2048]{0:T(1024)S(1)}, u32[]{:S(2)}, u32[]{:S(2)}) collective-permute-start(f32[2048]{0:T(1024)S(1)} %log_add_fusion), channel_id=1, source_target_pairs={{0,7},{1,6},{2,5},{3,4},{4,3},{5,2},{6,1},{7,0},{8,15},{9,14},{10,... | collective-permute-start | bytes 24584 | tf_op jit(solution)/shard_map/ppermute | solution.py:20
  99.3 11.5 %copy-start.2 = (f32[2048]{0:T(1024)}, f32[2048]{0:T(1024)S(1)}, u32[]{:S(2)}) copy-start(f32[2048]{0:T(1024)S(1)} %add_negate_fusion) | copy-start | bytes 24580
  103.2 3.7 %collective-permute-start.31 = (f32[1024]{0:T(1024)S(1)}, f32[1024]{0:T(1024)S(1)}, u32[]{:S(2)}, u32[]{:S(2)}) collective-permute-start(f32[1024]{0:T(1024)S(1)} %log_add_fusion.3), channel_id=1, source_target_pairs={{0,8},{8,0},{16,24},{24,16},{1,9},{9,1},{17,25},{25,17},{2,10},{10... | collective-permute-start | bytes 12296 | tf_op jit(solution)/shard_map/ppermute | solution.py:20
  104.7 3.6 %collective-permute-start.32 = (f32[1024]{0:T(1024)S(1)}, f32[1024]{0:T(1024)S(1)}, u32[]{:S(2)}, u32[]{:S(2)}) collective-permute-start(f32[1024]{0:T(1024)S(1)} %log_add_fusion.3), channel_id=1, source_target_pairs={{0,16},{8,24},{16,0},{24,8},{1,17},{9,25},{17,1},{25,9},{2,18},{10... | collective-permute-start | bytes 12296 | tf_op jit(solution)/shard_map/ppermute | solution.py:20
  106.3 4.5 %collective-permute-start.33 = (f32[1024]{0:T(1024)S(1)}, f32[1024]{0:T(1024)S(1)}, u32[]{:S(2)}, u32[]{:S(2)}) collective-permute-start(f32[1024]{0:T(1024)S(1)} %log_add_fusion.3), channel_id=1, source_target_pairs={{0,24},{8,16},{16,8},{24,0},{1,25},{9,17},{17,9},{25,1},{2,26},{10... | collective-permute-start | bytes 12296 | tf_op jit(solution)/shard_map/ppermute | solution.py:20
  110.8 9.6 %copy-start.3 = (f32[1024]{0:T(1024)}, f32[1024]{0:T(1024)S(1)}, u32[]{:S(2)}) copy-start(f32[1024]{0:T(1024)S(1)} %add_subtract_fusion) | copy-start | bytes 12292
  125.9 4.5 %collective-permute-start.34 = (bf16[4,2048,128]{2,1,0:T(8,128)(2,1)}, bf16[4,2048,128]{2,1,0:T(8,128)(2,1)}, u32[]{:S(2)}, u32[]{:S(2)}) collective-permute-start(bf16[4,2048,128]{2,1,0:T(8,128)(2,1)} %bitcast.136), channel_id=1, source_target_pairs={{0,1},{1,0},{2,3},{3,2},{4,5},{5,4},{6,7},{7,6},{8,9},{9,8},{10,11... | collective-permute-start | bytes 6291464 | tf_op jit(solution)/shard_map/ppermute | solution.py:71
  133.1 1.9 copy-start.1
  135.2 13.0 %collective-permute-start.35 = (bf16[2048,128]{1,0:T(8,128)(2,1)S(1)}, bf16[2048,128]{1,0:T(8,128)(2,1)S(1)}, u32[]{:S(2)}, u32[]{:S(2)}) collective-permute-start(bf16[2048,128]{1,0:T(8,128)(2,1)S(1)} %get-tuple-element.5), channel_id=1, source_target_pairs={{0,2},{1,3},{2,4},{3,5},{4,6},{5,7},{8,10},{9,11},{10,12},{11,13},... | collective-permute-start | bytes 1572872 | tf_op jit(solution)/shard_map/ppermute | solution.py:84
  136.5 17.5 %collective-permute-start.38 = (bf16[2048,128]{1,0:T(8,128)(2,1)S(1)}, bf16[2048,128]{1,0:T(8,128)(2,1)S(1)}, u32[]{:S(2)}, u32[]{:S(2)}) collective-permute-start(bf16[2048,128]{1,0:T(8,128)(2,1)S(1)} %get-tuple-element.6), channel_id=1, source_target_pairs={{2,0},{3,1},{4,2},{5,3},{6,4},{7,5},{10,8},{11,9},{12,10},{13,11},... | collective-permute-start | bytes 1572872 | tf_op jit(solution)/shard_map/ppermute | solution.py:85
  149.5 15.3 %collective-permute-start.36 = (bf16[2048,128]{1,0:T(8,128)(2,1)S(1)}, bf16[2048,128]{1,0:T(8,128)(2,1)S(1)}, u32[]{:S(2)}, u32[]{:S(2)}) collective-permute-start(bf16[2048,128]{1,0:T(8,128)(2,1)S(1)} %fusion.15), channel_id=1, source_target_pairs={{0,2},{1,3},{2,4},{3,5},{4,6},{5,7},{8,10},{9,11},{10,12},{11,13},... | collective-permute-start | bytes 1572872 | tf_op jit(solution)/shard_map/ppermute | solution.py:84
  166.6 15.2 %collective-permute-start.39 = (bf16[2048,128]{1,0:T(8,128)(2,1)S(1)}, bf16[2048,128]{1,0:T(8,128)(2,1)S(1)}, u32[]{:S(2)}, u32[]{:S(2)}) collective-permute-start(bf16[2048,128]{1,0:T(8,128)(2,1)S(1)} %get-tuple-element.4), channel_id=1, source_target_pairs={{2,0},{3,1},{4,2},{5,3},{6,4},{7,5},{10,8},{11,9},{12,10},{13,11},... | collective-permute-start | bytes 1572872 | tf_op jit(solution)/shard_map/ppermute | solution.py:85
  167.9 16.5 %collective-permute-start.37 = (bf16[2048,128]{1,0:T(8,128)(2,1)S(1)}, bf16[2048,128]{1,0:T(8,128)(2,1)S(1)}, u32[]{:S(2)}, u32[]{:S(2)}) collective-permute-start(bf16[2048,128]{1,0:T(8,128)(2,1)S(1)} %get-tuple-element.3), channel_id=1, source_target_pairs={{0,2},{1,3},{2,4},{3,5},{4,6},{5,7},{8,10},{9,11},{10,12},{11,13},... | collective-permute-start | bytes 1572872 | tf_op jit(solution)/shard_map/ppermute | solution.py:84
  183.2 13.8 %collective-permute-start.40 = (bf16[2048,128]{1,0:T(8,128)(2,1)S(1)}, bf16[2048,128]{1,0:T(8,128)(2,1)S(1)}, u32[]{:S(2)}, u32[]{:S(2)}) collective-permute-start(bf16[2048,128]{1,0:T(8,128)(2,1)S(1)} %fusion.14), channel_id=1, source_target_pairs={{2,0},{3,1},{4,2},{5,3},{6,4},{7,5},{10,8},{11,9},{12,10},{13,11},... | collective-permute-start | bytes 1572872 | tf_op jit(solution)/shard_map/ppermute | solution.py:85

commit v2 on v1

--- a/solution.py
+++ b/solution.py
@@ -20,18 +20,15 @@
     return lax.ppermute(x, axis, [(i, i ^ offset) for i in range(size)])
 
 
-def pair_sum(terms):
-    while len(terms) > 1:
-        terms = [terms[i] + terms[i + 1] for i in range(0, len(terms), 2)]
-    return terms[0]
-
-
 def exchange_lse(local, axis):
-    every = [local] + [swap(local, axis, j) for j in range(1, lax.axis_size(axis))]
-    peak = every[0]
-    for part in every[1:]:
-        peak = jnp.maximum(peak, part)
-    return peak + jnp.log(pair_sum([jnp.exp(part - peak) for part in every]))
+    size = lax.axis_size(axis)
+    if axis == "proto":
+        every = lax.all_gather(local, axis)
+    else:
+        copies = jnp.broadcast_to(local[None, :], (size, local.shape[0]))
+        every = lax.all_to_all(copies, axis, 0, 0)
+    peak = jnp.max(every, axis=0)
+    return peak + jnp.log(jnp.sum(jnp.exp(every - peak[None, :]), axis=0))
 
 
 def local_lse(values, allowed, axis):

time: 200 us -> 240 us (1.20)
  blocking collectives: 0 us -> 57.5 us
  starting transfers between devices: 56.6 us -> 27 us
  other arithmetic: 36.1 us -> 61.5 us
  waiting for transfers between devices: 81.4 us -> 63 us
  local copies, waits for them, and re-layouts: 12.5 us -> 17.5 us
    all_gather x0 -> x3, blocking collectives: none -> 42.2 us  [exchange_lse(): every = lax.all_gather(local, axis)]
    ppermute x34 -> x4, starting transfers between devices: 42 us -> 6.64 us  [swap(): return lax.ppermute(x, axis, [(i, i ^ offset) for i in range(size)])]
    ppermute x34 -> x4, waiting for transfers between devices: 36.7 us -> 15.2 us  [swap(): return lax.ppermute(x, axis, [(i, i ^ offset) for i in range(size)])]
    reduce_max x5, other arithmetic: 5.25 us -> 22.1 us  [local_lse(): peak = jnp.max(values, axis=axis, keepdims=True)]
    all_to_all x0 -> x2, blocking collectives: none -> 15.3 us  [exchange_lse(): every = lax.all_to_all(copies, axis, 0, 0)]
    reduce_sum x6, other arithmetic: 15.2 us -> 23.5 us  [local_lse(): total = jnp.sum(jnp.where(allowed, jnp.exp(values - peak), 0.0), axis=axis)]
    all_to_all x0 -> x1, waiting for transfers between devices: none -> 4.44 us  [exchange_lse(): every = lax.all_to_all(copies, axis, 0, 0)]
    unnamed x10 -> x12, local copies, waits for them, and re-layouts: 8.38 us -> 12.7 us
  transfers between devices with their start and end apart: 41 -> 12, of which waited for: 22 -> 9; matrix products, arithmetic and copies ran while one was open for 4% -> 3% of each run, Pallas kernels for 0% -> 0%
where the time goes in v2:
time: 240 us; the launch traced here: 239 us
  waiting for transfers between devices  63 us (26%)
  other arithmetic  61.5 us (26%)
  blocking collectives  57.5 us (24%)
  starting transfers between devices  27 us (11%)
  local copies, waits for them, and re-layouts  17.5 us (7%)
  matrix products  11.5 us (5%)
    all_gather x3, blocking collectives, exchange_lse(): every = lax.all_gather(local, axis)  42.2 us
    reduce_sum x6, other arithmetic, local_lse(): total = jnp.sum(jnp.where(allowed, jnp.exp(values - peak), 0.0), axis=axis)  23.5 us
    reduce_max x5, other arithmetic, local_lse(): peak = jnp.max(values, axis=axis, keepdims=True)  22.1 us
    ppermute x3, waiting for transfers between devices, scatter_partials(): lax.ppermute(send_up.astype(jnp.bfloat16), 'proto', up).astype(jnp.float32)  20.7 us
    ppermute x3, waiting for transfers between devices, scatter_partials(): lax.ppermute(send_down.astype(jnp.bfloat16), 'proto', down)  20.6 us
    all_to_all x2, blocking collectives, exchange_lse(): every = lax.all_to_all(copies, axis, 0, 0)  15.3 us
    ppermute x4, waiting for transfers between devices, swap(): return lax.ppermute(x, axis, [(i, i ^ offset) for i in range(size)])  15.2 us
    ppermute x3, starting transfers between devices, scatter_partials(): lax.ppermute(send_up.astype(jnp.bfloat16), 'proto', up).astype(jnp.float32)  13 us
  transfers between devices with their start and end apart: 12, of which 9 were waited for; matrix products, arithmetic and copies ran while one was open for 3% of the time, Pallas kernels for 0%

profile of v2, /device:TPU:0, one launch (start us, length us, event | category | flops | bytes accessed | tf_op | source)
XLA Modules:
  0.0 239.1 jit_solution(7112905054045846909)
XLA Ops:
  0.6 3.0 %collective-permute-start = (bf16[1024,256]{1,0:T(8,128)(2,1)}, bf16[1024,256]{1,0:T(8,128)(2,1)S(1)}, u32[]{:S(2)}, u32[]{:S(2)}) collective-permute-start(bf16[1024,256]{1,0:T(8,128)(2,1)} %param.4), channel_id=1, source_target_pairs={{0,8},{8,0},{16,24},{24,16},{1,9},{9,1},{17,25},{25,17},{2,10},{10... | collective-permute-start | bytes 1572872 | tf_op jit(solution)/shard_map/ppermute | solution.py:20
  3.6 1.5 collective-permute-start.1
  6.0 11.2 %collective-permute-done.1 = bf16[1024,256]{1,0:T(8,128)(2,1)S(1)} collective-permute-done((bf16[1024,256]{1,0:T(8,128)(2,1)}, bf16[1024,256]{1,0:T(8,128)(2,1)S(1)}, u32[]{:S(2)}, u32[]{:S(2)}) %collective-permute-start.1) | collective-permute-done | bytes 524320 | tf_op jit(solution)/shard_map/ppermute | solution.py:20
  18.4 1.7 collective-permute-start.3
  21.6 2.6 %collective-permute-done.2 = bf16[512,256]{1,0:T(8,128)(2,1)} collective-permute-done((bf16[512,256]{1,0:T(8,128)(2,1)S(1)}, bf16[512,256]{1,0:T(8,128)(2,1)}, u32[]{:S(2)}, u32[]{:S(2)}) %collective-permute-start.2) | collective-permute-done | bytes 262176 | tf_op jit(solution)/shard_map/ppermute | solution.py:20
  24.3 1.4 collective-permute-done.3
  26.7 6.4 %fusion.7 = (f32[2048]{0:T(1024)S(1)}, f32[1024,2048]{1,0:T(8,128)S(1)}) fusion(pred[2048,8]{0,1:T(8,128)(4,1)S(1)} %broadcast_bitcast_fusion, bf16[1024,1024]{1,0:T(8,128)(2,1)S(1)} %maximum_dynamic-update-slice_fusion, bf16[2048,1024]{1,0:T(8,128)(2,1)} %param.3), kind=kOutput, calls=%fused_computation.25 | convolution fusion | flops 4301256704 | bytes 14704640 | tf_op jit(solution)/shard_map/dot_general | solution.py:90
  33.2 3.2 %copy-done = f32[1024,2048]{1,0:T(8,128)} copy-done((f32[1024,2048]{1,0:T(8,128)}, f32[1024,2048]{1,0:T(8,128)S(1)}, u32[]{:S(2)}) %copy-start) | copy-done | bytes 8388632
  36.4 1.7 fusion
  38.1 14.0 %all-gather = f32[16384]{0:T(1024)S(1)} all-gather(f32[2048]{0:T(1024)S(1)} %log_add_fusion.2), channel_id=2, replica_groups=mesh['row'=4,'proto'=8] {'proto'}, dimensions={0}, use_global_device_ids=true | all-gather | bytes 73728 | tf_op jit(solution)/shard_map/all_gather | solution.py:26
  52.2 4.6 %fusion.8 = f32[1024]{0:T(1024)S(1)} fusion(f32[1024,2048]{1,0:T(8,128)} %copy-done, f32[2048]{0:T(1024)S(1)} %add_negate_fusion.2, pred[2048,8]{0,1:T(8,128)(4,1)S(1)} %broadcast_bitcast_fusion), kind=kLoop, calls=%fused_computation.26 | loop fusion | flops 6290432 | bytes 8417280 | tf_op jit(solution)/shard_map/reduce_max | solution.py:36
  57.9 2.7 %fusion.1 = f32[1024]{0:T(1024)S(1)} fusion(f32[1024,2048]{1,0:T(8,128)S(1)} %copy-done.1, f32[1024]{0:T(1024)S(1)} %fusion.8, f32[2048]{0:T(1024)S(1)} %add_negate_fusion.2, pred[2048,8]{0,1:T(8,128)(4,1)S(1)} %broadcast_bitcast_fusion), kind=kLoop, calls=%fused_computation.14 | loop fusion | flops 10484736 | bytes 8421376 | tf_op jit(solution)/shard_map/reduce_sum | solution.py:37
  60.7 8.2 %all_to_all.27 = f32[4,1,1024]{2,1,0:T(1,128)S(1)} all-to-all(f32[4,1,1024]{2,1,0:T(1,128)S(1)} %broadcast_in_dim.35), channel_id=1, replica_groups=mesh['row'=4,'proto'=8] {'row'}, dimensions={0} | all-to-all | bytes 32768 | tf_op jit(solution)/shard_map/all_to_all | solution.py:29
  69.0 4.3 %fusion.9 = f32[2048]{0:T(1024)S(1)} fusion(f32[1024,2048]{1,0:T(8,128)} %copy-done, f32[1024]{0:T(1024)S(1)} %add_subtract_fusion.2, pred[2048,8]{0,1:T(8,128)(4,1)S(1)} %broadcast_bitcast_fusion), kind=kLoop, calls=%fused_computation.27 | loop fusion | flops 6289408 | bytes 8417280 | tf_op jit(solution)/shard_map/reduce_max | solution.py:36
  73.3 4.7 %fusion.2 = f32[2048]{0:T(1024)S(1)} fusion(f32[1024,2048]{1,0:T(8,128)} %copy-done, f32[2048]{0:T(1024)S(1)} %fusion.9, f32[1024]{0:T(1024)S(1)} %add_subtract_fusion.2, pred[2048,8]{0,1:T(8,128)(4,1)S(1)} %broadcast_bitcast_fusion), kind=kLoop, calls=%fused_computation.15 | loop fusion | flops 10483712 | bytes 8425472 | tf_op jit(solution)/shard_map/reduce_sum | solution.py:37
  78.0 14.2 %all-gather.1 = f32[16384]{0:T(1024)S(1)} all-gather(f32[2048]{0:T(1024)S(1)} %log_add_fusion.1), channel_id=3, replica_groups=mesh['row'=4,'proto'=8] {'proto'}, dimensions={0}, use_global_device_ids=true | all-gather | bytes 73728 | tf_op jit(solution)/shard_map/all_gather | solution.py:26
  92.3 4.5 %fusion.10 = f32[1024]{0:T(1024)S(1)} fusion(f32[1024,2048]{1,0:T(8,128)} %copy-done, f32[2048]{0:T(1024)S(1)} %add_negate_fusion.1, pred[2048,8]{0,1:T(8,128)(4,1)S(1)} %broadcast_bitcast_fusion), kind=kLoop, calls=%fused_computation.28 | loop fusion | flops 6290432 | bytes 8417280 | tf_op jit(solution)/shard_map/reduce_max | solution.py:36
  96.7 4.9 %fusion.3 = f32[1024]{0:T(1024)S(1)} fusion(f32[1024,2048]{1,0:T(8,128)} %copy-done, f32[1024]{0:T(1024)S(1)} %fusion.10, f32[2048]{0:T(1024)S(1)} %add_negate_fusion.1, pred[2048,8]{0,1:T(8,128)(4,1)S(1)} %broadcast_bitcast_fusion), kind=kLoop, calls=%fused_computation.16 | loop fusion | flops 10484736 | bytes 8421376 | tf_op jit(solution)/shard_map/reduce_sum | solution.py:37
  101.6 7.1 %all_to_all.28 = f32[4,1,1024]{2,1,0:T(1,128)S(1)} all-to-all(f32[4,1,1024]{2,1,0:T(1,128)S(1)} %broadcast_in_dim.70), channel_id=1, replica_groups=mesh['row'=4,'proto'=8] {'row'}, dimensions={0} | all-to-all | bytes 32768 | tf_op jit(solution)/shard_map/all_to_all | solution.py:29
  108.8 4.3 %fusion.11 = f32[2048]{0:T(1024)S(1)} fusion(f32[1024,2048]{1,0:T(8,128)} %copy-done, f32[1024]{0:T(1024)S(1)} %add_subtract_fusion.1, pred[2048,8]{0,1:T(8,128)(4,1)S(1)} %broadcast_bitcast_fusion), kind=kLoop, calls=%fused_computation.29 | loop fusion | flops 6289408 | bytes 8417280 | tf_op jit(solution)/shard_map/reduce_max | solution.py:36
  113.1 4.7 %fusion.4 = f32[2048]{0:T(1024)S(1)} fusion(f32[1024,2048]{1,0:T(8,128)} %copy-done, f32[2048]{0:T(1024)S(1)} %fusion.11, f32[1024]{0:T(1024)S(1)} %add_subtract_fusion.1, pred[2048,8]{0,1:T(8,128)(4,1)S(1)} %broadcast_bitcast_fusion), kind=kLoop, calls=%fused_computation.17 | loop fusion | flops 10483712 | bytes 8425472 | tf_op jit(solution)/shard_map/reduce_sum | solution.py:37
  117.8 14.0 %all-gather.2 = f32[16384]{0:T(1024)S(1)} all-gather(f32[2048]{0:T(1024)S(1)} %log_add_fusion), channel_id=4, replica_groups=mesh['row'=4,'proto'=8] {'proto'}, dimensions={0}, use_global_device_ids=true | all-gather | bytes 73728 | tf_op jit(solution)/shard_map/all_gather | solution.py:26
  131.9 4.5 %fusion.12 = f32[1024]{0:T(1024)S(1)} fusion(f32[1024,2048]{1,0:T(8,128)} %copy-done, f32[2048]{0:T(1024)S(1)} %add_negate_fusion, pred[2048,8]{0,1:T(8,128)(4,1)S(1)} %broadcast_bitcast_fusion), kind=kLoop, calls=%fused_computation.30 | loop fusion | flops 6290432 | bytes 8417280 | tf_op jit(solution)/shard_map/reduce_max | solution.py:36
  136.4 4.9 %fusion.5 = f32[1024]{0:T(1024)S(1)} fusion(f32[1024,2048]{1,0:T(8,128)} %copy-done, f32[1024]{0:T(1024)S(1)} %fusion.12, f32[2048]{0:T(1024)S(1)} %add_negate_fusion, pred[2048,8]{0,1:T(8,128)(4,1)S(1)} %broadcast_bitcast_fusion), kind=kLoop, calls=%fused_computation.18 | loop fusion | flops 10484736 | bytes 8421376 | tf_op jit(solution)/shard_map/reduce_sum | solution.py:37
  141.8 3.5 %all-to-all-start.2 = ((f32[4,1,1024]{2,1,0:T(1,128)}), f32[4,1,1024]{2,1,0:T(1,128)S(1)}, u32[]{:S(2)}, u32[]{:S(2)}) async-start(f32[4,1,1024]{2,1,0:T(1,128)} %broadcast_in_dim.71), calls=%async_computation.2 | async-start | bytes 32768 | tf_op jit(solution)/shard_map/all_to_all | solution.py:29
  145.4 4.4 %all-to-all-done.2 = f32[4,1,1024]{2,1,0:T(1,128)S(1)} async-done(((f32[4,1,1024]{2,1,0:T(1,128)}), f32[4,1,1024]{2,1,0:T(1,128)S(1)}, u32[]{:S(2)}, u32[]{:S(2)}) %all-to-all-start.2) | async-done | bytes 16416 | tf_op jit(solution)/shard_map/all_to_all | solution.py:29
  149.9 4.5 %fusion.6 = bf16[2048,1024]{0,1:T(8,128)(2,1)S(1)} fusion(f32[1024,2048]{1,0:T(8,128)} %copy-done, f32[1024]{0:T(1024)S(1)} %add_subtract_fusion, f32[2048]{0:T(1024)S(1)} %add_negate_fusion, pred[2048,8]{0,1:T(8,128)(4,1)S(1)} %broadcast_bitcast_fusion), kind=kLoop, calls=%fused_computation.19 | loop fusion | flops 8388608 | bytes 12611584 | tf_op jit(solution)/shard_map/convert_element_type | solution.py:110
  154.4 5.0 %convolution_convert_fusion = bf16[2048,1024]{0,1:T(8,128)(2,1)S(1)} fusion(bf16[2048,1024]{0,1:T(8,128)(2,1)S(1)} %fusion.6, bf16[1024,1024]{1,0:T(8,128)(2,1)S(1)} %maximum_dynamic-update-slice_fusion), kind=kOutput, calls=%fused_computation.33 | convolution fusion | flops 4297064448 | bytes 10485760 | tf_op jit(solution)/shard_map/dot_general | solution.py:111
  159.4 1.6 constant_dynamic-slice_fusion
  161.1 4.0 %copy.28 = bf16[2048,4,1,128]{3,0,1,2:T(8,128)(2,1)} copy(bf16[2048,4,1,128]{0,3,2,1:T(8,128)(2,1)} %get-tuple-element.7) | data formatting | bytes 4194304
  165.0 2.5 %copy.27 = bf16[2048,4,1,128]{3,0,1,2:T(8,128)(2,1)} copy(bf16[2048,4,1,128]{0,3,2,1:T(8,128)(2,1)S(1)} %get-tuple-element.8) | data formatting | bytes 4194304
  167.5 2.0 collective-permute-done.4
  169.5 2.6 %bitcast_add_fusion.5 = f32[4,2048,128]{2,1,0:T(8,128)S(1)} fusion(bf16[2048,4,1,128]{3,0,1,2:T(8,128)(2,1)} %copy.27, bf16[4,2048,128]{2,1,0:T(8,128)(2,1)} %collective-permute-done.4), kind=kLoop, calls=%fused_computation.32 | loop fusion | flops 3145728 | bytes 8388608 | tf_op jit(solution)/shard_map/add | solution.py:69
  172.2 1.9 copy-done.2
  174.2 3.5 %collective-permute-start.5 = (bf16[2048,128]{1,0:T(8,128)(2,1)S(1)}, bf16[2048,128]{1,0:T(8,128)(2,1)S(1)}, u32[]{:S(2)}, u32[]{:S(2)}) collective-permute-start(bf16[2048,128]{1,0:T(8,128)(2,1)S(1)} %get-tuple-element.5), channel_id=1, source_target_pairs={{0,2},{1,3},{2,4},{3,5},{4,6},{5,7},{8,10},{9,11},{10,12},{11,13},... | collective-permute-start | bytes 1572872 | tf_op jit(solution)/shard_map/ppermute | solution.py:81
  177.7 1.3 collective-permute-start.8
  179.0 10.1 %collective-permute-done.5 = bf16[2048,128]{1,0:T(8,128)(2,1)S(1)} collective-permute-done((bf16[2048,128]{1,0:T(8,128)(2,1)S(1)}, bf16[2048,128]{1,0:T(8,128)(2,1)S(1)}, u32[]{:S(2)}, u32[]{:S(2)}) %collective-permute-start.5) | collective-permute-done | bytes 524320 | tf_op jit(solution)/shard_map/ppermute | solution.py:81
  189.1 1.3 fusion.15
  190.5 4.4 %collective-permute-start.6 = (bf16[2048,128]{1,0:T(8,128)(2,1)S(1)}, bf16[2048,128]{1,0:T(8,128)(2,1)S(1)}, u32[]{:S(2)}, u32[]{:S(2)}) collective-permute-start(bf16[2048,128]{1,0:T(8,128)(2,1)S(1)} %fusion.15), channel_id=1, source_target_pairs={{0,2},{1,3},{2,4},{3,5},{4,6},{5,7},{8,10},{9,11},{10,12},{11,13},... | collective-permute-start | bytes 1572872 | tf_op jit(solution)/shard_map/ppermute | solution.py:81
  194.9 10.6 %collective-permute-done.6 = bf16[2048,128]{1,0:T(8,128)(2,1)S(1)} collective-permute-done((bf16[2048,128]{1,0:T(8,128)(2,1)S(1)}, bf16[2048,128]{1,0:T(8,128)(2,1)S(1)}, u32[]{:S(2)}, u32[]{:S(2)}) %collective-permute-start.6) | collective-permute-done | bytes 524320 | tf_op jit(solution)/shard_map/ppermute | solution.py:81
  205.5 1.7 fusion.16
  207.3 1.3 collective-permute-start.9
  208.6 5.0 %collective-permute-start.7 = (bf16[2048,128]{1,0:T(8,128)(2,1)S(1)}, bf16[2048,128]{1,0:T(8,128)(2,1)S(1)}, u32[]{:S(2)}, u32[]{:S(2)}) collective-permute-start(bf16[2048,128]{1,0:T(8,128)(2,1)S(1)} %get-tuple-element.3), channel_id=1, source_target_pairs={{0,2},{1,3},{2,4},{3,5},{4,6},{5,7},{8,10},{9,11},{10,12},{11,13},... | collective-permute-start | bytes 1572872 | tf_op jit(solution)/shard_map/ppermute | solution.py:81
  213.6 8.5 %collective-permute-done.9 = bf16[2048,128]{1,0:T(8,128)(2,1)S(1)} collective-permute-done((bf16[2048,128]{1,0:T(8,128)(2,1)S(1)}, bf16[2048,128]{1,0:T(8,128)(2,1)S(1)}, u32[]{:S(2)}, u32[]{:S(2)}) %collective-permute-start.9) | collective-permute-done | bytes 524320 | tf_op jit(solution)/shard_map/ppermute | solution.py:82
  222.1 1.3 fusion.14
  223.4 1.3 collective-permute-start.10
  224.8 12.2 %collective-permute-done.10 = bf16[2048,128]{1,0:T(8,128)(2,1)S(1)} collective-permute-done((bf16[2048,128]{1,0:T(8,128)(2,1)S(1)}, bf16[2048,128]{1,0:T(8,128)(2,1)S(1)}, u32[]{:S(2)}, u32[]{:S(2)}) %collective-permute-start.10) | collective-permute-done | bytes 524320 | tf_op jit(solution)/shard_map/ppermute | solution.py:82
  236.9 2.2 fusion.18
  (54 shorter events, 7.0 us)
Async XLA Ops:
  0.6 17.1 %collective-permute-start = (bf16[1024,256]{1,0:T(8,128)(2,1)}, bf16[1024,256]{1,0:T(8,128)(2,1)S(1)}, u32[]{:S(2)}, u32[]{:S(2)}) collective-permute-start(bf16[1024,256]{1,0:T(8,128)(2,1)} %param.4), channel_id=1, source_target_pairs={{0,8},{8,0},{16,24},{24,16},{1,9},{9,1},{17,25},{25,17},{2,10},{10... | collective-permute-start | bytes 1572872 | tf_op jit(solution)/shard_map/ppermute | solution.py:20
  3.6 13.6 %collective-permute-start.1 = (bf16[1024,256]{1,0:T(8,128)(2,1)}, bf16[1024,256]{1,0:T(8,128)(2,1)S(1)}, u32[]{:S(2)}, u32[]{:S(2)}) collective-permute-start(bf16[1024,256]{1,0:T(8,128)(2,1)} %param.4), channel_id=1, source_target_pairs={{0,16},{8,24},{16,0},{24,8},{1,17},{9,25},{17,1},{25,9},{2,18},{10... | collective-permute-start | bytes 1572872 | tf_op jit(solution)/shard_map/ppermute | solution.py:20
  17.2 7.0 %collective-permute-start.2 = (bf16[512,256]{1,0:T(8,128)(2,1)S(1)}, bf16[512,256]{1,0:T(8,128)(2,1)}, u32[]{:S(2)}, u32[]{:S(2)}) collective-permute-start(bf16[512,256]{1,0:T(8,128)(2,1)S(1)} %slice.8), channel_id=1, source_target_pairs={{0,8},{8,0},{16,24},{24,16},{1,9},{9,1},{17,25},{25,17},{2,10},{10... | collective-permute-start | bytes 786440 | tf_op jit(solution)/shard_map/ppermute | solution.py:20
  18.4 7.2 %collective-permute-start.3 = (bf16[512,256]{1,0:T(8,128)(2,1)}, bf16[512,256]{1,0:T(8,128)(2,1)}, u32[]{:S(2)}, u32[]{:S(2)}) collective-permute-start(bf16[512,256]{1,0:T(8,128)(2,1)} %slice.9), channel_id=1, source_target_pairs={{0,16},{8,24},{16,0},{24,8},{1,17},{9,25},{17,1},{25,9},{2,18},{10... | collective-permute-start | bytes 786440 | tf_op jit(solution)/shard_map/ppermute | solution.py:20
  33.1 3.2 %copy-start = (f32[1024,2048]{1,0:T(8,128)}, f32[1024,2048]{1,0:T(8,128)S(1)}, u32[]{:S(2)}) copy-start(f32[1024,2048]{1,0:T(8,128)S(1)} %get-tuple-element.10) | copy-start | bytes 25165828
  52.2 5.8 %copy-start.1 = (f32[1024,2048]{1,0:T(8,128)S(1)}, f32[1024,2048]{1,0:T(8,128)}, u32[]{:S(2)}) copy-start(f32[1024,2048]{1,0:T(8,128)} %copy-done) | copy-start | bytes 25165828
  131.9 18.0 %copy-start.3 = (f32[2048]{0:T(1024)}, f32[2048]{0:T(1024)S(1)}, u32[]{:S(2)}) copy-start(f32[2048]{0:T(1024)S(1)} %add_negate_fusion) | copy-start | bytes 24580
  141.8 7.9 %all-to-all-start.2 = ((f32[4,1,1024]{2,1,0:T(1,128)}), f32[4,1,1024]{2,1,0:T(1,128)S(1)}, u32[]{:S(2)}, u32[]{:S(2)}) async-start(f32[4,1,1024]{2,1,0:T(1,128)} %broadcast_in_dim.71), calls=%async_computation.2 | async-start | bytes 32768 | tf_op jit(solution)/shard_map/all_to_all | solution.py:29
  149.9 9.6 %copy-start.4 = (f32[1024]{0:T(1024)}, f32[1024]{0:T(1024)S(1)}, u32[]{:S(2)}) copy-start(f32[1024]{0:T(1024)S(1)} %add_subtract_fusion) | copy-start | bytes 12292
  165.0 4.5 %collective-permute-start.4 = (bf16[4,2048,128]{2,1,0:T(8,128)(2,1)}, bf16[4,2048,128]{2,1,0:T(8,128)(2,1)}, u32[]{:S(2)}, u32[]{:S(2)}) collective-permute-start(bf16[4,2048,128]{2,1,0:T(8,128)(2,1)} %bitcast.154), channel_id=1, source_target_pairs={{0,1},{1,0},{2,3},{3,2},{4,5},{5,4},{6,7},{7,6},{8,9},{9,8},{10,11... | collective-permute-start | bytes 6291464 | tf_op jit(solution)/shard_map/ppermute | solution.py:68
  172.1 1.9 copy-start.2
  174.2 14.9 %collective-permute-start.5 = (bf16[2048,128]{1,0:T(8,128)(2,1)S(1)}, bf16[2048,128]{1,0:T(8,128)(2,1)S(1)}, u32[]{:S(2)}, u32[]{:S(2)}) collective-permute-start(bf16[2048,128]{1,0:T(8,128)(2,1)S(1)} %get-tuple-element.5), channel_id=1, source_target_pairs={{0,2},{1,3},{2,4},{3,5},{4,6},{5,7},{8,10},{9,11},{10,12},{11,13},... | collective-permute-start | bytes 1572872 | tf_op jit(solution)/shard_map/ppermute | solution.py:81
  177.7 17.2 %collective-permute-start.8 = (bf16[2048,128]{1,0:T(8,128)(2,1)S(1)}, bf16[2048,128]{1,0:T(8,128)(2,1)S(1)}, u32[]{:S(2)}, u32[]{:S(2)}) collective-permute-start(bf16[2048,128]{1,0:T(8,128)(2,1)S(1)} %get-tuple-element.6), channel_id=1, source_target_pairs={{2,0},{3,1},{4,2},{5,3},{6,4},{7,5},{10,8},{11,9},{12,10},{13,11},... | collective-permute-start | bytes 1572872 | tf_op jit(solution)/shard_map/ppermute | solution.py:82
  190.5 15.0 %collective-permute-start.6 = (bf16[2048,128]{1,0:T(8,128)(2,1)S(1)}, bf16[2048,128]{1,0:T(8,128)(2,1)S(1)}, u32[]{:S(2)}, u32[]{:S(2)}) collective-permute-start(bf16[2048,128]{1,0:T(8,128)(2,1)S(1)} %fusion.15), channel_id=1, source_target_pairs={{0,2},{1,3},{2,4},{3,5},{4,6},{5,7},{8,10},{9,11},{10,12},{11,13},... | collective-permute-start | bytes 1572872 | tf_op jit(solution)/shard_map/ppermute | solution.py:81
  207.3 14.9 %collective-permute-start.9 = (bf16[2048,128]{1,0:T(8,128)(2,1)S(1)}, bf16[2048,128]{1,0:T(8,128)(2,1)S(1)}, u32[]{:S(2)}, u32[]{:S(2)}) collective-permute-start(bf16[2048,128]{1,0:T(8,128)(2,1)S(1)} %get-tuple-element.4), channel_id=1, source_target_pairs={{2,0},{3,1},{4,2},{5,3},{6,4},{7,5},{10,8},{11,9},{12,10},{13,11},... | collective-permute-start | bytes 1572872 | tf_op jit(solution)/shard_map/ppermute | solution.py:82
  208.6 16.2 %collective-permute-start.7 = (bf16[2048,128]{1,0:T(8,128)(2,1)S(1)}, bf16[2048,128]{1,0:T(8,128)(2,1)S(1)}, u32[]{:S(2)}, u32[]{:S(2)}) collective-permute-start(bf16[2048,128]{1,0:T(8,128)(2,1)S(1)} %get-tuple-element.3), channel_id=1, source_target_pairs={{0,2},{1,3},{2,4},{3,5},{4,6},{5,7},{8,10},{9,11},{10,12},{11,13},... | collective-permute-start | bytes 1572872 | tf_op jit(solution)/shard_map/ppermute | solution.py:81
  223.4 13.5 %collective-permute-start.10 = (bf16[2048,128]{1,0:T(8,128)(2,1)S(1)}, bf16[2048,128]{1,0:T(8,128)(2,1)S(1)}, u32[]{:S(2)}, u32[]{:S(2)}) collective-permute-start(bf16[2048,128]{1,0:T(8,128)(2,1)S(1)} %fusion.14), channel_id=1, source_target_pairs={{2,0},{3,1},{4,2},{5,3},{6,4},{7,5},{10,8},{11,9},{12,10},{13,11},... | collective-permute-start | bytes 1572872 | tf_op jit(solution)/shard_map/ppermute | solution.py:82

commit v3 on v0

v3 whole, which is shorter than its diff:
```python
import functools
import math

import jax
import jax.numpy as jnp
from jax import lax
from jax.experimental import pallas as pl
from jax.experimental.pallas import tpu as pltpu
from jax.sharding import PartitionSpec as P

ITERS = 3
TILE = 128
NEGATIVE = -1e30

VMEM = pl.BlockSpec(memory_space=pltpu.VMEM)
SMEM = pl.BlockSpec(memory_space=pltpu.SMEM)


def swap(x, axis, offset):
    size = lax.axis_size(axis)
    return lax.ppermute(x, axis, [(i, i ^ offset) for i in range(size)])


def pair_sum(terms):
    while len(terms) > 1:
        terms = [terms[i] + terms[i + 1] for i in range(0, len(terms), 2)]
    return terms[0]


def combine(parts):
    peak = functools.reduce(jnp.maximum, parts)
    return peak + jnp.log(pair_sum([jnp.exp(part - peak) for part in parts]))


def tile_lists(mask):
    count = mask.shape[1]
    at = jnp.arange(count, dtype=jnp.int32)
    before = jnp.sum(jnp.where(at[None, :] < at[:, None], mask[:, None, :], 0), axis=2)
    hit = (mask[:, None, :] == 1) & (before[:, None, :] == at[None, :, None])
    places = jnp.sum(jnp.where(hit, at[None, None, :], 0), axis=2)
    return jnp.sum(mask, axis=1), places


def row_pass(count_ref, list_ref, s_ref, c_ref, out_ref):
    row_tiles, columns = list_ref.shape
    lane = lax.broadcasted_iota(jnp.int32, (TILE, TILE), 1)

    def one_row_tile(t, found):
        count = count_ref[t]

        def score(k):
            u = list_ref[t, k]
            tile = s_ref[t * columns + u]
            return tile if c_ref is None else tile + c_ref[pl.ds(u, 1), :]

        peak = lax.fori_loop(
            0, count, lambda k, a: jnp.maximum(a, score(k)), jnp.full((TILE, TILE), NEGATIVE, jnp.float32)
        )
        peak = jnp.max(peak, axis=1, keepdims=True)
        total = lax.fori_loop(
            0, count, lambda k, a: a + jnp.exp(score(k) - peak), jnp.zeros((TILE, TILE), jnp.float32)
        )
        total = jnp.sum(total, axis=1, keepdims=True)
        return jnp.where(lane == t, peak + jnp.log(total), found)

    found = lax.fori_loop(0, row_tiles, one_row_tile, jnp.zeros((TILE, TILE), jnp.float32))
    out_ref[...] = found.T[:row_tiles]


def spread_rows(row, wide_ref):
    row_tiles = row.shape[0]
    standing = jnp.concatenate(
        [row, jnp.zeros((TILE - row_tiles, TILE), jnp.float32)], axis=0
    ).T
    for t in range(row_tiles):
        wide_ref[t] = jnp.broadcast_to(standing[:, t : t + 1], (TILE, TILE))


def panel_kernel(widths, blocks, count_ref, list_ref, ccount_ref, clist_ref, offset_ref, *refs):
    e_ref, (s_ref, out_ref) = refs[0], refs[-2:]
    pieces = refs[1:-2]
    columns, row_tiles = clist_ref.shape
    scale = 4.0 / math.sqrt(e_ref.shape[1])
    core = offset_ref[0]
    half = columns // 2
    at = 0
    groups = []
    for group in range(2):
        groups.append([])
        for number in blocks:
            groups[-1].append(pieces[at : at + number])
            at += number
    for group in range(2):
        first = (core if group == 0 else 1 - core) * half
        for u in range(half):
            column = first + u

            def one_tile(k, carry, group=group, u=u, column=column):
                t = clist_ref[column, k]
                total = None
                for j, width in enumerate(widths):
                    parts = groups[group][j]
                    each = half // len(parts)
                    block = parts[u // each][(u % each) * TILE : (u % each + 1) * TILE, :]
                    start = pl.multiple_of(offset_ref[1 + j], TILE)
                    rows = e_ref[pl.ds(pl.multiple_of(t * TILE, TILE), TILE), pl.ds(start, width)]
                    product = lax.dot_general(
                        rows, block, (((1,), (1,)), ((), ())), preferred_element_type=jnp.float32
                    )
                    total = product if total is None else total + product
                s_ref[t * columns + column] = total * scale
                return carry

            lax.fori_loop(0, ccount_ref[column], one_tile, 0)
    row_pass(count_ref, list_ref, s_ref, None, out_ref)


def row_kernel(log_column, count_ref, list_ref, s_ref, *refs):
    parts, (out_ref, c_ref) = refs[:-2], refs[-2:]
    c_ref[...] = log_column - combine([part[...] for part in parts])
    row_pass(count_ref, list_ref, s_ref, c_ref, out_ref)


def column_kernel(ccount_ref, clist_ref, s_ref, *refs):
    parts, (out_ref, r_ref, wide_ref) = refs[:-3], refs[-3:]
    columns = clist_ref.shape[0]
    row = -combine([part[...] for part in parts])
    r_ref[...] = row
    spread_rows(row, wide_ref)

    def one_column_tile(u, carry):
        count = ccount_ref[u]

        def score(k):
            t = clist_ref[u, k]
            return s_ref[t * columns + u] + wide_ref[t]

        peak = lax.fori_loop(
            0, count, lambda k, a: jnp.maximum(a, score(k)), jnp.full((TILE, TILE), NEGATIVE, jnp.float32)
        )
        peak = jnp.max(peak, axis=0, keepdims=True)
        total = lax.fori_loop(
            0, count, lambda k, a: a + jnp.exp(score(k) - peak), jnp.zeros((TILE, TILE), jnp.float32)
        )
        total = jnp.sum(total, axis=0, keepdims=True)
        out_ref[pl.ds(u, 1), :] = peak + jnp.log(total)
        return carry

    lax.fori_loop(0, columns, one_column_tile, 0)


def plan_kernel(log_column, lines, count_ref, list_ref, s_ref, r_ref, p_ref, *refs):
    parts, (out_ref, c_ref, wide_ref) = refs[:-3], refs[-3:]
    row_tiles, columns = list_ref.shape
    c_ref[...] = log_column - combine([part[...] for part in parts])
    spread_rows(r_ref[...], wide_ref)
    width = p_ref.shape[1] // lines

    def one_row_tile(t, carry):
        def one_tile(k, total):
            u = list_ref[t, k]
            plan = jnp.exp(s_ref[t * columns + u] + wide_ref[t] + c_ref[pl.ds(u, 1), :])
            block = p_ref[pl.ds(pl.multiple_of(u * TILE, TILE), TILE), :]
            return total + jnp.dot(
                plan.astype(jnp.bfloat16), block, preferred_element_type=jnp.float32
            )

        total = lax.fori_loop(
            0, count_ref[t], one_tile, jnp.zeros((TILE, p_ref.shape[1]), jnp.float32)
        ).astype(jnp.bfloat16)
        for z in range(lines):
            out_ref[z, pl.ds(pl.multiple_of(t * TILE, TILE), TILE), :] = total[
                :, z * width : (z + 1) * width
            ]
        return carry

    lax.fori_loop(0, row_tiles, one_row_tile, 0)


def params(mebibytes):
    return pltpu.CompilerParams(vmem_limit_bytes=mebibytes * 2**20)


def gather_features(shard):
    width = shard.shape[1]
    me = lax.axis_index("row")
    if lax.axis_size("row") != 4 or width % TILE:
        return [(lax.all_gather(shard, "row", axis=1, tiled=True),)], [jnp.int32(0)]
    half = shard.shape[0] // 2
    near = swap(shard, "row", 1)
    far = swap(shard, "row", 2)
    top = swap(far[:half], "row", 1)
    bottom = swap(near[half:], "row", 2)
    starts = [(me ^ offset) * width for offset in range(4)]
    return [(shard,), (near,), (far,), (top, bottom)], starts


def chip_features(groups, starts, core, width, lines):
    halves = []
    for pieces in groups:
        whole = jnp.zeros((pieces[0][0].shape[0], 2 * lines * width), jnp.bfloat16)
        for blocks, start in zip(pieces, starts):
            block = blocks[0] if len(blocks) == 1 else jnp.concatenate(blocks, axis=0)
            whole = lax.dynamic_update_slice_in_dim(whole, block, start, 1)
        whole = whole.reshape(whole.shape[0], lines, 2, width)
        halves.append(lax.dynamic_index_in_dim(whole, core, 2, keepdims=False))
    first = jnp.where(core == 0, halves[0], halves[1])
    second = jnp.where(core == 0, halves[1], halves[0])
    return jnp.concatenate([first, second], axis=0).reshape(-1, lines * width)


def scatter_partials(split):
    size = lax.axis_size("proto")
    line = size // 2
    z = lax.axis_index("proto") // 2
    up = [(i, i + 2) for i in range(size - 2)]
    down = [(i + 2, i) for i in range(size - 2)]

    def chunk(index):
        index = jnp.clip(index, 0, line - 1)
        return lax.dynamic_index_in_dim(split, index, 0, keepdims=False).astype(jnp.float32)

    from_below = from_above = None
    for step in range(1, line):
        send_up, send_down = chunk(line - step + z), chunk(z - (line - step))
        if step > 1:
            send_up, send_down = send_up + from_below, send_down + from_above
        send_up, send_down = lax.optimization_barrier(
            (send_up.astype(jnp.bfloat16), send_down.astype(jnp.bfloat16))
        )
        from_below = lax.ppermute(send_up, "proto", up)
        from_above = lax.ppermute(send_down, "proto", down)
        from_below, from_above = lax.optimization_barrier((from_below, from_above))
        from_below, from_above = from_below.astype(jnp.float32), from_above.astype(jnp.float32)
    return (chunk(z) + from_below + from_above).astype(jnp.bfloat16)


def shards(embeddings, prototypes, block_mask):
    n_row, n_proto = lax.axis_size("row"), lax.axis_size("proto")
    lines = n_proto // 2
    core = lax.axis_index("proto") % 2
    rows, features = embeddings.shape
    protos = 2 * prototypes.shape[0]
    width = features // n_proto
    log_column = math.log(rows * n_row / (protos * lines))

    other_mask = swap(block_mask, "proto", 1)
    own, starts = gather_features(prototypes)
    sibling = [tuple(swap(block, "proto", 1) for block in blocks) for blocks in own]

    mask = jnp.where(block_mask == 1, 1, 0)
    other_mask = jnp.where(other_mask == 1, 1, 0)
    mask = jnp.where(
        core == 0,
        jnp.concatenate([mask, other_mask], axis=1),
        jnp.concatenate([other_mask, mask], axis=1),
    )
    row_tiles, columns = mask.shape
    counts, lists = tile_lists(mask)
    ccounts, clists = tile_lists(mask.T)

    row_shape = jax.ShapeDtypeStruct((row_tiles, TILE), jnp.float32)
    column_shape = jax.ShapeDtypeStruct((columns, TILE), jnp.float32)
    panel = pltpu.VMEM((row_tiles * columns, TILE, TILE), jnp.float32)
    wide = pltpu.VMEM((row_tiles, TILE, TILE), jnp.float32)
    offsets = jnp.stack([core.astype(jnp.int32)] + [s.astype(jnp.int32) for s in starts])
    pieces = [block for group in (own, sibling) for blocks in group for block in blocks]
    similar, row_part = pl.pallas_call(
        functools.partial(
            panel_kernel, [b[0].shape[1] for b in own], [len(b) for b in own]
        ),
        out_shape=(panel, row_shape),
        in_specs=[SMEM] * 5 + [VMEM] * (1 + len(pieces)),
        out_specs=(VMEM, VMEM),
        compiler_params=params(16),
        name="panel",
    )(counts, lists, ccounts, clists, offsets, embeddings, *pieces)
    chosen = chip_features((own, sibling), starts, core, width, lines)

    for sweep in range(ITERS):
        parts = [row_part] + [swap(row_part, "proto", 2 * j) for j in range(1, lines)]
        column_part, row_potential = pl.pallas_call(
            column_kernel,
            out_shape=(column_shape, row_shape),
            in_specs=[SMEM] * 2 + [VMEM] * (1 + len(parts)),
            out_specs=(VMEM, VMEM),
            scratch_shapes=[wide],
            compiler_params=params(8),
            name="column_pass",
        )(ccounts, clists, similar, *parts)
        parts = [column_part] + [swap(column_part, "row", j) for j in range(1, n_row)]
        if sweep < ITERS - 1:
            row_part, _ = pl.pallas_call(
                functools.partial(row_kernel, log_column),
                out_shape=(row_shape, column_shape),
                in_specs=[SMEM] * 2 + [VMEM] * (1 + len(parts)),
                out_specs=(VMEM, VMEM),
                compiler_params=params(8),
                name="row_pass",
            )(counts, lists, similar, *parts)
    split, column_potential = pl.pallas_call(
        functools.partial(plan_kernel, log_column, lines),
        out_shape=(jax.ShapeDtypeStruct((lines, rows, width), jnp.bfloat16), column_shape),
        in_specs=[SMEM] * 2 + [VMEM] * (3 + len(parts)),
        out_specs=(VMEM, VMEM),
        scratch_shapes=[wide],
        compiler_params=params(16),
        name="plan",
    )(counts, lists, similar, row_potential, chosen, *parts)
    targets = scatter_partials(split)
    half = columns // 2
    column_potential = lax.dynamic_slice_in_dim(column_potential, core * half, half, 0)
    return (targets, row_potential.reshape(rows), column_potential.reshape(protos // 2))


def solution(mesh):
    return jax.shard_map(
        shards,
        mesh=mesh,
        in_specs=(P("row", None), P("proto", "row"), P("row", "proto")),
        out_specs=(P("row", "proto"), P("row"), P("proto")),
        check_vma=False,
    )
```

time: 330 us -> 222 us (0.67); the launches traced: 330 us -> 218 us
  blocking collectives: 139 us -> 0 us
  starting transfers between devices: 0.08 us -> 58.4 us
  Pallas kernels: 0 us -> 43 us
  other arithmetic: 51.8 us -> 13.4 us
  waiting for transfers between devices: 87 us -> 55.8 us
  local copies, waits for them, and re-layouts: 15.1 us -> 46 us
  matrix products: 22.7 us -> 0 us
  between operations: 14.2 us -> 0.93 us
    pmax x6 -> x0, blocking collectives: 71.3 us -> none  [the longest x3 44.6 us: row_logsum(): lax.pmax(jnp.max(jnp.where(allowed, values, NEGATIVE), axis=1), 'proto')]
    psum x6 -> x0, blocking collectives: 67.6 us -> none  [the longest x3 41.8 us: row_logsum(): lax.psum(jnp.sum(jnp.where(allowed, jnp.exp(values - peak[:, None]), 0.0)...]
    ppermute x0 -> x34, starting transfers between devices: none -> 58.4 us  [the longest x28 43.6 us: swap(): return lax.ppermute(x, axis, [(i, i ^ offset) for i in range(size)])]
    ppermute x0 -> x34, waiting for transfers between devices: none -> 55.8 us  [the longest x28 25.8 us: swap(): return lax.ppermute(x, axis, [(i, i ^ offset) for i in range(size)])]
    unnamed x3 -> x0, waiting for transfers between devices: 48 us -> none
    pallas_call x0 -> x7, Pallas kernels: none -> 43 us  [the longest x1 12.8 us: shards(): pl.pallas_call(functools.partial(panel_kernel, [b[0].shape[1] for b in ow...]
    all_gather x1 -> x0, waiting for transfers between devices: 39 us -> none  [shards(): features = lax.all_gather(prototypes, 'row', axis=1, tiled=True)]
    reduce_sum x6 -> x3, other arithmetic: 28.3 us -> 1.35 us  [the longest x1 0.62 us: tile_lists(): places = jnp.sum(jnp.where(hit, at[None, None, :], 0), axis=2)]
  transfers between devices with their start and end apart: 2 -> 34, of which waited for: 2 -> 18; matrix products, arithmetic and copies ran while one was open for 0% -> 13% of each run, Pallas kernels for 0% -> 0%
where the time goes in v3:
time: 222 us; the launch traced here: 218 us
  starting transfers between devices  58.4 us (26%)
  waiting for transfers between devices  55.8 us (25%)
  local copies, waits for them, and re-layouts  46 us (21%)
  Pallas kernels  43 us (19%)
  other arithmetic  13.4 us (6%)
    ppermute x28, starting transfers between devices, swap(): return lax.ppermute(x, axis, [(i, i ^ offset) for i in range(size)])  43.6 us
    unnamed x25, local copies, waits for them, and re-layouts  26.6 us
    ppermute x28, waiting for transfers between devices, swap(): return lax.ppermute(x, axis, [(i, i ^ offset) for i in range(size)])  25.8 us
    ppermute x3, waiting for transfers between devices, scatter_partials(): from_below = lax.ppermute(send_up, 'proto', up)  16.4 us
    ppermute x3, waiting for transfers between devices, scatter_partials(): from_above = lax.ppermute(send_down, 'proto', down)  13.7 us
    pallas_call x1, Pallas kernels, shards(): pl.pallas_call(functools.partial(panel_kernel, [b[0].shape[1] for b in ow...  12.8 us
    pallas_call x3, Pallas kernels, shards(): pl.pallas_call(column_kernel, out_shape=(column_shape, row_shape), in_spe...  11.4 us
    pallas_call x2, Pallas kernels, shards(): pl.pallas_call(functools.partial(row_kernel, log_column), out_shape=(row_...  10.9 us
  transfers between devices with their start and end apart: 34, of which 18 were waited for; matrix products, arithmetic and copies ran while one was open for 13% of the time, Pallas kernels for 0%

profile of v3, /device:TPU:0, one launch (start us, length us, event | category | flops | bytes accessed | tf_op | source)
XLA Modules:
  0.0 217.6 jit_solution(7454709343921328117)
XLA Ops:
  1.1 2.6 %collective-permute-start.1 = (bf16[1024,256]{1,0:T(8,128)(2,1)}, bf16[1024,256]{1,0:T(8,128)(2,1)S(1)}, u32[]{:S(2)}, u32[]{:S(2)}) collective-permute-start(bf16[1024,256]{1,0:T(8,128)(2,1)} %refs_1_.1), channel_id=1, source_target_pairs={{0,8},{8,0},{16,24},{24,16},{1,9},{9,1},{17,25},{25,17},{2,10},{10... | collective-permute-start | bytes 1572872 | tf_op jit(solution)/shard_map/ppermute | solution.py:21
  3.7 1.5 collective-permute-start.2
  7.2 1.6 broadcast.35.clone.1
  10.5 7.5 %collective-permute-done.2.refs_3_ = bf16[1024,256]{1,0:T(8,128)(2,1)S(1)} collective-permute-done((bf16[1024,256]{1,0:T(8,128)(2,1)}, bf16[1024,256]{1,0:T(8,128)(2,1)S(1)}, u32[]{:S(2)}, u32[]{:S(2)}) %collective-permute-start.2) | collective-permute-done | bytes 524320 | tf_op jit(solution)/shard_map/ppermute | solution.py:21
  19.1 1.7 collective-permute-start.4
  23.3 1.6 broadcast.35.clone
  28.8 1.9 constant_dynamic-update-slice_fusion.5
  30.7 1.9 pad_maximum_fusion.1
  32.5 2.0 copy.25
  34.6 2.2 %copy-done.7 = bf16[2048,1024]{1,0:T(8,128)(2,1)S(1)} copy-done((bf16[2048,1024]{1,0:T(8,128)(2,1)S(1)}, bf16[2048,1024]{1,0:T(8,128)(2,1)}, u32[]{:S(2)}) %copy-start.7) | copy-done | bytes 4194328
  36.8 12.8 %panel.1 = (f32[256,128,128]{2,1,0:T(8,128)S(1)}, f32[16,128]{1,0:T(8,128)S(1)}) custom-call(s32[16]{0:T(128)S(1)} %get-tuple-element.48.count_ref, s32[16,16]{1,0:T(8,128)S(1)} %get-tuple-element.62.list_ref, s32[16]{0:T(128)S(1)} %get-tuple-element.47.ccount_ref, s32[16,16]{1,0:T(8,128)S(1)} %get-tuple-element.61.clist_ref, s32[5]{0:T(128)S(1)} %stack.23.offset_ref, ...), custom_call_target="tpu_custom_call" | custom-call | tf_op jit(solution)/shard_map/panel/pallas_call | solution.py:268
  49.7 5.8 %copy-done = f32[256,128,128]{2,1,0:T(8,128)} copy-done((f32[256,128,128]{2,1,0:T(8,128)}, f32[256,128,128]{2,1,0:T(8,128)S(1)}, u32[]{:S(2)}) %copy-start) | copy-done | bytes 16777240
  55.4 2.9 %collective-permute-start.10 = (f32[16,128]{1,0:T(8,128)S(1)}, f32[16,128]{1,0:T(8,128)S(1)}, u32[]{:S(2)}, u32[]{:S(2)}) collective-permute-start(f32[16,128]{1,0:T(8,128)S(1)} %get-tuple-element.26.refs_0_), channel_id=1, source_target_pairs={{0,2},{1,3},{2,0},{3,1},{4,6},{5,7},{6,4},{7,5},{8,10},{9,11},{10,... | collective-permute-start | bytes 24584 | tf_op jit(solution)/shard_map/ppermute | solution.py:21
  58.3 2.8 %collective-permute-start.11 = (f32[16,128]{1,0:T(8,128)S(1)}, f32[16,128]{1,0:T(8,128)S(1)}, u32[]{:S(2)}, u32[]{:S(2)}) collective-permute-start(f32[16,128]{1,0:T(8,128)S(1)} %get-tuple-element.26.refs_0_), channel_id=1, source_target_pairs={{0,4},{1,5},{2,6},{3,7},{4,0},{5,1},{6,2},{7,3},{8,12},{9,13},{10,... | collective-permute-start | bytes 24584 | tf_op jit(solution)/shard_map/ppermute | solution.py:21
  62.8 3.7 %collective-permute-done.12.refs_3_ = f32[16,128]{1,0:T(8,128)S(1)} collective-permute-done((f32[16,128]{1,0:T(8,128)S(1)}, f32[16,128]{1,0:T(8,128)S(1)}, u32[]{:S(2)}, u32[]{:S(2)}) %collective-permute-start.12) | collective-permute-done | bytes 8224 | tf_op jit(solution)/shard_map/ppermute | solution.py:21
  66.6 5.8 %copy-done.1 = f32[256,128,128]{2,1,0:T(8,128)S(1)} copy-done((f32[256,128,128]{2,1,0:T(8,128)S(1)}, f32[256,128,128]{2,1,0:T(8,128)}, u32[]{:S(2)}) %copy-start.1) | copy-done | bytes 16777240
  72.3 3.8 %column_pass.3 = (f32[16,128]{1,0:T(8,128)S(1)}, f32[16,128]{1,0:T(8,128)}) custom-call(s32[16]{0:T(128)S(1)} %get-tuple-element.47.ccount_ref, s32[16,16]{1,0:T(8,128)S(1)} %get-tuple-element.61.clist_ref, f32[256,128,128]{2,1,0:T(8,128)S(1)} %copy-done.1, f32[16,128]{1,0:T(8,128)S(1)} %get-tuple-element.26.refs_0_, ...), custom_call_target="tpu_custom_call" | custom-call | tf_op jit(solution)/shard_map/column_pass/pallas_call | solution.py:282
  76.1 3.0 %collective-permute-start.13 = (f32[16,128]{1,0:T(8,128)S(1)}, f32[16,128]{1,0:T(8,128)S(1)}, u32[]{:S(2)}, u32[]{:S(2)}) collective-permute-start(f32[16,128]{1,0:T(8,128)S(1)} %get-tuple-element.27.refs_0_), channel_id=1, source_target_pairs={{0,8},{8,0},{16,24},{24,16},{1,9},{9,1},{17,25},{25,17},{2,10},{10... | collective-permute-start | bytes 24584 | tf_op jit(solution)/shard_map/ppermute | solution.py:21
  79.1 11.7 %collective-permute-start.14 = (f32[16,128]{1,0:T(8,128)S(1)}, f32[16,128]{1,0:T(8,128)S(1)}, u32[]{:S(2)}, u32[]{:S(2)}) collective-permute-start(f32[16,128]{1,0:T(8,128)S(1)} %get-tuple-element.27.refs_0_), channel_id=1, source_target_pairs={{0,16},{8,24},{16,0},{24,8},{1,17},{9,25},{17,1},{25,9},{2,18},{10... | collective-permute-start | bytes 24584 | tf_op jit(solution)/shard_map/ppermute | solution.py:21
  92.4 2.9 %collective-permute-done.15.refs_3_ = f32[16,128]{1,0:T(8,128)S(1)} collective-permute-done((f32[16,128]{1,0:T(8,128)S(1)}, f32[16,128]{1,0:T(8,128)S(1)}, u32[]{:S(2)}, u32[]{:S(2)}) %collective-permute-start.15) | collective-permute-done | bytes 8224 | tf_op jit(solution)/shard_map/ppermute | solution.py:21
  95.3 5.5 %row_pass.2 = (f32[16,128]{1,0:T(8,128)S(1)}, f32[16,128]{1,0:T(8,128)}) custom-call(s32[16]{0:T(128)S(1)} %get-tuple-element.48.count_ref, s32[16,16]{1,0:T(8,128)S(1)} %get-tuple-element.62.list_ref, f32[256,128,128]{2,1,0:T(8,128)S(1)} %copy-done.2, f32[16,128]{1,0:T(8,128)S(1)} %get-tuple-element.27.refs_0_, ...), custom_call_target="tpu_custom_call" | custom-call | tf_op jit(solution)/shard_map/row_pass/pallas_call | solution.py:293
  101.5 1.3 collective-permute-start.17
  102.8 2.4 %collective-permute-start.18 = (f32[16,128]{1,0:T(8,128)S(1)}, f32[16,128]{1,0:T(8,128)S(1)}, u32[]{:S(2)}, u32[]{:S(2)}) collective-permute-start(f32[16,128]{1,0:T(8,128)S(1)} %get-tuple-element.28.refs_0_), channel_id=1, source_target_pairs={{0,6},{1,7},{2,4},{3,5},{4,2},{5,3},{6,0},{7,1},{8,14},{9,15},{10,... | collective-permute-start | bytes 24584 | tf_op jit(solution)/shard_map/ppermute | solution.py:21
  106.4 1.8 collective-permute-done.18.refs_3_
  108.3 5.8 %copy-done.3 = f32[256,128,128]{2,1,0:T(8,128)S(1)} copy-done((f32[256,128,128]{2,1,0:T(8,128)S(1)}, f32[256,128,128]{2,1,0:T(8,128)}, u32[]{:S(2)}) %copy-start.3) | copy-done | bytes 16777240
  114.0 3.8 %column_pass.4 = (f32[16,128]{1,0:T(8,128)S(1)}, f32[16,128]{1,0:T(8,128)}) custom-call(s32[16]{0:T(128)S(1)} %get-tuple-element.47.ccount_ref, s32[16,16]{1,0:T(8,128)S(1)} %get-tuple-element.61.clist_ref, f32[256,128,128]{2,1,0:T(8,128)S(1)} %copy-done.3, f32[16,128]{1,0:T(8,128)S(1)} %get-tuple-element.28.refs_0_, ...), custom_call_target="tpu_custom_call" | custom-call | tf_op jit(solution)/shard_map/column_pass/pallas_call | solution.py:282
  118.2 3.2 %collective-permute-start.20 = (f32[16,128]{1,0:T(8,128)S(1)}, f32[16,128]{1,0:T(8,128)S(1)}, u32[]{:S(2)}, u32[]{:S(2)}) collective-permute-start(f32[16,128]{1,0:T(8,128)S(1)} %get-tuple-element.29.refs_0_), channel_id=1, source_target_pairs={{0,16},{8,24},{16,0},{24,8},{1,17},{9,25},{17,1},{25,9},{2,18},{10... | collective-permute-start | bytes 24584 | tf_op jit(solution)/shard_map/ppermute | solution.py:21
  123.0 2.9 %collective-permute-done.21.refs_3_ = f32[16,128]{1,0:T(8,128)S(1)} collective-permute-done((f32[16,128]{1,0:T(8,128)S(1)}, f32[16,128]{1,0:T(8,128)S(1)}, u32[]{:S(2)}, u32[]{:S(2)}) %collective-permute-start.21) | collective-permute-done | bytes 8224 | tf_op jit(solution)/shard_map/ppermute | solution.py:21
  125.9 5.5 %row_pass.3 = (f32[16,128]{1,0:T(8,128)S(1)}, f32[16,128]{1,0:T(8,128)}) custom-call(s32[16]{0:T(128)S(1)} %get-tuple-element.48.count_ref, s32[16,16]{1,0:T(8,128)S(1)} %get-tuple-element.62.list_ref, f32[256,128,128]{2,1,0:T(8,128)S(1)} %copy-done.4, f32[16,128]{1,0:T(8,128)S(1)} %get-tuple-element.29.refs_0_, ...), custom_call_target="tpu_custom_call" | custom-call | tf_op jit(solution)/shard_map/row_pass/pallas_call | solution.py:293
  131.4 3.4 %collective-permute-start.23 = (f32[16,128]{1,0:T(8,128)S(1)}, f32[16,128]{1,0:T(8,128)S(1)}, u32[]{:S(2)}, u32[]{:S(2)}) collective-permute-start(f32[16,128]{1,0:T(8,128)S(1)} %get-tuple-element.30.refs_0_), channel_id=1, source_target_pairs={{0,4},{1,5},{2,6},{3,7},{4,0},{5,1},{6,2},{7,3},{8,12},{9,13},{10,... | collective-permute-start | bytes 24584 | tf_op jit(solution)/shard_map/ppermute | solution.py:21
  135.8 1.7 broadcast_select_fusion.1
  140.3 5.8 %copy-done.5 = f32[256,128,128]{2,1,0:T(8,128)S(1)} copy-done((f32[256,128,128]{2,1,0:T(8,128)S(1)}, f32[256,128,128]{2,1,0:T(8,128)}, u32[]{:S(2)}) %copy-start.5) | copy-done | bytes 16777240
  146.0 3.8 %column_pass.5 = (f32[16,128]{1,0:T(8,128)S(1)}, f32[16,128]{1,0:T(8,128)}) custom-call(s32[16]{0:T(128)S(1)} %get-tuple-element.47.ccount_ref, s32[16,16]{1,0:T(8,128)S(1)} %get-tuple-element.61.clist_ref, f32[256,128,128]{2,1,0:T(8,128)S(1)} %copy-done.5, f32[16,128]{1,0:T(8,128)S(1)} %get-tuple-element.30.refs_0_, ...), custom_call_target="tpu_custom_call" | custom-call | tf_op jit(solution)/shard_map/column_pass/pallas_call | solution.py:282
  150.2 3.2 %collective-permute-start.26 = (f32[16,128]{1,0:T(8,128)S(1)}, f32[16,128]{1,0:T(8,128)S(1)}, u32[]{:S(2)}, u32[]{:S(2)}) collective-permute-start(f32[16,128]{1,0:T(8,128)S(1)} %get-tuple-element.32.refs_0_), channel_id=1, source_target_pairs={{0,16},{8,24},{16,0},{24,8},{1,17},{9,25},{17,1},{25,9},{2,18},{10... | collective-permute-start | bytes 24584 | tf_op jit(solution)/shard_map/ppermute | solution.py:21
  153.4 1.4 pad_maximum_fusion.p_ref
  155.0 2.9 %collective-permute-done.27.refs_3_ = f32[16,128]{1,0:T(8,128)S(1)} collective-permute-done((f32[16,128]{1,0:T(8,128)S(1)}, f32[16,128]{1,0:T(8,128)S(1)}, u32[]{:S(2)}, u32[]{:S(2)}) %collective-permute-start.27) | collective-permute-done | bytes 8224 | tf_op jit(solution)/shard_map/ppermute | solution.py:21
  157.9 7.9 %plan.1 = (bf16[4,2048,128]{2,1,0:T(8,128)(2,1)S(1)}, f32[16,128]{1,0:T(8,128)S(1)}) custom-call(s32[16]{0:T(128)S(1)} %get-tuple-element.48.count_ref, s32[16,16]{1,0:T(8,128)S(1)} %get-tuple-element.62.list_ref, f32[256,128,128]{2,1,0:T(8,128)S(1)} %copy-done.6, f32[16,128]{1,0:T(8,128)S(1)} %copy-done.9, bf16[2048,512]{1,0:T(8,128)(2,1)S(1)} %pad_maximum_fusion.p_ref, ...), custom_call_target="tpu_custom_call" | custom-call | tf_op jit(solution)/shard_map/plan/pallas_call | solution.py:301
  166.7 1.8 collective-permute-start.28
  169.8 5.7 %collective-permute-done.28 = bf16[2048,128]{1,0:T(8,128)(2,1)S(1)} collective-permute-done((bf16[2048,128]{1,0:T(8,128)(2,1)}, bf16[2048,128]{1,0:T(8,128)(2,1)S(1)}, u32[]{:S(2)}, u32[]{:S(2)}) %collective-permute-start.28) | collective-permute-done | bytes 524320 | tf_op jit(solution)/shard_map/ppermute | solution.py:231
  175.4 4.2 %collective-permute-done.29 = bf16[2048,128]{1,0:T(8,128)(2,1)} collective-permute-done((bf16[2048,128]{1,0:T(8,128)(2,1)S(1)}, bf16[2048,128]{1,0:T(8,128)(2,1)}, u32[]{:S(2)}, u32[]{:S(2)}) %collective-permute-start.29) | collective-permute-done | bytes 524320 | tf_op jit(solution)/shard_map/ppermute | solution.py:232
  179.7 2.1 fusion.1
  181.8 4.0 %collective-permute-start.30 = (bf16[2048,128]{1,0:T(8,128)(2,1)}, bf16[2048,128]{1,0:T(8,128)(2,1)S(1)}, u32[]{:S(2)}, u32[]{:S(2)}) collective-permute-start(bf16[2048,128]{1,0:T(8,128)(2,1)} %get-tuple-element.38), channel_id=1, source_target_pairs={{0,2},{1,3},{2,4},{3,5},{4,6},{5,7},{8,10},{9,11},{10,12},{11,13},... | collective-permute-start | bytes 1572872 | tf_op jit(solution)/shard_map/ppermute | solution.py:231
  187.1 5.7 %collective-permute-done.30 = bf16[2048,128]{1,0:T(8,128)(2,1)S(1)} collective-permute-done((bf16[2048,128]{1,0:T(8,128)(2,1)}, bf16[2048,128]{1,0:T(8,128)(2,1)S(1)}, u32[]{:S(2)}, u32[]{:S(2)}) %collective-permute-start.30) | collective-permute-done | bytes 524320 | tf_op jit(solution)/shard_map/ppermute | solution.py:231
  192.8 5.1 %collective-permute-done.31 = bf16[2048,128]{1,0:T(8,128)(2,1)} collective-permute-done((bf16[2048,128]{1,0:T(8,128)(2,1)S(1)}, bf16[2048,128]{1,0:T(8,128)(2,1)}, u32[]{:S(2)}, u32[]{:S(2)}) %collective-permute-start.31) | collective-permute-done | bytes 524320 | tf_op jit(solution)/shard_map/ppermute | solution.py:232
  197.9 2.3 %fusion = (bf16[2048,128]{1,0:T(8,128)(2,1)}, bf16[2048,128]{1,0:T(8,128)(2,1)}) fusion(bf16[2048,128]{1,0:T(8,128)(2,1)} %collective-permute-done.31, bf16[4,2048,128]{2,1,0:T(8,128)(2,1)S(1)} %get-tuple-element.33, s32[]{:T(128)S(6)} %min.28, bf16[2048,128]{1,0:T(8,128)(2,1)S(1)} %collective-permute-done.30, s32[]{:T(128)S(6)} %min.23), kind=kLoop, calls=%fused_computation.2 | loop fusion | flops 2097152 | bytes 3145736 | tf_op jit(solution)/shard_map/convert_element_type | solution.py:229
  200.2 5.1 %collective-permute-start.32 = (bf16[2048,128]{1,0:T(8,128)(2,1)}, bf16[2048,128]{1,0:T(8,128)(2,1)S(1)}, u32[]{:S(2)}, u32[]{:S(2)}) collective-permute-start(bf16[2048,128]{1,0:T(8,128)(2,1)} %get-tuple-element.42), channel_id=1, source_target_pairs={{0,2},{1,3},{2,4},{3,5},{4,6},{5,7},{8,10},{9,11},{10,12},{11,13},... | collective-permute-start | bytes 1572872 | tf_op jit(solution)/shard_map/ppermute | solution.py:231
  207.2 5.0 %collective-permute-done.32 = bf16[2048,128]{1,0:T(8,128)(2,1)S(1)} collective-permute-done((bf16[2048,128]{1,0:T(8,128)(2,1)}, bf16[2048,128]{1,0:T(8,128)(2,1)S(1)}, u32[]{:S(2)}, u32[]{:S(2)}) %collective-permute-start.32) | collective-permute-done | bytes 524320 | tf_op jit(solution)/shard_map/ppermute | solution.py:231
  212.2 4.3 %collective-permute-done.33 = bf16[2048,128]{1,0:T(8,128)(2,1)S(1)} collective-permute-done((bf16[2048,128]{1,0:T(8,128)(2,1)}, bf16[2048,128]{1,0:T(8,128)(2,1)S(1)}, u32[]{:S(2)}, u32[]{:S(2)}) %collective-permute-start.33) | collective-permute-done | bytes 524320 | tf_op jit(solution)/shard_map/ppermute | solution.py:232
  (91 shorter events, 29.6 us)
Async XLA Ops:
  0.6 21.7 %collective-permute-start.5 = (bf16[1024,256]{1,0:T(8,128)(2,1)}, bf16[1024,256]{1,0:T(8,128)(2,1)S(1)}, u32[]{:S(2)}, u32[]{:S(2)}) collective-permute-start(bf16[1024,256]{1,0:T(8,128)(2,1)} %refs_1_.1), channel_id=1, source_target_pairs={{0,1},{1,0},{2,3},{3,2},{4,5},{5,4},{6,7},{7,6},{8,9},{9,8},{10,11... | collective-permute-start | bytes 1572872 | tf_op jit(solution)/shard_map/ppermute | solution.py:21
  1.1 17.2 %collective-permute-start.1 = (bf16[1024,256]{1,0:T(8,128)(2,1)}, bf16[1024,256]{1,0:T(8,128)(2,1)S(1)}, u32[]{:S(2)}, u32[]{:S(2)}) collective-permute-start(bf16[1024,256]{1,0:T(8,128)(2,1)} %refs_1_.1), channel_id=1, source_target_pairs={{0,8},{8,0},{16,24},{24,16},{1,9},{9,1},{17,25},{25,17},{2,10},{10... | collective-permute-start | bytes 1572872 | tf_op jit(solution)/shard_map/ppermute | solution.py:21
  3.7 14.2 %collective-permute-start.2 = (bf16[1024,256]{1,0:T(8,128)(2,1)}, bf16[1024,256]{1,0:T(8,128)(2,1)S(1)}, u32[]{:S(2)}, u32[]{:S(2)}) collective-permute-start(bf16[1024,256]{1,0:T(8,128)(2,1)} %refs_1_.1), channel_id=1, source_target_pairs={{0,16},{8,24},{16,0},{24,8},{1,17},{9,25},{17,1},{25,9},{2,18},{10... | collective-permute-start | bytes 1572872 | tf_op jit(solution)/shard_map/ppermute | solution.py:21
  5.2 4.5 %collective-permute-start = (s32[16,8]{0,1:T(8,128)}, s32[16,8]{0,1:T(8,128)S(1)}, u32[]{:S(2)}, u32[]{:S(2)}) collective-permute-start(s32[16,8]{0,1:T(8,128)} %param.5), channel_id=1, source_target_pairs={{0,1},{1,0},{2,3},{3,2},{4,5},{5,4},{6,7},{7,6},{8,9},{9,8},{10,11... | collective-permute-start | bytes 1544 | tf_op jit(solution)/shard_map/ppermute | solution.py:21
  17.9 7.9 %collective-permute-start.3 = (bf16[512,256]{1,0:T(8,128)(2,1)S(1)}, bf16[512,256]{1,0:T(8,128)(2,1)}, u32[]{:S(2)}, u32[]{:S(2)}) collective-permute-start(bf16[512,256]{1,0:T(8,128)(2,1)S(1)} %slice.8), channel_id=1, source_target_pairs={{0,8},{8,0},{16,24},{24,16},{1,9},{9,1},{17,25},{25,17},{2,10},{10... | collective-permute-start | bytes 786440 | tf_op jit(solution)/shard_map/ppermute | solution.py:21
  19.1 7.9 %collective-permute-start.4 = (bf16[512,256]{1,0:T(8,128)(2,1)}, bf16[512,256]{1,0:T(8,128)(2,1)}, u32[]{:S(2)}, u32[]{:S(2)}) collective-permute-start(bf16[512,256]{1,0:T(8,128)(2,1)} %slice.9), channel_id=1, source_target_pairs={{0,16},{8,24},{16,0},{24,8},{1,17},{9,25},{17,1},{25,9},{2,18},{10... | collective-permute-start | bytes 786440 | tf_op jit(solution)/shard_map/ppermute | solution.py:21
  21.4 13.2 %collective-permute-start.6 = (bf16[1024,256]{1,0:T(8,128)(2,1)S(1)}, bf16[1024,256]{1,0:T(8,128)(2,1)S(1)}, u32[]{:S(2)}, u32[]{:S(2)}) collective-permute-start(bf16[1024,256]{1,0:T(8,128)(2,1)S(1)} %collective-permute-done.1.refs_2_), channel_id=1, source_target_pairs={{0,1},{1,0},{2,3},{3,2},{4,5},{5,4},{6,7},{7,6},{8,9},{9,8},{10,11... | collective-permute-start | bytes 1572872 | tf_op jit(solution)/shard_map/ppermute | solution.py:21
  21.5 13.1 %collective-permute-start.7 = (bf16[1024,256]{1,0:T(8,128)(2,1)S(1)}, bf16[1024,256]{1,0:T(8,128)(2,1)S(1)}, u32[]{:S(2)}, u32[]{:S(2)}) collective-permute-start(bf16[1024,256]{1,0:T(8,128)(2,1)S(1)} %collective-permute-done.2.refs_3_), channel_id=1, source_target_pairs={{0,1},{1,0},{2,3},{3,2},{4,5},{5,4},{6,7},{7,6},{8,9},{9,8},{10,11... | collective-permute-start | bytes 1572872 | tf_op jit(solution)/shard_map/ppermute | solution.py:21
  23.3 1.6 copy-start.11
  25.8 8.8 %collective-permute-start.8 = (bf16[512,256]{1,0:T(8,128)(2,1)}, bf16[512,256]{1,0:T(8,128)(2,1)S(1)}, u32[]{:S(2)}, u32[]{:S(2)}) collective-permute-start(bf16[512,256]{1,0:T(8,128)(2,1)} %collective-permute-done.3.refs_4_), channel_id=1, source_target_pairs={{0,1},{1,0},{2,3},{3,2},{4,5},{5,4},{6,7},{7,6},{8,9},{9,8},{10,11... | collective-permute-start | bytes 786440 | tf_op jit(solution)/shard_map/ppermute | solution.py:21
  27.0 7.6 %collective-permute-start.9 = (bf16[512,256]{1,0:T(8,128)(2,1)}, bf16[512,256]{1,0:T(8,128)(2,1)}, u32[]{:S(2)}, u32[]{:S(2)}) collective-permute-start(bf16[512,256]{1,0:T(8,128)(2,1)} %collective-permute-done.4.refs_5_), channel_id=1, source_target_pairs={{0,1},{1,0},{2,3},{3,2},{4,5},{5,4},{6,7},{7,6},{8,9},{9,8},{10,11... | collective-permute-start | bytes 786440 | tf_op jit(solution)/shard_map/ppermute | solution.py:21
  27.8 6.8 %copy-start.8 = (bf16[1024,256]{1,0:T(8,128)(2,1)S(1)}, bf16[1024,256]{1,0:T(8,128)(2,1)}, u32[]{:S(2)}) copy-start(bf16[1024,256]{1,0:T(8,128)(2,1)} %refs_1_.1) | copy-start | bytes 1572868
  34.6 2.2 %copy-start.7 = (bf16[2048,1024]{1,0:T(8,128)(2,1)S(1)}, bf16[2048,1024]{1,0:T(8,128)(2,1)}, u32[]{:S(2)}) copy-start(bf16[2048,1024]{1,0:T(8,128)(2,1)} %refs_0_.1) | copy-start | bytes 12582916
  49.7 5.8 %copy-start = (f32[256,128,128]{2,1,0:T(8,128)}, f32[256,128,128]{2,1,0:T(8,128)S(1)}, u32[]{:S(2)}) copy-start(f32[256,128,128]{2,1,0:T(8,128)S(1)} %get-tuple-element.25.s_ref) | copy-start | bytes 50331652
  55.4 7.0 %collective-permute-start.10 = (f32[16,128]{1,0:T(8,128)S(1)}, f32[16,128]{1,0:T(8,128)S(1)}, u32[]{:S(2)}, u32[]{:S(2)}) collective-permute-start(f32[16,128]{1,0:T(8,128)S(1)} %get-tuple-element.26.refs_0_), channel_id=1, source_target_pairs={{0,2},{1,3},{2,0},{3,1},{4,6},{5,7},{6,4},{7,5},{8,10},{9,11},{10,... | collective-permute-start | bytes 24584 | tf_op jit(solution)/shard_map/ppermute | solution.py:21
  58.3 4.5 %collective-permute-start.11 = (f32[16,128]{1,0:T(8,128)S(1)}, f32[16,128]{1,0:T(8,128)S(1)}, u32[]{:S(2)}, u32[]{:S(2)}) collective-permute-start(f32[16,128]{1,0:T(8,128)S(1)} %get-tuple-element.26.refs_0_), channel_id=1, source_target_pairs={{0,4},{1,5},{2,6},{3,7},{4,0},{5,1},{6,2},{7,3},{8,12},{9,13},{10,... | collective-permute-start | bytes 24584 | tf_op jit(solution)/shard_map/ppermute | solution.py:21
  61.1 5.4 %collective-permute-start.12 = (f32[16,128]{1,0:T(8,128)S(1)}, f32[16,128]{1,0:T(8,128)S(1)}, u32[]{:S(2)}, u32[]{:S(2)}) collective-permute-start(f32[16,128]{1,0:T(8,128)S(1)} %get-tuple-element.26.refs_0_), channel_id=1, source_target_pairs={{0,6},{1,7},{2,4},{3,5},{4,2},{5,3},{6,0},{7,1},{8,14},{9,15},{10,... | collective-permute-start | bytes 24584 | tf_op jit(solution)/shard_map/ppermute | solution.py:21
  66.6 5.8 %copy-start.1 = (f32[256,128,128]{2,1,0:T(8,128)S(1)}, f32[256,128,128]{2,1,0:T(8,128)}, u32[]{:S(2)}) copy-start(f32[256,128,128]{2,1,0:T(8,128)} %copy-done) | copy-start | bytes 50331652
  72.3 23.0 %copy-start.2 = (f32[256,128,128]{2,1,0:T(8,128)S(1)}, f32[256,128,128]{2,1,0:T(8,128)}, u32[]{:S(2)}) copy-start(f32[256,128,128]{2,1,0:T(8,128)} %copy-done) | copy-start | bytes 50331652
  76.1 15.5 %collective-permute-start.13 = (f32[16,128]{1,0:T(8,128)S(1)}, f32[16,128]{1,0:T(8,128)S(1)}, u32[]{:S(2)}, u32[]{:S(2)}) collective-permute-start(f32[16,128]{1,0:T(8,128)S(1)} %get-tuple-element.27.refs_0_), channel_id=1, source_target_pairs={{0,8},{8,0},{16,24},{24,16},{1,9},{9,1},{17,25},{25,17},{2,10},{10... | collective-permute-start | bytes 24584 | tf_op jit(solution)/shard_map/ppermute | solution.py:21
  79.1 13.3 %collective-permute-start.14 = (f32[16,128]{1,0:T(8,128)S(1)}, f32[16,128]{1,0:T(8,128)S(1)}, u32[]{:S(2)}, u32[]{:S(2)}) collective-permute-start(f32[16,128]{1,0:T(8,128)S(1)} %get-tuple-element.27.refs_0_), channel_id=1, source_target_pairs={{0,16},{8,24},{16,0},{24,8},{1,17},{9,25},{17,1},{25,9},{2,18},{10... | collective-permute-start | bytes 24584 | tf_op jit(solution)/shard_map/ppermute | solution.py:21
  90.8 4.5 %collective-permute-start.15 = (f32[16,128]{1,0:T(8,128)S(1)}, f32[16,128]{1,0:T(8,128)S(1)}, u32[]{:S(2)}, u32[]{:S(2)}) collective-permute-start(f32[16,128]{1,0:T(8,128)S(1)} %get-tuple-element.27.refs_0_), channel_id=1, source_target_pairs={{0,24},{8,16},{16,8},{24,0},{1,25},{9,17},{17,9},{25,1},{2,26},{10... | collective-permute-start | bytes 24584 | tf_op jit(solution)/shard_map/ppermute | solution.py:21
  100.8 5.6 %collective-permute-start.16 = (f32[16,128]{1,0:T(8,128)S(1)}, f32[16,128]{1,0:T(8,128)S(1)}, u32[]{:S(2)}, u32[]{:S(2)}) collective-permute-start(f32[16,128]{1,0:T(8,128)S(1)} %get-tuple-element.28.refs_0_), channel_id=1, source_target_pairs={{0,2},{1,3},{2,0},{3,1},{4,6},{5,7},{6,4},{7,5},{8,10},{9,11},{10,... | collective-permute-start | bytes 24584 | tf_op jit(solution)/shard_map/ppermute | solution.py:21
  101.5 5.0 %collective-permute-start.17 = (f32[16,128]{1,0:T(8,128)S(1)}, f32[16,128]{1,0:T(8,128)S(1)}, u32[]{:S(2)}, u32[]{:S(2)}) collective-permute-start(f32[16,128]{1,0:T(8,128)S(1)} %get-tuple-element.28.refs_0_), channel_id=1, source_target_pairs={{0,4},{1,5},{2,6},{3,7},{4,0},{5,1},{6,2},{7,3},{8,12},{9,13},{10,... | collective-permute-start | bytes 24584 | tf_op jit(solution)/shard_map/ppermute | solution.py:21
  102.8 5.4 %collective-permute-start.18 = (f32[16,128]{1,0:T(8,128)S(1)}, f32[16,128]{1,0:T(8,128)S(1)}, u32[]{:S(2)}, u32[]{:S(2)}) collective-permute-start(f32[16,128]{1,0:T(8,128)S(1)} %get-tuple-element.28.refs_0_), channel_id=1, source_target_pairs={{0,6},{1,7},{2,4},{3,5},{4,2},{5,3},{6,0},{7,1},{8,14},{9,15},{10,... | collective-permute-start | bytes 24584 | tf_op jit(solution)/shard_map/ppermute | solution.py:21
  106.2 15.2 %copy-start.10 = (bf16[1024,256]{0,1:T(8,128)(2,1)S(1)}, bf16[1024,256]{0,1:T(8,128)(2,1)}, u32[]{:S(2)}) copy-start(bf16[1024,256]{0,1:T(8,128)(2,1)} %copy.25) | copy-start | bytes 1572868
  108.3 5.8 %copy-start.3 = (f32[256,128,128]{2,1,0:T(8,128)S(1)}, f32[256,128,128]{2,1,0:T(8,128)}, u32[]{:S(2)}) copy-start(f32[256,128,128]{2,1,0:T(8,128)} %copy-done) | copy-start | bytes 50331652
  114.0 11.9 %copy-start.4 = (f32[256,128,128]{2,1,0:T(8,128)S(1)}, f32[256,128,128]{2,1,0:T(8,128)}, u32[]{:S(2)}) copy-start(f32[256,128,128]{2,1,0:T(8,128)} %copy-done) | copy-start | bytes 50331652
  117.8 4.6 %collective-permute-start.19 = (f32[16,128]{1,0:T(8,128)S(1)}, f32[16,128]{1,0:T(8,128)S(1)}, u32[]{:S(2)}, u32[]{:S(2)}) collective-permute-start(f32[16,128]{1,0:T(8,128)S(1)} %get-tuple-element.29.refs_0_), channel_id=1, source_target_pairs={{0,8},{8,0},{16,24},{24,16},{1,9},{9,1},{17,25},{25,17},{2,10},{10... | collective-permute-start | bytes 24584 | tf_op jit(solution)/shard_map/ppermute | solution.py:21
  118.2 4.8 %collective-permute-start.20 = (f32[16,128]{1,0:T(8,128)S(1)}, f32[16,128]{1,0:T(8,128)S(1)}, u32[]{:S(2)}, u32[]{:S(2)}) collective-permute-start(f32[16,128]{1,0:T(8,128)S(1)} %get-tuple-element.29.refs_0_), channel_id=1, source_target_pairs={{0,16},{8,24},{16,0},{24,8},{1,17},{9,25},{17,1},{25,9},{2,18},{10... | collective-permute-start | bytes 24584 | tf_op jit(solution)/shard_map/ppermute | solution.py:21
  121.4 4.5 %collective-permute-start.21 = (f32[16,128]{1,0:T(8,128)S(1)}, f32[16,128]{1,0:T(8,128)S(1)}, u32[]{:S(2)}, u32[]{:S(2)}) collective-permute-start(f32[16,128]{1,0:T(8,128)S(1)} %get-tuple-element.29.refs_0_), channel_id=1, source_target_pairs={{0,24},{8,16},{16,8},{24,0},{1,25},{9,17},{17,9},{25,1},{2,26},{10... | collective-permute-start | bytes 24584 | tf_op jit(solution)/shard_map/ppermute | solution.py:21
  131.4 8.0 %collective-permute-start.22 = (f32[16,128]{1,0:T(8,128)S(1)}, f32[16,128]{1,0:T(8,128)S(1)}, u32[]{:S(2)}, u32[]{:S(2)}) collective-permute-start(f32[16,128]{1,0:T(8,128)S(1)} %get-tuple-element.30.refs_0_), channel_id=1, source_target_pairs={{0,2},{1,3},{2,0},{3,1},{4,6},{5,7},{6,4},{7,5},{8,10},{9,11},{10,... | collective-permute-start | bytes 24584 | tf_op jit(solution)/shard_map/ppermute | solution.py:21
  131.4 7.9 %collective-permute-start.23 = (f32[16,128]{1,0:T(8,128)S(1)}, f32[16,128]{1,0:T(8,128)S(1)}, u32[]{:S(2)}, u32[]{:S(2)}) collective-permute-start(f32[16,128]{1,0:T(8,128)S(1)} %get-tuple-element.30.refs_0_), channel_id=1, source_target_pairs={{0,4},{1,5},{2,6},{3,7},{4,0},{5,1},{6,2},{7,3},{8,12},{9,13},{10,... | collective-permute-start | bytes 24584 | tf_op jit(solution)/shard_map/ppermute | solution.py:21
  134.8 5.4 %collective-permute-start.24 = (f32[16,128]{1,0:T(8,128)S(1)}, f32[16,128]{1,0:T(8,128)S(1)}, u32[]{:S(2)}, u32[]{:S(2)}) collective-permute-start(f32[16,128]{1,0:T(8,128)S(1)} %get-tuple-element.30.refs_0_), channel_id=1, source_target_pairs={{0,6},{1,7},{2,4},{3,5},{4,2},{5,3},{6,0},{7,1},{8,14},{9,15},{10,... | collective-permute-start | bytes 24584 | tf_op jit(solution)/shard_map/ppermute | solution.py:21
  140.3 5.8 %copy-start.5 = (f32[256,128,128]{2,1,0:T(8,128)S(1)}, f32[256,128,128]{2,1,0:T(8,128)}, u32[]{:S(2)}) copy-start(f32[256,128,128]{2,1,0:T(8,128)} %copy-done) | copy-start | bytes 50331652
  146.0 11.9 %copy-start.6 = (f32[256,128,128]{2,1,0:T(8,128)S(1)}, f32[256,128,128]{2,1,0:T(8,128)}, u32[]{:S(2)}) copy-start(f32[256,128,128]{2,1,0:T(8,128)} %copy-done) | copy-start | bytes 50331652
  149.8 8.1 %copy-start.9 = (f32[16,128]{1,0:T(8,128)S(1)}, f32[16,128]{1,0:T(8,128)}, u32[]{:S(2)}) copy-start(f32[16,128]{1,0:T(8,128)} %get-tuple-element.31.r_ref) | copy-start | bytes 24580
  149.8 4.9 %collective-permute-start.25 = (f32[16,128]{1,0:T(8,128)S(1)}, f32[16,128]{1,0:T(8,128)S(1)}, u32[]{:S(2)}, u32[]{:S(2)}) collective-permute-start(f32[16,128]{1,0:T(8,128)S(1)} %get-tuple-element.32.refs_0_), channel_id=1, source_target_pairs={{0,8},{8,0},{16,24},{24,16},{1,9},{9,1},{17,25},{25,17},{2,10},{10... | collective-permute-start | bytes 24584 | tf_op jit(solution)/shard_map/ppermute | solution.py:21
  150.2 4.8 %collective-permute-start.26 = (f32[16,128]{1,0:T(8,128)S(1)}, f32[16,128]{1,0:T(8,128)S(1)}, u32[]{:S(2)}, u32[]{:S(2)}) collective-permute-start(f32[16,128]{1,0:T(8,128)S(1)} %get-tuple-element.32.refs_0_), channel_id=1, source_target_pairs={{0,16},{8,24},{16,0},{24,8},{1,17},{9,25},{17,1},{25,9},{2,18},{10... | collective-permute-start | bytes 24584 | tf_op jit(solution)/shard_map/ppermute | solution.py:21
  153.4 4.5 %collective-permute-start.27 = (f32[16,128]{1,0:T(8,128)S(1)}, f32[16,128]{1,0:T(8,128)S(1)}, u32[]{:S(2)}, u32[]{:S(2)}) collective-permute-start(f32[16,128]{1,0:T(8,128)S(1)} %get-tuple-element.32.refs_0_), channel_id=1, source_target_pairs={{0,24},{8,16},{16,8},{24,0},{1,25},{9,17},{17,9},{25,1},{2,26},{10... | collective-permute-start | bytes 24584 | tf_op jit(solution)/shard_map/ppermute | solution.py:21
  166.7 8.8 %collective-permute-start.28 = (bf16[2048,128]{1,0:T(8,128)(2,1)}, bf16[2048,128]{1,0:T(8,128)(2,1)S(1)}, u32[]{:S(2)}, u32[]{:S(2)}) collective-permute-start(bf16[2048,128]{1,0:T(8,128)(2,1)} %get-tuple-element.34), channel_id=1, source_target_pairs={{0,2},{1,3},{2,4},{3,5},{4,6},{5,7},{8,10},{9,11},{10,12},{11,13},... | collective-permute-start | bytes 1572872 | tf_op jit(solution)/shard_map/ppermute | solution.py:231
  168.5 11.2 %collective-permute-start.29 = (bf16[2048,128]{1,0:T(8,128)(2,1)S(1)}, bf16[2048,128]{1,0:T(8,128)(2,1)}, u32[]{:S(2)}, u32[]{:S(2)}) collective-permute-start(bf16[2048,128]{1,0:T(8,128)(2,1)S(1)} %get-tuple-element.35), channel_id=1, source_target_pairs={{2,0},{3,1},{4,2},{5,3},{6,4},{7,5},{10,8},{11,9},{12,10},{13,11},... | collective-permute-start | bytes 1572872 | tf_op jit(solution)/shard_map/ppermute | solution.py:232
  181.8 11.0 %collective-permute-start.30 = (bf16[2048,128]{1,0:T(8,128)(2,1)}, bf16[2048,128]{1,0:T(8,128)(2,1)S(1)}, u32[]{:S(2)}, u32[]{:S(2)}) collective-permute-start(bf16[2048,128]{1,0:T(8,128)(2,1)} %get-tuple-element.38), channel_id=1, source_target_pairs={{0,2},{1,3},{2,4},{3,5},{4,6},{5,7},{8,10},{9,11},{10,12},{11,13},... | collective-permute-start | bytes 1572872 | tf_op jit(solution)/shard_map/ppermute | solution.py:231
  185.8 12.1 %collective-permute-start.31 = (bf16[2048,128]{1,0:T(8,128)(2,1)S(1)}, bf16[2048,128]{1,0:T(8,128)(2,1)}, u32[]{:S(2)}, u32[]{:S(2)}) collective-permute-start(bf16[2048,128]{1,0:T(8,128)(2,1)S(1)} %get-tuple-element.39), channel_id=1, source_target_pairs={{2,0},{3,1},{4,2},{5,3},{6,4},{7,5},{10,8},{11,9},{12,10},{13,11},... | collective-permute-start | bytes 1572872 | tf_op jit(solution)/shard_map/ppermute | solution.py:232
  200.2 12.0 %collective-permute-start.32 = (bf16[2048,128]{1,0:T(8,128)(2,1)}, bf16[2048,128]{1,0:T(8,128)(2,1)S(1)}, u32[]{:S(2)}, u32[]{:S(2)}) collective-permute-start(bf16[2048,128]{1,0:T(8,128)(2,1)} %get-tuple-element.42), channel_id=1, source_target_pairs={{0,2},{1,3},{2,4},{3,5},{4,6},{5,7},{8,10},{9,11},{10,12},{11,13},... | collective-permute-start | bytes 1572872 | tf_op jit(solution)/shard_map/ppermute | solution.py:231
  205.3 11.3 %collective-permute-start.33 = (bf16[2048,128]{1,0:T(8,128)(2,1)}, bf16[2048,128]{1,0:T(8,128)(2,1)S(1)}, u32[]{:S(2)}, u32[]{:S(2)}) collective-permute-start(bf16[2048,128]{1,0:T(8,128)(2,1)} %get-tuple-element.43), channel_id=1, source_target_pairs={{2,0},{3,1},{4,2},{5,3},{6,4},{7,5},{10,8},{11,9},{12,10},{13,11},... | collective-permute-start | bytes 1572872 | tf_op jit(solution)/shard_map/ppermute | solution.py:232

commit v4 on v0

v4 whole, which is shorter than its diff:
```python
import functools
import math

import jax
import jax.numpy as jnp
from jax import lax
from jax.experimental import pallas as pl
from jax.experimental.pallas import tpu as pltpu
from jax.sharding import PartitionSpec as P

ITERS = 3
TILE = 128
NEGATIVE = -1e30

VMEM = pl.BlockSpec(memory_space=pltpu.VMEM)
SMEM = pl.BlockSpec(memory_space=pltpu.SMEM)


def swap(x, axis, offset):
    size = lax.axis_size(axis)
    return lax.ppermute(x, axis, [(i, i ^ offset) for i in range(size)])


def pair_sum(terms):
    while len(terms) > 1:
        terms = [terms[i] + terms[i + 1] for i in range(0, len(terms), 2)]
    return terms[0]


def combine(parts):
    peak = functools.reduce(jnp.maximum, parts)
    return peak + jnp.log(pair_sum([jnp.exp(part - peak) for part in parts]))


def ordered(mask):
    size = mask.shape[1]
    at = jnp.arange(size, dtype=jnp.int32)
    before = jnp.sum(jnp.where(at[None, :] < at[:, None], mask[:, None, :], 0), axis=2)
    hit = (mask[:, None, :] == 1) & (before[:, None, :] == at[None, :, None])
    places = jnp.sum(jnp.where(hit, at[None, None, :] - size, 0), axis=2) + size
    return places, jnp.sum(mask, axis=1)


def score_loop(count, step, start):
    return lax.fori_loop(0, count, lambda k, a: step(2 * k + 1, step(2 * k, a)), start)


def row_pass(list_ref, half_ref, s_ref, c_ref, acc_ref, out_ref):
    row_tiles, columns = list_ref.shape
    lane = lax.broadcasted_iota(jnp.int32, (TILE, TILE), 1)
    dummy = row_tiles * columns

    def score(t, k):
        u = list_ref[t, k]
        tile = s_ref[jnp.where(u == columns, dummy, t * columns + u)]
        return tile if c_ref is None else tile + c_ref[pl.ds(u, 1), :]

    for t in range(row_tiles):
        acc_ref[t] = score_loop(
            half_ref[t],
            lambda k, a, t=t: jnp.maximum(a, score(t, k)),
            jnp.full((TILE, TILE), NEGATIVE, jnp.float32),
        )
    peaks = jnp.zeros((TILE, TILE), jnp.float32)
    for t in range(row_tiles):
        peak = jnp.max(acc_ref[t], axis=1, keepdims=True)
        peaks = jnp.where(lane == t, peak, peaks)
        acc_ref[t] = jnp.broadcast_to(peak, (TILE, TILE))
    for t in range(row_tiles):
        acc_ref[t] = score_loop(
            half_ref[t],
            lambda k, a, t=t: a + jnp.exp(score(t, k) - acc_ref[t]),
            jnp.zeros((TILE, TILE), jnp.float32),
        )
    totals = jnp.zeros((TILE, TILE), jnp.float32)
    for t in range(row_tiles):
        totals = jnp.where(lane == t, jnp.sum(acc_ref[t], axis=1, keepdims=True), totals)
    out_ref[...] = (peaks + jnp.log(totals)).T[:row_tiles]


def spread_rows(row, wide_ref):
    row_tiles = row.shape[0]
    standing = jnp.concatenate(
        [row, jnp.zeros((TILE - row_tiles, TILE), jnp.float32)], axis=0
    ).T
    for t in range(row_tiles):
        wide_ref[t] = jnp.broadcast_to(standing[:, t : t + 1], (TILE, TILE))


def panel_kernel(row_blocks, list_ref, half_ref, plist_ref, pquarter_ref, offset_ref, *refs):
    e_ref, (s_ref, p_ref, out_ref, acc_ref) = refs[0], refs[-4:]
    pieces = refs[1:-4]
    row_tiles, columns = list_ref.shape
    scale = 4.0 / math.sqrt(e_ref.shape[1])
    core = offset_ref[0]
    protos = p_ref.shape[0] // 2
    for n, piece in enumerate(pieces):
        group, within = n * 2 // len(pieces), n % (len(pieces) // 2)
        rows, width = piece.shape
        first = (core if group == 0 else 1 - core) * protos + row_blocks[within]
        start = pl.multiple_of(offset_ref[1 + within], TILE)
        p_ref[pl.ds(pl.multiple_of(first, TILE), rows), pl.ds(start, width)] = piece[...]
    s_ref[row_tiles * columns] = jnp.full((TILE, TILE), NEGATIVE, jnp.float32)

    def one_pair(pair, carry):
        def four_tiles(k, carry):
            at = [jnp.minimum(plist_ref[pair, 4 * k + i], row_tiles - 1) for i in range(4)]
            rows = jnp.concatenate(
                [e_ref[pl.ds(pl.multiple_of(t * TILE, TILE), TILE), :] for t in at], axis=0
            )
            block = p_ref[pl.ds(pl.multiple_of(pair * 2 * TILE, TILE), 2 * TILE), :]
            product = scale * lax.dot_general(
                rows, block, (((1,), (1,)), ((), ())), preferred_element_type=jnp.float32
            )
            for i, t in enumerate(at):
                for side in range(2):
                    s_ref[t * columns + 2 * pair + side] = product[
                        i * TILE : (i + 1) * TILE, side * TILE : (side + 1) * TILE
                    ]
            return carry

        return lax.fori_loop(0, pquarter_ref[pair], four_tiles, carry)

    lax.fori_loop(0, columns // 2, one_pair, 0)
    row_pass(list_ref, half_ref, s_ref, None, acc_ref, out_ref)


def row_kernel(log_column, list_ref, half_ref, s_ref, *refs):
    parts, (out_ref, c_ref, acc_ref) = refs[:-3], refs[-3:]
    columns = list_ref.shape[1]
    c_ref[:columns] = log_column - combine([part[...] for part in parts])
    c_ref[columns:] = jnp.zeros((c_ref.shape[0] - columns, TILE), jnp.float32)
    row_pass(list_ref, half_ref, s_ref, c_ref, acc_ref, out_ref)


def column_kernel(list_ref, half_ref, s_ref, *refs):
    parts, (out_ref, r_ref, wide_ref, acc_ref) = refs[:-4], refs[-4:]
    columns, row_tiles = list_ref.shape
    dummy = row_tiles * columns
    row = -combine([part[...] for part in parts])
    r_ref[...] = row
    spread_rows(row, wide_ref)

    def score(u, k):
        t = list_ref[u, k]
        inside = jnp.minimum(t, row_tiles - 1)
        return s_ref[jnp.where(t == row_tiles, dummy, t * columns + u)] + wide_ref[inside]

    for u in range(columns):
        acc_ref[u] = score_loop(
            half_ref[u],
            lambda k, a, u=u: jnp.maximum(a, score(u, k)),
            jnp.full((TILE, TILE), NEGATIVE, jnp.float32),
        )
    peaks = [jnp.max(acc_ref[u], axis=0, keepdims=True) for u in range(columns)]
    for u in range(columns):
        acc_ref[u] = score_loop(
            half_ref[u],
            lambda k, a, u=u: a + jnp.exp(score(u, k) - peaks[u]),
            jnp.zeros((TILE, TILE), jnp.float32),
        )
    totals = [jnp.sum(acc_ref[u], axis=0, keepdims=True) for u in range(columns)]
    out_ref[...] = jnp.concatenate(peaks, axis=0) + jnp.log(jnp.concatenate(totals, axis=0))


def plan_kernel(log_column, lines, plist_ref, pquarter_ref, mask_ref, offset_ref, s_ref, r_ref, p_ref, *refs):
    parts, (out_ref, c_ref, wide_ref, total_ref) = refs[:-4], refs[-4:]
    row_tiles, columns = mask_ref.shape
    dummy = row_tiles * columns
    c_ref[...] = log_column - combine([part[...] for part in parts])
    spread_rows(r_ref[...], wide_ref)
    width = out_ref.shape[2]
    core = offset_ref[0]
    total_ref[...] = jnp.zeros(total_ref.shape, jnp.float32)

    def one_pair(pair, carry):
        first = pl.multiple_of(pair * 2 * TILE, TILE)
        if width % TILE:
            wide = p_ref[pl.ds(first, 2 * TILE), :]
            blocks = [
                jnp.where(core == 0, wide[:, z * 2 * width :][:, :width], wide[:, (z * 2 + 1) * width :][:, :width])
                for z in range(lines)
            ]
        else:
            blocks = [
                p_ref[pl.ds(first, 2 * TILE), pl.ds(pl.multiple_of((2 * z + core) * width, TILE), width)]
                for z in range(lines)
            ]
        block = jnp.concatenate(blocks, axis=1)

        def four_tiles(k, carry):
            at = [plist_ref[pair, 4 * k + i] for i in range(4)]
            inside = [jnp.minimum(t, row_tiles - 1) for t in at]
            strips = []
            for t, real in zip(at, inside):
                sides = []
                for side in range(2):
                    u = 2 * pair + side
                    good = (t < row_tiles) & (mask_ref[real, u] == 1)
                    tile = s_ref[jnp.where(good, t * columns + u, dummy)]
                    sides.append(jnp.exp(tile + wide_ref[real] + c_ref[pl.ds(u, 1), :]).astype(jnp.bfloat16))
                strips.append(jnp.concatenate(sides, axis=1))
            product = jnp.dot(
                jnp.concatenate(strips, axis=0), block, preferred_element_type=jnp.float32
            )
            for i, t in enumerate(inside):
                total_ref[t] += product[i * TILE : (i + 1) * TILE]
            return carry

        return lax.fori_loop(0, pquarter_ref[pair], four_tiles, carry)

    lax.fori_loop(0, columns // 2, one_pair, 0)
    for t in range(row_tiles):
        total = total_ref[t].astype(jnp.bfloat16)
        for z in range(lines):
            out_ref[z, t * TILE : (t + 1) * TILE, :] = total[:, z * width : (z + 1) * width]


def params(mebibytes):
    return pltpu.CompilerParams(vmem_limit_bytes=mebibytes * 2**20)


def gather_features(shard):
    width = shard.shape[1]
    me = lax.axis_index("row")

    def sibling(block):
        return swap(block, "proto", 1)

    if lax.axis_size("row") != 4 or width % TILE:
        whole = lax.all_gather(shard, "row", axis=1, tiled=True)
        return [whole, sibling(whole)], [0], [jnp.int32(0)]
    half = shard.shape[0] // 2
    top, bottom = shard[:half], shard[half:]
    near_bottom = swap(bottom, "row", 1)
    far_top = swap(top, "row", 2)
    near_top = swap(top, "row", 1)
    far_bottom = swap(bottom, "row", 2)
    cross_top = swap(far_top, "row", 1)
    cross_bottom = swap(near_bottom, "row", 2)
    pieces = [shard, near_top, near_bottom, far_top, far_bottom, cross_top, cross_bottom]
    firsts = [0, 0, half, 0, half, 0, half]
    starts = [(me ^ offset) * width for offset in (0, 1, 1, 2, 2, 3, 3)]
    return pieces + [sibling(piece) for piece in pieces], firsts, starts


def scatter_partials(split):
    size = lax.axis_size("proto")
    line = size // 2
    z = lax.axis_index("proto") // 2
    up = [(i, i + 2) for i in range(size - 2)]
    down = [(i + 2, i) for i in range(size - 2)]
    halves = []
    half = split.shape[1] // 2
    for part in range(2):

        def chunk(index):
            index = jnp.clip(index, 0, line - 1)
            at = lax.dynamic_slice(split, (index, part * half, 0), (1, half, split.shape[2]))
            return at[0].astype(jnp.float32)

        from_below = from_above = None
        for step in range(1, line):
            send_up, send_down = chunk(line - step + z), chunk(z - (line - step))
            if step > 1:
                send_up, send_down = send_up + from_below, send_down + from_above
            from_below = lax.ppermute(send_up.astype(jnp.bfloat16), "proto", up)
            from_above = lax.ppermute(send_down.astype(jnp.bfloat16), "proto", down)
            from_below, from_above = lax.optimization_barrier((from_below, from_above))
            from_below, from_above = from_below.astype(jnp.float32), from_above.astype(jnp.float32)
        halves.append((chunk(z) + from_below + from_above).astype(jnp.bfloat16))
    return jnp.concatenate(halves, axis=0)


def shards(embeddings, prototypes, block_mask):
    n_row, n_proto = lax.axis_size("row"), lax.axis_size("proto")
    lines = n_proto // 2
    core = lax.axis_index("proto") % 2
    rows, features = embeddings.shape
    protos = 2 * prototypes.shape[0]
    width = features // n_proto
    log_column = math.log(rows * n_row / (protos * lines))

    other_mask = swap(block_mask, "proto", 1)
    pieces, firsts, starts = gather_features(prototypes)

    mask = jnp.where(block_mask == 1, 1, 0)
    other_mask = jnp.where(other_mask == 1, 1, 0)
    mask = jnp.where(
        core == 0,
        jnp.concatenate([mask, other_mask], axis=1),
        jnp.concatenate([other_mask, mask], axis=1),
    )
    row_tiles, columns = mask.shape
    across = mask.T
    row_list, row_count = ordered(mask)
    column_list, column_count = ordered(across)
    pair_list, pair_count = ordered(jnp.max(across.reshape(columns // 2, 2, row_tiles), axis=1))
    row_half, column_half = (row_count + 1) // 2, (column_count + 1) // 2
    pair_quarter = (pair_count + 3) // 4
    offsets = jnp.stack([core.astype(jnp.int32)] + [s.astype(jnp.int32) for s in starts])

    row_shape = jax.ShapeDtypeStruct((row_tiles, TILE), jnp.float32)
    column_shape = jax.ShapeDtypeStruct((columns, TILE), jnp.float32)
    panel = pltpu.VMEM((row_tiles * columns + 1, TILE, TILE), jnp.float32)
    wide = pltpu.VMEM((row_tiles, TILE, TILE), jnp.float32)
    tall = pltpu.VMEM((columns, TILE, TILE), jnp.float32)
    similar, whole, row_part = pl.pallas_call(
        functools.partial(panel_kernel, firsts),
        out_shape=(panel, pltpu.VMEM((protos, features), jnp.bfloat16), row_shape),
        in_specs=[SMEM] * 5 + [VMEM] * (1 + len(pieces)),
        out_specs=(VMEM, VMEM, VMEM),
        scratch_shapes=[wide],
        compiler_params=params(12),
        name="panel",
    )(row_list, row_half, pair_list, pair_quarter, offsets, embeddings, *pieces)

    for sweep in range(ITERS):
        parts = [row_part] + [swap(row_part, "proto", 2 * j) for j in range(1, lines)]
        column_part, row_potential = pl.pallas_call(
            column_kernel,
            out_shape=(column_shape, row_shape),
            in_specs=[SMEM] * 2 + [VMEM] * (1 + len(parts)),
            out_specs=(VMEM, VMEM),
            scratch_shapes=[wide, tall],
            compiler_params=params(8),
            name="column_pass",
        )(column_list, column_half, similar, *parts)
        parts = [column_part] + [swap(column_part, "row", j) for j in range(1, n_row)]
        if sweep < ITERS - 1:
            row_part = pl.pallas_call(
                functools.partial(row_kernel, log_column),
                out_shape=row_shape,
                in_specs=[SMEM] * 2 + [VMEM] * (1 + len(parts)),
                out_specs=VMEM,
                scratch_shapes=[pltpu.VMEM((columns + 8, TILE), jnp.float32), wide],
                compiler_params=params(8),
                name="row_pass",
            )(row_list, row_half, similar, *parts)
    split, column_potential = pl.pallas_call(
        functools.partial(plan_kernel, log_column, lines),
        out_shape=(jax.ShapeDtypeStruct((lines, rows, width), jnp.bfloat16), column_shape),
        in_specs=[SMEM] * 4 + [VMEM] * (3 + len(parts)),
        out_specs=(VMEM, VMEM),
        scratch_shapes=[wide, pltpu.VMEM((row_tiles, TILE, lines * width), jnp.float32)],
        compiler_params=params(16),
        name="plan",
    )(pair_list, pair_quarter, mask, offsets, similar, row_potential, whole, *parts)
    targets = scatter_partials(split)
    half = columns // 2
    column_potential = lax.dynamic_slice_in_dim(column_potential, core * half, half, 0)
    return (targets, row_potential.reshape(rows), column_potential.reshape(protos // 2))


def solution(mesh):
    return jax.shard_map(
        shards,
        mesh=mesh,
        in_specs=(P("row", None), P("proto", "row"), P("row", "proto")),
        out_specs=(P("row", "proto"), P("row"), P("proto")),
        check_vma=False,
    )
```

time: 330 us -> 189 us (0.57)
  blocking collectives: 139 us -> 0 us
  starting transfers between devices: 0.08 us -> 66.2 us
  other arithmetic: 51.8 us -> 7.2 us
  Pallas kernels: 0 us -> 30.8 us
  matrix products: 22.7 us -> 0 us
  waiting for transfers between devices: 87 us -> 66.1 us
  between operations: 14.2 us -> 0.94 us
    pmax x6 -> x0, blocking collectives: 71.3 us -> none  [the longest x3 44.6 us: row_logsum(): lax.pmax(jnp.max(jnp.where(allowed, values, NEGATIVE), axis=1), 'proto')]
    psum x6 -> x0, blocking collectives: 67.6 us -> none  [the longest x3 41.8 us: row_logsum(): lax.psum(jnp.sum(jnp.where(allowed, jnp.exp(values - peak[:, None]), 0.0)...]
    ppermute x0 -> x44, starting transfers between devices: none -> 66.2 us  [the longest x32 38.4 us: swap(): return lax.ppermute(x, axis, [(i, i ^ offset) for i in range(size)])]
    ppermute x0 -> x44, waiting for transfers between devices: none -> 66.1 us  [the longest x32 41.8 us: swap(): return lax.ppermute(x, axis, [(i, i ^ offset) for i in range(size)])]
    unnamed x3 -> x0, waiting for transfers between devices: 48 us -> none
    all_gather x1 -> x0, waiting for transfers between devices: 39 us -> none  [shards(): features = lax.all_gather(prototypes, 'row', axis=1, tiled=True)]
    pallas_call x0 -> x7, Pallas kernels: none -> 30.8 us  [the longest x3 10.5 us: shards(): pl.pallas_call(column_kernel, out_shape=(column_shape, row_shape), in_spe...]
    reduce_sum x6, other arithmetic: 28.3 us -> 1.97 us  [the longest x2 0.84 us: ordered(): places = jnp.sum(jnp.where(hit, at[None, None, :] - size, 0), axis=2) + size]
  transfers between devices with their start and end apart: 2 -> 44, of which waited for: 2 -> 30; matrix products, arithmetic and copies ran while one was open for 0% -> 2% of each run, Pallas kernels for 0% -> 0%
where the time goes in v4:
time: 189 us; the launch traced here: 188 us
  starting transfers between devices  66.2 us (35%)
  waiting for transfers between devices  66.1 us (35%)
  Pallas kernels  30.8 us (16%)
  local copies, waits for them, and re-layouts  17.3 us (9%)
  other arithmetic  7.2 us (4%)
    ppermute x32, waiting for transfers between devices, swap(): return lax.ppermute(x, axis, [(i, i ^ offset) for i in range(size)])  41.8 us
    ppermute x32, starting transfers between devices, swap(): return lax.ppermute(x, axis, [(i, i ^ offset) for i in range(size)])  38.4 us
    ppermute x6, starting transfers between devices, scatter_partials(): from_below = lax.ppermute(send_up.astype(jnp.bfloat16), 'proto', up)  20 us
    ppermute x6, waiting for transfers between devices, scatter_partials(): from_above = lax.ppermute(send_down.astype(jnp.bfloat16), 'proto', down)  17.3 us
    unnamed x15, local copies, waits for them, and re-layouts  14.6 us
    pallas_call x3, Pallas kernels, shards(): pl.pallas_call(column_kernel, out_shape=(column_shape, row_shape), in_spe...  10.5 us
    pallas_call x1, Pallas kernels, shards(): pl.pallas_call(functools.partial(panel_kernel, firsts), out_shape=(panel,...  8.69 us
    ppermute x6, starting transfers between devices, scatter_partials(): from_above = lax.ppermute(send_down.astype(jnp.bfloat16), 'proto', down)  7.73 us
  transfers between devices with their start and end apart: 44, of which 30 were waited for; matrix products, arithmetic and copies ran while one was open for 2% of the time, Pallas kernels for 0%

profile of v4, /device:TPU:0, one launch (start us, length us, event | category | flops | bytes accessed | tf_op | source)
XLA Modules:
  0.0 188.5 jit_solution(16252678260884702573)
XLA Ops:
  1.7 3.0 %collective-permute-start.2 = (bf16[512,256]{1,0:T(8,128)(2,1)S(1)}, bf16[512,256]{1,0:T(8,128)(2,1)S(1)}, u32[]{:S(2)}, u32[]{:S(2)}) collective-permute-start(bf16[512,256]{1,0:T(8,128)(2,1)S(1)} %get-tuple-element.65), channel_id=1, source_target_pairs={{0,8},{8,0},{16,24},{24,16},{1,9},{9,1},{17,25},{25,17},{2,10},{10... | collective-permute-start | bytes 786440 | tf_op jit(solution)/shard_map/ppermute | solution.py:21
  4.7 1.5 collective-permute-start.4
  10.7 7.3 %collective-permute-done.3.refs_4_ = bf16[512,256]{1,0:T(8,128)(2,1)S(1)} collective-permute-done((bf16[512,256]{1,0:T(8,128)(2,1)S(1)}, bf16[512,256]{1,0:T(8,128)(2,1)S(1)}, u32[]{:S(2)}, u32[]{:S(2)}) %collective-permute-start.3) | collective-permute-done | bytes 262176 | tf_op jit(solution)/shard_map/ppermute | solution.py:21
  18.5 1.7 collective-permute-start.6
  20.9 4.1 %collective-permute-done.5.refs_6_ = bf16[512,256]{1,0:T(8,128)(2,1)S(1)} collective-permute-done((bf16[512,256]{1,0:T(8,128)(2,1)S(1)}, bf16[512,256]{1,0:T(8,128)(2,1)S(1)}, u32[]{:S(2)}, u32[]{:S(2)}) %collective-permute-start.5) | collective-permute-done | bytes 262176 | tf_op jit(solution)/shard_map/ppermute | solution.py:21
  24.9 2.2 %collective-permute-done.6.refs_7_ = bf16[512,256]{1,0:T(8,128)(2,1)S(1)} collective-permute-done((bf16[512,256]{1,0:T(8,128)(2,1)S(1)}, bf16[512,256]{1,0:T(8,128)(2,1)S(1)}, u32[]{:S(2)}, u32[]{:S(2)}) %collective-permute-start.6) | collective-permute-done | bytes 262176 | tf_op jit(solution)/shard_map/ppermute | solution.py:21
  29.5 2.2 %copy-done.4 = bf16[2048,1024]{1,0:T(8,128)(2,1)S(1)} copy-done((bf16[2048,1024]{1,0:T(8,128)(2,1)S(1)}, bf16[2048,1024]{1,0:T(8,128)(2,1)}, u32[]{:S(2)}) %copy-start.4) | copy-done | bytes 4194328
  32.7 8.7 %panel.1 = (f32[257,128,128]{2,1,0:T(8,128)S(1)}, bf16[2048,1024]{1,0:T(8,128)(2,1)S(1)}, f32[16,128]{1,0:T(8,128)S(1)}) custom-call(s32[16,16]{1,0:T(8,128)S(1)} %broadcast_add_fusion.1.list_ref, s32[16]{0:T(128)S(1)} %and_select_fusion.1.half_ref, s32[8,16]{1,0:T(8,128)S(1)} %broadcast_add_fusion.2.plist_ref, s32[8]{0:T(128)S(1)} %and_select_fusion.2.pquarter_ref, ...), custom_call_target="tpu_custom_call" | custom-call | tf_op jit(solution)/shard_map/panel/pallas_call | solution.py:308
  41.4 2.0 %copy-done.2 = bf16[2048,1024]{1,0:T(8,128)(2,1)} copy-done((bf16[2048,1024]{1,0:T(8,128)(2,1)}, bf16[2048,1024]{1,0:T(8,128)(2,1)S(1)}, u32[]{:S(2)}) %copy-start.2) | copy-done | bytes 4194328
  43.4 2.4 %collective-permute-start.14 = (f32[16,128]{1,0:T(8,128)S(1)}, f32[16,128]{1,0:T(8,128)S(1)}, u32[]{:S(2)}, u32[]{:S(2)}) collective-permute-start(f32[16,128]{1,0:T(8,128)S(1)} %get-tuple-element.25.refs_0_), channel_id=1, source_target_pairs={{0,2},{1,3},{2,0},{3,1},{4,6},{5,7},{6,4},{7,5},{8,10},{9,11},{10,... | collective-permute-start | bytes 24584 | tf_op jit(solution)/shard_map/ppermute | solution.py:21
  45.8 2.5 %collective-permute-start.15 = (f32[16,128]{1,0:T(8,128)S(1)}, f32[16,128]{1,0:T(8,128)S(1)}, u32[]{:S(2)}, u32[]{:S(2)}) collective-permute-start(f32[16,128]{1,0:T(8,128)S(1)} %get-tuple-element.25.refs_0_), channel_id=1, source_target_pairs={{0,4},{1,5},{2,6},{3,7},{4,0},{5,1},{6,2},{7,3},{8,12},{9,13},{10,... | collective-permute-start | bytes 24584 | tf_op jit(solution)/shard_map/ppermute | solution.py:21
  48.3 2.0 %collective-permute-done.15.refs_2_ = f32[16,128]{1,0:T(8,128)S(1)} collective-permute-done((f32[16,128]{1,0:T(8,128)S(1)}, f32[16,128]{1,0:T(8,128)S(1)}, u32[]{:S(2)}, u32[]{:S(2)}) %collective-permute-start.15) | collective-permute-done | bytes 8224 | tf_op jit(solution)/shard_map/ppermute | solution.py:21
  50.3 3.4 %collective-permute-done.16.refs_3_ = f32[16,128]{1,0:T(8,128)S(1)} collective-permute-done((f32[16,128]{1,0:T(8,128)S(1)}, f32[16,128]{1,0:T(8,128)S(1)}, u32[]{:S(2)}, u32[]{:S(2)}) %collective-permute-start.16) | collective-permute-done | bytes 8224 | tf_op jit(solution)/shard_map/ppermute | solution.py:21
  53.7 3.5 %column_pass.3 = (f32[16,128]{1,0:T(8,128)S(1)}, f32[16,128]{1,0:T(8,128)}) custom-call(s32[16,16]{1,0:T(8,128)S(1)} %broadcast_add_fusion.list_ref, s32[16]{0:T(128)S(1)} %and_select_fusion.half_ref, f32[257,128,128]{2,1,0:T(8,128)S(1)} %get-tuple-element.24.s_ref, f32[16,128]{1,0:T(8,128)S(1)} %get-tuple-element.25.refs_0_, ...), custom_call_target="tpu_custom_call" | custom-call | tf_op jit(solution)/shard_map/column_pass/pallas_call | solution.py:320
  57.2 3.4 %collective-permute-start.17 = (f32[16,128]{1,0:T(8,128)S(1)}, f32[16,128]{1,0:T(8,128)S(1)}, u32[]{:S(2)}, u32[]{:S(2)}) collective-permute-start(f32[16,128]{1,0:T(8,128)S(1)} %get-tuple-element.26.refs_0_), channel_id=1, source_target_pairs={{0,8},{8,0},{16,24},{24,16},{1,9},{9,1},{17,25},{25,17},{2,10},{10... | collective-permute-start | bytes 24584 | tf_op jit(solution)/shard_map/ppermute | solution.py:21
  60.6 5.9 %collective-permute-start.18 = (f32[16,128]{1,0:T(8,128)S(1)}, f32[16,128]{1,0:T(8,128)S(1)}, u32[]{:S(2)}, u32[]{:S(2)}) collective-permute-start(f32[16,128]{1,0:T(8,128)S(1)} %get-tuple-element.26.refs_0_), channel_id=1, source_target_pairs={{0,16},{8,24},{16,0},{24,8},{1,17},{9,25},{17,1},{25,9},{2,18},{10... | collective-permute-start | bytes 24584 | tf_op jit(solution)/shard_map/ppermute | solution.py:21
  66.6 1.6 collective-permute-done.18.refs_2_
  68.2 2.9 %collective-permute-done.19.refs_3_ = f32[16,128]{1,0:T(8,128)S(1)} collective-permute-done((f32[16,128]{1,0:T(8,128)S(1)}, f32[16,128]{1,0:T(8,128)S(1)}, u32[]{:S(2)}, u32[]{:S(2)}) %collective-permute-start.19) | collective-permute-done | bytes 8224 | tf_op jit(solution)/shard_map/ppermute | solution.py:21
  71.1 2.8 %row_pass.2.refs_0_ = f32[16,128]{1,0:T(8,128)S(1)} custom-call(s32[16,16]{1,0:T(8,128)S(1)} %broadcast_add_fusion.1.list_ref, s32[16]{0:T(128)S(1)} %and_select_fusion.1.half_ref, f32[257,128,128]{2,1,0:T(8,128)S(1)} %get-tuple-element.24.s_ref, f32[16,128]{1,0:T(8,128)S(1)} %get-tuple-element.26.refs_0_, f32[16,128]{1,0:T(8,128)S(1)} %collective-permute-done.17.refs_1_, ...), custom_call_target="tpu_custom_call" | custom-call | tf_op jit(solution)/shard_map/row_pass/pallas_call | solution.py:331
  74.7 3.6 %collective-permute-start.22 = (f32[16,128]{1,0:T(8,128)S(1)}, f32[16,128]{1,0:T(8,128)S(1)}, u32[]{:S(2)}, u32[]{:S(2)}) collective-permute-start(f32[16,128]{1,0:T(8,128)S(1)} %row_pass.2.refs_0_), channel_id=1, source_target_pairs={{0,6},{1,7},{2,4},{3,5},{4,2},{5,3},{6,0},{7,1},{8,14},{9,15},{10,... | collective-permute-start | bytes 24584 | tf_op jit(solution)/shard_map/ppermute | solution.py:21
  78.6 1.6 collective-permute-done.22.refs_3_
  80.2 3.5 %column_pass.4 = (f32[16,128]{1,0:T(8,128)S(1)}, f32[16,128]{1,0:T(8,128)}) custom-call(s32[16,16]{1,0:T(8,128)S(1)} %broadcast_add_fusion.list_ref, s32[16]{0:T(128)S(1)} %and_select_fusion.half_ref, f32[257,128,128]{2,1,0:T(8,128)S(1)} %get-tuple-element.24.s_ref, f32[16,128]{1,0:T(8,128)S(1)} %row_pass.2.refs_0_, ...), custom_call_target="tpu_custom_call" | custom-call | tf_op jit(solution)/shard_map/column_pass/pallas_call | solution.py:320
  84.3 2.2 %collective-permute-start.24 = (f32[16,128]{1,0:T(8,128)S(1)}, f32[16,128]{1,0:T(8,128)S(1)}, u32[]{:S(2)}, u32[]{:S(2)}) collective-permute-start(f32[16,128]{1,0:T(8,128)S(1)} %get-tuple-element.27.refs_0_), channel_id=1, source_target_pairs={{0,16},{8,24},{16,0},{24,8},{1,17},{9,25},{17,1},{25,9},{2,18},{10... | collective-permute-start | bytes 24584 | tf_op jit(solution)/shard_map/ppermute | solution.py:21
  88.1 2.9 %collective-permute-done.25.refs_3_ = f32[16,128]{1,0:T(8,128)S(1)} collective-permute-done((f32[16,128]{1,0:T(8,128)S(1)}, f32[16,128]{1,0:T(8,128)S(1)}, u32[]{:S(2)}, u32[]{:S(2)}) %collective-permute-start.25) | collective-permute-done | bytes 8224 | tf_op jit(solution)/shard_map/ppermute | solution.py:21
  91.0 3.0 %row_pass.3.refs_0_ = f32[16,128]{1,0:T(8,128)S(1)} custom-call(s32[16,16]{1,0:T(8,128)S(1)} %broadcast_add_fusion.1.list_ref, s32[16]{0:T(128)S(1)} %and_select_fusion.1.half_ref, f32[257,128,128]{2,1,0:T(8,128)S(1)} %get-tuple-element.24.s_ref, f32[16,128]{1,0:T(8,128)S(1)} %get-tuple-element.27.refs_0_, f32[16,128]{1,0:T(8,128)S(1)} %collective-permute-done.23.refs_1_, ...), custom_call_target="tpu_custom_call" | custom-call | tf_op jit(solution)/shard_map/row_pass/pallas_call | solution.py:331
  94.9 3.5 %collective-permute-start.27 = (f32[16,128]{1,0:T(8,128)S(1)}, f32[16,128]{1,0:T(8,128)S(1)}, u32[]{:S(2)}, u32[]{:S(2)}) collective-permute-start(f32[16,128]{1,0:T(8,128)S(1)} %row_pass.3.refs_0_), channel_id=1, source_target_pairs={{0,4},{1,5},{2,6},{3,7},{4,0},{5,1},{6,2},{7,3},{8,12},{9,13},{10,... | collective-permute-start | bytes 24584 | tf_op jit(solution)/shard_map/ppermute | solution.py:21
  98.4 1.6 collective-permute-done.27.refs_2_
  100.0 3.8 %collective-permute-done.28.refs_3_ = f32[16,128]{1,0:T(8,128)S(1)} collective-permute-done((f32[16,128]{1,0:T(8,128)S(1)}, f32[16,128]{1,0:T(8,128)S(1)}, u32[]{:S(2)}, u32[]{:S(2)}) %collective-permute-start.28) | collective-permute-done | bytes 8224 | tf_op jit(solution)/shard_map/ppermute | solution.py:21
  103.9 3.5 %column_pass.5 = (f32[16,128]{1,0:T(8,128)S(1)}, f32[16,128]{1,0:T(8,128)}) custom-call(s32[16,16]{1,0:T(8,128)S(1)} %broadcast_add_fusion.list_ref, s32[16]{0:T(128)S(1)} %and_select_fusion.half_ref, f32[257,128,128]{2,1,0:T(8,128)S(1)} %get-tuple-element.24.s_ref, f32[16,128]{1,0:T(8,128)S(1)} %row_pass.3.refs_0_, ...), custom_call_target="tpu_custom_call" | custom-call | tf_op jit(solution)/shard_map/column_pass/pallas_call | solution.py:320
  108.5 2.2 %collective-permute-start.30 = (f32[16,128]{1,0:T(8,128)S(1)}, f32[16,128]{1,0:T(8,128)S(1)}, u32[]{:S(2)}, u32[]{:S(2)}) collective-permute-start(f32[16,128]{1,0:T(8,128)S(1)} %get-tuple-element.30.refs_0_), channel_id=1, source_target_pairs={{0,16},{8,24},{16,0},{24,8},{1,17},{9,25},{17,1},{25,9},{2,18},{10... | collective-permute-start | bytes 24584 | tf_op jit(solution)/shard_map/ppermute | solution.py:21
  112.4 2.9 %collective-permute-done.31.refs_3_ = f32[16,128]{1,0:T(8,128)S(1)} collective-permute-done((f32[16,128]{1,0:T(8,128)S(1)}, f32[16,128]{1,0:T(8,128)S(1)}, u32[]{:S(2)}, u32[]{:S(2)}) %collective-permute-start.31) | collective-permute-done | bytes 8224 | tf_op jit(solution)/shard_map/ppermute | solution.py:21
  115.3 5.8 %copy-done.1 = f32[257,128,128]{2,1,0:T(8,128)S(1)} copy-done((f32[257,128,128]{2,1,0:T(8,128)S(1)}, f32[257,128,128]{2,1,0:T(8,128)}, u32[]{:S(2)}) %copy-start.1) | copy-done | bytes 16842776
  121.1 2.2 %copy-done.3 = bf16[2048,1024]{1,0:T(8,128)(2,1)S(1)} copy-done((bf16[2048,1024]{1,0:T(8,128)(2,1)S(1)}, bf16[2048,1024]{1,0:T(8,128)(2,1)}, u32[]{:S(2)}) %copy-start.3) | copy-done | bytes 4194328
  123.9 5.8 %plan.1 = (bf16[4,2048,128]{2,1,0:T(8,128)(2,1)S(1)}, f32[16,128]{1,0:T(8,128)S(1)}) custom-call(s32[8,16]{1,0:T(8,128)S(1)} %broadcast_add_fusion.2.plist_ref, s32[8]{0:T(128)S(1)} %and_select_fusion.2.pquarter_ref, s32[16,16]{1,0:T(8,128)S(1)} %get-tuple-element.51.mask_ref, s32[8]{0:T(128)S(1)} %stack.26.offset_ref, f32[257,128,128]{2,1,0:T(8,128)S(1)} %copy-done.1, ...), custom_call_target="tpu_custom_call" | custom-call | tf_op jit(solution)/shard_map/plan/pallas_call | solution.py:340
  133.1 5.3 %collective-permute-start.38 = (bf16[1024,128]{1,0:T(8,128)(2,1)}, bf16[1024,128]{1,0:T(8,128)(2,1)}, u32[]{:S(2)}, u32[]{:S(2)}) collective-permute-start(bf16[1024,128]{1,0:T(8,128)(2,1)} %get-tuple-element.63), channel_id=1, source_target_pairs={{0,2},{1,3},{2,4},{3,5},{4,6},{5,7},{8,10},{9,11},{10,12},{11,13},... | collective-permute-start | bytes 786440 | tf_op jit(solution)/shard_map/ppermute | solution.py:267
  139.7 2.9 %collective-permute-done.33 = bf16[1024,128]{1,0:T(8,128)(2,1)S(1)} collective-permute-done((bf16[1024,128]{1,0:T(8,128)(2,1)S(1)}, bf16[1024,128]{1,0:T(8,128)(2,1)S(1)}, u32[]{:S(2)}, u32[]{:S(2)}) %collective-permute-start.33) | collective-permute-done | bytes 262176 | tf_op jit(solution)/shard_map/ppermute | solution.py:268
  142.7 1.7 collective-permute-start.34
  146.7 2.0 %collective-permute-done.34 = bf16[1024,128]{1,0:T(8,128)(2,1)S(1)} collective-permute-done((bf16[1024,128]{1,0:T(8,128)(2,1)S(1)}, bf16[1024,128]{1,0:T(8,128)(2,1)S(1)}, u32[]{:S(2)}, u32[]{:S(2)}) %collective-permute-start.34) | collective-permute-done | bytes 262176 | tf_op jit(solution)/shard_map/ppermute | solution.py:267
  148.8 4.7 %collective-permute-done.35 = bf16[1024,128]{1,0:T(8,128)(2,1)S(1)} collective-permute-done((bf16[1024,128]{1,0:T(8,128)(2,1)S(1)}, bf16[1024,128]{1,0:T(8,128)(2,1)S(1)}, u32[]{:S(2)}, u32[]{:S(2)}) %collective-permute-start.35) | collective-permute-done | bytes 262176 | tf_op jit(solution)/shard_map/ppermute | solution.py:268
  153.5 2.1 %fusion.6 = (bf16[1024,128]{1,0:T(8,128)(2,1)S(1)}, bf16[1024,128]{1,0:T(8,128)(2,1)}, bf16[1024,128]{1,0:T(8,128)(2,1)}, bf16[1024,128]{1,0:T(8,128)(2,1)S(1)}) fusion(bf16[1024,128]{1,0:T(8,128)(2,1)S(1)} %collective-permute-done.35, bf16[4,2048,128]{2,1,0:T(8,128)(2,1)S(1)} %get-tuple-element.31, s32[]{:T(128)S(6)} %min.35, ...), kind=kLoop, calls=%fused_computation.13 | loop fusion | flops 2097152 | bytes 3145744 | tf_op jit(solution)/shard_map/convert_element_type | solution.py:268
  155.6 4.3 %collective-permute-start.40 = (bf16[1024,128]{1,0:T(8,128)(2,1)}, bf16[1024,128]{1,0:T(8,128)(2,1)S(1)}, u32[]{:S(2)}, u32[]{:S(2)}) collective-permute-start(bf16[1024,128]{1,0:T(8,128)(2,1)} %get-tuple-element.57), channel_id=1, source_target_pairs={{0,2},{1,3},{2,4},{3,5},{4,6},{5,7},{8,10},{9,11},{10,12},{11,13},... | collective-permute-start | bytes 786440 | tf_op jit(solution)/shard_map/ppermute | solution.py:267
  161.2 5.3 %collective-permute-start.36 = (bf16[1024,128]{1,0:T(8,128)(2,1)S(1)}, bf16[1024,128]{1,0:T(8,128)(2,1)}, u32[]{:S(2)}, u32[]{:S(2)}) collective-permute-start(bf16[1024,128]{1,0:T(8,128)(2,1)S(1)} %get-tuple-element.58), channel_id=1, source_target_pairs={{0,2},{1,3},{2,4},{3,5},{4,6},{5,7},{8,10},{9,11},{10,12},{11,13},... | collective-permute-start | bytes 786440 | tf_op jit(solution)/shard_map/ppermute | solution.py:267
  168.4 2.7 %collective-permute-done.36 = bf16[1024,128]{1,0:T(8,128)(2,1)} collective-permute-done((bf16[1024,128]{1,0:T(8,128)(2,1)S(1)}, bf16[1024,128]{1,0:T(8,128)(2,1)}, u32[]{:S(2)}, u32[]{:S(2)}) %collective-permute-start.36) | collective-permute-done | bytes 262176 | tf_op jit(solution)/shard_map/ppermute | solution.py:267
  171.0 4.0 %collective-permute-done.37 = bf16[1024,128]{1,0:T(8,128)(2,1)} collective-permute-done((bf16[1024,128]{1,0:T(8,128)(2,1)S(1)}, bf16[1024,128]{1,0:T(8,128)(2,1)}, u32[]{:S(2)}, u32[]{:S(2)}) %collective-permute-start.37) | collective-permute-done | bytes 262176 | tf_op jit(solution)/shard_map/ppermute | solution.py:268
  175.1 2.0 %fusion.11 = (bf16[1024,128]{1,0:T(8,128)(2,1)S(1)}, bf16[1024,128]{1,0:T(8,128)(2,1)S(1)}, bf16[1024,128]{1,0:T(8,128)(2,1)}) fusion(bf16[1024,128]{1,0:T(8,128)(2,1)} %collective-permute-done.37, bf16[1024,128]{1,0:T(8,128)(2,1)} %collective-permute-done.36, bf16[4,2048,128]{2,1,0:T(8,128)(2,1)S(1)} %get-tuple-element.31, s32[]{:T(128)S(6)} %min.29, ...), kind=kLoop, calls=%fused_computation.22 | loop fusion | flops 1835008 | bytes 2621452 | tf_op jit(solution)/shard_map/convert_element_type | solution.py:271
  177.0 2.2 %collective-permute-start.42 = (bf16[1024,128]{1,0:T(8,128)(2,1)}, bf16[1024,128]{1,0:T(8,128)(2,1)S(1)}, u32[]{:S(2)}, u32[]{:S(2)}) collective-permute-start(bf16[1024,128]{1,0:T(8,128)(2,1)} %get-tuple-element.54), channel_id=1, source_target_pairs={{0,2},{1,3},{2,4},{3,5},{4,6},{5,7},{8,10},{9,11},{10,12},{11,13},... | collective-permute-start | bytes 786440 | tf_op jit(solution)/shard_map/ppermute | solution.py:267
  181.2 2.3 %collective-permute-done.42 = bf16[1024,128]{1,0:T(8,128)(2,1)S(1)} collective-permute-done((bf16[1024,128]{1,0:T(8,128)(2,1)}, bf16[1024,128]{1,0:T(8,128)(2,1)S(1)}, u32[]{:S(2)}, u32[]{:S(2)}) %collective-permute-start.42) | collective-permute-done | bytes 262176 | tf_op jit(solution)/shard_map/ppermute | solution.py:267
  183.4 4.1 %collective-permute-done.43 = bf16[1024,128]{1,0:T(8,128)(2,1)S(1)} collective-permute-done((bf16[1024,128]{1,0:T(8,128)(2,1)S(1)}, bf16[1024,128]{1,0:T(8,128)(2,1)S(1)}, u32[]{:S(2)}, u32[]{:S(2)}) %collective-permute-start.43) | collective-permute-done | bytes 262176 | tf_op jit(solution)/shard_map/ppermute | solution.py:268
  (91 shorter events, 30.7 us)
Async XLA Ops:
  1.7 16.8 %collective-permute-start.2 = (bf16[512,256]{1,0:T(8,128)(2,1)S(1)}, bf16[512,256]{1,0:T(8,128)(2,1)S(1)}, u32[]{:S(2)}, u32[]{:S(2)}) collective-permute-start(bf16[512,256]{1,0:T(8,128)(2,1)S(1)} %get-tuple-element.65), channel_id=1, source_target_pairs={{0,8},{8,0},{16,24},{24,16},{1,9},{9,1},{17,25},{25,17},{2,10},{10... | collective-permute-start | bytes 786440 | tf_op jit(solution)/shard_map/ppermute | solution.py:21
  4.7 15.4 %collective-permute-start.4 = (bf16[512,256]{1,0:T(8,128)(2,1)S(1)}, bf16[512,256]{1,0:T(8,128)(2,1)S(1)}, u32[]{:S(2)}, u32[]{:S(2)}) collective-permute-start(bf16[512,256]{1,0:T(8,128)(2,1)S(1)} %get-tuple-element.65), channel_id=1, source_target_pairs={{0,16},{8,24},{16,0},{24,8},{1,17},{9,25},{17,1},{25,9},{2,18},{10... | collective-permute-start | bytes 786440 | tf_op jit(solution)/shard_map/ppermute | solution.py:21
  6.2 11.9 %collective-permute-start.3 = (bf16[512,256]{1,0:T(8,128)(2,1)S(1)}, bf16[512,256]{1,0:T(8,128)(2,1)S(1)}, u32[]{:S(2)}, u32[]{:S(2)}) collective-permute-start(bf16[512,256]{1,0:T(8,128)(2,1)S(1)} %get-tuple-element.66), channel_id=1, source_target_pairs={{0,16},{8,24},{16,0},{24,8},{1,17},{9,25},{17,1},{25,9},{2,18},{10... | collective-permute-start | bytes 786440 | tf_op jit(solution)/shard_map/ppermute | solution.py:21
  6.7 13.8 %collective-permute-start.1 = (bf16[512,256]{1,0:T(8,128)(2,1)S(1)}, bf16[512,256]{1,0:T(8,128)(2,1)S(1)}, u32[]{:S(2)}, u32[]{:S(2)}) collective-permute-start(bf16[512,256]{1,0:T(8,128)(2,1)S(1)} %get-tuple-element.66), channel_id=1, source_target_pairs={{0,8},{8,0},{16,24},{24,16},{1,9},{9,1},{17,25},{25,17},{2,10},{10... | collective-permute-start | bytes 786440 | tf_op jit(solution)/shard_map/ppermute | solution.py:21
  7.6 1.2 collective-permute-start
  18.1 6.9 %collective-permute-start.5 = (bf16[512,256]{1,0:T(8,128)(2,1)S(1)}, bf16[512,256]{1,0:T(8,128)(2,1)S(1)}, u32[]{:S(2)}, u32[]{:S(2)}) collective-permute-start(bf16[512,256]{1,0:T(8,128)(2,1)S(1)} %collective-permute-done.3.refs_4_), channel_id=1, source_target_pairs={{0,8},{8,0},{16,24},{24,16},{1,9},{9,1},{17,25},{25,17},{2,10},{10... | collective-permute-start | bytes 786440 | tf_op jit(solution)/shard_map/ppermute | solution.py:21
  18.4 8.7 %collective-permute-start.10 = (bf16[512,256]{1,0:T(8,128)(2,1)S(1)}, bf16[512,256]{1,0:T(8,128)(2,1)S(1)}, u32[]{:S(2)}, u32[]{:S(2)}) collective-permute-start(bf16[512,256]{1,0:T(8,128)(2,1)S(1)} %collective-permute-done.3.refs_4_), channel_id=1, source_target_pairs={{0,1},{1,0},{2,3},{3,2},{4,5},{5,4},{6,7},{7,6},{8,9},{9,8},{10,11... | collective-permute-start | bytes 786440 | tf_op jit(solution)/shard_map/ppermute | solution.py:21
  18.5 8.7 %collective-permute-start.6 = (bf16[512,256]{1,0:T(8,128)(2,1)S(1)}, bf16[512,256]{1,0:T(8,128)(2,1)S(1)}, u32[]{:S(2)}, u32[]{:S(2)}) collective-permute-start(bf16[512,256]{1,0:T(8,128)(2,1)S(1)} %collective-permute-done.2.refs_3_), channel_id=1, source_target_pairs={{0,16},{8,24},{16,0},{24,8},{1,17},{9,25},{17,1},{25,9},{2,18},{10... | collective-permute-start | bytes 786440 | tf_op jit(solution)/shard_map/ppermute | solution.py:21
  20.2 7.5 %collective-permute-start.9 = (bf16[512,256]{1,0:T(8,128)(2,1)S(1)}, bf16[512,256]{1,0:T(8,128)(2,1)S(1)}, u32[]{:S(2)}, u32[]{:S(2)}) collective-permute-start(bf16[512,256]{1,0:T(8,128)(2,1)S(1)} %collective-permute-done.2.refs_3_), channel_id=1, source_target_pairs={{0,1},{1,0},{2,3},{3,2},{4,5},{5,4},{6,7},{7,6},{8,9},{9,8},{10,11... | collective-permute-start | bytes 786440 | tf_op jit(solution)/shard_map/ppermute | solution.py:21
  20.5 8.2 %collective-permute-start.7 = (bf16[1024,256]{1,0:T(8,128)(2,1)}, bf16[1024,256]{1,0:T(8,128)(2,1)S(1)}, u32[]{:S(2)}, u32[]{:S(2)}) collective-permute-start(bf16[1024,256]{1,0:T(8,128)(2,1)} %refs_1_.1), channel_id=1, source_target_pairs={{0,1},{1,0},{2,3},{3,2},{4,5},{5,4},{6,7},{7,6},{8,9},{9,8},{10,11... | collective-permute-start | bytes 1572872 | tf_op jit(solution)/shard_map/ppermute | solution.py:21
  24.9 2.8 %collective-permute-start.11 = (bf16[512,256]{1,0:T(8,128)(2,1)S(1)}, bf16[512,256]{1,0:T(8,128)(2,1)S(1)}, u32[]{:S(2)}, u32[]{:S(2)}) collective-permute-start(bf16[512,256]{1,0:T(8,128)(2,1)S(1)} %collective-permute-done.4.refs_5_), channel_id=1, source_target_pairs={{0,1},{1,0},{2,3},{3,2},{4,5},{5,4},{6,7},{7,6},{8,9},{9,8},{10,11... | collective-permute-start | bytes 786440 | tf_op jit(solution)/shard_map/ppermute | solution.py:21
  27.2 1.5 collective-permute-start.8
  27.2 1.9 %collective-permute-start.12 = (bf16[512,256]{1,0:T(8,128)(2,1)S(1)}, bf16[512,256]{1,0:T(8,128)(2,1)S(1)}, u32[]{:S(2)}, u32[]{:S(2)}) collective-permute-start(bf16[512,256]{1,0:T(8,128)(2,1)S(1)} %collective-permute-done.5.refs_6_), channel_id=1, source_target_pairs={{0,1},{1,0},{2,3},{3,2},{4,5},{5,4},{6,7},{7,6},{8,9},{9,8},{10,11... | collective-permute-start | bytes 786440 | tf_op jit(solution)/shard_map/ppermute | solution.py:21
  27.7 1.8 collective-permute-start.13
  29.5 2.2 %copy-start.4 = (bf16[2048,1024]{1,0:T(8,128)(2,1)S(1)}, bf16[2048,1024]{1,0:T(8,128)(2,1)}, u32[]{:S(2)}) copy-start(bf16[2048,1024]{1,0:T(8,128)(2,1)} %refs_0_.1) | copy-start | bytes 12582916
  43.4 60.5 %copy-start = (f32[257,128,128]{2,1,0:T(8,128)}, f32[257,128,128]{2,1,0:T(8,128)S(1)}, u32[]{:S(2)}) copy-start(f32[257,128,128]{2,1,0:T(8,128)S(1)} %get-tuple-element.24.s_ref) | copy-start | bytes 50528260
  43.4 4.9 %collective-permute-start.14 = (f32[16,128]{1,0:T(8,128)S(1)}, f32[16,128]{1,0:T(8,128)S(1)}, u32[]{:S(2)}, u32[]{:S(2)}) collective-permute-start(f32[16,128]{1,0:T(8,128)S(1)} %get-tuple-element.25.refs_0_), channel_id=1, source_target_pairs={{0,2},{1,3},{2,0},{3,1},{4,6},{5,7},{6,4},{7,5},{8,10},{9,11},{10,... | collective-permute-start | bytes 24584 | tf_op jit(solution)/shard_map/ppermute | solution.py:21
  45.8 4.6 %collective-permute-start.15 = (f32[16,128]{1,0:T(8,128)S(1)}, f32[16,128]{1,0:T(8,128)S(1)}, u32[]{:S(2)}, u32[]{:S(2)}) collective-permute-start(f32[16,128]{1,0:T(8,128)S(1)} %get-tuple-element.25.refs_0_), channel_id=1, source_target_pairs={{0,4},{1,5},{2,6},{3,7},{4,0},{5,1},{6,2},{7,3},{8,12},{9,13},{10,... | collective-permute-start | bytes 24584 | tf_op jit(solution)/shard_map/ppermute | solution.py:21
  48.2 5.4 %collective-permute-start.16 = (f32[16,128]{1,0:T(8,128)S(1)}, f32[16,128]{1,0:T(8,128)S(1)}, u32[]{:S(2)}, u32[]{:S(2)}) collective-permute-start(f32[16,128]{1,0:T(8,128)S(1)} %get-tuple-element.25.refs_0_), channel_id=1, source_target_pairs={{0,6},{1,7},{2,4},{3,5},{4,2},{5,3},{6,0},{7,1},{8,14},{9,15},{10,... | collective-permute-start | bytes 24584 | tf_op jit(solution)/shard_map/ppermute | solution.py:21
  57.2 9.4 %collective-permute-start.17 = (f32[16,128]{1,0:T(8,128)S(1)}, f32[16,128]{1,0:T(8,128)S(1)}, u32[]{:S(2)}, u32[]{:S(2)}) collective-permute-start(f32[16,128]{1,0:T(8,128)S(1)} %get-tuple-element.26.refs_0_), channel_id=1, source_target_pairs={{0,8},{8,0},{16,24},{24,16},{1,9},{9,1},{17,25},{25,17},{2,10},{10... | collective-permute-start | bytes 24584 | tf_op jit(solution)/shard_map/ppermute | solution.py:21
  60.6 7.5 %collective-permute-start.18 = (f32[16,128]{1,0:T(8,128)S(1)}, f32[16,128]{1,0:T(8,128)S(1)}, u32[]{:S(2)}, u32[]{:S(2)}) collective-permute-start(f32[16,128]{1,0:T(8,128)S(1)} %get-tuple-element.26.refs_0_), channel_id=1, source_target_pairs={{0,16},{8,24},{16,0},{24,8},{1,17},{9,25},{17,1},{25,9},{2,18},{10... | collective-permute-start | bytes 24584 | tf_op jit(solution)/shard_map/ppermute | solution.py:21
  66.5 4.5 %collective-permute-start.19 = (f32[16,128]{1,0:T(8,128)S(1)}, f32[16,128]{1,0:T(8,128)S(1)}, u32[]{:S(2)}, u32[]{:S(2)}) collective-permute-start(f32[16,128]{1,0:T(8,128)S(1)} %get-tuple-element.26.refs_0_), channel_id=1, source_target_pairs={{0,24},{8,16},{16,8},{24,0},{1,25},{9,17},{17,9},{25,1},{2,26},{10... | collective-permute-start | bytes 24584 | tf_op jit(solution)/shard_map/ppermute | solution.py:21
  73.9 4.4 %collective-permute-start.20 = (f32[16,128]{1,0:T(8,128)S(1)}, f32[16,128]{1,0:T(8,128)S(1)}, u32[]{:S(2)}, u32[]{:S(2)}) collective-permute-start(f32[16,128]{1,0:T(8,128)S(1)} %row_pass.2.refs_0_), channel_id=1, source_target_pairs={{0,2},{1,3},{2,0},{3,1},{4,6},{5,7},{6,4},{7,5},{8,10},{9,11},{10,... | collective-permute-start | bytes 24584 | tf_op jit(solution)/shard_map/ppermute | solution.py:21
  74.0 4.6 %collective-permute-start.21 = (f32[16,128]{1,0:T(8,128)S(1)}, f32[16,128]{1,0:T(8,128)S(1)}, u32[]{:S(2)}, u32[]{:S(2)}) collective-permute-start(f32[16,128]{1,0:T(8,128)S(1)} %row_pass.2.refs_0_), channel_id=1, source_target_pairs={{0,4},{1,5},{2,6},{3,7},{4,0},{5,1},{6,2},{7,3},{8,12},{9,13},{10,... | collective-permute-start | bytes 24584 | tf_op jit(solution)/shard_map/ppermute | solution.py:21
  74.7 5.4 %collective-permute-start.22 = (f32[16,128]{1,0:T(8,128)S(1)}, f32[16,128]{1,0:T(8,128)S(1)}, u32[]{:S(2)}, u32[]{:S(2)}) collective-permute-start(f32[16,128]{1,0:T(8,128)S(1)} %row_pass.2.refs_0_), channel_id=1, source_target_pairs={{0,6},{1,7},{2,4},{3,5},{4,2},{5,3},{6,0},{7,1},{8,14},{9,15},{10,... | collective-permute-start | bytes 24584 | tf_op jit(solution)/shard_map/ppermute | solution.py:21
  83.7 3.7 %collective-permute-start.23 = (f32[16,128]{1,0:T(8,128)S(1)}, f32[16,128]{1,0:T(8,128)S(1)}, u32[]{:S(2)}, u32[]{:S(2)}) collective-permute-start(f32[16,128]{1,0:T(8,128)S(1)} %get-tuple-element.27.refs_0_), channel_id=1, source_target_pairs={{0,8},{8,0},{16,24},{24,16},{1,9},{9,1},{17,25},{25,17},{2,10},{10... | collective-permute-start | bytes 24584 | tf_op jit(solution)/shard_map/ppermute | solution.py:21
  84.3 3.8 %collective-permute-start.24 = (f32[16,128]{1,0:T(8,128)S(1)}, f32[16,128]{1,0:T(8,128)S(1)}, u32[]{:S(2)}, u32[]{:S(2)}) collective-permute-start(f32[16,128]{1,0:T(8,128)S(1)} %get-tuple-element.27.refs_0_), channel_id=1, source_target_pairs={{0,16},{8,24},{16,0},{24,8},{1,17},{9,25},{17,1},{25,9},{2,18},{10... | collective-permute-start | bytes 24584 | tf_op jit(solution)/shard_map/ppermute | solution.py:21
  86.4 4.5 %collective-permute-start.25 = (f32[16,128]{1,0:T(8,128)S(1)}, f32[16,128]{1,0:T(8,128)S(1)}, u32[]{:S(2)}, u32[]{:S(2)}) collective-permute-start(f32[16,128]{1,0:T(8,128)S(1)} %get-tuple-element.27.refs_0_), channel_id=1, source_target_pairs={{0,24},{8,16},{16,8},{24,0},{1,25},{9,17},{17,9},{25,1},{2,26},{10... | collective-permute-start | bytes 24584 | tf_op jit(solution)/shard_map/ppermute | solution.py:21
  94.0 4.4 %collective-permute-start.26 = (f32[16,128]{1,0:T(8,128)S(1)}, f32[16,128]{1,0:T(8,128)S(1)}, u32[]{:S(2)}, u32[]{:S(2)}) collective-permute-start(f32[16,128]{1,0:T(8,128)S(1)} %row_pass.3.refs_0_), channel_id=1, source_target_pairs={{0,2},{1,3},{2,0},{3,1},{4,6},{5,7},{6,4},{7,5},{8,10},{9,11},{10,... | collective-permute-start | bytes 24584 | tf_op jit(solution)/shard_map/ppermute | solution.py:21
  94.9 5.2 %collective-permute-start.27 = (f32[16,128]{1,0:T(8,128)S(1)}, f32[16,128]{1,0:T(8,128)S(1)}, u32[]{:S(2)}, u32[]{:S(2)}) collective-permute-start(f32[16,128]{1,0:T(8,128)S(1)} %row_pass.3.refs_0_), channel_id=1, source_target_pairs={{0,4},{1,5},{2,6},{3,7},{4,0},{5,1},{6,2},{7,3},{8,12},{9,13},{10,... | collective-permute-start | bytes 24584 | tf_op jit(solution)/shard_map/ppermute | solution.py:21
  98.4 5.4 %collective-permute-start.28 = (f32[16,128]{1,0:T(8,128)S(1)}, f32[16,128]{1,0:T(8,128)S(1)}, u32[]{:S(2)}, u32[]{:S(2)}) collective-permute-start(f32[16,128]{1,0:T(8,128)S(1)} %row_pass.3.refs_0_), channel_id=1, source_target_pairs={{0,6},{1,7},{2,4},{3,5},{4,2},{5,3},{6,0},{7,1},{8,14},{9,15},{10,... | collective-permute-start | bytes 24584 | tf_op jit(solution)/shard_map/ppermute | solution.py:21
  107.3 3.7 %collective-permute-start.29 = (f32[16,128]{1,0:T(8,128)S(1)}, f32[16,128]{1,0:T(8,128)S(1)}, u32[]{:S(2)}, u32[]{:S(2)}) collective-permute-start(f32[16,128]{1,0:T(8,128)S(1)} %get-tuple-element.30.refs_0_), channel_id=1, source_target_pairs={{0,8},{8,0},{16,24},{24,16},{1,9},{9,1},{17,25},{25,17},{2,10},{10... | collective-permute-start | bytes 24584 | tf_op jit(solution)/shard_map/ppermute | solution.py:21
  108.5 3.8 %collective-permute-start.30 = (f32[16,128]{1,0:T(8,128)S(1)}, f32[16,128]{1,0:T(8,128)S(1)}, u32[]{:S(2)}, u32[]{:S(2)}) collective-permute-start(f32[16,128]{1,0:T(8,128)S(1)} %get-tuple-element.30.refs_0_), channel_id=1, source_target_pairs={{0,16},{8,24},{16,0},{24,8},{1,17},{9,25},{17,1},{25,9},{2,18},{10... | collective-permute-start | bytes 24584 | tf_op jit(solution)/shard_map/ppermute | solution.py:21
  110.7 4.5 %collective-permute-start.31 = (f32[16,128]{1,0:T(8,128)S(1)}, f32[16,128]{1,0:T(8,128)S(1)}, u32[]{:S(2)}, u32[]{:S(2)}) collective-permute-start(f32[16,128]{1,0:T(8,128)S(1)} %get-tuple-element.30.refs_0_), channel_id=1, source_target_pairs={{0,24},{8,16},{16,8},{24,0},{1,25},{9,17},{17,9},{25,1},{2,26},{10... | collective-permute-start | bytes 24584 | tf_op jit(solution)/shard_map/ppermute | solution.py:21
  115.3 5.8 %copy-start.1 = (f32[257,128,128]{2,1,0:T(8,128)S(1)}, f32[257,128,128]{2,1,0:T(8,128)}, u32[]{:S(2)}) copy-start(f32[257,128,128]{2,1,0:T(8,128)} %copy-done) | copy-start | bytes 50528260
  121.1 2.2 %copy-start.3 = (bf16[2048,1024]{1,0:T(8,128)(2,1)S(1)}, bf16[2048,1024]{1,0:T(8,128)(2,1)}, u32[]{:S(2)}) copy-start(bf16[2048,1024]{1,0:T(8,128)(2,1)} %copy-done.2) | copy-start | bytes 12582916
  130.5 9.2 %collective-permute-start.32 = (bf16[1024,128]{1,0:T(8,128)(2,1)S(1)}, bf16[1024,128]{1,0:T(8,128)(2,1)S(1)}, u32[]{:S(2)}, u32[]{:S(2)}) collective-permute-start(bf16[1024,128]{1,0:T(8,128)(2,1)S(1)} %get-tuple-element.64), channel_id=1, source_target_pairs={{0,2},{1,3},{2,4},{3,5},{4,6},{5,7},{8,10},{9,11},{10,12},{11,13},... | collective-permute-start | bytes 786440 | tf_op jit(solution)/shard_map/ppermute | solution.py:267
  131.8 10.7 %collective-permute-start.33 = (bf16[1024,128]{1,0:T(8,128)(2,1)S(1)}, bf16[1024,128]{1,0:T(8,128)(2,1)S(1)}, u32[]{:S(2)}, u32[]{:S(2)}) collective-permute-start(bf16[1024,128]{1,0:T(8,128)(2,1)S(1)} %get-tuple-element.61), channel_id=1, source_target_pairs={{2,0},{3,1},{4,2},{5,3},{6,4},{7,5},{10,8},{11,9},{12,10},{13,11},... | collective-permute-start | bytes 786440 | tf_op jit(solution)/shard_map/ppermute | solution.py:268
  133.1 12.6 %collective-permute-start.38 = (bf16[1024,128]{1,0:T(8,128)(2,1)}, bf16[1024,128]{1,0:T(8,128)(2,1)}, u32[]{:S(2)}, u32[]{:S(2)}) collective-permute-start(bf16[1024,128]{1,0:T(8,128)(2,1)} %get-tuple-element.63), channel_id=1, source_target_pairs={{0,2},{1,3},{2,4},{3,5},{4,6},{5,7},{8,10},{9,11},{10,12},{11,13},... | collective-permute-start | bytes 786440 | tf_op jit(solution)/shard_map/ppermute | solution.py:267
  138.4 8.4 %collective-permute-start.39 = (bf16[1024,128]{1,0:T(8,128)(2,1)S(1)}, bf16[1024,128]{1,0:T(8,128)(2,1)}, u32[]{:S(2)}, u32[]{:S(2)}) collective-permute-start(bf16[1024,128]{1,0:T(8,128)(2,1)S(1)} %get-tuple-element.62), channel_id=1, source_target_pairs={{2,0},{3,1},{4,2},{5,3},{6,4},{7,5},{10,8},{11,9},{12,10},{13,11},... | collective-permute-start | bytes 786440 | tf_op jit(solution)/shard_map/ppermute | solution.py:268
  142.7 6.1 %collective-permute-start.34 = (bf16[1024,128]{1,0:T(8,128)(2,1)S(1)}, bf16[1024,128]{1,0:T(8,128)(2,1)S(1)}, u32[]{:S(2)}, u32[]{:S(2)}) collective-permute-start(bf16[1024,128]{1,0:T(8,128)(2,1)S(1)} %get-tuple-element.60), channel_id=1, source_target_pairs={{0,2},{1,3},{2,4},{3,5},{4,6},{5,7},{8,10},{9,11},{10,12},{11,13},... | collective-permute-start | bytes 786440 | tf_op jit(solution)/shard_map/ppermute | solution.py:267
  144.4 9.1 %collective-permute-start.35 = (bf16[1024,128]{1,0:T(8,128)(2,1)S(1)}, bf16[1024,128]{1,0:T(8,128)(2,1)S(1)}, u32[]{:S(2)}, u32[]{:S(2)}) collective-permute-start(bf16[1024,128]{1,0:T(8,128)(2,1)S(1)} %get-tuple-element.59), channel_id=1, source_target_pairs={{2,0},{3,1},{4,2},{5,3},{6,4},{7,5},{10,8},{11,9},{12,10},{13,11},... | collective-permute-start | bytes 786440 | tf_op jit(solution)/shard_map/ppermute | solution.py:268
  155.6 12.2 %collective-permute-start.40 = (bf16[1024,128]{1,0:T(8,128)(2,1)}, bf16[1024,128]{1,0:T(8,128)(2,1)S(1)}, u32[]{:S(2)}, u32[]{:S(2)}) collective-permute-start(bf16[1024,128]{1,0:T(8,128)(2,1)} %get-tuple-element.57), channel_id=1, source_target_pairs={{0,2},{1,3},{2,4},{3,5},{4,6},{5,7},{8,10},{9,11},{10,12},{11,13},... | collective-permute-start | bytes 786440 | tf_op jit(solution)/shard_map/ppermute | solution.py:267
  159.9 8.5 %collective-permute-start.41 = (bf16[1024,128]{1,0:T(8,128)(2,1)}, bf16[1024,128]{1,0:T(8,128)(2,1)S(1)}, u32[]{:S(2)}, u32[]{:S(2)}) collective-permute-start(bf16[1024,128]{1,0:T(8,128)(2,1)} %get-tuple-element.56), channel_id=1, source_target_pairs={{2,0},{3,1},{4,2},{5,3},{6,4},{7,5},{10,8},{11,9},{12,10},{13,11},... | collective-permute-start | bytes 786440 | tf_op jit(solution)/shard_map/ppermute | solution.py:268
  161.2 9.8 %collective-permute-start.36 = (bf16[1024,128]{1,0:T(8,128)(2,1)S(1)}, bf16[1024,128]{1,0:T(8,128)(2,1)}, u32[]{:S(2)}, u32[]{:S(2)}) collective-permute-start(bf16[1024,128]{1,0:T(8,128)(2,1)S(1)} %get-tuple-element.58), channel_id=1, source_target_pairs={{0,2},{1,3},{2,4},{3,5},{4,6},{5,7},{8,10},{9,11},{10,12},{11,13},... | collective-permute-start | bytes 786440 | tf_op jit(solution)/shard_map/ppermute | solution.py:267
  166.4 8.6 %collective-permute-start.37 = (bf16[1024,128]{1,0:T(8,128)(2,1)S(1)}, bf16[1024,128]{1,0:T(8,128)(2,1)}, u32[]{:S(2)}, u32[]{:S(2)}) collective-permute-start(bf16[1024,128]{1,0:T(8,128)(2,1)S(1)} %get-tuple-element.55), channel_id=1, source_target_pairs={{2,0},{3,1},{4,2},{5,3},{6,4},{7,5},{10,8},{11,9},{12,10},{13,11},... | collective-permute-start | bytes 786440 | tf_op jit(solution)/shard_map/ppermute | solution.py:268
  177.0 6.4 %collective-permute-start.42 = (bf16[1024,128]{1,0:T(8,128)(2,1)}, bf16[1024,128]{1,0:T(8,128)(2,1)S(1)}, u32[]{:S(2)}, u32[]{:S(2)}) collective-permute-start(bf16[1024,128]{1,0:T(8,128)(2,1)} %get-tuple-element.54), channel_id=1, source_target_pairs={{0,2},{1,3},{2,4},{3,5},{4,6},{5,7},{8,10},{9,11},{10,12},{11,13},... | collective-permute-start | bytes 786440 | tf_op jit(solution)/shard_map/ppermute | solution.py:267
  179.2 8.3 %collective-permute-start.43 = (bf16[1024,128]{1,0:T(8,128)(2,1)S(1)}, bf16[1024,128]{1,0:T(8,128)(2,1)S(1)}, u32[]{:S(2)}, u32[]{:S(2)}) collective-permute-start(bf16[1024,128]{1,0:T(8,128)(2,1)S(1)} %get-tuple-element.53), channel_id=1, source_target_pairs={{2,0},{3,1},{4,2},{5,3},{6,4},{7,5},{10,8},{11,9},{12,10},{13,11},... | collective-permute-start | bytes 786440 | tf_op jit(solution)/shard_map/ppermute | solution.py:268
  (3 other events, 3.7 us)

commit v5 on v4

--- a/solution.py
+++ b/solution.py
@@ -13,6 +13,7 @@
 NEGATIVE = -1e30
 
 VMEM = pl.BlockSpec(memory_space=pltpu.VMEM)
+HBM = pl.BlockSpec(memory_space=pltpu.HBM)
 SMEM = pl.BlockSpec(memory_space=pltpu.SMEM)
 
 
@@ -87,20 +88,28 @@
         wide_ref[t] = jnp.broadcast_to(standing[:, t : t + 1], (TILE, TILE))
 
 
-def panel_kernel(row_blocks, list_ref, half_ref, plist_ref, pquarter_ref, offset_ref, *refs):
-    e_ref, (s_ref, p_ref, out_ref, acc_ref) = refs[0], refs[-4:]
-    pieces = refs[1:-4]
+def panel_kernel(row_blocks, list_ref, half_ref, plist_ref, pquarter_ref, place_ref, e_hbm_ref, *refs):
+    pieces, (s_ref, p_ref, out_ref, acc_ref, e_ref, sem) = refs[:-6], refs[-6:]
+    load = pltpu.make_async_copy(e_hbm_ref, e_ref, sem.at[0])
+    load.start()
     row_tiles, columns = list_ref.shape
     scale = 4.0 / math.sqrt(e_ref.shape[1])
-    core = offset_ref[0]
+    core = place_ref[0]
     protos = p_ref.shape[0] // 2
     for n, piece in enumerate(pieces):
         group, within = n * 2 // len(pieces), n % (len(pieces) // 2)
         rows, width = piece.shape
         first = (core if group == 0 else 1 - core) * protos + row_blocks[within]
-        start = pl.multiple_of(offset_ref[1 + within], TILE)
-        p_ref[pl.ds(pl.multiple_of(first, TILE), rows), pl.ds(start, width)] = piece[...]
+        start = pl.multiple_of(place_ref[2 + within], TILE)
+        place = p_ref.at[pl.ds(pl.multiple_of(first, TILE), rows), pl.ds(start, width)]
+        if n == 0:
+            own = pltpu.make_async_copy(piece, place, sem.at[1])
+            own.start()
+        else:
+            place[...] = piece[...]
     s_ref[row_tiles * columns] = jnp.full((TILE, TILE), NEGATIVE, jnp.float32)
+    own.wait()
+    load.wait()
 
     def one_pair(pair, carry):
         def four_tiles(k, carry):
@@ -163,29 +172,30 @@
     out_ref[...] = jnp.concatenate(peaks, axis=0) + jnp.log(jnp.concatenate(totals, axis=0))
 
 
-def plan_kernel(log_column, lines, plist_ref, pquarter_ref, mask_ref, offset_ref, s_ref, r_ref, p_ref, *refs):
-    parts, (out_ref, c_ref, wide_ref, total_ref) = refs[:-4], refs[-4:]
+def plan_kernel(log_column, lines, plist_ref, pquarter_ref, mask_ref, place_ref, s_ref, r_ref, p_ref, *refs):
+    parts, outs = refs[: -4 - lines], refs[-4 - lines : -4]
+    own_ref, c_ref, wide_ref, total_ref = refs[-4:]
     row_tiles, columns = mask_ref.shape
     dummy = row_tiles * columns
+    core, z = place_ref[0], place_ref[1]
     c_ref[...] = log_column - combine([part[...] for part in parts])
+    half = columns // 2
+    own_ref[...] = c_ref[pl.ds(pl.multiple_of(core * half, half), half), :]
     spread_rows(r_ref[...], wide_ref)
-    width = out_ref.shape[2]
-    core = offset_ref[0]
+    width = outs[0].shape[1]
+    fits = width % TILE == 0
     total_ref[...] = jnp.zeros(total_ref.shape, jnp.float32)
 
     def one_pair(pair, carry):
         first = pl.multiple_of(pair * 2 * TILE, TILE)
-        if width % TILE:
-            wide = p_ref[pl.ds(first, 2 * TILE), :]
-            blocks = [
-                jnp.where(core == 0, wide[:, z * 2 * width :][:, :width], wide[:, (z * 2 + 1) * width :][:, :width])
-                for z in range(lines)
-            ]
-        else:
-            blocks = [
-                p_ref[pl.ds(first, 2 * TILE), pl.ds(pl.multiple_of((2 * z + core) * width, TILE), width)]
-                for z in range(lines)
-            ]
+        blocks = []
+        for j in range(lines):
+            if fits:
+                start = (2 * jnp.bitwise_xor(z, j) + core) * width
+                blocks.append(p_ref[pl.ds(first, 2 * TILE), pl.ds(pl.multiple_of(start, TILE), width)])
+            else:
+                both = p_ref[pl.ds(first, 2 * TILE), 2 * j * width : 2 * (j + 1) * width]
+                blocks.append(jnp.where(core == 0, both[:, :width], both[:, width:]))
         block = jnp.concatenate(blocks, axis=1)
 
         def four_tiles(k, carry):
@@ -212,8 +222,16 @@
     lax.fori_loop(0, columns // 2, one_pair, 0)
     for t in range(row_tiles):
         total = total_ref[t].astype(jnp.bfloat16)
-        for z in range(lines):
-            out_ref[z, t * TILE : (t + 1) * TILE, :] = total[:, z * width : (z + 1) * width]
+        for j in range(lines):
+            block = total[:, j * width : (j + 1) * width]
+            if fits:
+                outs[j][t * TILE : (t + 1) * TILE, :] = block
+            else:
+                for k in range(lines):
+
+                    @pl.when(jnp.bitwise_xor(z, k) == j)
+                    def _():
+                        outs[k][t * TILE : (t + 1) * TILE, :] = block
 
 
 def params(mebibytes):
@@ -234,42 +252,26 @@
     top, bottom = shard[:half], shard[half:]
     near_bottom = swap(bottom, "row", 1)
     far_top = swap(top, "row", 2)
+    near_bottom, far_top, top, bottom = lax.optimization_barrier((near_bottom, far_top, top, bottom))
+    cross_top = swap(far_top, "row", 1)
+    cross_bottom = swap(near_bottom, "row", 2)
     near_top = swap(top, "row", 1)
     far_bottom = swap(bottom, "row", 2)
-    cross_top = swap(far_top, "row", 1)
-    cross_bottom = swap(near_bottom, "row", 2)
     pieces = [shard, near_top, near_bottom, far_top, far_bottom, cross_top, cross_bottom]
     firsts = [0, 0, half, 0, half, 0, half]
     starts = [(me ^ offset) * width for offset in (0, 1, 1, 2, 2, 3, 3)]
     return pieces + [sibling(piece) for piece in pieces], firsts, starts
 
 
-def scatter_partials(split):
-    size = lax.axis_size("proto")
-    line = size // 2
-    z = lax.axis_index("proto") // 2
-    up = [(i, i + 2) for i in range(size - 2)]
-    down = [(i + 2, i) for i in range(size - 2)]
-    halves = []
-    half = split.shape[1] // 2
-    for part in range(2):
-
-        def chunk(index):
-            index = jnp.clip(index, 0, line - 1)
-            at = lax.dynamic_slice(split, (index, part * half, 0), (1, half, split.shape[2]))
-            return at[0].astype(jnp.float32)
-
-        from_below = from_above = None
-        for step in range(1, line):
-            send_up, send_down = chunk(line - step + z), chunk(z - (line - step))
-            if step > 1:
-                send_up, send_down = send_up + from_below, send_down + from_above
-            from_below = lax.ppermute(send_up.astype(jnp.bfloat16), "proto", up)
-            from_above = lax.ppermute(send_down.astype(jnp.bfloat16), "proto", down)
-            from_below, from_above = lax.optimization_barrier((from_below, from_above))
-            from_below, from_above = from_below.astype(jnp.float32), from_above.astype(jnp.float32)
-        halves.append((chunk(z) + from_below + from_above).astype(jnp.bfloat16))
-    return jnp.concatenate(halves, axis=0)
+def scatter_partials(blocks):
+    blocks = list(blocks)
+    distance = 1
+    while distance < len(blocks):
+        for j in range(len(blocks) - distance, 0, -2 * distance):
+            got = swap(blocks[j].astype(jnp.bfloat16), "proto", 2 * distance).astype(jnp.float32)
+            blocks[j ^ distance] = blocks[j ^ distance].astype(jnp.float32) + got
+        distance *= 2
+    return blocks[0].astype(jnp.bfloat16)
 
 
 def shards(embeddings, prototypes, block_mask):
@@ -298,7 +300,8 @@
     pair_list, pair_count = ordered(jnp.max(across.reshape(columns // 2, 2, row_tiles), axis=1))
     row_half, column_half = (row_count + 1) // 2, (column_count + 1) // 2
     pair_quarter = (pair_count + 3) // 4
-    offsets = jnp.stack([core.astype(jnp.int32)] + [s.astype(jnp.int32) for s in starts])
+    z = lax.axis_index("proto") // 2
+    places = jnp.stack([place.astype(jnp.int32) for place in [core, z] + starts])
 
     row_shape = jax.ShapeDtypeStruct((row_tiles, TILE), jnp.float32)
     column_shape = jax.ShapeDtypeStruct((columns, TILE), jnp.float32)
@@ -308,12 +311,12 @@
     similar, whole, row_part = pl.pallas_call(
         functools.partial(panel_kernel, firsts),
         out_shape=(panel, pltpu.VMEM((protos, features), jnp.bfloat16), row_shape),
-        in_specs=[SMEM] * 5 + [VMEM] * (1 + len(pieces)),
+        in_specs=[SMEM] * 5 + [HBM] * 2 + [VMEM] * (len(pieces) - 1),
         out_specs=(VMEM, VMEM, VMEM),
-        scratch_shapes=[wide],
-        compiler_params=params(12),
+        scratch_shapes=[wide, pltpu.VMEM(embeddings.shape, jnp.bfloat16), pltpu.SemaphoreType.DMA((2,))],
+        compiler_params=params(16),
         name="panel",
-    )(row_list, row_half, pair_list, pair_quarter, offsets, embeddings, *pieces)
+    )(row_list, row_half, pair_list, pair_quarter, places, embeddings, *pieces)
 
     for sweep in range(ITERS):
         parts = [row_part] + [swap(row_part, "proto", 2 * j) for j in range(1, lines)]
@@ -337,18 +340,22 @@
                 compiler_params=params(8),
                 name="row_pass",
             )(row_list, row_half, similar, *parts)
-    split, column_potential = pl.pallas_call(
+    half = columns // 2
+    *blocks, column_potential = pl.pallas_call(
         functools.partial(plan_kernel, log_column, lines),
-        out_shape=(jax.ShapeDtypeStruct((lines, rows, width), jnp.bfloat16), column_shape),
+        out_shape=[jax.ShapeDtypeStruct((rows, width), jnp.bfloat16)] * lines
+        + [jax.ShapeDtypeStruct((half, TILE), jnp.float32)],
         in_specs=[SMEM] * 4 + [VMEM] * (3 + len(parts)),
-        out_specs=(VMEM, VMEM),
-        scratch_shapes=[wide, pltpu.VMEM((row_tiles, TILE, lines * width), jnp.float32)],
+        out_specs=[VMEM] * (lines + 1),
+        scratch_shapes=[
+            pltpu.VMEM((columns, TILE), jnp.float32),
+            wide,
+            pltpu.VMEM((row_tiles, TILE, lines * width), jnp.float32),
+        ],
         compiler_params=params(16),
         name="plan",
-    )(pair_list, pair_quarter, mask, offsets, similar, row_potential, whole, *parts)
-    targets = scatter_partials(split)
-    half = columns // 2
-    column_potential = lax.dynamic_slice_in_dim(column_potential, core * half, half, 0)
+    )(pair_list, pair_quarter, mask, places, similar, row_potential, whole, *parts)
+    targets = scatter_partials(blocks)
     return (targets, row_potential.reshape(rows), column_potential.reshape(protos // 2))
 
 

time: 189 us -> 148 us (0.78); the launches traced: 188 us -> 145 us
  starting transfers between devices: 66.2 us -> 42.8 us
  local copies, waits for them, and re-layouts: 17.3 us -> 5.9 us
  waiting for transfers between devices: 66.1 us -> 61.8 us
  other arithmetic: 7.2 us -> 3.2 us
    ppermute x12 -> x0, starting transfers between devices: 27.8 us -> none  [the longest x6 20 us: scatter_partials(): from_below = lax.ppermute(send_up.astype(jnp.bfloat16), 'proto', up)]
    ppermute x12 -> x0, waiting for transfers between devices: 24.3 us -> none  [the longest x6 17.3 us: scatter_partials(): from_above = lax.ppermute(send_down.astype(jnp.bfloat16), 'proto', down)]
    ppermute x32 -> x35, waiting for transfers between devices: 41.8 us -> 61.8 us  [swap(): return lax.ppermute(x, axis, [(i, i ^ offset) for i in range(size)])]
    unnamed x15 -> x7, local copies, waits for them, and re-layouts: 14.6 us -> 4.69 us
    ppermute x32 -> x35, starting transfers between devices: 38.4 us -> 42.8 us  [swap(): return lax.ppermute(x, axis, [(i, i ^ offset) for i in range(size)])]
    convert_element_type x4 -> x2, other arithmetic: 4.3 us -> 1.14 us  [the longest x1 1 us: scatter_partials(): return blocks[0].astype(jnp.bfloat16)]
  transfers between devices with their start and end apart: 44 -> 35, of which waited for: 30 -> 24; matrix products, arithmetic and copies ran while one was open for 2% -> 2% of each run, Pallas kernels for 0% -> 0%
where the time goes in v5:
time: 148 us; the launch traced here: 145 us
  waiting for transfers between devices  61.8 us (42%)
  starting transfers between devices  42.8 us (29%)
  Pallas kernels  31 us (21%)
  local copies, waits for them, and re-layouts  5.9 us (4%)
  other arithmetic  3.2 us (2%)
    ppermute x35, waiting for transfers between devices, swap(): return lax.ppermute(x, axis, [(i, i ^ offset) for i in range(size)])  61.8 us
    ppermute x35, starting transfers between devices, swap(): return lax.ppermute(x, axis, [(i, i ^ offset) for i in range(size)])  42.8 us
    pallas_call x3, Pallas kernels, shards(): pl.pallas_call(column_kernel, out_shape=(column_shape, row_shape), in_spe...  10.1 us
    pallas_call x1, Pallas kernels, shards(): pl.pallas_call(functools.partial(panel_kernel, firsts), out_shape=(panel,...  8.97 us
    pallas_call x1, Pallas kernels, shards(): pl.pallas_call(functools.partial(plan_kernel, log_column, lines), out_sha...  6.17 us
    pallas_call x2, Pallas kernels, shards(): pl.pallas_call(functools.partial(row_kernel, log_column), out_shape=row_s...  5.75 us
    unnamed x7, local copies, waits for them, and re-layouts  4.69 us
  transfers between devices with their start and end apart: 35, of which 24 were waited for; matrix products, arithmetic and copies ran while one was open for 2% of the time, Pallas kernels for 0%

profile of v5, /device:TPU:0, one launch (start us, length us, event | category | flops | bytes accessed | tf_op | source)
XLA Modules:
  0.0 145.4 jit_solution(706050151263548786)
XLA Ops:
  0.6 0.8 copy.9
  1.8 1.1 fusion.4
  2.9 2.6 %collective-permute-start.2 = (bf16[512,256]{1,0:T(8,128)(2,1)S(1)}, bf16[512,256]{1,0:T(8,128)(2,1)S(1)}, u32[]{:S(2)}, u32[]{:S(2)}) collective-permute-start(bf16[512,256]{1,0:T(8,128)(2,1)S(1)} %get-tuple-element.19), channel_id=1, source_target_pairs={{0,16},{8,24},{16,0},{24,8},{1,17},{9,25},{17,1},{25,9},{2,18},{10... | collective-permute-start | bytes 786440 | tf_op jit(solution)/shard_map/ppermute | solution.py:22
  5.5 1.5 %collective-permute-start.1 = (bf16[512,256]{1,0:T(8,128)(2,1)S(1)}, bf16[512,256]{1,0:T(8,128)(2,1)S(1)}, u32[]{:S(2)}, u32[]{:S(2)}) collective-permute-start(bf16[512,256]{1,0:T(8,128)(2,1)S(1)} %get-tuple-element.22), channel_id=1, source_target_pairs={{0,8},{8,0},{16,24},{24,16},{1,9},{9,1},{17,25},{25,17},{2,10},{10... | collective-permute-start | bytes 786440 | tf_op jit(solution)/shard_map/ppermute | solution.py:22
  8.7 3.8 %collective-permute-done.2.refs_3_ = bf16[512,256]{1,0:T(8,128)(2,1)S(1)} collective-permute-done((bf16[512,256]{1,0:T(8,128)(2,1)S(1)}, bf16[512,256]{1,0:T(8,128)(2,1)S(1)}, u32[]{:S(2)}, u32[]{:S(2)}) %collective-permute-start.2) | collective-permute-done | bytes 262176 | tf_op jit(solution)/shard_map/ppermute | solution.py:22
  12.5 1.5 %collective-permute-done.1.refs_2_ = bf16[512,256]{1,0:T(8,128)(2,1)S(1)} collective-permute-done((bf16[512,256]{1,0:T(8,128)(2,1)S(1)}, bf16[512,256]{1,0:T(8,128)(2,1)S(1)}, u32[]{:S(2)}, u32[]{:S(2)}) %collective-permute-start.1) | collective-permute-done | bytes 262176 | tf_op jit(solution)/shard_map/ppermute | solution.py:22
  13.9 1.5 %collective-permute-start.3 = (bf16[512,256]{1,0:T(8,128)(2,1)S(1)}, bf16[512,256]{1,0:T(8,128)(2,1)S(1)}, u32[]{:S(2)}, u32[]{:S(2)}) collective-permute-start(bf16[512,256]{1,0:T(8,128)(2,1)S(1)} %get-tuple-element.19), channel_id=1, source_target_pairs={{0,8},{8,0},{16,24},{24,16},{1,9},{9,1},{17,25},{25,17},{2,10},{10... | collective-permute-start | bytes 786440 | tf_op jit(solution)/shard_map/ppermute | solution.py:22
  16.5 1.6 %collective-permute-start.6 = (bf16[512,256]{1,0:T(8,128)(2,1)S(1)}, bf16[512,256]{1,0:T(8,128)(2,1)S(1)}, u32[]{:S(2)}, u32[]{:S(2)}) collective-permute-start(bf16[512,256]{1,0:T(8,128)(2,1)S(1)} %collective-permute-done.1.refs_2_), channel_id=1, source_target_pairs={{0,16},{8,24},{16,0},{24,8},{1,17},{9,25},{17,1},{25,9},{2,18},{10... | collective-permute-start | bytes 786440 | tf_op jit(solution)/shard_map/ppermute | solution.py:22
  18.3 3.3 %collective-permute-done.3.refs_1_ = bf16[512,256]{1,0:T(8,128)(2,1)S(1)} collective-permute-done((bf16[512,256]{1,0:T(8,128)(2,1)S(1)}, bf16[512,256]{1,0:T(8,128)(2,1)S(1)}, u32[]{:S(2)}, u32[]{:S(2)}) %collective-permute-start.3) | collective-permute-done | bytes 262176 | tf_op jit(solution)/shard_map/ppermute | solution.py:22
  21.5 1.5 %collective-permute-start.5 = (bf16[512,256]{1,0:T(8,128)(2,1)S(1)}, bf16[512,256]{1,0:T(8,128)(2,1)S(1)}, u32[]{:S(2)}, u32[]{:S(2)}) collective-permute-start(bf16[512,256]{1,0:T(8,128)(2,1)S(1)} %collective-permute-done.2.refs_3_), channel_id=1, source_target_pairs={{0,8},{8,0},{16,24},{24,16},{1,9},{9,1},{17,25},{25,17},{2,10},{10... | collective-permute-start | bytes 786440 | tf_op jit(solution)/shard_map/ppermute | solution.py:22
  23.0 1.9 %collective-permute-done.4.refs_4_ = bf16[512,256]{1,0:T(8,128)(2,1)S(1)} collective-permute-done((bf16[512,256]{1,0:T(8,128)(2,1)S(1)}, bf16[512,256]{1,0:T(8,128)(2,1)S(1)}, u32[]{:S(2)}, u32[]{:S(2)}) %collective-permute-start.4) | collective-permute-done | bytes 262176 | tf_op jit(solution)/shard_map/ppermute | solution.py:22
  25.7 3.0 %collective-permute-done.6.refs_6_ = bf16[512,256]{1,0:T(8,128)(2,1)S(1)} collective-permute-done((bf16[512,256]{1,0:T(8,128)(2,1)S(1)}, bf16[512,256]{1,0:T(8,128)(2,1)S(1)}, u32[]{:S(2)}, u32[]{:S(2)}) %collective-permute-start.6) | collective-permute-done | bytes 262176 | tf_op jit(solution)/shard_map/ppermute | solution.py:22
  29.3 0.9 collective-permute-done.11.refs_11_
  30.9 2.2 %copy-done = bf16[2048,1024]{1,0:T(8,128)(2,1)S(1)} copy-done((bf16[2048,1024]{1,0:T(8,128)(2,1)S(1)}, bf16[2048,1024]{1,0:T(8,128)(2,1)}, u32[]{:S(2)}) %copy-start) | copy-done | bytes 4194328
  33.1 1.0 copy-done.1
  34.2 9.0 %panel.1 = (f32[257,128,128]{2,1,0:T(8,128)S(1)}, bf16[2048,1024]{1,0:T(8,128)(2,1)S(1)}, f32[16,128]{1,0:T(8,128)S(1)}) custom-call(s32[16,16]{1,0:T(8,128)S(1)} %broadcast_add_fusion.1.list_ref, s32[16]{0:T(128)S(1)} %and_select_fusion.1.half_ref, s32[8,16]{1,0:T(8,128)S(1)} %broadcast_add_fusion.2.plist_ref, s32[8]{0:T(128)S(1)} %and_select_fusion.2.pquarter_ref, ...), custom_call_target="tpu_custom_call" | custom-call | tf_op jit(solution)/shard_map/panel/pallas_call | solution.py:311
  43.2 3.8 %collective-permute-start.16 = (f32[16,128]{1,0:T(8,128)S(1)}, f32[16,128]{1,0:T(8,128)S(1)}, u32[]{:S(2)}, u32[]{:S(2)}) collective-permute-start(f32[16,128]{1,0:T(8,128)S(1)} %get-tuple-element.24.refs_0_), channel_id=1, source_target_pairs={{0,6},{1,7},{2,4},{3,5},{4,2},{5,3},{6,0},{7,1},{8,14},{9,15},{10,... | collective-permute-start | bytes 24584 | tf_op jit(solution)/shard_map/ppermute | solution.py:22
  47.0 1.1 collective-permute-start.15
  48.7 2.9 %collective-permute-done.15.refs_2_ = f32[16,128]{1,0:T(8,128)S(1)} collective-permute-done((f32[16,128]{1,0:T(8,128)S(1)}, f32[16,128]{1,0:T(8,128)S(1)}, u32[]{:S(2)}, u32[]{:S(2)}) %collective-permute-start.15) | collective-permute-done | bytes 8224 | tf_op jit(solution)/shard_map/ppermute | solution.py:22
  51.7 3.4 %column_pass.3 = (f32[16,128]{1,0:T(8,128)S(1)}, f32[16,128]{1,0:T(8,128)}) custom-call(s32[16,16]{1,0:T(8,128)S(1)} %broadcast_add_fusion.list_ref, s32[16]{0:T(128)S(1)} %and_select_fusion.half_ref, f32[257,128,128]{2,1,0:T(8,128)S(1)} %get-tuple-element.23.s_ref, f32[16,128]{1,0:T(8,128)S(1)} %get-tuple-element.24.refs_0_, ...), custom_call_target="tpu_custom_call" | custom-call | tf_op jit(solution)/shard_map/column_pass/pallas_call | solution.py:323
  55.1 5.1 %collective-permute-start.19 = (f32[16,128]{1,0:T(8,128)S(1)}, f32[16,128]{1,0:T(8,128)S(1)}, u32[]{:S(2)}, u32[]{:S(2)}) collective-permute-start(f32[16,128]{1,0:T(8,128)S(1)} %get-tuple-element.25.refs_0_), channel_id=1, source_target_pairs={{0,24},{8,16},{16,8},{24,0},{1,25},{9,17},{17,9},{25,1},{2,26},{10... | collective-permute-start | bytes 24584 | tf_op jit(solution)/shard_map/ppermute | solution.py:22
  60.8 1.1 collective-permute-done.19.refs_3_
  61.8 2.0 %collective-permute-done.18.refs_2_ = f32[16,128]{1,0:T(8,128)S(1)} collective-permute-done((f32[16,128]{1,0:T(8,128)S(1)}, f32[16,128]{1,0:T(8,128)S(1)}, u32[]{:S(2)}, u32[]{:S(2)}) %collective-permute-start.18) | collective-permute-done | bytes 8224 | tf_op jit(solution)/shard_map/ppermute | solution.py:22
  63.9 2.8 %row_pass.2.refs_0_ = f32[16,128]{1,0:T(8,128)S(1)} custom-call(s32[16,16]{1,0:T(8,128)S(1)} %broadcast_add_fusion.1.list_ref, s32[16]{0:T(128)S(1)} %and_select_fusion.1.half_ref, f32[257,128,128]{2,1,0:T(8,128)S(1)} %get-tuple-element.23.s_ref, f32[16,128]{1,0:T(8,128)S(1)} %get-tuple-element.25.refs_0_, f32[16,128]{1,0:T(8,128)S(1)} %collective-permute-done.17.refs_1_, ...), custom_call_target="tpu_custom_call" | custom-call | tf_op jit(solution)/shard_map/row_pass/pallas_call | solution.py:334
  66.6 2.1 %collective-permute-start.22 = (f32[16,128]{1,0:T(8,128)S(1)}, f32[16,128]{1,0:T(8,128)S(1)}, u32[]{:S(2)}, u32[]{:S(2)}) collective-permute-start(f32[16,128]{1,0:T(8,128)S(1)} %row_pass.2.refs_0_), channel_id=1, source_target_pairs={{0,6},{1,7},{2,4},{3,5},{4,2},{5,3},{6,0},{7,1},{8,14},{9,15},{10,... | collective-permute-start | bytes 24584 | tf_op jit(solution)/shard_map/ppermute | solution.py:22
  69.2 1.8 %collective-permute-start.20 = (f32[16,128]{1,0:T(8,128)S(1)}, f32[16,128]{1,0:T(8,128)S(1)}, u32[]{:S(2)}, u32[]{:S(2)}) collective-permute-start(f32[16,128]{1,0:T(8,128)S(1)} %row_pass.2.refs_0_), channel_id=1, source_target_pairs={{0,2},{1,3},{2,0},{3,1},{4,6},{5,7},{6,4},{7,5},{8,10},{9,11},{10,... | collective-permute-start | bytes 24584 | tf_op jit(solution)/shard_map/ppermute | solution.py:22
  71.1 1.1 collective-permute-done.22.refs_3_
  72.1 1.2 collective-permute-done.21.refs_2_
  73.3 3.4 %column_pass.4 = (f32[16,128]{1,0:T(8,128)S(1)}, f32[16,128]{1,0:T(8,128)}) custom-call(s32[16,16]{1,0:T(8,128)S(1)} %broadcast_add_fusion.list_ref, s32[16]{0:T(128)S(1)} %and_select_fusion.half_ref, f32[257,128,128]{2,1,0:T(8,128)S(1)} %get-tuple-element.23.s_ref, f32[16,128]{1,0:T(8,128)S(1)} %row_pass.2.refs_0_, ...), custom_call_target="tpu_custom_call" | custom-call | tf_op jit(solution)/shard_map/column_pass/pallas_call | solution.py:323
  76.7 3.8 %collective-permute-start.25 = (f32[16,128]{1,0:T(8,128)S(1)}, f32[16,128]{1,0:T(8,128)S(1)}, u32[]{:S(2)}, u32[]{:S(2)}) collective-permute-start(f32[16,128]{1,0:T(8,128)S(1)} %get-tuple-element.26.refs_0_), channel_id=1, source_target_pairs={{0,24},{8,16},{16,8},{24,0},{1,25},{9,17},{17,9},{25,1},{2,26},{10... | collective-permute-start | bytes 24584 | tf_op jit(solution)/shard_map/ppermute | solution.py:22
  80.5 1.0 collective-permute-start.23
  82.1 2.0 %collective-permute-done.24.refs_2_ = f32[16,128]{1,0:T(8,128)S(1)} collective-permute-done((f32[16,128]{1,0:T(8,128)S(1)}, f32[16,128]{1,0:T(8,128)S(1)}, u32[]{:S(2)}, u32[]{:S(2)}) %collective-permute-start.24) | collective-permute-done | bytes 8224 | tf_op jit(solution)/shard_map/ppermute | solution.py:22
  84.1 3.0 %row_pass.3.refs_0_ = f32[16,128]{1,0:T(8,128)S(1)} custom-call(s32[16,16]{1,0:T(8,128)S(1)} %broadcast_add_fusion.1.list_ref, s32[16]{0:T(128)S(1)} %and_select_fusion.1.half_ref, f32[257,128,128]{2,1,0:T(8,128)S(1)} %get-tuple-element.23.s_ref, f32[16,128]{1,0:T(8,128)S(1)} %get-tuple-element.26.refs_0_, f32[16,128]{1,0:T(8,128)S(1)} %collective-permute-done.23.refs_1_, ...), custom_call_target="tpu_custom_call" | custom-call | tf_op jit(solution)/shard_map/row_pass/pallas_call | solution.py:334
  87.1 2.6 %collective-permute-start.28 = (f32[16,128]{1,0:T(8,128)S(1)}, f32[16,128]{1,0:T(8,128)S(1)}, u32[]{:S(2)}, u32[]{:S(2)}) collective-permute-start(f32[16,128]{1,0:T(8,128)S(1)} %row_pass.3.refs_0_), channel_id=1, source_target_pairs={{0,6},{1,7},{2,4},{3,5},{4,2},{5,3},{6,0},{7,1},{8,14},{9,15},{10,... | collective-permute-start | bytes 24584 | tf_op jit(solution)/shard_map/ppermute | solution.py:22
  89.7 0.8 collective-permute-start.27
  90.5 1.1 collective-permute-start.26
  91.5 1.1 collective-permute-done.28.refs_3_
  92.6 1.7 %collective-permute-done.27.refs_2_ = f32[16,128]{1,0:T(8,128)S(1)} collective-permute-done((f32[16,128]{1,0:T(8,128)S(1)}, f32[16,128]{1,0:T(8,128)S(1)}, u32[]{:S(2)}, u32[]{:S(2)}) %collective-permute-start.27) | collective-permute-done | bytes 8224 | tf_op jit(solution)/shard_map/ppermute | solution.py:22
  94.3 3.4 %column_pass.5 = (f32[16,128]{1,0:T(8,128)S(1)}, f32[16,128]{1,0:T(8,128)}) custom-call(s32[16,16]{1,0:T(8,128)S(1)} %broadcast_add_fusion.list_ref, s32[16]{0:T(128)S(1)} %and_select_fusion.half_ref, f32[257,128,128]{2,1,0:T(8,128)S(1)} %get-tuple-element.23.s_ref, f32[16,128]{1,0:T(8,128)S(1)} %row_pass.3.refs_0_, ...), custom_call_target="tpu_custom_call" | custom-call | tf_op jit(solution)/shard_map/column_pass/pallas_call | solution.py:323
  97.6 4.3 %collective-permute-start.31 = (f32[16,128]{1,0:T(8,128)S(1)}, f32[16,128]{1,0:T(8,128)S(1)}, u32[]{:S(2)}, u32[]{:S(2)}) collective-permute-start(f32[16,128]{1,0:T(8,128)S(1)} %get-tuple-element.29.refs_0_), channel_id=1, source_target_pairs={{0,24},{8,16},{16,8},{24,0},{1,25},{9,17},{17,9},{25,1},{2,26},{10... | collective-permute-start | bytes 24584 | tf_op jit(solution)/shard_map/ppermute | solution.py:22
  102.5 1.1 collective-permute-done.31.refs_3_
  103.6 2.0 %collective-permute-done.30.refs_2_ = f32[16,128]{1,0:T(8,128)S(1)} collective-permute-done((f32[16,128]{1,0:T(8,128)S(1)}, f32[16,128]{1,0:T(8,128)S(1)}, u32[]{:S(2)}, u32[]{:S(2)}) %collective-permute-start.30) | collective-permute-done | bytes 8224 | tf_op jit(solution)/shard_map/ppermute | solution.py:22
  106.3 6.2 %plan.1 = (bf16[2048,128]{1,0:T(8,128)(2,1)S(1)}, bf16[2048,128]{1,0:T(8,128)(2,1)S(1)}, bf16[2048,128]{1,0:T(8,128)(2,1)S(1)}, bf16[2048,128]{1,0:T(8,128)(2,1)S(1)}, f32[8,128]{1,0:T(8,128)}) custom-call(s32[8,16]{1,0:T(8,128)S(1)} %broadcast_add_fusion.2.plist_ref, s32[8]{0:T(128)S(1)} %and_select_fusion.2.pquarter_ref, ...), custom_call_target="tpu_custom_call" | custom-call | tf_op jit(solution)/shard_map/plan/pallas_call | solution.py:344
  112.5 1.9 %collective-permute-start.33 = (bf16[2048,128]{1,0:T(8,128)(2,1)S(1)}, bf16[2048,128]{1,0:T(8,128)(2,1)S(1)}, u32[]{:S(2)}, u32[]{:S(2)}) collective-permute-start(bf16[2048,128]{1,0:T(8,128)(2,1)S(1)} %get-tuple-element.33), channel_id=1, source_target_pairs={{0,2},{1,3},{2,0},{3,1},{4,6},{5,7},{6,4},{7,5},{8,10},{9,11},{10,... | collective-permute-start | bytes 1572872 | tf_op jit(solution)/shard_map/ppermute | solution.py:22
  114.5 14.0 %collective-permute-done.33 = bf16[2048,128]{1,0:T(8,128)(2,1)S(1)} collective-permute-done((bf16[2048,128]{1,0:T(8,128)(2,1)S(1)}, bf16[2048,128]{1,0:T(8,128)(2,1)S(1)}, u32[]{:S(2)}, u32[]{:S(2)}) %collective-permute-start.33) | collective-permute-done | bytes 524320 | tf_op jit(solution)/shard_map/ppermute | solution.py:22
  129.2 6.6 %collective-permute-done.32 = bf16[2048,128]{1,0:T(8,128)(2,1)S(1)} collective-permute-done((bf16[2048,128]{1,0:T(8,128)(2,1)S(1)}, bf16[2048,128]{1,0:T(8,128)(2,1)S(1)}, u32[]{:S(2)}, u32[]{:S(2)}) %collective-permute-start.32) | collective-permute-done | bytes 524320 | tf_op jit(solution)/shard_map/ppermute | solution.py:22
  135.8 8.7 %collective-permute-done.34 = bf16[2048,128]{1,0:T(8,128)(2,1)S(1)} collective-permute-done((bf16[2048,128]{1,0:T(8,128)(2,1)S(1)}, bf16[2048,128]{1,0:T(8,128)(2,1)S(1)}, u32[]{:S(2)}, u32[]{:S(2)}) %collective-permute-start.34) | collective-permute-done | bytes 524320 | tf_op jit(solution)/shard_map/ppermute | solution.py:22
  144.4 1.0 add_convert_fusion
  (60 shorter events, 9.8 us)
Async XLA Ops:
  1.4 5.7 %collective-permute-start = (s32[16,8]{1,0:T(8,128)S(1)}, s32[16,8]{1,0:T(8,128)S(1)}, u32[]{:S(2)}, u32[]{:S(2)}) collective-permute-start(s32[16,8]{1,0:T(8,128)S(1)} %copy.9), channel_id=1, source_target_pairs={{0,1},{1,0},{2,3},{3,2},{4,5},{5,4},{6,7},{7,6},{8,9},{9,8},{10,11... | collective-permute-start | bytes 1544 | tf_op jit(solution)/shard_map/ppermute | solution.py:22
  2.9 9.6 %collective-permute-start.2 = (bf16[512,256]{1,0:T(8,128)(2,1)S(1)}, bf16[512,256]{1,0:T(8,128)(2,1)S(1)}, u32[]{:S(2)}, u32[]{:S(2)}) collective-permute-start(bf16[512,256]{1,0:T(8,128)(2,1)S(1)} %get-tuple-element.19), channel_id=1, source_target_pairs={{0,16},{8,24},{16,0},{24,8},{1,17},{9,25},{17,1},{25,9},{2,18},{10... | collective-permute-start | bytes 786440 | tf_op jit(solution)/shard_map/ppermute | solution.py:22
  5.5 8.4 %collective-permute-start.1 = (bf16[512,256]{1,0:T(8,128)(2,1)S(1)}, bf16[512,256]{1,0:T(8,128)(2,1)S(1)}, u32[]{:S(2)}, u32[]{:S(2)}) collective-permute-start(bf16[512,256]{1,0:T(8,128)(2,1)S(1)} %get-tuple-element.22), channel_id=1, source_target_pairs={{0,8},{8,0},{16,24},{24,16},{1,9},{9,1},{17,25},{25,17},{2,10},{10... | collective-permute-start | bytes 786440 | tf_op jit(solution)/shard_map/ppermute | solution.py:22
  13.9 7.6 %collective-permute-start.3 = (bf16[512,256]{1,0:T(8,128)(2,1)S(1)}, bf16[512,256]{1,0:T(8,128)(2,1)S(1)}, u32[]{:S(2)}, u32[]{:S(2)}) collective-permute-start(bf16[512,256]{1,0:T(8,128)(2,1)S(1)} %get-tuple-element.19), channel_id=1, source_target_pairs={{0,8},{8,0},{16,24},{24,16},{1,9},{9,1},{17,25},{25,17},{2,10},{10... | collective-permute-start | bytes 786440 | tf_op jit(solution)/shard_map/ppermute | solution.py:22
  15.6 9.3 %collective-permute-start.4 = (bf16[512,256]{1,0:T(8,128)(2,1)S(1)}, bf16[512,256]{1,0:T(8,128)(2,1)S(1)}, u32[]{:S(2)}, u32[]{:S(2)}) collective-permute-start(bf16[512,256]{1,0:T(8,128)(2,1)S(1)} %get-tuple-element.22), channel_id=1, source_target_pairs={{0,16},{8,24},{16,0},{24,8},{1,17},{9,25},{17,1},{25,9},{2,18},{10... | collective-permute-start | bytes 786440 | tf_op jit(solution)/shard_map/ppermute | solution.py:22
  16.4 8.7 %collective-permute-start.9 = (bf16[512,256]{1,0:T(8,128)(2,1)S(1)}, bf16[512,256]{1,0:T(8,128)(2,1)S(1)}, u32[]{:S(2)}, u32[]{:S(2)}) collective-permute-start(bf16[512,256]{1,0:T(8,128)(2,1)S(1)} %collective-permute-done.1.refs_2_), channel_id=1, source_target_pairs={{0,1},{1,0},{2,3},{3,2},{4,5},{5,4},{6,7},{7,6},{8,9},{9,8},{10,11... | collective-permute-start | bytes 786440 | tf_op jit(solution)/shard_map/ppermute | solution.py:22
  16.5 12.2 %collective-permute-start.6 = (bf16[512,256]{1,0:T(8,128)(2,1)S(1)}, bf16[512,256]{1,0:T(8,128)(2,1)S(1)}, u32[]{:S(2)}, u32[]{:S(2)}) collective-permute-start(bf16[512,256]{1,0:T(8,128)(2,1)S(1)} %collective-permute-done.1.refs_2_), channel_id=1, source_target_pairs={{0,16},{8,24},{16,0},{24,8},{1,17},{9,25},{17,1},{25,9},{2,18},{10... | collective-permute-start | bytes 786440 | tf_op jit(solution)/shard_map/ppermute | solution.py:22
  18.1 10.6 %collective-permute-start.10 = (bf16[512,256]{1,0:T(8,128)(2,1)S(1)}, bf16[512,256]{1,0:T(8,128)(2,1)S(1)}, u32[]{:S(2)}, u32[]{:S(2)}) collective-permute-start(bf16[512,256]{1,0:T(8,128)(2,1)S(1)} %collective-permute-done.2.refs_3_), channel_id=1, source_target_pairs={{0,1},{1,0},{2,3},{3,2},{4,5},{5,4},{6,7},{7,6},{8,9},{9,8},{10,11... | collective-permute-start | bytes 786440 | tf_op jit(solution)/shard_map/ppermute | solution.py:22
  21.5 7.6 %collective-permute-start.5 = (bf16[512,256]{1,0:T(8,128)(2,1)S(1)}, bf16[512,256]{1,0:T(8,128)(2,1)S(1)}, u32[]{:S(2)}, u32[]{:S(2)}) collective-permute-start(bf16[512,256]{1,0:T(8,128)(2,1)S(1)} %collective-permute-done.2.refs_3_), channel_id=1, source_target_pairs={{0,8},{8,0},{16,24},{24,16},{1,9},{9,1},{17,25},{25,17},{2,10},{10... | collective-permute-start | bytes 786440 | tf_op jit(solution)/shard_map/ppermute | solution.py:22
  24.9 4.3 %collective-permute-start.7 = (bf16[1024,256]{1,0:T(8,128)(2,1)}, bf16[1024,256]{1,0:T(8,128)(2,1)S(1)}, u32[]{:S(2)}, u32[]{:S(2)}) collective-permute-start(bf16[1024,256]{1,0:T(8,128)(2,1)} %refs_0_.1), channel_id=1, source_target_pairs={{0,1},{1,0},{2,3},{3,2},{4,5},{5,4},{6,7},{7,6},{8,9},{9,8},{10,11... | collective-permute-start | bytes 1572872 | tf_op jit(solution)/shard_map/ppermute | solution.py:22
  25.1 4.2 %collective-permute-start.8 = (bf16[512,256]{1,0:T(8,128)(2,1)S(1)}, bf16[512,256]{1,0:T(8,128)(2,1)S(1)}, u32[]{:S(2)}, u32[]{:S(2)}) collective-permute-start(bf16[512,256]{1,0:T(8,128)(2,1)S(1)} %collective-permute-done.3.refs_1_), channel_id=1, source_target_pairs={{0,1},{1,0},{2,3},{3,2},{4,5},{5,4},{6,7},{7,6},{8,9},{9,8},{10,11... | collective-permute-start | bytes 786440 | tf_op jit(solution)/shard_map/ppermute | solution.py:22
  28.7 1.5 %collective-permute-start.11 = (bf16[512,256]{1,0:T(8,128)(2,1)S(1)}, bf16[512,256]{1,0:T(8,128)(2,1)S(1)}, u32[]{:S(2)}, u32[]{:S(2)}) collective-permute-start(bf16[512,256]{1,0:T(8,128)(2,1)S(1)} %collective-permute-done.4.refs_4_), channel_id=1, source_target_pairs={{0,1},{1,0},{2,3},{3,2},{4,5},{5,4},{6,7},{7,6},{8,9},{9,8},{10,11... | collective-permute-start | bytes 786440 | tf_op jit(solution)/shard_map/ppermute | solution.py:22
  28.7 1.9 %collective-permute-start.13 = (bf16[512,256]{1,0:T(8,128)(2,1)S(1)}, bf16[512,256]{1,0:T(8,128)(2,1)S(1)}, u32[]{:S(2)}, u32[]{:S(2)}) collective-permute-start(bf16[512,256]{1,0:T(8,128)(2,1)S(1)} %collective-permute-done.6.refs_6_), channel_id=1, source_target_pairs={{0,1},{1,0},{2,3},{3,2},{4,5},{5,4},{6,7},{7,6},{8,9},{9,8},{10,11... | collective-permute-start | bytes 786440 | tf_op jit(solution)/shard_map/ppermute | solution.py:22
  29.2 1.8 %collective-permute-start.12 = (bf16[512,256]{1,0:T(8,128)(2,1)S(1)}, bf16[512,256]{1,0:T(8,128)(2,1)S(1)}, u32[]{:S(2)}, u32[]{:S(2)}) collective-permute-start(bf16[512,256]{1,0:T(8,128)(2,1)S(1)} %collective-permute-done.5.refs_5_), channel_id=1, source_target_pairs={{0,1},{1,0},{2,3},{3,2},{4,5},{5,4},{6,7},{7,6},{8,9},{9,8},{10,11... | collective-permute-start | bytes 786440 | tf_op jit(solution)/shard_map/ppermute | solution.py:22
  30.9 2.2 %copy-start = (bf16[2048,1024]{1,0:T(8,128)(2,1)S(1)}, bf16[2048,1024]{1,0:T(8,128)(2,1)}, u32[]{:S(2)}) copy-start(bf16[2048,1024]{1,0:T(8,128)(2,1)} %e_hbm_ref.1) | copy-start | bytes 12582916
  33.1 1.0 copy-start.1
  43.2 5.5 %collective-permute-start.16 = (f32[16,128]{1,0:T(8,128)S(1)}, f32[16,128]{1,0:T(8,128)S(1)}, u32[]{:S(2)}, u32[]{:S(2)}) collective-permute-start(f32[16,128]{1,0:T(8,128)S(1)} %get-tuple-element.24.refs_0_), channel_id=1, source_target_pairs={{0,6},{1,7},{2,4},{3,5},{4,2},{5,3},{6,0},{7,1},{8,14},{9,15},{10,... | collective-permute-start | bytes 24584 | tf_op jit(solution)/shard_map/ppermute | solution.py:22
  47.0 4.5 %collective-permute-start.15 = (f32[16,128]{1,0:T(8,128)S(1)}, f32[16,128]{1,0:T(8,128)S(1)}, u32[]{:S(2)}, u32[]{:S(2)}) collective-permute-start(f32[16,128]{1,0:T(8,128)S(1)} %get-tuple-element.24.refs_0_), channel_id=1, source_target_pairs={{0,4},{1,5},{2,6},{3,7},{4,0},{5,1},{6,2},{7,3},{8,12},{9,13},{10,... | collective-permute-start | bytes 24584 | tf_op jit(solution)/shard_map/ppermute | solution.py:22
  48.1 3.7 %collective-permute-start.14 = (f32[16,128]{1,0:T(8,128)S(1)}, f32[16,128]{1,0:T(8,128)S(1)}, u32[]{:S(2)}, u32[]{:S(2)}) collective-permute-start(f32[16,128]{1,0:T(8,128)S(1)} %get-tuple-element.24.refs_0_), channel_id=1, source_target_pairs={{0,2},{1,3},{2,0},{3,1},{4,6},{5,7},{6,4},{7,5},{8,10},{9,11},{10,... | collective-permute-start | bytes 24584 | tf_op jit(solution)/shard_map/ppermute | solution.py:22
  55.1 6.7 %collective-permute-start.19 = (f32[16,128]{1,0:T(8,128)S(1)}, f32[16,128]{1,0:T(8,128)S(1)}, u32[]{:S(2)}, u32[]{:S(2)}) collective-permute-start(f32[16,128]{1,0:T(8,128)S(1)} %get-tuple-element.25.refs_0_), channel_id=1, source_target_pairs={{0,24},{8,16},{16,8},{24,0},{1,25},{9,17},{17,9},{25,1},{2,26},{10... | collective-permute-start | bytes 24584 | tf_op jit(solution)/shard_map/ppermute | solution.py:22
  60.2 3.7 %collective-permute-start.18 = (f32[16,128]{1,0:T(8,128)S(1)}, f32[16,128]{1,0:T(8,128)S(1)}, u32[]{:S(2)}, u32[]{:S(2)}) collective-permute-start(f32[16,128]{1,0:T(8,128)S(1)} %get-tuple-element.25.refs_0_), channel_id=1, source_target_pairs={{0,16},{8,24},{16,0},{24,8},{1,17},{9,25},{17,1},{25,9},{2,18},{10... | collective-permute-start | bytes 24584 | tf_op jit(solution)/shard_map/ppermute | solution.py:22
  60.2 3.7 %collective-permute-start.17 = (f32[16,128]{1,0:T(8,128)S(1)}, f32[16,128]{1,0:T(8,128)S(1)}, u32[]{:S(2)}, u32[]{:S(2)}) collective-permute-start(f32[16,128]{1,0:T(8,128)S(1)} %get-tuple-element.25.refs_0_), channel_id=1, source_target_pairs={{0,8},{8,0},{16,24},{24,16},{1,9},{9,1},{17,25},{25,17},{2,10},{10... | collective-permute-start | bytes 24584 | tf_op jit(solution)/shard_map/ppermute | solution.py:22
  66.6 5.5 %collective-permute-start.22 = (f32[16,128]{1,0:T(8,128)S(1)}, f32[16,128]{1,0:T(8,128)S(1)}, u32[]{:S(2)}, u32[]{:S(2)}) collective-permute-start(f32[16,128]{1,0:T(8,128)S(1)} %row_pass.2.refs_0_), channel_id=1, source_target_pairs={{0,6},{1,7},{2,4},{3,5},{4,2},{5,3},{6,0},{7,1},{8,14},{9,15},{10,... | collective-permute-start | bytes 24584 | tf_op jit(solution)/shard_map/ppermute | solution.py:22
  68.8 4.6 %collective-permute-start.21 = (f32[16,128]{1,0:T(8,128)S(1)}, f32[16,128]{1,0:T(8,128)S(1)}, u32[]{:S(2)}, u32[]{:S(2)}) collective-permute-start(f32[16,128]{1,0:T(8,128)S(1)} %row_pass.2.refs_0_), channel_id=1, source_target_pairs={{0,4},{1,5},{2,6},{3,7},{4,0},{5,1},{6,2},{7,3},{8,12},{9,13},{10,... | collective-permute-start | bytes 24584 | tf_op jit(solution)/shard_map/ppermute | solution.py:22
  69.2 4.1 %collective-permute-start.20 = (f32[16,128]{1,0:T(8,128)S(1)}, f32[16,128]{1,0:T(8,128)S(1)}, u32[]{:S(2)}, u32[]{:S(2)}) collective-permute-start(f32[16,128]{1,0:T(8,128)S(1)} %row_pass.2.refs_0_), channel_id=1, source_target_pairs={{0,2},{1,3},{2,0},{3,1},{4,6},{5,7},{6,4},{7,5},{8,10},{9,11},{10,... | collective-permute-start | bytes 24584 | tf_op jit(solution)/shard_map/ppermute | solution.py:22
  76.7 5.4 %collective-permute-start.25 = (f32[16,128]{1,0:T(8,128)S(1)}, f32[16,128]{1,0:T(8,128)S(1)}, u32[]{:S(2)}, u32[]{:S(2)}) collective-permute-start(f32[16,128]{1,0:T(8,128)S(1)} %get-tuple-element.26.refs_0_), channel_id=1, source_target_pairs={{0,24},{8,16},{16,8},{24,0},{1,25},{9,17},{17,9},{25,1},{2,26},{10... | collective-permute-start | bytes 24584 | tf_op jit(solution)/shard_map/ppermute | solution.py:22
  80.5 3.7 %collective-permute-start.24 = (f32[16,128]{1,0:T(8,128)S(1)}, f32[16,128]{1,0:T(8,128)S(1)}, u32[]{:S(2)}, u32[]{:S(2)}) collective-permute-start(f32[16,128]{1,0:T(8,128)S(1)} %get-tuple-element.26.refs_0_), channel_id=1, source_target_pairs={{0,16},{8,24},{16,0},{24,8},{1,17},{9,25},{17,1},{25,9},{2,18},{10... | collective-permute-start | bytes 24584 | tf_op jit(solution)/shard_map/ppermute | solution.py:22
  80.5 3.7 %collective-permute-start.23 = (f32[16,128]{1,0:T(8,128)S(1)}, f32[16,128]{1,0:T(8,128)S(1)}, u32[]{:S(2)}, u32[]{:S(2)}) collective-permute-start(f32[16,128]{1,0:T(8,128)S(1)} %get-tuple-element.26.refs_0_), channel_id=1, source_target_pairs={{0,8},{8,0},{16,24},{24,16},{1,9},{9,1},{17,25},{25,17},{2,10},{10... | collective-permute-start | bytes 24584 | tf_op jit(solution)/shard_map/ppermute | solution.py:22
  87.1 5.5 %collective-permute-start.28 = (f32[16,128]{1,0:T(8,128)S(1)}, f32[16,128]{1,0:T(8,128)S(1)}, u32[]{:S(2)}, u32[]{:S(2)}) collective-permute-start(f32[16,128]{1,0:T(8,128)S(1)} %row_pass.3.refs_0_), channel_id=1, source_target_pairs={{0,6},{1,7},{2,4},{3,5},{4,2},{5,3},{6,0},{7,1},{8,14},{9,15},{10,... | collective-permute-start | bytes 24584 | tf_op jit(solution)/shard_map/ppermute | solution.py:22
  89.7 4.5 %collective-permute-start.27 = (f32[16,128]{1,0:T(8,128)S(1)}, f32[16,128]{1,0:T(8,128)S(1)}, u32[]{:S(2)}, u32[]{:S(2)}) collective-permute-start(f32[16,128]{1,0:T(8,128)S(1)} %row_pass.3.refs_0_), channel_id=1, source_target_pairs={{0,4},{1,5},{2,6},{3,7},{4,0},{5,1},{6,2},{7,3},{8,12},{9,13},{10,... | collective-permute-start | bytes 24584 | tf_op jit(solution)/shard_map/ppermute | solution.py:22
  90.5 3.8 %collective-permute-start.26 = (f32[16,128]{1,0:T(8,128)S(1)}, f32[16,128]{1,0:T(8,128)S(1)}, u32[]{:S(2)}, u32[]{:S(2)}) collective-permute-start(f32[16,128]{1,0:T(8,128)S(1)} %row_pass.3.refs_0_), channel_id=1, source_target_pairs={{0,2},{1,3},{2,0},{3,1},{4,6},{5,7},{6,4},{7,5},{8,10},{9,11},{10,... | collective-permute-start | bytes 24584 | tf_op jit(solution)/shard_map/ppermute | solution.py:22
  97.6 5.9 %collective-permute-start.31 = (f32[16,128]{1,0:T(8,128)S(1)}, f32[16,128]{1,0:T(8,128)S(1)}, u32[]{:S(2)}, u32[]{:S(2)}) collective-permute-start(f32[16,128]{1,0:T(8,128)S(1)} %get-tuple-element.29.refs_0_), channel_id=1, source_target_pairs={{0,24},{8,16},{16,8},{24,0},{1,25},{9,17},{17,9},{25,1},{2,26},{10... | collective-permute-start | bytes 24584 | tf_op jit(solution)/shard_map/ppermute | solution.py:22
  101.9 3.7 %collective-permute-start.30 = (f32[16,128]{1,0:T(8,128)S(1)}, f32[16,128]{1,0:T(8,128)S(1)}, u32[]{:S(2)}, u32[]{:S(2)}) collective-permute-start(f32[16,128]{1,0:T(8,128)S(1)} %get-tuple-element.29.refs_0_), channel_id=1, source_target_pairs={{0,16},{8,24},{16,0},{24,8},{1,17},{9,25},{17,1},{25,9},{2,18},{10... | collective-permute-start | bytes 24584 | tf_op jit(solution)/shard_map/ppermute | solution.py:22
  101.9 3.7 %collective-permute-start.29 = (f32[16,128]{1,0:T(8,128)S(1)}, f32[16,128]{1,0:T(8,128)S(1)}, u32[]{:S(2)}, u32[]{:S(2)}) collective-permute-start(f32[16,128]{1,0:T(8,128)S(1)} %get-tuple-element.29.refs_0_), channel_id=1, source_target_pairs={{0,8},{8,0},{16,24},{24,16},{1,9},{9,1},{17,25},{25,17},{2,10},{10... | collective-permute-start | bytes 24584 | tf_op jit(solution)/shard_map/ppermute | solution.py:22
  105.6 0.7 copy-start.2
  112.5 16.0 %collective-permute-start.33 = (bf16[2048,128]{1,0:T(8,128)(2,1)S(1)}, bf16[2048,128]{1,0:T(8,128)(2,1)S(1)}, u32[]{:S(2)}, u32[]{:S(2)}) collective-permute-start(bf16[2048,128]{1,0:T(8,128)(2,1)S(1)} %get-tuple-element.33), channel_id=1, source_target_pairs={{0,2},{1,3},{2,0},{3,1},{4,6},{5,7},{6,4},{7,5},{8,10},{9,11},{10,... | collective-permute-start | bytes 1572872 | tf_op jit(solution)/shard_map/ppermute | solution.py:22
  114.4 21.3 %collective-permute-start.32 = (bf16[2048,128]{1,0:T(8,128)(2,1)S(1)}, bf16[2048,128]{1,0:T(8,128)(2,1)S(1)}, u32[]{:S(2)}, u32[]{:S(2)}) collective-permute-start(bf16[2048,128]{1,0:T(8,128)(2,1)S(1)} %get-tuple-element.31), channel_id=1, source_target_pairs={{0,2},{1,3},{2,0},{3,1},{4,6},{5,7},{6,4},{7,5},{8,10},{9,11},{10,... | collective-permute-start | bytes 1572872 | tf_op jit(solution)/shard_map/ppermute | solution.py:22
  128.6 15.8 %collective-permute-start.34 = (bf16[2048,128]{1,0:T(8,128)(2,1)S(1)}, bf16[2048,128]{1,0:T(8,128)(2,1)S(1)}, u32[]{:S(2)}, u32[]{:S(2)}) collective-permute-start(bf16[2048,128]{1,0:T(8,128)(2,1)S(1)} %add_convert_fusion.1), channel_id=1, source_target_pairs={{0,4},{1,5},{2,6},{3,7},{4,0},{5,1},{6,2},{7,3},{8,12},{9,13},{10,... | collective-permute-start | bytes 1572872 | tf_op jit(solution)/shard_map/ppermute | solution.py:22

commit v6 on v5

--- a/solution.py
+++ b/solution.py
@@ -134,42 +134,151 @@
     row_pass(list_ref, half_ref, s_ref, None, acc_ref, out_ref)
 
 
-def row_kernel(log_column, list_ref, half_ref, s_ref, *refs):
-    parts, (out_ref, c_ref, acc_ref) = refs[:-3], refs[-3:]
-    columns = list_ref.shape[1]
-    c_ref[:columns] = log_column - combine([part[...] for part in parts])
-    c_ref[columns:] = jnp.zeros((c_ref.shape[0] - columns, TILE), jnp.float32)
-    row_pass(list_ref, half_ref, s_ref, c_ref, acc_ref, out_ref)
-
-
-def column_kernel(list_ref, half_ref, s_ref, *refs):
+def four_loop(count, step, start):
+    return lax.fori_loop(
+        0, count, lambda k, a: functools.reduce(lambda b, i: step(4 * k + i, b), range(4), a), start
+    )
+
+
+def row_kernel(log_column, list_ref, half_ref, quarter_ref, s_ref, w_ref, m_ref, r_ref, *refs):
+    parts, (out_ref, c_ref, v_ref, acc_ref) = refs[:-4], refs[-4:]
+    row_tiles, columns = list_ref.shape
+    dummy = row_tiles * columns
+    column = log_column - combine([part[...] for part in parts])
+    c_ref[:columns] = column
+    v_ref[:columns] = jnp.exp(column + m_ref[...])
+    rest = jnp.zeros((c_ref.shape[0] - columns, TILE), jnp.float32)
+    c_ref[columns:] = rest
+    v_ref[columns:] = rest
+    lane = lax.broadcasted_iota(jnp.int32, (TILE, TILE), 1)
+
+    def place(t, u):
+        return jnp.where(u == columns, dummy, t * columns + u)
+
+    for t in range(row_tiles):
+
+        def one_tile(k, a, t=t):
+            u = list_ref[t, k]
+            return a + w_ref[place(t, u)].astype(jnp.float32) * v_ref[pl.ds(u, 1), :]
+
+        acc_ref[t] = four_loop(quarter_ref[t], one_tile, jnp.zeros((TILE, TILE), jnp.float32))
+    totals = jnp.zeros((TILE, TILE), jnp.float32)
+    for t in range(row_tiles):
+        totals = jnp.where(lane == t, jnp.sum(acc_ref[t], axis=1, keepdims=True), totals)
+    totals = totals.T[:row_tiles]
+    out_ref[...] = jnp.log(totals) - r_ref[...]
+    small = jnp.min(totals, axis=1, keepdims=True)
+    least = [jnp.min(small[t : t + 1, :]) for t in range(row_tiles)]
+    for t in range(row_tiles):
+
+        @pl.when(jnp.logical_not(least[t] > 1e-15))
+        def _():
+            def score(k):
+                u = list_ref[t, k]
+                return s_ref[place(t, u)] + c_ref[pl.ds(u, 1), :]
+
+            peak = score_loop(
+                half_ref[t],
+                lambda k, a: jnp.maximum(a, score(k)),
+                jnp.full((TILE, TILE), NEGATIVE, jnp.float32),
+            )
+            peak = jnp.max(peak, axis=1, keepdims=True)
+            total = score_loop(
+                half_ref[t],
+                lambda k, a: a + jnp.exp(score(k) - peak),
+                jnp.zeros((TILE, TILE), jnp.float32),
+            )
+            found = peak + jnp.log(jnp.sum(total, axis=1, keepdims=True))
+            out_ref[t : t + 1, :] = jnp.broadcast_to(found, (TILE, TILE)).T[:1]
+
+
+def first_column_kernel(list_ref, half_ref, s_ref, *refs):
+    parts, (out_ref, r_ref, w_ref, m_ref, wide_ref, acc_ref) = refs[:-6], refs[-6:]
+    columns, row_tiles = list_ref.shape
+    dummy = row_tiles * columns
+    row = -combine([part[...] for part in parts])
+    r_ref[...] = row
+    spread_rows(row, wide_ref)
+    w_ref[dummy] = jnp.zeros((TILE, TILE), jnp.bfloat16)
+
+    def score(u, k):
+        t = list_ref[u, k]
+        at = jnp.where(t == row_tiles, dummy, t * columns + u)
+        return at, s_ref[at] + wide_ref[jnp.minimum(t, row_tiles - 1)]
+
+    for u in range(columns):
+        acc_ref[u] = score_loop(
+            half_ref[u],
+            lambda k, a, u=u: jnp.maximum(a, score(u, k)[1]),
+            jnp.full((TILE, TILE), NEGATIVE, jnp.float32),
+        )
+    peaks = [jnp.max(acc_ref[u], axis=0, keepdims=True) for u in range(columns)]
+    for u in range(columns):
+
+        def one_tile(k, a, u=u):
+            at, value = score(u, k)
+            value = jnp.exp(value - peaks[u])
+            w_ref[at] = value.astype(jnp.bfloat16)
+            return a + value
+
+        acc_ref[u] = score_loop(half_ref[u], one_tile, jnp.zeros((TILE, TILE), jnp.float32))
+    totals = [jnp.sum(acc_ref[u], axis=0, keepdims=True) for u in range(columns)]
+    peaks = jnp.concatenate(peaks, axis=0)
+    m_ref[...] = peaks
+    out_ref[...] = peaks + jnp.log(jnp.concatenate(totals, axis=0))
+
+
+def column_kernel(list_ref, half_ref, quarter_ref, s_ref, w_ref, m_ref, first_ref, *refs):
     parts, (out_ref, r_ref, wide_ref, acc_ref) = refs[:-4], refs[-4:]
     columns, row_tiles = list_ref.shape
     dummy = row_tiles * columns
     row = -combine([part[...] for part in parts])
     r_ref[...] = row
-    spread_rows(row, wide_ref)
-
-    def score(u, k):
-        t = list_ref[u, k]
-        inside = jnp.minimum(t, row_tiles - 1)
-        return s_ref[jnp.where(t == row_tiles, dummy, t * columns + u)] + wide_ref[inside]
+    factor = jnp.exp(row - first_ref[...])
+    spread_rows(factor, wide_ref)
+
+    def place(t, u):
+        return jnp.where(t == row_tiles, dummy, t * columns + u)
 
     for u in range(columns):
-        acc_ref[u] = score_loop(
-            half_ref[u],
-            lambda k, a, u=u: jnp.maximum(a, score(u, k)),
-            jnp.full((TILE, TILE), NEGATIVE, jnp.float32),
-        )
-    peaks = [jnp.max(acc_ref[u], axis=0, keepdims=True) for u in range(columns)]
-    for u in range(columns):
-        acc_ref[u] = score_loop(
-            half_ref[u],
-            lambda k, a, u=u: a + jnp.exp(score(u, k) - peaks[u]),
-            jnp.zeros((TILE, TILE), jnp.float32),
-        )
-    totals = [jnp.sum(acc_ref[u], axis=0, keepdims=True) for u in range(columns)]
-    out_ref[...] = jnp.concatenate(peaks, axis=0) + jnp.log(jnp.concatenate(totals, axis=0))
+
+        def one_tile(k, a, u=u):
+            t = list_ref[u, k]
+            return a + w_ref[place(t, u)].astype(jnp.float32) * wide_ref[jnp.minimum(t, row_tiles - 1)]
+
+        acc_ref[u] = four_loop(quarter_ref[u], one_tile, jnp.zeros((TILE, TILE), jnp.float32))
+    totals = jnp.concatenate(
+        [jnp.sum(acc_ref[u], axis=0, keepdims=True) for u in range(columns)], axis=0
+    )
+    out_ref[...] = m_ref[...] + jnp.log(totals)
+    fine = (totals > 1e-15) & (totals < 1e30)
+    fine = jnp.min(jnp.where(fine, 1.0, 0.0), axis=1, keepdims=True)
+    fine = jnp.where(jnp.max(factor) < 1e15, fine, 0.0)
+    least = [jnp.min(fine[u : u + 1, :]) for u in range(columns)]
+
+    @pl.when(jnp.logical_not(jnp.min(fine) > 0.5))
+    def _():
+        spread_rows(row, wide_ref)
+        for u in range(columns):
+
+            @pl.when(jnp.logical_not(least[u] > 0.5))
+            def _():
+                def score(k):
+                    t = list_ref[u, k]
+                    return s_ref[place(t, u)] + wide_ref[jnp.minimum(t, row_tiles - 1)]
+
+                peak = score_loop(
+                    half_ref[u],
+                    lambda k, a: jnp.maximum(a, score(k)),
+                    jnp.full((TILE, TILE), NEGATIVE, jnp.float32),
+                )
+                peak = jnp.max(peak, axis=0, keepdims=True)
+                total = score_loop(
+                    half_ref[u],
+                    lambda k, a: a + jnp.exp(score(k) - peak),
+                    jnp.zeros((TILE, TILE), jnp.float32),
+                )
+                out_ref[u : u + 1, :] = peak + jnp.log(jnp.sum(total, axis=0, keepdims=True))
 
 
 def plan_kernel(log_column, lines, plist_ref, pquarter_ref, mask_ref, place_ref, s_ref, r_ref, p_ref, *refs):
@@ -299,6 +408,7 @@
     column_list, column_count = ordered(across)
     pair_list, pair_count = ordered(jnp.max(across.reshape(columns // 2, 2, row_tiles), axis=1))
     row_half, column_half = (row_count + 1) // 2, (column_count + 1) // 2
+    row_quarter, column_quarter = (row_count + 3) // 4, (column_count + 3) // 4
     pair_quarter = (pair_count + 3) // 4
     z = lax.axis_index("proto") // 2
     places = jnp.stack([place.astype(jnp.int32) for place in [core, z] + starts])
@@ -314,32 +424,47 @@
         in_specs=[SMEM] * 5 + [HBM] * 2 + [VMEM] * (len(pieces) - 1),
         out_specs=(VMEM, VMEM, VMEM),
         scratch_shapes=[wide, pltpu.VMEM(embeddings.shape, jnp.bfloat16), pltpu.SemaphoreType.DMA((2,))],
-        compiler_params=params(16),
+        compiler_params=params(12),
         name="panel",
     )(row_list, row_half, pair_list, pair_quarter, places, embeddings, *pieces)
 
     for sweep in range(ITERS):
-        parts = [row_part] + [swap(row_part, "proto", 2 * j) for j in range(1, lines)]
-        column_part, row_potential = pl.pallas_call(
-            column_kernel,
-            out_shape=(column_shape, row_shape),
-            in_specs=[SMEM] * 2 + [VMEM] * (1 + len(parts)),
-            out_specs=(VMEM, VMEM),
-            scratch_shapes=[wide, tall],
-            compiler_params=params(8),
-            name="column_pass",
-        )(column_list, column_half, similar, *parts)
-        parts = [column_part] + [swap(column_part, "row", j) for j in range(1, n_row)]
+        parts = [row_part] + [swap(row_part, "proto", 2 * j) for j in range(lines - 1, 0, -1)]
+        parts = parts[:1] + parts[:0:-1]
+        if sweep == 0:
+            column_part, row_potential, kept, peaks = pl.pallas_call(
+                first_column_kernel,
+                out_shape=(column_shape, row_shape, pltpu.VMEM(panel.shape, jnp.bfloat16), column_shape),
+                in_specs=[SMEM] * 2 + [VMEM] * (1 + len(parts)),
+                out_specs=(VMEM,) * 4,
+                scratch_shapes=[wide, tall],
+                compiler_params=params(4),
+                name="first_column_pass",
+            )(column_list, column_half, similar, *parts)
+            first_row = row_potential
+        else:
+            column_part, row_potential = pl.pallas_call(
+                column_kernel,
+                out_shape=(column_shape, row_shape),
+                in_specs=[SMEM] * 3 + [VMEM] * (4 + len(parts)),
+                out_specs=(VMEM, VMEM),
+                scratch_shapes=[wide, tall],
+                compiler_params=params(4),
+                name="column_pass",
+            )(column_list, column_half, column_quarter, similar, kept, peaks, first_row, *parts)
+        parts = [column_part] + [swap(column_part, "row", j) for j in range(n_row - 1, 0, -1)]
+        parts = parts[:1] + parts[:0:-1]
         if sweep < ITERS - 1:
+            factors = pltpu.VMEM((columns + 8, TILE), jnp.float32)
             row_part = pl.pallas_call(
                 functools.partial(row_kernel, log_column),
                 out_shape=row_shape,
-                in_specs=[SMEM] * 2 + [VMEM] * (1 + len(parts)),
+                in_specs=[SMEM] * 3 + [VMEM] * (4 + len(parts)),
                 out_specs=VMEM,
-                scratch_shapes=[pltpu.VMEM((columns + 8, TILE), jnp.float32), wide],
-                compiler_params=params(8),
+                scratch_shapes=[factors, factors, wide],
+                compiler_params=params(4),
                 name="row_pass",
-            )(row_list, row_half, similar, *parts)
+            )(row_list, row_half, row_quarter, similar, kept, peaks, first_row, *parts)
     half = columns // 2
     *blocks, column_potential = pl.pallas_call(
         functools.partial(plan_kernel, log_column, lines),
@@ -352,7 +477,7 @@
             wide,
             pltpu.VMEM((row_tiles, TILE, lines * width), jnp.float32),
         ],
-        compiler_params=params(16),
+        compiler_params=params(12),
         name="plan",
     )(pair_list, pair_quarter, mask, places, similar, row_potential, whole, *parts)
     targets = scatter_partials(blocks)

time: 148 us -> 142 us (0.959); the launches traced: 145 us -> 142 us
  Pallas kernels: 31 us -> 29.5 us
  starting transfers between devices: 42.8 us -> 41.3 us
    pallas_call x3 -> x2, Pallas kernels: 10.1 us -> 6.61 us  [shards(): pl.pallas_call(column_kernel, out_shape=(column_shape, row_shape), in_spe...]
    pallas_call x0 -> x1, Pallas kernels: none -> 2.83 us  [shards(): pl.pallas_call(first_column_kernel, out_shape=(column_shape, row_shape, p...]
    ppermute x35, starting transfers between devices: 42.8 us -> 41.3 us  [swap(): return lax.ppermute(x, axis, [(i, i ^ offset) for i in range(size)])]
  transfers between devices with their start and end apart: 35 -> 35, of which waited for: 24 -> 26; matrix products, arithmetic and copies ran while one was open for 2% -> 2% of each run, Pallas kernels for 0% -> 0%
where the time goes in v6:
time: 142 us
  waiting for transfers between devices  61.1 us (43%)
  starting transfers between devices  41.3 us (29%)
  Pallas kernels  29.5 us (21%)
  local copies, waits for them, and re-layouts  5.9 us (4%)
  other arithmetic  3.2 us (2%)
    ppermute x35, waiting for transfers between devices, swap(): return lax.ppermute(x, axis, [(i, i ^ offset) for i in range(size)])  61.1 us
    ppermute x35, starting transfers between devices, swap(): return lax.ppermute(x, axis, [(i, i ^ offset) for i in range(size)])  41.3 us
    pallas_call x1, Pallas kernels, shards(): pl.pallas_call(functools.partial(panel_kernel, firsts), out_shape=(panel,...  8.91 us
    pallas_call x2, Pallas kernels, shards(): pl.pallas_call(column_kernel, out_shape=(column_shape, row_shape), in_spe...  6.61 us
    pallas_call x1, Pallas kernels, shards(): pl.pallas_call(functools.partial(plan_kernel, log_column, lines), out_sha...  6.13 us
    pallas_call x2, Pallas kernels, shards(): pl.pallas_call(functools.partial(row_kernel, log_column), out_shape=row_s...  4.97 us
    unnamed x7, local copies, waits for them, and re-layouts  4.68 us
  transfers between devices with their start and end apart: 35, of which 26 were waited for; matrix products, arithmetic and copies ran while one was open for 2% of the time, Pallas kernels for 0%

profile of v6, /device:TPU:0, one launch (start us, length us, event | category | flops | bytes accessed | tf_op | source)
XLA Modules:
  0.0 141.7 jit_solution(5967436777731400880)
XLA Ops:
  1.8 1.1 fusion.4
  2.9 2.6 %collective-permute-start.2 = (bf16[512,256]{1,0:T(8,128)(2,1)S(1)}, bf16[512,256]{1,0:T(8,128)(2,1)S(1)}, u32[]{:S(2)}, u32[]{:S(2)}) collective-permute-start(bf16[512,256]{1,0:T(8,128)(2,1)S(1)} %get-tuple-element.22), channel_id=1, source_target_pairs={{0,16},{8,24},{16,0},{24,8},{1,17},{9,25},{17,1},{25,9},{2,18},{10... | collective-permute-start | bytes 786440 | tf_op jit(solution)/shard_map/ppermute | solution.py:22
  5.5 1.5 %collective-permute-start.1 = (bf16[512,256]{1,0:T(8,128)(2,1)S(1)}, bf16[512,256]{1,0:T(8,128)(2,1)S(1)}, u32[]{:S(2)}, u32[]{:S(2)}) collective-permute-start(bf16[512,256]{1,0:T(8,128)(2,1)S(1)} %get-tuple-element.25), channel_id=1, source_target_pairs={{0,8},{8,0},{16,24},{24,16},{1,9},{9,1},{17,25},{25,17},{2,10},{10... | collective-permute-start | bytes 786440 | tf_op jit(solution)/shard_map/ppermute | solution.py:22
  8.7 3.8 %collective-permute-done.2.refs_3_ = bf16[512,256]{1,0:T(8,128)(2,1)S(1)} collective-permute-done((bf16[512,256]{1,0:T(8,128)(2,1)S(1)}, bf16[512,256]{1,0:T(8,128)(2,1)S(1)}, u32[]{:S(2)}, u32[]{:S(2)}) %collective-permute-start.2) | collective-permute-done | bytes 262176 | tf_op jit(solution)/shard_map/ppermute | solution.py:22
  12.5 1.5 %collective-permute-done.1.refs_2_ = bf16[512,256]{1,0:T(8,128)(2,1)S(1)} collective-permute-done((bf16[512,256]{1,0:T(8,128)(2,1)S(1)}, bf16[512,256]{1,0:T(8,128)(2,1)S(1)}, u32[]{:S(2)}, u32[]{:S(2)}) %collective-permute-start.1) | collective-permute-done | bytes 262176 | tf_op jit(solution)/shard_map/ppermute | solution.py:22
  13.9 1.5 %collective-permute-start.3 = (bf16[512,256]{1,0:T(8,128)(2,1)S(1)}, bf16[512,256]{1,0:T(8,128)(2,1)S(1)}, u32[]{:S(2)}, u32[]{:S(2)}) collective-permute-start(bf16[512,256]{1,0:T(8,128)(2,1)S(1)} %get-tuple-element.22), channel_id=1, source_target_pairs={{0,8},{8,0},{16,24},{24,16},{1,9},{9,1},{17,25},{25,17},{2,10},{10... | collective-permute-start | bytes 786440 | tf_op jit(solution)/shard_map/ppermute | solution.py:22
  16.5 1.6 %collective-permute-start.6 = (bf16[512,256]{1,0:T(8,128)(2,1)S(1)}, bf16[512,256]{1,0:T(8,128)(2,1)S(1)}, u32[]{:S(2)}, u32[]{:S(2)}) collective-permute-start(bf16[512,256]{1,0:T(8,128)(2,1)S(1)} %collective-permute-done.1.refs_2_), channel_id=1, source_target_pairs={{0,16},{8,24},{16,0},{24,8},{1,17},{9,25},{17,1},{25,9},{2,18},{10... | collective-permute-start | bytes 786440 | tf_op jit(solution)/shard_map/ppermute | solution.py:22
  18.3 3.3 %collective-permute-done.3.refs_1_ = bf16[512,256]{1,0:T(8,128)(2,1)S(1)} collective-permute-done((bf16[512,256]{1,0:T(8,128)(2,1)S(1)}, bf16[512,256]{1,0:T(8,128)(2,1)S(1)}, u32[]{:S(2)}, u32[]{:S(2)}) %collective-permute-start.3) | collective-permute-done | bytes 262176 | tf_op jit(solution)/shard_map/ppermute | solution.py:22
  21.5 1.5 %collective-permute-start.5 = (bf16[512,256]{1,0:T(8,128)(2,1)S(1)}, bf16[512,256]{1,0:T(8,128)(2,1)S(1)}, u32[]{:S(2)}, u32[]{:S(2)}) collective-permute-start(bf16[512,256]{1,0:T(8,128)(2,1)S(1)} %collective-permute-done.2.refs_3_), channel_id=1, source_target_pairs={{0,8},{8,0},{16,24},{24,16},{1,9},{9,1},{17,25},{25,17},{2,10},{10... | collective-permute-start | bytes 786440 | tf_op jit(solution)/shard_map/ppermute | solution.py:22
  23.0 1.9 %collective-permute-done.4.refs_4_ = bf16[512,256]{1,0:T(8,128)(2,1)S(1)} collective-permute-done((bf16[512,256]{1,0:T(8,128)(2,1)S(1)}, bf16[512,256]{1,0:T(8,128)(2,1)S(1)}, u32[]{:S(2)}, u32[]{:S(2)}) %collective-permute-start.4) | collective-permute-done | bytes 262176 | tf_op jit(solution)/shard_map/ppermute | solution.py:22
  25.7 3.0 %collective-permute-done.6.refs_6_ = bf16[512,256]{1,0:T(8,128)(2,1)S(1)} collective-permute-done((bf16[512,256]{1,0:T(8,128)(2,1)S(1)}, bf16[512,256]{1,0:T(8,128)(2,1)S(1)}, u32[]{:S(2)}, u32[]{:S(2)}) %collective-permute-start.6) | collective-permute-done | bytes 262176 | tf_op jit(solution)/shard_map/ppermute | solution.py:22
  30.9 2.2 %copy-done = bf16[2048,1024]{1,0:T(8,128)(2,1)S(1)} copy-done((bf16[2048,1024]{1,0:T(8,128)(2,1)S(1)}, bf16[2048,1024]{1,0:T(8,128)(2,1)}, u32[]{:S(2)}) %copy-start) | copy-done | bytes 4194328
  33.1 1.0 copy-done.1
  34.2 8.9 %panel.1 = (f32[257,128,128]{2,1,0:T(8,128)S(1)}, bf16[2048,1024]{1,0:T(8,128)(2,1)S(1)}, f32[16,128]{1,0:T(8,128)S(1)}) custom-call(s32[16,16]{1,0:T(8,128)S(1)} %broadcast_add_fusion.1.list_ref, s32[16]{0:T(128)S(1)} %get-tuple-element.51.half_ref, s32[8,16]{1,0:T(8,128)S(1)} %broadcast_add_fusion.2.plist_ref, s32[8]{0:T(128)S(1)} %and_select_fusion.4.pquarter_ref, ...), custom_call_target="tpu_custom_call" | custom-call | tf_op jit(solution)/shard_map/panel/pallas_call | solution.py:421
  43.1 4.5 %collective-permute-start.16 = (f32[16,128]{1,0:T(8,128)S(1)}, f32[16,128]{1,0:T(8,128)S(1)}, u32[]{:S(2)}, u32[]{:S(2)}) collective-permute-start(f32[16,128]{1,0:T(8,128)S(1)} %get-tuple-element.27.refs_0_), channel_id=1, source_target_pairs={{0,6},{1,7},{2,4},{3,5},{4,2},{5,3},{6,0},{7,1},{8,14},{9,15},{10,... | collective-permute-start | bytes 24584 | tf_op jit(solution)/shard_map/ppermute | solution.py:22
  48.2 1.0 collective-permute-done.16.refs_3_
  49.2 2.9 %collective-permute-done.15.refs_2_ = f32[16,128]{1,0:T(8,128)S(1)} collective-permute-done((f32[16,128]{1,0:T(8,128)S(1)}, f32[16,128]{1,0:T(8,128)S(1)}, u32[]{:S(2)}, u32[]{:S(2)}) %collective-permute-start.15) | collective-permute-done | bytes 8224 | tf_op jit(solution)/shard_map/ppermute | solution.py:22
  52.1 2.8 %first_column_pass.1 = (f32[16,128]{1,0:T(8,128)S(1)}, f32[16,128]{1,0:T(8,128)S(1)}, bf16[257,128,128]{2,1,0:T(8,128)(2,1)S(1)}, f32[16,128]{1,0:T(8,128)S(1)}) custom-call(s32[16,16]{1,0:T(8,128)S(1)} %broadcast_add_fusion.list_ref, s32[16]{0:T(128)S(1)} %get-tuple-element.53.half_ref, f32[257,128,128]{2,1,0:T(8,128)S(1)} %get-tuple-element.26.s_ref, ...), custom_call_target="tpu_custom_call" | custom-call | tf_op jit(solution)/shard_map/first_column_pass/pallas_call | solution.py:435
  55.0 6.1 %collective-permute-start.19 = (f32[16,128]{1,0:T(8,128)S(1)}, f32[16,128]{1,0:T(8,128)S(1)}, u32[]{:S(2)}, u32[]{:S(2)}) collective-permute-start(f32[16,128]{1,0:T(8,128)S(1)} %get-tuple-element.31.refs_0_), channel_id=1, source_target_pairs={{0,24},{8,16},{16,8},{24,0},{1,25},{9,17},{17,9},{25,1},{2,26},{10... | collective-permute-start | bytes 24584 | tf_op jit(solution)/shard_map/ppermute | solution.py:22
  61.7 1.0 collective-permute-done.19.refs_3_
  62.7 2.0 %collective-permute-done.18.refs_2_ = f32[16,128]{1,0:T(8,128)S(1)} collective-permute-done((f32[16,128]{1,0:T(8,128)S(1)}, f32[16,128]{1,0:T(8,128)S(1)}, u32[]{:S(2)}, u32[]{:S(2)}) %collective-permute-start.18) | collective-permute-done | bytes 8224 | tf_op jit(solution)/shard_map/ppermute | solution.py:22
  64.7 2.5 %row_pass.2.refs_0_ = f32[16,128]{1,0:T(8,128)S(1)} custom-call(s32[16,16]{1,0:T(8,128)S(1)} %broadcast_add_fusion.1.list_ref, s32[16]{0:T(128)S(1)} %get-tuple-element.51.half_ref, s32[16]{0:T(128)S(1)} %get-tuple-element.50.quarter_ref, f32[257,128,128]{2,1,0:T(8,128)S(1)} %get-tuple-element.26.s_ref, bf16[257,128,128]{2,1,0:T(8,128)(2,1)S(1)} %get-tuple-element.28.w_ref, ...), custom_call_target="tpu_custom_call" | custom-call | tf_op jit(solution)/shard_map/row_pass/pallas_call | solution.py:459
  67.8 2.1 %collective-permute-start.21 = (f32[16,128]{1,0:T(8,128)S(1)}, f32[16,128]{1,0:T(8,128)S(1)}, u32[]{:S(2)}, u32[]{:S(2)}) collective-permute-start(f32[16,128]{1,0:T(8,128)S(1)} %row_pass.2.refs_0_), channel_id=1, source_target_pairs={{0,4},{1,5},{2,6},{3,7},{4,0},{5,1},{6,2},{7,3},{8,12},{9,13},{10,... | collective-permute-start | bytes 24584 | tf_op jit(solution)/shard_map/ppermute | solution.py:22
  69.9 1.8 %collective-permute-start.20 = (f32[16,128]{1,0:T(8,128)S(1)}, f32[16,128]{1,0:T(8,128)S(1)}, u32[]{:S(2)}, u32[]{:S(2)}) collective-permute-start(f32[16,128]{1,0:T(8,128)S(1)} %row_pass.2.refs_0_), channel_id=1, source_target_pairs={{0,2},{1,3},{2,0},{3,1},{4,6},{5,7},{6,4},{7,5},{8,10},{9,11},{10,... | collective-permute-start | bytes 24584 | tf_op jit(solution)/shard_map/ppermute | solution.py:22
  71.7 1.1 collective-permute-done.22.refs_3_
  73.6 3.4 %column_pass.2 = (f32[16,128]{1,0:T(8,128)S(1)}, f32[16,128]{1,0:T(8,128)}) custom-call(s32[16,16]{1,0:T(8,128)S(1)} %broadcast_add_fusion.list_ref, s32[16]{0:T(128)S(1)} %get-tuple-element.53.half_ref, s32[16]{0:T(128)S(1)} %get-tuple-element.52.quarter_ref, f32[257,128,128]{2,1,0:T(8,128)S(1)} %get-tuple-element.26.s_ref, ...), custom_call_target="tpu_custom_call" | custom-call | tf_op jit(solution)/shard_map/column_pass/pallas_call | solution.py:446
  77.0 1.4 collective-permute-start.25
  78.4 0.9 collective-permute-start.24
  79.3 1.2 collective-permute-start.23
  80.5 1.1 collective-permute-done.25.refs_3_
  82.0 0.9 collective-permute-done.23.refs_1_
  82.9 2.5 %row_pass.3.refs_0_ = f32[16,128]{1,0:T(8,128)S(1)} custom-call(s32[16,16]{1,0:T(8,128)S(1)} %broadcast_add_fusion.1.list_ref, s32[16]{0:T(128)S(1)} %get-tuple-element.51.half_ref, s32[16]{0:T(128)S(1)} %get-tuple-element.50.quarter_ref, f32[257,128,128]{2,1,0:T(8,128)S(1)} %get-tuple-element.26.s_ref, bf16[257,128,128]{2,1,0:T(8,128)(2,1)S(1)} %get-tuple-element.28.w_ref, ...), custom_call_target="tpu_custom_call" | custom-call | tf_op jit(solution)/shard_map/row_pass/pallas_call | solution.py:459
  85.4 2.0 %collective-permute-start.28 = (f32[16,128]{1,0:T(8,128)S(1)}, f32[16,128]{1,0:T(8,128)S(1)}, u32[]{:S(2)}, u32[]{:S(2)}) collective-permute-start(f32[16,128]{1,0:T(8,128)S(1)} %row_pass.3.refs_0_), channel_id=1, source_target_pairs={{0,6},{1,7},{2,4},{3,5},{4,2},{5,3},{6,0},{7,1},{8,14},{9,15},{10,... | collective-permute-start | bytes 24584 | tf_op jit(solution)/shard_map/ppermute | solution.py:22
  87.4 1.2 collective-permute-start.27
  88.6 1.3 collective-permute-start.26
  89.9 1.1 collective-permute-done.28.refs_3_
  90.9 1.0 collective-permute-done.27.refs_2_
  92.3 3.2 %column_pass.3 = (f32[16,128]{1,0:T(8,128)S(1)}, f32[16,128]{1,0:T(8,128)}) custom-call(s32[16,16]{1,0:T(8,128)S(1)} %broadcast_add_fusion.list_ref, s32[16]{0:T(128)S(1)} %get-tuple-element.53.half_ref, s32[16]{0:T(128)S(1)} %get-tuple-element.52.quarter_ref, f32[257,128,128]{2,1,0:T(8,128)S(1)} %get-tuple-element.26.s_ref, ...), custom_call_target="tpu_custom_call" | custom-call | tf_op jit(solution)/shard_map/column_pass/pallas_call | solution.py:446
  95.5 2.6 %collective-permute-start.31 = (f32[16,128]{1,0:T(8,128)S(1)}, f32[16,128]{1,0:T(8,128)S(1)}, u32[]{:S(2)}, u32[]{:S(2)}) collective-permute-start(f32[16,128]{1,0:T(8,128)S(1)} %get-tuple-element.35.refs_0_), channel_id=1, source_target_pairs={{0,24},{8,16},{16,8},{24,0},{1,25},{9,17},{17,9},{25,1},{2,26},{10... | collective-permute-start | bytes 24584 | tf_op jit(solution)/shard_map/ppermute | solution.py:22
  99.0 1.1 collective-permute-done.31.refs_3_
  100.0 1.7 %collective-permute-done.30.refs_2_ = f32[16,128]{1,0:T(8,128)S(1)} collective-permute-done((f32[16,128]{1,0:T(8,128)S(1)}, f32[16,128]{1,0:T(8,128)S(1)}, u32[]{:S(2)}, u32[]{:S(2)}) %collective-permute-start.30) | collective-permute-done | bytes 8224 | tf_op jit(solution)/shard_map/ppermute | solution.py:22
  102.8 6.1 %plan.1 = (bf16[2048,128]{1,0:T(8,128)(2,1)S(1)}, bf16[2048,128]{1,0:T(8,128)(2,1)S(1)}, bf16[2048,128]{1,0:T(8,128)(2,1)S(1)}, bf16[2048,128]{1,0:T(8,128)(2,1)S(1)}, f32[8,128]{1,0:T(8,128)}) custom-call(s32[8,16]{1,0:T(8,128)S(1)} %broadcast_add_fusion.2.plist_ref, s32[8]{0:T(128)S(1)} %and_select_fusion.4.pquarter_ref, ...), custom_call_target="tpu_custom_call" | custom-call | tf_op jit(solution)/shard_map/plan/pallas_call | solution.py:469
  109.0 1.1 collective-permute-start.33
  110.1 0.9 collective-permute-start.32
  111.0 13.7 %collective-permute-done.33 = bf16[2048,128]{1,0:T(8,128)(2,1)S(1)} collective-permute-done((bf16[2048,128]{1,0:T(8,128)(2,1)S(1)}, bf16[2048,128]{1,0:T(8,128)(2,1)S(1)}, u32[]{:S(2)}, u32[]{:S(2)}) %collective-permute-start.33) | collective-permute-done | bytes 524320 | tf_op jit(solution)/shard_map/ppermute | solution.py:22
  125.3 6.8 %collective-permute-done.32 = bf16[2048,128]{1,0:T(8,128)(2,1)S(1)} collective-permute-done((bf16[2048,128]{1,0:T(8,128)(2,1)S(1)}, bf16[2048,128]{1,0:T(8,128)(2,1)S(1)}, u32[]{:S(2)}, u32[]{:S(2)}) %collective-permute-start.32) | collective-permute-done | bytes 524320 | tf_op jit(solution)/shard_map/ppermute | solution.py:22
  132.1 8.6 %collective-permute-done.34 = bf16[2048,128]{1,0:T(8,128)(2,1)S(1)} collective-permute-done((bf16[2048,128]{1,0:T(8,128)(2,1)S(1)}, bf16[2048,128]{1,0:T(8,128)(2,1)S(1)}, u32[]{:S(2)}, u32[]{:S(2)}) %collective-permute-start.34) | collective-permute-done | bytes 524320 | tf_op jit(solution)/shard_map/ppermute | solution.py:22
  140.7 1.0 add_convert_fusion
  (60 shorter events, 13.2 us)
Async XLA Ops:
  1.4 5.7 %collective-permute-start = (s32[16,8]{1,0:T(8,128)S(1)}, s32[16,8]{1,0:T(8,128)S(1)}, u32[]{:S(2)}, u32[]{:S(2)}) collective-permute-start(s32[16,8]{1,0:T(8,128)S(1)} %copy.9), channel_id=1, source_target_pairs={{0,1},{1,0},{2,3},{3,2},{4,5},{5,4},{6,7},{7,6},{8,9},{9,8},{10,11... | collective-permute-start | bytes 1544 | tf_op jit(solution)/shard_map/ppermute | solution.py:22
  2.9 9.6 %collective-permute-start.2 = (bf16[512,256]{1,0:T(8,128)(2,1)S(1)}, bf16[512,256]{1,0:T(8,128)(2,1)S(1)}, u32[]{:S(2)}, u32[]{:S(2)}) collective-permute-start(bf16[512,256]{1,0:T(8,128)(2,1)S(1)} %get-tuple-element.22), channel_id=1, source_target_pairs={{0,16},{8,24},{16,0},{24,8},{1,17},{9,25},{17,1},{25,9},{2,18},{10... | collective-permute-start | bytes 786440 | tf_op jit(solution)/shard_map/ppermute | solution.py:22
  5.5 8.4 %collective-permute-start.1 = (bf16[512,256]{1,0:T(8,128)(2,1)S(1)}, bf16[512,256]{1,0:T(8,128)(2,1)S(1)}, u32[]{:S(2)}, u32[]{:S(2)}) collective-permute-start(bf16[512,256]{1,0:T(8,128)(2,1)S(1)} %get-tuple-element.25), channel_id=1, source_target_pairs={{0,8},{8,0},{16,24},{24,16},{1,9},{9,1},{17,25},{25,17},{2,10},{10... | collective-permute-start | bytes 786440 | tf_op jit(solution)/shard_map/ppermute | solution.py:22
  13.9 7.6 %collective-permute-start.3 = (bf16[512,256]{1,0:T(8,128)(2,1)S(1)}, bf16[512,256]{1,0:T(8,128)(2,1)S(1)}, u32[]{:S(2)}, u32[]{:S(2)}) collective-permute-start(bf16[512,256]{1,0:T(8,128)(2,1)S(1)} %get-tuple-element.22), channel_id=1, source_target_pairs={{0,8},{8,0},{16,24},{24,16},{1,9},{9,1},{17,25},{25,17},{2,10},{10... | collective-permute-start | bytes 786440 | tf_op jit(solution)/shard_map/ppermute | solution.py:22
  15.6 9.3 %collective-permute-start.4 = (bf16[512,256]{1,0:T(8,128)(2,1)S(1)}, bf16[512,256]{1,0:T(8,128)(2,1)S(1)}, u32[]{:S(2)}, u32[]{:S(2)}) collective-permute-start(bf16[512,256]{1,0:T(8,128)(2,1)S(1)} %get-tuple-element.25), channel_id=1, source_target_pairs={{0,16},{8,24},{16,0},{24,8},{1,17},{9,25},{17,1},{25,9},{2,18},{10... | collective-permute-start | bytes 786440 | tf_op jit(solution)/shard_map/ppermute | solution.py:22
  16.4 8.7 %collective-permute-start.9 = (bf16[512,256]{1,0:T(8,128)(2,1)S(1)}, bf16[512,256]{1,0:T(8,128)(2,1)S(1)}, u32[]{:S(2)}, u32[]{:S(2)}) collective-permute-start(bf16[512,256]{1,0:T(8,128)(2,1)S(1)} %collective-permute-done.1.refs_2_), channel_id=1, source_target_pairs={{0,1},{1,0},{2,3},{3,2},{4,5},{5,4},{6,7},{7,6},{8,9},{9,8},{10,11... | collective-permute-start | bytes 786440 | tf_op jit(solution)/shard_map/ppermute | solution.py:22
  16.5 12.2 %collective-permute-start.6 = (bf16[512,256]{1,0:T(8,128)(2,1)S(1)}, bf16[512,256]{1,0:T(8,128)(2,1)S(1)}, u32[]{:S(2)}, u32[]{:S(2)}) collective-permute-start(bf16[512,256]{1,0:T(8,128)(2,1)S(1)} %collective-permute-done.1.refs_2_), channel_id=1, source_target_pairs={{0,16},{8,24},{16,0},{24,8},{1,17},{9,25},{17,1},{25,9},{2,18},{10... | collective-permute-start | bytes 786440 | tf_op jit(solution)/shard_map/ppermute | solution.py:22
  18.1 10.6 %collective-permute-start.10 = (bf16[512,256]{1,0:T(8,128)(2,1)S(1)}, bf16[512,256]{1,0:T(8,128)(2,1)S(1)}, u32[]{:S(2)}, u32[]{:S(2)}) collective-permute-start(bf16[512,256]{1,0:T(8,128)(2,1)S(1)} %collective-permute-done.2.refs_3_), channel_id=1, source_target_pairs={{0,1},{1,0},{2,3},{3,2},{4,5},{5,4},{6,7},{7,6},{8,9},{9,8},{10,11... | collective-permute-start | bytes 786440 | tf_op jit(solution)/shard_map/ppermute | solution.py:22
  21.5 7.6 %collective-permute-start.5 = (bf16[512,256]{1,0:T(8,128)(2,1)S(1)}, bf16[512,256]{1,0:T(8,128)(2,1)S(1)}, u32[]{:S(2)}, u32[]{:S(2)}) collective-permute-start(bf16[512,256]{1,0:T(8,128)(2,1)S(1)} %collective-permute-done.2.refs_3_), channel_id=1, source_target_pairs={{0,8},{8,0},{16,24},{24,16},{1,9},{9,1},{17,25},{25,17},{2,10},{10... | collective-permute-start | bytes 786440 | tf_op jit(solution)/shard_map/ppermute | solution.py:22
  24.9 4.3 %collective-permute-start.7 = (bf16[1024,256]{1,0:T(8,128)(2,1)}, bf16[1024,256]{1,0:T(8,128)(2,1)S(1)}, u32[]{:S(2)}, u32[]{:S(2)}) collective-permute-start(bf16[1024,256]{1,0:T(8,128)(2,1)} %refs_0_.1), channel_id=1, source_target_pairs={{0,1},{1,0},{2,3},{3,2},{4,5},{5,4},{6,7},{7,6},{8,9},{9,8},{10,11... | collective-permute-start | bytes 1572872 | tf_op jit(solution)/shard_map/ppermute | solution.py:22
  25.1 4.2 %collective-permute-start.8 = (bf16[512,256]{1,0:T(8,128)(2,1)S(1)}, bf16[512,256]{1,0:T(8,128)(2,1)S(1)}, u32[]{:S(2)}, u32[]{:S(2)}) collective-permute-start(bf16[512,256]{1,0:T(8,128)(2,1)S(1)} %collective-permute-done.3.refs_1_), channel_id=1, source_target_pairs={{0,1},{1,0},{2,3},{3,2},{4,5},{5,4},{6,7},{7,6},{8,9},{9,8},{10,11... | collective-permute-start | bytes 786440 | tf_op jit(solution)/shard_map/ppermute | solution.py:22
  28.7 1.5 %collective-permute-start.11 = (bf16[512,256]{1,0:T(8,128)(2,1)S(1)}, bf16[512,256]{1,0:T(8,128)(2,1)S(1)}, u32[]{:S(2)}, u32[]{:S(2)}) collective-permute-start(bf16[512,256]{1,0:T(8,128)(2,1)S(1)} %collective-permute-done.4.refs_4_), channel_id=1, source_target_pairs={{0,1},{1,0},{2,3},{3,2},{4,5},{5,4},{6,7},{7,6},{8,9},{9,8},{10,11... | collective-permute-start | bytes 786440 | tf_op jit(solution)/shard_map/ppermute | solution.py:22
  28.7 1.9 %collective-permute-start.13 = (bf16[512,256]{1,0:T(8,128)(2,1)S(1)}, bf16[512,256]{1,0:T(8,128)(2,1)S(1)}, u32[]{:S(2)}, u32[]{:S(2)}) collective-permute-start(bf16[512,256]{1,0:T(8,128)(2,1)S(1)} %collective-permute-done.6.refs_6_), channel_id=1, source_target_pairs={{0,1},{1,0},{2,3},{3,2},{4,5},{5,4},{6,7},{7,6},{8,9},{9,8},{10,11... | collective-permute-start | bytes 786440 | tf_op jit(solution)/shard_map/ppermute | solution.py:22
  29.2 1.8 %collective-permute-start.12 = (bf16[512,256]{1,0:T(8,128)(2,1)S(1)}, bf16[512,256]{1,0:T(8,128)(2,1)S(1)}, u32[]{:S(2)}, u32[]{:S(2)}) collective-permute-start(bf16[512,256]{1,0:T(8,128)(2,1)S(1)} %collective-permute-done.5.refs_5_), channel_id=1, source_target_pairs={{0,1},{1,0},{2,3},{3,2},{4,5},{5,4},{6,7},{7,6},{8,9},{9,8},{10,11... | collective-permute-start | bytes 786440 | tf_op jit(solution)/shard_map/ppermute | solution.py:22
  30.9 2.2 %copy-start = (bf16[2048,1024]{1,0:T(8,128)(2,1)S(1)}, bf16[2048,1024]{1,0:T(8,128)(2,1)}, u32[]{:S(2)}) copy-start(bf16[2048,1024]{1,0:T(8,128)(2,1)} %e_hbm_ref.1) | copy-start | bytes 12582916
  33.1 1.0 copy-start.1
  43.1 6.1 %collective-permute-start.16 = (f32[16,128]{1,0:T(8,128)S(1)}, f32[16,128]{1,0:T(8,128)S(1)}, u32[]{:S(2)}, u32[]{:S(2)}) collective-permute-start(f32[16,128]{1,0:T(8,128)S(1)} %get-tuple-element.27.refs_0_), channel_id=1, source_target_pairs={{0,6},{1,7},{2,4},{3,5},{4,2},{5,3},{6,0},{7,1},{8,14},{9,15},{10,... | collective-permute-start | bytes 24584 | tf_op jit(solution)/shard_map/ppermute | solution.py:22
  47.6 4.5 %collective-permute-start.15 = (f32[16,128]{1,0:T(8,128)S(1)}, f32[16,128]{1,0:T(8,128)S(1)}, u32[]{:S(2)}, u32[]{:S(2)}) collective-permute-start(f32[16,128]{1,0:T(8,128)S(1)} %get-tuple-element.27.refs_0_), channel_id=1, source_target_pairs={{0,4},{1,5},{2,6},{3,7},{4,0},{5,1},{6,2},{7,3},{8,12},{9,13},{10,... | collective-permute-start | bytes 24584 | tf_op jit(solution)/shard_map/ppermute | solution.py:22
  47.6 4.5 %collective-permute-start.14 = (f32[16,128]{1,0:T(8,128)S(1)}, f32[16,128]{1,0:T(8,128)S(1)}, u32[]{:S(2)}, u32[]{:S(2)}) collective-permute-start(f32[16,128]{1,0:T(8,128)S(1)} %get-tuple-element.27.refs_0_), channel_id=1, source_target_pairs={{0,2},{1,3},{2,0},{3,1},{4,6},{5,7},{6,4},{7,5},{8,10},{9,11},{10,... | collective-permute-start | bytes 24584 | tf_op jit(solution)/shard_map/ppermute | solution.py:22
  55.0 7.7 %collective-permute-start.19 = (f32[16,128]{1,0:T(8,128)S(1)}, f32[16,128]{1,0:T(8,128)S(1)}, u32[]{:S(2)}, u32[]{:S(2)}) collective-permute-start(f32[16,128]{1,0:T(8,128)S(1)} %get-tuple-element.31.refs_0_), channel_id=1, source_target_pairs={{0,24},{8,16},{16,8},{24,0},{1,25},{9,17},{17,9},{25,1},{2,26},{10... | collective-permute-start | bytes 24584 | tf_op jit(solution)/shard_map/ppermute | solution.py:22
  61.1 3.7 %collective-permute-start.18 = (f32[16,128]{1,0:T(8,128)S(1)}, f32[16,128]{1,0:T(8,128)S(1)}, u32[]{:S(2)}, u32[]{:S(2)}) collective-permute-start(f32[16,128]{1,0:T(8,128)S(1)} %get-tuple-element.31.refs_0_), channel_id=1, source_target_pairs={{0,16},{8,24},{16,0},{24,8},{1,17},{9,25},{17,1},{25,9},{2,18},{10... | collective-permute-start | bytes 24584 | tf_op jit(solution)/shard_map/ppermute | solution.py:22
  61.1 3.7 %collective-permute-start.17 = (f32[16,128]{1,0:T(8,128)S(1)}, f32[16,128]{1,0:T(8,128)S(1)}, u32[]{:S(2)}, u32[]{:S(2)}) collective-permute-start(f32[16,128]{1,0:T(8,128)S(1)} %get-tuple-element.31.refs_0_), channel_id=1, source_target_pairs={{0,8},{8,0},{16,24},{24,16},{1,9},{9,1},{17,25},{25,17},{2,10},{10... | collective-permute-start | bytes 24584 | tf_op jit(solution)/shard_map/ppermute | solution.py:22
  67.2 5.5 %collective-permute-start.22 = (f32[16,128]{1,0:T(8,128)S(1)}, f32[16,128]{1,0:T(8,128)S(1)}, u32[]{:S(2)}, u32[]{:S(2)}) collective-permute-start(f32[16,128]{1,0:T(8,128)S(1)} %row_pass.2.refs_0_), channel_id=1, source_target_pairs={{0,6},{1,7},{2,4},{3,5},{4,2},{5,3},{6,0},{7,1},{8,14},{9,15},{10,... | collective-permute-start | bytes 24584 | tf_op jit(solution)/shard_map/ppermute | solution.py:22
  67.8 4.9 %collective-permute-start.21 = (f32[16,128]{1,0:T(8,128)S(1)}, f32[16,128]{1,0:T(8,128)S(1)}, u32[]{:S(2)}, u32[]{:S(2)}) collective-permute-start(f32[16,128]{1,0:T(8,128)S(1)} %row_pass.2.refs_0_), channel_id=1, source_target_pairs={{0,4},{1,5},{2,6},{3,7},{4,0},{5,1},{6,2},{7,3},{8,12},{9,13},{10,... | collective-permute-start | bytes 24584 | tf_op jit(solution)/shard_map/ppermute | solution.py:22
  69.9 3.7 %collective-permute-start.20 = (f32[16,128]{1,0:T(8,128)S(1)}, f32[16,128]{1,0:T(8,128)S(1)}, u32[]{:S(2)}, u32[]{:S(2)}) collective-permute-start(f32[16,128]{1,0:T(8,128)S(1)} %row_pass.2.refs_0_), channel_id=1, source_target_pairs={{0,2},{1,3},{2,0},{3,1},{4,6},{5,7},{6,4},{7,5},{8,10},{9,11},{10,... | collective-permute-start | bytes 24584 | tf_op jit(solution)/shard_map/ppermute | solution.py:22
  77.0 4.5 %collective-permute-start.25 = (f32[16,128]{1,0:T(8,128)S(1)}, f32[16,128]{1,0:T(8,128)S(1)}, u32[]{:S(2)}, u32[]{:S(2)}) collective-permute-start(f32[16,128]{1,0:T(8,128)S(1)} %get-tuple-element.32.refs_0_), channel_id=1, source_target_pairs={{0,24},{8,16},{16,8},{24,0},{1,25},{9,17},{17,9},{25,1},{2,26},{10... | collective-permute-start | bytes 24584 | tf_op jit(solution)/shard_map/ppermute | solution.py:22
  78.4 3.7 %collective-permute-start.24 = (f32[16,128]{1,0:T(8,128)S(1)}, f32[16,128]{1,0:T(8,128)S(1)}, u32[]{:S(2)}, u32[]{:S(2)}) collective-permute-start(f32[16,128]{1,0:T(8,128)S(1)} %get-tuple-element.32.refs_0_), channel_id=1, source_target_pairs={{0,16},{8,24},{16,0},{24,8},{1,17},{9,25},{17,1},{25,9},{2,18},{10... | collective-permute-start | bytes 24584 | tf_op jit(solution)/shard_map/ppermute | solution.py:22
  79.3 3.7 %collective-permute-start.23 = (f32[16,128]{1,0:T(8,128)S(1)}, f32[16,128]{1,0:T(8,128)S(1)}, u32[]{:S(2)}, u32[]{:S(2)}) collective-permute-start(f32[16,128]{1,0:T(8,128)S(1)} %get-tuple-element.32.refs_0_), channel_id=1, source_target_pairs={{0,8},{8,0},{16,24},{24,16},{1,9},{9,1},{17,25},{25,17},{2,10},{10... | collective-permute-start | bytes 24584 | tf_op jit(solution)/shard_map/ppermute | solution.py:22
  85.4 5.5 %collective-permute-start.28 = (f32[16,128]{1,0:T(8,128)S(1)}, f32[16,128]{1,0:T(8,128)S(1)}, u32[]{:S(2)}, u32[]{:S(2)}) collective-permute-start(f32[16,128]{1,0:T(8,128)S(1)} %row_pass.3.refs_0_), channel_id=1, source_target_pairs={{0,6},{1,7},{2,4},{3,5},{4,2},{5,3},{6,0},{7,1},{8,14},{9,15},{10,... | collective-permute-start | bytes 24584 | tf_op jit(solution)/shard_map/ppermute | solution.py:22
  87.4 4.5 %collective-permute-start.27 = (f32[16,128]{1,0:T(8,128)S(1)}, f32[16,128]{1,0:T(8,128)S(1)}, u32[]{:S(2)}, u32[]{:S(2)}) collective-permute-start(f32[16,128]{1,0:T(8,128)S(1)} %row_pass.3.refs_0_), channel_id=1, source_target_pairs={{0,4},{1,5},{2,6},{3,7},{4,0},{5,1},{6,2},{7,3},{8,12},{9,13},{10,... | collective-permute-start | bytes 24584 | tf_op jit(solution)/shard_map/ppermute | solution.py:22
  88.6 3.7 %collective-permute-start.26 = (f32[16,128]{1,0:T(8,128)S(1)}, f32[16,128]{1,0:T(8,128)S(1)}, u32[]{:S(2)}, u32[]{:S(2)}) collective-permute-start(f32[16,128]{1,0:T(8,128)S(1)} %row_pass.3.refs_0_), channel_id=1, source_target_pairs={{0,2},{1,3},{2,0},{3,1},{4,6},{5,7},{6,4},{7,5},{8,10},{9,11},{10,... | collective-permute-start | bytes 24584 | tf_op jit(solution)/shard_map/ppermute | solution.py:22
  95.5 4.5 %collective-permute-start.31 = (f32[16,128]{1,0:T(8,128)S(1)}, f32[16,128]{1,0:T(8,128)S(1)}, u32[]{:S(2)}, u32[]{:S(2)}) collective-permute-start(f32[16,128]{1,0:T(8,128)S(1)} %get-tuple-element.35.refs_0_), channel_id=1, source_target_pairs={{0,24},{8,16},{16,8},{24,0},{1,25},{9,17},{17,9},{25,1},{2,26},{10... | collective-permute-start | bytes 24584 | tf_op jit(solution)/shard_map/ppermute | solution.py:22
  98.0 3.7 %collective-permute-start.30 = (f32[16,128]{1,0:T(8,128)S(1)}, f32[16,128]{1,0:T(8,128)S(1)}, u32[]{:S(2)}, u32[]{:S(2)}) collective-permute-start(f32[16,128]{1,0:T(8,128)S(1)} %get-tuple-element.35.refs_0_), channel_id=1, source_target_pairs={{0,16},{8,24},{16,0},{24,8},{1,17},{9,25},{17,1},{25,9},{2,18},{10... | collective-permute-start | bytes 24584 | tf_op jit(solution)/shard_map/ppermute | solution.py:22
  98.5 3.7 %collective-permute-start.29 = (f32[16,128]{1,0:T(8,128)S(1)}, f32[16,128]{1,0:T(8,128)S(1)}, u32[]{:S(2)}, u32[]{:S(2)}) collective-permute-start(f32[16,128]{1,0:T(8,128)S(1)} %get-tuple-element.35.refs_0_), channel_id=1, source_target_pairs={{0,8},{8,0},{16,24},{24,16},{1,9},{9,1},{17,25},{25,17},{2,10},{10... | collective-permute-start | bytes 24584 | tf_op jit(solution)/shard_map/ppermute | solution.py:22
  102.1 0.7 copy-start.2
  109.0 15.8 %collective-permute-start.33 = (bf16[2048,128]{1,0:T(8,128)(2,1)S(1)}, bf16[2048,128]{1,0:T(8,128)(2,1)S(1)}, u32[]{:S(2)}, u32[]{:S(2)}) collective-permute-start(bf16[2048,128]{1,0:T(8,128)(2,1)S(1)} %get-tuple-element.39), channel_id=1, source_target_pairs={{0,2},{1,3},{2,0},{3,1},{4,6},{5,7},{6,4},{7,5},{8,10},{9,11},{10,... | collective-permute-start | bytes 1572872 | tf_op jit(solution)/shard_map/ppermute | solution.py:22
  110.1 22.0 %collective-permute-start.32 = (bf16[2048,128]{1,0:T(8,128)(2,1)S(1)}, bf16[2048,128]{1,0:T(8,128)(2,1)S(1)}, u32[]{:S(2)}, u32[]{:S(2)}) collective-permute-start(bf16[2048,128]{1,0:T(8,128)(2,1)S(1)} %get-tuple-element.37), channel_id=1, source_target_pairs={{0,2},{1,3},{2,0},{3,1},{4,6},{5,7},{6,4},{7,5},{8,10},{9,11},{10,... | collective-permute-start | bytes 1572872 | tf_op jit(solution)/shard_map/ppermute | solution.py:22
  124.9 15.8 %collective-permute-start.34 = (bf16[2048,128]{1,0:T(8,128)(2,1)S(1)}, bf16[2048,128]{1,0:T(8,128)(2,1)S(1)}, u32[]{:S(2)}, u32[]{:S(2)}) collective-permute-start(bf16[2048,128]{1,0:T(8,128)(2,1)S(1)} %add_convert_fusion.1), channel_id=1, source_target_pairs={{0,4},{1,5},{2,6},{3,7},{4,0},{5,1},{6,2},{7,3},{8,12},{9,13},{10,... | collective-permute-start | bytes 1572872 | tf_op jit(solution)/shard_map/ppermute | solution.py:22

commit v7 on v5

v7 whole, which is shorter than its diff:
```python
import functools
import math

import jax
import jax.numpy as jnp
from jax import lax
from jax.experimental import pallas as pl
from jax.experimental.pallas import tpu as pltpu
from jax.sharding import PartitionSpec as P

ITERS = 3
TILE = 128
NEGATIVE = -1e30

VMEM = pl.BlockSpec(memory_space=pltpu.VMEM)
HBM = pl.BlockSpec(memory_space=pltpu.HBM)
SMEM = pl.BlockSpec(memory_space=pltpu.SMEM)


def swap(x, axis, offset):
    size = lax.axis_size(axis)
    return lax.ppermute(x, axis, [(i, i ^ offset) for i in range(size)])


def pair_sum(terms):
    while len(terms) > 1:
        terms = [terms[i] + terms[i + 1] for i in range(0, len(terms), 2)]
    return terms[0]


def combine(parts):
    peak = functools.reduce(jnp.maximum, parts)
    return peak + jnp.log(pair_sum([jnp.exp(part - peak) for part in parts]))


class Table:
    def __init__(self, row_tiles, columns):
        self.row_tiles, self.columns = row_tiles, columns
        self.end = max(row_tiles, columns) + 4
        self.column_base = row_tiles
        self.pair_base = row_tiles + columns
        self.mask_base = self.pair_base + columns // 2
        self.shape = (self.mask_base + row_tiles, self.end + 1)
        self.dummy = row_tiles * columns

    def loop(self, ref, line, unroll, step, start):
        count = (ref[line, self.end] + unroll - 1) // unroll

        def several(k, a):
            for i in range(unroll):
                a = step(ref[line, unroll * k + i], a)
            return a

        return lax.fori_loop(0, count, several, start)

    def place(self, t, u):
        padding = (t == self.row_tiles) | (u == self.columns)
        return jnp.where(padding, self.dummy, t * self.columns + u)


def setup_kernel(table, own_ref, other_ref, out_ref):
    core = lax.rem(lax.axis_index("proto"), 2)
    half = table.columns // 2

    def mask_row(t, carry):
        for u in range(half):
            out_ref[table.mask_base + t, core * half + u] = jnp.where(own_ref[t, u] == 1, 1, 0)
            out_ref[table.mask_base + t, (1 - core) * half + u] = jnp.where(other_ref[t, u] == 1, 1, 0)
        return carry

    lax.fori_loop(0, table.row_tiles, mask_row, 0)

    def fill(line, size, allowed):
        count = jnp.int32(0)
        for i in range(size):
            out_ref[line, count] = i
            count = count + allowed(i)
        for i in range(4):
            out_ref[line, count + i] = size
        out_ref[line, table.end] = count

    def row_list(t, carry):
        fill(t, table.columns, lambda u: out_ref[table.mask_base + t, u])
        return carry

    def column_list(u, carry):
        fill(table.column_base + u, table.row_tiles, lambda t: out_ref[table.mask_base + t, u])
        return carry

    def pair_list(p, carry):
        fill(
            table.pair_base + p,
            table.row_tiles,
            lambda t: jnp.maximum(out_ref[table.mask_base + t, 2 * p], out_ref[table.mask_base + t, 2 * p + 1]),
        )
        return carry

    lax.fori_loop(0, table.row_tiles, row_list, 0)
    lax.fori_loop(0, table.columns, column_list, 0)
    lax.fori_loop(0, table.columns // 2, pair_list, 0)


def blank():
    return jnp.zeros((TILE, TILE), jnp.float32)


def lowest():
    return jnp.full((TILE, TILE), NEGATIVE, jnp.float32)


def bad_bits(good):
    bad = jnp.max(jnp.where(good, 0.0, 1.0), axis=1, keepdims=True)
    bit = jnp.left_shift(1, lax.broadcasted_iota(jnp.int32, bad.shape, 0))
    return jnp.sum(bad * bit.astype(jnp.float32)).astype(jnp.int32)


def has_bit(bits, i):
    return jnp.bitwise_and(bits, 1 << i) != 0


def spread_rows(row, wide_ref):
    row_tiles = row.shape[0]
    standing = jnp.concatenate(
        [row, jnp.zeros((TILE - row_tiles, TILE), jnp.float32)], axis=0
    ).T
    for t in range(row_tiles):
        wide_ref[t] = jnp.broadcast_to(standing[:, t : t + 1], (TILE, TILE))


def lying(tiles):
    lane = lax.broadcasted_iota(jnp.int32, (TILE, TILE), 1)
    found = blank()
    for t, tile in enumerate(tiles):
        found = jnp.where(lane == t, jnp.sum(tile, axis=1, keepdims=True), found)
    return found.T[: len(tiles)]


def panel_kernel(table, row_blocks, first_features, table_ref, e_hbm_ref, *refs):
    pieces, (s_ref, p_ref, out_ref, acc_ref, e_ref, sem) = refs[:-6], refs[-6:]
    load = pltpu.make_async_copy(e_hbm_ref, e_ref, sem.at[0])
    load.start()
    row_tiles, columns = table.row_tiles, table.columns
    scale = 4.0 / math.sqrt(e_ref.shape[1])
    core = lax.rem(lax.axis_index("proto"), 2)
    me = lax.axis_index("row")
    protos = p_ref.shape[0] // 2
    for n, piece in enumerate(pieces):
        group, within = n * 2 // len(pieces), n % (len(pieces) // 2)
        rows, width = piece.shape
        first = (core if group == 0 else 1 - core) * protos + row_blocks[within]
        start = 0
        if first_features[within] is not None:
            start = pl.multiple_of(jnp.bitwise_xor(me, first_features[within]) * width, TILE)
        place = p_ref.at[pl.ds(pl.multiple_of(first, TILE), rows), pl.ds(start, width)]
        if n == 0:
            own = pltpu.make_async_copy(piece, place, sem.at[1])
            own.start()
        else:
            place[...] = piece[...]
    s_ref[table.dummy] = lowest()
    for t in range(row_tiles):
        acc_ref[t] = lowest()
    own.wait()
    load.wait()

    def one_pair(pair, carry):
        line = table.pair_base + pair

        def four_tiles(k, carry):
            at = [jnp.minimum(table_ref[line, 4 * k + i], row_tiles - 1) for i in range(4)]
            rows = jnp.concatenate(
                [e_ref[pl.ds(pl.multiple_of(t * TILE, TILE), TILE), :] for t in at], axis=0
            )
            block = p_ref[pl.ds(pl.multiple_of(pair * 2 * TILE, TILE), 2 * TILE), :]
            product = scale * lax.dot_general(
                rows, block, (((1,), (1,)), ((), ())), preferred_element_type=jnp.float32
            )
            for i, t in enumerate(at):
                peak = acc_ref[t]
                for side in range(2):
                    u = 2 * pair + side
                    tile = product[i * TILE : (i + 1) * TILE, side * TILE : (side + 1) * TILE]
                    s_ref[t * columns + u] = tile
                    off = jnp.where(table_ref[table.mask_base + t, u] == 1, 0.0, NEGATIVE)
                    peak = jnp.maximum(peak, tile + off)
                acc_ref[t] = peak
            return carry

        return lax.fori_loop(0, (table_ref[line, table.end] + 3) // 4, four_tiles, carry)

    lax.fori_loop(0, columns // 2, one_pair, 0)

    lane = lax.broadcasted_iota(jnp.int32, (TILE, TILE), 1)
    peaks = blank()
    for t in range(row_tiles):
        peak = jnp.max(acc_ref[t], axis=1, keepdims=True)
        peaks = jnp.where(lane == t, peak, peaks)
        acc_ref[t] = jnp.broadcast_to(peak, (TILE, TILE))
    for t in range(row_tiles):
        acc_ref[t] = table.loop(
            table_ref,
            t,
            4,
            lambda u, a, t=t: a + jnp.exp(s_ref[table.place(t, u)] - acc_ref[t]),
            blank(),
        )
    out_ref[...] = peaks.T[:row_tiles] + jnp.log(lying([acc_ref[t] for t in range(row_tiles)]))


def row_kernel(table, log_column, table_ref, s_ref, w_ref, m_ref, r_ref, *refs):
    parts, (out_ref, c_ref, v_ref, acc_ref) = refs[:-4], refs[-4:]
    row_tiles, columns = table.row_tiles, table.columns
    column = log_column - combine([part[...] for part in parts])
    c_ref[:columns] = column
    v_ref[:columns] = jnp.exp(column + m_ref[...])
    rest = jnp.zeros((c_ref.shape[0] - columns, TILE), jnp.float32)
    c_ref[columns:] = rest
    v_ref[columns:] = rest

    for t in range(row_tiles):

        def one_tile(u, a, t=t):
            return a + w_ref[table.place(t, u)].astype(jnp.float32) * v_ref[pl.ds(u, 1), :]

        acc_ref[t] = table.loop(table_ref, t, 4, one_tile, blank())
    totals = lying([acc_ref[t] for t in range(row_tiles)])
    out_ref[...] = jnp.log(totals) - r_ref[...]
    bits = bad_bits(totals > 1e-15)

    @pl.when(bits != 0)
    def _():
        for t in range(row_tiles):

            @pl.when(has_bit(bits, t))
            def _():
                def score(u):
                    return s_ref[table.place(t, u)] + c_ref[pl.ds(u, 1), :]

                peak = table.loop(table_ref, t, 2, lambda u, a: jnp.maximum(a, score(u)), lowest())
                peak = jnp.max(peak, axis=1, keepdims=True)
                total = table.loop(table_ref, t, 2, lambda u, a: a + jnp.exp(score(u) - peak), blank())
                found = peak + jnp.log(jnp.sum(total, axis=1, keepdims=True))
                out_ref[t : t + 1, :] = jnp.broadcast_to(found, (TILE, TILE)).T[:1]


def slow_column(table, table_ref, u, s_ref, wide_ref, keep):
    line = table.column_base + u

    def score(t):
        at = table.place(t, u)
        return at, s_ref[at] + wide_ref[jnp.minimum(t, table.row_tiles - 1)]

    peak = table.loop(table_ref, line, 2, lambda t, a: jnp.maximum(a, score(t)[1]), lowest())
    peak = jnp.max(peak, axis=0, keepdims=True)

    def one_tile(t, a):
        at, value = score(t)
        value = jnp.exp(value - peak)
        keep(at, value)
        return a + value

    total = table.loop(table_ref, line, 2, one_tile, blank())
    return peak, jnp.sum(total, axis=0, keepdims=True)


def first_column_kernel(table, table_ref, s_ref, *refs):
    parts, (out_ref, r_ref, w_ref, m_ref, wide_ref, acc_ref) = refs[:-6], refs[-6:]
    row = -combine([part[...] for part in parts])
    r_ref[...] = row
    spread_rows(row, wide_ref)
    w_ref[table.dummy] = blank().astype(jnp.bfloat16)

    def keep(at, value):
        w_ref[at] = value.astype(jnp.bfloat16)

    for u in range(table.columns):

        def one_tile(t, a, u=u):
            at = table.place(t, u)
            value = jnp.exp(s_ref[at] + wide_ref[jnp.minimum(t, table.row_tiles - 1)])
            keep(at, value)
            return a + value

        acc_ref[u] = table.loop(table_ref, table.column_base + u, 4, one_tile, blank())
    totals = jnp.concatenate(
        [jnp.sum(acc_ref[u], axis=0, keepdims=True) for u in range(table.columns)], axis=0
    )
    m_ref[...] = jnp.zeros(m_ref.shape, jnp.float32)
    out_ref[...] = jnp.log(totals)
    bits = bad_bits(totals > 1e-15)

    @pl.when(bits != 0)
    def _():
        for u in range(table.columns):

            @pl.when(has_bit(bits, u))
            def _():
                peak, total = slow_column(table, table_ref, u, s_ref, wide_ref, keep)
                m_ref[u : u + 1, :] = peak
                out_ref[u : u + 1, :] = peak + jnp.log(total)


def column_kernel(table, table_ref, s_ref, w_ref, m_ref, first_ref, *refs):
    parts, (out_ref, r_ref, r_out_ref, wide_ref, acc_ref) = refs[:-5], refs[-5:]
    row = -combine([part[...] for part in parts])
    r_ref[...] = row
    r_out_ref[...] = row
    factor = jnp.exp(row - first_ref[...])
    spread_rows(factor, wide_ref)

    for u in range(table.columns):

        def one_tile(t, a, u=u):
            kept = w_ref[table.place(t, u)].astype(jnp.float32)
            return a + kept * wide_ref[jnp.minimum(t, table.row_tiles - 1)]

        acc_ref[u] = table.loop(table_ref, table.column_base + u, 4, one_tile, blank())
    totals = jnp.concatenate(
        [jnp.sum(acc_ref[u], axis=0, keepdims=True) for u in range(table.columns)], axis=0
    )
    out_ref[...] = m_ref[...] + jnp.log(totals)
    largest = jnp.max(jnp.max(factor, axis=1, keepdims=True), axis=0, keepdims=True)
    bits = bad_bits((totals > 1e-15) & (totals < 1e30) & (largest < 1e15))

    @pl.when(bits != 0)
    def _():
        spread_rows(row, wide_ref)
        for u in range(table.columns):

            @pl.when(has_bit(bits, u))
            def _():
                peak, total = slow_column(table, table_ref, u, s_ref, wide_ref, lambda at, value: None)
                out_ref[u : u + 1, :] = peak + jnp.log(total)


def plan_kernel(table, log_column, lines, table_ref, s_ref, r_ref, p_ref, *refs):
    parts, outs = refs[: -4 - lines], refs[-4 - lines : -4]
    own_ref, c_ref, wide_ref, total_ref = refs[-4:]
    row_tiles, columns = table.row_tiles, table.columns
    index = lax.axis_index("proto")
    core, z = lax.rem(index, 2), lax.div(index, 2)
    c_ref[...] = log_column - combine([part[...] for part in parts])
    half = columns // 2
    own_ref[...] = c_ref[pl.ds(pl.multiple_of(core * half, half), half), :]
    spread_rows(r_ref[...], wide_ref)
    width = outs[0].shape[1]
    fits = width % TILE == 0
    total_ref[...] = jnp.zeros(total_ref.shape, jnp.float32)

    def one_pair(pair, carry):
        first = pl.multiple_of(pair * 2 * TILE, TILE)
        line = table.pair_base + pair
        blocks = []
        for j in range(lines):
            if fits:
                start = (2 * jnp.bitwise_xor(z, j) + core) * width
                blocks.append(p_ref[pl.ds(first, 2 * TILE), pl.ds(pl.multiple_of(start, TILE), width)])
            else:
                both = p_ref[pl.ds(first, 2 * TILE), 2 * j * width : 2 * (j + 1) * width]
                blocks.append(jnp.where(core == 0, both[:, :width], both[:, width:]))
        block = jnp.concatenate(blocks, axis=1)

        def four_tiles(k, carry):
            at = [table_ref[line, 4 * k + i] for i in range(4)]
            inside = [jnp.minimum(t, row_tiles - 1) for t in at]
            strips = []
            for t, real in zip(at, inside):
                sides = []
                for side in range(2):
                    u = 2 * pair + side
                    good = (t < row_tiles) & (table_ref[table.mask_base + real, u] == 1)
                    tile = s_ref[jnp.where(good, t * columns + u, table.dummy)]
                    sides.append(jnp.exp(tile + wide_ref[real] + c_ref[pl.ds(u, 1), :]).astype(jnp.bfloat16))
                strips.append(jnp.concatenate(sides, axis=1))
            product = jnp.dot(
                jnp.concatenate(strips, axis=0), block, preferred_element_type=jnp.float32
            )
            for i, t in enumerate(inside):
                total_ref[t] += product[i * TILE : (i + 1) * TILE]
            return carry

        return lax.fori_loop(0, (table_ref[line, table.end] + 3) // 4, four_tiles, carry)

    lax.fori_loop(0, columns // 2, one_pair, 0)
    for t in range(row_tiles):
        total = total_ref[t].astype(jnp.bfloat16)
        for j in range(lines):
            block = total[:, j * width : (j + 1) * width]
            if fits:
                outs[j][t * TILE : (t + 1) * TILE, :] = block
            else:
                for k in range(lines):

                    @pl.when(jnp.bitwise_xor(z, k) == j)
                    def _():
                        outs[k][t * TILE : (t + 1) * TILE, :] = block


def params(mebibytes):
    return pltpu.CompilerParams(vmem_limit_bytes=mebibytes * 2**20)


def gather_features(shard):
    width = shard.shape[1]

    def sibling(block):
        return swap(block, "proto", 1)

    if lax.axis_size("row") != 4 or width % TILE:
        whole = lax.all_gather(shard, "row", axis=1, tiled=True)
        return [whole, sibling(whole)], [0], [None]
    half = shard.shape[0] // 2
    top, bottom = shard[:half], shard[half:]
    near_bottom = swap(bottom, "row", 1)
    far_top = swap(top, "row", 2)
    near_bottom, far_top, top, bottom = lax.optimization_barrier((near_bottom, far_top, top, bottom))
    cross_top = swap(far_top, "row", 1)
    cross_bottom = swap(near_bottom, "row", 2)
    near_top = swap(top, "row", 1)
    far_bottom = swap(bottom, "row", 2)
    pieces = [shard, near_top, near_bottom, far_top, far_bottom, cross_top, cross_bottom]
    firsts = [0, 0, half, 0, half, 0, half]
    return pieces + [sibling(piece) for piece in pieces], firsts, [0, 1, 1, 2, 2, 3, 3]


def scatter_partials(blocks):
    blocks = list(blocks)
    distance = 1
    while distance < len(blocks):
        for j in range(len(blocks) - distance, 0, -2 * distance):
            got = swap(blocks[j].astype(jnp.bfloat16), "proto", 2 * distance).astype(jnp.float32)
            blocks[j ^ distance] = blocks[j ^ distance].astype(jnp.float32) + got
        distance *= 2
    return blocks[0].astype(jnp.bfloat16)


def shards(embeddings, prototypes, block_mask):
    n_row, n_proto = lax.axis_size("row"), lax.axis_size("proto")
    lines = n_proto // 2
    rows, features = embeddings.shape
    protos = 2 * prototypes.shape[0]
    width = features // n_proto
    row_tiles, columns = block_mask.shape[0], 2 * block_mask.shape[1]
    log_column = math.log(rows * n_row / (protos * lines))
    table = Table(row_tiles, columns)

    other_mask = swap(block_mask, "proto", 1)
    pieces, firsts, owners = gather_features(prototypes)
    lists = pl.pallas_call(
        functools.partial(setup_kernel, table),
        out_shape=jax.ShapeDtypeStruct(table.shape, jnp.int32),
        in_specs=[SMEM] * 2,
        out_specs=SMEM,
        name="setup",
    )(block_mask, other_mask)

    row_shape = jax.ShapeDtypeStruct((row_tiles, TILE), jnp.float32)
    column_shape = jax.ShapeDtypeStruct((columns, TILE), jnp.float32)
    half = columns // 2
    panel = (table.dummy + 1, TILE, TILE)
    wide = pltpu.VMEM((row_tiles, TILE, TILE), jnp.float32)
    tall = pltpu.VMEM((columns, TILE, TILE), jnp.float32)
    factors = pltpu.VMEM((columns + 8, TILE), jnp.float32)
    similar, whole, row_part = pl.pallas_call(
        functools.partial(panel_kernel, table, firsts, owners),
        out_shape=(pltpu.VMEM(panel, jnp.float32), pltpu.VMEM((protos, features), jnp.bfloat16), row_shape),
        in_specs=[SMEM] + [pl.BlockSpec(memory_space=pl.ANY)] * 2 + [VMEM] * (len(pieces) - 1),
        out_specs=(VMEM, VMEM, VMEM),
        scratch_shapes=[wide, pltpu.VMEM(embeddings.shape, jnp.bfloat16), pltpu.SemaphoreType.DMA((2,))],
        compiler_params=params(12),
        name="panel",
    )(lists, embeddings, *pieces)

    def row_exchange(part):
        others = [swap(part, "proto", 2 * j) for j in range(lines - 1, 0, -1)]
        return [part] + others[::-1]

    def column_exchange(part):
        others = [swap(part, "row", j) for j in range(n_row - 1, 0, -1)]
        return [part] + others[::-1]

    parts = row_exchange(row_part)
    column_part, first_row, kept, peaks = pl.pallas_call(
        functools.partial(first_column_kernel, table),
        out_shape=(column_shape, row_shape, pltpu.VMEM(panel, jnp.bfloat16), column_shape),
        in_specs=[SMEM] + [VMEM] * (1 + len(parts)),
        out_specs=(VMEM,) * 4,
        scratch_shapes=[wide, tall],
        compiler_params=params(4),
        name="first_column_pass",
    )(lists, similar, *parts)
    for sweep in range(1, ITERS):
        parts = column_exchange(column_part)
        row_part = pl.pallas_call(
            functools.partial(row_kernel, table, log_column),
            out_shape=row_shape,
            in_specs=[SMEM] + [VMEM] * (4 + len(parts)),
            out_specs=VMEM,
            scratch_shapes=[factors, factors, wide],
            compiler_params=params(4),
            name="row_pass",
        )(lists, similar, kept, peaks, first_row, *parts)
        parts = row_exchange(row_part)
        column_part, row_potential, row_out = pl.pallas_call(
            functools.partial(column_kernel, table),
            out_shape=(column_shape, row_shape, row_shape),
            in_specs=[SMEM] + [VMEM] * (4 + len(parts)),
            out_specs=(VMEM,) * 3,
            scratch_shapes=[wide, tall],
            compiler_params=params(4),
            name="column_pass",
        )(lists, similar, kept, peaks, first_row, *parts)
    parts = column_exchange(column_part)
    *blocks, column_potential = pl.pallas_call(
        functools.partial(plan_kernel, table, log_column, lines),
        out_shape=[jax.ShapeDtypeStruct((rows, width), jnp.bfloat16)] * lines
        + [jax.ShapeDtypeStruct((half, TILE), jnp.float32)],
        in_specs=[SMEM] + [VMEM] * (3 + len(parts)),
        out_specs=[VMEM] * (lines + 1),
        scratch_shapes=[
            pltpu.VMEM((columns, TILE), jnp.float32),
            wide,
            pltpu.VMEM((row_tiles, TILE, lines * width), jnp.float32),
        ],
        compiler_params=params(12),
        name="plan",
    )(lists, similar, row_potential, whole, *parts)
    targets = scatter_partials(blocks)
    return (targets, row_out.reshape(rows), column_potential.reshape(protos // 2))


def solution(mesh):
    return jax.shard_map(
        shards,
        mesh=mesh,
        in_specs=(P("row", None), P("proto", "row"), P("row", "proto")),
        out_specs=(P("row", "proto"), P("row"), P("proto")),
        check_vma=False,
    )
```

time: 148 us -> 151 us (1.020)
  Pallas kernels: 31 us -> 40.6 us
  starting transfers between devices: 42.8 us -> 39 us
  other arithmetic: 3.2 us -> 1.14 us
    pallas_call x7 -> x8, Pallas kernels: 31 us -> 40.6 us  [the longest x1 9.69 us: shards(): pl.pallas_call(functools.partial(panel_kernel, table, firsts, owners), ou...]
    ppermute x35, starting transfers between devices: 42.8 us -> 39 us  [swap(): return lax.ppermute(x, axis, [(i, i ^ offset) for i in range(size)])]
    reduce_sum x6 -> x0, other arithmetic: 1.96 us -> none  [the longest x2 0.83 us: ordered(): places = jnp.sum(jnp.where(hit, at[None, None, :] - size, 0), axis=2) + size]
    unnamed x7 -> x11, local copies, waits for them, and re-layouts: 4.69 us -> 4.74 us
  transfers between devices with their start and end apart: 35 -> 35, of which waited for: 24 -> 25; matrix products, arithmetic and copies ran while one was open for 2% -> 1% of each run, Pallas kernels for 0% -> 6%
where the time goes in v7:
time: 151 us; the launch traced here: 149 us
  waiting for transfers between devices  61.6 us (41%)
  Pallas kernels  40.6 us (27%)
  starting transfers between devices  39 us (26%)
  local copies, waits for them, and re-layouts  5.8 us (4%)
    ppermute x35, waiting for transfers between devices, swap(): return lax.ppermute(x, axis, [(i, i ^ offset) for i in range(size)])  61.6 us
    ppermute x35, starting transfers between devices, swap(): return lax.ppermute(x, axis, [(i, i ^ offset) for i in range(size)])  39 us
    pallas_call x1, Pallas kernels, shards(): pl.pallas_call(functools.partial(panel_kernel, table, firsts, owners), ou...  9.69 us
    pallas_call x1, Pallas kernels, shards(): pl.pallas_call(functools.partial(setup_kernel, table), out_shape=jax.Shap...  8.26 us
    pallas_call x1, Pallas kernels, shards(): pl.pallas_call(functools.partial(plan_kernel, table, log_column, lines),...  6.8 us
    pallas_call x2, Pallas kernels, shards(): pl.pallas_call(functools.partial(column_kernel, table), out_shape=(column...  6.69 us
    pallas_call x2, Pallas kernels, shards(): pl.pallas_call(functools.partial(row_kernel, table, log_column), out_shap...  6.22 us
    unnamed x11, local copies, waits for them, and re-layouts  4.74 us
  transfers between devices with their start and end apart: 35, of which 25 were waited for; matrix products, arithmetic and copies ran while one was open for 1% of the time, Pallas kernels for 6%

profile of v7, /device:TPU:0, one launch (start us, length us, event | category | flops | bytes accessed | tf_op | source)
XLA Modules:
  0.0 149.0 jit_solution(747716719676822800)
XLA Ops:
  0.6 1.1 fusion
  1.7 3.0 %collective-permute-start.2 = (bf16[512,256]{1,0:T(8,128)(2,1)S(1)}, bf16[512,256]{1,0:T(8,128)(2,1)S(1)}, u32[]{:S(2)}, u32[]{:S(2)}) collective-permute-start(bf16[512,256]{1,0:T(8,128)(2,1)S(1)} %get-tuple-element.23), channel_id=1, source_target_pairs={{0,16},{8,24},{16,0},{24,8},{1,17},{9,25},{17,1},{25,9},{2,18},{10... | collective-permute-start | bytes 786440 | tf_op jit(solution)/shard_map/ppermute | solution.py:22
  4.7 1.5 %collective-permute-start.1 = (bf16[512,256]{1,0:T(8,128)(2,1)S(1)}, bf16[512,256]{1,0:T(8,128)(2,1)S(1)}, u32[]{:S(2)}, u32[]{:S(2)}) collective-permute-start(bf16[512,256]{1,0:T(8,128)(2,1)S(1)} %get-tuple-element.26), channel_id=1, source_target_pairs={{0,8},{8,0},{16,24},{24,16},{1,9},{9,1},{17,25},{25,17},{2,10},{10... | collective-permute-start | bytes 786440 | tf_op jit(solution)/shard_map/ppermute | solution.py:22
  6.2 4.8 %collective-permute-done.2.refs_3_ = bf16[512,256]{1,0:T(8,128)(2,1)S(1)} collective-permute-done((bf16[512,256]{1,0:T(8,128)(2,1)S(1)}, bf16[512,256]{1,0:T(8,128)(2,1)S(1)}, u32[]{:S(2)}, u32[]{:S(2)}) %collective-permute-start.2) | collective-permute-done | bytes 262176 | tf_op jit(solution)/shard_map/ppermute | solution.py:22
  11.0 1.5 collective-permute-done.1.refs_2_
  12.5 1.5 %collective-permute-start.3 = (bf16[512,256]{1,0:T(8,128)(2,1)S(1)}, bf16[512,256]{1,0:T(8,128)(2,1)S(1)}, u32[]{:S(2)}, u32[]{:S(2)}) collective-permute-start(bf16[512,256]{1,0:T(8,128)(2,1)S(1)} %get-tuple-element.23), channel_id=1, source_target_pairs={{0,8},{8,0},{16,24},{24,16},{1,9},{9,1},{17,25},{25,17},{2,10},{10... | collective-permute-start | bytes 786440 | tf_op jit(solution)/shard_map/ppermute | solution.py:22
  16.4 1.5 %collective-permute-start.6 = (bf16[512,256]{1,0:T(8,128)(2,1)S(1)}, bf16[512,256]{1,0:T(8,128)(2,1)S(1)}, u32[]{:S(2)}, u32[]{:S(2)}) collective-permute-start(bf16[512,256]{1,0:T(8,128)(2,1)S(1)} %collective-permute-done.1.refs_2_), channel_id=1, source_target_pairs={{0,16},{8,24},{16,0},{24,8},{1,17},{9,25},{17,1},{25,9},{2,18},{10... | collective-permute-start | bytes 786440 | tf_op jit(solution)/shard_map/ppermute | solution.py:22
  18.0 1.4 collective-permute-done.3.refs_1_
  19.4 2.5 %collective-permute-done.4.refs_4_ = bf16[512,256]{1,0:T(8,128)(2,1)S(1)} collective-permute-done((bf16[512,256]{1,0:T(8,128)(2,1)S(1)}, bf16[512,256]{1,0:T(8,128)(2,1)S(1)}, u32[]{:S(2)}, u32[]{:S(2)}) %collective-permute-start.4) | collective-permute-done | bytes 262176 | tf_op jit(solution)/shard_map/ppermute | solution.py:22
  22.6 3.6 %collective-permute-done.6.refs_6_ = bf16[512,256]{1,0:T(8,128)(2,1)S(1)} collective-permute-done((bf16[512,256]{1,0:T(8,128)(2,1)S(1)}, bf16[512,256]{1,0:T(8,128)(2,1)S(1)}, u32[]{:S(2)}, u32[]{:S(2)}) %collective-permute-start.6) | collective-permute-done | bytes 262176 | tf_op jit(solution)/shard_map/ppermute | solution.py:22
  26.7 1.5 %collective-permute-done.5.refs_5_ = bf16[512,256]{1,0:T(8,128)(2,1)S(1)} collective-permute-done((bf16[512,256]{1,0:T(8,128)(2,1)S(1)}, bf16[512,256]{1,0:T(8,128)(2,1)S(1)}, u32[]{:S(2)}, u32[]{:S(2)}) %collective-permute-start.5) | collective-permute-done | bytes 262176 | tf_op jit(solution)/shard_map/ppermute | solution.py:22
  28.3 8.3 %setup.1.table_ref = s32[56,21]{1,0:T(8,128)} custom-call(s32[16,8]{1,0:T(8,128)} %copy-done.3, s32[16,8]{1,0:T(8,128)} %copy-done.4), custom_call_target="tpu_custom_call" | custom-call | tf_op jit(solution)/shard_map/setup/pallas_call | solution.py:449
  36.6 2.2 %copy-done = bf16[2048,1024]{1,0:T(8,128)(2,1)S(1)} copy-done((bf16[2048,1024]{1,0:T(8,128)(2,1)S(1)}, bf16[2048,1024]{1,0:T(8,128)(2,1)}, u32[]{:S(2)}) %copy-start) | copy-done | bytes 4194328
  38.8 1.0 copy-done.1
  40.6 9.7 %panel.1 = (f32[257,128,128]{2,1,0:T(8,128)S(1)}, bf16[2048,1024]{1,0:T(8,128)(2,1)S(1)}, f32[16,128]{1,0:T(8,128)S(1)}) custom-call(s32[56,21]{1,0:T(8,128)S(1)} %copy-done.2, bf16[2048,1024]{1,0:T(8,128)(2,1)S(1)} %copy-done, bf16[1024,256]{1,0:T(8,128)(2,1)S(1)} %copy-done.1, bf16[512,256]{1,0:T(8,128)(2,1)S(1)} %collective-permute-done.3.refs_1_, ...), custom_call_target="tpu_custom_call" | custom-call | tf_op jit(solution)/shard_map/panel/pallas_call | solution.py:464
  50.2 3.2 %collective-permute-start.16 = (f32[16,128]{1,0:T(8,128)S(1)}, f32[16,128]{1,0:T(8,128)S(1)}, u32[]{:S(2)}, u32[]{:S(2)}) collective-permute-start(f32[16,128]{1,0:T(8,128)S(1)} %get-tuple-element.28.refs_0_), channel_id=1, source_target_pairs={{0,6},{1,7},{2,4},{3,5},{4,2},{5,3},{6,0},{7,1},{8,14},{9,15},{10,... | collective-permute-start | bytes 24584 | tf_op jit(solution)/shard_map/ppermute | solution.py:22
  53.4 1.3 collective-permute-start.14
  54.7 1.1 collective-permute-done.16.refs_3_
  55.8 2.2 %collective-permute-done.15.refs_2_ = f32[16,128]{1,0:T(8,128)S(1)} collective-permute-done((f32[16,128]{1,0:T(8,128)S(1)}, f32[16,128]{1,0:T(8,128)S(1)}, u32[]{:S(2)}, u32[]{:S(2)}) %collective-permute-start.15) | collective-permute-done | bytes 8224 | tf_op jit(solution)/shard_map/ppermute | solution.py:22
  58.0 3.0 %first_column_pass.1 = (f32[16,128]{1,0:T(8,128)S(1)}, f32[16,128]{1,0:T(8,128)S(1)}, bf16[257,128,128]{2,1,0:T(8,128)(2,1)S(1)}, f32[16,128]{1,0:T(8,128)S(1)}) custom-call(s32[56,21]{1,0:T(8,128)S(1)} %copy-done.2, f32[257,128,128]{2,1,0:T(8,128)S(1)} %get-tuple-element.27.s_ref, f32[16,128]{1,0:T(8,128)S(1)} %get-tuple-element.28.refs_0_, ...), custom_call_target="tpu_custom_call" | custom-call | tf_op jit(solution)/shard_map/first_column_pass/pallas_call | solution.py:483
  61.0 4.7 %collective-permute-start.19 = (f32[16,128]{1,0:T(8,128)S(1)}, f32[16,128]{1,0:T(8,128)S(1)}, u32[]{:S(2)}, u32[]{:S(2)}) collective-permute-start(f32[16,128]{1,0:T(8,128)S(1)} %get-tuple-element.32.refs_0_), channel_id=1, source_target_pairs={{0,24},{8,16},{16,8},{24,0},{1,25},{9,17},{17,9},{25,1},{2,26},{10... | collective-permute-start | bytes 24584 | tf_op jit(solution)/shard_map/ppermute | solution.py:22
  67.3 2.0 %collective-permute-done.18.refs_2_ = f32[16,128]{1,0:T(8,128)S(1)} collective-permute-done((f32[16,128]{1,0:T(8,128)S(1)}, f32[16,128]{1,0:T(8,128)S(1)}, u32[]{:S(2)}, u32[]{:S(2)}) %collective-permute-start.18) | collective-permute-done | bytes 8224 | tf_op jit(solution)/shard_map/ppermute | solution.py:22
  70.1 3.1 %row_pass.2.refs_0_ = f32[16,128]{1,0:T(8,128)S(1)} custom-call(s32[56,21]{1,0:T(8,128)S(1)} %copy-done.2, f32[257,128,128]{2,1,0:T(8,128)S(1)} %get-tuple-element.27.s_ref, bf16[257,128,128]{2,1,0:T(8,128)(2,1)S(1)} %get-tuple-element.29.w_ref, f32[16,128]{1,0:T(8,128)S(1)} %get-tuple-element.30.m_ref, f32[16,128]{1,0:T(8,128)S(1)} %get-tuple-element.31.r_ref.first_ref, ...), custom_call_target="tpu_custom_call" | custom-call | tf_op jit(solution)/shard_map/row_pass/pallas_call | solution.py:494
  73.2 1.9 %collective-permute-start.22 = (f32[16,128]{1,0:T(8,128)S(1)}, f32[16,128]{1,0:T(8,128)S(1)}, u32[]{:S(2)}, u32[]{:S(2)}) collective-permute-start(f32[16,128]{1,0:T(8,128)S(1)} %row_pass.2.refs_0_), channel_id=1, source_target_pairs={{0,6},{1,7},{2,4},{3,5},{4,2},{5,3},{6,0},{7,1},{8,14},{9,15},{10,... | collective-permute-start | bytes 24584 | tf_op jit(solution)/shard_map/ppermute | solution.py:22
  76.0 1.7 %collective-permute-start.20 = (f32[16,128]{1,0:T(8,128)S(1)}, f32[16,128]{1,0:T(8,128)S(1)}, u32[]{:S(2)}, u32[]{:S(2)}) collective-permute-start(f32[16,128]{1,0:T(8,128)S(1)} %row_pass.2.refs_0_), channel_id=1, source_target_pairs={{0,2},{1,3},{2,0},{3,1},{4,6},{5,7},{6,4},{7,5},{8,10},{9,11},{10,... | collective-permute-start | bytes 24584 | tf_op jit(solution)/shard_map/ppermute | solution.py:22
  77.7 1.1 collective-permute-done.22.refs_3_
  78.7 1.0 collective-permute-done.21.refs_2_
  79.7 3.4 %column_pass.2 = (f32[16,128]{1,0:T(8,128)S(1)}, f32[16,128]{1,0:T(8,128)}, f32[16,128]{1,0:T(8,128)}) custom-call(s32[56,21]{1,0:T(8,128)S(1)} %copy-done.2, f32[257,128,128]{2,1,0:T(8,128)S(1)} %get-tuple-element.27.s_ref, bf16[257,128,128]{2,1,0:T(8,128)(2,1)S(1)} %get-tuple-element.29.w_ref, f32[16,128]{1,0:T(8,128)S(1)} %get-tuple-element.30.m_ref, ...), custom_call_target="tpu_custom_call" | custom-call | tf_op jit(solution)/shard_map/column_pass/pallas_call | solution.py:504
  83.2 1.8 %collective-permute-start.25 = (f32[16,128]{1,0:T(8,128)S(1)}, f32[16,128]{1,0:T(8,128)S(1)}, u32[]{:S(2)}, u32[]{:S(2)}) collective-permute-start(f32[16,128]{1,0:T(8,128)S(1)} %get-tuple-element.33.refs_0_), channel_id=1, source_target_pairs={{0,24},{8,16},{16,8},{24,0},{1,25},{9,17},{17,9},{25,1},{2,26},{10... | collective-permute-start | bytes 24584 | tf_op jit(solution)/shard_map/ppermute | solution.py:22
  85.0 1.1 collective-permute-start.24
  86.1 1.5 collective-permute-start.23
  87.7 0.9 collective-permute-done.24.refs_2_
  88.6 1.1 collective-permute-done.23.refs_1_
  89.7 3.1 %row_pass.3.refs_0_ = f32[16,128]{1,0:T(8,128)S(1)} custom-call(s32[56,21]{1,0:T(8,128)S(1)} %copy-done.2, f32[257,128,128]{2,1,0:T(8,128)S(1)} %get-tuple-element.27.s_ref, bf16[257,128,128]{2,1,0:T(8,128)(2,1)S(1)} %get-tuple-element.29.w_ref, f32[16,128]{1,0:T(8,128)S(1)} %get-tuple-element.30.m_ref, f32[16,128]{1,0:T(8,128)S(1)} %get-tuple-element.31.r_ref.first_ref, ...), custom_call_target="tpu_custom_call" | custom-call | tf_op jit(solution)/shard_map/row_pass/pallas_call | solution.py:494
  92.8 1.2 collective-permute-start.28
  94.1 1.8 %collective-permute-start.27 = (f32[16,128]{1,0:T(8,128)S(1)}, f32[16,128]{1,0:T(8,128)S(1)}, u32[]{:S(2)}, u32[]{:S(2)}) collective-permute-start(f32[16,128]{1,0:T(8,128)S(1)} %row_pass.3.refs_0_), channel_id=1, source_target_pairs={{0,4},{1,5},{2,6},{3,7},{4,0},{5,1},{6,2},{7,3},{8,12},{9,13},{10,... | collective-permute-start | bytes 24584 | tf_op jit(solution)/shard_map/ppermute | solution.py:22
  95.8 1.5 collective-permute-start.26
  97.3 1.1 collective-permute-done.28.refs_3_
  99.5 3.3 %column_pass.3 = (f32[16,128]{1,0:T(8,128)S(1)}, f32[16,128]{1,0:T(8,128)S(1)}, f32[16,128]{1,0:T(8,128)}) custom-call(s32[56,21]{1,0:T(8,128)S(1)} %copy-done.2, f32[257,128,128]{2,1,0:T(8,128)S(1)} %get-tuple-element.27.s_ref, bf16[257,128,128]{2,1,0:T(8,128)(2,1)S(1)} %get-tuple-element.29.w_ref, f32[16,128]{1,0:T(8,128)S(1)} %get-tuple-element.30.m_ref, ...), custom_call_target="tpu_custom_call" | custom-call | tf_op jit(solution)/shard_map/column_pass/pallas_call | solution.py:504
  102.7 2.7 %collective-permute-start.31 = (f32[16,128]{1,0:T(8,128)S(1)}, f32[16,128]{1,0:T(8,128)S(1)}, u32[]{:S(2)}, u32[]{:S(2)}) collective-permute-start(f32[16,128]{1,0:T(8,128)S(1)} %get-tuple-element.36.refs_0_), channel_id=1, source_target_pairs={{0,24},{8,16},{16,8},{24,0},{1,25},{9,17},{17,9},{25,1},{2,26},{10... | collective-permute-start | bytes 24584 | tf_op jit(solution)/shard_map/ppermute | solution.py:22
  106.2 1.1 collective-permute-done.31.refs_3_
  107.3 1.8 %collective-permute-done.30.refs_2_ = f32[16,128]{1,0:T(8,128)S(1)} collective-permute-done((f32[16,128]{1,0:T(8,128)S(1)}, f32[16,128]{1,0:T(8,128)S(1)}, u32[]{:S(2)}, u32[]{:S(2)}) %collective-permute-start.30) | collective-permute-done | bytes 8224 | tf_op jit(solution)/shard_map/ppermute | solution.py:22
  109.1 6.8 %plan.1 = (bf16[2048,128]{1,0:T(8,128)(2,1)S(1)}, bf16[2048,128]{1,0:T(8,128)(2,1)S(1)}, bf16[2048,128]{1,0:T(8,128)(2,1)S(1)}, bf16[2048,128]{1,0:T(8,128)(2,1)S(1)}, f32[8,128]{1,0:T(8,128)}) custom-call(s32[56,21]{1,0:T(8,128)S(1)} %copy-done.2, f32[257,128,128]{2,1,0:T(8,128)S(1)} %get-tuple-element.27.s_ref, f32[16,128]{1,0:T(8,128)S(1)} %get-tuple-element.34.r_ref, ...), custom_call_target="tpu_custom_call" | custom-call | tf_op jit(solution)/shard_map/plan/pallas_call | solution.py:514
  116.7 1.3 collective-permute-start.32
  118.0 14.1 %collective-permute-done.33 = bf16[2048,128]{1,0:T(8,128)(2,1)S(1)} collective-permute-done((bf16[2048,128]{1,0:T(8,128)(2,1)S(1)}, bf16[2048,128]{1,0:T(8,128)(2,1)S(1)}, u32[]{:S(2)}, u32[]{:S(2)}) %collective-permute-start.33) | collective-permute-done | bytes 524320 | tf_op jit(solution)/shard_map/ppermute | solution.py:22
  132.8 6.6 %collective-permute-done.32 = bf16[2048,128]{1,0:T(8,128)(2,1)S(1)} collective-permute-done((bf16[2048,128]{1,0:T(8,128)(2,1)S(1)}, bf16[2048,128]{1,0:T(8,128)(2,1)S(1)}, u32[]{:S(2)}, u32[]{:S(2)}) %collective-permute-start.32) | collective-permute-done | bytes 524320 | tf_op jit(solution)/shard_map/ppermute | solution.py:22
  139.3 8.7 %collective-permute-done.34 = bf16[2048,128]{1,0:T(8,128)(2,1)S(1)} collective-permute-done((bf16[2048,128]{1,0:T(8,128)(2,1)S(1)}, bf16[2048,128]{1,0:T(8,128)(2,1)S(1)}, u32[]{:S(2)}, u32[]{:S(2)}) %collective-permute-start.34) | collective-permute-done | bytes 524320 | tf_op jit(solution)/shard_map/ppermute | solution.py:22
  148.0 1.0 add_convert_fusion
  (44 shorter events, 11.2 us)
Async XLA Ops:
  1.7 9.3 %collective-permute-start.2 = (bf16[512,256]{1,0:T(8,128)(2,1)S(1)}, bf16[512,256]{1,0:T(8,128)(2,1)S(1)}, u32[]{:S(2)}, u32[]{:S(2)}) collective-permute-start(bf16[512,256]{1,0:T(8,128)(2,1)S(1)} %get-tuple-element.23), channel_id=1, source_target_pairs={{0,16},{8,24},{16,0},{24,8},{1,17},{9,25},{17,1},{25,9},{2,18},{10... | collective-permute-start | bytes 786440 | tf_op jit(solution)/shard_map/ppermute | solution.py:22
  4.7 7.8 %collective-permute-start.1 = (bf16[512,256]{1,0:T(8,128)(2,1)S(1)}, bf16[512,256]{1,0:T(8,128)(2,1)S(1)}, u32[]{:S(2)}, u32[]{:S(2)}) collective-permute-start(bf16[512,256]{1,0:T(8,128)(2,1)S(1)} %get-tuple-element.26), channel_id=1, source_target_pairs={{0,8},{8,0},{16,24},{24,16},{1,9},{9,1},{17,25},{25,17},{2,10},{10... | collective-permute-start | bytes 786440 | tf_op jit(solution)/shard_map/ppermute | solution.py:22
  12.5 6.9 %collective-permute-start.3 = (bf16[512,256]{1,0:T(8,128)(2,1)S(1)}, bf16[512,256]{1,0:T(8,128)(2,1)S(1)}, u32[]{:S(2)}, u32[]{:S(2)}) collective-permute-start(bf16[512,256]{1,0:T(8,128)(2,1)S(1)} %get-tuple-element.23), channel_id=1, source_target_pairs={{0,8},{8,0},{16,24},{24,16},{1,9},{9,1},{17,25},{25,17},{2,10},{10... | collective-permute-start | bytes 786440 | tf_op jit(solution)/shard_map/ppermute | solution.py:22
  14.0 7.9 %collective-permute-start.4 = (bf16[512,256]{1,0:T(8,128)(2,1)S(1)}, bf16[512,256]{1,0:T(8,128)(2,1)S(1)}, u32[]{:S(2)}, u32[]{:S(2)}) collective-permute-start(bf16[512,256]{1,0:T(8,128)(2,1)S(1)} %get-tuple-element.26), channel_id=1, source_target_pairs={{0,16},{8,24},{16,0},{24,8},{1,17},{9,25},{17,1},{25,9},{2,18},{10... | collective-permute-start | bytes 786440 | tf_op jit(solution)/shard_map/ppermute | solution.py:22
  15.3 13.0 %copy-start.3 = (s32[16,8]{1,0:T(8,128)}, s32[16,8]{1,0:T(8,128)S(1)}, u32[]{:S(2)}) copy-start(s32[16,8]{1,0:T(8,128)S(1)} %copy.7.own_ref) | copy-start | bytes 1540
  15.3 1.2 collective-permute-start
  15.3 21.3 %collective-permute-start.7 = (bf16[1024,256]{1,0:T(8,128)(2,1)}, bf16[1024,256]{1,0:T(8,128)(2,1)S(1)}, u32[]{:S(2)}, u32[]{:S(2)}) collective-permute-start(bf16[1024,256]{1,0:T(8,128)(2,1)} %refs_0_.1), channel_id=1, source_target_pairs={{0,1},{1,0},{2,3},{3,2},{4,5},{5,4},{6,7},{7,6},{8,9},{9,8},{10,11... | collective-permute-start | bytes 1572872 | tf_op jit(solution)/shard_map/ppermute | solution.py:22
  15.8 6.8 %collective-permute-start.9 = (bf16[512,256]{1,0:T(8,128)(2,1)S(1)}, bf16[512,256]{1,0:T(8,128)(2,1)S(1)}, u32[]{:S(2)}, u32[]{:S(2)}) collective-permute-start(bf16[512,256]{1,0:T(8,128)(2,1)S(1)} %collective-permute-done.1.refs_2_), channel_id=1, source_target_pairs={{0,1},{1,0},{2,3},{3,2},{4,5},{5,4},{6,7},{7,6},{8,9},{9,8},{10,11... | collective-permute-start | bytes 786440 | tf_op jit(solution)/shard_map/ppermute | solution.py:22
  16.4 11.8 %copy-start.4 = (s32[16,8]{1,0:T(8,128)}, s32[16,8]{1,0:T(8,128)S(1)}, u32[]{:S(2)}) copy-start(s32[16,8]{1,0:T(8,128)S(1)} %collective-permute-done.other_ref) | copy-start | bytes 1540
  16.4 9.8 %collective-permute-start.6 = (bf16[512,256]{1,0:T(8,128)(2,1)S(1)}, bf16[512,256]{1,0:T(8,128)(2,1)S(1)}, u32[]{:S(2)}, u32[]{:S(2)}) collective-permute-start(bf16[512,256]{1,0:T(8,128)(2,1)S(1)} %collective-permute-done.1.refs_2_), channel_id=1, source_target_pairs={{0,16},{8,24},{16,0},{24,8},{1,17},{9,25},{17,1},{25,9},{2,18},{10... | collective-permute-start | bytes 786440 | tf_op jit(solution)/shard_map/ppermute | solution.py:22
  19.4 6.8 %collective-permute-start.10 = (bf16[512,256]{1,0:T(8,128)(2,1)S(1)}, bf16[512,256]{1,0:T(8,128)(2,1)S(1)}, u32[]{:S(2)}, u32[]{:S(2)}) collective-permute-start(bf16[512,256]{1,0:T(8,128)(2,1)S(1)} %collective-permute-done.2.refs_3_), channel_id=1, source_target_pairs={{0,1},{1,0},{2,3},{3,2},{4,5},{5,4},{6,7},{7,6},{8,9},{9,8},{10,11... | collective-permute-start | bytes 786440 | tf_op jit(solution)/shard_map/ppermute | solution.py:22
  21.9 6.4 %collective-permute-start.5 = (bf16[512,256]{1,0:T(8,128)(2,1)S(1)}, bf16[512,256]{1,0:T(8,128)(2,1)S(1)}, u32[]{:S(2)}, u32[]{:S(2)}) collective-permute-start(bf16[512,256]{1,0:T(8,128)(2,1)S(1)} %collective-permute-done.2.refs_3_), channel_id=1, source_target_pairs={{0,8},{8,0},{16,24},{24,16},{1,9},{9,1},{17,25},{25,17},{2,10},{10... | collective-permute-start | bytes 786440 | tf_op jit(solution)/shard_map/ppermute | solution.py:22
  22.6 14.0 %collective-permute-start.8 = (bf16[512,256]{1,0:T(8,128)(2,1)S(1)}, bf16[512,256]{1,0:T(8,128)(2,1)S(1)}, u32[]{:S(2)}, u32[]{:S(2)}) collective-permute-start(bf16[512,256]{1,0:T(8,128)(2,1)S(1)} %collective-permute-done.3.refs_1_), channel_id=1, source_target_pairs={{0,1},{1,0},{2,3},{3,2},{4,5},{5,4},{6,7},{7,6},{8,9},{9,8},{10,11... | collective-permute-start | bytes 786440 | tf_op jit(solution)/shard_map/ppermute | solution.py:22
  26.2 10.4 %collective-permute-start.11 = (bf16[512,256]{1,0:T(8,128)(2,1)S(1)}, bf16[512,256]{1,0:T(8,128)(2,1)S(1)}, u32[]{:S(2)}, u32[]{:S(2)}) collective-permute-start(bf16[512,256]{1,0:T(8,128)(2,1)S(1)} %collective-permute-done.4.refs_4_), channel_id=1, source_target_pairs={{0,1},{1,0},{2,3},{3,2},{4,5},{5,4},{6,7},{7,6},{8,9},{9,8},{10,11... | collective-permute-start | bytes 786440 | tf_op jit(solution)/shard_map/ppermute | solution.py:22
  26.2 10.4 %collective-permute-start.13 = (bf16[512,256]{1,0:T(8,128)(2,1)S(1)}, bf16[512,256]{1,0:T(8,128)(2,1)S(1)}, u32[]{:S(2)}, u32[]{:S(2)}) collective-permute-start(bf16[512,256]{1,0:T(8,128)(2,1)S(1)} %collective-permute-done.6.refs_6_), channel_id=1, source_target_pairs={{0,1},{1,0},{2,3},{3,2},{4,5},{5,4},{6,7},{7,6},{8,9},{9,8},{10,11... | collective-permute-start | bytes 786440 | tf_op jit(solution)/shard_map/ppermute | solution.py:22
  28.2 8.3 %collective-permute-start.12 = (bf16[512,256]{1,0:T(8,128)(2,1)S(1)}, bf16[512,256]{1,0:T(8,128)(2,1)}, u32[]{:S(2)}, u32[]{:S(2)}) collective-permute-start(bf16[512,256]{1,0:T(8,128)(2,1)S(1)} %collective-permute-done.5.refs_5_), channel_id=1, source_target_pairs={{0,1},{1,0},{2,3},{3,2},{4,5},{5,4},{6,7},{7,6},{8,9},{9,8},{10,11... | collective-permute-start | bytes 786440 | tf_op jit(solution)/shard_map/ppermute | solution.py:22
  36.6 2.2 %copy-start = (bf16[2048,1024]{1,0:T(8,128)(2,1)S(1)}, bf16[2048,1024]{1,0:T(8,128)(2,1)}, u32[]{:S(2)}) copy-start(bf16[2048,1024]{1,0:T(8,128)(2,1)} %e_hbm_ref.1) | copy-start | bytes 12582916
  38.8 1.0 copy-start.1
  39.8 0.7 copy-start.2
  50.2 5.5 %collective-permute-start.16 = (f32[16,128]{1,0:T(8,128)S(1)}, f32[16,128]{1,0:T(8,128)S(1)}, u32[]{:S(2)}, u32[]{:S(2)}) collective-permute-start(f32[16,128]{1,0:T(8,128)S(1)} %get-tuple-element.28.refs_0_), channel_id=1, source_target_pairs={{0,6},{1,7},{2,4},{3,5},{4,2},{5,3},{6,0},{7,1},{8,14},{9,15},{10,... | collective-permute-start | bytes 24584 | tf_op jit(solution)/shard_map/ppermute | solution.py:22
  53.4 4.5 %collective-permute-start.15 = (f32[16,128]{1,0:T(8,128)S(1)}, f32[16,128]{1,0:T(8,128)S(1)}, u32[]{:S(2)}, u32[]{:S(2)}) collective-permute-start(f32[16,128]{1,0:T(8,128)S(1)} %get-tuple-element.28.refs_0_), channel_id=1, source_target_pairs={{0,4},{1,5},{2,6},{3,7},{4,0},{5,1},{6,2},{7,3},{8,12},{9,13},{10,... | collective-permute-start | bytes 24584 | tf_op jit(solution)/shard_map/ppermute | solution.py:22
  53.4 4.5 %collective-permute-start.14 = (f32[16,128]{1,0:T(8,128)S(1)}, f32[16,128]{1,0:T(8,128)S(1)}, u32[]{:S(2)}, u32[]{:S(2)}) collective-permute-start(f32[16,128]{1,0:T(8,128)S(1)} %get-tuple-element.28.refs_0_), channel_id=1, source_target_pairs={{0,2},{1,3},{2,0},{3,1},{4,6},{5,7},{6,4},{7,5},{8,10},{9,11},{10,... | collective-permute-start | bytes 24584 | tf_op jit(solution)/shard_map/ppermute | solution.py:22
  61.0 6.3 %collective-permute-start.19 = (f32[16,128]{1,0:T(8,128)S(1)}, f32[16,128]{1,0:T(8,128)S(1)}, u32[]{:S(2)}, u32[]{:S(2)}) collective-permute-start(f32[16,128]{1,0:T(8,128)S(1)} %get-tuple-element.32.refs_0_), channel_id=1, source_target_pairs={{0,24},{8,16},{16,8},{24,0},{1,25},{9,17},{17,9},{25,1},{2,26},{10... | collective-permute-start | bytes 24584 | tf_op jit(solution)/shard_map/ppermute | solution.py:22
  65.7 3.7 %collective-permute-start.18 = (f32[16,128]{1,0:T(8,128)S(1)}, f32[16,128]{1,0:T(8,128)S(1)}, u32[]{:S(2)}, u32[]{:S(2)}) collective-permute-start(f32[16,128]{1,0:T(8,128)S(1)} %get-tuple-element.32.refs_0_), channel_id=1, source_target_pairs={{0,16},{8,24},{16,0},{24,8},{1,17},{9,25},{17,1},{25,9},{2,18},{10... | collective-permute-start | bytes 24584 | tf_op jit(solution)/shard_map/ppermute | solution.py:22
  66.5 3.7 %collective-permute-start.17 = (f32[16,128]{1,0:T(8,128)S(1)}, f32[16,128]{1,0:T(8,128)S(1)}, u32[]{:S(2)}, u32[]{:S(2)}) collective-permute-start(f32[16,128]{1,0:T(8,128)S(1)} %get-tuple-element.32.refs_0_), channel_id=1, source_target_pairs={{0,8},{8,0},{16,24},{24,16},{1,9},{9,1},{17,25},{25,17},{2,10},{10... | collective-permute-start | bytes 24584 | tf_op jit(solution)/shard_map/ppermute | solution.py:22
  73.2 5.5 %collective-permute-start.22 = (f32[16,128]{1,0:T(8,128)S(1)}, f32[16,128]{1,0:T(8,128)S(1)}, u32[]{:S(2)}, u32[]{:S(2)}) collective-permute-start(f32[16,128]{1,0:T(8,128)S(1)} %row_pass.2.refs_0_), channel_id=1, source_target_pairs={{0,6},{1,7},{2,4},{3,5},{4,2},{5,3},{6,0},{7,1},{8,14},{9,15},{10,... | collective-permute-start | bytes 24584 | tf_op jit(solution)/shard_map/ppermute | solution.py:22
  75.1 4.6 %collective-permute-start.21 = (f32[16,128]{1,0:T(8,128)S(1)}, f32[16,128]{1,0:T(8,128)S(1)}, u32[]{:S(2)}, u32[]{:S(2)}) collective-permute-start(f32[16,128]{1,0:T(8,128)S(1)} %row_pass.2.refs_0_), channel_id=1, source_target_pairs={{0,4},{1,5},{2,6},{3,7},{4,0},{5,1},{6,2},{7,3},{8,12},{9,13},{10,... | collective-permute-start | bytes 24584 | tf_op jit(solution)/shard_map/ppermute | solution.py:22
  76.0 3.7 %collective-permute-start.20 = (f32[16,128]{1,0:T(8,128)S(1)}, f32[16,128]{1,0:T(8,128)S(1)}, u32[]{:S(2)}, u32[]{:S(2)}) collective-permute-start(f32[16,128]{1,0:T(8,128)S(1)} %row_pass.2.refs_0_), channel_id=1, source_target_pairs={{0,2},{1,3},{2,0},{3,1},{4,6},{5,7},{6,4},{7,5},{8,10},{9,11},{10,... | collective-permute-start | bytes 24584 | tf_op jit(solution)/shard_map/ppermute | solution.py:22
  83.2 4.5 %collective-permute-start.25 = (f32[16,128]{1,0:T(8,128)S(1)}, f32[16,128]{1,0:T(8,128)S(1)}, u32[]{:S(2)}, u32[]{:S(2)}) collective-permute-start(f32[16,128]{1,0:T(8,128)S(1)} %get-tuple-element.33.refs_0_), channel_id=1, source_target_pairs={{0,24},{8,16},{16,8},{24,0},{1,25},{9,17},{17,9},{25,1},{2,26},{10... | collective-permute-start | bytes 24584 | tf_op jit(solution)/shard_map/ppermute | solution.py:22
  85.0 3.7 %collective-permute-start.24 = (f32[16,128]{1,0:T(8,128)S(1)}, f32[16,128]{1,0:T(8,128)S(1)}, u32[]{:S(2)}, u32[]{:S(2)}) collective-permute-start(f32[16,128]{1,0:T(8,128)S(1)} %get-tuple-element.33.refs_0_), channel_id=1, source_target_pairs={{0,16},{8,24},{16,0},{24,8},{1,17},{9,25},{17,1},{25,9},{2,18},{10... | collective-permute-start | bytes 24584 | tf_op jit(solution)/shard_map/ppermute | solution.py:22
  86.1 3.7 %collective-permute-start.23 = (f32[16,128]{1,0:T(8,128)S(1)}, f32[16,128]{1,0:T(8,128)S(1)}, u32[]{:S(2)}, u32[]{:S(2)}) collective-permute-start(f32[16,128]{1,0:T(8,128)S(1)} %get-tuple-element.33.refs_0_), channel_id=1, source_target_pairs={{0,8},{8,0},{16,24},{24,16},{1,9},{9,1},{17,25},{25,17},{2,10},{10... | collective-permute-start | bytes 24584 | tf_op jit(solution)/shard_map/ppermute | solution.py:22
  92.8 5.5 %collective-permute-start.28 = (f32[16,128]{1,0:T(8,128)S(1)}, f32[16,128]{1,0:T(8,128)S(1)}, u32[]{:S(2)}, u32[]{:S(2)}) collective-permute-start(f32[16,128]{1,0:T(8,128)S(1)} %row_pass.3.refs_0_), channel_id=1, source_target_pairs={{0,6},{1,7},{2,4},{3,5},{4,2},{5,3},{6,0},{7,1},{8,14},{9,15},{10,... | collective-permute-start | bytes 24584 | tf_op jit(solution)/shard_map/ppermute | solution.py:22
  94.1 4.5 %collective-permute-start.27 = (f32[16,128]{1,0:T(8,128)S(1)}, f32[16,128]{1,0:T(8,128)S(1)}, u32[]{:S(2)}, u32[]{:S(2)}) collective-permute-start(f32[16,128]{1,0:T(8,128)S(1)} %row_pass.3.refs_0_), channel_id=1, source_target_pairs={{0,4},{1,5},{2,6},{3,7},{4,0},{5,1},{6,2},{7,3},{8,12},{9,13},{10,... | collective-permute-start | bytes 24584 | tf_op jit(solution)/shard_map/ppermute | solution.py:22
  95.8 3.7 %collective-permute-start.26 = (f32[16,128]{1,0:T(8,128)S(1)}, f32[16,128]{1,0:T(8,128)S(1)}, u32[]{:S(2)}, u32[]{:S(2)}) collective-permute-start(f32[16,128]{1,0:T(8,128)S(1)} %row_pass.3.refs_0_), channel_id=1, source_target_pairs={{0,2},{1,3},{2,0},{3,1},{4,6},{5,7},{6,4},{7,5},{8,10},{9,11},{10,... | collective-permute-start | bytes 24584 | tf_op jit(solution)/shard_map/ppermute | solution.py:22
  102.7 4.5 %collective-permute-start.31 = (f32[16,128]{1,0:T(8,128)S(1)}, f32[16,128]{1,0:T(8,128)S(1)}, u32[]{:S(2)}, u32[]{:S(2)}) collective-permute-start(f32[16,128]{1,0:T(8,128)S(1)} %get-tuple-element.36.refs_0_), channel_id=1, source_target_pairs={{0,24},{8,16},{16,8},{24,0},{1,25},{9,17},{17,9},{25,1},{2,26},{10... | collective-permute-start | bytes 24584 | tf_op jit(solution)/shard_map/ppermute | solution.py:22
  105.5 3.7 %collective-permute-start.30 = (f32[16,128]{1,0:T(8,128)S(1)}, f32[16,128]{1,0:T(8,128)S(1)}, u32[]{:S(2)}, u32[]{:S(2)}) collective-permute-start(f32[16,128]{1,0:T(8,128)S(1)} %get-tuple-element.36.refs_0_), channel_id=1, source_target_pairs={{0,16},{8,24},{16,0},{24,8},{1,17},{9,25},{17,1},{25,9},{2,18},{10... | collective-permute-start | bytes 24584 | tf_op jit(solution)/shard_map/ppermute | solution.py:22
  105.5 3.7 %collective-permute-start.29 = (f32[16,128]{1,0:T(8,128)S(1)}, f32[16,128]{1,0:T(8,128)S(1)}, u32[]{:S(2)}, u32[]{:S(2)}) collective-permute-start(f32[16,128]{1,0:T(8,128)S(1)} %get-tuple-element.36.refs_0_), channel_id=1, source_target_pairs={{0,8},{8,0},{16,24},{24,16},{1,9},{9,1},{17,25},{25,17},{2,10},{10... | collective-permute-start | bytes 24584 | tf_op jit(solution)/shard_map/ppermute | solution.py:22
  115.9 16.1 %collective-permute-start.33 = (bf16[2048,128]{1,0:T(8,128)(2,1)S(1)}, bf16[2048,128]{1,0:T(8,128)(2,1)S(1)}, u32[]{:S(2)}, u32[]{:S(2)}) collective-permute-start(bf16[2048,128]{1,0:T(8,128)(2,1)S(1)} %get-tuple-element.40), channel_id=1, source_target_pairs={{0,2},{1,3},{2,0},{3,1},{4,6},{5,7},{6,4},{7,5},{8,10},{9,11},{10,... | collective-permute-start | bytes 1572872 | tf_op jit(solution)/shard_map/ppermute | solution.py:22
  116.7 22.6 %collective-permute-start.32 = (bf16[2048,128]{1,0:T(8,128)(2,1)S(1)}, bf16[2048,128]{1,0:T(8,128)(2,1)S(1)}, u32[]{:S(2)}, u32[]{:S(2)}) collective-permute-start(bf16[2048,128]{1,0:T(8,128)(2,1)S(1)} %get-tuple-element.38), channel_id=1, source_target_pairs={{0,2},{1,3},{2,0},{3,1},{4,6},{5,7},{6,4},{7,5},{8,10},{9,11},{10,... | collective-permute-start | bytes 1572872 | tf_op jit(solution)/shard_map/ppermute | solution.py:22
  132.2 15.8 %collective-permute-start.34 = (bf16[2048,128]{1,0:T(8,128)(2,1)S(1)}, bf16[2048,128]{1,0:T(8,128)(2,1)S(1)}, u32[]{:S(2)}, u32[]{:S(2)}) collective-permute-start(bf16[2048,128]{1,0:T(8,128)(2,1)S(1)} %add_convert_fusion.1), channel_id=1, source_target_pairs={{0,4},{1,5},{2,6},{3,7},{4,0},{5,1},{6,2},{7,3},{8,12},{9,13},{10,... | collective-permute-start | bytes 1572872 | tf_op jit(solution)/shard_map/ppermute | solution.py:22

commit v8 on v7

--- a/solution.py
+++ b/solution.py
@@ -36,68 +36,49 @@
 class Table:
     def __init__(self, row_tiles, columns):
         self.row_tiles, self.columns = row_tiles, columns
-        self.end = max(row_tiles, columns) + 4
+        self.line = max(row_tiles, columns) + 8
         self.column_base = row_tiles
         self.pair_base = row_tiles + columns
-        self.mask_base = self.pair_base + columns // 2
-        self.shape = (self.mask_base + row_tiles, self.end + 1)
+        self.mask_at = (self.pair_base + columns // 2) * self.line
         self.dummy = row_tiles * columns
 
+    def build(self, mask):
+        across = mask.T
+        pairs = jnp.max(across.reshape(self.columns // 2, 2, self.row_tiles), axis=1)
+        lines = [self.lines(mask), self.lines(across), self.lines(pairs)]
+        return jnp.concatenate([part.reshape(-1) for part in lines] + [mask.reshape(-1)])
+
+    def lines(self, mask):
+        size = mask.shape[1]
+        at = jnp.arange(size, dtype=jnp.int32)
+        slot = jnp.arange(self.line, dtype=jnp.int32)
+        before = jnp.sum(jnp.where(at[None, :] < at[:, None], mask[:, None, :], 0), axis=2)
+        hit = (mask[:, None, :] == 1) & (before[:, None, :] == slot[None, :, None])
+        places = jnp.sum(jnp.where(hit, at[None, None, :] - size, 0), axis=2) + size
+        count = jnp.sum(mask, axis=1, keepdims=True)
+        places = jnp.where(slot[None, :] == self.line - 2, (count + 1) // 2, places)
+        return jnp.where(slot[None, :] == self.line - 1, (count + 3) // 4, places)
+
+    def steps(self, ref, line, unroll):
+        return ref[line * self.line + self.line - (2 if unroll == 2 else 1)]
+
+    def entry(self, ref, line, k):
+        return ref[line * self.line + k]
+
+    def allowed(self, ref, t, u):
+        return ref[self.mask_at + t * self.columns + u]
+
     def loop(self, ref, line, unroll, step, start):
-        count = (ref[line, self.end] + unroll - 1) // unroll
-
         def several(k, a):
             for i in range(unroll):
-                a = step(ref[line, unroll * k + i], a)
+                a = step(self.entry(ref, line, unroll * k + i), a)
             return a
 
-        return lax.fori_loop(0, count, several, start)
+        return lax.fori_loop(0, self.steps(ref, line, unroll), several, start)
 
     def place(self, t, u):
         padding = (t == self.row_tiles) | (u == self.columns)
         return jnp.where(padding, self.dummy, t * self.columns + u)
-
-
-def setup_kernel(table, own_ref, other_ref, out_ref):
-    core = lax.rem(lax.axis_index("proto"), 2)
-    half = table.columns // 2
-
-    def mask_row(t, carry):
-        for u in range(half):
-            out_ref[table.mask_base + t, core * half + u] = jnp.where(own_ref[t, u] == 1, 1, 0)
-            out_ref[table.mask_base + t, (1 - core) * half + u] = jnp.where(other_ref[t, u] == 1, 1, 0)
-        return carry
-
-    lax.fori_loop(0, table.row_tiles, mask_row, 0)
-
-    def fill(line, size, allowed):
-        count = jnp.int32(0)
-        for i in range(size):
-            out_ref[line, count] = i
-            count = count + allowed(i)
-        for i in range(4):
-            out_ref[line, count + i] = size
-        out_ref[line, table.end] = count
-
-    def row_list(t, carry):
-        fill(t, table.columns, lambda u: out_ref[table.mask_base + t, u])
-        return carry
-
-    def column_list(u, carry):
-        fill(table.column_base + u, table.row_tiles, lambda t: out_ref[table.mask_base + t, u])
-        return carry
-
-    def pair_list(p, carry):
-        fill(
-            table.pair_base + p,
-            table.row_tiles,
-            lambda t: jnp.maximum(out_ref[table.mask_base + t, 2 * p], out_ref[table.mask_base + t, 2 * p + 1]),
-        )
-        return carry
-
-    lax.fori_loop(0, table.row_tiles, row_list, 0)
-    lax.fori_loop(0, table.columns, column_list, 0)
-    lax.fori_loop(0, table.columns // 2, pair_list, 0)
 
 
 def blank():
@@ -135,60 +116,110 @@
     return found.T[: len(tiles)]
 
 
-def panel_kernel(table, row_blocks, first_features, table_ref, e_hbm_ref, *refs):
-    pieces, (s_ref, p_ref, out_ref, acc_ref, e_ref, sem) = refs[:-6], refs[-6:]
-    load = pltpu.make_async_copy(e_hbm_ref, e_ref, sem.at[0])
-    load.start()
+class Piece:
+    def __init__(self, own, first, owner):
+        self.own, self.first, self.owner = own, first, owner
+
+    def copy_to(self, p_ref, piece):
+        core, me = lax.rem(lax.axis_index("proto"), 2), lax.axis_index("row")
+        rows, width = piece.shape
+        first = (core if self.own else 1 - core) * (p_ref.shape[0] // 2) + self.first
+        start = 0
+        if self.owner is not None:
+            start = pl.multiple_of(jnp.bitwise_xor(me, self.owner) * width, TILE)
+        p_ref[pl.ds(pl.multiple_of(first, TILE), rows), pl.ds(start, width)] = piece[...]
+
+
+def score_pairs(table, table_ref, e_ref, p_ref, s_ref, features, add, done):
     row_tiles, columns = table.row_tiles, table.columns
     scale = 4.0 / math.sqrt(e_ref.shape[1])
-    core = lax.rem(lax.axis_index("proto"), 2)
+
+    def one_pair(pair, carry):
+        line = table.pair_base + pair
+        spans = features(pair)
+
+        def four_tiles(k, carry):
+            at = [jnp.minimum(table.entry(table_ref, line, 4 * k + i), row_tiles - 1) for i in range(4)]
+            product = None
+            for span in spans:
+                rows = jnp.concatenate(
+                    [e_ref[pl.ds(pl.multiple_of(t * TILE, TILE), TILE), span] for t in at], axis=0
+                )
+                block = p_ref[pl.ds(pl.multiple_of(pair * 2 * TILE, TILE), 2 * TILE), span]
+                part = lax.dot_general(
+                    rows, block, (((1,), (1,)), ((), ())), preferred_element_type=jnp.float32
+                )
+                product = part if product is None else product + part
+            product = scale * product
+            tiles = {}
+            for i, t in enumerate(at):
+                for side in range(2):
+                    where = t * columns + 2 * pair + side
+                    tile = product[i * TILE : (i + 1) * TILE, side * TILE : (side + 1) * TILE]
+                    tiles[i, side] = (where, s_ref[where] + tile if add else tile)
+            for where, tile in tiles.values():
+                s_ref[where] = tile
+            if done is not None:
+                for i, t in enumerate(at):
+                    done(t, 2 * pair, tiles[i, 0][1], tiles[i, 1][1])
+            return carry
+
+        return lax.fori_loop(0, table.steps(table_ref, line, 4), four_tiles, carry)
+
+    lax.fori_loop(0, columns // 2, one_pair, 0)
+
+
+def quarters(owners, p_ref, columns):
     me = lax.axis_index("row")
-    protos = p_ref.shape[0] // 2
-    for n, piece in enumerate(pieces):
-        group, within = n * 2 // len(pieces), n % (len(pieces) // 2)
-        rows, width = piece.shape
-        first = (core if group == 0 else 1 - core) * protos + row_blocks[within]
-        start = 0
-        if first_features[within] is not None:
-            start = pl.multiple_of(jnp.bitwise_xor(me, first_features[within]) * width, TILE)
-        place = p_ref.at[pl.ds(pl.multiple_of(first, TILE), rows), pl.ds(start, width)]
-        if n == 0:
-            own = pltpu.make_async_copy(piece, place, sem.at[1])
-            own.start()
-        else:
-            place[...] = piece[...]
+    width = p_ref.shape[1] // 4
+    pairs = columns // 4
+
+    def features(pair):
+        top = lax.rem(pair, pairs) < pairs // 2
+        spans = []
+        for first, second in owners:
+            owner = jnp.bitwise_xor(me, jnp.where(top, first, second))
+            spans.append(pl.ds(pl.multiple_of(owner * width, TILE), width))
+        return spans
+
+    return features
+
+
+def early_panel_kernel(table, places, table_ref, e_hbm_ref, *refs):
+    pieces, (s_ref, p_ref, e_ref, sem) = refs[:-4], refs[-4:]
+    load = pltpu.make_async_copy(e_hbm_ref, e_ref, sem)
+    load.start()
+    for place, piece in zip(places, pieces):
+        place.copy_to(p_ref, piece)
     s_ref[table.dummy] = lowest()
+    load.wait()
+    features = quarters([(0, 0), (2, 1)], p_ref, table.columns)
+    score_pairs(table, table_ref, e_ref, p_ref, s_ref, features, False, None)
+
+
+def panel_kernel(table, places, add, table_ref, e_ref, *refs):
+    pieces, (s_ref, p_ref, out_ref, acc_ref) = refs[:-4], refs[-4:]
+    if add:
+        pieces = pieces[:-2]
+    row_tiles = table.row_tiles
+    for place, piece in zip(places, pieces):
+        place.copy_to(p_ref, piece)
     for t in range(row_tiles):
         acc_ref[t] = lowest()
-    own.wait()
-    load.wait()
-
-    def one_pair(pair, carry):
-        line = table.pair_base + pair
-
-        def four_tiles(k, carry):
-            at = [jnp.minimum(table_ref[line, 4 * k + i], row_tiles - 1) for i in range(4)]
-            rows = jnp.concatenate(
-                [e_ref[pl.ds(pl.multiple_of(t * TILE, TILE), TILE), :] for t in at], axis=0
-            )
-            block = p_ref[pl.ds(pl.multiple_of(pair * 2 * TILE, TILE), 2 * TILE), :]
-            product = scale * lax.dot_general(
-                rows, block, (((1,), (1,)), ((), ())), preferred_element_type=jnp.float32
-            )
-            for i, t in enumerate(at):
-                peak = acc_ref[t]
-                for side in range(2):
-                    u = 2 * pair + side
-                    tile = product[i * TILE : (i + 1) * TILE, side * TILE : (side + 1) * TILE]
-                    s_ref[t * columns + u] = tile
-                    off = jnp.where(table_ref[table.mask_base + t, u] == 1, 0.0, NEGATIVE)
-                    peak = jnp.maximum(peak, tile + off)
-                acc_ref[t] = peak
-            return carry
-
-        return lax.fori_loop(0, (table_ref[line, table.end] + 3) // 4, four_tiles, carry)
-
-    lax.fori_loop(0, columns // 2, one_pair, 0)
+
+    def done(t, u, left, right):
+        peak = acc_ref[t]
+        for side, tile in enumerate((left, right)):
+            off = jnp.where(table.allowed(table_ref, t, u + side) == 1, 0.0, NEGATIVE)
+            peak = jnp.maximum(peak, tile + off)
+        acc_ref[t] = peak
+
+    if add:
+        features = quarters([(1, 2), (3, 3)], p_ref, table.columns)
+    else:
+        s_ref[table.dummy] = lowest()
+        features = lambda pair: [slice(None)]
+    score_pairs(table, table_ref, e_ref, p_ref, s_ref, features, add, done)
 
     lane = lax.broadcasted_iota(jnp.int32, (TILE, TILE), 1)
     peaks = blank()
@@ -361,14 +392,14 @@
         block = jnp.concatenate(blocks, axis=1)
 
         def four_tiles(k, carry):
-            at = [table_ref[line, 4 * k + i] for i in range(4)]
+            at = [table.entry(table_ref, line, 4 * k + i) for i in range(4)]
             inside = [jnp.minimum(t, row_tiles - 1) for t in at]
             strips = []
             for t, real in zip(at, inside):
                 sides = []
                 for side in range(2):
                     u = 2 * pair + side
-                    good = (t < row_tiles) & (table_ref[table.mask_base + real, u] == 1)
+                    good = (t < row_tiles) & (table.allowed(table_ref, real, u) == 1)
                     tile = s_ref[jnp.where(good, t * columns + u, table.dummy)]
                     sides.append(jnp.exp(tile + wide_ref[real] + c_ref[pl.ds(u, 1), :]).astype(jnp.bfloat16))
                 strips.append(jnp.concatenate(sides, axis=1))
@@ -379,7 +410,7 @@
                 total_ref[t] += product[i * TILE : (i + 1) * TILE]
             return carry
 
-        return lax.fori_loop(0, (table_ref[line, table.end] + 3) // 4, four_tiles, carry)
+        return lax.fori_loop(0, table.steps(table_ref, line, 4), four_tiles, carry)
 
     lax.fori_loop(0, columns // 2, one_pair, 0)
     for t in range(row_tiles):
@@ -400,27 +431,71 @@
     return pltpu.CompilerParams(vmem_limit_bytes=mebibytes * 2**20)
 
 
-def gather_features(shard):
+def sibling(block):
+    return swap(block, "proto", 1)
+
+
+def tied(*arrays):
+    return lax.optimization_barrier(arrays)
+
+
+def make_panel(table, lists, embeddings, shard, rows, features):
     width = shard.shape[1]
-
-    def sibling(block):
-        return swap(block, "proto", 1)
+    protos = 2 * shard.shape[0]
+    panel = pltpu.VMEM((table.dummy + 1, TILE, TILE), jnp.float32)
+    whole = pltpu.VMEM((protos, features), jnp.bfloat16)
+    row_shape = jax.ShapeDtypeStruct((table.row_tiles, TILE), jnp.float32)
+    peaks = pltpu.VMEM((table.row_tiles, TILE, TILE), jnp.float32)
+
+    def late(places, add, e, pieces, before):
+        at = 2 + len(pieces)
+        return pl.pallas_call(
+            functools.partial(panel_kernel, table, places, add),
+            out_shape=(panel, whole, row_shape),
+            in_specs=[SMEM] + [VMEM] * (1 + len(pieces) + len(before)),
+            out_specs=(VMEM, VMEM, VMEM),
+            scratch_shapes=[peaks],
+            input_output_aliases={at: 0, at + 1: 1} if add else {},
+            compiler_params=params(8),
+            name="panel",
+        )(lists, e, *pieces, *before)
 
     if lax.axis_size("row") != 4 or width % TILE:
-        whole = lax.all_gather(shard, "row", axis=1, tiled=True)
-        return [whole, sibling(whole)], [0], [None]
+        every = lax.all_gather(shard, "row", axis=1, tiled=True)
+        places = [Piece(True, 0, None), Piece(False, 0, None)]
+        return late(places, False, embeddings, [every, sibling(every)], [])
     half = shard.shape[0] // 2
     top, bottom = shard[:half], shard[half:]
     near_bottom = swap(bottom, "row", 1)
     far_top = swap(top, "row", 2)
-    near_bottom, far_top, top, bottom = lax.optimization_barrier((near_bottom, far_top, top, bottom))
+    near_bottom, far_top, top, bottom = tied(near_bottom, far_top, top, bottom)
     cross_top = swap(far_top, "row", 1)
     cross_bottom = swap(near_bottom, "row", 2)
     near_top = swap(top, "row", 1)
     far_bottom = swap(bottom, "row", 2)
-    pieces = [shard, near_top, near_bottom, far_top, far_bottom, cross_top, cross_bottom]
-    firsts = [0, 0, half, 0, half, 0, half]
-    return pieces + [sibling(piece) for piece in pieces], firsts, [0, 1, 1, 2, 2, 3, 3]
+    pieces = [shard, near_bottom, far_top]
+    pieces += [sibling(piece) for piece in pieces]
+    places = [Piece(own, *at) for own in (True, False) for at in ((0, 0), (half, 1), (0, 2))]
+    visits = table.dummy * TILE * TILE
+    similar, known, e = pl.pallas_call(
+        functools.partial(early_panel_kernel, table, places),
+        out_shape=(panel, whole, pltpu.VMEM(embeddings.shape, jnp.bfloat16)),
+        in_specs=[SMEM, pl.BlockSpec(memory_space=pl.ANY)] + [VMEM] * len(pieces),
+        out_specs=(VMEM, VMEM, VMEM),
+        scratch_shapes=[pltpu.SemaphoreType.DMA],
+        compiler_params=params(6),
+        cost_estimate=pl.CostEstimate(
+            flops=visits * features, bytes_accessed=8 * visits, transcendentals=0
+        ),
+        name="early_panel",
+    )(lists, embeddings, *pieces)
+    cross_top, cross_bottom, near_top, far_bottom, similar, known, e = tied(
+        cross_top, cross_bottom, near_top, far_bottom, similar, known, e
+    )
+    pieces = [near_top, far_bottom, cross_top, cross_bottom]
+    pieces += [sibling(piece) for piece in pieces]
+    places = [Piece(own, *at) for own in (True, False) for at in ((0, 1), (half, 2), (0, 3), (half, 3))]
+    return late(places, True, e, pieces, [similar, known])
 
 
 def scatter_partials(blocks):
@@ -445,14 +520,14 @@
     table = Table(row_tiles, columns)
 
     other_mask = swap(block_mask, "proto", 1)
-    pieces, firsts, owners = gather_features(prototypes)
-    lists = pl.pallas_call(
-        functools.partial(setup_kernel, table),
-        out_shape=jax.ShapeDtypeStruct(table.shape, jnp.int32),
-        in_specs=[SMEM] * 2,
-        out_specs=SMEM,
-        name="setup",
-    )(block_mask, other_mask)
+    mask, other_mask = jnp.where(block_mask == 1, 1, 0), jnp.where(other_mask == 1, 1, 0)
+    lists = table.build(
+        jnp.where(
+            lax.axis_index("proto") % 2 == 0,
+            jnp.concatenate([mask, other_mask], axis=1),
+            jnp.concatenate([other_mask, mask], axis=1),
+        )
+    )
 
     row_shape = jax.ShapeDtypeStruct((row_tiles, TILE), jnp.float32)
     column_shape = jax.ShapeDtypeStruct((columns, TILE), jnp.float32)
@@ -461,15 +536,7 @@
     wide = pltpu.VMEM((row_tiles, TILE, TILE), jnp.float32)
     tall = pltpu.VMEM((columns, TILE, TILE), jnp.float32)
     factors = pltpu.VMEM((columns + 8, TILE), jnp.float32)
-    similar, whole, row_part = pl.pallas_call(
-        functools.partial(panel_kernel, table, firsts, owners),
-        out_shape=(pltpu.VMEM(panel, jnp.float32), pltpu.VMEM((protos, features), jnp.bfloat16), row_shape),
-        in_specs=[SMEM] + [pl.BlockSpec(memory_space=pl.ANY)] * 2 + [VMEM] * (len(pieces) - 1),
-        out_specs=(VMEM, VMEM, VMEM),
-        scratch_shapes=[wide, pltpu.VMEM(embeddings.shape, jnp.bfloat16), pltpu.SemaphoreType.DMA((2,))],
-        compiler_params=params(12),
-        name="panel",
-    )(lists, embeddings, *pieces)
+    similar, whole, row_part = make_panel(table, lists, embeddings, prototypes, rows, features)
 
     def row_exchange(part):
         others = [swap(part, "proto", 2 * j) for j in range(lines - 1, 0, -1)]

time: 151 us -> 136 us (0.901)
  waiting for transfers between devices: 61.6 us -> 52.8 us
  Pallas kernels: 40.6 us -> 33.9 us
  other arithmetic: 1.14 us -> 3.46 us
    ppermute x35, waiting for transfers between devices: 61.6 us -> 52.8 us  [swap(): return lax.ppermute(x, axis, [(i, i ^ offset) for i in range(size)])]
    pallas_call x2, Pallas kernels: 17.9 us -> 13 us  [the longest x1 7.3 us: late(): pl.pallas_call(functools.partial(panel_kernel, table, places, add), out_s...]
    unnamed x11 -> x4, local copies, waits for them, and re-layouts: 4.74 us -> 3.23 us
  transfers between devices with their start and end apart: 35 -> 35, of which waited for: 25 -> 24; matrix products, arithmetic and copies ran while one was open for 1% -> 3% of each run, Pallas kernels for 6% -> 4%
where the time goes in v8:
time: 136 us; the launch traced here: 135 us
  waiting for transfers between devices  52.8 us (39%)
  starting transfers between devices  38.9 us (29%)
  Pallas kernels  33.9 us (25%)
  local copies, waits for them, and re-layouts  4.78 us (4%)
  other arithmetic  3.46 us (3%)
    ppermute x35, waiting for transfers between devices, swap(): return lax.ppermute(x, axis, [(i, i ^ offset) for i in range(size)])  52.8 us
    ppermute x35, starting transfers between devices, swap(): return lax.ppermute(x, axis, [(i, i ^ offset) for i in range(size)])  38.9 us
    pallas_call x1, Pallas kernels, late(): pl.pallas_call(functools.partial(panel_kernel, table, places, add), out_s...  7.3 us
    pallas_call x2, Pallas kernels, shards(): pl.pallas_call(functools.partial(column_kernel, table), out_shape=(column...  6.74 us
    pallas_call x1, Pallas kernels, shards(): pl.pallas_call(functools.partial(plan_kernel, table, log_column, lines),...  6.68 us
    pallas_call x1, Pallas kernels, make_panel(): pl.pallas_call(functools.partial(early_panel_kernel, table, places), out_...  5.68 us
    pallas_call x2, Pallas kernels, shards(): pl.pallas_call(functools.partial(row_kernel, table, log_column), out_shap...  5.03 us
    unnamed x4, local copies, waits for them, and re-layouts  3.23 us
  transfers between devices with their start and end apart: 35, of which 24 were waited for; matrix products, arithmetic and copies ran while one was open for 3% of the time, Pallas kernels for 4%

profile of v8, /device:TPU:0, one launch (start us, length us, event | category | flops | bytes accessed | tf_op | source)
XLA Modules:
  0.0 134.7 jit_solution(16114433033678103852)
XLA Ops:
  1.2 1.1 fusion.4
  2.3 3.0 %collective-permute-start.2 = (bf16[512,256]{1,0:T(8,128)(2,1)S(1)}, bf16[512,256]{1,0:T(8,128)(2,1)S(1)}, u32[]{:S(2)}, u32[]{:S(2)}) collective-permute-start(bf16[512,256]{1,0:T(8,128)(2,1)S(1)} %get-tuple-element.35), channel_id=1, source_target_pairs={{0,16},{8,24},{16,0},{24,8},{1,17},{9,25},{17,1},{25,9},{2,18},{10... | collective-permute-start | bytes 786440 | tf_op jit(solution)/shard_map/ppermute | solution.py:22
  5.3 1.5 %collective-permute-start.1 = (bf16[512,256]{1,0:T(8,128)(2,1)S(1)}, bf16[512,256]{1,0:T(8,128)(2,1)S(1)}, u32[]{:S(2)}, u32[]{:S(2)}) collective-permute-start(bf16[512,256]{1,0:T(8,128)(2,1)S(1)} %get-tuple-element.36), channel_id=1, source_target_pairs={{0,8},{8,0},{16,24},{24,16},{1,9},{9,1},{17,25},{25,17},{2,10},{10... | collective-permute-start | bytes 786440 | tf_op jit(solution)/shard_map/ppermute | solution.py:22
  6.8 0.7 compare_select_fusion.1
  8.9 2.9 %collective-permute-done.2.refs_2_ = bf16[512,256]{1,0:T(8,128)(2,1)S(1)} collective-permute-done((bf16[512,256]{1,0:T(8,128)(2,1)S(1)}, bf16[512,256]{1,0:T(8,128)(2,1)S(1)}, u32[]{:S(2)}, u32[]{:S(2)}) %collective-permute-start.2) | collective-permute-done | bytes 262176 | tf_op jit(solution)/shard_map/ppermute | solution.py:22
  11.9 1.5 %collective-permute-done.1.refs_1_ = bf16[512,256]{1,0:T(8,128)(2,1)S(1)} collective-permute-done((bf16[512,256]{1,0:T(8,128)(2,1)S(1)}, bf16[512,256]{1,0:T(8,128)(2,1)S(1)}, u32[]{:S(2)}, u32[]{:S(2)}) %collective-permute-start.1) | collective-permute-done | bytes 262176 | tf_op jit(solution)/shard_map/ppermute | solution.py:22
  14.6 1.5 %collective-permute-start.3 = (bf16[512,256]{1,0:T(8,128)(2,1)S(1)}, bf16[512,256]{1,0:T(8,128)(2,1)S(1)}, u32[]{:S(2)}, u32[]{:S(2)}) collective-permute-start(bf16[512,256]{1,0:T(8,128)(2,1)S(1)} %collective-permute-done.2.refs_2_), channel_id=1, source_target_pairs={{0,8},{8,0},{16,24},{24,16},{1,9},{9,1},{17,25},{25,17},{2,10},{10... | collective-permute-start | bytes 786440 | tf_op jit(solution)/shard_map/ppermute | solution.py:22
  17.0 1.7 %collective-permute-start.6 = (bf16[512,256]{1,0:T(8,128)(2,1)S(1)}, bf16[512,256]{1,0:T(8,128)(2,1)S(1)}, u32[]{:S(2)}, u32[]{:S(2)}) collective-permute-start(bf16[512,256]{1,0:T(8,128)(2,1)S(1)} %get-tuple-element.36), channel_id=1, source_target_pairs={{0,16},{8,24},{16,0},{24,8},{1,17},{9,25},{17,1},{25,9},{2,18},{10... | collective-permute-start | bytes 786440 | tf_op jit(solution)/shard_map/ppermute | solution.py:22
  18.6 1.0 copy-done
  19.7 2.2 %copy-done.1 = bf16[2048,1024]{1,0:T(8,128)(2,1)S(1)} copy-done((bf16[2048,1024]{1,0:T(8,128)(2,1)S(1)}, bf16[2048,1024]{1,0:T(8,128)(2,1)}, u32[]{:S(2)}) %copy-start.1) | copy-done | bytes 4194328
  21.9 5.7 %early_panel.1 = (f32[257,128,128]{2,1,0:T(8,128)S(1)}, bf16[2048,1024]{1,0:T(8,128)(2,1)S(1)}, bf16[2048,1024]{1,0:T(8,128)(2,1)S(1)}) custom-call(s32[1216]{0:T(1024)S(1)} %concatenate.25.table_ref, bf16[2048,1024]{1,0:T(8,128)(2,1)S(1)} %copy-done.1, bf16[1024,256]{1,0:T(8,128)(2,1)S(1)} %copy-done, bf16[512,256]{1,0:T(8,128)(2,1)S(1)} %collective-permute-done.1.refs_1_, ...), custom_call_target="tpu_custom_call" | custom-call | flops 4294967296 | bytes 33554432 | tf_op jit(solution)/shard_map/early_panel/pallas_call | solution.py:480
  27.5 0.9 collective-permute-done.5.refs_0_
  28.4 1.2 collective-permute-done.6.refs_1_
  32.3 7.3 %panel.1 = (f32[257,128,128]{2,1,0:T(8,128)S(1)}, bf16[2048,1024]{1,0:T(8,128)(2,1)S(1)}, f32[16,128]{1,0:T(8,128)S(1)}) custom-call(s32[1216]{0:T(1024)S(1)} %concatenate.25.table_ref, bf16[2048,1024]{1,0:T(8,128)(2,1)S(1)} %get-tuple-element.40.e_ref, ...), custom_call_target="tpu_custom_call", output_to_operand_aliasing={{0}: (10, {}), {1}: (11, {})} | custom-call | tf_op jit(solution)/shard_map/panel/pallas_call | solution.py:452
  39.6 2.6 %collective-permute-start.16 = (f32[16,128]{1,0:T(8,128)S(1)}, f32[16,128]{1,0:T(8,128)S(1)}, u32[]{:S(2)}, u32[]{:S(2)}) collective-permute-start(f32[16,128]{1,0:T(8,128)S(1)} %get-tuple-element.48.refs_0_), channel_id=1, source_target_pairs={{0,6},{1,7},{2,4},{3,5},{4,2},{5,3},{6,0},{7,1},{8,14},{9,15},{10,... | collective-permute-start | bytes 24584 | tf_op jit(solution)/shard_map/ppermute | solution.py:22
  42.3 1.7 %collective-permute-start.14 = (f32[16,128]{1,0:T(8,128)S(1)}, f32[16,128]{1,0:T(8,128)S(1)}, u32[]{:S(2)}, u32[]{:S(2)}) collective-permute-start(f32[16,128]{1,0:T(8,128)S(1)} %get-tuple-element.48.refs_0_), channel_id=1, source_target_pairs={{0,2},{1,3},{2,0},{3,1},{4,6},{5,7},{6,4},{7,5},{8,10},{9,11},{10,... | collective-permute-start | bytes 24584 | tf_op jit(solution)/shard_map/ppermute | solution.py:22
  44.0 1.1 collective-permute-done.16.refs_3_
  45.1 1.7 %collective-permute-done.15.refs_2_ = f32[16,128]{1,0:T(8,128)S(1)} collective-permute-done((f32[16,128]{1,0:T(8,128)S(1)}, f32[16,128]{1,0:T(8,128)S(1)}, u32[]{:S(2)}, u32[]{:S(2)}) %collective-permute-start.15) | collective-permute-done | bytes 8224 | tf_op jit(solution)/shard_map/ppermute | solution.py:22
  46.7 2.5 %first_column_pass.1 = (f32[16,128]{1,0:T(8,128)S(1)}, f32[16,128]{1,0:T(8,128)S(1)}, bf16[257,128,128]{2,1,0:T(8,128)(2,1)S(1)}, f32[16,128]{1,0:T(8,128)S(1)}) custom-call(s32[1216]{0:T(1024)S(1)} %concatenate.25.table_ref, f32[257,128,128]{2,1,0:T(8,128)S(1)} %get-tuple-element.47.s_ref, f32[16,128]{1,0:T(8,128)S(1)} %get-tuple-element.48.refs_0_, ...), custom_call_target="tpu_custom_call" | custom-call | tf_op jit(solution)/shard_map/first_column_pass/pallas_call | solution.py:550
  49.3 4.3 %collective-permute-start.19 = (f32[16,128]{1,0:T(8,128)S(1)}, f32[16,128]{1,0:T(8,128)S(1)}, u32[]{:S(2)}, u32[]{:S(2)}) collective-permute-start(f32[16,128]{1,0:T(8,128)S(1)} %get-tuple-element.52.refs_0_), channel_id=1, source_target_pairs={{0,24},{8,16},{16,8},{24,0},{1,25},{9,17},{17,9},{25,1},{2,26},{10... | collective-permute-start | bytes 24584 | tf_op jit(solution)/shard_map/ppermute | solution.py:22
  54.2 1.0 collective-permute-done.19.refs_3_
  55.2 2.0 %collective-permute-done.18.refs_2_ = f32[16,128]{1,0:T(8,128)S(1)} collective-permute-done((f32[16,128]{1,0:T(8,128)S(1)}, f32[16,128]{1,0:T(8,128)S(1)}, u32[]{:S(2)}, u32[]{:S(2)}) %collective-permute-start.18) | collective-permute-done | bytes 8224 | tf_op jit(solution)/shard_map/ppermute | solution.py:22
  57.3 2.5 %row_pass.2.refs_0_ = f32[16,128]{1,0:T(8,128)S(1)} custom-call(s32[1216]{0:T(1024)S(1)} %concatenate.25.table_ref, f32[257,128,128]{2,1,0:T(8,128)S(1)} %get-tuple-element.47.s_ref, bf16[257,128,128]{2,1,0:T(8,128)(2,1)S(1)} %get-tuple-element.49.w_ref, f32[16,128]{1,0:T(8,128)S(1)} %get-tuple-element.50.m_ref, ...), custom_call_target="tpu_custom_call" | custom-call | tf_op jit(solution)/shard_map/row_pass/pallas_call | solution.py:561
  59.8 2.9 %collective-permute-start.22 = (f32[16,128]{1,0:T(8,128)S(1)}, f32[16,128]{1,0:T(8,128)S(1)}, u32[]{:S(2)}, u32[]{:S(2)}) collective-permute-start(f32[16,128]{1,0:T(8,128)S(1)} %row_pass.2.refs_0_), channel_id=1, source_target_pairs={{0,6},{1,7},{2,4},{3,5},{4,2},{5,3},{6,0},{7,1},{8,14},{9,15},{10,... | collective-permute-start | bytes 24584 | tf_op jit(solution)/shard_map/ppermute | solution.py:22
  62.8 1.4 %collective-permute-start.20 = (f32[16,128]{1,0:T(8,128)S(1)}, f32[16,128]{1,0:T(8,128)S(1)}, u32[]{:S(2)}, u32[]{:S(2)}) collective-permute-start(f32[16,128]{1,0:T(8,128)S(1)} %row_pass.2.refs_0_), channel_id=1, source_target_pairs={{0,2},{1,3},{2,0},{3,1},{4,6},{5,7},{6,4},{7,5},{8,10},{9,11},{10,... | collective-permute-start | bytes 24584 | tf_op jit(solution)/shard_map/ppermute | solution.py:22
  64.2 1.1 collective-permute-done.22.refs_3_
  65.3 2.0 %collective-permute-done.21.refs_2_ = f32[16,128]{1,0:T(8,128)S(1)} collective-permute-done((f32[16,128]{1,0:T(8,128)S(1)}, f32[16,128]{1,0:T(8,128)S(1)}, u32[]{:S(2)}, u32[]{:S(2)}) %collective-permute-start.21) | collective-permute-done | bytes 8224 | tf_op jit(solution)/shard_map/ppermute | solution.py:22
  67.3 3.5 %column_pass.2 = (f32[16,128]{1,0:T(8,128)S(1)}, f32[16,128]{1,0:T(8,128)}, f32[16,128]{1,0:T(8,128)}) custom-call(s32[1216]{0:T(1024)S(1)} %concatenate.25.table_ref, f32[257,128,128]{2,1,0:T(8,128)S(1)} %get-tuple-element.47.s_ref, bf16[257,128,128]{2,1,0:T(8,128)(2,1)S(1)} %get-tuple-element.49.w_ref, f32[16,128]{1,0:T(8,128)S(1)} %get-tuple-element.50.m_ref, ...), custom_call_target="tpu_custom_call" | custom-call | tf_op jit(solution)/shard_map/column_pass/pallas_call | solution.py:571
  70.7 1.3 collective-permute-start.25
  72.7 1.6 %collective-permute-start.23 = (f32[16,128]{1,0:T(8,128)S(1)}, f32[16,128]{1,0:T(8,128)S(1)}, u32[]{:S(2)}, u32[]{:S(2)}) collective-permute-start(f32[16,128]{1,0:T(8,128)S(1)} %get-tuple-element.53.refs_0_), channel_id=1, source_target_pairs={{0,8},{8,0},{16,24},{24,16},{1,9},{9,1},{17,25},{25,17},{2,10},{10... | collective-permute-start | bytes 24584 | tf_op jit(solution)/shard_map/ppermute | solution.py:22
  74.2 1.1 collective-permute-done.25.refs_3_
  76.3 2.5 %row_pass.3.refs_0_ = f32[16,128]{1,0:T(8,128)S(1)} custom-call(s32[1216]{0:T(1024)S(1)} %concatenate.25.table_ref, f32[257,128,128]{2,1,0:T(8,128)S(1)} %get-tuple-element.47.s_ref, bf16[257,128,128]{2,1,0:T(8,128)(2,1)S(1)} %get-tuple-element.49.w_ref, f32[16,128]{1,0:T(8,128)S(1)} %get-tuple-element.50.m_ref, ...), custom_call_target="tpu_custom_call" | custom-call | tf_op jit(solution)/shard_map/row_pass/pallas_call | solution.py:561
  78.8 2.1 %collective-permute-start.28 = (f32[16,128]{1,0:T(8,128)S(1)}, f32[16,128]{1,0:T(8,128)S(1)}, u32[]{:S(2)}, u32[]{:S(2)}) collective-permute-start(f32[16,128]{1,0:T(8,128)S(1)} %row_pass.3.refs_0_), channel_id=1, source_target_pairs={{0,6},{1,7},{2,4},{3,5},{4,2},{5,3},{6,0},{7,1},{8,14},{9,15},{10,... | collective-permute-start | bytes 24584 | tf_op jit(solution)/shard_map/ppermute | solution.py:22
  81.5 1.8 %collective-permute-start.26 = (f32[16,128]{1,0:T(8,128)S(1)}, f32[16,128]{1,0:T(8,128)S(1)}, u32[]{:S(2)}, u32[]{:S(2)}) collective-permute-start(f32[16,128]{1,0:T(8,128)S(1)} %row_pass.3.refs_0_), channel_id=1, source_target_pairs={{0,2},{1,3},{2,0},{3,1},{4,6},{5,7},{6,4},{7,5},{8,10},{9,11},{10,... | collective-permute-start | bytes 24584 | tf_op jit(solution)/shard_map/ppermute | solution.py:22
  83.3 1.1 collective-permute-done.28.refs_3_
  84.4 1.1 collective-permute-done.27.refs_2_
  85.5 3.3 %column_pass.3 = (f32[16,128]{1,0:T(8,128)S(1)}, f32[16,128]{1,0:T(8,128)S(1)}, f32[16,128]{1,0:T(8,128)}) custom-call(s32[1216]{0:T(1024)S(1)} %concatenate.25.table_ref, f32[257,128,128]{2,1,0:T(8,128)S(1)} %get-tuple-element.47.s_ref, bf16[257,128,128]{2,1,0:T(8,128)(2,1)S(1)} %get-tuple-element.49.w_ref, f32[16,128]{1,0:T(8,128)S(1)} %get-tuple-element.50.m_ref, ...), custom_call_target="tpu_custom_call" | custom-call | tf_op jit(solution)/shard_map/column_pass/pallas_call | solution.py:571
  88.8 2.8 %collective-permute-start.31 = (f32[16,128]{1,0:T(8,128)S(1)}, f32[16,128]{1,0:T(8,128)S(1)}, u32[]{:S(2)}, u32[]{:S(2)}) collective-permute-start(f32[16,128]{1,0:T(8,128)S(1)} %get-tuple-element.56.refs_0_), channel_id=1, source_target_pairs={{0,24},{8,16},{16,8},{24,0},{1,25},{9,17},{17,9},{25,1},{2,26},{10... | collective-permute-start | bytes 24584 | tf_op jit(solution)/shard_map/ppermute | solution.py:22
  91.6 0.7 collective-permute-start.29
  92.3 1.1 collective-permute-done.31.refs_3_
  93.3 1.9 %collective-permute-done.30.refs_2_ = f32[16,128]{1,0:T(8,128)S(1)} collective-permute-done((f32[16,128]{1,0:T(8,128)S(1)}, f32[16,128]{1,0:T(8,128)S(1)}, u32[]{:S(2)}, u32[]{:S(2)}) %collective-permute-start.30) | collective-permute-done | bytes 8224 | tf_op jit(solution)/shard_map/ppermute | solution.py:22
  95.2 6.7 %plan.1 = (bf16[2048,128]{1,0:T(8,128)(2,1)S(1)}, bf16[2048,128]{1,0:T(8,128)(2,1)S(1)}, bf16[2048,128]{1,0:T(8,128)(2,1)S(1)}, bf16[2048,128]{1,0:T(8,128)(2,1)S(1)}, f32[8,128]{1,0:T(8,128)}) custom-call(s32[1216]{0:T(1024)S(1)} %concatenate.25.table_ref, f32[257,128,128]{2,1,0:T(8,128)S(1)} %get-tuple-element.47.s_ref, ...), custom_call_target="tpu_custom_call" | custom-call | tf_op jit(solution)/shard_map/plan/pallas_call | solution.py:581
  101.9 1.5 %collective-permute-start.33 = (bf16[2048,128]{1,0:T(8,128)(2,1)S(1)}, bf16[2048,128]{1,0:T(8,128)(2,1)S(1)}, u32[]{:S(2)}, u32[]{:S(2)}) collective-permute-start(bf16[2048,128]{1,0:T(8,128)(2,1)S(1)} %get-tuple-element.60), channel_id=1, source_target_pairs={{0,2},{1,3},{2,0},{3,1},{4,6},{5,7},{6,4},{7,5},{8,10},{9,11},{10,... | collective-permute-start | bytes 1572872 | tf_op jit(solution)/shard_map/ppermute | solution.py:22
  103.9 13.9 %collective-permute-done.33 = bf16[2048,128]{1,0:T(8,128)(2,1)S(1)} collective-permute-done((bf16[2048,128]{1,0:T(8,128)(2,1)S(1)}, bf16[2048,128]{1,0:T(8,128)(2,1)S(1)}, u32[]{:S(2)}, u32[]{:S(2)}) %collective-permute-start.33) | collective-permute-done | bytes 524320 | tf_op jit(solution)/shard_map/ppermute | solution.py:22
  117.9 1.0 collective-permute-start.34
  118.9 6.7 %collective-permute-done.32 = bf16[2048,128]{1,0:T(8,128)(2,1)S(1)} collective-permute-done((bf16[2048,128]{1,0:T(8,128)(2,1)S(1)}, bf16[2048,128]{1,0:T(8,128)(2,1)S(1)}, u32[]{:S(2)}, u32[]{:S(2)}) %collective-permute-start.32) | collective-permute-done | bytes 524320 | tf_op jit(solution)/shard_map/ppermute | solution.py:22
  125.5 8.2 %collective-permute-done.34 = bf16[2048,128]{1,0:T(8,128)(2,1)S(1)} collective-permute-done((bf16[2048,128]{1,0:T(8,128)(2,1)S(1)}, bf16[2048,128]{1,0:T(8,128)(2,1)S(1)}, u32[]{:S(2)}, u32[]{:S(2)}) %collective-permute-start.34) | collective-permute-done | bytes 524320 | tf_op jit(solution)/shard_map/ppermute | solution.py:22
  133.7 1.0 add_convert_fusion
  (61 shorter events, 10.5 us)
Async XLA Ops:
  0.6 6.9 %collective-permute-start = (s32[16,8]{0,1:T(8,128)}, s32[16,8]{0,1:T(8,128)S(1)}, u32[]{:S(2)}, u32[]{:S(2)}) collective-permute-start(s32[16,8]{0,1:T(8,128)} %param.5), channel_id=1, source_target_pairs={{0,1},{1,0},{2,3},{3,2},{4,5},{5,4},{6,7},{7,6},{8,9},{9,8},{10,11... | collective-permute-start | bytes 1544 | tf_op jit(solution)/shard_map/ppermute | solution.py:22
  1.1 17.5 %collective-permute-start.7 = (bf16[1024,256]{1,0:T(8,128)(2,1)}, bf16[1024,256]{1,0:T(8,128)(2,1)S(1)}, u32[]{:S(2)}, u32[]{:S(2)}) collective-permute-start(bf16[1024,256]{1,0:T(8,128)(2,1)} %refs_0_.1), channel_id=1, source_target_pairs={{0,1},{1,0},{2,3},{3,2},{4,5},{5,4},{6,7},{7,6},{8,9},{9,8},{10,11... | collective-permute-start | bytes 1572872 | tf_op jit(solution)/shard_map/ppermute | solution.py:22
  2.3 9.6 %collective-permute-start.2 = (bf16[512,256]{1,0:T(8,128)(2,1)S(1)}, bf16[512,256]{1,0:T(8,128)(2,1)S(1)}, u32[]{:S(2)}, u32[]{:S(2)}) collective-permute-start(bf16[512,256]{1,0:T(8,128)(2,1)S(1)} %get-tuple-element.35), channel_id=1, source_target_pairs={{0,16},{8,24},{16,0},{24,8},{1,17},{9,25},{17,1},{25,9},{2,18},{10... | collective-permute-start | bytes 786440 | tf_op jit(solution)/shard_map/ppermute | solution.py:22
  5.3 8.0 %collective-permute-start.1 = (bf16[512,256]{1,0:T(8,128)(2,1)S(1)}, bf16[512,256]{1,0:T(8,128)(2,1)S(1)}, u32[]{:S(2)}, u32[]{:S(2)}) collective-permute-start(bf16[512,256]{1,0:T(8,128)(2,1)S(1)} %get-tuple-element.36), channel_id=1, source_target_pairs={{0,8},{8,0},{16,24},{24,16},{1,9},{9,1},{17,25},{25,17},{2,10},{10... | collective-permute-start | bytes 786440 | tf_op jit(solution)/shard_map/ppermute | solution.py:22
  13.3 3.2 %collective-permute-start.9 = (bf16[512,256]{1,0:T(8,128)(2,1)S(1)}, bf16[512,256]{1,0:T(8,128)(2,1)S(1)}, u32[]{:S(2)}, u32[]{:S(2)}) collective-permute-start(bf16[512,256]{1,0:T(8,128)(2,1)S(1)} %collective-permute-done.2.refs_2_), channel_id=1, source_target_pairs={{0,1},{1,0},{2,3},{3,2},{4,5},{5,4},{6,7},{7,6},{8,9},{9,8},{10,11... | collective-permute-start | bytes 786440 | tf_op jit(solution)/shard_map/ppermute | solution.py:22
  13.3 3.6 %collective-permute-start.8 = (bf16[512,256]{1,0:T(8,128)(2,1)S(1)}, bf16[512,256]{1,0:T(8,128)(2,1)S(1)}, u32[]{:S(2)}, u32[]{:S(2)}) collective-permute-start(bf16[512,256]{1,0:T(8,128)(2,1)S(1)} %collective-permute-done.1.refs_1_), channel_id=1, source_target_pairs={{0,1},{1,0},{2,3},{3,2},{4,5},{5,4},{6,7},{7,6},{8,9},{9,8},{10,11... | collective-permute-start | bytes 786440 | tf_op jit(solution)/shard_map/ppermute | solution.py:22
  14.6 15.1 %collective-permute-start.3 = (bf16[512,256]{1,0:T(8,128)(2,1)S(1)}, bf16[512,256]{1,0:T(8,128)(2,1)S(1)}, u32[]{:S(2)}, u32[]{:S(2)}) collective-permute-start(bf16[512,256]{1,0:T(8,128)(2,1)S(1)} %collective-permute-done.2.refs_2_), channel_id=1, source_target_pairs={{0,8},{8,0},{16,24},{24,16},{1,9},{9,1},{17,25},{25,17},{2,10},{10... | collective-permute-start | bytes 786440 | tf_op jit(solution)/shard_map/ppermute | solution.py:22
  16.1 13.6 %collective-permute-start.4 = (bf16[512,256]{1,0:T(8,128)(2,1)S(1)}, bf16[512,256]{1,0:T(8,128)(2,1)S(1)}, u32[]{:S(2)}, u32[]{:S(2)}) collective-permute-start(bf16[512,256]{1,0:T(8,128)(2,1)S(1)} %collective-permute-done.1.refs_1_), channel_id=1, source_target_pairs={{0,16},{8,24},{16,0},{24,8},{1,17},{9,25},{17,1},{25,9},{2,18},{10... | collective-permute-start | bytes 786440 | tf_op jit(solution)/shard_map/ppermute | solution.py:22
  16.6 11.8 %collective-permute-start.5 = (bf16[512,256]{1,0:T(8,128)(2,1)S(1)}, bf16[512,256]{1,0:T(8,128)(2,1)S(1)}, u32[]{:S(2)}, u32[]{:S(2)}) collective-permute-start(bf16[512,256]{1,0:T(8,128)(2,1)S(1)} %get-tuple-element.35), channel_id=1, source_target_pairs={{0,8},{8,0},{16,24},{24,16},{1,9},{9,1},{17,25},{25,17},{2,10},{10... | collective-permute-start | bytes 786440 | tf_op jit(solution)/shard_map/ppermute | solution.py:22
  17.0 12.7 %collective-permute-start.6 = (bf16[512,256]{1,0:T(8,128)(2,1)S(1)}, bf16[512,256]{1,0:T(8,128)(2,1)S(1)}, u32[]{:S(2)}, u32[]{:S(2)}) collective-permute-start(bf16[512,256]{1,0:T(8,128)(2,1)S(1)} %get-tuple-element.36), channel_id=1, source_target_pairs={{0,16},{8,24},{16,0},{24,8},{1,17},{9,25},{17,1},{25,9},{2,18},{10... | collective-permute-start | bytes 786440 | tf_op jit(solution)/shard_map/ppermute | solution.py:22
  18.6 1.0 copy-start
  19.7 2.2 %copy-start.1 = (bf16[2048,1024]{1,0:T(8,128)(2,1)S(1)}, bf16[2048,1024]{1,0:T(8,128)(2,1)}, u32[]{:S(2)}) copy-start(bf16[2048,1024]{1,0:T(8,128)(2,1)} %e_hbm_ref.1) | copy-start | bytes 12582916
  29.6 1.5 %collective-permute-start.10 = (bf16[512,256]{1,0:T(8,128)(2,1)S(1)}, bf16[512,256]{1,0:T(8,128)(2,1)S(1)}, u32[]{:S(2)}, u32[]{:S(2)}) collective-permute-start(bf16[512,256]{1,0:T(8,128)(2,1)S(1)} %collective-permute-done.5.refs_0_), channel_id=1, source_target_pairs={{0,1},{1,0},{2,3},{3,2},{4,5},{5,4},{6,7},{7,6},{8,9},{9,8},{10,11... | collective-permute-start | bytes 786440 | tf_op jit(solution)/shard_map/ppermute | solution.py:22
  29.6 1.9 %collective-permute-start.11 = (bf16[512,256]{1,0:T(8,128)(2,1)S(1)}, bf16[512,256]{1,0:T(8,128)(2,1)S(1)}, u32[]{:S(2)}, u32[]{:S(2)}) collective-permute-start(bf16[512,256]{1,0:T(8,128)(2,1)S(1)} %collective-permute-done.6.refs_1_), channel_id=1, source_target_pairs={{0,1},{1,0},{2,3},{3,2},{4,5},{5,4},{6,7},{7,6},{8,9},{9,8},{10,11... | collective-permute-start | bytes 786440 | tf_op jit(solution)/shard_map/ppermute | solution.py:22
  30.1 1.8 %collective-permute-start.12 = (bf16[512,256]{1,0:T(8,128)(2,1)S(1)}, bf16[512,256]{1,0:T(8,128)(2,1)S(1)}, u32[]{:S(2)}, u32[]{:S(2)}) collective-permute-start(bf16[512,256]{1,0:T(8,128)(2,1)S(1)} %collective-permute-done.3.refs_2_), channel_id=1, source_target_pairs={{0,1},{1,0},{2,3},{3,2},{4,5},{5,4},{6,7},{7,6},{8,9},{9,8},{10,11... | collective-permute-start | bytes 786440 | tf_op jit(solution)/shard_map/ppermute | solution.py:22
  30.2 2.1 %collective-permute-start.13 = (bf16[512,256]{1,0:T(8,128)(2,1)S(1)}, bf16[512,256]{1,0:T(8,128)(2,1)S(1)}, u32[]{:S(2)}, u32[]{:S(2)}) collective-permute-start(bf16[512,256]{1,0:T(8,128)(2,1)S(1)} %collective-permute-done.4.refs_3_), channel_id=1, source_target_pairs={{0,1},{1,0},{2,3},{3,2},{4,5},{5,4},{6,7},{7,6},{8,9},{9,8},{10,11... | collective-permute-start | bytes 786440 | tf_op jit(solution)/shard_map/ppermute | solution.py:22
  39.6 5.5 %collective-permute-start.16 = (f32[16,128]{1,0:T(8,128)S(1)}, f32[16,128]{1,0:T(8,128)S(1)}, u32[]{:S(2)}, u32[]{:S(2)}) collective-permute-start(f32[16,128]{1,0:T(8,128)S(1)} %get-tuple-element.48.refs_0_), channel_id=1, source_target_pairs={{0,6},{1,7},{2,4},{3,5},{4,2},{5,3},{6,0},{7,1},{8,14},{9,15},{10,... | collective-permute-start | bytes 24584 | tf_op jit(solution)/shard_map/ppermute | solution.py:22
  42.2 4.5 %collective-permute-start.15 = (f32[16,128]{1,0:T(8,128)S(1)}, f32[16,128]{1,0:T(8,128)S(1)}, u32[]{:S(2)}, u32[]{:S(2)}) collective-permute-start(f32[16,128]{1,0:T(8,128)S(1)} %get-tuple-element.48.refs_0_), channel_id=1, source_target_pairs={{0,4},{1,5},{2,6},{3,7},{4,0},{5,1},{6,2},{7,3},{8,12},{9,13},{10,... | collective-permute-start | bytes 24584 | tf_op jit(solution)/shard_map/ppermute | solution.py:22
  42.3 4.4 %collective-permute-start.14 = (f32[16,128]{1,0:T(8,128)S(1)}, f32[16,128]{1,0:T(8,128)S(1)}, u32[]{:S(2)}, u32[]{:S(2)}) collective-permute-start(f32[16,128]{1,0:T(8,128)S(1)} %get-tuple-element.48.refs_0_), channel_id=1, source_target_pairs={{0,2},{1,3},{2,0},{3,1},{4,6},{5,7},{6,4},{7,5},{8,10},{9,11},{10,... | collective-permute-start | bytes 24584 | tf_op jit(solution)/shard_map/ppermute | solution.py:22
  49.3 6.0 %collective-permute-start.19 = (f32[16,128]{1,0:T(8,128)S(1)}, f32[16,128]{1,0:T(8,128)S(1)}, u32[]{:S(2)}, u32[]{:S(2)}) collective-permute-start(f32[16,128]{1,0:T(8,128)S(1)} %get-tuple-element.52.refs_0_), channel_id=1, source_target_pairs={{0,24},{8,16},{16,8},{24,0},{1,25},{9,17},{17,9},{25,1},{2,26},{10... | collective-permute-start | bytes 24584 | tf_op jit(solution)/shard_map/ppermute | solution.py:22
  53.6 3.7 %collective-permute-start.18 = (f32[16,128]{1,0:T(8,128)S(1)}, f32[16,128]{1,0:T(8,128)S(1)}, u32[]{:S(2)}, u32[]{:S(2)}) collective-permute-start(f32[16,128]{1,0:T(8,128)S(1)} %get-tuple-element.52.refs_0_), channel_id=1, source_target_pairs={{0,16},{8,24},{16,0},{24,8},{1,17},{9,25},{17,1},{25,9},{2,18},{10... | collective-permute-start | bytes 24584 | tf_op jit(solution)/shard_map/ppermute | solution.py:22
  53.6 3.7 %collective-permute-start.17 = (f32[16,128]{1,0:T(8,128)S(1)}, f32[16,128]{1,0:T(8,128)S(1)}, u32[]{:S(2)}, u32[]{:S(2)}) collective-permute-start(f32[16,128]{1,0:T(8,128)S(1)} %get-tuple-element.52.refs_0_), channel_id=1, source_target_pairs={{0,8},{8,0},{16,24},{24,16},{1,9},{9,1},{17,25},{25,17},{2,10},{10... | collective-permute-start | bytes 24584 | tf_op jit(solution)/shard_map/ppermute | solution.py:22
  59.8 5.5 %collective-permute-start.22 = (f32[16,128]{1,0:T(8,128)S(1)}, f32[16,128]{1,0:T(8,128)S(1)}, u32[]{:S(2)}, u32[]{:S(2)}) collective-permute-start(f32[16,128]{1,0:T(8,128)S(1)} %row_pass.2.refs_0_), channel_id=1, source_target_pairs={{0,6},{1,7},{2,4},{3,5},{4,2},{5,3},{6,0},{7,1},{8,14},{9,15},{10,... | collective-permute-start | bytes 24584 | tf_op jit(solution)/shard_map/ppermute | solution.py:22
  62.7 4.5 %collective-permute-start.21 = (f32[16,128]{1,0:T(8,128)S(1)}, f32[16,128]{1,0:T(8,128)S(1)}, u32[]{:S(2)}, u32[]{:S(2)}) collective-permute-start(f32[16,128]{1,0:T(8,128)S(1)} %row_pass.2.refs_0_), channel_id=1, source_target_pairs={{0,4},{1,5},{2,6},{3,7},{4,0},{5,1},{6,2},{7,3},{8,12},{9,13},{10,... | collective-permute-start | bytes 24584 | tf_op jit(solution)/shard_map/ppermute | solution.py:22
  62.8 4.5 %collective-permute-start.20 = (f32[16,128]{1,0:T(8,128)S(1)}, f32[16,128]{1,0:T(8,128)S(1)}, u32[]{:S(2)}, u32[]{:S(2)}) collective-permute-start(f32[16,128]{1,0:T(8,128)S(1)} %row_pass.2.refs_0_), channel_id=1, source_target_pairs={{0,2},{1,3},{2,0},{3,1},{4,6},{5,7},{6,4},{7,5},{8,10},{9,11},{10,... | collective-permute-start | bytes 24584 | tf_op jit(solution)/shard_map/ppermute | solution.py:22
  70.7 4.5 %collective-permute-start.25 = (f32[16,128]{1,0:T(8,128)S(1)}, f32[16,128]{1,0:T(8,128)S(1)}, u32[]{:S(2)}, u32[]{:S(2)}) collective-permute-start(f32[16,128]{1,0:T(8,128)S(1)} %get-tuple-element.53.refs_0_), channel_id=1, source_target_pairs={{0,24},{8,16},{16,8},{24,0},{1,25},{9,17},{17,9},{25,1},{2,26},{10... | collective-permute-start | bytes 24584 | tf_op jit(solution)/shard_map/ppermute | solution.py:22
  72.0 3.7 %collective-permute-start.24 = (f32[16,128]{1,0:T(8,128)S(1)}, f32[16,128]{1,0:T(8,128)S(1)}, u32[]{:S(2)}, u32[]{:S(2)}) collective-permute-start(f32[16,128]{1,0:T(8,128)S(1)} %get-tuple-element.53.refs_0_), channel_id=1, source_target_pairs={{0,16},{8,24},{16,0},{24,8},{1,17},{9,25},{17,1},{25,9},{2,18},{10... | collective-permute-start | bytes 24584 | tf_op jit(solution)/shard_map/ppermute | solution.py:22
  72.7 3.7 %collective-permute-start.23 = (f32[16,128]{1,0:T(8,128)S(1)}, f32[16,128]{1,0:T(8,128)S(1)}, u32[]{:S(2)}, u32[]{:S(2)}) collective-permute-start(f32[16,128]{1,0:T(8,128)S(1)} %get-tuple-element.53.refs_0_), channel_id=1, source_target_pairs={{0,8},{8,0},{16,24},{24,16},{1,9},{9,1},{17,25},{25,17},{2,10},{10... | collective-permute-start | bytes 24584 | tf_op jit(solution)/shard_map/ppermute | solution.py:22
  78.8 5.5 %collective-permute-start.28 = (f32[16,128]{1,0:T(8,128)S(1)}, f32[16,128]{1,0:T(8,128)S(1)}, u32[]{:S(2)}, u32[]{:S(2)}) collective-permute-start(f32[16,128]{1,0:T(8,128)S(1)} %row_pass.3.refs_0_), channel_id=1, source_target_pairs={{0,6},{1,7},{2,4},{3,5},{4,2},{5,3},{6,0},{7,1},{8,14},{9,15},{10,... | collective-permute-start | bytes 24584 | tf_op jit(solution)/shard_map/ppermute | solution.py:22
  80.9 4.5 %collective-permute-start.27 = (f32[16,128]{1,0:T(8,128)S(1)}, f32[16,128]{1,0:T(8,128)S(1)}, u32[]{:S(2)}, u32[]{:S(2)}) collective-permute-start(f32[16,128]{1,0:T(8,128)S(1)} %row_pass.3.refs_0_), channel_id=1, source_target_pairs={{0,4},{1,5},{2,6},{3,7},{4,0},{5,1},{6,2},{7,3},{8,12},{9,13},{10,... | collective-permute-start | bytes 24584 | tf_op jit(solution)/shard_map/ppermute | solution.py:22
  81.5 4.0 %collective-permute-start.26 = (f32[16,128]{1,0:T(8,128)S(1)}, f32[16,128]{1,0:T(8,128)S(1)}, u32[]{:S(2)}, u32[]{:S(2)}) collective-permute-start(f32[16,128]{1,0:T(8,128)S(1)} %row_pass.3.refs_0_), channel_id=1, source_target_pairs={{0,2},{1,3},{2,0},{3,1},{4,6},{5,7},{6,4},{7,5},{8,10},{9,11},{10,... | collective-permute-start | bytes 24584 | tf_op jit(solution)/shard_map/ppermute | solution.py:22
  88.8 4.5 %collective-permute-start.31 = (f32[16,128]{1,0:T(8,128)S(1)}, f32[16,128]{1,0:T(8,128)S(1)}, u32[]{:S(2)}, u32[]{:S(2)}) collective-permute-start(f32[16,128]{1,0:T(8,128)S(1)} %get-tuple-element.56.refs_0_), channel_id=1, source_target_pairs={{0,24},{8,16},{16,8},{24,0},{1,25},{9,17},{17,9},{25,1},{2,26},{10... | collective-permute-start | bytes 24584 | tf_op jit(solution)/shard_map/ppermute | solution.py:22
  91.6 3.7 %collective-permute-start.30 = (f32[16,128]{1,0:T(8,128)S(1)}, f32[16,128]{1,0:T(8,128)S(1)}, u32[]{:S(2)}, u32[]{:S(2)}) collective-permute-start(f32[16,128]{1,0:T(8,128)S(1)} %get-tuple-element.56.refs_0_), channel_id=1, source_target_pairs={{0,16},{8,24},{16,0},{24,8},{1,17},{9,25},{17,1},{25,9},{2,18},{10... | collective-permute-start | bytes 24584 | tf_op jit(solution)/shard_map/ppermute | solution.py:22
  91.6 3.7 %collective-permute-start.29 = (f32[16,128]{1,0:T(8,128)S(1)}, f32[16,128]{1,0:T(8,128)S(1)}, u32[]{:S(2)}, u32[]{:S(2)}) collective-permute-start(f32[16,128]{1,0:T(8,128)S(1)} %get-tuple-element.56.refs_0_), channel_id=1, source_target_pairs={{0,8},{8,0},{16,24},{24,16},{1,9},{9,1},{17,25},{25,17},{2,10},{10... | collective-permute-start | bytes 24584 | tf_op jit(solution)/shard_map/ppermute | solution.py:22
  101.9 15.9 %collective-permute-start.33 = (bf16[2048,128]{1,0:T(8,128)(2,1)S(1)}, bf16[2048,128]{1,0:T(8,128)(2,1)S(1)}, u32[]{:S(2)}, u32[]{:S(2)}) collective-permute-start(bf16[2048,128]{1,0:T(8,128)(2,1)S(1)} %get-tuple-element.60), channel_id=1, source_target_pairs={{0,2},{1,3},{2,0},{3,1},{4,6},{5,7},{6,4},{7,5},{8,10},{9,11},{10,... | collective-permute-start | bytes 1572872 | tf_op jit(solution)/shard_map/ppermute | solution.py:22
  103.4 22.2 %collective-permute-start.32 = (bf16[2048,128]{1,0:T(8,128)(2,1)S(1)}, bf16[2048,128]{1,0:T(8,128)(2,1)S(1)}, u32[]{:S(2)}, u32[]{:S(2)}) collective-permute-start(bf16[2048,128]{1,0:T(8,128)(2,1)S(1)} %get-tuple-element.58), channel_id=1, source_target_pairs={{0,2},{1,3},{2,0},{3,1},{4,6},{5,7},{6,4},{7,5},{8,10},{9,11},{10,... | collective-permute-start | bytes 1572872 | tf_op jit(solution)/shard_map/ppermute | solution.py:22
  117.9 15.8 %collective-permute-start.34 = (bf16[2048,128]{1,0:T(8,128)(2,1)S(1)}, bf16[2048,128]{1,0:T(8,128)(2,1)S(1)}, u32[]{:S(2)}, u32[]{:S(2)}) collective-permute-start(bf16[2048,128]{1,0:T(8,128)(2,1)S(1)} %add_convert_fusion.1), channel_id=1, source_target_pairs={{0,4},{1,5},{2,6},{3,7},{4,0},{5,1},{6,2},{7,3},{8,12},{9,13},{10,... | collective-permute-start | bytes 1572872 | tf_op jit(solution)/shard_map/ppermute | solution.py:22

commit v9 on v8

--- a/solution.py
+++ b/solution.py
@@ -40,13 +40,46 @@
         self.column_base = row_tiles
         self.pair_base = row_tiles + columns
         self.mask_at = (self.pair_base + columns // 2) * self.line
+        self.item_at = self.mask_at + row_tiles * columns
+        self.items = (columns // 2) * -(-row_tiles // 4)
+        self.total_at = self.item_at + 2 * (self.items + 1)
         self.dummy = row_tiles * columns
 
     def build(self, mask):
         across = mask.T
         pairs = jnp.max(across.reshape(self.columns // 2, 2, self.row_tiles), axis=1)
         lines = [self.lines(mask), self.lines(across), self.lines(pairs)]
-        return jnp.concatenate([part.reshape(-1) for part in lines] + [mask.reshape(-1)])
+        flat = [part.reshape(-1) for part in lines] + [mask.reshape(-1)]
+        steps = (jnp.sum(pairs, axis=1) + 3) // 4
+        at = jnp.arange(self.columns // 2, dtype=jnp.int32)
+        first = jnp.sum(jnp.where(at[None, :] < at[:, None], steps[None, :], 0), axis=1)
+        total = jnp.sum(steps)
+        item = jnp.minimum(jnp.arange(self.items + 1, dtype=jnp.int32), total - 1)
+        pair = jnp.sum(jnp.where(item[:, None] >= (first + steps)[None, :], 1, 0), axis=1)
+        step = item - jnp.sum(jnp.where(pair[:, None] == at[None, :], first[None, :], 0), axis=1)
+        flat += [(self.pair_base + pair) * self.line + 4 * step, pair]
+        return jnp.concatenate(flat + [jnp.stack([total, (total + 1) // 2])])
+
+    def each_item(self, ref, visit):
+        def two(k, carry):
+            for i in range(2):
+                number = 2 * k + i
+                at = ref[self.item_at + number]
+                visit(
+                    number,
+                    number < ref[self.total_at],
+                    ref[self.item_at + self.items + 1 + number],
+                    [ref[at + n] for n in range(4)],
+                )
+            return carry
+
+        lax.fori_loop(0, ref[self.total_at + 1], two, 0)
+
+    def empty_bits(self, ref, base, count):
+        bits = jnp.int32(0)
+        for i in range(count):
+            bits = bits + jnp.where(self.steps(ref, base + i, 4) == 0, 1 << i, 0)
+        return bits
 
     def lines(self, mask):
         size = mask.shape[1]
@@ -134,39 +167,32 @@
     row_tiles, columns = table.row_tiles, table.columns
     scale = 4.0 / math.sqrt(e_ref.shape[1])
 
-    def one_pair(pair, carry):
-        line = table.pair_base + pair
-        spans = features(pair)
-
-        def four_tiles(k, carry):
-            at = [jnp.minimum(table.entry(table_ref, line, 4 * k + i), row_tiles - 1) for i in range(4)]
-            product = None
-            for span in spans:
-                rows = jnp.concatenate(
-                    [e_ref[pl.ds(pl.multiple_of(t * TILE, TILE), TILE), span] for t in at], axis=0
-                )
-                block = p_ref[pl.ds(pl.multiple_of(pair * 2 * TILE, TILE), 2 * TILE), span]
-                part = lax.dot_general(
-                    rows, block, (((1,), (1,)), ((), ())), preferred_element_type=jnp.float32
-                )
-                product = part if product is None else product + part
-            product = scale * product
-            tiles = {}
+    def visit(number, real, pair, tiles):
+        at = [jnp.minimum(t, row_tiles - 1) for t in tiles]
+        product = None
+        for span in features(pair):
+            rows = jnp.concatenate(
+                [e_ref[pl.ds(pl.multiple_of(t * TILE, TILE), TILE), span] for t in at], axis=0
+            )
+            block = p_ref[pl.ds(pl.multiple_of(pair * 2 * TILE, TILE), 2 * TILE), span]
+            part = lax.dot_general(
+                rows, block, (((1,), (1,)), ((), ())), preferred_element_type=jnp.float32
+            )
+            product = part if product is None else product + part
+        product = (jnp.where(real, scale, 0.0) if add else scale) * product
+        found = {}
+        for i, t in enumerate(at):
+            for side in range(2):
+                where = t * columns + 2 * pair + side
+                tile = product[i * TILE : (i + 1) * TILE, side * TILE : (side + 1) * TILE]
+                found[i, side] = (where, s_ref[where] + tile if add else tile)
+        for where, tile in found.values():
+            s_ref[where] = tile
+        if done is not None:
             for i, t in enumerate(at):
-                for side in range(2):
-                    where = t * columns + 2 * pair + side
-                    tile = product[i * TILE : (i + 1) * TILE, side * TILE : (side + 1) * TILE]
-                    tiles[i, side] = (where, s_ref[where] + tile if add else tile)
-            for where, tile in tiles.values():
-                s_ref[where] = tile
-            if done is not None:
-                for i, t in enumerate(at):
-                    done(t, 2 * pair, tiles[i, 0][1], tiles[i, 1][1])
-            return carry
-
-        return lax.fori_loop(0, table.steps(table_ref, line, 4), four_tiles, carry)
-
-    lax.fori_loop(0, columns // 2, one_pair, 0)
+                done(t, 2 * pair, found[i, 0][1], found[i, 1][1])
+
+    table.each_item(table_ref, visit)
 
 
 def quarters(owners, p_ref, columns):
@@ -256,7 +282,7 @@
         acc_ref[t] = table.loop(table_ref, t, 4, one_tile, blank())
     totals = lying([acc_ref[t] for t in range(row_tiles)])
     out_ref[...] = jnp.log(totals) - r_ref[...]
-    bits = bad_bits(totals > 1e-15)
+    bits = bad_bits(totals > 1e-15) - table.empty_bits(table_ref, 0, row_tiles)
 
     @pl.when(bits != 0)
     def _():
@@ -318,7 +344,7 @@
     )
     m_ref[...] = jnp.zeros(m_ref.shape, jnp.float32)
     out_ref[...] = jnp.log(totals)
-    bits = bad_bits(totals > 1e-15)
+    bits = bad_bits(totals > 1e-15) - table.empty_bits(table_ref, table.column_base, table.columns)
 
     @pl.when(bits != 0)
     def _():
@@ -352,6 +378,7 @@
     out_ref[...] = m_ref[...] + jnp.log(totals)
     largest = jnp.max(jnp.max(factor, axis=1, keepdims=True), axis=0, keepdims=True)
     bits = bad_bits((totals > 1e-15) & (totals < 1e30) & (largest < 1e15))
+    bits = bits - table.empty_bits(table_ref, table.column_base, table.columns)
 
     @pl.when(bits != 0)
     def _():
@@ -364,67 +391,79 @@
                 out_ref[u : u + 1, :] = peak + jnp.log(total)
 
 
-def plan_kernel(table, log_column, lines, table_ref, s_ref, r_ref, p_ref, *refs):
-    parts, outs = refs[: -4 - lines], refs[-4 - lines : -4]
-    own_ref, c_ref, wide_ref, total_ref = refs[-4:]
-    row_tiles, columns = table.row_tiles, table.columns
+def plan_blocks(table, table_ref, p_ref, lines, wanted, width, strip, outs, total_ref):
+    row_tiles = table.row_tiles
     index = lax.axis_index("proto")
     core, z = lax.rem(index, 2), lax.div(index, 2)
-    c_ref[...] = log_column - combine([part[...] for part in parts])
-    half = columns // 2
-    own_ref[...] = c_ref[pl.ds(pl.multiple_of(core * half, half), half), :]
-    spread_rows(r_ref[...], wide_ref)
-    width = outs[0].shape[1]
     fits = width % TILE == 0
     total_ref[...] = jnp.zeros(total_ref.shape, jnp.float32)
 
-    def one_pair(pair, carry):
+    def visit(number, real, pair, tiles):
         first = pl.multiple_of(pair * 2 * TILE, TILE)
-        line = table.pair_base + pair
         blocks = []
-        for j in range(lines):
+        for j in wanted if fits else range(lines):
             if fits:
                 start = (2 * jnp.bitwise_xor(z, j) + core) * width
                 blocks.append(p_ref[pl.ds(first, 2 * TILE), pl.ds(pl.multiple_of(start, TILE), width)])
             else:
                 both = p_ref[pl.ds(first, 2 * TILE), 2 * j * width : 2 * (j + 1) * width]
                 blocks.append(jnp.where(core == 0, both[:, :width], both[:, width:]))
-        block = jnp.concatenate(blocks, axis=1)
-
-        def four_tiles(k, carry):
-            at = [table.entry(table_ref, line, 4 * k + i) for i in range(4)]
-            inside = [jnp.minimum(t, row_tiles - 1) for t in at]
-            strips = []
-            for t, real in zip(at, inside):
-                sides = []
-                for side in range(2):
-                    u = 2 * pair + side
-                    good = (t < row_tiles) & (table.allowed(table_ref, real, u) == 1)
-                    tile = s_ref[jnp.where(good, t * columns + u, table.dummy)]
-                    sides.append(jnp.exp(tile + wide_ref[real] + c_ref[pl.ds(u, 1), :]).astype(jnp.bfloat16))
-                strips.append(jnp.concatenate(sides, axis=1))
-            product = jnp.dot(
-                jnp.concatenate(strips, axis=0), block, preferred_element_type=jnp.float32
-            )
-            for i, t in enumerate(inside):
-                total_ref[t] += product[i * TILE : (i + 1) * TILE]
-            return carry
-
-        return lax.fori_loop(0, table.steps(table_ref, line, 4), four_tiles, carry)
-
-    lax.fori_loop(0, columns // 2, one_pair, 0)
+        product = jnp.dot(
+            strip(number, real, pair, tiles),
+            jnp.concatenate(blocks, axis=1),
+            preferred_element_type=jnp.float32,
+        )
+        for i, t in enumerate(tiles):
+            total_ref[jnp.minimum(t, row_tiles - 1)] += product[i * TILE : (i + 1) * TILE]
+
+    table.each_item(table_ref, visit)
     for t in range(row_tiles):
         total = total_ref[t].astype(jnp.bfloat16)
-        for j in range(lines):
-            block = total[:, j * width : (j + 1) * width]
+        rows = slice(t * TILE, (t + 1) * TILE)
+        for n, j in enumerate(wanted):
             if fits:
-                outs[j][t * TILE : (t + 1) * TILE, :] = block
-            else:
-                for k in range(lines):
-
-                    @pl.when(jnp.bitwise_xor(z, k) == j)
-                    def _():
-                        outs[k][t * TILE : (t + 1) * TILE, :] = block
+                outs[n][rows, :] = total[:, n * width : (n + 1) * width]
+                continue
+            for k in range(lines):
+
+                @pl.when(jnp.bitwise_xor(z, j) == k)
+                def _():
+                    outs[n][rows, :] = total[:, k * width : (k + 1) * width]
+
+
+def plan_kernel(table, log_column, lines, table_ref, s_ref, r_ref, p_ref, *refs):
+    parts, (out_ref, kept_ref, own_ref, c_ref, wide_ref, total_ref) = refs[:-6], refs[-6:]
+    row_tiles, columns = table.row_tiles, table.columns
+    core = lax.rem(lax.axis_index("proto"), 2)
+    c_ref[...] = log_column - combine([part[...] for part in parts])
+    half = columns // 2
+    own_ref[...] = c_ref[pl.ds(pl.multiple_of(core * half, half), half), :]
+    spread_rows(r_ref[...], wide_ref)
+
+    def strip(number, real, pair, tiles):
+        strips = []
+        for t in tiles:
+            inside = jnp.minimum(t, row_tiles - 1)
+            sides = []
+            for side in range(2):
+                u = 2 * pair + side
+                good = real & (t < row_tiles) & (table.allowed(table_ref, inside, u) == 1)
+                tile = s_ref[jnp.where(good, t * columns + u, table.dummy)]
+                sides.append(jnp.exp(tile + wide_ref[inside] + c_ref[pl.ds(u, 1), :]).astype(jnp.bfloat16))
+            strips.append(jnp.concatenate(sides, axis=1))
+        strips = jnp.concatenate(strips, axis=0)
+        kept_ref[number] = strips
+        return strips
+
+    width = out_ref.shape[1]
+    plan_blocks(table, table_ref, p_ref, lines, [lines - 1], width, strip, [out_ref], total_ref)
+
+
+def rest_kernel(table, lines, table_ref, kept_ref, p_ref, *refs):
+    outs, total_ref = refs[:-1], refs[-1]
+    width = outs[0].shape[1]
+    strip = lambda number, real, pair, tiles: kept_ref[number]
+    plan_blocks(table, table_ref, p_ref, lines, list(range(lines - 1)), width, strip, outs, total_ref)
 
 
 def params(mebibytes):
@@ -578,20 +617,39 @@
             name="column_pass",
         )(lists, similar, kept, peaks, first_row, *parts)
     parts = column_exchange(column_part)
-    *blocks, column_potential = pl.pallas_call(
+    block = jax.ShapeDtypeStruct((rows, width), jnp.bfloat16)
+
+    def sums(blocks):
+        taken = blocks if width % TILE == 0 else lines
+        return pltpu.VMEM((row_tiles, TILE, taken * width), jnp.float32)
+
+    last, plan, column_potential = pl.pallas_call(
         functools.partial(plan_kernel, table, log_column, lines),
-        out_shape=[jax.ShapeDtypeStruct((rows, width), jnp.bfloat16)] * lines
-        + [jax.ShapeDtypeStruct((half, TILE), jnp.float32)],
+        out_shape=[
+            block,
+            pltpu.VMEM((table.items + 1, 4 * TILE, 2 * TILE), jnp.bfloat16),
+            jax.ShapeDtypeStruct((half, TILE), jnp.float32),
+        ],
         in_specs=[SMEM] + [VMEM] * (3 + len(parts)),
-        out_specs=[VMEM] * (lines + 1),
-        scratch_shapes=[
-            pltpu.VMEM((columns, TILE), jnp.float32),
-            wide,
-            pltpu.VMEM((row_tiles, TILE, lines * width), jnp.float32),
-        ],
+        out_specs=[VMEM] * 3,
+        scratch_shapes=[pltpu.VMEM((columns, TILE), jnp.float32), wide, sums(1)],
         compiler_params=params(12),
         name="plan",
     )(lists, similar, row_potential, whole, *parts)
+    visits = table.dummy * TILE * TILE
+    blocks = pl.pallas_call(
+        functools.partial(rest_kernel, table, lines),
+        out_shape=[block] * (lines - 1),
+        in_specs=[SMEM] + [VMEM] * 2,
+        out_specs=[VMEM] * (lines - 1),
+        scratch_shapes=[sums(lines - 1)],
+        compiler_params=params(12),
+        cost_estimate=pl.CostEstimate(
+            flops=2 * visits * (lines - 1) * width, bytes_accessed=4 * visits, transcendentals=0
+        ),
+        name="rest_of_plan",
+    )(lists, plan, whole)
+    blocks = list(blocks) + [last]
     targets = scatter_partials(blocks)
     return (targets, row_out.reshape(rows), column_potential.reshape(protos // 2))
 

time: 136 us -> 131 us (0.963)
  waiting for transfers between devices: 52.8 us -> 48.3 us
  Pallas kernels: 33.9 us -> 30.9 us
    ppermute x35, waiting for transfers between devices: 52.8 us -> 48.3 us  [swap(): return lax.ppermute(x, axis, [(i, i ^ offset) for i in range(size)])]
    pallas_call x0 -> x1, Pallas kernels: none -> 3.81 us  [shards(): pl.pallas_call(functools.partial(rest_kernel, table, lines), out_shape=[b...]
    pallas_call x1, Pallas kernels: 6.68 us -> 3.93 us  [shards(): pl.pallas_call(functools.partial(plan_kernel, table, log_column, lines),...]
    pallas_call x2, Pallas kernels: 6.74 us -> 5.19 us  [shards(): pl.pallas_call(functools.partial(column_kernel, table), out_shape=(column...]
    pallas_call x1, Pallas kernels: 5.68 us -> 4.31 us  [make_panel(): pl.pallas_call(functools.partial(early_panel_kernel, table, places), out_...]
  transfers between devices with their start and end apart: 35 -> 35, of which waited for: 24 -> 25; matrix products, arithmetic and copies ran while one was open for 3% -> 4% of each run, Pallas kernels for 4% -> 6%
where the time goes in v9:
time: 131 us
  waiting for transfers between devices  48.3 us (37%)
  starting transfers between devices  39.6 us (30%)
  Pallas kernels  30.9 us (24%)
  local copies, waits for them, and re-layouts  5.43 us (4%)
  other arithmetic  4.4 us (3%)
  between operations  2.12 us (2%)
    ppermute x35, waiting for transfers between devices, swap(): return lax.ppermute(x, axis, [(i, i ^ offset) for i in range(size)])  48.3 us
    ppermute x35, starting transfers between devices, swap(): return lax.ppermute(x, axis, [(i, i ^ offset) for i in range(size)])  39.6 us
    pallas_call x1, Pallas kernels, late(): pl.pallas_call(functools.partial(panel_kernel, table, places, add), out_s...  6.26 us
    pallas_call x2, Pallas kernels, shards(): pl.pallas_call(functools.partial(column_kernel, table), out_shape=(column...  5.19 us
    pallas_call x2, Pallas kernels, shards(): pl.pallas_call(functools.partial(row_kernel, table, log_column), out_shap...  5.17 us
    pallas_call x1, Pallas kernels, make_panel(): pl.pallas_call(functools.partial(early_panel_kernel, table, places), out_...  4.31 us
    pallas_call x1, Pallas kernels, shards(): pl.pallas_call(functools.partial(plan_kernel, table, log_column, lines),...  3.93 us
    pallas_call x1, Pallas kernels, shards(): pl.pallas_call(functools.partial(rest_kernel, table, lines), out_shape=[b...  3.81 us
  transfers between devices with their start and end apart: 35, of which 25 were waited for; matrix products, arithmetic and copies ran while one was open for 4% of the time, Pallas kernels for 6%

profile of v9, /device:TPU:0, one launch (start us, length us, event | category | flops | bytes accessed | tf_op | source)
XLA Modules:
  0.0 130.8 jit_solution(8522321643290515030)
XLA Ops:
  1.2 1.1 fusion.5
  2.3 3.0 %collective-permute-start.2 = (bf16[512,256]{1,0:T(8,128)(2,1)S(1)}, bf16[512,256]{1,0:T(8,128)(2,1)S(1)}, u32[]{:S(2)}, u32[]{:S(2)}) collective-permute-start(bf16[512,256]{1,0:T(8,128)(2,1)S(1)} %get-tuple-element.36), channel_id=1, source_target_pairs={{0,16},{8,24},{16,0},{24,8},{1,17},{9,25},{17,1},{25,9},{2,18},{10... | collective-permute-start | bytes 786440 | tf_op jit(solution)/shard_map/ppermute | solution.py:22
  5.3 1.5 %collective-permute-start.1 = (bf16[512,256]{1,0:T(8,128)(2,1)S(1)}, bf16[512,256]{1,0:T(8,128)(2,1)S(1)}, u32[]{:S(2)}, u32[]{:S(2)}) collective-permute-start(bf16[512,256]{1,0:T(8,128)(2,1)S(1)} %get-tuple-element.37), channel_id=1, source_target_pairs={{0,8},{8,0},{16,24},{24,16},{1,9},{9,1},{17,25},{25,17},{2,10},{10... | collective-permute-start | bytes 786440 | tf_op jit(solution)/shard_map/ppermute | solution.py:22
  10.8 1.1 collective-permute-done.2.refs_2_
  11.9 1.5 %collective-permute-done.1.refs_1_ = bf16[512,256]{1,0:T(8,128)(2,1)S(1)} collective-permute-done((bf16[512,256]{1,0:T(8,128)(2,1)S(1)}, bf16[512,256]{1,0:T(8,128)(2,1)S(1)}, u32[]{:S(2)}, u32[]{:S(2)}) %collective-permute-start.1) | collective-permute-done | bytes 262176 | tf_op jit(solution)/shard_map/ppermute | solution.py:22
  14.9 0.7 concatenate.25.table_ref
  15.7 1.5 %collective-permute-start.3 = (bf16[512,256]{1,0:T(8,128)(2,1)S(1)}, bf16[512,256]{1,0:T(8,128)(2,1)S(1)}, u32[]{:S(2)}, u32[]{:S(2)}) collective-permute-start(bf16[512,256]{1,0:T(8,128)(2,1)S(1)} %collective-permute-done.2.refs_2_), channel_id=1, source_target_pairs={{0,8},{8,0},{16,24},{24,16},{1,9},{9,1},{17,25},{25,17},{2,10},{10... | collective-permute-start | bytes 786440 | tf_op jit(solution)/shard_map/ppermute | solution.py:22
  18.1 1.7 %collective-permute-start.6 = (bf16[512,256]{1,0:T(8,128)(2,1)S(1)}, bf16[512,256]{1,0:T(8,128)(2,1)S(1)}, u32[]{:S(2)}, u32[]{:S(2)}) collective-permute-start(bf16[512,256]{1,0:T(8,128)(2,1)S(1)} %get-tuple-element.37), channel_id=1, source_target_pairs={{0,16},{8,24},{16,0},{24,8},{1,17},{9,25},{17,1},{25,9},{2,18},{10... | collective-permute-start | bytes 786440 | tf_op jit(solution)/shard_map/ppermute | solution.py:22
  19.7 1.0 copy-done
  20.8 2.2 %copy-done.1 = bf16[2048,1024]{1,0:T(8,128)(2,1)S(1)} copy-done((bf16[2048,1024]{1,0:T(8,128)(2,1)S(1)}, bf16[2048,1024]{1,0:T(8,128)(2,1)}, u32[]{:S(2)}) %copy-start.1) | copy-done | bytes 4194328
  23.0 4.3 %early_panel.1 = (f32[257,128,128]{2,1,0:T(8,128)S(1)}, bf16[2048,1024]{1,0:T(8,128)(2,1)S(1)}, bf16[2048,1024]{1,0:T(8,128)(2,1)S(1)}) custom-call(s32[1284]{0:T(1024)S(1)} %concatenate.25.table_ref, bf16[2048,1024]{1,0:T(8,128)(2,1)S(1)} %copy-done.1, bf16[1024,256]{1,0:T(8,128)(2,1)S(1)} %copy-done, bf16[512,256]{1,0:T(8,128)(2,1)S(1)} %collective-permute-done.1.refs_1_, ...), custom_call_target="tpu_custom_call" | custom-call | flops 4294967296 | bytes 33554432 | tf_op jit(solution)/shard_map/early_panel/pallas_call | solution.py:519
  27.3 2.2 %collective-permute-done.5.refs_0_ = bf16[512,256]{1,0:T(8,128)(2,1)S(1)} collective-permute-done((bf16[512,256]{1,0:T(8,128)(2,1)S(1)}, bf16[512,256]{1,0:T(8,128)(2,1)S(1)}, u32[]{:S(2)}, u32[]{:S(2)}) %collective-permute-start.5) | collective-permute-done | bytes 262176 | tf_op jit(solution)/shard_map/ppermute | solution.py:22
  29.5 1.2 collective-permute-done.6.refs_1_
  33.4 6.3 %panel.1 = (f32[257,128,128]{2,1,0:T(8,128)S(1)}, bf16[2048,1024]{1,0:T(8,128)(2,1)S(1)}, f32[16,128]{1,0:T(8,128)S(1)}) custom-call(s32[1284]{0:T(1024)S(1)} %concatenate.25.table_ref, bf16[2048,1024]{1,0:T(8,128)(2,1)S(1)} %get-tuple-element.41.e_ref, ...), custom_call_target="tpu_custom_call", output_to_operand_aliasing={{0}: (10, {}), {1}: (11, {})} | custom-call | tf_op jit(solution)/shard_map/panel/pallas_call | solution.py:491
  39.6 3.7 %collective-permute-start.16 = (f32[16,128]{1,0:T(8,128)S(1)}, f32[16,128]{1,0:T(8,128)S(1)}, u32[]{:S(2)}, u32[]{:S(2)}) collective-permute-start(f32[16,128]{1,0:T(8,128)S(1)} %get-tuple-element.49.refs_0_), channel_id=1, source_target_pairs={{0,6},{1,7},{2,4},{3,5},{4,2},{5,3},{6,0},{7,1},{8,14},{9,15},{10,... | collective-permute-start | bytes 24584 | tf_op jit(solution)/shard_map/ppermute | solution.py:22
  43.3 0.7 collective-permute-start.14
  44.1 1.1 collective-permute-done.16.refs_3_
  45.1 2.8 %collective-permute-done.15.refs_2_ = f32[16,128]{1,0:T(8,128)S(1)} collective-permute-done((f32[16,128]{1,0:T(8,128)S(1)}, f32[16,128]{1,0:T(8,128)S(1)}, u32[]{:S(2)}, u32[]{:S(2)}) %collective-permute-start.15) | collective-permute-done | bytes 8224 | tf_op jit(solution)/shard_map/ppermute | solution.py:22
  47.9 2.2 %first_column_pass.1 = (f32[16,128]{1,0:T(8,128)S(1)}, f32[16,128]{1,0:T(8,128)S(1)}, bf16[257,128,128]{2,1,0:T(8,128)(2,1)S(1)}, f32[16,128]{1,0:T(8,128)S(1)}) custom-call(s32[1284]{0:T(1024)S(1)} %concatenate.25.table_ref, f32[257,128,128]{2,1,0:T(8,128)S(1)} %get-tuple-element.48.s_ref, f32[16,128]{1,0:T(8,128)S(1)} %get-tuple-element.49.refs_0_, ...), custom_call_target="tpu_custom_call" | custom-call | tf_op jit(solution)/shard_map/first_column_pass/pallas_call | solution.py:589
  50.1 2.6 %collective-permute-start.19 = (f32[16,128]{1,0:T(8,128)S(1)}, f32[16,128]{1,0:T(8,128)S(1)}, u32[]{:S(2)}, u32[]{:S(2)}) collective-permute-start(f32[16,128]{1,0:T(8,128)S(1)} %get-tuple-element.53.refs_0_), channel_id=1, source_target_pairs={{0,24},{8,16},{16,8},{24,0},{1,25},{9,17},{17,9},{25,1},{2,26},{10... | collective-permute-start | bytes 24584 | tf_op jit(solution)/shard_map/ppermute | solution.py:22
  53.3 1.4 %collective-permute-start.17 = (f32[16,128]{1,0:T(8,128)S(1)}, f32[16,128]{1,0:T(8,128)S(1)}, u32[]{:S(2)}, u32[]{:S(2)}) collective-permute-start(f32[16,128]{1,0:T(8,128)S(1)} %get-tuple-element.53.refs_0_), channel_id=1, source_target_pairs={{0,8},{8,0},{16,24},{24,16},{1,9},{9,1},{17,25},{25,17},{2,10},{10... | collective-permute-start | bytes 24584 | tf_op jit(solution)/shard_map/ppermute | solution.py:22
  54.7 1.6 %collective-permute-done.18.refs_2_ = f32[16,128]{1,0:T(8,128)S(1)} collective-permute-done((f32[16,128]{1,0:T(8,128)S(1)}, f32[16,128]{1,0:T(8,128)S(1)}, u32[]{:S(2)}, u32[]{:S(2)}) %collective-permute-start.18) | collective-permute-done | bytes 8224 | tf_op jit(solution)/shard_map/ppermute | solution.py:22
  57.0 2.7 %row_pass.2.refs_0_ = f32[16,128]{1,0:T(8,128)S(1)} custom-call(s32[1284]{0:T(1024)S(1)} %concatenate.25.table_ref, f32[257,128,128]{2,1,0:T(8,128)S(1)} %get-tuple-element.48.s_ref, bf16[257,128,128]{2,1,0:T(8,128)(2,1)S(1)} %get-tuple-element.50.w_ref, f32[16,128]{1,0:T(8,128)S(1)} %get-tuple-element.51.m_ref, ...), custom_call_target="tpu_custom_call" | custom-call | tf_op jit(solution)/shard_map/row_pass/pallas_call | solution.py:600
  59.7 1.5 %collective-permute-start.22 = (f32[16,128]{1,0:T(8,128)S(1)}, f32[16,128]{1,0:T(8,128)S(1)}, u32[]{:S(2)}, u32[]{:S(2)}) collective-permute-start(f32[16,128]{1,0:T(8,128)S(1)} %row_pass.2.refs_0_), channel_id=1, source_target_pairs={{0,6},{1,7},{2,4},{3,5},{4,2},{5,3},{6,0},{7,1},{8,14},{9,15},{10,... | collective-permute-start | bytes 24584 | tf_op jit(solution)/shard_map/ppermute | solution.py:22
  61.5 2.6 %collective-permute-start.20 = (f32[16,128]{1,0:T(8,128)S(1)}, f32[16,128]{1,0:T(8,128)S(1)}, u32[]{:S(2)}, u32[]{:S(2)}) collective-permute-start(f32[16,128]{1,0:T(8,128)S(1)} %row_pass.2.refs_0_), channel_id=1, source_target_pairs={{0,2},{1,3},{2,0},{3,1},{4,6},{5,7},{6,4},{7,5},{8,10},{9,11},{10,... | collective-permute-start | bytes 24584 | tf_op jit(solution)/shard_map/ppermute | solution.py:22
  64.1 1.1 collective-permute-done.22.refs_3_
  65.8 2.6 %column_pass.2 = (f32[16,128]{1,0:T(8,128)S(1)}, f32[16,128]{1,0:T(8,128)}, f32[16,128]{1,0:T(8,128)}) custom-call(s32[1284]{0:T(1024)S(1)} %concatenate.25.table_ref, f32[257,128,128]{2,1,0:T(8,128)S(1)} %get-tuple-element.48.s_ref, bf16[257,128,128]{2,1,0:T(8,128)(2,1)S(1)} %get-tuple-element.50.w_ref, f32[16,128]{1,0:T(8,128)S(1)} %get-tuple-element.51.m_ref, ...), custom_call_target="tpu_custom_call" | custom-call | tf_op jit(solution)/shard_map/column_pass/pallas_call | solution.py:610
  68.4 3.7 %collective-permute-start.25 = (f32[16,128]{1,0:T(8,128)S(1)}, f32[16,128]{1,0:T(8,128)S(1)}, u32[]{:S(2)}, u32[]{:S(2)}) collective-permute-start(f32[16,128]{1,0:T(8,128)S(1)} %get-tuple-element.54.refs_0_), channel_id=1, source_target_pairs={{0,24},{8,16},{16,8},{24,0},{1,25},{9,17},{17,9},{25,1},{2,26},{10... | collective-permute-start | bytes 24584 | tf_op jit(solution)/shard_map/ppermute | solution.py:22
  72.7 1.1 collective-permute-done.25.refs_3_
  73.7 2.0 %collective-permute-done.24.refs_2_ = f32[16,128]{1,0:T(8,128)S(1)} collective-permute-done((f32[16,128]{1,0:T(8,128)S(1)}, f32[16,128]{1,0:T(8,128)S(1)}, u32[]{:S(2)}, u32[]{:S(2)}) %collective-permute-start.24) | collective-permute-done | bytes 8224 | tf_op jit(solution)/shard_map/ppermute | solution.py:22
  75.7 2.5 %row_pass.3.refs_0_ = f32[16,128]{1,0:T(8,128)S(1)} custom-call(s32[1284]{0:T(1024)S(1)} %concatenate.25.table_ref, f32[257,128,128]{2,1,0:T(8,128)S(1)} %get-tuple-element.48.s_ref, bf16[257,128,128]{2,1,0:T(8,128)(2,1)S(1)} %get-tuple-element.50.w_ref, f32[16,128]{1,0:T(8,128)S(1)} %get-tuple-element.51.m_ref, ...), custom_call_target="tpu_custom_call" | custom-call | tf_op jit(solution)/shard_map/row_pass/pallas_call | solution.py:600
  78.3 1.9 %collective-permute-start.28 = (f32[16,128]{1,0:T(8,128)S(1)}, f32[16,128]{1,0:T(8,128)S(1)}, u32[]{:S(2)}, u32[]{:S(2)}) collective-permute-start(f32[16,128]{1,0:T(8,128)S(1)} %row_pass.3.refs_0_), channel_id=1, source_target_pairs={{0,6},{1,7},{2,4},{3,5},{4,2},{5,3},{6,0},{7,1},{8,14},{9,15},{10,... | collective-permute-start | bytes 24584 | tf_op jit(solution)/shard_map/ppermute | solution.py:22
  80.7 2.0 %collective-permute-start.26 = (f32[16,128]{1,0:T(8,128)S(1)}, f32[16,128]{1,0:T(8,128)S(1)}, u32[]{:S(2)}, u32[]{:S(2)}) collective-permute-start(f32[16,128]{1,0:T(8,128)S(1)} %row_pass.3.refs_0_), channel_id=1, source_target_pairs={{0,2},{1,3},{2,0},{3,1},{4,6},{5,7},{6,4},{7,5},{8,10},{9,11},{10,... | collective-permute-start | bytes 24584 | tf_op jit(solution)/shard_map/ppermute | solution.py:22
  82.7 1.1 collective-permute-done.28.refs_3_
  83.8 0.9 collective-permute-done.27.refs_2_
  84.7 2.6 %column_pass.3 = (f32[16,128]{1,0:T(8,128)S(1)}, f32[16,128]{1,0:T(8,128)S(1)}, f32[16,128]{1,0:T(8,128)}) custom-call(s32[1284]{0:T(1024)S(1)} %concatenate.25.table_ref, f32[257,128,128]{2,1,0:T(8,128)S(1)} %get-tuple-element.48.s_ref, bf16[257,128,128]{2,1,0:T(8,128)(2,1)S(1)} %get-tuple-element.50.w_ref, f32[16,128]{1,0:T(8,128)S(1)} %get-tuple-element.51.m_ref, ...), custom_call_target="tpu_custom_call" | custom-call | tf_op jit(solution)/shard_map/column_pass/pallas_call | solution.py:610
  87.3 2.7 %collective-permute-start.31 = (f32[16,128]{1,0:T(8,128)S(1)}, f32[16,128]{1,0:T(8,128)S(1)}, u32[]{:S(2)}, u32[]{:S(2)}) collective-permute-start(f32[16,128]{1,0:T(8,128)S(1)} %get-tuple-element.57.refs_0_), channel_id=1, source_target_pairs={{0,24},{8,16},{16,8},{24,0},{1,25},{9,17},{17,9},{25,1},{2,26},{10... | collective-permute-start | bytes 24584 | tf_op jit(solution)/shard_map/ppermute | solution.py:22
  90.1 1.5 %collective-permute-start.29 = (f32[16,128]{1,0:T(8,128)S(1)}, f32[16,128]{1,0:T(8,128)S(1)}, u32[]{:S(2)}, u32[]{:S(2)}) collective-permute-start(f32[16,128]{1,0:T(8,128)S(1)} %get-tuple-element.57.refs_0_), channel_id=1, source_target_pairs={{0,8},{8,0},{16,24},{24,16},{1,9},{9,1},{17,25},{25,17},{2,10},{10... | collective-permute-start | bytes 24584 | tf_op jit(solution)/shard_map/ppermute | solution.py:22
  91.8 1.8 %collective-permute-done.30.refs_2_ = f32[16,128]{1,0:T(8,128)S(1)} collective-permute-done((f32[16,128]{1,0:T(8,128)S(1)}, f32[16,128]{1,0:T(8,128)S(1)}, u32[]{:S(2)}, u32[]{:S(2)}) %collective-permute-start.30) | collective-permute-done | bytes 8224 | tf_op jit(solution)/shard_map/ppermute | solution.py:22
  93.8 3.9 %plan.1 = (bf16[2048,128]{1,0:T(8,128)(2,1)S(1)}, bf16[33,512,256]{2,1,0:T(8,128)(2,1)S(1)}, f32[8,128]{1,0:T(8,128)}) custom-call(s32[1284]{0:T(1024)S(1)} %concatenate.25.table_ref, f32[257,128,128]{2,1,0:T(8,128)S(1)} %get-tuple-element.48.s_ref, f32[16,128]{1,0:T(8,128)S(1)} %get-tuple-element.55.r_ref, bf16[2048,1024]{1,0:T(8,128)(2,1)S(1)} %get-tuple-element.56.p_ref, ...), custom_call_target="tpu_custom_call" | custom-call | tf_op jit(solution)/shard_map/plan/pallas_call | solution.py:626
  97.7 0.7 collective-permute-start.33
  98.4 3.8 %rest_of_plan.1 = (bf16[2048,128]{1,0:T(8,128)(2,1)S(1)}, bf16[2048,128]{1,0:T(8,128)(2,1)S(1)}, bf16[2048,128]{1,0:T(8,128)(2,1)S(1)}) custom-call(s32[1284]{0:T(1024)S(1)} %concatenate.25.table_ref, bf16[33,512,256]{2,1,0:T(8,128)(2,1)S(1)} %get-tuple-element.58.kept_ref, bf16[2048,1024]{1,0:T(8,128)(2,1)S(1)} %get-tuple-element.56.p_ref), custom_call_target="tpu_custom_call" | custom-call | flops 3221225472 | bytes 16777216 | tf_op jit(solution)/shard_map/rest_of_plan/pallas_call | solution.py:640
  102.2 0.9 collective-permute-start.32
  103.2 10.7 %collective-permute-done.33 = bf16[2048,128]{1,0:T(8,128)(2,1)S(1)} collective-permute-done((bf16[2048,128]{1,0:T(8,128)(2,1)S(1)}, bf16[2048,128]{1,0:T(8,128)(2,1)S(1)}, u32[]{:S(2)}, u32[]{:S(2)}) %collective-permute-start.33) | collective-permute-done | bytes 524320 | tf_op jit(solution)/shard_map/ppermute | solution.py:22
  114.0 0.8 collective-permute-start.34
  114.8 7.1 %collective-permute-done.32 = bf16[2048,128]{1,0:T(8,128)(2,1)S(1)} collective-permute-done((bf16[2048,128]{1,0:T(8,128)(2,1)S(1)}, bf16[2048,128]{1,0:T(8,128)(2,1)S(1)}, u32[]{:S(2)}, u32[]{:S(2)}) %collective-permute-start.32) | collective-permute-done | bytes 524320 | tf_op jit(solution)/shard_map/ppermute | solution.py:22
  121.8 7.9 %collective-permute-done.34 = bf16[2048,128]{1,0:T(8,128)(2,1)S(1)} collective-permute-done((bf16[2048,128]{1,0:T(8,128)(2,1)S(1)}, bf16[2048,128]{1,0:T(8,128)(2,1)S(1)}, u32[]{:S(2)}, u32[]{:S(2)}) %collective-permute-start.34) | collective-permute-done | bytes 524320 | tf_op jit(solution)/shard_map/ppermute | solution.py:22
  129.8 1.0 add_convert_fusion
  (68 shorter events, 12.4 us)
Async XLA Ops:
  0.6 6.9 %collective-permute-start = (s32[16,8]{0,1:T(8,128)}, s32[16,8]{0,1:T(8,128)S(1)}, u32[]{:S(2)}, u32[]{:S(2)}) collective-permute-start(s32[16,8]{0,1:T(8,128)} %param.5), channel_id=1, source_target_pairs={{0,1},{1,0},{2,3},{3,2},{4,5},{5,4},{6,7},{7,6},{8,9},{9,8},{10,11... | collective-permute-start | bytes 1544 | tf_op jit(solution)/shard_map/ppermute | solution.py:22
  1.1 18.6 %collective-permute-start.7 = (bf16[1024,256]{1,0:T(8,128)(2,1)}, bf16[1024,256]{1,0:T(8,128)(2,1)S(1)}, u32[]{:S(2)}, u32[]{:S(2)}) collective-permute-start(bf16[1024,256]{1,0:T(8,128)(2,1)} %refs_0_.1), channel_id=1, source_target_pairs={{0,1},{1,0},{2,3},{3,2},{4,5},{5,4},{6,7},{7,6},{8,9},{9,8},{10,11... | collective-permute-start | bytes 1572872 | tf_op jit(solution)/shard_map/ppermute | solution.py:22
  2.3 9.6 %collective-permute-start.2 = (bf16[512,256]{1,0:T(8,128)(2,1)S(1)}, bf16[512,256]{1,0:T(8,128)(2,1)S(1)}, u32[]{:S(2)}, u32[]{:S(2)}) collective-permute-start(bf16[512,256]{1,0:T(8,128)(2,1)S(1)} %get-tuple-element.36), channel_id=1, source_target_pairs={{0,16},{8,24},{16,0},{24,8},{1,17},{9,25},{17,1},{25,9},{2,18},{10... | collective-permute-start | bytes 786440 | tf_op jit(solution)/shard_map/ppermute | solution.py:22
  5.3 8.0 %collective-permute-start.1 = (bf16[512,256]{1,0:T(8,128)(2,1)S(1)}, bf16[512,256]{1,0:T(8,128)(2,1)S(1)}, u32[]{:S(2)}, u32[]{:S(2)}) collective-permute-start(bf16[512,256]{1,0:T(8,128)(2,1)S(1)} %get-tuple-element.37), channel_id=1, source_target_pairs={{0,8},{8,0},{16,24},{24,16},{1,9},{9,1},{17,25},{25,17},{2,10},{10... | collective-permute-start | bytes 786440 | tf_op jit(solution)/shard_map/ppermute | solution.py:22
  13.3 4.4 %collective-permute-start.9 = (bf16[512,256]{1,0:T(8,128)(2,1)S(1)}, bf16[512,256]{1,0:T(8,128)(2,1)S(1)}, u32[]{:S(2)}, u32[]{:S(2)}) collective-permute-start(bf16[512,256]{1,0:T(8,128)(2,1)S(1)} %collective-permute-done.2.refs_2_), channel_id=1, source_target_pairs={{0,1},{1,0},{2,3},{3,2},{4,5},{5,4},{6,7},{7,6},{8,9},{9,8},{10,11... | collective-permute-start | bytes 786440 | tf_op jit(solution)/shard_map/ppermute | solution.py:22
  13.3 4.7 %collective-permute-start.8 = (bf16[512,256]{1,0:T(8,128)(2,1)S(1)}, bf16[512,256]{1,0:T(8,128)(2,1)S(1)}, u32[]{:S(2)}, u32[]{:S(2)}) collective-permute-start(bf16[512,256]{1,0:T(8,128)(2,1)S(1)} %collective-permute-done.1.refs_1_), channel_id=1, source_target_pairs={{0,1},{1,0},{2,3},{3,2},{4,5},{5,4},{6,7},{7,6},{8,9},{9,8},{10,11... | collective-permute-start | bytes 786440 | tf_op jit(solution)/shard_map/ppermute | solution.py:22
  15.7 15.1 %collective-permute-start.3 = (bf16[512,256]{1,0:T(8,128)(2,1)S(1)}, bf16[512,256]{1,0:T(8,128)(2,1)S(1)}, u32[]{:S(2)}, u32[]{:S(2)}) collective-permute-start(bf16[512,256]{1,0:T(8,128)(2,1)S(1)} %collective-permute-done.2.refs_2_), channel_id=1, source_target_pairs={{0,8},{8,0},{16,24},{24,16},{1,9},{9,1},{17,25},{25,17},{2,10},{10... | collective-permute-start | bytes 786440 | tf_op jit(solution)/shard_map/ppermute | solution.py:22
  17.2 13.6 %collective-permute-start.4 = (bf16[512,256]{1,0:T(8,128)(2,1)S(1)}, bf16[512,256]{1,0:T(8,128)(2,1)S(1)}, u32[]{:S(2)}, u32[]{:S(2)}) collective-permute-start(bf16[512,256]{1,0:T(8,128)(2,1)S(1)} %collective-permute-done.1.refs_1_), channel_id=1, source_target_pairs={{0,16},{8,24},{16,0},{24,8},{1,17},{9,25},{17,1},{25,9},{2,18},{10... | collective-permute-start | bytes 786440 | tf_op jit(solution)/shard_map/ppermute | solution.py:22
  17.7 11.8 %collective-permute-start.5 = (bf16[512,256]{1,0:T(8,128)(2,1)S(1)}, bf16[512,256]{1,0:T(8,128)(2,1)S(1)}, u32[]{:S(2)}, u32[]{:S(2)}) collective-permute-start(bf16[512,256]{1,0:T(8,128)(2,1)S(1)} %get-tuple-element.36), channel_id=1, source_target_pairs={{0,8},{8,0},{16,24},{24,16},{1,9},{9,1},{17,25},{25,17},{2,10},{10... | collective-permute-start | bytes 786440 | tf_op jit(solution)/shard_map/ppermute | solution.py:22
  18.1 12.7 %collective-permute-start.6 = (bf16[512,256]{1,0:T(8,128)(2,1)S(1)}, bf16[512,256]{1,0:T(8,128)(2,1)S(1)}, u32[]{:S(2)}, u32[]{:S(2)}) collective-permute-start(bf16[512,256]{1,0:T(8,128)(2,1)S(1)} %get-tuple-element.37), channel_id=1, source_target_pairs={{0,16},{8,24},{16,0},{24,8},{1,17},{9,25},{17,1},{25,9},{2,18},{10... | collective-permute-start | bytes 786440 | tf_op jit(solution)/shard_map/ppermute | solution.py:22
  19.7 1.0 copy-start
  20.8 2.2 %copy-start.1 = (bf16[2048,1024]{1,0:T(8,128)(2,1)S(1)}, bf16[2048,1024]{1,0:T(8,128)(2,1)}, u32[]{:S(2)}) copy-start(bf16[2048,1024]{1,0:T(8,128)(2,1)} %e_hbm_ref.1) | copy-start | bytes 12582916
  30.7 1.5 %collective-permute-start.10 = (bf16[512,256]{1,0:T(8,128)(2,1)S(1)}, bf16[512,256]{1,0:T(8,128)(2,1)S(1)}, u32[]{:S(2)}, u32[]{:S(2)}) collective-permute-start(bf16[512,256]{1,0:T(8,128)(2,1)S(1)} %collective-permute-done.5.refs_0_), channel_id=1, source_target_pairs={{0,1},{1,0},{2,3},{3,2},{4,5},{5,4},{6,7},{7,6},{8,9},{9,8},{10,11... | collective-permute-start | bytes 786440 | tf_op jit(solution)/shard_map/ppermute | solution.py:22
  30.7 1.9 %collective-permute-start.11 = (bf16[512,256]{1,0:T(8,128)(2,1)S(1)}, bf16[512,256]{1,0:T(8,128)(2,1)S(1)}, u32[]{:S(2)}, u32[]{:S(2)}) collective-permute-start(bf16[512,256]{1,0:T(8,128)(2,1)S(1)} %collective-permute-done.6.refs_1_), channel_id=1, source_target_pairs={{0,1},{1,0},{2,3},{3,2},{4,5},{5,4},{6,7},{7,6},{8,9},{9,8},{10,11... | collective-permute-start | bytes 786440 | tf_op jit(solution)/shard_map/ppermute | solution.py:22
  31.2 1.8 %collective-permute-start.12 = (bf16[512,256]{1,0:T(8,128)(2,1)S(1)}, bf16[512,256]{1,0:T(8,128)(2,1)S(1)}, u32[]{:S(2)}, u32[]{:S(2)}) collective-permute-start(bf16[512,256]{1,0:T(8,128)(2,1)S(1)} %collective-permute-done.3.refs_2_), channel_id=1, source_target_pairs={{0,1},{1,0},{2,3},{3,2},{4,5},{5,4},{6,7},{7,6},{8,9},{9,8},{10,11... | collective-permute-start | bytes 786440 | tf_op jit(solution)/shard_map/ppermute | solution.py:22
  31.3 2.1 %collective-permute-start.13 = (bf16[512,256]{1,0:T(8,128)(2,1)S(1)}, bf16[512,256]{1,0:T(8,128)(2,1)S(1)}, u32[]{:S(2)}, u32[]{:S(2)}) collective-permute-start(bf16[512,256]{1,0:T(8,128)(2,1)S(1)} %collective-permute-done.4.refs_3_), channel_id=1, source_target_pairs={{0,1},{1,0},{2,3},{3,2},{4,5},{5,4},{6,7},{7,6},{8,9},{9,8},{10,11... | collective-permute-start | bytes 786440 | tf_op jit(solution)/shard_map/ppermute | solution.py:22
  39.6 5.5 %collective-permute-start.16 = (f32[16,128]{1,0:T(8,128)S(1)}, f32[16,128]{1,0:T(8,128)S(1)}, u32[]{:S(2)}, u32[]{:S(2)}) collective-permute-start(f32[16,128]{1,0:T(8,128)S(1)} %get-tuple-element.49.refs_0_), channel_id=1, source_target_pairs={{0,6},{1,7},{2,4},{3,5},{4,2},{5,3},{6,0},{7,1},{8,14},{9,15},{10,... | collective-permute-start | bytes 24584 | tf_op jit(solution)/shard_map/ppermute | solution.py:22
  43.3 4.5 %collective-permute-start.15 = (f32[16,128]{1,0:T(8,128)S(1)}, f32[16,128]{1,0:T(8,128)S(1)}, u32[]{:S(2)}, u32[]{:S(2)}) collective-permute-start(f32[16,128]{1,0:T(8,128)S(1)} %get-tuple-element.49.refs_0_), channel_id=1, source_target_pairs={{0,4},{1,5},{2,6},{3,7},{4,0},{5,1},{6,2},{7,3},{8,12},{9,13},{10,... | collective-permute-start | bytes 24584 | tf_op jit(solution)/shard_map/ppermute | solution.py:22
  43.3 4.5 %collective-permute-start.14 = (f32[16,128]{1,0:T(8,128)S(1)}, f32[16,128]{1,0:T(8,128)S(1)}, u32[]{:S(2)}, u32[]{:S(2)}) collective-permute-start(f32[16,128]{1,0:T(8,128)S(1)} %get-tuple-element.49.refs_0_), channel_id=1, source_target_pairs={{0,2},{1,3},{2,0},{3,1},{4,6},{5,7},{6,4},{7,5},{8,10},{9,11},{10,... | collective-permute-start | bytes 24584 | tf_op jit(solution)/shard_map/ppermute | solution.py:22
  50.1 4.6 %collective-permute-start.19 = (f32[16,128]{1,0:T(8,128)S(1)}, f32[16,128]{1,0:T(8,128)S(1)}, u32[]{:S(2)}, u32[]{:S(2)}) collective-permute-start(f32[16,128]{1,0:T(8,128)S(1)} %get-tuple-element.53.refs_0_), channel_id=1, source_target_pairs={{0,24},{8,16},{16,8},{24,0},{1,25},{9,17},{17,9},{25,1},{2,26},{10... | collective-permute-start | bytes 24584 | tf_op jit(solution)/shard_map/ppermute | solution.py:22
  52.7 3.7 %collective-permute-start.18 = (f32[16,128]{1,0:T(8,128)S(1)}, f32[16,128]{1,0:T(8,128)S(1)}, u32[]{:S(2)}, u32[]{:S(2)}) collective-permute-start(f32[16,128]{1,0:T(8,128)S(1)} %get-tuple-element.53.refs_0_), channel_id=1, source_target_pairs={{0,16},{8,24},{16,0},{24,8},{1,17},{9,25},{17,1},{25,9},{2,18},{10... | collective-permute-start | bytes 24584 | tf_op jit(solution)/shard_map/ppermute | solution.py:22
  53.3 3.7 %collective-permute-start.17 = (f32[16,128]{1,0:T(8,128)S(1)}, f32[16,128]{1,0:T(8,128)S(1)}, u32[]{:S(2)}, u32[]{:S(2)}) collective-permute-start(f32[16,128]{1,0:T(8,128)S(1)} %get-tuple-element.53.refs_0_), channel_id=1, source_target_pairs={{0,8},{8,0},{16,24},{24,16},{1,9},{9,1},{17,25},{25,17},{2,10},{10... | collective-permute-start | bytes 24584 | tf_op jit(solution)/shard_map/ppermute | solution.py:22
  59.7 5.5 %collective-permute-start.22 = (f32[16,128]{1,0:T(8,128)S(1)}, f32[16,128]{1,0:T(8,128)S(1)}, u32[]{:S(2)}, u32[]{:S(2)}) collective-permute-start(f32[16,128]{1,0:T(8,128)S(1)} %row_pass.2.refs_0_), channel_id=1, source_target_pairs={{0,6},{1,7},{2,4},{3,5},{4,2},{5,3},{6,0},{7,1},{8,14},{9,15},{10,... | collective-permute-start | bytes 24584 | tf_op jit(solution)/shard_map/ppermute | solution.py:22
  61.1 4.5 %collective-permute-start.21 = (f32[16,128]{1,0:T(8,128)S(1)}, f32[16,128]{1,0:T(8,128)S(1)}, u32[]{:S(2)}, u32[]{:S(2)}) collective-permute-start(f32[16,128]{1,0:T(8,128)S(1)} %row_pass.2.refs_0_), channel_id=1, source_target_pairs={{0,4},{1,5},{2,6},{3,7},{4,0},{5,1},{6,2},{7,3},{8,12},{9,13},{10,... | collective-permute-start | bytes 24584 | tf_op jit(solution)/shard_map/ppermute | solution.py:22
  61.5 4.3 %collective-permute-start.20 = (f32[16,128]{1,0:T(8,128)S(1)}, f32[16,128]{1,0:T(8,128)S(1)}, u32[]{:S(2)}, u32[]{:S(2)}) collective-permute-start(f32[16,128]{1,0:T(8,128)S(1)} %row_pass.2.refs_0_), channel_id=1, source_target_pairs={{0,2},{1,3},{2,0},{3,1},{4,6},{5,7},{6,4},{7,5},{8,10},{9,11},{10,... | collective-permute-start | bytes 24584 | tf_op jit(solution)/shard_map/ppermute | solution.py:22
  68.4 5.3 %collective-permute-start.25 = (f32[16,128]{1,0:T(8,128)S(1)}, f32[16,128]{1,0:T(8,128)S(1)}, u32[]{:S(2)}, u32[]{:S(2)}) collective-permute-start(f32[16,128]{1,0:T(8,128)S(1)} %get-tuple-element.54.refs_0_), channel_id=1, source_target_pairs={{0,24},{8,16},{16,8},{24,0},{1,25},{9,17},{17,9},{25,1},{2,26},{10... | collective-permute-start | bytes 24584 | tf_op jit(solution)/shard_map/ppermute | solution.py:22
  72.1 3.7 %collective-permute-start.24 = (f32[16,128]{1,0:T(8,128)S(1)}, f32[16,128]{1,0:T(8,128)S(1)}, u32[]{:S(2)}, u32[]{:S(2)}) collective-permute-start(f32[16,128]{1,0:T(8,128)S(1)} %get-tuple-element.54.refs_0_), channel_id=1, source_target_pairs={{0,16},{8,24},{16,0},{24,8},{1,17},{9,25},{17,1},{25,9},{2,18},{10... | collective-permute-start | bytes 24584 | tf_op jit(solution)/shard_map/ppermute | solution.py:22
  72.1 3.7 %collective-permute-start.23 = (f32[16,128]{1,0:T(8,128)S(1)}, f32[16,128]{1,0:T(8,128)S(1)}, u32[]{:S(2)}, u32[]{:S(2)}) collective-permute-start(f32[16,128]{1,0:T(8,128)S(1)} %get-tuple-element.54.refs_0_), channel_id=1, source_target_pairs={{0,8},{8,0},{16,24},{24,16},{1,9},{9,1},{17,25},{25,17},{2,10},{10... | collective-permute-start | bytes 24584 | tf_op jit(solution)/shard_map/ppermute | solution.py:22
  78.3 5.5 %collective-permute-start.28 = (f32[16,128]{1,0:T(8,128)S(1)}, f32[16,128]{1,0:T(8,128)S(1)}, u32[]{:S(2)}, u32[]{:S(2)}) collective-permute-start(f32[16,128]{1,0:T(8,128)S(1)} %row_pass.3.refs_0_), channel_id=1, source_target_pairs={{0,6},{1,7},{2,4},{3,5},{4,2},{5,3},{6,0},{7,1},{8,14},{9,15},{10,... | collective-permute-start | bytes 24584 | tf_op jit(solution)/shard_map/ppermute | solution.py:22
  80.1 4.6 %collective-permute-start.27 = (f32[16,128]{1,0:T(8,128)S(1)}, f32[16,128]{1,0:T(8,128)S(1)}, u32[]{:S(2)}, u32[]{:S(2)}) collective-permute-start(f32[16,128]{1,0:T(8,128)S(1)} %row_pass.3.refs_0_), channel_id=1, source_target_pairs={{0,4},{1,5},{2,6},{3,7},{4,0},{5,1},{6,2},{7,3},{8,12},{9,13},{10,... | collective-permute-start | bytes 24584 | tf_op jit(solution)/shard_map/ppermute | solution.py:22
  80.7 3.9 %collective-permute-start.26 = (f32[16,128]{1,0:T(8,128)S(1)}, f32[16,128]{1,0:T(8,128)S(1)}, u32[]{:S(2)}, u32[]{:S(2)}) collective-permute-start(f32[16,128]{1,0:T(8,128)S(1)} %row_pass.3.refs_0_), channel_id=1, source_target_pairs={{0,2},{1,3},{2,0},{3,1},{4,6},{5,7},{6,4},{7,5},{8,10},{9,11},{10,... | collective-permute-start | bytes 24584 | tf_op jit(solution)/shard_map/ppermute | solution.py:22
  87.3 4.5 %collective-permute-start.31 = (f32[16,128]{1,0:T(8,128)S(1)}, f32[16,128]{1,0:T(8,128)S(1)}, u32[]{:S(2)}, u32[]{:S(2)}) collective-permute-start(f32[16,128]{1,0:T(8,128)S(1)} %get-tuple-element.57.refs_0_), channel_id=1, source_target_pairs={{0,24},{8,16},{16,8},{24,0},{1,25},{9,17},{17,9},{25,1},{2,26},{10... | collective-permute-start | bytes 24584 | tf_op jit(solution)/shard_map/ppermute | solution.py:22
  90.0 3.7 %collective-permute-start.30 = (f32[16,128]{1,0:T(8,128)S(1)}, f32[16,128]{1,0:T(8,128)S(1)}, u32[]{:S(2)}, u32[]{:S(2)}) collective-permute-start(f32[16,128]{1,0:T(8,128)S(1)} %get-tuple-element.57.refs_0_), channel_id=1, source_target_pairs={{0,16},{8,24},{16,0},{24,8},{1,17},{9,25},{17,1},{25,9},{2,18},{10... | collective-permute-start | bytes 24584 | tf_op jit(solution)/shard_map/ppermute | solution.py:22
  90.1 3.7 %collective-permute-start.29 = (f32[16,128]{1,0:T(8,128)S(1)}, f32[16,128]{1,0:T(8,128)S(1)}, u32[]{:S(2)}, u32[]{:S(2)}) collective-permute-start(f32[16,128]{1,0:T(8,128)S(1)} %get-tuple-element.57.refs_0_), channel_id=1, source_target_pairs={{0,8},{8,0},{16,24},{24,16},{1,9},{9,1},{17,25},{25,17},{2,10},{10... | collective-permute-start | bytes 24584 | tf_op jit(solution)/shard_map/ppermute | solution.py:22
  97.7 16.1 %collective-permute-start.33 = (bf16[2048,128]{1,0:T(8,128)(2,1)S(1)}, bf16[2048,128]{1,0:T(8,128)(2,1)S(1)}, u32[]{:S(2)}, u32[]{:S(2)}) collective-permute-start(bf16[2048,128]{1,0:T(8,128)(2,1)S(1)} %get-tuple-element.62), channel_id=1, source_target_pairs={{0,2},{1,3},{2,0},{3,1},{4,6},{5,7},{6,4},{7,5},{8,10},{9,11},{10,... | collective-permute-start | bytes 1572872 | tf_op jit(solution)/shard_map/ppermute | solution.py:22
  102.2 19.6 %collective-permute-start.32 = (bf16[2048,128]{1,0:T(8,128)(2,1)S(1)}, bf16[2048,128]{1,0:T(8,128)(2,1)S(1)}, u32[]{:S(2)}, u32[]{:S(2)}) collective-permute-start(bf16[2048,128]{1,0:T(8,128)(2,1)S(1)} %get-tuple-element.60), channel_id=1, source_target_pairs={{0,2},{1,3},{2,0},{3,1},{4,6},{5,7},{6,4},{7,5},{8,10},{9,11},{10,... | collective-permute-start | bytes 1572872 | tf_op jit(solution)/shard_map/ppermute | solution.py:22
  114.0 15.8 %collective-permute-start.34 = (bf16[2048,128]{1,0:T(8,128)(2,1)S(1)}, bf16[2048,128]{1,0:T(8,128)(2,1)S(1)}, u32[]{:S(2)}, u32[]{:S(2)}) collective-permute-start(bf16[2048,128]{1,0:T(8,128)(2,1)S(1)} %add_convert_fusion.1), channel_id=1, source_target_pairs={{0,4},{1,5},{2,6},{3,7},{4,0},{5,1},{6,2},{7,3},{8,12},{9,13},{10,... | collective-permute-start | bytes 1572872 | tf_op jit(solution)/shard_map/ppermute | solution.py:22

commit v10 on v9

--- a/solution.py
+++ b/solution.py
@@ -13,8 +13,7 @@
 NEGATIVE = -1e30
 
 VMEM = pl.BlockSpec(memory_space=pltpu.VMEM)
-HBM = pl.BlockSpec(memory_space=pltpu.HBM)
-SMEM = pl.BlockSpec(memory_space=pltpu.SMEM)
+ANY = pl.BlockSpec(memory_space=pl.ANY)
 
 
 def swap(x, axis, offset):
@@ -112,6 +111,25 @@
     def place(self, t, u):
         padding = (t == self.row_tiles) | (u == self.columns)
         return jnp.where(padding, self.dummy, t * self.columns + u)
+
+
+def with_table(kernel, table, *settings):
+    def body(hbm_ref, *refs):
+        *refs, smem_ref, sem = refs
+        copy = pltpu.make_async_copy(hbm_ref, smem_ref, sem)
+        copy.start()
+
+        def arrived():
+            copy.wait()
+            return smem_ref
+
+        kernel(table, *settings, arrived, *refs)
+
+    return body
+
+
+def table_scratch(lists):
+    return [pltpu.SMEM(lists.shape, jnp.int32), pltpu.SemaphoreType.DMA]
 
 
 def blank():
@@ -211,19 +229,20 @@
     return features
 
 
-def early_panel_kernel(table, places, table_ref, e_hbm_ref, *refs):
+def early_panel_kernel(table, places, arrived, e_hbm_ref, *refs):
     pieces, (s_ref, p_ref, e_ref, sem) = refs[:-4], refs[-4:]
     load = pltpu.make_async_copy(e_hbm_ref, e_ref, sem)
     load.start()
     for place, piece in zip(places, pieces):
         place.copy_to(p_ref, piece)
     s_ref[table.dummy] = lowest()
+    table_ref = arrived()
     load.wait()
     features = quarters([(0, 0), (2, 1)], p_ref, table.columns)
     score_pairs(table, table_ref, e_ref, p_ref, s_ref, features, False, None)
 
 
-def panel_kernel(table, places, add, table_ref, e_ref, *refs):
+def panel_kernel(table, places, add, arrived, e_ref, *refs):
     pieces, (s_ref, p_ref, out_ref, acc_ref) = refs[:-4], refs[-4:]
     if add:
         pieces = pieces[:-2]
@@ -232,6 +251,7 @@
         place.copy_to(p_ref, piece)
     for t in range(row_tiles):
         acc_ref[t] = lowest()
+    table_ref = arrived()
 
     def done(t, u, left, right):
         peak = acc_ref[t]
@@ -264,7 +284,7 @@
     out_ref[...] = peaks.T[:row_tiles] + jnp.log(lying([acc_ref[t] for t in range(row_tiles)]))
 
 
-def row_kernel(table, log_column, table_ref, s_ref, w_ref, m_ref, r_ref, *refs):
+def row_kernel(table, log_column, arrived, s_ref, w_ref, m_ref, r_ref, *refs):
     parts, (out_ref, c_ref, v_ref, acc_ref) = refs[:-4], refs[-4:]
     row_tiles, columns = table.row_tiles, table.columns
     column = log_column - combine([part[...] for part in parts])
@@ -273,6 +293,7 @@
     rest = jnp.zeros((c_ref.shape[0] - columns, TILE), jnp.float32)
     c_ref[columns:] = rest
     v_ref[columns:] = rest
+    table_ref = arrived()
 
     for t in range(row_tiles):
 
@@ -320,12 +341,13 @@
     return peak, jnp.sum(total, axis=0, keepdims=True)
 
 
-def first_column_kernel(table, table_ref, s_ref, *refs):
+def first_column_kernel(table, arrived, s_ref, *refs):
     parts, (out_ref, r_ref, w_ref, m_ref, wide_ref, acc_ref) = refs[:-6], refs[-6:]
     row = -combine([part[...] for part in parts])
     r_ref[...] = row
     spread_rows(row, wide_ref)
     w_ref[table.dummy] = blank().astype(jnp.bfloat16)
+    table_ref = arrived()
 
     def keep(at, value):
         w_ref[at] = value.astype(jnp.bfloat16)
@@ -357,13 +379,14 @@
                 out_ref[u : u + 1, :] = peak + jnp.log(total)
 
 
-def column_kernel(table, table_ref, s_ref, w_ref, m_ref, first_ref, *refs):
+def column_kernel(table, arrived, s_ref, w_ref, m_ref, first_ref, *refs):
     parts, (out_ref, r_ref, r_out_ref, wide_ref, acc_ref) = refs[:-5], refs[-5:]
     row = -combine([part[...] for part in parts])
     r_ref[...] = row
     r_out_ref[...] = row
     factor = jnp.exp(row - first_ref[...])
     spread_rows(factor, wide_ref)
+    table_ref = arrived()
 
     for u in range(table.columns):
 
@@ -431,7 +454,7 @@
                     outs[n][rows, :] = total[:, k * width : (k + 1) * width]
 
 
-def plan_kernel(table, log_column, lines, table_ref, s_ref, r_ref, p_ref, *refs):
+def plan_kernel(table, log_column, lines, arrived, s_ref, r_ref, p_ref, *refs):
     parts, (out_ref, kept_ref, own_ref, c_ref, wide_ref, total_ref) = refs[:-6], refs[-6:]
     row_tiles, columns = table.row_tiles, table.columns
     core = lax.rem(lax.axis_index("proto"), 2)
@@ -439,6 +462,7 @@
     half = columns // 2
     own_ref[...] = c_ref[pl.ds(pl.multiple_of(core * half, half), half), :]
     spread_rows(r_ref[...], wide_ref)
+    table_ref = arrived()
 
     def strip(number, real, pair, tiles):
         strips = []
@@ -459,11 +483,11 @@
     plan_blocks(table, table_ref, p_ref, lines, [lines - 1], width, strip, [out_ref], total_ref)
 
 
-def rest_kernel(table, lines, table_ref, kept_ref, p_ref, *refs):
+def rest_kernel(table, lines, arrived, kept_ref, p_ref, *refs):
     outs, total_ref = refs[:-1], refs[-1]
     width = outs[0].shape[1]
     strip = lambda number, real, pair, tiles: kept_ref[number]
-    plan_blocks(table, table_ref, p_ref, lines, list(range(lines - 1)), width, strip, outs, total_ref)
+    plan_blocks(table, arrived(), p_ref, lines, list(range(lines - 1)), width, strip, outs, total_ref)
 
 
 def params(mebibytes):
@@ -489,11 +513,11 @@
     def late(places, add, e, pieces, before):
         at = 2 + len(pieces)
         return pl.pallas_call(
-            functools.partial(panel_kernel, table, places, add),
+            with_table(panel_kernel, table, places, add),
             out_shape=(panel, whole, row_shape),
-            in_specs=[SMEM] + [VMEM] * (1 + len(pieces) + len(before)),
+            in_specs=[ANY] + [VMEM] * (1 + len(pieces) + len(before)),
             out_specs=(VMEM, VMEM, VMEM),
-            scratch_shapes=[peaks],
+            scratch_shapes=[peaks] + table_scratch(lists),
             input_output_aliases={at: 0, at + 1: 1} if add else {},
             compiler_params=params(8),
             name="panel",
@@ -507,7 +531,7 @@
     top, bottom = shard[:half], shard[half:]
     near_bottom = swap(bottom, "row", 1)
     far_top = swap(top, "row", 2)
-    near_bottom, far_top, top, bottom = tied(near_bottom, far_top, top, bottom)
+    near_bottom, far_top, top, bottom, lists = tied(near_bottom, far_top, top, bottom, lists)
     cross_top = swap(far_top, "row", 1)
     cross_bottom = swap(near_bottom, "row", 2)
     near_top = swap(top, "row", 1)
@@ -517,11 +541,11 @@
     places = [Piece(own, *at) for own in (True, False) for at in ((0, 0), (half, 1), (0, 2))]
     visits = table.dummy * TILE * TILE
     similar, known, e = pl.pallas_call(
-        functools.partial(early_panel_kernel, table, places),
+        with_table(early_panel_kernel, table, places),
         out_shape=(panel, whole, pltpu.VMEM(embeddings.shape, jnp.bfloat16)),
-        in_specs=[SMEM, pl.BlockSpec(memory_space=pl.ANY)] + [VMEM] * len(pieces),
+        in_specs=[ANY, ANY] + [VMEM] * len(pieces),
         out_specs=(VMEM, VMEM, VMEM),
-        scratch_shapes=[pltpu.SemaphoreType.DMA],
+        scratch_shapes=[pltpu.SemaphoreType.DMA] + table_scratch(lists),
         compiler_params=params(6),
         cost_estimate=pl.CostEstimate(
             flops=visits * features, bytes_accessed=8 * visits, transcendentals=0
@@ -587,32 +611,32 @@
 
     parts = row_exchange(row_part)
     column_part, first_row, kept, peaks = pl.pallas_call(
-        functools.partial(first_column_kernel, table),
+        with_table(first_column_kernel, table),
         out_shape=(column_shape, row_shape, pltpu.VMEM(panel, jnp.bfloat16), column_shape),
-        in_specs=[SMEM] + [VMEM] * (1 + len(parts)),
+        in_specs=[ANY] + [VMEM] * (1 + len(parts)),
         out_specs=(VMEM,) * 4,
-        scratch_shapes=[wide, tall],
+        scratch_shapes=[wide, tall] + table_scratch(lists),
         compiler_params=params(4),
         name="first_column_pass",
     )(lists, similar, *parts)
     for sweep in range(1, ITERS):
         parts = column_exchange(column_part)
         row_part = pl.pallas_call(
-            functools.partial(row_kernel, table, log_column),
+            with_table(row_kernel, table, log_column),
             out_shape=row_shape,
-            in_specs=[SMEM] + [VMEM] * (4 + len(parts)),
+            in_specs=[ANY] + [VMEM] * (4 + len(parts)),
             out_specs=VMEM,
-            scratch_shapes=[factors, factors, wide],
+            scratch_shapes=[factors, factors, wide] + table_scratch(lists),
             compiler_params=params(4),
             name="row_pass",
         )(lists, similar, kept, peaks, first_row, *parts)
         parts = row_exchange(row_part)
         column_part, row_potential, row_out = pl.pallas_call(
-            functools.partial(column_kernel, table),
+            with_table(column_kernel, table),
             out_shape=(column_shape, row_shape, row_shape),
-            in_specs=[SMEM] + [VMEM] * (4 + len(parts)),
+            in_specs=[ANY] + [VMEM] * (4 + len(parts)),
             out_specs=(VMEM,) * 3,
-            scratch_shapes=[wide, tall],
+            scratch_shapes=[wide, tall] + table_scratch(lists),
             compiler_params=params(4),
             name="column_pass",
         )(lists, similar, kept, peaks, first_row, *parts)
@@ -624,25 +648,25 @@
         return pltpu.VMEM((row_tiles, TILE, taken * width), jnp.float32)
 
     last, plan, column_potential = pl.pallas_call(
-        functools.partial(plan_kernel, table, log_column, lines),
+        with_table(plan_kernel, table, log_column, lines),
         out_shape=[
             block,
             pltpu.VMEM((table.items + 1, 4 * TILE, 2 * TILE), jnp.bfloat16),
             jax.ShapeDtypeStruct((half, TILE), jnp.float32),
         ],
-        in_specs=[SMEM] + [VMEM] * (3 + len(parts)),
+        in_specs=[ANY] + [VMEM] * (3 + len(parts)),
         out_specs=[VMEM] * 3,
-        scratch_shapes=[pltpu.VMEM((columns, TILE), jnp.float32), wide, sums(1)],
+        scratch_shapes=[pltpu.VMEM((columns, TILE), jnp.float32), wide, sums(1)] + table_scratch(lists),
         compiler_params=params(12),
         name="plan",
     )(lists, similar, row_potential, whole, *parts)
     visits = table.dummy * TILE * TILE
     blocks = pl.pallas_call(
-        functools.partial(rest_kernel, table, lines),
+        with_table(rest_kernel, table, lines),
         out_shape=[block] * (lines - 1),
-        in_specs=[SMEM] + [VMEM] * 2,
+        in_specs=[ANY] + [VMEM] * 2,
         out_specs=[VMEM] * (lines - 1),
-        scratch_shapes=[sums(lines - 1)],
+        scratch_shapes=[sums(lines - 1)] + table_scratch(lists),
         compiler_params=params(12),
         cost_estimate=pl.CostEstimate(
             flops=2 * visits * (lines - 1) * width, bytes_accessed=4 * visits, transcendentals=0

time: 131 us -> 129 us (0.985); the launches traced: 131 us -> 127 us
  Pallas kernels: 30.9 us -> 25.9 us
    pallas_call x9, Pallas kernels: 30.9 us -> 25.9 us  [the longest x1 5.4 us: late(): pl.pallas_call(with_table(panel_kernel, table, places, add), out_shape=(p...]
  transfers between devices with their start and end apart: 35 -> 35, of which waited for: 25 -> 23; matrix products, arithmetic and copies ran while one was open for 4% -> 4% of each run, Pallas kernels for 6% -> 5%
where the time goes in v10:
time: 129 us; the launch traced here: 127 us
  waiting for transfers between devices  48.9 us (38%)
  starting transfers between devices  40.4 us (31%)
  Pallas kernels  25.9 us (20%)
  local copies, waits for them, and re-layouts  5.43 us (4%)
  other arithmetic  4.4 us (3%)
  between operations  2.15 us (2%)
    ppermute x35, waiting for transfers between devices, swap(): return lax.ppermute(x, axis, [(i, i ^ offset) for i in range(size)])  48.9 us
    ppermute x35, starting transfers between devices, swap(): return lax.ppermute(x, axis, [(i, i ^ offset) for i in range(size)])  40.4 us
    pallas_call x1, Pallas kernels, late(): pl.pallas_call(with_table(panel_kernel, table, places, add), out_shape=(p...  5.4 us
    pallas_call x2, Pallas kernels, shards(): pl.pallas_call(with_table(row_kernel, table, log_column), out_shape=row_s...  4.65 us
    pallas_call x2, Pallas kernels, shards(): pl.pallas_call(with_table(column_kernel, table), out_shape=(column_shape,...  4.29 us
    pallas_call x1, Pallas kernels, shards(): pl.pallas_call(with_table(rest_kernel, table, lines), out_shape=[block] *...  3.35 us
    pallas_call x1, Pallas kernels, make_panel(): pl.pallas_call(with_table(early_panel_kernel, table, places), out_shape=(...  3.23 us
    unnamed x4, local copies, waits for them, and re-layouts  3.23 us
  transfers between devices with their start and end apart: 35, of which 23 were waited for; matrix products, arithmetic and copies ran while one was open for 4% of the time, Pallas kernels for 5%

profile of v10, /device:TPU:0, one launch (start us, length us, event | category | flops | bytes accessed | tf_op | source)
XLA Modules:
  0.0 127.1 jit_solution(12345975110363120457)
XLA Ops:
  1.2 1.1 fusion.5
  2.3 3.0 %collective-permute-start.2 = (bf16[512,256]{1,0:T(8,128)(2,1)S(1)}, bf16[512,256]{1,0:T(8,128)(2,1)S(1)}, u32[]{:S(2)}, u32[]{:S(2)}) collective-permute-start(bf16[512,256]{1,0:T(8,128)(2,1)S(1)} %get-tuple-element.38), channel_id=1, source_target_pairs={{0,16},{8,24},{16,0},{24,8},{1,17},{9,25},{17,1},{25,9},{2,18},{10... | collective-permute-start | bytes 786440 | tf_op jit(solution)/shard_map/ppermute | solution.py:21
  5.3 1.5 %collective-permute-start.1 = (bf16[512,256]{1,0:T(8,128)(2,1)S(1)}, bf16[512,256]{1,0:T(8,128)(2,1)S(1)}, u32[]{:S(2)}, u32[]{:S(2)}) collective-permute-start(bf16[512,256]{1,0:T(8,128)(2,1)S(1)} %get-tuple-element.39), channel_id=1, source_target_pairs={{0,8},{8,0},{16,24},{24,16},{1,9},{9,1},{17,25},{25,17},{2,10},{10... | collective-permute-start | bytes 786440 | tf_op jit(solution)/shard_map/ppermute | solution.py:21
  11.9 0.7 concatenate.25.hbm_ref
  13.8 1.5 %collective-permute-start.3 = (bf16[512,256]{1,0:T(8,128)(2,1)S(1)}, bf16[512,256]{1,0:T(8,128)(2,1)S(1)}, u32[]{:S(2)}, u32[]{:S(2)}) collective-permute-start(bf16[512,256]{1,0:T(8,128)(2,1)S(1)} %collective-permute-done.2.refs_3_), channel_id=1, source_target_pairs={{0,8},{8,0},{16,24},{24,16},{1,9},{9,1},{17,25},{25,17},{2,10},{10... | collective-permute-start | bytes 786440 | tf_op jit(solution)/shard_map/ppermute | solution.py:21
  16.3 1.5 %collective-permute-start.6 = (bf16[512,256]{1,0:T(8,128)(2,1)S(1)}, bf16[512,256]{1,0:T(8,128)(2,1)S(1)}, u32[]{:S(2)}, u32[]{:S(2)}) collective-permute-start(bf16[512,256]{1,0:T(8,128)(2,1)S(1)} %get-tuple-element.39), channel_id=1, source_target_pairs={{0,16},{8,24},{16,0},{24,8},{1,17},{9,25},{17,1},{25,9},{2,18},{10... | collective-permute-start | bytes 786440 | tf_op jit(solution)/shard_map/ppermute | solution.py:21
  17.9 1.0 copy-done
  18.9 2.2 %copy-done.1 = bf16[2048,1024]{1,0:T(8,128)(2,1)S(1)} copy-done((bf16[2048,1024]{1,0:T(8,128)(2,1)S(1)}, bf16[2048,1024]{1,0:T(8,128)(2,1)}, u32[]{:S(2)}) %copy-start.1) | copy-done | bytes 4194328
  21.1 3.2 %early_panel.1 = (f32[257,128,128]{2,1,0:T(8,128)S(1)}, bf16[2048,1024]{1,0:T(8,128)(2,1)S(1)}, bf16[2048,1024]{1,0:T(8,128)(2,1)S(1)}) custom-call(s32[1284]{0:T(1024)S(1)} %concatenate.25.hbm_ref, bf16[2048,1024]{1,0:T(8,128)(2,1)S(1)} %copy-done.1, bf16[1024,256]{1,0:T(8,128)(2,1)S(1)} %copy-done, bf16[512,256]{1,0:T(8,128)(2,1)S(1)} %collective-permute-done.1.refs_2_, ...), custom_call_target="tpu_custom_call" | custom-call | flops 4294967296 | bytes 33554432 | tf_op jit(solution)/shard_map/early_panel/pallas_call | solution.py:543
  24.4 3.3 %collective-permute-done.5.refs_1_ = bf16[512,256]{1,0:T(8,128)(2,1)S(1)} collective-permute-done((bf16[512,256]{1,0:T(8,128)(2,1)S(1)}, bf16[512,256]{1,0:T(8,128)(2,1)S(1)}, u32[]{:S(2)}, u32[]{:S(2)}) %collective-permute-start.5) | collective-permute-done | bytes 262176 | tf_op jit(solution)/shard_map/ppermute | solution.py:21
  27.7 1.2 collective-permute-done.6.refs_2_
  31.5 5.4 %panel.1 = (f32[257,128,128]{2,1,0:T(8,128)S(1)}, bf16[2048,1024]{1,0:T(8,128)(2,1)S(1)}, f32[16,128]{1,0:T(8,128)S(1)}) custom-call(s32[1284]{0:T(1024)S(1)} %concatenate.25.hbm_ref, bf16[2048,1024]{1,0:T(8,128)(2,1)S(1)} %get-tuple-element.43.refs_0_, ...), custom_call_target="tpu_custom_call", output_to_operand_aliasing={{0}: (10, {}), {1}: (11, {})} | custom-call | tf_op jit(solution)/shard_map/panel/pallas_call | solution.py:515
  36.9 4.2 %collective-permute-start.16 = (f32[16,128]{1,0:T(8,128)S(1)}, f32[16,128]{1,0:T(8,128)S(1)}, u32[]{:S(2)}, u32[]{:S(2)}) collective-permute-start(f32[16,128]{1,0:T(8,128)S(1)} %get-tuple-element.51.refs_1_), channel_id=1, source_target_pairs={{0,6},{1,7},{2,4},{3,5},{4,2},{5,3},{6,0},{7,1},{8,14},{9,15},{10,... | collective-permute-start | bytes 24584 | tf_op jit(solution)/shard_map/ppermute | solution.py:21
  41.8 1.0 collective-permute-done.16.refs_4_
  42.8 2.9 %collective-permute-done.15.refs_3_ = f32[16,128]{1,0:T(8,128)S(1)} collective-permute-done((f32[16,128]{1,0:T(8,128)S(1)}, f32[16,128]{1,0:T(8,128)S(1)}, u32[]{:S(2)}, u32[]{:S(2)}) %collective-permute-start.15) | collective-permute-done | bytes 8224 | tf_op jit(solution)/shard_map/ppermute | solution.py:21
  45.7 1.8 %first_column_pass.1 = (f32[16,128]{1,0:T(8,128)S(1)}, f32[16,128]{1,0:T(8,128)S(1)}, bf16[257,128,128]{2,1,0:T(8,128)(2,1)S(1)}, f32[16,128]{1,0:T(8,128)S(1)}) custom-call(s32[1284]{0:T(1024)S(1)} %concatenate.25.hbm_ref, f32[257,128,128]{2,1,0:T(8,128)S(1)} %get-tuple-element.50.refs_0_, f32[16,128]{1,0:T(8,128)S(1)} %get-tuple-element.51.refs_1_, ...), custom_call_target="tpu_custom_call" | custom-call | tf_op jit(solution)/shard_map/first_column_pass/pallas_call | solution.py:613
  47.5 3.4 %collective-permute-start.19 = (f32[16,128]{1,0:T(8,128)S(1)}, f32[16,128]{1,0:T(8,128)S(1)}, u32[]{:S(2)}, u32[]{:S(2)}) collective-permute-start(f32[16,128]{1,0:T(8,128)S(1)} %get-tuple-element.55.refs_4_), channel_id=1, source_target_pairs={{0,24},{8,16},{16,8},{24,0},{1,25},{9,17},{17,9},{25,1},{2,26},{10... | collective-permute-start | bytes 24584 | tf_op jit(solution)/shard_map/ppermute | solution.py:21
  51.0 1.1 collective-permute-start.17
  52.6 2.0 %collective-permute-done.18.refs_6_ = f32[16,128]{1,0:T(8,128)S(1)} collective-permute-done((f32[16,128]{1,0:T(8,128)S(1)}, f32[16,128]{1,0:T(8,128)S(1)}, u32[]{:S(2)}, u32[]{:S(2)}) %collective-permute-start.18) | collective-permute-done | bytes 8224 | tf_op jit(solution)/shard_map/ppermute | solution.py:21
  54.6 2.4 %row_pass.2.refs_4_ = f32[16,128]{1,0:T(8,128)S(1)} custom-call(s32[1284]{0:T(1024)S(1)} %concatenate.25.hbm_ref, f32[257,128,128]{2,1,0:T(8,128)S(1)} %get-tuple-element.50.refs_0_, bf16[257,128,128]{2,1,0:T(8,128)(2,1)S(1)} %get-tuple-element.52.refs_1_, f32[16,128]{1,0:T(8,128)S(1)} %get-tuple-element.53.refs_2_, ...), custom_call_target="tpu_custom_call" | custom-call | tf_op jit(solution)/shard_map/row_pass/pallas_call | solution.py:624
  57.0 1.9 %collective-permute-start.22 = (f32[16,128]{1,0:T(8,128)S(1)}, f32[16,128]{1,0:T(8,128)S(1)}, u32[]{:S(2)}, u32[]{:S(2)}) collective-permute-start(f32[16,128]{1,0:T(8,128)S(1)} %row_pass.2.refs_4_), channel_id=1, source_target_pairs={{0,6},{1,7},{2,4},{3,5},{4,2},{5,3},{6,0},{7,1},{8,14},{9,15},{10,... | collective-permute-start | bytes 24584 | tf_op jit(solution)/shard_map/ppermute | solution.py:21
  59.4 2.1 %collective-permute-start.20 = (f32[16,128]{1,0:T(8,128)S(1)}, f32[16,128]{1,0:T(8,128)S(1)}, u32[]{:S(2)}, u32[]{:S(2)}) collective-permute-start(f32[16,128]{1,0:T(8,128)S(1)} %row_pass.2.refs_4_), channel_id=1, source_target_pairs={{0,2},{1,3},{2,0},{3,1},{4,6},{5,7},{6,4},{7,5},{8,10},{9,11},{10,... | collective-permute-start | bytes 24584 | tf_op jit(solution)/shard_map/ppermute | solution.py:21
  61.5 1.1 collective-permute-done.22.refs_7_
  62.5 1.0 collective-permute-done.21.refs_6_
  63.5 2.1 %column_pass.2 = (f32[16,128]{1,0:T(8,128)S(1)}, f32[16,128]{1,0:T(8,128)}, f32[16,128]{1,0:T(8,128)}) custom-call(s32[1284]{0:T(1024)S(1)} %concatenate.25.hbm_ref, f32[257,128,128]{2,1,0:T(8,128)S(1)} %get-tuple-element.50.refs_0_, bf16[257,128,128]{2,1,0:T(8,128)(2,1)S(1)} %get-tuple-element.52.refs_1_, f32[16,128]{1,0:T(8,128)S(1)} %get-tuple-element.53.refs_2_, ...), custom_call_target="tpu_custom_call" | custom-call | tf_op jit(solution)/shard_map/column_pass/pallas_call | solution.py:634
  65.7 3.4 %collective-permute-start.25 = (f32[16,128]{1,0:T(8,128)S(1)}, f32[16,128]{1,0:T(8,128)S(1)}, u32[]{:S(2)}, u32[]{:S(2)}) collective-permute-start(f32[16,128]{1,0:T(8,128)S(1)} %get-tuple-element.56.refs_4_), channel_id=1, source_target_pairs={{0,24},{8,16},{16,8},{24,0},{1,25},{9,17},{17,9},{25,1},{2,26},{10... | collective-permute-start | bytes 24584 | tf_op jit(solution)/shard_map/ppermute | solution.py:21
  69.1 0.9 collective-permute-start.23
  70.0 0.7 collective-permute-done.25.refs_7_
  70.8 2.0 %collective-permute-done.24.refs_6_ = f32[16,128]{1,0:T(8,128)S(1)} collective-permute-done((f32[16,128]{1,0:T(8,128)S(1)}, f32[16,128]{1,0:T(8,128)S(1)}, u32[]{:S(2)}, u32[]{:S(2)}) %collective-permute-start.24) | collective-permute-done | bytes 8224 | tf_op jit(solution)/shard_map/ppermute | solution.py:21
  72.8 2.2 %row_pass.3.refs_4_ = f32[16,128]{1,0:T(8,128)S(1)} custom-call(s32[1284]{0:T(1024)S(1)} %concatenate.25.hbm_ref, f32[257,128,128]{2,1,0:T(8,128)S(1)} %get-tuple-element.50.refs_0_, bf16[257,128,128]{2,1,0:T(8,128)(2,1)S(1)} %get-tuple-element.52.refs_1_, f32[16,128]{1,0:T(8,128)S(1)} %get-tuple-element.53.refs_2_, ...), custom_call_target="tpu_custom_call" | custom-call | tf_op jit(solution)/shard_map/row_pass/pallas_call | solution.py:624
  75.0 2.4 %collective-permute-start.28 = (f32[16,128]{1,0:T(8,128)S(1)}, f32[16,128]{1,0:T(8,128)S(1)}, u32[]{:S(2)}, u32[]{:S(2)}) collective-permute-start(f32[16,128]{1,0:T(8,128)S(1)} %row_pass.3.refs_4_), channel_id=1, source_target_pairs={{0,6},{1,7},{2,4},{3,5},{4,2},{5,3},{6,0},{7,1},{8,14},{9,15},{10,... | collective-permute-start | bytes 24584 | tf_op jit(solution)/shard_map/ppermute | solution.py:21
  77.5 1.0 collective-permute-start.27
  78.5 1.0 collective-permute-start.26
  79.5 1.1 collective-permute-done.28.refs_7_
  80.5 1.5 %collective-permute-done.27.refs_6_ = f32[16,128]{1,0:T(8,128)S(1)} collective-permute-done((f32[16,128]{1,0:T(8,128)S(1)}, f32[16,128]{1,0:T(8,128)S(1)}, u32[]{:S(2)}, u32[]{:S(2)}) %collective-permute-start.27) | collective-permute-done | bytes 8224 | tf_op jit(solution)/shard_map/ppermute | solution.py:21
  82.1 2.1 %column_pass.3 = (f32[16,128]{1,0:T(8,128)S(1)}, f32[16,128]{1,0:T(8,128)S(1)}, f32[16,128]{1,0:T(8,128)}) custom-call(s32[1284]{0:T(1024)S(1)} %concatenate.25.hbm_ref, f32[257,128,128]{2,1,0:T(8,128)S(1)} %get-tuple-element.50.refs_0_, bf16[257,128,128]{2,1,0:T(8,128)(2,1)S(1)} %get-tuple-element.52.refs_1_, f32[16,128]{1,0:T(8,128)S(1)} %get-tuple-element.53.refs_2_, ...), custom_call_target="tpu_custom_call" | custom-call | tf_op jit(solution)/shard_map/column_pass/pallas_call | solution.py:634
  84.3 3.2 %collective-permute-start.31 = (f32[16,128]{1,0:T(8,128)S(1)}, f32[16,128]{1,0:T(8,128)S(1)}, u32[]{:S(2)}, u32[]{:S(2)}) collective-permute-start(f32[16,128]{1,0:T(8,128)S(1)} %get-tuple-element.59.refs_3_), channel_id=1, source_target_pairs={{0,24},{8,16},{16,8},{24,0},{1,25},{9,17},{17,9},{25,1},{2,26},{10... | collective-permute-start | bytes 24584 | tf_op jit(solution)/shard_map/ppermute | solution.py:21
  87.5 1.0 collective-permute-start.29
  89.1 2.0 %collective-permute-done.30.refs_5_ = f32[16,128]{1,0:T(8,128)S(1)} collective-permute-done((f32[16,128]{1,0:T(8,128)S(1)}, f32[16,128]{1,0:T(8,128)S(1)}, u32[]{:S(2)}, u32[]{:S(2)}) %collective-permute-start.30) | collective-permute-done | bytes 8224 | tf_op jit(solution)/shard_map/ppermute | solution.py:21
  91.2 3.2 %plan.1 = (bf16[2048,128]{1,0:T(8,128)(2,1)S(1)}, bf16[33,512,256]{2,1,0:T(8,128)(2,1)S(1)}, f32[8,128]{1,0:T(8,128)}) custom-call(s32[1284]{0:T(1024)S(1)} %concatenate.25.hbm_ref, f32[257,128,128]{2,1,0:T(8,128)S(1)} %get-tuple-element.50.refs_0_, f32[16,128]{1,0:T(8,128)S(1)} %get-tuple-element.57.refs_1_, ...), custom_call_target="tpu_custom_call" | custom-call | tf_op jit(solution)/shard_map/plan/pallas_call | solution.py:650
  94.3 1.1 collective-permute-start.33
  95.4 3.3 %rest_of_plan.1 = (bf16[2048,128]{1,0:T(8,128)(2,1)S(1)}, bf16[2048,128]{1,0:T(8,128)(2,1)S(1)}, bf16[2048,128]{1,0:T(8,128)(2,1)S(1)}) custom-call(s32[1284]{0:T(1024)S(1)} %concatenate.25.hbm_ref, bf16[33,512,256]{2,1,0:T(8,128)(2,1)S(1)} %get-tuple-element.60.refs_0_, bf16[2048,1024]{1,0:T(8,128)(2,1)S(1)} %get-tuple-element.58.refs_2_.refs_1_), custom_call_target="tpu_custom_call" | custom-call | flops 3221225472 | bytes 16777216 | tf_op jit(solution)/shard_map/rest_of_plan/pallas_call | solution.py:664
  98.8 1.0 collective-permute-start.32
  99.8 10.3 %collective-permute-done.33 = bf16[2048,128]{1,0:T(8,128)(2,1)S(1)} collective-permute-done((bf16[2048,128]{1,0:T(8,128)(2,1)S(1)}, bf16[2048,128]{1,0:T(8,128)(2,1)S(1)}, u32[]{:S(2)}, u32[]{:S(2)}) %collective-permute-start.33) | collective-permute-done | bytes 524320 | tf_op jit(solution)/shard_map/ppermute | solution.py:21
  110.3 0.8 collective-permute-start.34
  111.1 6.5 %collective-permute-done.32 = bf16[2048,128]{1,0:T(8,128)(2,1)S(1)} collective-permute-done((bf16[2048,128]{1,0:T(8,128)(2,1)S(1)}, bf16[2048,128]{1,0:T(8,128)(2,1)S(1)}, u32[]{:S(2)}, u32[]{:S(2)}) %collective-permute-start.32) | collective-permute-done | bytes 524320 | tf_op jit(solution)/shard_map/ppermute | solution.py:21
  117.6 8.5 %collective-permute-done.34 = bf16[2048,128]{1,0:T(8,128)(2,1)S(1)} collective-permute-done((bf16[2048,128]{1,0:T(8,128)(2,1)S(1)}, bf16[2048,128]{1,0:T(8,128)(2,1)S(1)}, u32[]{:S(2)}, u32[]{:S(2)}) %collective-permute-start.34) | collective-permute-done | bytes 524320 | tf_op jit(solution)/shard_map/ppermute | solution.py:21
  126.1 1.0 add_convert_fusion
  (68 shorter events, 11.7 us)
Async XLA Ops:
  0.6 6.9 %collective-permute-start = (s32[16,8]{0,1:T(8,128)}, s32[16,8]{0,1:T(8,128)S(1)}, u32[]{:S(2)}, u32[]{:S(2)}) collective-permute-start(s32[16,8]{0,1:T(8,128)} %param.5), channel_id=1, source_target_pairs={{0,1},{1,0},{2,3},{3,2},{4,5},{5,4},{6,7},{7,6},{8,9},{9,8},{10,11... | collective-permute-start | bytes 1544 | tf_op jit(solution)/shard_map/ppermute | solution.py:21
  1.1 16.7 %collective-permute-start.7 = (bf16[1024,256]{1,0:T(8,128)(2,1)}, bf16[1024,256]{1,0:T(8,128)(2,1)S(1)}, u32[]{:S(2)}, u32[]{:S(2)}) collective-permute-start(bf16[1024,256]{1,0:T(8,128)(2,1)} %refs_1_.1), channel_id=1, source_target_pairs={{0,1},{1,0},{2,3},{3,2},{4,5},{5,4},{6,7},{7,6},{8,9},{9,8},{10,11... | collective-permute-start | bytes 1572872 | tf_op jit(solution)/shard_map/ppermute | solution.py:21
  2.3 10.3 %collective-permute-start.2 = (bf16[512,256]{1,0:T(8,128)(2,1)S(1)}, bf16[512,256]{1,0:T(8,128)(2,1)S(1)}, u32[]{:S(2)}, u32[]{:S(2)}) collective-permute-start(bf16[512,256]{1,0:T(8,128)(2,1)S(1)} %get-tuple-element.38), channel_id=1, source_target_pairs={{0,16},{8,24},{16,0},{24,8},{1,17},{9,25},{17,1},{25,9},{2,18},{10... | collective-permute-start | bytes 786440 | tf_op jit(solution)/shard_map/ppermute | solution.py:21
  5.3 8.0 %collective-permute-start.1 = (bf16[512,256]{1,0:T(8,128)(2,1)S(1)}, bf16[512,256]{1,0:T(8,128)(2,1)S(1)}, u32[]{:S(2)}, u32[]{:S(2)}) collective-permute-start(bf16[512,256]{1,0:T(8,128)(2,1)S(1)} %get-tuple-element.39), channel_id=1, source_target_pairs={{0,8},{8,0},{16,24},{24,16},{1,9},{9,1},{17,25},{25,17},{2,10},{10... | collective-permute-start | bytes 786440 | tf_op jit(solution)/shard_map/ppermute | solution.py:21
  13.3 2.5 %collective-permute-start.9 = (bf16[512,256]{1,0:T(8,128)(2,1)S(1)}, bf16[512,256]{1,0:T(8,128)(2,1)S(1)}, u32[]{:S(2)}, u32[]{:S(2)}) collective-permute-start(bf16[512,256]{1,0:T(8,128)(2,1)S(1)} %collective-permute-done.2.refs_3_), channel_id=1, source_target_pairs={{0,1},{1,0},{2,3},{3,2},{4,5},{5,4},{6,7},{7,6},{8,9},{9,8},{10,11... | collective-permute-start | bytes 786440 | tf_op jit(solution)/shard_map/ppermute | solution.py:21
  13.3 3.0 %collective-permute-start.8 = (bf16[512,256]{1,0:T(8,128)(2,1)S(1)}, bf16[512,256]{1,0:T(8,128)(2,1)S(1)}, u32[]{:S(2)}, u32[]{:S(2)}) collective-permute-start(bf16[512,256]{1,0:T(8,128)(2,1)S(1)} %collective-permute-done.1.refs_2_), channel_id=1, source_target_pairs={{0,1},{1,0},{2,3},{3,2},{4,5},{5,4},{6,7},{7,6},{8,9},{9,8},{10,11... | collective-permute-start | bytes 786440 | tf_op jit(solution)/shard_map/ppermute | solution.py:21
  13.8 15.0 %collective-permute-start.3 = (bf16[512,256]{1,0:T(8,128)(2,1)S(1)}, bf16[512,256]{1,0:T(8,128)(2,1)S(1)}, u32[]{:S(2)}, u32[]{:S(2)}) collective-permute-start(bf16[512,256]{1,0:T(8,128)(2,1)S(1)} %collective-permute-done.2.refs_3_), channel_id=1, source_target_pairs={{0,8},{8,0},{16,24},{24,16},{1,9},{9,1},{17,25},{25,17},{2,10},{10... | collective-permute-start | bytes 786440 | tf_op jit(solution)/shard_map/ppermute | solution.py:21
  15.3 13.6 %collective-permute-start.4 = (bf16[512,256]{1,0:T(8,128)(2,1)S(1)}, bf16[512,256]{1,0:T(8,128)(2,1)S(1)}, u32[]{:S(2)}, u32[]{:S(2)}) collective-permute-start(bf16[512,256]{1,0:T(8,128)(2,1)S(1)} %collective-permute-done.1.refs_2_), channel_id=1, source_target_pairs={{0,16},{8,24},{16,0},{24,8},{1,17},{9,25},{17,1},{25,9},{2,18},{10... | collective-permute-start | bytes 786440 | tf_op jit(solution)/shard_map/ppermute | solution.py:21
  15.8 11.8 %collective-permute-start.5 = (bf16[512,256]{1,0:T(8,128)(2,1)S(1)}, bf16[512,256]{1,0:T(8,128)(2,1)S(1)}, u32[]{:S(2)}, u32[]{:S(2)}) collective-permute-start(bf16[512,256]{1,0:T(8,128)(2,1)S(1)} %get-tuple-element.38), channel_id=1, source_target_pairs={{0,8},{8,0},{16,24},{24,16},{1,9},{9,1},{17,25},{25,17},{2,10},{10... | collective-permute-start | bytes 786440 | tf_op jit(solution)/shard_map/ppermute | solution.py:21
  16.3 12.5 %collective-permute-start.6 = (bf16[512,256]{1,0:T(8,128)(2,1)S(1)}, bf16[512,256]{1,0:T(8,128)(2,1)S(1)}, u32[]{:S(2)}, u32[]{:S(2)}) collective-permute-start(bf16[512,256]{1,0:T(8,128)(2,1)S(1)} %get-tuple-element.39), channel_id=1, source_target_pairs={{0,16},{8,24},{16,0},{24,8},{1,17},{9,25},{17,1},{25,9},{2,18},{10... | collective-permute-start | bytes 786440 | tf_op jit(solution)/shard_map/ppermute | solution.py:21
  17.9 1.0 copy-start
  18.9 2.2 %copy-start.1 = (bf16[2048,1024]{1,0:T(8,128)(2,1)S(1)}, bf16[2048,1024]{1,0:T(8,128)(2,1)}, u32[]{:S(2)}) copy-start(bf16[2048,1024]{1,0:T(8,128)(2,1)} %refs_0_.1) | copy-start | bytes 12582916
  28.9 1.5 %collective-permute-start.10 = (bf16[512,256]{1,0:T(8,128)(2,1)S(1)}, bf16[512,256]{1,0:T(8,128)(2,1)S(1)}, u32[]{:S(2)}, u32[]{:S(2)}) collective-permute-start(bf16[512,256]{1,0:T(8,128)(2,1)S(1)} %collective-permute-done.5.refs_1_), channel_id=1, source_target_pairs={{0,1},{1,0},{2,3},{3,2},{4,5},{5,4},{6,7},{7,6},{8,9},{9,8},{10,11... | collective-permute-start | bytes 786440 | tf_op jit(solution)/shard_map/ppermute | solution.py:21
  28.9 1.9 %collective-permute-start.11 = (bf16[512,256]{1,0:T(8,128)(2,1)S(1)}, bf16[512,256]{1,0:T(8,128)(2,1)S(1)}, u32[]{:S(2)}, u32[]{:S(2)}) collective-permute-start(bf16[512,256]{1,0:T(8,128)(2,1)S(1)} %collective-permute-done.6.refs_2_), channel_id=1, source_target_pairs={{0,1},{1,0},{2,3},{3,2},{4,5},{5,4},{6,7},{7,6},{8,9},{9,8},{10,11... | collective-permute-start | bytes 786440 | tf_op jit(solution)/shard_map/ppermute | solution.py:21
  29.4 1.8 %collective-permute-start.12 = (bf16[512,256]{1,0:T(8,128)(2,1)S(1)}, bf16[512,256]{1,0:T(8,128)(2,1)S(1)}, u32[]{:S(2)}, u32[]{:S(2)}) collective-permute-start(bf16[512,256]{1,0:T(8,128)(2,1)S(1)} %collective-permute-done.3.refs_3_), channel_id=1, source_target_pairs={{0,1},{1,0},{2,3},{3,2},{4,5},{5,4},{6,7},{7,6},{8,9},{9,8},{10,11... | collective-permute-start | bytes 786440 | tf_op jit(solution)/shard_map/ppermute | solution.py:21
  29.5 2.1 %collective-permute-start.13 = (bf16[512,256]{1,0:T(8,128)(2,1)S(1)}, bf16[512,256]{1,0:T(8,128)(2,1)S(1)}, u32[]{:S(2)}, u32[]{:S(2)}) collective-permute-start(bf16[512,256]{1,0:T(8,128)(2,1)S(1)} %collective-permute-done.4.refs_4_), channel_id=1, source_target_pairs={{0,1},{1,0},{2,3},{3,2},{4,5},{5,4},{6,7},{7,6},{8,9},{9,8},{10,11... | collective-permute-start | bytes 786440 | tf_op jit(solution)/shard_map/ppermute | solution.py:21
  36.9 5.8 %collective-permute-start.16 = (f32[16,128]{1,0:T(8,128)S(1)}, f32[16,128]{1,0:T(8,128)S(1)}, u32[]{:S(2)}, u32[]{:S(2)}) collective-permute-start(f32[16,128]{1,0:T(8,128)S(1)} %get-tuple-element.51.refs_1_), channel_id=1, source_target_pairs={{0,6},{1,7},{2,4},{3,5},{4,2},{5,3},{6,0},{7,1},{8,14},{9,15},{10,... | collective-permute-start | bytes 24584 | tf_op jit(solution)/shard_map/ppermute | solution.py:21
  41.2 4.5 %collective-permute-start.15 = (f32[16,128]{1,0:T(8,128)S(1)}, f32[16,128]{1,0:T(8,128)S(1)}, u32[]{:S(2)}, u32[]{:S(2)}) collective-permute-start(f32[16,128]{1,0:T(8,128)S(1)} %get-tuple-element.51.refs_1_), channel_id=1, source_target_pairs={{0,4},{1,5},{2,6},{3,7},{4,0},{5,1},{6,2},{7,3},{8,12},{9,13},{10,... | collective-permute-start | bytes 24584 | tf_op jit(solution)/shard_map/ppermute | solution.py:21
  41.2 4.5 %collective-permute-start.14 = (f32[16,128]{1,0:T(8,128)S(1)}, f32[16,128]{1,0:T(8,128)S(1)}, u32[]{:S(2)}, u32[]{:S(2)}) collective-permute-start(f32[16,128]{1,0:T(8,128)S(1)} %get-tuple-element.51.refs_1_), channel_id=1, source_target_pairs={{0,2},{1,3},{2,0},{3,1},{4,6},{5,7},{6,4},{7,5},{8,10},{9,11},{10,... | collective-permute-start | bytes 24584 | tf_op jit(solution)/shard_map/ppermute | solution.py:21
  47.5 5.1 %collective-permute-start.19 = (f32[16,128]{1,0:T(8,128)S(1)}, f32[16,128]{1,0:T(8,128)S(1)}, u32[]{:S(2)}, u32[]{:S(2)}) collective-permute-start(f32[16,128]{1,0:T(8,128)S(1)} %get-tuple-element.55.refs_4_), channel_id=1, source_target_pairs={{0,24},{8,16},{16,8},{24,0},{1,25},{9,17},{17,9},{25,1},{2,26},{10... | collective-permute-start | bytes 24584 | tf_op jit(solution)/shard_map/ppermute | solution.py:21
  50.9 3.7 %collective-permute-start.18 = (f32[16,128]{1,0:T(8,128)S(1)}, f32[16,128]{1,0:T(8,128)S(1)}, u32[]{:S(2)}, u32[]{:S(2)}) collective-permute-start(f32[16,128]{1,0:T(8,128)S(1)} %get-tuple-element.55.refs_4_), channel_id=1, source_target_pairs={{0,16},{8,24},{16,0},{24,8},{1,17},{9,25},{17,1},{25,9},{2,18},{10... | collective-permute-start | bytes 24584 | tf_op jit(solution)/shard_map/ppermute | solution.py:21
  51.0 3.7 %collective-permute-start.17 = (f32[16,128]{1,0:T(8,128)S(1)}, f32[16,128]{1,0:T(8,128)S(1)}, u32[]{:S(2)}, u32[]{:S(2)}) collective-permute-start(f32[16,128]{1,0:T(8,128)S(1)} %get-tuple-element.55.refs_4_), channel_id=1, source_target_pairs={{0,8},{8,0},{16,24},{24,16},{1,9},{9,1},{17,25},{25,17},{2,10},{10... | collective-permute-start | bytes 24584 | tf_op jit(solution)/shard_map/ppermute | solution.py:21
  57.0 5.5 %collective-permute-start.22 = (f32[16,128]{1,0:T(8,128)S(1)}, f32[16,128]{1,0:T(8,128)S(1)}, u32[]{:S(2)}, u32[]{:S(2)}) collective-permute-start(f32[16,128]{1,0:T(8,128)S(1)} %row_pass.2.refs_4_), channel_id=1, source_target_pairs={{0,6},{1,7},{2,4},{3,5},{4,2},{5,3},{6,0},{7,1},{8,14},{9,15},{10,... | collective-permute-start | bytes 24584 | tf_op jit(solution)/shard_map/ppermute | solution.py:21
  59.0 4.5 %collective-permute-start.21 = (f32[16,128]{1,0:T(8,128)S(1)}, f32[16,128]{1,0:T(8,128)S(1)}, u32[]{:S(2)}, u32[]{:S(2)}) collective-permute-start(f32[16,128]{1,0:T(8,128)S(1)} %row_pass.2.refs_4_), channel_id=1, source_target_pairs={{0,4},{1,5},{2,6},{3,7},{4,0},{5,1},{6,2},{7,3},{8,12},{9,13},{10,... | collective-permute-start | bytes 24584 | tf_op jit(solution)/shard_map/ppermute | solution.py:21
  59.4 4.1 %collective-permute-start.20 = (f32[16,128]{1,0:T(8,128)S(1)}, f32[16,128]{1,0:T(8,128)S(1)}, u32[]{:S(2)}, u32[]{:S(2)}) collective-permute-start(f32[16,128]{1,0:T(8,128)S(1)} %row_pass.2.refs_4_), channel_id=1, source_target_pairs={{0,2},{1,3},{2,0},{3,1},{4,6},{5,7},{6,4},{7,5},{8,10},{9,11},{10,... | collective-permute-start | bytes 24584 | tf_op jit(solution)/shard_map/ppermute | solution.py:21
  65.7 5.1 %collective-permute-start.25 = (f32[16,128]{1,0:T(8,128)S(1)}, f32[16,128]{1,0:T(8,128)S(1)}, u32[]{:S(2)}, u32[]{:S(2)}) collective-permute-start(f32[16,128]{1,0:T(8,128)S(1)} %get-tuple-element.56.refs_4_), channel_id=1, source_target_pairs={{0,24},{8,16},{16,8},{24,0},{1,25},{9,17},{17,9},{25,1},{2,26},{10... | collective-permute-start | bytes 24584 | tf_op jit(solution)/shard_map/ppermute | solution.py:21
  69.1 3.7 %collective-permute-start.24 = (f32[16,128]{1,0:T(8,128)S(1)}, f32[16,128]{1,0:T(8,128)S(1)}, u32[]{:S(2)}, u32[]{:S(2)}) collective-permute-start(f32[16,128]{1,0:T(8,128)S(1)} %get-tuple-element.56.refs_4_), channel_id=1, source_target_pairs={{0,16},{8,24},{16,0},{24,8},{1,17},{9,25},{17,1},{25,9},{2,18},{10... | collective-permute-start | bytes 24584 | tf_op jit(solution)/shard_map/ppermute | solution.py:21
  69.1 3.7 %collective-permute-start.23 = (f32[16,128]{1,0:T(8,128)S(1)}, f32[16,128]{1,0:T(8,128)S(1)}, u32[]{:S(2)}, u32[]{:S(2)}) collective-permute-start(f32[16,128]{1,0:T(8,128)S(1)} %get-tuple-element.56.refs_4_), channel_id=1, source_target_pairs={{0,8},{8,0},{16,24},{24,16},{1,9},{9,1},{17,25},{25,17},{2,10},{10... | collective-permute-start | bytes 24584 | tf_op jit(solution)/shard_map/ppermute | solution.py:21
  75.0 5.5 %collective-permute-start.28 = (f32[16,128]{1,0:T(8,128)S(1)}, f32[16,128]{1,0:T(8,128)S(1)}, u32[]{:S(2)}, u32[]{:S(2)}) collective-permute-start(f32[16,128]{1,0:T(8,128)S(1)} %row_pass.3.refs_4_), channel_id=1, source_target_pairs={{0,6},{1,7},{2,4},{3,5},{4,2},{5,3},{6,0},{7,1},{8,14},{9,15},{10,... | collective-permute-start | bytes 24584 | tf_op jit(solution)/shard_map/ppermute | solution.py:21
  77.5 4.5 %collective-permute-start.27 = (f32[16,128]{1,0:T(8,128)S(1)}, f32[16,128]{1,0:T(8,128)S(1)}, u32[]{:S(2)}, u32[]{:S(2)}) collective-permute-start(f32[16,128]{1,0:T(8,128)S(1)} %row_pass.3.refs_4_), channel_id=1, source_target_pairs={{0,4},{1,5},{2,6},{3,7},{4,0},{5,1},{6,2},{7,3},{8,12},{9,13},{10,... | collective-permute-start | bytes 24584 | tf_op jit(solution)/shard_map/ppermute | solution.py:21
  78.5 3.7 %collective-permute-start.26 = (f32[16,128]{1,0:T(8,128)S(1)}, f32[16,128]{1,0:T(8,128)S(1)}, u32[]{:S(2)}, u32[]{:S(2)}) collective-permute-start(f32[16,128]{1,0:T(8,128)S(1)} %row_pass.3.refs_4_), channel_id=1, source_target_pairs={{0,2},{1,3},{2,0},{3,1},{4,6},{5,7},{6,4},{7,5},{8,10},{9,11},{10,... | collective-permute-start | bytes 24584 | tf_op jit(solution)/shard_map/ppermute | solution.py:21
  84.3 4.8 %collective-permute-start.31 = (f32[16,128]{1,0:T(8,128)S(1)}, f32[16,128]{1,0:T(8,128)S(1)}, u32[]{:S(2)}, u32[]{:S(2)}) collective-permute-start(f32[16,128]{1,0:T(8,128)S(1)} %get-tuple-element.59.refs_3_), channel_id=1, source_target_pairs={{0,24},{8,16},{16,8},{24,0},{1,25},{9,17},{17,9},{25,1},{2,26},{10... | collective-permute-start | bytes 24584 | tf_op jit(solution)/shard_map/ppermute | solution.py:21
  87.5 3.7 %collective-permute-start.30 = (f32[16,128]{1,0:T(8,128)S(1)}, f32[16,128]{1,0:T(8,128)S(1)}, u32[]{:S(2)}, u32[]{:S(2)}) collective-permute-start(f32[16,128]{1,0:T(8,128)S(1)} %get-tuple-element.59.refs_3_), channel_id=1, source_target_pairs={{0,16},{8,24},{16,0},{24,8},{1,17},{9,25},{17,1},{25,9},{2,18},{10... | collective-permute-start | bytes 24584 | tf_op jit(solution)/shard_map/ppermute | solution.py:21
  87.5 3.7 %collective-permute-start.29 = (f32[16,128]{1,0:T(8,128)S(1)}, f32[16,128]{1,0:T(8,128)S(1)}, u32[]{:S(2)}, u32[]{:S(2)}) collective-permute-start(f32[16,128]{1,0:T(8,128)S(1)} %get-tuple-element.59.refs_3_), channel_id=1, source_target_pairs={{0,8},{8,0},{16,24},{24,16},{1,9},{9,1},{17,25},{25,17},{2,10},{10... | collective-permute-start | bytes 24584 | tf_op jit(solution)/shard_map/ppermute | solution.py:21
  94.3 15.9 %collective-permute-start.33 = (bf16[2048,128]{1,0:T(8,128)(2,1)S(1)}, bf16[2048,128]{1,0:T(8,128)(2,1)S(1)}, u32[]{:S(2)}, u32[]{:S(2)}) collective-permute-start(bf16[2048,128]{1,0:T(8,128)(2,1)S(1)} %get-tuple-element.64), channel_id=1, source_target_pairs={{0,2},{1,3},{2,0},{3,1},{4,6},{5,7},{6,4},{7,5},{8,10},{9,11},{10,... | collective-permute-start | bytes 1572872 | tf_op jit(solution)/shard_map/ppermute | solution.py:21
  98.8 18.8 %collective-permute-start.32 = (bf16[2048,128]{1,0:T(8,128)(2,1)S(1)}, bf16[2048,128]{1,0:T(8,128)(2,1)S(1)}, u32[]{:S(2)}, u32[]{:S(2)}) collective-permute-start(bf16[2048,128]{1,0:T(8,128)(2,1)S(1)} %get-tuple-element.62), channel_id=1, source_target_pairs={{0,2},{1,3},{2,0},{3,1},{4,6},{5,7},{6,4},{7,5},{8,10},{9,11},{10,... | collective-permute-start | bytes 1572872 | tf_op jit(solution)/shard_map/ppermute | solution.py:21
  110.3 15.8 %collective-permute-start.34 = (bf16[2048,128]{1,0:T(8,128)(2,1)S(1)}, bf16[2048,128]{1,0:T(8,128)(2,1)S(1)}, u32[]{:S(2)}, u32[]{:S(2)}) collective-permute-start(bf16[2048,128]{1,0:T(8,128)(2,1)S(1)} %add_convert_fusion.1), channel_id=1, source_target_pairs={{0,4},{1,5},{2,6},{3,7},{4,0},{5,1},{6,2},{7,3},{8,12},{9,13},{10,... | collective-permute-start | bytes 1572872 | tf_op jit(solution)/shard_map/ppermute | solution.py:21

commit v11 on v10

--- a/solution.py
+++ b/solution.py
@@ -27,8 +27,19 @@
     return terms[0]
 
 
+def butterfly(part, axis, unit, size):
+    distance = 1
+    while distance < size:
+        other = swap(part, axis, unit * distance)
+        if 2 * distance >= size:
+            return [part, other]
+        part = combine([part, other])
+        distance *= 2
+    return [part]
+
+
 def combine(parts):
-    peak = functools.reduce(jnp.maximum, parts)
+    peak = jnp.maximum(functools.reduce(jnp.maximum, parts), NEGATIVE)
     return peak + jnp.log(pair_sum([jnp.exp(part - peak) for part in parts]))
 
 
@@ -502,7 +513,7 @@
     return lax.optimization_barrier(arrays)
 
 
-def make_panel(table, lists, embeddings, shard, rows, features):
+def make_panel(table, mask, embeddings, shard, rows, features):
     width = shard.shape[1]
     protos = 2 * shard.shape[0]
     panel = pltpu.VMEM((table.dummy + 1, TILE, TILE), jnp.float32)
@@ -510,7 +521,7 @@
     row_shape = jax.ShapeDtypeStruct((table.row_tiles, TILE), jnp.float32)
     peaks = pltpu.VMEM((table.row_tiles, TILE, TILE), jnp.float32)
 
-    def late(places, add, e, pieces, before):
+    def late(lists, places, add, e, pieces, before):
         at = 2 + len(pieces)
         return pl.pallas_call(
             with_table(panel_kernel, table, places, add),
@@ -524,18 +535,21 @@
         )(lists, e, *pieces, *before)
 
     if lax.axis_size("row") != 4 or width % TILE:
+        lists = table.build(mask)
         every = lax.all_gather(shard, "row", axis=1, tiled=True)
         places = [Piece(True, 0, None), Piece(False, 0, None)]
-        return late(places, False, embeddings, [every, sibling(every)], [])
+        return (lists, *late(lists, places, False, embeddings, [every, sibling(every)], []))
     half = shard.shape[0] // 2
     top, bottom = shard[:half], shard[half:]
     near_bottom = swap(bottom, "row", 1)
     far_top = swap(top, "row", 2)
-    near_bottom, far_top, top, bottom, lists = tied(near_bottom, far_top, top, bottom, lists)
+    top, bottom, mask = tied(top, bottom, mask)
+    near_top = swap(top, "row", 1)
+    far_bottom = swap(bottom, "row", 2)
+    lists = table.build(mask)
+    near_bottom, far_top, lists = tied(near_bottom, far_top, lists)
     cross_top = swap(far_top, "row", 1)
     cross_bottom = swap(near_bottom, "row", 2)
-    near_top = swap(top, "row", 1)
-    far_bottom = swap(bottom, "row", 2)
     pieces = [shard, near_bottom, far_top]
     pieces += [sibling(piece) for piece in pieces]
     places = [Piece(own, *at) for own in (True, False) for at in ((0, 0), (half, 1), (0, 2))]
@@ -558,7 +572,7 @@
     pieces = [near_top, far_bottom, cross_top, cross_bottom]
     pieces += [sibling(piece) for piece in pieces]
     places = [Piece(own, *at) for own in (True, False) for at in ((0, 1), (half, 2), (0, 3), (half, 3))]
-    return late(places, True, e, pieces, [similar, known])
+    return (lists, *late(lists, places, True, e, pieces, [similar, known]))
 
 
 def scatter_partials(blocks):
@@ -584,12 +598,10 @@
 
     other_mask = swap(block_mask, "proto", 1)
     mask, other_mask = jnp.where(block_mask == 1, 1, 0), jnp.where(other_mask == 1, 1, 0)
-    lists = table.build(
-        jnp.where(
-            lax.axis_index("proto") % 2 == 0,
-            jnp.concatenate([mask, other_mask], axis=1),
-            jnp.concatenate([other_mask, mask], axis=1),
-        )
+    mask = jnp.where(
+        lax.axis_index("proto") % 2 == 0,
+        jnp.concatenate([mask, other_mask], axis=1),
+        jnp.concatenate([other_mask, mask], axis=1),
     )
 
     row_shape = jax.ShapeDtypeStruct((row_tiles, TILE), jnp.float32)
@@ -599,15 +611,13 @@
     wide = pltpu.VMEM((row_tiles, TILE, TILE), jnp.float32)
     tall = pltpu.VMEM((columns, TILE, TILE), jnp.float32)
     factors = pltpu.VMEM((columns + 8, TILE), jnp.float32)
-    similar, whole, row_part = make_panel(table, lists, embeddings, prototypes, rows, features)
+    lists, similar, whole, row_part = make_panel(table, mask, embeddings, prototypes, rows, features)
 
     def row_exchange(part):
-        others = [swap(part, "proto", 2 * j) for j in range(lines - 1, 0, -1)]
-        return [part] + others[::-1]
+        return butterfly(part, "proto", 2, lines)
 
     def column_exchange(part):
-        others = [swap(part, "row", j) for j in range(n_row - 1, 0, -1)]
-        return [part] + others[::-1]
+        return butterfly(part, "row", 1, n_row)
 
     parts = row_exchange(row_part)
     column_part, first_row, kept, peaks = pl.pallas_call(

time: 129 us -> 134 us (1.039)
  starting transfers between devices: 40.4 us -> 45.1 us
    ppermute x35 -> x29, starting transfers between devices: 40.4 us -> 45.1 us  [swap(): return lax.ppermute(x, axis, [(i, i ^ offset) for i in range(size)])]
    ppermute x35 -> x29, waiting for transfers between devices: 48.9 us -> 48.2 us  [swap(): return lax.ppermute(x, axis, [(i, i ^ offset) for i in range(size)])]
  transfers between devices with their start and end apart: 35 -> 29, of which waited for: 23 -> 23; matrix products, arithmetic and copies ran while one was open for 4% -> 4% of each run, Pallas kernels for 5% -> 5%
where the time goes in v11:
time: 134 us; the launch traced here: 132 us
  waiting for transfers between devices  48.2 us (36%)
  starting transfers between devices  45.1 us (34%)
  Pallas kernels  26.2 us (20%)
  local copies, waits for them, and re-layouts  5.43 us (4%)
  other arithmetic  4.5 us (3%)
  between operations  2.16 us (2%)
    ppermute x29, waiting for transfers between devices, swap(): return lax.ppermute(x, axis, [(i, i ^ offset) for i in range(size)])  48.2 us
    ppermute x29, starting transfers between devices, swap(): return lax.ppermute(x, axis, [(i, i ^ offset) for i in range(size)])  45.1 us
    pallas_call x1, Pallas kernels, late(): pl.pallas_call(with_table(panel_kernel, table, places, add), out_shape=(p...  5.39 us
    pallas_call x2, Pallas kernels, shards(): pl.pallas_call(with_table(row_kernel, table, log_column), out_shape=row_s...  4.67 us
    pallas_call x2, Pallas kernels, shards(): pl.pallas_call(with_table(column_kernel, table), out_shape=(column_shape,...  4.47 us
    pallas_call x1, Pallas kernels, shards(): pl.pallas_call(with_table(rest_kernel, table, lines), out_shape=[block] *...  3.35 us
    pallas_call x1, Pallas kernels, make_panel(): pl.pallas_call(with_table(early_panel_kernel, table, places), out_shape=(...  3.23 us
    unnamed x4, local copies, waits for them, and re-layouts  3.23 us
  transfers between devices with their start and end apart: 29, of which 23 were waited for; matrix products, arithmetic and copies ran while one was open for 4% of the time, Pallas kernels for 5%

profile of v11, /device:TPU:0, one launch (start us, length us, event | category | flops | bytes accessed | tf_op | source)
XLA Modules:
  0.0 131.6 jit_solution(6574865091349890928)
XLA Ops:
  1.2 1.1 fusion.5
  2.3 3.0 %collective-permute-start.1 = (bf16[512,256]{1,0:T(8,128)(2,1)S(1)}, bf16[512,256]{1,0:T(8,128)(2,1)S(1)}, u32[]{:S(2)}, u32[]{:S(2)}) collective-permute-start(bf16[512,256]{1,0:T(8,128)(2,1)S(1)} %get-tuple-element.40), channel_id=1, source_target_pairs={{0,16},{8,24},{16,0},{24,8},{1,17},{9,25},{17,1},{25,9},{2,18},{10... | collective-permute-start | bytes 786440 | tf_op jit(solution)/shard_map/ppermute | solution.py:21
  5.3 1.5 %collective-permute-start = (bf16[512,256]{1,0:T(8,128)(2,1)S(1)}, bf16[512,256]{1,0:T(8,128)(2,1)S(1)}, u32[]{:S(2)}, u32[]{:S(2)}) collective-permute-start(bf16[512,256]{1,0:T(8,128)(2,1)S(1)} %get-tuple-element.41), channel_id=1, source_target_pairs={{0,8},{8,0},{16,24},{24,16},{1,9},{9,1},{17,25},{25,17},{2,10},{10... | collective-permute-start | bytes 786440 | tf_op jit(solution)/shard_map/ppermute | solution.py:21
  13.8 1.5 %collective-permute-start.5 = (bf16[512,256]{1,0:T(8,128)(2,1)S(1)}, bf16[512,256]{1,0:T(8,128)(2,1)S(1)}, u32[]{:S(2)}, u32[]{:S(2)}) collective-permute-start(bf16[512,256]{1,0:T(8,128)(2,1)S(1)} %get-tuple-element.40), channel_id=1, source_target_pairs={{0,8},{8,0},{16,24},{24,16},{1,9},{9,1},{17,25},{25,17},{2,10},{10... | collective-permute-start | bytes 786440 | tf_op jit(solution)/shard_map/ppermute | solution.py:21
  16.3 1.5 %collective-permute-start.4 = (bf16[512,256]{1,0:T(8,128)(2,1)S(1)}, bf16[512,256]{1,0:T(8,128)(2,1)S(1)}, u32[]{:S(2)}, u32[]{:S(2)}) collective-permute-start(bf16[512,256]{1,0:T(8,128)(2,1)S(1)} %collective-permute-done.refs_2_), channel_id=1, source_target_pairs={{0,16},{8,24},{16,0},{24,8},{1,17},{9,25},{17,1},{25,9},{2,18},{10... | collective-permute-start | bytes 786440 | tf_op jit(solution)/shard_map/ppermute | solution.py:21
  17.9 1.0 copy-done
  18.9 2.2 %copy-done.1 = bf16[2048,1024]{1,0:T(8,128)(2,1)S(1)} copy-done((bf16[2048,1024]{1,0:T(8,128)(2,1)S(1)}, bf16[2048,1024]{1,0:T(8,128)(2,1)}, u32[]{:S(2)}) %copy-start.1) | copy-done | bytes 4194328
  21.1 3.2 %early_panel.1 = (f32[257,128,128]{2,1,0:T(8,128)S(1)}, bf16[2048,1024]{1,0:T(8,128)(2,1)S(1)}, bf16[2048,1024]{1,0:T(8,128)(2,1)S(1)}) custom-call(s32[1284]{0:T(1024)S(1)} %concatenate.11.hbm_ref, bf16[2048,1024]{1,0:T(8,128)(2,1)S(1)} %copy-done.1, bf16[1024,256]{1,0:T(8,128)(2,1)S(1)} %copy-done, bf16[512,256]{1,0:T(8,128)(2,1)S(1)} %collective-permute-done.refs_2_, ...), custom_call_target="tpu_custom_call" | custom-call | flops 4294967296 | bytes 33554432 | tf_op jit(solution)/shard_map/early_panel/pallas_call | solution.py:557
  24.5 3.1 %collective-permute-done.3.refs_3_ = bf16[512,256]{1,0:T(8,128)(2,1)S(1)} collective-permute-done((bf16[512,256]{1,0:T(8,128)(2,1)S(1)}, bf16[512,256]{1,0:T(8,128)(2,1)S(1)}, u32[]{:S(2)}, u32[]{:S(2)}) %collective-permute-start.3) | collective-permute-done | bytes 262176 | tf_op jit(solution)/shard_map/ppermute | solution.py:21
  27.7 1.2 collective-permute-done.4.refs_4_
  31.5 5.4 %panel.1 = (f32[257,128,128]{2,1,0:T(8,128)S(1)}, bf16[2048,1024]{1,0:T(8,128)(2,1)S(1)}, f32[16,128]{1,0:T(8,128)S(1)}) custom-call(s32[1284]{0:T(1024)S(1)} %concatenate.11.hbm_ref, bf16[2048,1024]{1,0:T(8,128)(2,1)S(1)} %get-tuple-element.45.refs_0_, ...), custom_call_target="tpu_custom_call", output_to_operand_aliasing={{0}: (10, {}), {1}: (11, {})} | custom-call | tf_op jit(solution)/shard_map/panel/pallas_call | solution.py:526
  36.9 2.3 %collective-permute-start.14 = (f32[16,128]{1,0:T(8,128)S(1)}, f32[16,128]{1,0:T(8,128)S(1)}, u32[]{:S(2)}, u32[]{:S(2)}) collective-permute-start(f32[16,128]{1,0:T(8,128)S(1)} %get-tuple-element.53), channel_id=1, source_target_pairs={{0,2},{1,3},{2,0},{3,1},{4,6},{5,7},{6,4},{7,5},{8,10},{9,11},{10,... | collective-permute-start | bytes 24584 | tf_op jit(solution)/shard_map/ppermute | solution.py:21
  39.2 1.6 %collective-permute-done.14 = f32[16,128]{1,0:T(8,128)S(1)} collective-permute-done((f32[16,128]{1,0:T(8,128)S(1)}, f32[16,128]{1,0:T(8,128)S(1)}, u32[]{:S(2)}, u32[]{:S(2)}) %collective-permute-start.14) | collective-permute-done | bytes 8224 | tf_op jit(solution)/shard_map/ppermute | solution.py:21
  40.8 2.6 %collective-permute-start.15 = (f32[16,128]{1,0:T(8,128)S(1)}, f32[16,128]{1,0:T(8,128)S(1)}, u32[]{:S(2)}, u32[]{:S(2)}) collective-permute-start(f32[16,128]{1,0:T(8,128)S(1)} %log_add_fusion.5.refs_1_), channel_id=1, source_target_pairs={{0,4},{1,5},{2,6},{3,7},{4,0},{5,1},{6,2},{7,3},{8,12},{9,13},{10,... | collective-permute-start | bytes 24584 | tf_op jit(solution)/shard_map/ppermute | solution.py:21
  43.4 2.0 %collective-permute-done.15.refs_2_ = f32[16,128]{1,0:T(8,128)S(1)} collective-permute-done((f32[16,128]{1,0:T(8,128)S(1)}, f32[16,128]{1,0:T(8,128)S(1)}, u32[]{:S(2)}, u32[]{:S(2)}) %collective-permute-start.15) | collective-permute-done | bytes 8224 | tf_op jit(solution)/shard_map/ppermute | solution.py:21
  45.5 1.9 %first_column_pass.1 = (f32[16,128]{1,0:T(8,128)S(1)}, f32[16,128]{1,0:T(8,128)S(1)}, bf16[257,128,128]{2,1,0:T(8,128)(2,1)S(1)}, f32[16,128]{1,0:T(8,128)S(1)}) custom-call(s32[1284]{0:T(1024)S(1)} %concatenate.11.hbm_ref, f32[257,128,128]{2,1,0:T(8,128)S(1)} %get-tuple-element.52.refs_0_, f32[16,128]{1,0:T(8,128)S(1)} %log_add_fusion.5.refs_1_, ...), custom_call_target="tpu_custom_call" | custom-call | tf_op jit(solution)/shard_map/first_column_pass/pallas_call | solution.py:623
  47.4 1.4 %collective-permute-start.16 = (f32[16,128]{1,0:T(8,128)S(1)}, f32[16,128]{1,0:T(8,128)S(1)}, u32[]{:S(2)}, u32[]{:S(2)}) collective-permute-start(f32[16,128]{1,0:T(8,128)S(1)} %get-tuple-element.57), channel_id=1, source_target_pairs={{0,8},{8,0},{16,24},{24,16},{1,9},{9,1},{17,25},{25,17},{2,10},{10... | collective-permute-start | bytes 24584 | tf_op jit(solution)/shard_map/ppermute | solution.py:21
  48.7 2.4 %collective-permute-done.16 = f32[16,128]{1,0:T(8,128)S(1)} collective-permute-done((f32[16,128]{1,0:T(8,128)S(1)}, f32[16,128]{1,0:T(8,128)S(1)}, u32[]{:S(2)}, u32[]{:S(2)}) %collective-permute-start.16) | collective-permute-done | bytes 8224 | tf_op jit(solution)/shard_map/ppermute | solution.py:21
  51.1 3.1 %collective-permute-start.17 = (f32[16,128]{1,0:T(8,128)S(1)}, f32[16,128]{1,0:T(8,128)S(1)}, u32[]{:S(2)}, u32[]{:S(2)}) collective-permute-start(f32[16,128]{1,0:T(8,128)S(1)} %log_add_fusion.4.refs_4_), channel_id=1, source_target_pairs={{0,16},{8,24},{16,0},{24,8},{1,17},{9,25},{17,1},{25,9},{2,18},{10... | collective-permute-start | bytes 24584 | tf_op jit(solution)/shard_map/ppermute | solution.py:21
  54.2 1.6 %collective-permute-done.17.refs_5_ = f32[16,128]{1,0:T(8,128)S(1)} collective-permute-done((f32[16,128]{1,0:T(8,128)S(1)}, f32[16,128]{1,0:T(8,128)S(1)}, u32[]{:S(2)}, u32[]{:S(2)}) %collective-permute-start.17) | collective-permute-done | bytes 8224 | tf_op jit(solution)/shard_map/ppermute | solution.py:21
  55.9 2.4 %row_pass.2 = f32[16,128]{1,0:T(8,128)S(1)} custom-call(s32[1284]{0:T(1024)S(1)} %concatenate.11.hbm_ref, f32[257,128,128]{2,1,0:T(8,128)S(1)} %get-tuple-element.52.refs_0_, bf16[257,128,128]{2,1,0:T(8,128)(2,1)S(1)} %get-tuple-element.54.refs_1_, f32[16,128]{1,0:T(8,128)S(1)} %get-tuple-element.55.refs_2_, f32[16,128]{1,0:T(8,128)S(1)} %get-tuple-element.56.refs_3_, ...), custom_call_target="tpu_custom_call" | custom-call | tf_op jit(solution)/shard_map/row_pass/pallas_call | solution.py:634
  58.3 2.4 %collective-permute-start.18 = (f32[16,128]{1,0:T(8,128)S(1)}, f32[16,128]{1,0:T(8,128)S(1)}, u32[]{:S(2)}, u32[]{:S(2)}) collective-permute-start(f32[16,128]{1,0:T(8,128)S(1)} %row_pass.2), channel_id=1, source_target_pairs={{0,2},{1,3},{2,0},{3,1},{4,6},{5,7},{6,4},{7,5},{8,10},{9,11},{10,... | collective-permute-start | bytes 24584 | tf_op jit(solution)/shard_map/ppermute | solution.py:21
  60.7 1.6 %collective-permute-done.18 = f32[16,128]{1,0:T(8,128)S(1)} collective-permute-done((f32[16,128]{1,0:T(8,128)S(1)}, f32[16,128]{1,0:T(8,128)S(1)}, u32[]{:S(2)}, u32[]{:S(2)}) %collective-permute-start.18) | collective-permute-done | bytes 8224 | tf_op jit(solution)/shard_map/ppermute | solution.py:21
  62.4 2.7 %collective-permute-start.19 = (f32[16,128]{1,0:T(8,128)S(1)}, f32[16,128]{1,0:T(8,128)S(1)}, u32[]{:S(2)}, u32[]{:S(2)}) collective-permute-start(f32[16,128]{1,0:T(8,128)S(1)} %log_add_fusion.3.refs_4_), channel_id=1, source_target_pairs={{0,4},{1,5},{2,6},{3,7},{4,0},{5,1},{6,2},{7,3},{8,12},{9,13},{10,... | collective-permute-start | bytes 24584 | tf_op jit(solution)/shard_map/ppermute | solution.py:21
  65.0 1.9 %collective-permute-done.19.refs_5_ = f32[16,128]{1,0:T(8,128)S(1)} collective-permute-done((f32[16,128]{1,0:T(8,128)S(1)}, f32[16,128]{1,0:T(8,128)S(1)}, u32[]{:S(2)}, u32[]{:S(2)}) %collective-permute-start.19) | collective-permute-done | bytes 8224 | tf_op jit(solution)/shard_map/ppermute | solution.py:21
  67.0 2.2 %column_pass.2 = (f32[16,128]{1,0:T(8,128)S(1)}, f32[16,128]{1,0:T(8,128)}, f32[16,128]{1,0:T(8,128)}) custom-call(s32[1284]{0:T(1024)S(1)} %concatenate.11.hbm_ref, f32[257,128,128]{2,1,0:T(8,128)S(1)} %get-tuple-element.52.refs_0_, bf16[257,128,128]{2,1,0:T(8,128)(2,1)S(1)} %get-tuple-element.54.refs_1_, f32[16,128]{1,0:T(8,128)S(1)} %get-tuple-element.55.refs_2_, ...), custom_call_target="tpu_custom_call" | custom-call | tf_op jit(solution)/shard_map/column_pass/pallas_call | solution.py:644
  69.2 2.2 %collective-permute-start.20 = (f32[16,128]{1,0:T(8,128)S(1)}, f32[16,128]{1,0:T(8,128)S(1)}, u32[]{:S(2)}, u32[]{:S(2)}) collective-permute-start(f32[16,128]{1,0:T(8,128)S(1)} %get-tuple-element.58), channel_id=1, source_target_pairs={{0,8},{8,0},{16,24},{24,16},{1,9},{9,1},{17,25},{25,17},{2,10},{10... | collective-permute-start | bytes 24584 | tf_op jit(solution)/shard_map/ppermute | solution.py:21
  71.4 1.6 %collective-permute-done.20 = f32[16,128]{1,0:T(8,128)S(1)} collective-permute-done((f32[16,128]{1,0:T(8,128)S(1)}, f32[16,128]{1,0:T(8,128)S(1)}, u32[]{:S(2)}, u32[]{:S(2)}) %collective-permute-start.20) | collective-permute-done | bytes 8224 | tf_op jit(solution)/shard_map/ppermute | solution.py:21
  73.0 2.6 %collective-permute-start.21 = (f32[16,128]{1,0:T(8,128)S(1)}, f32[16,128]{1,0:T(8,128)S(1)}, u32[]{:S(2)}, u32[]{:S(2)}) collective-permute-start(f32[16,128]{1,0:T(8,128)S(1)} %log_add_fusion.2.refs_4_), channel_id=1, source_target_pairs={{0,16},{8,24},{16,0},{24,8},{1,17},{9,25},{17,1},{25,9},{2,18},{10... | collective-permute-start | bytes 24584 | tf_op jit(solution)/shard_map/ppermute | solution.py:21
  75.6 1.6 %collective-permute-done.21.refs_5_ = f32[16,128]{1,0:T(8,128)S(1)} collective-permute-done((f32[16,128]{1,0:T(8,128)S(1)}, f32[16,128]{1,0:T(8,128)S(1)}, u32[]{:S(2)}, u32[]{:S(2)}) %collective-permute-start.21) | collective-permute-done | bytes 8224 | tf_op jit(solution)/shard_map/ppermute | solution.py:21
  77.2 2.3 %row_pass.3 = f32[16,128]{1,0:T(8,128)S(1)} custom-call(s32[1284]{0:T(1024)S(1)} %concatenate.11.hbm_ref, f32[257,128,128]{2,1,0:T(8,128)S(1)} %get-tuple-element.52.refs_0_, bf16[257,128,128]{2,1,0:T(8,128)(2,1)S(1)} %get-tuple-element.54.refs_1_, f32[16,128]{1,0:T(8,128)S(1)} %get-tuple-element.55.refs_2_, f32[16,128]{1,0:T(8,128)S(1)} %get-tuple-element.56.refs_3_, ...), custom_call_target="tpu_custom_call" | custom-call | tf_op jit(solution)/shard_map/row_pass/pallas_call | solution.py:634
  79.5 2.1 %collective-permute-start.22 = (f32[16,128]{1,0:T(8,128)S(1)}, f32[16,128]{1,0:T(8,128)S(1)}, u32[]{:S(2)}, u32[]{:S(2)}) collective-permute-start(f32[16,128]{1,0:T(8,128)S(1)} %row_pass.3), channel_id=1, source_target_pairs={{0,2},{1,3},{2,0},{3,1},{4,6},{5,7},{6,4},{7,5},{8,10},{9,11},{10,... | collective-permute-start | bytes 24584 | tf_op jit(solution)/shard_map/ppermute | solution.py:21
  81.6 1.6 %collective-permute-done.22 = f32[16,128]{1,0:T(8,128)S(1)} collective-permute-done((f32[16,128]{1,0:T(8,128)S(1)}, f32[16,128]{1,0:T(8,128)S(1)}, u32[]{:S(2)}, u32[]{:S(2)}) %collective-permute-start.22) | collective-permute-done | bytes 8224 | tf_op jit(solution)/shard_map/ppermute | solution.py:21
  83.3 2.9 %collective-permute-start.23 = (f32[16,128]{1,0:T(8,128)S(1)}, f32[16,128]{1,0:T(8,128)S(1)}, u32[]{:S(2)}, u32[]{:S(2)}) collective-permute-start(f32[16,128]{1,0:T(8,128)S(1)} %log_add_fusion.1.refs_4_), channel_id=1, source_target_pairs={{0,4},{1,5},{2,6},{3,7},{4,0},{5,1},{6,2},{7,3},{8,12},{9,13},{10,... | collective-permute-start | bytes 24584 | tf_op jit(solution)/shard_map/ppermute | solution.py:21
  86.2 1.7 %collective-permute-done.23.refs_5_ = f32[16,128]{1,0:T(8,128)S(1)} collective-permute-done((f32[16,128]{1,0:T(8,128)S(1)}, f32[16,128]{1,0:T(8,128)S(1)}, u32[]{:S(2)}, u32[]{:S(2)}) %collective-permute-start.23) | collective-permute-done | bytes 8224 | tf_op jit(solution)/shard_map/ppermute | solution.py:21
  87.9 2.2 %column_pass.3 = (f32[16,128]{1,0:T(8,128)S(1)}, f32[16,128]{1,0:T(8,128)S(1)}, f32[16,128]{1,0:T(8,128)}) custom-call(s32[1284]{0:T(1024)S(1)} %concatenate.11.hbm_ref, f32[257,128,128]{2,1,0:T(8,128)S(1)} %get-tuple-element.52.refs_0_, bf16[257,128,128]{2,1,0:T(8,128)(2,1)S(1)} %get-tuple-element.54.refs_1_, f32[16,128]{1,0:T(8,128)S(1)} %get-tuple-element.55.refs_2_, ...), custom_call_target="tpu_custom_call" | custom-call | tf_op jit(solution)/shard_map/column_pass/pallas_call | solution.py:644
  90.1 2.5 %collective-permute-start.24 = (f32[16,128]{1,0:T(8,128)S(1)}, f32[16,128]{1,0:T(8,128)S(1)}, u32[]{:S(2)}, u32[]{:S(2)}) collective-permute-start(f32[16,128]{1,0:T(8,128)S(1)} %get-tuple-element.61), channel_id=1, source_target_pairs={{0,8},{8,0},{16,24},{24,16},{1,9},{9,1},{17,25},{25,17},{2,10},{10... | collective-permute-start | bytes 24584 | tf_op jit(solution)/shard_map/ppermute | solution.py:21
  92.6 1.6 %collective-permute-done.24 = f32[16,128]{1,0:T(8,128)S(1)} collective-permute-done((f32[16,128]{1,0:T(8,128)S(1)}, f32[16,128]{1,0:T(8,128)S(1)}, u32[]{:S(2)}, u32[]{:S(2)}) %collective-permute-start.24) | collective-permute-done | bytes 8224 | tf_op jit(solution)/shard_map/ppermute | solution.py:21
  94.2 2.5 %collective-permute-start.25 = (f32[16,128]{1,0:T(8,128)S(1)}, f32[16,128]{1,0:T(8,128)S(1)}, u32[]{:S(2)}, u32[]{:S(2)}) collective-permute-start(f32[16,128]{1,0:T(8,128)S(1)} %log_add_fusion.refs_3_), channel_id=1, source_target_pairs={{0,16},{8,24},{16,0},{24,8},{1,17},{9,25},{17,1},{25,9},{2,18},{10... | collective-permute-start | bytes 24584 | tf_op jit(solution)/shard_map/ppermute | solution.py:21
  96.7 1.6 %collective-permute-done.25.refs_4_ = f32[16,128]{1,0:T(8,128)S(1)} collective-permute-done((f32[16,128]{1,0:T(8,128)S(1)}, f32[16,128]{1,0:T(8,128)S(1)}, u32[]{:S(2)}, u32[]{:S(2)}) %collective-permute-start.25) | collective-permute-done | bytes 8224 | tf_op jit(solution)/shard_map/ppermute | solution.py:21
  98.4 3.2 %plan.1 = (bf16[2048,128]{1,0:T(8,128)(2,1)S(1)}, bf16[33,512,256]{2,1,0:T(8,128)(2,1)S(1)}, f32[8,128]{1,0:T(8,128)}) custom-call(s32[1284]{0:T(1024)S(1)} %concatenate.11.hbm_ref, f32[257,128,128]{2,1,0:T(8,128)S(1)} %get-tuple-element.52.refs_0_, f32[16,128]{1,0:T(8,128)S(1)} %get-tuple-element.59.refs_1_, ...), custom_call_target="tpu_custom_call" | custom-call | tf_op jit(solution)/shard_map/plan/pallas_call | solution.py:660
  101.5 2.2 %collective-permute-start.27 = (bf16[2048,128]{1,0:T(8,128)(2,1)S(1)}, bf16[2048,128]{1,0:T(8,128)(2,1)S(1)}, u32[]{:S(2)}, u32[]{:S(2)}) collective-permute-start(bf16[2048,128]{1,0:T(8,128)(2,1)S(1)} %get-tuple-element.66), channel_id=1, source_target_pairs={{0,2},{1,3},{2,0},{3,1},{4,6},{5,7},{6,4},{7,5},{8,10},{9,11},{10,... | collective-permute-start | bytes 1572872 | tf_op jit(solution)/shard_map/ppermute | solution.py:21
  103.7 3.3 %rest_of_plan.1 = (bf16[2048,128]{1,0:T(8,128)(2,1)S(1)}, bf16[2048,128]{1,0:T(8,128)(2,1)S(1)}, bf16[2048,128]{1,0:T(8,128)(2,1)S(1)}) custom-call(s32[1284]{0:T(1024)S(1)} %concatenate.11.hbm_ref, bf16[33,512,256]{2,1,0:T(8,128)(2,1)S(1)} %get-tuple-element.62.refs_0_, bf16[2048,1024]{1,0:T(8,128)(2,1)S(1)} %get-tuple-element.60.refs_2_.refs_1_), custom_call_target="tpu_custom_call" | custom-call | flops 3221225472 | bytes 16777216 | tf_op jit(solution)/shard_map/rest_of_plan/pallas_call | solution.py:674
  107.6 7.0 %collective-permute-done.27 = bf16[2048,128]{1,0:T(8,128)(2,1)S(1)} collective-permute-done((bf16[2048,128]{1,0:T(8,128)(2,1)S(1)}, bf16[2048,128]{1,0:T(8,128)(2,1)S(1)}, u32[]{:S(2)}, u32[]{:S(2)}) %collective-permute-start.27) | collective-permute-done | bytes 524320 | tf_op jit(solution)/shard_map/ppermute | solution.py:21
  114.8 2.5 %collective-permute-start.28 = (bf16[2048,128]{1,0:T(8,128)(2,1)S(1)}, bf16[2048,128]{1,0:T(8,128)(2,1)S(1)}, u32[]{:S(2)}, u32[]{:S(2)}) collective-permute-start(bf16[2048,128]{1,0:T(8,128)(2,1)S(1)} %add_convert_fusion.1), channel_id=1, source_target_pairs={{0,4},{1,5},{2,6},{3,7},{4,0},{5,1},{6,2},{7,3},{8,12},{9,13},{10,... | collective-permute-start | bytes 1572872 | tf_op jit(solution)/shard_map/ppermute | solution.py:21
  117.3 5.8 %collective-permute-done.26 = bf16[2048,128]{1,0:T(8,128)(2,1)S(1)} collective-permute-done((bf16[2048,128]{1,0:T(8,128)(2,1)S(1)}, bf16[2048,128]{1,0:T(8,128)(2,1)S(1)}, u32[]{:S(2)}, u32[]{:S(2)}) %collective-permute-start.26) | collective-permute-done | bytes 524320 | tf_op jit(solution)/shard_map/ppermute | solution.py:21
  123.2 7.4 %collective-permute-done.28 = bf16[2048,128]{1,0:T(8,128)(2,1)S(1)} collective-permute-done((bf16[2048,128]{1,0:T(8,128)(2,1)S(1)}, bf16[2048,128]{1,0:T(8,128)(2,1)S(1)}, u32[]{:S(2)}, u32[]{:S(2)}) %collective-permute-start.28) | collective-permute-done | bytes 524320 | tf_op jit(solution)/shard_map/ppermute | solution.py:21
  130.6 1.0 add_convert_fusion
  (64 shorter events, 10.9 us)
Async XLA Ops:
  0.6 6.9 %collective-permute-start.2 = (s32[16,8]{0,1:T(8,128)}, s32[16,8]{0,1:T(8,128)S(1)}, u32[]{:S(2)}, u32[]{:S(2)}) collective-permute-start(s32[16,8]{0,1:T(8,128)} %param.5), channel_id=1, source_target_pairs={{0,1},{1,0},{2,3},{3,2},{4,5},{5,4},{6,7},{7,6},{8,9},{9,8},{10,11... | collective-permute-start | bytes 1544 | tf_op jit(solution)/shard_map/ppermute | solution.py:21
  1.1 16.7 %collective-permute-start.7 = (bf16[1024,256]{1,0:T(8,128)(2,1)}, bf16[1024,256]{1,0:T(8,128)(2,1)S(1)}, u32[]{:S(2)}, u32[]{:S(2)}) collective-permute-start(bf16[1024,256]{1,0:T(8,128)(2,1)} %refs_1_.1), channel_id=1, source_target_pairs={{0,1},{1,0},{2,3},{3,2},{4,5},{5,4},{6,7},{7,6},{8,9},{9,8},{10,11... | collective-permute-start | bytes 1572872 | tf_op jit(solution)/shard_map/ppermute | solution.py:21
  2.3 10.3 %collective-permute-start.1 = (bf16[512,256]{1,0:T(8,128)(2,1)S(1)}, bf16[512,256]{1,0:T(8,128)(2,1)S(1)}, u32[]{:S(2)}, u32[]{:S(2)}) collective-permute-start(bf16[512,256]{1,0:T(8,128)(2,1)S(1)} %get-tuple-element.40), channel_id=1, source_target_pairs={{0,16},{8,24},{16,0},{24,8},{1,17},{9,25},{17,1},{25,9},{2,18},{10... | collective-permute-start | bytes 786440 | tf_op jit(solution)/shard_map/ppermute | solution.py:21
  5.3 8.0 %collective-permute-start = (bf16[512,256]{1,0:T(8,128)(2,1)S(1)}, bf16[512,256]{1,0:T(8,128)(2,1)S(1)}, u32[]{:S(2)}, u32[]{:S(2)}) collective-permute-start(bf16[512,256]{1,0:T(8,128)(2,1)S(1)} %get-tuple-element.41), channel_id=1, source_target_pairs={{0,8},{8,0},{16,24},{24,16},{1,9},{9,1},{17,25},{25,17},{2,10},{10... | collective-permute-start | bytes 786440 | tf_op jit(solution)/shard_map/ppermute | solution.py:21
  13.3 2.5 %collective-permute-start.9 = (bf16[512,256]{1,0:T(8,128)(2,1)S(1)}, bf16[512,256]{1,0:T(8,128)(2,1)S(1)}, u32[]{:S(2)}, u32[]{:S(2)}) collective-permute-start(bf16[512,256]{1,0:T(8,128)(2,1)S(1)} %collective-permute-done.1.refs_3_), channel_id=1, source_target_pairs={{0,1},{1,0},{2,3},{3,2},{4,5},{5,4},{6,7},{7,6},{8,9},{9,8},{10,11... | collective-permute-start | bytes 786440 | tf_op jit(solution)/shard_map/ppermute | solution.py:21
  13.3 3.0 %collective-permute-start.8 = (bf16[512,256]{1,0:T(8,128)(2,1)S(1)}, bf16[512,256]{1,0:T(8,128)(2,1)S(1)}, u32[]{:S(2)}, u32[]{:S(2)}) collective-permute-start(bf16[512,256]{1,0:T(8,128)(2,1)S(1)} %collective-permute-done.refs_2_), channel_id=1, source_target_pairs={{0,1},{1,0},{2,3},{3,2},{4,5},{5,4},{6,7},{7,6},{8,9},{9,8},{10,11... | collective-permute-start | bytes 786440 | tf_op jit(solution)/shard_map/ppermute | solution.py:21
  13.8 10.5 %collective-permute-start.5 = (bf16[512,256]{1,0:T(8,128)(2,1)S(1)}, bf16[512,256]{1,0:T(8,128)(2,1)S(1)}, u32[]{:S(2)}, u32[]{:S(2)}) collective-permute-start(bf16[512,256]{1,0:T(8,128)(2,1)S(1)} %get-tuple-element.40), channel_id=1, source_target_pairs={{0,8},{8,0},{16,24},{24,16},{1,9},{9,1},{17,25},{25,17},{2,10},{10... | collective-permute-start | bytes 786440 | tf_op jit(solution)/shard_map/ppermute | solution.py:21
  15.3 9.2 %collective-permute-start.6 = (bf16[512,256]{1,0:T(8,128)(2,1)S(1)}, bf16[512,256]{1,0:T(8,128)(2,1)S(1)}, u32[]{:S(2)}, u32[]{:S(2)}) collective-permute-start(bf16[512,256]{1,0:T(8,128)(2,1)S(1)} %get-tuple-element.41), channel_id=1, source_target_pairs={{0,16},{8,24},{16,0},{24,8},{1,17},{9,25},{17,1},{25,9},{2,18},{10... | collective-permute-start | bytes 786440 | tf_op jit(solution)/shard_map/ppermute | solution.py:21
  15.8 11.8 %collective-permute-start.3 = (bf16[512,256]{1,0:T(8,128)(2,1)S(1)}, bf16[512,256]{1,0:T(8,128)(2,1)S(1)}, u32[]{:S(2)}, u32[]{:S(2)}) collective-permute-start(bf16[512,256]{1,0:T(8,128)(2,1)S(1)} %collective-permute-done.1.refs_3_), channel_id=1, source_target_pairs={{0,8},{8,0},{16,24},{24,16},{1,9},{9,1},{17,25},{25,17},{2,10},{10... | collective-permute-start | bytes 786440 | tf_op jit(solution)/shard_map/ppermute | solution.py:21
  16.3 12.5 %collective-permute-start.4 = (bf16[512,256]{1,0:T(8,128)(2,1)S(1)}, bf16[512,256]{1,0:T(8,128)(2,1)S(1)}, u32[]{:S(2)}, u32[]{:S(2)}) collective-permute-start(bf16[512,256]{1,0:T(8,128)(2,1)S(1)} %collective-permute-done.refs_2_), channel_id=1, source_target_pairs={{0,16},{8,24},{16,0},{24,8},{1,17},{9,25},{17,1},{25,9},{2,18},{10... | collective-permute-start | bytes 786440 | tf_op jit(solution)/shard_map/ppermute | solution.py:21
  17.9 1.0 copy-start
  18.9 2.2 %copy-start.1 = (bf16[2048,1024]{1,0:T(8,128)(2,1)S(1)}, bf16[2048,1024]{1,0:T(8,128)(2,1)}, u32[]{:S(2)}) copy-start(bf16[2048,1024]{1,0:T(8,128)(2,1)} %refs_0_.1) | copy-start | bytes 12582916
  28.9 1.5 %collective-permute-start.10 = (bf16[512,256]{1,0:T(8,128)(2,1)S(1)}, bf16[512,256]{1,0:T(8,128)(2,1)S(1)}, u32[]{:S(2)}, u32[]{:S(2)}) collective-permute-start(bf16[512,256]{1,0:T(8,128)(2,1)S(1)} %collective-permute-done.5.refs_1_), channel_id=1, source_target_pairs={{0,1},{1,0},{2,3},{3,2},{4,5},{5,4},{6,7},{7,6},{8,9},{9,8},{10,11... | collective-permute-start | bytes 786440 | tf_op jit(solution)/shard_map/ppermute | solution.py:21
  28.9 1.9 %collective-permute-start.11 = (bf16[512,256]{1,0:T(8,128)(2,1)S(1)}, bf16[512,256]{1,0:T(8,128)(2,1)S(1)}, u32[]{:S(2)}, u32[]{:S(2)}) collective-permute-start(bf16[512,256]{1,0:T(8,128)(2,1)S(1)} %collective-permute-done.6.refs_2_), channel_id=1, source_target_pairs={{0,1},{1,0},{2,3},{3,2},{4,5},{5,4},{6,7},{7,6},{8,9},{9,8},{10,11... | collective-permute-start | bytes 786440 | tf_op jit(solution)/shard_map/ppermute | solution.py:21
  29.4 1.8 %collective-permute-start.12 = (bf16[512,256]{1,0:T(8,128)(2,1)S(1)}, bf16[512,256]{1,0:T(8,128)(2,1)S(1)}, u32[]{:S(2)}, u32[]{:S(2)}) collective-permute-start(bf16[512,256]{1,0:T(8,128)(2,1)S(1)} %collective-permute-done.3.refs_3_), channel_id=1, source_target_pairs={{0,1},{1,0},{2,3},{3,2},{4,5},{5,4},{6,7},{7,6},{8,9},{9,8},{10,11... | collective-permute-start | bytes 786440 | tf_op jit(solution)/shard_map/ppermute | solution.py:21
  29.4 2.1 %collective-permute-start.13 = (bf16[512,256]{1,0:T(8,128)(2,1)S(1)}, bf16[512,256]{1,0:T(8,128)(2,1)S(1)}, u32[]{:S(2)}, u32[]{:S(2)}) collective-permute-start(bf16[512,256]{1,0:T(8,128)(2,1)S(1)} %collective-permute-done.4.refs_4_), channel_id=1, source_target_pairs={{0,1},{1,0},{2,3},{3,2},{4,5},{5,4},{6,7},{7,6},{8,9},{9,8},{10,11... | collective-permute-start | bytes 786440 | tf_op jit(solution)/shard_map/ppermute | solution.py:21
  36.9 3.9 %collective-permute-start.14 = (f32[16,128]{1,0:T(8,128)S(1)}, f32[16,128]{1,0:T(8,128)S(1)}, u32[]{:S(2)}, u32[]{:S(2)}) collective-permute-start(f32[16,128]{1,0:T(8,128)S(1)} %get-tuple-element.53), channel_id=1, source_target_pairs={{0,2},{1,3},{2,0},{3,1},{4,6},{5,7},{6,4},{7,5},{8,10},{9,11},{10,... | collective-permute-start | bytes 24584 | tf_op jit(solution)/shard_map/ppermute | solution.py:21
  40.8 4.6 %collective-permute-start.15 = (f32[16,128]{1,0:T(8,128)S(1)}, f32[16,128]{1,0:T(8,128)S(1)}, u32[]{:S(2)}, u32[]{:S(2)}) collective-permute-start(f32[16,128]{1,0:T(8,128)S(1)} %log_add_fusion.5.refs_1_), channel_id=1, source_target_pairs={{0,4},{1,5},{2,6},{3,7},{4,0},{5,1},{6,2},{7,3},{8,12},{9,13},{10,... | collective-permute-start | bytes 24584 | tf_op jit(solution)/shard_map/ppermute | solution.py:21
  47.4 3.7 %collective-permute-start.16 = (f32[16,128]{1,0:T(8,128)S(1)}, f32[16,128]{1,0:T(8,128)S(1)}, u32[]{:S(2)}, u32[]{:S(2)}) collective-permute-start(f32[16,128]{1,0:T(8,128)S(1)} %get-tuple-element.57), channel_id=1, source_target_pairs={{0,8},{8,0},{16,24},{24,16},{1,9},{9,1},{17,25},{25,17},{2,10},{10... | collective-permute-start | bytes 24584 | tf_op jit(solution)/shard_map/ppermute | solution.py:21
  51.1 4.8 %collective-permute-start.17 = (f32[16,128]{1,0:T(8,128)S(1)}, f32[16,128]{1,0:T(8,128)S(1)}, u32[]{:S(2)}, u32[]{:S(2)}) collective-permute-start(f32[16,128]{1,0:T(8,128)S(1)} %log_add_fusion.4.refs_4_), channel_id=1, source_target_pairs={{0,16},{8,24},{16,0},{24,8},{1,17},{9,25},{17,1},{25,9},{2,18},{10... | collective-permute-start | bytes 24584 | tf_op jit(solution)/shard_map/ppermute | solution.py:21
  58.3 4.0 %collective-permute-start.18 = (f32[16,128]{1,0:T(8,128)S(1)}, f32[16,128]{1,0:T(8,128)S(1)}, u32[]{:S(2)}, u32[]{:S(2)}) collective-permute-start(f32[16,128]{1,0:T(8,128)S(1)} %row_pass.2), channel_id=1, source_target_pairs={{0,2},{1,3},{2,0},{3,1},{4,6},{5,7},{6,4},{7,5},{8,10},{9,11},{10,... | collective-permute-start | bytes 24584 | tf_op jit(solution)/shard_map/ppermute | solution.py:21
  62.4 4.6 %collective-permute-start.19 = (f32[16,128]{1,0:T(8,128)S(1)}, f32[16,128]{1,0:T(8,128)S(1)}, u32[]{:S(2)}, u32[]{:S(2)}) collective-permute-start(f32[16,128]{1,0:T(8,128)S(1)} %log_add_fusion.3.refs_4_), channel_id=1, source_target_pairs={{0,4},{1,5},{2,6},{3,7},{4,0},{5,1},{6,2},{7,3},{8,12},{9,13},{10,... | collective-permute-start | bytes 24584 | tf_op jit(solution)/shard_map/ppermute | solution.py:21
  69.2 3.8 %collective-permute-start.20 = (f32[16,128]{1,0:T(8,128)S(1)}, f32[16,128]{1,0:T(8,128)S(1)}, u32[]{:S(2)}, u32[]{:S(2)}) collective-permute-start(f32[16,128]{1,0:T(8,128)S(1)} %get-tuple-element.58), channel_id=1, source_target_pairs={{0,8},{8,0},{16,24},{24,16},{1,9},{9,1},{17,25},{25,17},{2,10},{10... | collective-permute-start | bytes 24584 | tf_op jit(solution)/shard_map/ppermute | solution.py:21
  73.0 4.2 %collective-permute-start.21 = (f32[16,128]{1,0:T(8,128)S(1)}, f32[16,128]{1,0:T(8,128)S(1)}, u32[]{:S(2)}, u32[]{:S(2)}) collective-permute-start(f32[16,128]{1,0:T(8,128)S(1)} %log_add_fusion.2.refs_4_), channel_id=1, source_target_pairs={{0,16},{8,24},{16,0},{24,8},{1,17},{9,25},{17,1},{25,9},{2,18},{10... | collective-permute-start | bytes 24584 | tf_op jit(solution)/shard_map/ppermute | solution.py:21
  79.5 3.8 %collective-permute-start.22 = (f32[16,128]{1,0:T(8,128)S(1)}, f32[16,128]{1,0:T(8,128)S(1)}, u32[]{:S(2)}, u32[]{:S(2)}) collective-permute-start(f32[16,128]{1,0:T(8,128)S(1)} %row_pass.3), channel_id=1, source_target_pairs={{0,2},{1,3},{2,0},{3,1},{4,6},{5,7},{6,4},{7,5},{8,10},{9,11},{10,... | collective-permute-start | bytes 24584 | tf_op jit(solution)/shard_map/ppermute | solution.py:21
  83.3 4.6 %collective-permute-start.23 = (f32[16,128]{1,0:T(8,128)S(1)}, f32[16,128]{1,0:T(8,128)S(1)}, u32[]{:S(2)}, u32[]{:S(2)}) collective-permute-start(f32[16,128]{1,0:T(8,128)S(1)} %log_add_fusion.1.refs_4_), channel_id=1, source_target_pairs={{0,4},{1,5},{2,6},{3,7},{4,0},{5,1},{6,2},{7,3},{8,12},{9,13},{10,... | collective-permute-start | bytes 24584 | tf_op jit(solution)/shard_map/ppermute | solution.py:21
  90.1 4.1 %collective-permute-start.24 = (f32[16,128]{1,0:T(8,128)S(1)}, f32[16,128]{1,0:T(8,128)S(1)}, u32[]{:S(2)}, u32[]{:S(2)}) collective-permute-start(f32[16,128]{1,0:T(8,128)S(1)} %get-tuple-element.61), channel_id=1, source_target_pairs={{0,8},{8,0},{16,24},{24,16},{1,9},{9,1},{17,25},{25,17},{2,10},{10... | collective-permute-start | bytes 24584 | tf_op jit(solution)/shard_map/ppermute | solution.py:21
  94.2 4.1 %collective-permute-start.25 = (f32[16,128]{1,0:T(8,128)S(1)}, f32[16,128]{1,0:T(8,128)S(1)}, u32[]{:S(2)}, u32[]{:S(2)}) collective-permute-start(f32[16,128]{1,0:T(8,128)S(1)} %log_add_fusion.refs_3_), channel_id=1, source_target_pairs={{0,16},{8,24},{16,0},{24,8},{1,17},{9,25},{17,1},{25,9},{2,18},{10... | collective-permute-start | bytes 24584 | tf_op jit(solution)/shard_map/ppermute | solution.py:21
  101.5 13.1 %collective-permute-start.27 = (bf16[2048,128]{1,0:T(8,128)(2,1)S(1)}, bf16[2048,128]{1,0:T(8,128)(2,1)S(1)}, u32[]{:S(2)}, u32[]{:S(2)}) collective-permute-start(bf16[2048,128]{1,0:T(8,128)(2,1)S(1)} %get-tuple-element.66), channel_id=1, source_target_pairs={{0,2},{1,3},{2,0},{3,1},{4,6},{5,7},{6,4},{7,5},{8,10},{9,11},{10,... | collective-permute-start | bytes 1572872 | tf_op jit(solution)/shard_map/ppermute | solution.py:21
  107.1 16.1 %collective-permute-start.26 = (bf16[2048,128]{1,0:T(8,128)(2,1)S(1)}, bf16[2048,128]{1,0:T(8,128)(2,1)S(1)}, u32[]{:S(2)}, u32[]{:S(2)}) collective-permute-start(bf16[2048,128]{1,0:T(8,128)(2,1)S(1)} %get-tuple-element.64), channel_id=1, source_target_pairs={{0,2},{1,3},{2,0},{3,1},{4,6},{5,7},{6,4},{7,5},{8,10},{9,11},{10,... | collective-permute-start | bytes 1572872 | tf_op jit(solution)/shard_map/ppermute | solution.py:21
  114.8 15.8 %collective-permute-start.28 = (bf16[2048,128]{1,0:T(8,128)(2,1)S(1)}, bf16[2048,128]{1,0:T(8,128)(2,1)S(1)}, u32[]{:S(2)}, u32[]{:S(2)}) collective-permute-start(bf16[2048,128]{1,0:T(8,128)(2,1)S(1)} %add_convert_fusion.1), channel_id=1, source_target_pairs={{0,4},{1,5},{2,6},{3,7},{4,0},{5,1},{6,2},{7,3},{8,12},{9,13},{10,... | collective-permute-start | bytes 1572872 | tf_op jit(solution)/shard_map/ppermute | solution.py:21

commit v12 on v10

--- a/solution.py
+++ b/solution.py
@@ -108,6 +108,23 @@
 
         return lax.fori_loop(0, self.steps(ref, line, unroll), several, start)
 
+    def sums(self, ref, base, acc_ref, visit):
+        lists = range(acc_ref.shape[0])
+
+        def four(i, k):
+            tiles = [visit(i, self.entry(ref, base + i, 4 * k + n)) for n in range(4)]
+            return (tiles[0] + tiles[1]) + (tiles[2] + tiles[3])
+
+        for i in lists:
+            acc_ref[i] = four(i, 0)
+        for i in lists:
+
+            @pl.when(self.steps(ref, base + i, 4) > 1)
+            def _(i=i):
+                acc_ref[i] = lax.fori_loop(
+                    1, self.steps(ref, base + i, 4), lambda k, a: a + four(i, k), acc_ref[i]
+                )
+
     def place(self, t, u):
         padding = (t == self.row_tiles) | (u == self.columns)
         return jnp.where(padding, self.dummy, t * self.columns + u)
@@ -144,6 +161,11 @@
     bad = jnp.max(jnp.where(good, 0.0, 1.0), axis=1, keepdims=True)
     bit = jnp.left_shift(1, lax.broadcasted_iota(jnp.int32, bad.shape, 0))
     return jnp.sum(bad * bit.astype(jnp.float32)).astype(jnp.int32)
+
+
+def in_range(totals, factor):
+    largest = jnp.max(jnp.max(factor, axis=1, keepdims=True), axis=0, keepdims=True)
+    return (totals > 1e-15) & (totals < 1e30) & (largest < 1e15)
 
 
 def has_bit(bits, i):
@@ -229,21 +251,17 @@
     return features
 
 
-def early_panel_kernel(table, places, arrived, e_hbm_ref, *refs):
-    pieces, (s_ref, p_ref, e_ref, sem) = refs[:-4], refs[-4:]
-    load = pltpu.make_async_copy(e_hbm_ref, e_ref, sem)
-    load.start()
+def early_panel_kernel(table, places, arrived, e_ref, *refs):
+    pieces, (s_ref, p_ref) = refs[:-2], refs[-2:]
     for place, piece in zip(places, pieces):
         place.copy_to(p_ref, piece)
     s_ref[table.dummy] = lowest()
-    table_ref = arrived()
-    load.wait()
     features = quarters([(0, 0), (2, 1)], p_ref, table.columns)
-    score_pairs(table, table_ref, e_ref, p_ref, s_ref, features, False, None)
+    score_pairs(table, arrived(), e_ref, p_ref, s_ref, features, False, None)
 
 
 def panel_kernel(table, places, add, arrived, e_ref, *refs):
-    pieces, (s_ref, p_ref, out_ref, acc_ref) = refs[:-4], refs[-4:]
+    pieces, (s_ref, p_ref, w_ref, first_ref, out_ref, acc_ref, wide_ref) = refs[:-7], refs[-7:]
     if add:
         pieces = pieces[:-2]
     row_tiles = table.row_tiles
@@ -272,38 +290,40 @@
     for t in range(row_tiles):
         peak = jnp.max(acc_ref[t], axis=1, keepdims=True)
         peaks = jnp.where(lane == t, peak, peaks)
-        acc_ref[t] = jnp.broadcast_to(peak, (TILE, TILE))
-    for t in range(row_tiles):
-        acc_ref[t] = table.loop(
-            table_ref,
-            t,
-            4,
-            lambda u, a, t=t: a + jnp.exp(s_ref[table.place(t, u)] - acc_ref[t]),
-            blank(),
-        )
-    out_ref[...] = peaks.T[:row_tiles] + jnp.log(lying([acc_ref[t] for t in range(row_tiles)]))
-
-
-def row_kernel(table, log_column, arrived, s_ref, w_ref, m_ref, r_ref, *refs):
+        wide_ref[t] = jnp.broadcast_to(peak, (TILE, TILE))
+    w_ref[table.dummy] = blank().astype(jnp.bfloat16)
+
+    def visit(t, u):
+        at = table.place(t, u)
+        value = jnp.exp(s_ref[at] - wide_ref[t])
+        w_ref[at] = value.astype(jnp.bfloat16)
+        return value
+
+    table.sums(table_ref, 0, acc_ref, visit)
+    peaks = peaks.T[:row_tiles]
+    first_ref[...] = -peaks
+    out_ref[...] = peaks + jnp.log(lying([acc_ref[t] for t in range(row_tiles)]))
+
+
+def row_kernel(table, log_column, arrived, s_ref, w_ref, first_ref, *refs):
     parts, (out_ref, c_ref, v_ref, acc_ref) = refs[:-4], refs[-4:]
     row_tiles, columns = table.row_tiles, table.columns
     column = log_column - combine([part[...] for part in parts])
+    factor = jnp.exp(column)
     c_ref[:columns] = column
-    v_ref[:columns] = jnp.exp(column + m_ref[...])
+    v_ref[:columns] = factor
     rest = jnp.zeros((c_ref.shape[0] - columns, TILE), jnp.float32)
     c_ref[columns:] = rest
     v_ref[columns:] = rest
     table_ref = arrived()
 
-    for t in range(row_tiles):
-
-        def one_tile(u, a, t=t):
-            return a + w_ref[table.place(t, u)].astype(jnp.float32) * v_ref[pl.ds(u, 1), :]
-
-        acc_ref[t] = table.loop(table_ref, t, 4, one_tile, blank())
+    def visit(t, u):
+        return w_ref[table.place(t, u)].astype(jnp.float32) * v_ref[pl.ds(u, 1), :]
+
+    table.sums(table_ref, 0, acc_ref, visit)
     totals = lying([acc_ref[t] for t in range(row_tiles)])
-    out_ref[...] = jnp.log(totals) - r_ref[...]
-    bits = bad_bits(totals > 1e-15) - table.empty_bits(table_ref, 0, row_tiles)
+    out_ref[...] = jnp.log(totals) - first_ref[...]
+    bits = bad_bits(in_range(totals, factor)) - table.empty_bits(table_ref, 0, row_tiles)
 
     @pl.when(bits != 0)
     def _():
@@ -321,65 +341,7 @@
                 out_ref[t : t + 1, :] = jnp.broadcast_to(found, (TILE, TILE)).T[:1]
 
 
-def slow_column(table, table_ref, u, s_ref, wide_ref, keep):
-    line = table.column_base + u
-
-    def score(t):
-        at = table.place(t, u)
-        return at, s_ref[at] + wide_ref[jnp.minimum(t, table.row_tiles - 1)]
-
-    peak = table.loop(table_ref, line, 2, lambda t, a: jnp.maximum(a, score(t)[1]), lowest())
-    peak = jnp.max(peak, axis=0, keepdims=True)
-
-    def one_tile(t, a):
-        at, value = score(t)
-        value = jnp.exp(value - peak)
-        keep(at, value)
-        return a + value
-
-    total = table.loop(table_ref, line, 2, one_tile, blank())
-    return peak, jnp.sum(total, axis=0, keepdims=True)
-
-
-def first_column_kernel(table, arrived, s_ref, *refs):
-    parts, (out_ref, r_ref, w_ref, m_ref, wide_ref, acc_ref) = refs[:-6], refs[-6:]
-    row = -combine([part[...] for part in parts])
-    r_ref[...] = row
-    spread_rows(row, wide_ref)
-    w_ref[table.dummy] = blank().astype(jnp.bfloat16)
-    table_ref = arrived()
-
-    def keep(at, value):
-        w_ref[at] = value.astype(jnp.bfloat16)
-
-    for u in range(table.columns):
-
-        def one_tile(t, a, u=u):
-            at = table.place(t, u)
-            value = jnp.exp(s_ref[at] + wide_ref[jnp.minimum(t, table.row_tiles - 1)])
-            keep(at, value)
-            return a + value
-
-        acc_ref[u] = table.loop(table_ref, table.column_base + u, 4, one_tile, blank())
-    totals = jnp.concatenate(
-        [jnp.sum(acc_ref[u], axis=0, keepdims=True) for u in range(table.columns)], axis=0
-    )
-    m_ref[...] = jnp.zeros(m_ref.shape, jnp.float32)
-    out_ref[...] = jnp.log(totals)
-    bits = bad_bits(totals > 1e-15) - table.empty_bits(table_ref, table.column_base, table.columns)
-
-    @pl.when(bits != 0)
-    def _():
-        for u in range(table.columns):
-
-            @pl.when(has_bit(bits, u))
-            def _():
-                peak, total = slow_column(table, table_ref, u, s_ref, wide_ref, keep)
-                m_ref[u : u + 1, :] = peak
-                out_ref[u : u + 1, :] = peak + jnp.log(total)
-
-
-def column_kernel(table, arrived, s_ref, w_ref, m_ref, first_ref, *refs):
+def column_kernel(table, arrived, s_ref, w_ref, first_ref, *refs):
     parts, (out_ref, r_ref, r_out_ref, wide_ref, acc_ref) = refs[:-5], refs[-5:]
     row = -combine([part[...] for part in parts])
     r_ref[...] = row
@@ -388,20 +350,16 @@
     spread_rows(factor, wide_ref)
     table_ref = arrived()
 
-    for u in range(table.columns):
-
-        def one_tile(t, a, u=u):
-            kept = w_ref[table.place(t, u)].astype(jnp.float32)
-            return a + kept * wide_ref[jnp.minimum(t, table.row_tiles - 1)]
-
-        acc_ref[u] = table.loop(table_ref, table.column_base + u, 4, one_tile, blank())
+    def visit(u, t):
+        kept = w_ref[table.place(t, u)].astype(jnp.float32)
+        return kept * wide_ref[jnp.minimum(t, table.row_tiles - 1)]
+
+    table.sums(table_ref, table.column_base, acc_ref, visit)
     totals = jnp.concatenate(
         [jnp.sum(acc_ref[u], axis=0, keepdims=True) for u in range(table.columns)], axis=0
     )
-    out_ref[...] = m_ref[...] + jnp.log(totals)
-    largest = jnp.max(jnp.max(factor, axis=1, keepdims=True), axis=0, keepdims=True)
-    bits = bad_bits((totals > 1e-15) & (totals < 1e30) & (largest < 1e15))
-    bits = bits - table.empty_bits(table_ref, table.column_base, table.columns)
+    out_ref[...] = jnp.log(totals)
+    bits = bad_bits(in_range(totals, factor)) - table.empty_bits(table_ref, table.column_base, table.columns)
 
     @pl.when(bits != 0)
     def _():
@@ -410,8 +368,15 @@
 
             @pl.when(has_bit(bits, u))
             def _():
-                peak, total = slow_column(table, table_ref, u, s_ref, wide_ref, lambda at, value: None)
-                out_ref[u : u + 1, :] = peak + jnp.log(total)
+                line = table.column_base + u
+
+                def score(t):
+                    return s_ref[table.place(t, u)] + wide_ref[jnp.minimum(t, table.row_tiles - 1)]
+
+                peak = table.loop(table_ref, line, 2, lambda t, a: jnp.maximum(a, score(t)), lowest())
+                peak = jnp.max(peak, axis=0, keepdims=True)
+                total = table.loop(table_ref, line, 2, lambda t, a: a + jnp.exp(score(t) - peak), blank())
+                out_ref[u : u + 1, :] = peak + jnp.log(jnp.sum(total, axis=0, keepdims=True))
 
 
 def plan_blocks(table, table_ref, p_ref, lines, wanted, width, strip, outs, total_ref):
@@ -508,16 +473,17 @@
     panel = pltpu.VMEM((table.dummy + 1, TILE, TILE), jnp.float32)
     whole = pltpu.VMEM((protos, features), jnp.bfloat16)
     row_shape = jax.ShapeDtypeStruct((table.row_tiles, TILE), jnp.float32)
-    peaks = pltpu.VMEM((table.row_tiles, TILE, TILE), jnp.float32)
+    kept = pltpu.VMEM((table.dummy + 1, TILE, TILE), jnp.bfloat16)
+    tiles = pltpu.VMEM((table.row_tiles, TILE, TILE), jnp.float32)
 
     def late(places, add, e, pieces, before):
         at = 2 + len(pieces)
         return pl.pallas_call(
             with_table(panel_kernel, table, places, add),
-            out_shape=(panel, whole, row_shape),
+            out_shape=(panel, whole, kept, row_shape, row_shape),
             in_specs=[ANY] + [VMEM] * (1 + len(pieces) + len(before)),
-            out_specs=(VMEM, VMEM, VMEM),
-            scratch_shapes=[peaks] + table_scratch(lists),
+            out_specs=(VMEM,) * 5,
+            scratch_shapes=[tiles, tiles] + table_scratch(lists),
             input_output_aliases={at: 0, at + 1: 1} if add else {},
             compiler_params=params(8),
             name="panel",
@@ -536,29 +502,29 @@
     cross_bottom = swap(near_bottom, "row", 2)
     near_top = swap(top, "row", 1)
     far_bottom = swap(bottom, "row", 2)
-    pieces = [shard, near_bottom, far_top]
-    pieces += [sibling(piece) for piece in pieces]
-    places = [Piece(own, *at) for own in (True, False) for at in ((0, 0), (half, 1), (0, 2))]
+    pieces = [top, bottom, near_bottom, far_top, sibling(shard), sibling(near_bottom), sibling(far_top)]
+    places = [Piece(True, 0, 0), Piece(True, half, 0), Piece(True, half, 1), Piece(True, 0, 2)]
+    places += [Piece(False, 0, 0), Piece(False, half, 1), Piece(False, 0, 2)]
     visits = table.dummy * TILE * TILE
-    similar, known, e = pl.pallas_call(
+    similar, known = pl.pallas_call(
         with_table(early_panel_kernel, table, places),
-        out_shape=(panel, whole, pltpu.VMEM(embeddings.shape, jnp.bfloat16)),
-        in_specs=[ANY, ANY] + [VMEM] * len(pieces),
-        out_specs=(VMEM, VMEM, VMEM),
-        scratch_shapes=[pltpu.SemaphoreType.DMA] + table_scratch(lists),
+        out_shape=(panel, whole),
+        in_specs=[ANY] + [VMEM] * (1 + len(pieces)),
+        out_specs=(VMEM, VMEM),
+        scratch_shapes=table_scratch(lists),
         compiler_params=params(6),
         cost_estimate=pl.CostEstimate(
             flops=visits * features, bytes_accessed=8 * visits, transcendentals=0
         ),
         name="early_panel",
     )(lists, embeddings, *pieces)
-    cross_top, cross_bottom, near_top, far_bottom, similar, known, e = tied(
-        cross_top, cross_bottom, near_top, far_bottom, similar, known, e
+    cross_top, cross_bottom, near_top, far_bottom, similar, known = tied(
+        cross_top, cross_bottom, near_top, far_bottom, similar, known
     )
     pieces = [near_top, far_bottom, cross_top, cross_bottom]
     pieces += [sibling(piece) for piece in pieces]
     places = [Piece(own, *at) for own in (True, False) for at in ((0, 1), (half, 2), (0, 3), (half, 3))]
-    return late(places, True, e, pieces, [similar, known])
+    return late(places, True, embeddings, pieces, [similar, known])
 
 
 def scatter_partials(blocks):
@@ -595,11 +561,10 @@
     row_shape = jax.ShapeDtypeStruct((row_tiles, TILE), jnp.float32)
     column_shape = jax.ShapeDtypeStruct((columns, TILE), jnp.float32)
     half = columns // 2
-    panel = (table.dummy + 1, TILE, TILE)
     wide = pltpu.VMEM((row_tiles, TILE, TILE), jnp.float32)
     tall = pltpu.VMEM((columns, TILE, TILE), jnp.float32)
     factors = pltpu.VMEM((columns + 8, TILE), jnp.float32)
-    similar, whole, row_part = make_panel(table, lists, embeddings, prototypes, rows, features)
+    similar, whole, kept, first, row_part = make_panel(table, lists, embeddings, prototypes, rows, features)
 
     def row_exchange(part):
         others = [swap(part, "proto", 2 * j) for j in range(lines - 1, 0, -1)]
@@ -609,37 +574,28 @@
         others = [swap(part, "row", j) for j in range(n_row - 1, 0, -1)]
         return [part] + others[::-1]
 
-    parts = row_exchange(row_part)
-    column_part, first_row, kept, peaks = pl.pallas_call(
-        with_table(first_column_kernel, table),
-        out_shape=(column_shape, row_shape, pltpu.VMEM(panel, jnp.bfloat16), column_shape),
-        in_specs=[ANY] + [VMEM] * (1 + len(parts)),
-        out_specs=(VMEM,) * 4,
-        scratch_shapes=[wide, tall] + table_scratch(lists),
-        compiler_params=params(4),
-        name="first_column_pass",
-    )(lists, similar, *parts)
-    for sweep in range(1, ITERS):
-        parts = column_exchange(column_part)
-        row_part = pl.pallas_call(
-            with_table(row_kernel, table, log_column),
-            out_shape=row_shape,
-            in_specs=[ANY] + [VMEM] * (4 + len(parts)),
-            out_specs=VMEM,
-            scratch_shapes=[factors, factors, wide] + table_scratch(lists),
-            compiler_params=params(4),
-            name="row_pass",
-        )(lists, similar, kept, peaks, first_row, *parts)
+    for sweep in range(ITERS):
+        if sweep:
+            parts = column_exchange(column_part)
+            row_part = pl.pallas_call(
+                with_table(row_kernel, table, log_column),
+                out_shape=row_shape,
+                in_specs=[ANY] + [VMEM] * (3 + len(parts)),
+                out_specs=VMEM,
+                scratch_shapes=[factors, factors, wide] + table_scratch(lists),
+                compiler_params=params(4),
+                name="row_pass",
+            )(lists, similar, kept, first, *parts)
         parts = row_exchange(row_part)
         column_part, row_potential, row_out = pl.pallas_call(
             with_table(column_kernel, table),
             out_shape=(column_shape, row_shape, row_shape),
-            in_specs=[ANY] + [VMEM] * (4 + len(parts)),
+            in_specs=[ANY] + [VMEM] * (3 + len(parts)),
             out_specs=(VMEM,) * 3,
             scratch_shapes=[wide, tall] + table_scratch(lists),
             compiler_params=params(4),
             name="column_pass",
-        )(lists, similar, kept, peaks, first_row, *parts)
+        )(lists, similar, kept, first, *parts)
     parts = column_exchange(column_part)
     block = jax.ShapeDtypeStruct((rows, width), jnp.bfloat16)
 

time: 129 us -> 139 us (1.078)
  starting transfers between devices: 40.4 us -> 49.5 us
  waiting for transfers between devices: 48.9 us -> 50.5 us
    ppermute x35, starting transfers between devices: 40.4 us -> 49.5 us  [swap(): return lax.ppermute(x, axis, [(i, i ^ offset) for i in range(size)])]
    pallas_call x2 -> x3, Pallas kernels: 4.29 us -> 6.73 us  [shards(): pl.pallas_call(with_table(column_kernel, table), out_shape=(column_shape,...]
    pallas_call x1 -> x0, Pallas kernels: 1.8 us -> none  [shards(): pl.pallas_call(with_table(first_column_kernel, table), out_shape=(column_...]
    ppermute x35, waiting for transfers between devices: 48.9 us -> 50.5 us  [swap(): return lax.ppermute(x, axis, [(i, i ^ offset) for i in range(size)])]
  transfers between devices with their start and end apart: 35 -> 35, of which waited for: 23 -> 22; matrix products, arithmetic and copies ran while one was open for 4% -> 4% of each run, Pallas kernels for 5% -> 6%
where the time goes in v12:
time: 139 us; the launch traced here: 138 us
  waiting for transfers between devices  50.5 us (36%)
  starting transfers between devices  49.5 us (36%)
  Pallas kernels  27.2 us (20%)
  other arithmetic  4.4 us (3%)
  local copies, waits for them, and re-layouts  4.39 us (3%)
  between operations  2.15 us (2%)
    ppermute x35, waiting for transfers between devices, swap(): return lax.ppermute(x, axis, [(i, i ^ offset) for i in range(size)])  50.5 us
    ppermute x35, starting transfers between devices, swap(): return lax.ppermute(x, axis, [(i, i ^ offset) for i in range(size)])  49.5 us
    pallas_call x3, Pallas kernels, shards(): pl.pallas_call(with_table(column_kernel, table), out_shape=(column_shape,...  6.73 us
    pallas_call x1, Pallas kernels, late(): pl.pallas_call(with_table(panel_kernel, table, places, add), out_shape=(p...  5.73 us
    pallas_call x1, Pallas kernels, shards(): pl.pallas_call(with_table(rest_kernel, table, lines), out_shape=[block] *...  3.82 us
    pallas_call x1, Pallas kernels, make_panel(): pl.pallas_call(with_table(early_panel_kernel, table, places), out_shape=(...  3.8 us
    pallas_call x2, Pallas kernels, shards(): pl.pallas_call(with_table(row_kernel, table, log_column), out_shape=row_s...  3.63 us
    pallas_call x1, Pallas kernels, shards(): pl.pallas_call(with_table(plan_kernel, table, log_column, lines), out_sha...  3.52 us
  transfers between devices with their start and end apart: 35, of which 22 were waited for; matrix products, arithmetic and copies ran while one was open for 4% of the time, Pallas kernels for 6%

profile of v12, /device:TPU:0, one launch (start us, length us, event | category | flops | bytes accessed | tf_op | source)
XLA Modules:
  0.0 138.1 jit_solution(3761300299146075956)
XLA Ops:
  1.2 1.1 fusion.5
  2.3 3.0 %collective-permute-start.2 = (bf16[512,256]{1,0:T(8,128)(2,1)S(1)}, bf16[512,256]{1,0:T(8,128)(2,1)S(1)}, u32[]{:S(2)}, u32[]{:S(2)}) collective-permute-start(bf16[512,256]{1,0:T(8,128)(2,1)S(1)} %get-tuple-element.35.refs_1_), channel_id=1, source_target_pairs={{0,16},{8,24},{16,0},{24,8},{1,17},{9,25},{17,1},{25,9},{2,18},{10... | collective-permute-start | bytes 786440 | tf_op jit(solution)/shard_map/ppermute | solution.py:21
  5.3 1.5 %collective-permute-start.1 = (bf16[512,256]{1,0:T(8,128)(2,1)S(1)}, bf16[512,256]{1,0:T(8,128)(2,1)S(1)}, u32[]{:S(2)}, u32[]{:S(2)}) collective-permute-start(bf16[512,256]{1,0:T(8,128)(2,1)S(1)} %get-tuple-element.36.refs_2_), channel_id=1, source_target_pairs={{0,8},{8,0},{16,24},{24,16},{1,9},{9,1},{17,25},{25,17},{2,10},{10... | collective-permute-start | bytes 786440 | tf_op jit(solution)/shard_map/ppermute | solution.py:21
  6.8 0.7 compare_select_fusion.1
  8.1 0.6 fusion.4
  11.9 0.7 concatenate.25.hbm_ref
  12.6 0.7 collective-permute-done.1.refs_3_
  13.8 1.5 %collective-permute-start.3 = (bf16[512,256]{1,0:T(8,128)(2,1)S(1)}, bf16[512,256]{1,0:T(8,128)(2,1)S(1)}, u32[]{:S(2)}, u32[]{:S(2)}) collective-permute-start(bf16[512,256]{1,0:T(8,128)(2,1)S(1)} %collective-permute-done.2.refs_4_), channel_id=1, source_target_pairs={{0,8},{8,0},{16,24},{24,16},{1,9},{9,1},{17,25},{25,17},{2,10},{10... | collective-permute-start | bytes 786440 | tf_op jit(solution)/shard_map/ppermute | solution.py:21
  16.3 1.5 %collective-permute-start.6 = (bf16[512,256]{1,0:T(8,128)(2,1)S(1)}, bf16[512,256]{1,0:T(8,128)(2,1)S(1)}, u32[]{:S(2)}, u32[]{:S(2)}) collective-permute-start(bf16[512,256]{1,0:T(8,128)(2,1)S(1)} %get-tuple-element.36.refs_2_), channel_id=1, source_target_pairs={{0,16},{8,24},{16,0},{24,8},{1,17},{9,25},{17,1},{25,9},{2,18},{10... | collective-permute-start | bytes 786440 | tf_op jit(solution)/shard_map/ppermute | solution.py:21
  17.9 2.2 %copy-done = bf16[2048,1024]{1,0:T(8,128)(2,1)S(1)} copy-done((bf16[2048,1024]{1,0:T(8,128)(2,1)S(1)}, bf16[2048,1024]{1,0:T(8,128)(2,1)}, u32[]{:S(2)}) %copy-start) | copy-done | bytes 4194328
  20.1 3.8 %early_panel.1 = (f32[257,128,128]{2,1,0:T(8,128)S(1)}, bf16[2048,1024]{1,0:T(8,128)(2,1)S(1)}) custom-call(s32[1284]{0:T(1024)S(1)} %concatenate.25.hbm_ref, bf16[2048,1024]{1,0:T(8,128)(2,1)S(1)} %copy-done, bf16[512,256]{1,0:T(8,128)(2,1)S(1)} %get-tuple-element.35.refs_1_, bf16[512,256]{1,0:T(8,128)(2,1)S(1)} %get-tuple-element.36.refs_2_, ...), custom_call_target="tpu_custom_call" | custom-call | flops 4294967296 | bytes 33554432 | tf_op jit(solution)/shard_map/early_panel/pallas_call | solution.py:509
  23.9 3.8 %collective-permute-done.5.refs_1_ = bf16[512,256]{1,0:T(8,128)(2,1)S(1)} collective-permute-done((bf16[512,256]{1,0:T(8,128)(2,1)S(1)}, bf16[512,256]{1,0:T(8,128)(2,1)S(1)}, u32[]{:S(2)}, u32[]{:S(2)}) %collective-permute-start.5) | collective-permute-done | bytes 262176 | tf_op jit(solution)/shard_map/ppermute | solution.py:21
  27.7 1.2 collective-permute-done.6.refs_2_
  31.5 5.7 %panel.1 = (f32[257,128,128]{2,1,0:T(8,128)S(1)}, bf16[2048,1024]{1,0:T(8,128)(2,1)S(1)}, bf16[257,128,128]{2,1,0:T(8,128)(2,1)S(1)}, f32[16,128]{1,0:T(8,128)S(1)}, f32[16,128]{1,0:T(8,128)S(1)}) custom-call(s32[1284]{0:T(1024)S(1)} %concatenate.25.hbm_ref, bf16[2048,1024]{1,0:T(8,128)(2,1)S(1)} %copy-done.1, ...), custom_call_target="tpu_custom_call", output_to_operand_aliasing={{0}: (10, {}), {1}: (11, {})} | custom-call | tf_op jit(solution)/shard_map/panel/pallas_call | solution.py:481
  37.3 3.7 %collective-permute-start.16 = (f32[16,128]{1,0:T(8,128)S(1)}, f32[16,128]{1,0:T(8,128)S(1)}, u32[]{:S(2)}, u32[]{:S(2)}) collective-permute-start(f32[16,128]{1,0:T(8,128)S(1)} %get-tuple-element.48.refs_3_), channel_id=1, source_target_pairs={{0,6},{1,7},{2,4},{3,5},{4,2},{5,3},{6,0},{7,1},{8,14},{9,15},{10,... | collective-permute-start | bytes 24584 | tf_op jit(solution)/shard_map/ppermute | solution.py:21
  40.9 0.8 collective-permute-start.14
  41.7 1.1 collective-permute-done.16.refs_6_
  42.8 2.7 %collective-permute-done.15.refs_5_ = f32[16,128]{1,0:T(8,128)S(1)} collective-permute-done((f32[16,128]{1,0:T(8,128)S(1)}, f32[16,128]{1,0:T(8,128)S(1)}, u32[]{:S(2)}, u32[]{:S(2)}) %collective-permute-start.15) | collective-permute-done | bytes 8224 | tf_op jit(solution)/shard_map/ppermute | solution.py:21
  45.5 2.2 %column_pass.3 = (f32[16,128]{1,0:T(8,128)S(1)}, f32[16,128]{1,0:T(8,128)}, f32[16,128]{1,0:T(8,128)}) custom-call(s32[1284]{0:T(1024)S(1)} %concatenate.25.hbm_ref, f32[257,128,128]{2,1,0:T(8,128)S(1)} %get-tuple-element.45.refs_0_, bf16[257,128,128]{2,1,0:T(8,128)(2,1)S(1)} %get-tuple-element.46.refs_1_, f32[16,128]{1,0:T(8,128)S(1)} %get-tuple-element.47.refs_2_, ...), custom_call_target="tpu_custom_call" | custom-call | tf_op jit(solution)/shard_map/column_pass/pallas_call | solution.py:590
  47.7 3.7 %collective-permute-start.19 = (f32[16,128]{1,0:T(8,128)S(1)}, f32[16,128]{1,0:T(8,128)S(1)}, u32[]{:S(2)}, u32[]{:S(2)}) collective-permute-start(f32[16,128]{1,0:T(8,128)S(1)} %get-tuple-element.49.refs_3_), channel_id=1, source_target_pairs={{0,24},{8,16},{16,8},{24,0},{1,25},{9,17},{17,9},{25,1},{2,26},{10... | collective-permute-start | bytes 24584 | tf_op jit(solution)/shard_map/ppermute | solution.py:21
  52.1 1.0 collective-permute-done.19.refs_6_
  53.0 2.0 %collective-permute-done.18.refs_5_ = f32[16,128]{1,0:T(8,128)S(1)} collective-permute-done((f32[16,128]{1,0:T(8,128)S(1)}, f32[16,128]{1,0:T(8,128)S(1)}, u32[]{:S(2)}, u32[]{:S(2)}) %collective-permute-start.18) | collective-permute-done | bytes 8224 | tf_op jit(solution)/shard_map/ppermute | solution.py:21
  55.1 1.9 %row_pass.2.refs_3_ = f32[16,128]{1,0:T(8,128)S(1)} custom-call(s32[1284]{0:T(1024)S(1)} %concatenate.25.hbm_ref, f32[257,128,128]{2,1,0:T(8,128)S(1)} %get-tuple-element.45.refs_0_, bf16[257,128,128]{2,1,0:T(8,128)(2,1)S(1)} %get-tuple-element.46.refs_1_, f32[16,128]{1,0:T(8,128)S(1)} %get-tuple-element.47.refs_2_, ...), custom_call_target="tpu_custom_call" | custom-call | tf_op jit(solution)/shard_map/row_pass/pallas_call | solution.py:580
  57.0 2.1 %collective-permute-start.22 = (f32[16,128]{1,0:T(8,128)S(1)}, f32[16,128]{1,0:T(8,128)S(1)}, u32[]{:S(2)}, u32[]{:S(2)}) collective-permute-start(f32[16,128]{1,0:T(8,128)S(1)} %row_pass.2.refs_3_), channel_id=1, source_target_pairs={{0,6},{1,7},{2,4},{3,5},{4,2},{5,3},{6,0},{7,1},{8,14},{9,15},{10,... | collective-permute-start | bytes 24584 | tf_op jit(solution)/shard_map/ppermute | solution.py:21
  59.1 5.7 %collective-permute-start.21 = (f32[16,128]{1,0:T(8,128)S(1)}, f32[16,128]{1,0:T(8,128)S(1)}, u32[]{:S(2)}, u32[]{:S(2)}) collective-permute-start(f32[16,128]{1,0:T(8,128)S(1)} %row_pass.2.refs_3_), channel_id=1, source_target_pairs={{0,4},{1,5},{2,6},{3,7},{4,0},{5,1},{6,2},{7,3},{8,12},{9,13},{10,... | collective-permute-start | bytes 24584 | tf_op jit(solution)/shard_map/ppermute | solution.py:21
  65.3 1.1 collective-permute-done.21.refs_5_
  66.5 2.0 %collective-permute-done.20.refs_4_ = f32[16,128]{1,0:T(8,128)S(1)} collective-permute-done((f32[16,128]{1,0:T(8,128)S(1)}, f32[16,128]{1,0:T(8,128)S(1)}, u32[]{:S(2)}, u32[]{:S(2)}) %collective-permute-start.20) | collective-permute-done | bytes 8224 | tf_op jit(solution)/shard_map/ppermute | solution.py:21
  68.5 2.2 %column_pass.4 = (f32[16,128]{1,0:T(8,128)S(1)}, f32[16,128]{1,0:T(8,128)}, f32[16,128]{1,0:T(8,128)}) custom-call(s32[1284]{0:T(1024)S(1)} %concatenate.25.hbm_ref, f32[257,128,128]{2,1,0:T(8,128)S(1)} %get-tuple-element.45.refs_0_, bf16[257,128,128]{2,1,0:T(8,128)(2,1)S(1)} %get-tuple-element.46.refs_1_, f32[16,128]{1,0:T(8,128)S(1)} %get-tuple-element.47.refs_2_, ...), custom_call_target="tpu_custom_call" | custom-call | tf_op jit(solution)/shard_map/column_pass/pallas_call | solution.py:590
  70.7 3.9 %collective-permute-start.25 = (f32[16,128]{1,0:T(8,128)S(1)}, f32[16,128]{1,0:T(8,128)S(1)}, u32[]{:S(2)}, u32[]{:S(2)}) collective-permute-start(f32[16,128]{1,0:T(8,128)S(1)} %get-tuple-element.50.refs_3_), channel_id=1, source_target_pairs={{0,24},{8,16},{16,8},{24,0},{1,25},{9,17},{17,9},{25,1},{2,26},{10... | collective-permute-start | bytes 24584 | tf_op jit(solution)/shard_map/ppermute | solution.py:21
  74.6 1.1 collective-permute-start.23
  76.3 2.0 %collective-permute-done.24.refs_5_ = f32[16,128]{1,0:T(8,128)S(1)} collective-permute-done((f32[16,128]{1,0:T(8,128)S(1)}, f32[16,128]{1,0:T(8,128)S(1)}, u32[]{:S(2)}, u32[]{:S(2)}) %collective-permute-start.24) | collective-permute-done | bytes 8224 | tf_op jit(solution)/shard_map/ppermute | solution.py:21
  78.3 1.7 %row_pass.3.refs_3_ = f32[16,128]{1,0:T(8,128)S(1)} custom-call(s32[1284]{0:T(1024)S(1)} %concatenate.25.hbm_ref, f32[257,128,128]{2,1,0:T(8,128)S(1)} %get-tuple-element.45.refs_0_, bf16[257,128,128]{2,1,0:T(8,128)(2,1)S(1)} %get-tuple-element.46.refs_1_, f32[16,128]{1,0:T(8,128)S(1)} %get-tuple-element.47.refs_2_, ...), custom_call_target="tpu_custom_call" | custom-call | tf_op jit(solution)/shard_map/row_pass/pallas_call | solution.py:580
  80.0 3.1 %collective-permute-start.28 = (f32[16,128]{1,0:T(8,128)S(1)}, f32[16,128]{1,0:T(8,128)S(1)}, u32[]{:S(2)}, u32[]{:S(2)}) collective-permute-start(f32[16,128]{1,0:T(8,128)S(1)} %row_pass.3.refs_3_), channel_id=1, source_target_pairs={{0,6},{1,7},{2,4},{3,5},{4,2},{5,3},{6,0},{7,1},{8,14},{9,15},{10,... | collective-permute-start | bytes 24584 | tf_op jit(solution)/shard_map/ppermute | solution.py:21
  83.1 4.2 %collective-permute-start.27 = (f32[16,128]{1,0:T(8,128)S(1)}, f32[16,128]{1,0:T(8,128)S(1)}, u32[]{:S(2)}, u32[]{:S(2)}) collective-permute-start(f32[16,128]{1,0:T(8,128)S(1)} %row_pass.3.refs_3_), channel_id=1, source_target_pairs={{0,4},{1,5},{2,6},{3,7},{4,0},{5,1},{6,2},{7,3},{8,12},{9,13},{10,... | collective-permute-start | bytes 24584 | tf_op jit(solution)/shard_map/ppermute | solution.py:21
  87.9 1.1 collective-permute-done.27.refs_5_
  89.0 2.0 %collective-permute-done.26.refs_4_ = f32[16,128]{1,0:T(8,128)S(1)} collective-permute-done((f32[16,128]{1,0:T(8,128)S(1)}, f32[16,128]{1,0:T(8,128)S(1)}, u32[]{:S(2)}, u32[]{:S(2)}) %collective-permute-start.26) | collective-permute-done | bytes 8224 | tf_op jit(solution)/shard_map/ppermute | solution.py:21
  91.0 2.2 %column_pass.5 = (f32[16,128]{1,0:T(8,128)S(1)}, f32[16,128]{1,0:T(8,128)S(1)}, f32[16,128]{1,0:T(8,128)}) custom-call(s32[1284]{0:T(1024)S(1)} %concatenate.25.hbm_ref, f32[257,128,128]{2,1,0:T(8,128)S(1)} %get-tuple-element.45.refs_0_, bf16[257,128,128]{2,1,0:T(8,128)(2,1)S(1)} %get-tuple-element.46.refs_1_, f32[16,128]{1,0:T(8,128)S(1)} %get-tuple-element.47.refs_2_, ...), custom_call_target="tpu_custom_call" | custom-call | tf_op jit(solution)/shard_map/column_pass/pallas_call | solution.py:590
  93.3 4.6 %collective-permute-start.31 = (f32[16,128]{1,0:T(8,128)S(1)}, f32[16,128]{1,0:T(8,128)S(1)}, u32[]{:S(2)}, u32[]{:S(2)}) collective-permute-start(f32[16,128]{1,0:T(8,128)S(1)} %get-tuple-element.53.refs_3_), channel_id=1, source_target_pairs={{0,24},{8,16},{16,8},{24,0},{1,25},{9,17},{17,9},{25,1},{2,26},{10... | collective-permute-start | bytes 24584 | tf_op jit(solution)/shard_map/ppermute | solution.py:21
  98.5 1.0 collective-permute-done.31.refs_6_
  99.5 2.0 %collective-permute-done.30.refs_5_ = f32[16,128]{1,0:T(8,128)S(1)} collective-permute-done((f32[16,128]{1,0:T(8,128)S(1)}, f32[16,128]{1,0:T(8,128)S(1)}, u32[]{:S(2)}, u32[]{:S(2)}) %collective-permute-start.30) | collective-permute-done | bytes 8224 | tf_op jit(solution)/shard_map/ppermute | solution.py:21
  101.5 3.5 %plan.1 = (bf16[2048,128]{1,0:T(8,128)(2,1)S(1)}, bf16[33,512,256]{2,1,0:T(8,128)(2,1)S(1)}, f32[8,128]{1,0:T(8,128)}) custom-call(s32[1284]{0:T(1024)S(1)} %concatenate.25.hbm_ref, f32[257,128,128]{2,1,0:T(8,128)S(1)} %get-tuple-element.45.refs_0_, f32[16,128]{1,0:T(8,128)S(1)} %get-tuple-element.51.refs_1_, ...), custom_call_target="tpu_custom_call" | custom-call | tf_op jit(solution)/shard_map/plan/pallas_call | solution.py:606
  105.0 1.5 %collective-permute-start.33 = (bf16[2048,128]{1,0:T(8,128)(2,1)S(1)}, bf16[2048,128]{1,0:T(8,128)(2,1)S(1)}, u32[]{:S(2)}, u32[]{:S(2)}) collective-permute-start(bf16[2048,128]{1,0:T(8,128)(2,1)S(1)} %get-tuple-element.58), channel_id=1, source_target_pairs={{0,2},{1,3},{2,0},{3,1},{4,6},{5,7},{6,4},{7,5},{8,10},{9,11},{10,... | collective-permute-start | bytes 1572872 | tf_op jit(solution)/shard_map/ppermute | solution.py:21
  106.6 3.8 %rest_of_plan.1 = (bf16[2048,128]{1,0:T(8,128)(2,1)S(1)}, bf16[2048,128]{1,0:T(8,128)(2,1)S(1)}, bf16[2048,128]{1,0:T(8,128)(2,1)S(1)}) custom-call(s32[1284]{0:T(1024)S(1)} %concatenate.25.hbm_ref, bf16[33,512,256]{2,1,0:T(8,128)(2,1)S(1)} %get-tuple-element.54.refs_0_, bf16[2048,1024]{1,0:T(8,128)(2,1)S(1)} %get-tuple-element.52.refs_2_.refs_1_), custom_call_target="tpu_custom_call" | custom-call | flops 3221225472 | bytes 16777216 | tf_op jit(solution)/shard_map/rest_of_plan/pallas_call | solution.py:620
  111.0 10.1 %collective-permute-done.33 = bf16[2048,128]{1,0:T(8,128)(2,1)S(1)} collective-permute-done((bf16[2048,128]{1,0:T(8,128)(2,1)S(1)}, bf16[2048,128]{1,0:T(8,128)(2,1)S(1)}, u32[]{:S(2)}, u32[]{:S(2)}) %collective-permute-start.33) | collective-permute-done | bytes 524320 | tf_op jit(solution)/shard_map/ppermute | solution.py:21
  121.3 1.5 %collective-permute-start.34 = (bf16[2048,128]{1,0:T(8,128)(2,1)S(1)}, bf16[2048,128]{1,0:T(8,128)(2,1)S(1)}, u32[]{:S(2)}, u32[]{:S(2)}) collective-permute-start(bf16[2048,128]{1,0:T(8,128)(2,1)S(1)} %add_convert_fusion.1), channel_id=1, source_target_pairs={{0,4},{1,5},{2,6},{3,7},{4,0},{5,1},{6,2},{7,3},{8,12},{9,13},{10,... | collective-permute-start | bytes 1572872 | tf_op jit(solution)/shard_map/ppermute | solution.py:21
  122.8 6.8 %collective-permute-done.32 = bf16[2048,128]{1,0:T(8,128)(2,1)S(1)} collective-permute-done((bf16[2048,128]{1,0:T(8,128)(2,1)S(1)}, bf16[2048,128]{1,0:T(8,128)(2,1)S(1)}, u32[]{:S(2)}, u32[]{:S(2)}) %collective-permute-start.32) | collective-permute-done | bytes 524320 | tf_op jit(solution)/shard_map/ppermute | solution.py:21
  129.6 7.6 %collective-permute-done.34 = bf16[2048,128]{1,0:T(8,128)(2,1)S(1)} collective-permute-done((bf16[2048,128]{1,0:T(8,128)(2,1)S(1)}, bf16[2048,128]{1,0:T(8,128)(2,1)S(1)}, u32[]{:S(2)}, u32[]{:S(2)}) %collective-permute-start.34) | collective-permute-done | bytes 524320 | tf_op jit(solution)/shard_map/ppermute | solution.py:21
  137.1 1.0 add_convert_fusion
  (68 shorter events, 10.7 us)
Async XLA Ops:
  0.6 6.9 %collective-permute-start = (s32[16,8]{0,1:T(8,128)}, s32[16,8]{0,1:T(8,128)S(1)}, u32[]{:S(2)}, u32[]{:S(2)}) collective-permute-start(s32[16,8]{0,1:T(8,128)} %param.5), channel_id=1, source_target_pairs={{0,1},{1,0},{2,3},{3,2},{4,5},{5,4},{6,7},{7,6},{8,9},{9,8},{10,11... | collective-permute-start | bytes 1544 | tf_op jit(solution)/shard_map/ppermute | solution.py:21
  1.1 16.7 %collective-permute-start.7 = (bf16[1024,256]{1,0:T(8,128)(2,1)}, bf16[1024,256]{1,0:T(8,128)(2,1)S(1)}, u32[]{:S(2)}, u32[]{:S(2)}) collective-permute-start(bf16[1024,256]{1,0:T(8,128)(2,1)} %param.4), channel_id=1, source_target_pairs={{0,1},{1,0},{2,3},{3,2},{4,5},{5,4},{6,7},{7,6},{8,9},{9,8},{10,11... | collective-permute-start | bytes 1572872 | tf_op jit(solution)/shard_map/ppermute | solution.py:21
  2.3 10.3 %collective-permute-start.2 = (bf16[512,256]{1,0:T(8,128)(2,1)S(1)}, bf16[512,256]{1,0:T(8,128)(2,1)S(1)}, u32[]{:S(2)}, u32[]{:S(2)}) collective-permute-start(bf16[512,256]{1,0:T(8,128)(2,1)S(1)} %get-tuple-element.35.refs_1_), channel_id=1, source_target_pairs={{0,16},{8,24},{16,0},{24,8},{1,17},{9,25},{17,1},{25,9},{2,18},{10... | collective-permute-start | bytes 786440 | tf_op jit(solution)/shard_map/ppermute | solution.py:21
  5.3 8.0 %collective-permute-start.1 = (bf16[512,256]{1,0:T(8,128)(2,1)S(1)}, bf16[512,256]{1,0:T(8,128)(2,1)S(1)}, u32[]{:S(2)}, u32[]{:S(2)}) collective-permute-start(bf16[512,256]{1,0:T(8,128)(2,1)S(1)} %get-tuple-element.36.refs_2_), channel_id=1, source_target_pairs={{0,8},{8,0},{16,24},{24,16},{1,9},{9,1},{17,25},{25,17},{2,10},{10... | collective-permute-start | bytes 786440 | tf_op jit(solution)/shard_map/ppermute | solution.py:21
  13.3 2.5 %collective-permute-start.9 = (bf16[512,256]{1,0:T(8,128)(2,1)S(1)}, bf16[512,256]{1,0:T(8,128)(2,1)S(1)}, u32[]{:S(2)}, u32[]{:S(2)}) collective-permute-start(bf16[512,256]{1,0:T(8,128)(2,1)S(1)} %collective-permute-done.2.refs_4_), channel_id=1, source_target_pairs={{0,1},{1,0},{2,3},{3,2},{4,5},{5,4},{6,7},{7,6},{8,9},{9,8},{10,11... | collective-permute-start | bytes 786440 | tf_op jit(solution)/shard_map/ppermute | solution.py:21
  13.3 3.0 %collective-permute-start.8 = (bf16[512,256]{1,0:T(8,128)(2,1)S(1)}, bf16[512,256]{1,0:T(8,128)(2,1)S(1)}, u32[]{:S(2)}, u32[]{:S(2)}) collective-permute-start(bf16[512,256]{1,0:T(8,128)(2,1)S(1)} %collective-permute-done.1.refs_3_), channel_id=1, source_target_pairs={{0,1},{1,0},{2,3},{3,2},{4,5},{5,4},{6,7},{7,6},{8,9},{9,8},{10,11... | collective-permute-start | bytes 786440 | tf_op jit(solution)/shard_map/ppermute | solution.py:21
  13.8 15.0 %collective-permute-start.3 = (bf16[512,256]{1,0:T(8,128)(2,1)S(1)}, bf16[512,256]{1,0:T(8,128)(2,1)S(1)}, u32[]{:S(2)}, u32[]{:S(2)}) collective-permute-start(bf16[512,256]{1,0:T(8,128)(2,1)S(1)} %collective-permute-done.2.refs_4_), channel_id=1, source_target_pairs={{0,8},{8,0},{16,24},{24,16},{1,9},{9,1},{17,25},{25,17},{2,10},{10... | collective-permute-start | bytes 786440 | tf_op jit(solution)/shard_map/ppermute | solution.py:21
  15.3 13.6 %collective-permute-start.4 = (bf16[512,256]{1,0:T(8,128)(2,1)S(1)}, bf16[512,256]{1,0:T(8,128)(2,1)S(1)}, u32[]{:S(2)}, u32[]{:S(2)}) collective-permute-start(bf16[512,256]{1,0:T(8,128)(2,1)S(1)} %collective-permute-done.1.refs_3_), channel_id=1, source_target_pairs={{0,16},{8,24},{16,0},{24,8},{1,17},{9,25},{17,1},{25,9},{2,18},{10... | collective-permute-start | bytes 786440 | tf_op jit(solution)/shard_map/ppermute | solution.py:21
  15.8 11.8 %collective-permute-start.5 = (bf16[512,256]{1,0:T(8,128)(2,1)S(1)}, bf16[512,256]{1,0:T(8,128)(2,1)S(1)}, u32[]{:S(2)}, u32[]{:S(2)}) collective-permute-start(bf16[512,256]{1,0:T(8,128)(2,1)S(1)} %get-tuple-element.35.refs_1_), channel_id=1, source_target_pairs={{0,8},{8,0},{16,24},{24,16},{1,9},{9,1},{17,25},{25,17},{2,10},{10... | collective-permute-start | bytes 786440 | tf_op jit(solution)/shard_map/ppermute | solution.py:21
  16.3 12.5 %collective-permute-start.6 = (bf16[512,256]{1,0:T(8,128)(2,1)S(1)}, bf16[512,256]{1,0:T(8,128)(2,1)S(1)}, u32[]{:S(2)}, u32[]{:S(2)}) collective-permute-start(bf16[512,256]{1,0:T(8,128)(2,1)S(1)} %get-tuple-element.36.refs_2_), channel_id=1, source_target_pairs={{0,16},{8,24},{16,0},{24,8},{1,17},{9,25},{17,1},{25,9},{2,18},{10... | collective-permute-start | bytes 786440 | tf_op jit(solution)/shard_map/ppermute | solution.py:21
  17.9 2.2 %copy-start = (bf16[2048,1024]{1,0:T(8,128)(2,1)S(1)}, bf16[2048,1024]{1,0:T(8,128)(2,1)}, u32[]{:S(2)}) copy-start(bf16[2048,1024]{1,0:T(8,128)(2,1)} %refs_0_.3) | copy-start | bytes 12582916
  20.1 11.5 %copy-start.1 = (bf16[2048,1024]{1,0:T(8,128)(2,1)S(1)}, bf16[2048,1024]{1,0:T(8,128)(2,1)}, u32[]{:S(2)}) copy-start(bf16[2048,1024]{1,0:T(8,128)(2,1)} %refs_0_.3) | copy-start | bytes 12582916
  28.9 1.5 %collective-permute-start.10 = (bf16[512,256]{1,0:T(8,128)(2,1)S(1)}, bf16[512,256]{1,0:T(8,128)(2,1)S(1)}, u32[]{:S(2)}, u32[]{:S(2)}) collective-permute-start(bf16[512,256]{1,0:T(8,128)(2,1)S(1)} %collective-permute-done.5.refs_1_), channel_id=1, source_target_pairs={{0,1},{1,0},{2,3},{3,2},{4,5},{5,4},{6,7},{7,6},{8,9},{9,8},{10,11... | collective-permute-start | bytes 786440 | tf_op jit(solution)/shard_map/ppermute | solution.py:21
  28.9 1.9 %collective-permute-start.11 = (bf16[512,256]{1,0:T(8,128)(2,1)S(1)}, bf16[512,256]{1,0:T(8,128)(2,1)S(1)}, u32[]{:S(2)}, u32[]{:S(2)}) collective-permute-start(bf16[512,256]{1,0:T(8,128)(2,1)S(1)} %collective-permute-done.6.refs_2_), channel_id=1, source_target_pairs={{0,1},{1,0},{2,3},{3,2},{4,5},{5,4},{6,7},{7,6},{8,9},{9,8},{10,11... | collective-permute-start | bytes 786440 | tf_op jit(solution)/shard_map/ppermute | solution.py:21
  29.4 1.8 %collective-permute-start.12 = (bf16[512,256]{1,0:T(8,128)(2,1)S(1)}, bf16[512,256]{1,0:T(8,128)(2,1)S(1)}, u32[]{:S(2)}, u32[]{:S(2)}) collective-permute-start(bf16[512,256]{1,0:T(8,128)(2,1)S(1)} %collective-permute-done.3.refs_3_), channel_id=1, source_target_pairs={{0,1},{1,0},{2,3},{3,2},{4,5},{5,4},{6,7},{7,6},{8,9},{9,8},{10,11... | collective-permute-start | bytes 786440 | tf_op jit(solution)/shard_map/ppermute | solution.py:21
  29.5 2.1 %collective-permute-start.13 = (bf16[512,256]{1,0:T(8,128)(2,1)S(1)}, bf16[512,256]{1,0:T(8,128)(2,1)S(1)}, u32[]{:S(2)}, u32[]{:S(2)}) collective-permute-start(bf16[512,256]{1,0:T(8,128)(2,1)S(1)} %collective-permute-done.4.refs_4_), channel_id=1, source_target_pairs={{0,1},{1,0},{2,3},{3,2},{4,5},{5,4},{6,7},{7,6},{8,9},{9,8},{10,11... | collective-permute-start | bytes 786440 | tf_op jit(solution)/shard_map/ppermute | solution.py:21
  37.3 5.5 %collective-permute-start.16 = (f32[16,128]{1,0:T(8,128)S(1)}, f32[16,128]{1,0:T(8,128)S(1)}, u32[]{:S(2)}, u32[]{:S(2)}) collective-permute-start(f32[16,128]{1,0:T(8,128)S(1)} %get-tuple-element.48.refs_3_), channel_id=1, source_target_pairs={{0,6},{1,7},{2,4},{3,5},{4,2},{5,3},{6,0},{7,1},{8,14},{9,15},{10,... | collective-permute-start | bytes 24584 | tf_op jit(solution)/shard_map/ppermute | solution.py:21
  40.9 4.5 %collective-permute-start.15 = (f32[16,128]{1,0:T(8,128)S(1)}, f32[16,128]{1,0:T(8,128)S(1)}, u32[]{:S(2)}, u32[]{:S(2)}) collective-permute-start(f32[16,128]{1,0:T(8,128)S(1)} %get-tuple-element.48.refs_3_), channel_id=1, source_target_pairs={{0,4},{1,5},{2,6},{3,7},{4,0},{5,1},{6,2},{7,3},{8,12},{9,13},{10,... | collective-permute-start | bytes 24584 | tf_op jit(solution)/shard_map/ppermute | solution.py:21
  40.9 4.5 %collective-permute-start.14 = (f32[16,128]{1,0:T(8,128)S(1)}, f32[16,128]{1,0:T(8,128)S(1)}, u32[]{:S(2)}, u32[]{:S(2)}) collective-permute-start(f32[16,128]{1,0:T(8,128)S(1)} %get-tuple-element.48.refs_3_), channel_id=1, source_target_pairs={{0,2},{1,3},{2,0},{3,1},{4,6},{5,7},{6,4},{7,5},{8,10},{9,11},{10,... | collective-permute-start | bytes 24584 | tf_op jit(solution)/shard_map/ppermute | solution.py:21
  47.7 5.3 %collective-permute-start.19 = (f32[16,128]{1,0:T(8,128)S(1)}, f32[16,128]{1,0:T(8,128)S(1)}, u32[]{:S(2)}, u32[]{:S(2)}) collective-permute-start(f32[16,128]{1,0:T(8,128)S(1)} %get-tuple-element.49.refs_3_), channel_id=1, source_target_pairs={{0,24},{8,16},{16,8},{24,0},{1,25},{9,17},{17,9},{25,1},{2,26},{10... | collective-permute-start | bytes 24584 | tf_op jit(solution)/shard_map/ppermute | solution.py:21
  51.4 3.7 %collective-permute-start.18 = (f32[16,128]{1,0:T(8,128)S(1)}, f32[16,128]{1,0:T(8,128)S(1)}, u32[]{:S(2)}, u32[]{:S(2)}) collective-permute-start(f32[16,128]{1,0:T(8,128)S(1)} %get-tuple-element.49.refs_3_), channel_id=1, source_target_pairs={{0,16},{8,24},{16,0},{24,8},{1,17},{9,25},{17,1},{25,9},{2,18},{10... | collective-permute-start | bytes 24584 | tf_op jit(solution)/shard_map/ppermute | solution.py:21
  51.4 3.7 %collective-permute-start.17 = (f32[16,128]{1,0:T(8,128)S(1)}, f32[16,128]{1,0:T(8,128)S(1)}, u32[]{:S(2)}, u32[]{:S(2)}) collective-permute-start(f32[16,128]{1,0:T(8,128)S(1)} %get-tuple-element.49.refs_3_), channel_id=1, source_target_pairs={{0,8},{8,0},{16,24},{24,16},{1,9},{9,1},{17,25},{25,17},{2,10},{10... | collective-permute-start | bytes 24584 | tf_op jit(solution)/shard_map/ppermute | solution.py:21
  57.0 8.3 %collective-permute-start.22 = (f32[16,128]{1,0:T(8,128)S(1)}, f32[16,128]{1,0:T(8,128)S(1)}, u32[]{:S(2)}, u32[]{:S(2)}) collective-permute-start(f32[16,128]{1,0:T(8,128)S(1)} %row_pass.2.refs_3_), channel_id=1, source_target_pairs={{0,6},{1,7},{2,4},{3,5},{4,2},{5,3},{6,0},{7,1},{8,14},{9,15},{10,... | collective-permute-start | bytes 24584 | tf_op jit(solution)/shard_map/ppermute | solution.py:21
  59.1 7.4 %collective-permute-start.21 = (f32[16,128]{1,0:T(8,128)S(1)}, f32[16,128]{1,0:T(8,128)S(1)}, u32[]{:S(2)}, u32[]{:S(2)}) collective-permute-start(f32[16,128]{1,0:T(8,128)S(1)} %row_pass.2.refs_3_), channel_id=1, source_target_pairs={{0,4},{1,5},{2,6},{3,7},{4,0},{5,1},{6,2},{7,3},{8,12},{9,13},{10,... | collective-permute-start | bytes 24584 | tf_op jit(solution)/shard_map/ppermute | solution.py:21
  64.8 3.7 %collective-permute-start.20 = (f32[16,128]{1,0:T(8,128)S(1)}, f32[16,128]{1,0:T(8,128)S(1)}, u32[]{:S(2)}, u32[]{:S(2)}) collective-permute-start(f32[16,128]{1,0:T(8,128)S(1)} %row_pass.2.refs_3_), channel_id=1, source_target_pairs={{0,2},{1,3},{2,0},{3,1},{4,6},{5,7},{6,4},{7,5},{8,10},{9,11},{10,... | collective-permute-start | bytes 24584 | tf_op jit(solution)/shard_map/ppermute | solution.py:21
  70.7 5.5 %collective-permute-start.25 = (f32[16,128]{1,0:T(8,128)S(1)}, f32[16,128]{1,0:T(8,128)S(1)}, u32[]{:S(2)}, u32[]{:S(2)}) collective-permute-start(f32[16,128]{1,0:T(8,128)S(1)} %get-tuple-element.50.refs_3_), channel_id=1, source_target_pairs={{0,24},{8,16},{16,8},{24,0},{1,25},{9,17},{17,9},{25,1},{2,26},{10... | collective-permute-start | bytes 24584 | tf_op jit(solution)/shard_map/ppermute | solution.py:21
  74.6 3.7 %collective-permute-start.24 = (f32[16,128]{1,0:T(8,128)S(1)}, f32[16,128]{1,0:T(8,128)S(1)}, u32[]{:S(2)}, u32[]{:S(2)}) collective-permute-start(f32[16,128]{1,0:T(8,128)S(1)} %get-tuple-element.50.refs_3_), channel_id=1, source_target_pairs={{0,16},{8,24},{16,0},{24,8},{1,17},{9,25},{17,1},{25,9},{2,18},{10... | collective-permute-start | bytes 24584 | tf_op jit(solution)/shard_map/ppermute | solution.py:21
  74.6 3.7 %collective-permute-start.23 = (f32[16,128]{1,0:T(8,128)S(1)}, f32[16,128]{1,0:T(8,128)S(1)}, u32[]{:S(2)}, u32[]{:S(2)}) collective-permute-start(f32[16,128]{1,0:T(8,128)S(1)} %get-tuple-element.50.refs_3_), channel_id=1, source_target_pairs={{0,8},{8,0},{16,24},{24,16},{1,9},{9,1},{17,25},{25,17},{2,10},{10... | collective-permute-start | bytes 24584 | tf_op jit(solution)/shard_map/ppermute | solution.py:21
  80.0 7.8 %collective-permute-start.28 = (f32[16,128]{1,0:T(8,128)S(1)}, f32[16,128]{1,0:T(8,128)S(1)}, u32[]{:S(2)}, u32[]{:S(2)}) collective-permute-start(f32[16,128]{1,0:T(8,128)S(1)} %row_pass.3.refs_3_), channel_id=1, source_target_pairs={{0,6},{1,7},{2,4},{3,5},{4,2},{5,3},{6,0},{7,1},{8,14},{9,15},{10,... | collective-permute-start | bytes 24584 | tf_op jit(solution)/shard_map/ppermute | solution.py:21
  83.1 5.9 %collective-permute-start.27 = (f32[16,128]{1,0:T(8,128)S(1)}, f32[16,128]{1,0:T(8,128)S(1)}, u32[]{:S(2)}, u32[]{:S(2)}) collective-permute-start(f32[16,128]{1,0:T(8,128)S(1)} %row_pass.3.refs_3_), channel_id=1, source_target_pairs={{0,4},{1,5},{2,6},{3,7},{4,0},{5,1},{6,2},{7,3},{8,12},{9,13},{10,... | collective-permute-start | bytes 24584 | tf_op jit(solution)/shard_map/ppermute | solution.py:21
  87.4 3.7 %collective-permute-start.26 = (f32[16,128]{1,0:T(8,128)S(1)}, f32[16,128]{1,0:T(8,128)S(1)}, u32[]{:S(2)}, u32[]{:S(2)}) collective-permute-start(f32[16,128]{1,0:T(8,128)S(1)} %row_pass.3.refs_3_), channel_id=1, source_target_pairs={{0,2},{1,3},{2,0},{3,1},{4,6},{5,7},{6,4},{7,5},{8,10},{9,11},{10,... | collective-permute-start | bytes 24584 | tf_op jit(solution)/shard_map/ppermute | solution.py:21
  93.3 6.2 %collective-permute-start.31 = (f32[16,128]{1,0:T(8,128)S(1)}, f32[16,128]{1,0:T(8,128)S(1)}, u32[]{:S(2)}, u32[]{:S(2)}) collective-permute-start(f32[16,128]{1,0:T(8,128)S(1)} %get-tuple-element.53.refs_3_), channel_id=1, source_target_pairs={{0,24},{8,16},{16,8},{24,0},{1,25},{9,17},{17,9},{25,1},{2,26},{10... | collective-permute-start | bytes 24584 | tf_op jit(solution)/shard_map/ppermute | solution.py:21
  97.8 3.7 %collective-permute-start.30 = (f32[16,128]{1,0:T(8,128)S(1)}, f32[16,128]{1,0:T(8,128)S(1)}, u32[]{:S(2)}, u32[]{:S(2)}) collective-permute-start(f32[16,128]{1,0:T(8,128)S(1)} %get-tuple-element.53.refs_3_), channel_id=1, source_target_pairs={{0,16},{8,24},{16,0},{24,8},{1,17},{9,25},{17,1},{25,9},{2,18},{10... | collective-permute-start | bytes 24584 | tf_op jit(solution)/shard_map/ppermute | solution.py:21
  97.8 3.7 %collective-permute-start.29 = (f32[16,128]{1,0:T(8,128)S(1)}, f32[16,128]{1,0:T(8,128)S(1)}, u32[]{:S(2)}, u32[]{:S(2)}) collective-permute-start(f32[16,128]{1,0:T(8,128)S(1)} %get-tuple-element.53.refs_3_), channel_id=1, source_target_pairs={{0,8},{8,0},{16,24},{24,16},{1,9},{9,1},{17,25},{25,17},{2,10},{10... | collective-permute-start | bytes 24584 | tf_op jit(solution)/shard_map/ppermute | solution.py:21
  105.0 16.1 %collective-permute-start.33 = (bf16[2048,128]{1,0:T(8,128)(2,1)S(1)}, bf16[2048,128]{1,0:T(8,128)(2,1)S(1)}, u32[]{:S(2)}, u32[]{:S(2)}) collective-permute-start(bf16[2048,128]{1,0:T(8,128)(2,1)S(1)} %get-tuple-element.58), channel_id=1, source_target_pairs={{0,2},{1,3},{2,0},{3,1},{4,6},{5,7},{6,4},{7,5},{8,10},{9,11},{10,... | collective-permute-start | bytes 1572872 | tf_op jit(solution)/shard_map/ppermute | solution.py:21
  110.4 19.2 %collective-permute-start.32 = (bf16[2048,128]{1,0:T(8,128)(2,1)S(1)}, bf16[2048,128]{1,0:T(8,128)(2,1)S(1)}, u32[]{:S(2)}, u32[]{:S(2)}) collective-permute-start(bf16[2048,128]{1,0:T(8,128)(2,1)S(1)} %get-tuple-element.56), channel_id=1, source_target_pairs={{0,2},{1,3},{2,0},{3,1},{4,6},{5,7},{6,4},{7,5},{8,10},{9,11},{10,... | collective-permute-start | bytes 1572872 | tf_op jit(solution)/shard_map/ppermute | solution.py:21
  121.3 15.8 %collective-permute-start.34 = (bf16[2048,128]{1,0:T(8,128)(2,1)S(1)}, bf16[2048,128]{1,0:T(8,128)(2,1)S(1)}, u32[]{:S(2)}, u32[]{:S(2)}) collective-permute-start(bf16[2048,128]{1,0:T(8,128)(2,1)S(1)} %add_convert_fusion.1), channel_id=1, source_target_pairs={{0,4},{1,5},{2,6},{3,7},{4,0},{5,1},{6,2},{7,3},{8,12},{9,13},{10,... | collective-permute-start | bytes 1572872 | tf_op jit(solution)/shard_map/ppermute | solution.py:21

commit v13 on v12

--- a/solution.py
+++ b/solution.py
@@ -235,29 +235,24 @@
     table.each_item(table_ref, visit)
 
 
-def quarters(owners, p_ref, columns):
+def quarters(owners, p_ref):
     me = lax.axis_index("row")
     width = p_ref.shape[1] // 4
-    pairs = columns // 4
 
     def features(pair):
-        top = lax.rem(pair, pairs) < pairs // 2
-        spans = []
-        for first, second in owners:
-            owner = jnp.bitwise_xor(me, jnp.where(top, first, second))
-            spans.append(pl.ds(pl.multiple_of(owner * width, TILE), width))
-        return spans
+        return [pl.ds(pl.multiple_of(jnp.bitwise_xor(me, owner) * width, TILE), width) for owner in owners]
 
     return features
 
 
-def early_panel_kernel(table, places, arrived, e_ref, *refs):
+def early_panel_kernel(table, places, owners, add, arrived, e_ref, *refs):
     pieces, (s_ref, p_ref) = refs[:-2], refs[-2:]
     for place, piece in zip(places, pieces):
         place.copy_to(p_ref, piece)
-    s_ref[table.dummy] = lowest()
-    features = quarters([(0, 0), (2, 1)], p_ref, table.columns)
-    score_pairs(table, arrived(), e_ref, p_ref, s_ref, features, False, None)
+    if not add:
+        s_ref[table.dummy] = lowest()
+    features = quarters(owners, p_ref)
+    score_pairs(table, arrived(), e_ref, p_ref, s_ref, features, add, None)
 
 
 def panel_kernel(table, places, add, arrived, e_ref, *refs):
@@ -279,7 +274,7 @@
         acc_ref[t] = peak
 
     if add:
-        features = quarters([(1, 2), (3, 3)], p_ref, table.columns)
+        features = quarters([3], p_ref)
     else:
         s_ref[table.dummy] = lowest()
         features = lambda pair: [slice(None)]
@@ -467,7 +462,7 @@
     return lax.optimization_barrier(arrays)
 
 
-def make_panel(table, lists, embeddings, shard, rows, features):
+def make_panel(table, mask, embeddings, shard, rows, features):
     width = shard.shape[1]
     protos = 2 * shard.shape[0]
     panel = pltpu.VMEM((table.dummy + 1, TILE, TILE), jnp.float32)
@@ -476,7 +471,7 @@
     kept = pltpu.VMEM((table.dummy + 1, TILE, TILE), jnp.bfloat16)
     tiles = pltpu.VMEM((table.row_tiles, TILE, TILE), jnp.float32)
 
-    def late(places, add, e, pieces, before):
+    def late(lists, places, add, e, pieces, before):
         at = 2 + len(pieces)
         return pl.pallas_call(
             with_table(panel_kernel, table, places, add),
@@ -490,41 +485,44 @@
         )(lists, e, *pieces, *before)
 
     if lax.axis_size("row") != 4 or width % TILE:
+        lists = table.build(mask)
         every = lax.all_gather(shard, "row", axis=1, tiled=True)
         places = [Piece(True, 0, None), Piece(False, 0, None)]
-        return late(places, False, embeddings, [every, sibling(every)], [])
+        return (lists, *late(lists, places, False, embeddings, [every, sibling(every)], []))
     half = shard.shape[0] // 2
-    top, bottom = shard[:half], shard[half:]
-    near_bottom = swap(bottom, "row", 1)
-    far_top = swap(top, "row", 2)
-    near_bottom, far_top, top, bottom, lists = tied(near_bottom, far_top, top, bottom, lists)
-    cross_top = swap(far_top, "row", 1)
-    cross_bottom = swap(near_bottom, "row", 2)
-    near_top = swap(top, "row", 1)
-    far_bottom = swap(bottom, "row", 2)
-    pieces = [top, bottom, near_bottom, far_top, sibling(shard), sibling(near_bottom), sibling(far_top)]
-    places = [Piece(True, 0, 0), Piece(True, half, 0), Piece(True, half, 1), Piece(True, 0, 2)]
-    places += [Piece(False, 0, 0), Piece(False, half, 1), Piece(False, 0, 2)]
     visits = table.dummy * TILE * TILE
-    similar, known = pl.pallas_call(
-        with_table(early_panel_kernel, table, places),
-        out_shape=(panel, whole),
-        in_specs=[ANY] + [VMEM] * (1 + len(pieces)),
-        out_specs=(VMEM, VMEM),
-        scratch_shapes=table_scratch(lists),
-        compiler_params=params(6),
-        cost_estimate=pl.CostEstimate(
-            flops=visits * features, bytes_accessed=8 * visits, transcendentals=0
-        ),
-        name="early_panel",
-    )(lists, embeddings, *pieces)
-    cross_top, cross_bottom, near_top, far_bottom, similar, known = tied(
-        cross_top, cross_bottom, near_top, far_bottom, similar, known
-    )
-    pieces = [near_top, far_bottom, cross_top, cross_bottom]
-    pieces += [sibling(piece) for piece in pieces]
-    places = [Piece(own, *at) for own in (True, False) for at in ((0, 1), (half, 2), (0, 3), (half, 3))]
-    return late(places, True, embeddings, pieces, [similar, known])
+
+    def early(lists, places, owners, pieces, before):
+        at = 2 + len(pieces)
+        return pl.pallas_call(
+            with_table(early_panel_kernel, table, places, owners, bool(before)),
+            out_shape=(panel, whole),
+            in_specs=[ANY] + [VMEM] * (1 + len(pieces) + len(before)),
+            out_specs=(VMEM, VMEM),
+            scratch_shapes=table_scratch(lists),
+            input_output_aliases={at: 0, at + 1: 1} if before else {},
+            compiler_params=params(6),
+            cost_estimate=pl.CostEstimate(
+                flops=visits * width * len(owners), bytes_accessed=8 * visits, transcendentals=0
+            ),
+            name="early_panel",
+        )(lists, embeddings, *pieces, *before)
+
+    near = swap(shard, "row", 1)
+    far = swap(shard, "row", 2)
+    lists = table.build(mask)
+    places = [Piece(True, 0, 0), Piece(False, 0, 0)]
+    similar, known = early(lists, places, [0], [shard, sibling(shard)], [])
+    near, far, similar, known = tied(near, far, similar, known)
+    cross_top = swap(far[:half], "row", 1)
+    cross_bottom = swap(near[half:], "row", 2)
+    places = [Piece(own, 0, owner) for own in (True, False) for owner in (1, 2)]
+    pieces = [near, far, sibling(near), sibling(far)]
+    similar, known = early(lists, places, [1, 2], pieces, [similar, known])
+    cross_top, cross_bottom, similar, known = tied(cross_top, cross_bottom, similar, known)
+    places = [Piece(own, first, 3) for own in (True, False) for first in (0, half)]
+    pieces = [cross_top, cross_bottom, sibling(cross_top), sibling(cross_bottom)]
+    return (lists, *late(lists, places, True, embeddings, pieces, [similar, known]))
 
 
 def scatter_partials(blocks):
@@ -550,12 +548,10 @@
 
     other_mask = swap(block_mask, "proto", 1)
     mask, other_mask = jnp.where(block_mask == 1, 1, 0), jnp.where(other_mask == 1, 1, 0)
-    lists = table.build(
-        jnp.where(
-            lax.axis_index("proto") % 2 == 0,
-            jnp.concatenate([mask, other_mask], axis=1),
-            jnp.concatenate([other_mask, mask], axis=1),
-        )
+    mask = jnp.where(
+        lax.axis_index("proto") % 2 == 0,
+        jnp.concatenate([mask, other_mask], axis=1),
+        jnp.concatenate([other_mask, mask], axis=1),
     )
 
     row_shape = jax.ShapeDtypeStruct((row_tiles, TILE), jnp.float32)
@@ -564,7 +560,7 @@
     wide = pltpu.VMEM((row_tiles, TILE, TILE), jnp.float32)
     tall = pltpu.VMEM((columns, TILE, TILE), jnp.float32)
     factors = pltpu.VMEM((columns + 8, TILE), jnp.float32)
-    similar, whole, kept, first, row_part = make_panel(table, lists, embeddings, prototypes, rows, features)
+    lists, similar, whole, kept, first, row_part = make_panel(table, mask, embeddings, prototypes, rows, features)
 
     def row_exchange(part):
         others = [swap(part, "proto", 2 * j) for j in range(lines - 1, 0, -1)]

time: 139 us -> 137 us (0.986)
  Pallas kernels: 27.2 us -> 38 us
  starting transfers between devices: 49.5 us -> 39.6 us
  waiting for transfers between devices: 50.5 us -> 47.5 us
    ppermute x35 -> x31, starting transfers between devices: 49.5 us -> 39.6 us  [swap(): return lax.ppermute(x, axis, [(i, i ^ offset) for i in range(size)])]
    pallas_call x2, Pallas kernels: 3.63 us -> 12.7 us  [shards(): pl.pallas_call(with_table(row_kernel, table, log_column), out_shape=row_s...]
    ppermute x35 -> x31, waiting for transfers between devices: 50.5 us -> 47.5 us  [swap(): return lax.ppermute(x, axis, [(i, i ^ offset) for i in range(size)])]
    pallas_call x1 -> x2, Pallas kernels: 3.8 us -> 6.07 us  [early(): pl.pallas_call(with_table(early_panel_kernel, table, places, owners, bool...]
    pallas_call x3, Pallas kernels: 6.73 us -> 8.36 us  [shards(): pl.pallas_call(with_table(column_kernel, table), out_shape=(column_shape,...]
    unnamed x4 -> x6, local copies, waits for them, and re-layouts: 2.19 us -> 3.23 us
  transfers between devices with their start and end apart: 35 -> 31, of which waited for: 22 -> 20; matrix products, arithmetic and copies ran while one was open for 4% -> 3% of each run, Pallas kernels for 6% -> 7%
where the time goes in v13:
time: 137 us; the launch traced here: 136 us
  waiting for transfers between devices  47.5 us (35%)
  starting transfers between devices  39.6 us (29%)
  Pallas kernels  38 us (28%)
  local copies, waits for them, and re-layouts  4.41 us (3%)
  other arithmetic  4.4 us (3%)
  between operations  2.21 us (2%)
    ppermute x31, waiting for transfers between devices, swap(): return lax.ppermute(x, axis, [(i, i ^ offset) for i in range(size)])  47.5 us
    ppermute x31, starting transfers between devices, swap(): return lax.ppermute(x, axis, [(i, i ^ offset) for i in range(size)])  39.6 us
    pallas_call x2, Pallas kernels, shards(): pl.pallas_call(with_table(row_kernel, table, log_column), out_shape=row_s...  12.7 us
    pallas_call x3, Pallas kernels, shards(): pl.pallas_call(with_table(column_kernel, table), out_shape=(column_shape,...  8.36 us
    pallas_call x2, Pallas kernels, early(): pl.pallas_call(with_table(early_panel_kernel, table, places, owners, bool...  6.07 us
    pallas_call x1, Pallas kernels, late(): pl.pallas_call(with_table(panel_kernel, table, places, add), out_shape=(p...  4.36 us
    pallas_call x1, Pallas kernels, shards(): pl.pallas_call(with_table(rest_kernel, table, lines), out_shape=[block] *...  3.35 us
    unnamed x6, local copies, waits for them, and re-layouts  3.23 us
  transfers between devices with their start and end apart: 31, of which 20 were waited for; matrix products, arithmetic and copies ran while one was open for 3% of the time, Pallas kernels for 7%

profile of v13, /device:TPU:0, one launch (start us, length us, event | category | flops | bytes accessed | tf_op | source)
XLA Modules:
  0.0 136.0 jit_solution(12175459708302825624)
XLA Ops:
  0.6 3.0 %collective-permute-start.2 = (bf16[1024,256]{1,0:T(8,128)(2,1)}, bf16[1024,256]{1,0:T(8,128)(2,1)S(1)}, u32[]{:S(2)}, u32[]{:S(2)}) collective-permute-start(bf16[1024,256]{1,0:T(8,128)(2,1)} %refs_1_.1), channel_id=1, source_target_pairs={{0,16},{8,24},{16,0},{24,8},{1,17},{9,25},{17,1},{25,9},{2,18},{10... | collective-permute-start | bytes 1572872 | tf_op jit(solution)/shard_map/ppermute | solution.py:21
  3.7 1.5 %collective-permute-start.1 = (bf16[1024,256]{1,0:T(8,128)(2,1)}, bf16[1024,256]{1,0:T(8,128)(2,1)S(1)}, u32[]{:S(2)}, u32[]{:S(2)}) collective-permute-start(bf16[1024,256]{1,0:T(8,128)(2,1)} %refs_1_.1), channel_id=1, source_target_pairs={{0,8},{8,0},{16,24},{24,16},{1,9},{9,1},{17,25},{25,17},{2,10},{10... | collective-permute-start | bytes 1572872 | tf_op jit(solution)/shard_map/ppermute | solution.py:21
  5.7 0.7 compare_select_fusion.1
  6.4 0.9 collective-permute-done
  7.6 0.6 fusion.4
  10.3 0.6 select_reduce_fusion.1
  11.6 0.7 concatenate.25.hbm_ref
  12.4 2.2 %copy-done = bf16[2048,1024]{1,0:T(8,128)(2,1)S(1)} copy-done((bf16[2048,1024]{1,0:T(8,128)(2,1)S(1)}, bf16[2048,1024]{1,0:T(8,128)(2,1)}, u32[]{:S(2)}) %copy-start) | copy-done | bytes 4194328
  14.6 1.0 copy-done.2
  15.6 2.5 %early_panel.2 = (f32[257,128,128]{2,1,0:T(8,128)S(1)}, bf16[2048,1024]{1,0:T(8,128)(2,1)S(1)}) custom-call(s32[1284]{0:T(1024)S(1)} %concatenate.25.hbm_ref, bf16[2048,1024]{1,0:T(8,128)(2,1)S(1)} %copy-done, bf16[1024,256]{1,0:T(8,128)(2,1)S(1)} %copy-done.2, bf16[1024,256]{1,0:T(8,128)(2,1)S(1)} %collective-permute-done.3.refs_2_), custom_call_target="tpu_custom_call" | custom-call | flops 1073741824 | bytes 33554432 | tf_op jit(solution)/shard_map/early_panel/pallas_call | solution.py:497
  18.8 1.7 %collective-permute-start.5 = (bf16[512,256]{1,0:T(8,128)(2,1)S(1)}, bf16[512,256]{1,0:T(8,128)(2,1)S(1)}, u32[]{:S(2)}, u32[]{:S(2)}) collective-permute-start(bf16[512,256]{1,0:T(8,128)(2,1)S(1)} %slice.7), channel_id=1, source_target_pairs={{0,16},{8,24},{16,0},{24,8},{1,17},{9,25},{17,1},{25,9},{2,18},{10... | collective-permute-start | bytes 786440 | tf_op jit(solution)/shard_map/ppermute | solution.py:21
  20.9 3.6 %early_panel.3 = (f32[257,128,128]{2,1,0:T(8,128)S(1)}, bf16[2048,1024]{1,0:T(8,128)(2,1)S(1)}) custom-call(s32[1284]{0:T(1024)S(1)} %concatenate.25.hbm_ref, bf16[2048,1024]{1,0:T(8,128)(2,1)S(1)} %copy-done.1, bf16[1024,256]{1,0:T(8,128)(2,1)S(1)} %collective-permute-done.1.refs_1_, ...), custom_call_target="tpu_custom_call", output_to_operand_aliasing={{0}: (6, {}), {1}: (7, {})} | custom-call | flops 2147483648 | bytes 33554432 | tf_op jit(solution)/shard_map/early_panel/pallas_call | solution.py:497
  24.5 2.7 %collective-permute-done.5.refs_2_ = bf16[512,256]{1,0:T(8,128)(2,1)S(1)} collective-permute-done((bf16[512,256]{1,0:T(8,128)(2,1)S(1)}, bf16[512,256]{1,0:T(8,128)(2,1)S(1)}, u32[]{:S(2)}, u32[]{:S(2)}) %collective-permute-start.5) | collective-permute-done | bytes 262176 | tf_op jit(solution)/shard_map/ppermute | solution.py:21
  27.2 1.3 collective-permute-done.4.refs_1_
  29.0 1.0 collective-permute-done.8.refs_3_
  30.4 4.4 %panel.1 = (f32[257,128,128]{2,1,0:T(8,128)S(1)}, bf16[2048,1024]{1,0:T(8,128)(2,1)S(1)}, bf16[257,128,128]{2,1,0:T(8,128)(2,1)S(1)}, f32[16,128]{1,0:T(8,128)S(1)}, f32[16,128]{1,0:T(8,128)S(1)}) custom-call(s32[1284]{0:T(1024)S(1)} %concatenate.25.hbm_ref, bf16[2048,1024]{1,0:T(8,128)(2,1)S(1)} %copy-done.1, ...), custom_call_target="tpu_custom_call", output_to_operand_aliasing={{0}: (6, {}), {1}: (7, {})} | custom-call | tf_op jit(solution)/shard_map/panel/pallas_call | solution.py:476
  34.8 4.6 %collective-permute-start.12 = (f32[16,128]{1,0:T(8,128)S(1)}, f32[16,128]{1,0:T(8,128)S(1)}, u32[]{:S(2)}, u32[]{:S(2)}) collective-permute-start(f32[16,128]{1,0:T(8,128)S(1)} %get-tuple-element.46.refs_3_), channel_id=1, source_target_pairs={{0,6},{1,7},{2,4},{3,5},{4,2},{5,3},{6,0},{7,1},{8,14},{9,15},{10,... | collective-permute-start | bytes 24584 | tf_op jit(solution)/shard_map/ppermute | solution.py:21
  39.4 0.6 collective-permute-start.10
  40.1 1.0 collective-permute-done.12.refs_6_
  41.0 2.9 %collective-permute-done.11.refs_5_ = f32[16,128]{1,0:T(8,128)S(1)} collective-permute-done((f32[16,128]{1,0:T(8,128)S(1)}, f32[16,128]{1,0:T(8,128)S(1)}, u32[]{:S(2)}, u32[]{:S(2)}) %collective-permute-start.11) | collective-permute-done | bytes 8224 | tf_op jit(solution)/shard_map/ppermute | solution.py:21
  44.0 2.8 %column_pass.3 = (f32[16,128]{1,0:T(8,128)S(1)}, f32[16,128]{1,0:T(8,128)}, f32[16,128]{1,0:T(8,128)}) custom-call(s32[1284]{0:T(1024)S(1)} %concatenate.25.hbm_ref, f32[257,128,128]{2,1,0:T(8,128)S(1)} %get-tuple-element.43.refs_0_, bf16[257,128,128]{2,1,0:T(8,128)(2,1)S(1)} %get-tuple-element.44.refs_1_, f32[16,128]{1,0:T(8,128)S(1)} %get-tuple-element.45.refs_2_, ...), custom_call_target="tpu_custom_call" | custom-call | tf_op jit(solution)/shard_map/column_pass/pallas_call | solution.py:586
  46.8 3.4 %collective-permute-start.15 = (f32[16,128]{1,0:T(8,128)S(1)}, f32[16,128]{1,0:T(8,128)S(1)}, u32[]{:S(2)}, u32[]{:S(2)}) collective-permute-start(f32[16,128]{1,0:T(8,128)S(1)} %get-tuple-element.47.refs_3_), channel_id=1, source_target_pairs={{0,24},{8,16},{16,8},{24,0},{1,25},{9,17},{17,9},{25,1},{2,26},{10... | collective-permute-start | bytes 24584 | tf_op jit(solution)/shard_map/ppermute | solution.py:21
  50.2 0.6 collective-permute-start.13
  50.9 1.0 collective-permute-done.15.refs_6_
  51.8 2.0 %collective-permute-done.14.refs_5_ = f32[16,128]{1,0:T(8,128)S(1)} collective-permute-done((f32[16,128]{1,0:T(8,128)S(1)}, f32[16,128]{1,0:T(8,128)S(1)}, u32[]{:S(2)}, u32[]{:S(2)}) %collective-permute-start.14) | collective-permute-done | bytes 8224 | tf_op jit(solution)/shard_map/ppermute | solution.py:21
  53.9 6.4 %row_pass.2.refs_3_ = f32[16,128]{1,0:T(8,128)S(1)} custom-call(s32[1284]{0:T(1024)S(1)} %concatenate.25.hbm_ref, f32[257,128,128]{2,1,0:T(8,128)S(1)} %get-tuple-element.43.refs_0_, bf16[257,128,128]{2,1,0:T(8,128)(2,1)S(1)} %get-tuple-element.44.refs_1_, f32[16,128]{1,0:T(8,128)S(1)} %get-tuple-element.45.refs_2_, ...), custom_call_target="tpu_custom_call" | custom-call | tf_op jit(solution)/shard_map/row_pass/pallas_call | solution.py:576
  60.5 4.3 %collective-permute-start.16 = (f32[16,128]{1,0:T(8,128)S(1)}, f32[16,128]{1,0:T(8,128)S(1)}, u32[]{:S(2)}, u32[]{:S(2)}) collective-permute-start(f32[16,128]{1,0:T(8,128)S(1)} %row_pass.2.refs_3_), channel_id=1, source_target_pairs={{0,2},{1,3},{2,0},{3,1},{4,6},{5,7},{6,4},{7,5},{8,10},{9,11},{10,... | collective-permute-start | bytes 24584 | tf_op jit(solution)/shard_map/ppermute | solution.py:21
  64.8 1.1 collective-permute-done.18.refs_6_
  66.4 2.8 %column_pass.4 = (f32[16,128]{1,0:T(8,128)S(1)}, f32[16,128]{1,0:T(8,128)}, f32[16,128]{1,0:T(8,128)}) custom-call(s32[1284]{0:T(1024)S(1)} %concatenate.25.hbm_ref, f32[257,128,128]{2,1,0:T(8,128)S(1)} %get-tuple-element.43.refs_0_, bf16[257,128,128]{2,1,0:T(8,128)(2,1)S(1)} %get-tuple-element.44.refs_1_, f32[16,128]{1,0:T(8,128)S(1)} %get-tuple-element.45.refs_2_, ...), custom_call_target="tpu_custom_call" | custom-call | tf_op jit(solution)/shard_map/column_pass/pallas_call | solution.py:586
  69.2 3.3 %collective-permute-start.21 = (f32[16,128]{1,0:T(8,128)S(1)}, f32[16,128]{1,0:T(8,128)S(1)}, u32[]{:S(2)}, u32[]{:S(2)}) collective-permute-start(f32[16,128]{1,0:T(8,128)S(1)} %get-tuple-element.48.refs_3_), channel_id=1, source_target_pairs={{0,24},{8,16},{16,8},{24,0},{1,25},{9,17},{17,9},{25,1},{2,26},{10... | collective-permute-start | bytes 24584 | tf_op jit(solution)/shard_map/ppermute | solution.py:21
  73.0 1.4 %collective-permute-start.19 = (f32[16,128]{1,0:T(8,128)S(1)}, f32[16,128]{1,0:T(8,128)S(1)}, u32[]{:S(2)}, u32[]{:S(2)}) collective-permute-start(f32[16,128]{1,0:T(8,128)S(1)} %get-tuple-element.48.refs_3_), channel_id=1, source_target_pairs={{0,8},{8,0},{16,24},{24,16},{1,9},{9,1},{17,25},{25,17},{2,10},{10... | collective-permute-start | bytes 24584 | tf_op jit(solution)/shard_map/ppermute | solution.py:21
  74.4 1.7 %collective-permute-done.20.refs_5_ = f32[16,128]{1,0:T(8,128)S(1)} collective-permute-done((f32[16,128]{1,0:T(8,128)S(1)}, f32[16,128]{1,0:T(8,128)S(1)}, u32[]{:S(2)}, u32[]{:S(2)}) %collective-permute-start.20) | collective-permute-done | bytes 8224 | tf_op jit(solution)/shard_map/ppermute | solution.py:21
  76.6 6.3 %row_pass.3.refs_3_ = f32[16,128]{1,0:T(8,128)S(1)} custom-call(s32[1284]{0:T(1024)S(1)} %concatenate.25.hbm_ref, f32[257,128,128]{2,1,0:T(8,128)S(1)} %get-tuple-element.43.refs_0_, bf16[257,128,128]{2,1,0:T(8,128)(2,1)S(1)} %get-tuple-element.44.refs_1_, f32[16,128]{1,0:T(8,128)S(1)} %get-tuple-element.45.refs_2_, ...), custom_call_target="tpu_custom_call" | custom-call | tf_op jit(solution)/shard_map/row_pass/pallas_call | solution.py:576
  83.1 4.3 %collective-permute-start.22 = (f32[16,128]{1,0:T(8,128)S(1)}, f32[16,128]{1,0:T(8,128)S(1)}, u32[]{:S(2)}, u32[]{:S(2)}) collective-permute-start(f32[16,128]{1,0:T(8,128)S(1)} %row_pass.3.refs_3_), channel_id=1, source_target_pairs={{0,2},{1,3},{2,0},{3,1},{4,6},{5,7},{6,4},{7,5},{8,10},{9,11},{10,... | collective-permute-start | bytes 24584 | tf_op jit(solution)/shard_map/ppermute | solution.py:21
  87.4 1.1 collective-permute-done.24.refs_6_
  89.0 2.8 %column_pass.5 = (f32[16,128]{1,0:T(8,128)S(1)}, f32[16,128]{1,0:T(8,128)S(1)}, f32[16,128]{1,0:T(8,128)}) custom-call(s32[1284]{0:T(1024)S(1)} %concatenate.25.hbm_ref, f32[257,128,128]{2,1,0:T(8,128)S(1)} %get-tuple-element.43.refs_0_, bf16[257,128,128]{2,1,0:T(8,128)(2,1)S(1)} %get-tuple-element.44.refs_1_, f32[16,128]{1,0:T(8,128)S(1)} %get-tuple-element.45.refs_2_, ...), custom_call_target="tpu_custom_call" | custom-call | tf_op jit(solution)/shard_map/column_pass/pallas_call | solution.py:586
  91.8 4.3 %collective-permute-start.27 = (f32[16,128]{1,0:T(8,128)S(1)}, f32[16,128]{1,0:T(8,128)S(1)}, u32[]{:S(2)}, u32[]{:S(2)}) collective-permute-start(f32[16,128]{1,0:T(8,128)S(1)} %get-tuple-element.51.refs_3_), channel_id=1, source_target_pairs={{0,24},{8,16},{16,8},{24,0},{1,25},{9,17},{17,9},{25,1},{2,26},{10... | collective-permute-start | bytes 24584 | tf_op jit(solution)/shard_map/ppermute | solution.py:21
  96.1 0.6 collective-permute-start.25
  96.8 1.0 collective-permute-done.27.refs_6_
  97.8 2.0 %collective-permute-done.26.refs_5_ = f32[16,128]{1,0:T(8,128)S(1)} collective-permute-done((f32[16,128]{1,0:T(8,128)S(1)}, f32[16,128]{1,0:T(8,128)S(1)}, u32[]{:S(2)}, u32[]{:S(2)}) %collective-permute-start.26) | collective-permute-done | bytes 8224 | tf_op jit(solution)/shard_map/ppermute | solution.py:21
  99.8 3.1 %plan.1 = (bf16[2048,128]{1,0:T(8,128)(2,1)S(1)}, bf16[33,512,256]{2,1,0:T(8,128)(2,1)S(1)}, f32[8,128]{1,0:T(8,128)}) custom-call(s32[1284]{0:T(1024)S(1)} %concatenate.25.hbm_ref, f32[257,128,128]{2,1,0:T(8,128)S(1)} %get-tuple-element.43.refs_0_, f32[16,128]{1,0:T(8,128)S(1)} %get-tuple-element.49.refs_1_, ...), custom_call_target="tpu_custom_call" | custom-call | tf_op jit(solution)/shard_map/plan/pallas_call | solution.py:602
  103.0 2.0 %collective-permute-start.29 = (bf16[2048,128]{1,0:T(8,128)(2,1)S(1)}, bf16[2048,128]{1,0:T(8,128)(2,1)S(1)}, u32[]{:S(2)}, u32[]{:S(2)}) collective-permute-start(bf16[2048,128]{1,0:T(8,128)(2,1)S(1)} %get-tuple-element.56), channel_id=1, source_target_pairs={{0,2},{1,3},{2,0},{3,1},{4,6},{5,7},{6,4},{7,5},{8,10},{9,11},{10,... | collective-permute-start | bytes 1572872 | tf_op jit(solution)/shard_map/ppermute | solution.py:21
  104.9 3.3 %rest_of_plan.1 = (bf16[2048,128]{1,0:T(8,128)(2,1)S(1)}, bf16[2048,128]{1,0:T(8,128)(2,1)S(1)}, bf16[2048,128]{1,0:T(8,128)(2,1)S(1)}) custom-call(s32[1284]{0:T(1024)S(1)} %concatenate.25.hbm_ref, bf16[33,512,256]{2,1,0:T(8,128)(2,1)S(1)} %get-tuple-element.52.refs_0_, bf16[2048,1024]{1,0:T(8,128)(2,1)S(1)} %get-tuple-element.50.refs_2_.refs_1_), custom_call_target="tpu_custom_call" | custom-call | flops 3221225472 | bytes 16777216 | tf_op jit(solution)/shard_map/rest_of_plan/pallas_call | solution.py:616
  108.3 0.7 collective-permute-start.28
  109.0 10.1 %collective-permute-done.29 = bf16[2048,128]{1,0:T(8,128)(2,1)S(1)} collective-permute-done((bf16[2048,128]{1,0:T(8,128)(2,1)S(1)}, bf16[2048,128]{1,0:T(8,128)(2,1)S(1)}, u32[]{:S(2)}, u32[]{:S(2)}) %collective-permute-start.29) | collective-permute-done | bytes 524320 | tf_op jit(solution)/shard_map/ppermute | solution.py:21
  119.5 6.6 %collective-permute-done.28 = bf16[2048,128]{1,0:T(8,128)(2,1)S(1)} collective-permute-done((bf16[2048,128]{1,0:T(8,128)(2,1)S(1)}, bf16[2048,128]{1,0:T(8,128)(2,1)S(1)}, u32[]{:S(2)}, u32[]{:S(2)}) %collective-permute-start.28) | collective-permute-done | bytes 524320 | tf_op jit(solution)/shard_map/ppermute | solution.py:21
  126.1 9.0 %collective-permute-done.30 = bf16[2048,128]{1,0:T(8,128)(2,1)S(1)} collective-permute-done((bf16[2048,128]{1,0:T(8,128)(2,1)S(1)}, bf16[2048,128]{1,0:T(8,128)(2,1)S(1)}, u32[]{:S(2)}, u32[]{:S(2)}) %collective-permute-start.30) | collective-permute-done | bytes 524320 | tf_op jit(solution)/shard_map/ppermute | solution.py:21
  135.0 1.0 add_convert_fusion
  (64 shorter events, 7.1 us)
Async XLA Ops:
  0.6 17.5 %collective-permute-start.2 = (bf16[1024,256]{1,0:T(8,128)(2,1)}, bf16[1024,256]{1,0:T(8,128)(2,1)S(1)}, u32[]{:S(2)}, u32[]{:S(2)}) collective-permute-start(bf16[1024,256]{1,0:T(8,128)(2,1)} %refs_1_.1), channel_id=1, source_target_pairs={{0,16},{8,24},{16,0},{24,8},{1,17},{9,25},{17,1},{25,9},{2,18},{10... | collective-permute-start | bytes 1572872 | tf_op jit(solution)/shard_map/ppermute | solution.py:21
  3.7 14.5 %collective-permute-start.1 = (bf16[1024,256]{1,0:T(8,128)(2,1)}, bf16[1024,256]{1,0:T(8,128)(2,1)S(1)}, u32[]{:S(2)}, u32[]{:S(2)}) collective-permute-start(bf16[1024,256]{1,0:T(8,128)(2,1)} %refs_1_.1), channel_id=1, source_target_pairs={{0,8},{8,0},{16,24},{24,16},{1,9},{9,1},{17,25},{25,17},{2,10},{10... | collective-permute-start | bytes 1572872 | tf_op jit(solution)/shard_map/ppermute | solution.py:21
  5.2 7.2 %collective-permute-start.3 = (bf16[1024,256]{1,0:T(8,128)(2,1)}, bf16[1024,256]{1,0:T(8,128)(2,1)S(1)}, u32[]{:S(2)}, u32[]{:S(2)}) collective-permute-start(bf16[1024,256]{1,0:T(8,128)(2,1)} %refs_1_.1), channel_id=1, source_target_pairs={{0,1},{1,0},{2,3},{3,2},{4,5},{5,4},{6,7},{7,6},{8,9},{9,8},{10,11... | collective-permute-start | bytes 1572872 | tf_op jit(solution)/shard_map/ppermute | solution.py:21
  5.2 2.1 %collective-permute-start = (s32[16,8]{0,1:T(8,128)}, s32[16,8]{0,1:T(8,128)S(1)}, u32[]{:S(2)}, u32[]{:S(2)}) collective-permute-start(s32[16,8]{0,1:T(8,128)} %param.5), channel_id=1, source_target_pairs={{0,1},{1,0},{2,3},{3,2},{4,5},{5,4},{6,7},{7,6},{8,9},{9,8},{10,11... | collective-permute-start | bytes 1544 | tf_op jit(solution)/shard_map/ppermute | solution.py:21
  12.4 2.2 %copy-start = (bf16[2048,1024]{1,0:T(8,128)(2,1)S(1)}, bf16[2048,1024]{1,0:T(8,128)(2,1)}, u32[]{:S(2)}) copy-start(bf16[2048,1024]{1,0:T(8,128)(2,1)} %refs_0_.5) | copy-start | bytes 12582916
  14.6 1.0 copy-start.2
  15.6 5.3 %copy-start.1 = (bf16[2048,1024]{1,0:T(8,128)(2,1)S(1)}, bf16[2048,1024]{1,0:T(8,128)(2,1)}, u32[]{:S(2)}) copy-start(bf16[2048,1024]{1,0:T(8,128)(2,1)} %refs_0_.5) | copy-start | bytes 12582916
  18.1 2.8 %collective-permute-start.7 = (bf16[1024,256]{1,0:T(8,128)(2,1)S(1)}, bf16[1024,256]{1,0:T(8,128)(2,1)S(1)}, u32[]{:S(2)}, u32[]{:S(2)}) collective-permute-start(bf16[1024,256]{1,0:T(8,128)(2,1)S(1)} %collective-permute-done.2.refs_2_), channel_id=1, source_target_pairs={{0,1},{1,0},{2,3},{3,2},{4,5},{5,4},{6,7},{7,6},{8,9},{9,8},{10,11... | collective-permute-start | bytes 1572872 | tf_op jit(solution)/shard_map/ppermute | solution.py:21
  18.3 2.6 %collective-permute-start.6 = (bf16[1024,256]{1,0:T(8,128)(2,1)S(1)}, bf16[1024,256]{1,0:T(8,128)(2,1)S(1)}, u32[]{:S(2)}, u32[]{:S(2)}) collective-permute-start(bf16[1024,256]{1,0:T(8,128)(2,1)S(1)} %collective-permute-done.1.refs_1_), channel_id=1, source_target_pairs={{0,1},{1,0},{2,3},{3,2},{4,5},{5,4},{6,7},{7,6},{8,9},{9,8},{10,11... | collective-permute-start | bytes 1572872 | tf_op jit(solution)/shard_map/ppermute | solution.py:21
  18.8 8.4 %collective-permute-start.5 = (bf16[512,256]{1,0:T(8,128)(2,1)S(1)}, bf16[512,256]{1,0:T(8,128)(2,1)S(1)}, u32[]{:S(2)}, u32[]{:S(2)}) collective-permute-start(bf16[512,256]{1,0:T(8,128)(2,1)S(1)} %slice.7), channel_id=1, source_target_pairs={{0,16},{8,24},{16,0},{24,8},{1,17},{9,25},{17,1},{25,9},{2,18},{10... | collective-permute-start | bytes 786440 | tf_op jit(solution)/shard_map/ppermute | solution.py:21
  20.4 8.1 %collective-permute-start.4 = (bf16[512,256]{1,0:T(8,128)(2,1)S(1)}, bf16[512,256]{1,0:T(8,128)(2,1)S(1)}, u32[]{:S(2)}, u32[]{:S(2)}) collective-permute-start(bf16[512,256]{1,0:T(8,128)(2,1)S(1)} %slice.6), channel_id=1, source_target_pairs={{0,8},{8,0},{16,24},{24,16},{1,9},{9,1},{17,25},{25,17},{2,10},{10... | collective-permute-start | bytes 786440 | tf_op jit(solution)/shard_map/ppermute | solution.py:21
  28.5 1.5 %collective-permute-start.8 = (bf16[512,256]{1,0:T(8,128)(2,1)S(1)}, bf16[512,256]{1,0:T(8,128)(2,1)S(1)}, u32[]{:S(2)}, u32[]{:S(2)}) collective-permute-start(bf16[512,256]{1,0:T(8,128)(2,1)S(1)} %collective-permute-done.4.refs_1_), channel_id=1, source_target_pairs={{0,1},{1,0},{2,3},{3,2},{4,5},{5,4},{6,7},{7,6},{8,9},{9,8},{10,11... | collective-permute-start | bytes 786440 | tf_op jit(solution)/shard_map/ppermute | solution.py:21
  28.5 1.9 %collective-permute-start.9 = (bf16[512,256]{1,0:T(8,128)(2,1)S(1)}, bf16[512,256]{1,0:T(8,128)(2,1)S(1)}, u32[]{:S(2)}, u32[]{:S(2)}) collective-permute-start(bf16[512,256]{1,0:T(8,128)(2,1)S(1)} %collective-permute-done.5.refs_2_), channel_id=1, source_target_pairs={{0,1},{1,0},{2,3},{3,2},{4,5},{5,4},{6,7},{7,6},{8,9},{9,8},{10,11... | collective-permute-start | bytes 786440 | tf_op jit(solution)/shard_map/ppermute | solution.py:21
  34.8 6.3 %collective-permute-start.12 = (f32[16,128]{1,0:T(8,128)S(1)}, f32[16,128]{1,0:T(8,128)S(1)}, u32[]{:S(2)}, u32[]{:S(2)}) collective-permute-start(f32[16,128]{1,0:T(8,128)S(1)} %get-tuple-element.46.refs_3_), channel_id=1, source_target_pairs={{0,6},{1,7},{2,4},{3,5},{4,2},{5,3},{6,0},{7,1},{8,14},{9,15},{10,... | collective-permute-start | bytes 24584 | tf_op jit(solution)/shard_map/ppermute | solution.py:21
  39.4 4.5 %collective-permute-start.11 = (f32[16,128]{1,0:T(8,128)S(1)}, f32[16,128]{1,0:T(8,128)S(1)}, u32[]{:S(2)}, u32[]{:S(2)}) collective-permute-start(f32[16,128]{1,0:T(8,128)S(1)} %get-tuple-element.46.refs_3_), channel_id=1, source_target_pairs={{0,4},{1,5},{2,6},{3,7},{4,0},{5,1},{6,2},{7,3},{8,12},{9,13},{10,... | collective-permute-start | bytes 24584 | tf_op jit(solution)/shard_map/ppermute | solution.py:21
  39.4 4.5 %collective-permute-start.10 = (f32[16,128]{1,0:T(8,128)S(1)}, f32[16,128]{1,0:T(8,128)S(1)}, u32[]{:S(2)}, u32[]{:S(2)}) collective-permute-start(f32[16,128]{1,0:T(8,128)S(1)} %get-tuple-element.46.refs_3_), channel_id=1, source_target_pairs={{0,2},{1,3},{2,0},{3,1},{4,6},{5,7},{6,4},{7,5},{8,10},{9,11},{10,... | collective-permute-start | bytes 24584 | tf_op jit(solution)/shard_map/ppermute | solution.py:21
  46.8 5.1 %collective-permute-start.15 = (f32[16,128]{1,0:T(8,128)S(1)}, f32[16,128]{1,0:T(8,128)S(1)}, u32[]{:S(2)}, u32[]{:S(2)}) collective-permute-start(f32[16,128]{1,0:T(8,128)S(1)} %get-tuple-element.47.refs_3_), channel_id=1, source_target_pairs={{0,24},{8,16},{16,8},{24,0},{1,25},{9,17},{17,9},{25,1},{2,26},{10... | collective-permute-start | bytes 24584 | tf_op jit(solution)/shard_map/ppermute | solution.py:21
  50.2 3.7 %collective-permute-start.14 = (f32[16,128]{1,0:T(8,128)S(1)}, f32[16,128]{1,0:T(8,128)S(1)}, u32[]{:S(2)}, u32[]{:S(2)}) collective-permute-start(f32[16,128]{1,0:T(8,128)S(1)} %get-tuple-element.47.refs_3_), channel_id=1, source_target_pairs={{0,16},{8,24},{16,0},{24,8},{1,17},{9,25},{17,1},{25,9},{2,18},{10... | collective-permute-start | bytes 24584 | tf_op jit(solution)/shard_map/ppermute | solution.py:21
  50.2 3.7 %collective-permute-start.13 = (f32[16,128]{1,0:T(8,128)S(1)}, f32[16,128]{1,0:T(8,128)S(1)}, u32[]{:S(2)}, u32[]{:S(2)}) collective-permute-start(f32[16,128]{1,0:T(8,128)S(1)} %get-tuple-element.47.refs_3_), channel_id=1, source_target_pairs={{0,8},{8,0},{16,24},{24,16},{1,9},{9,1},{17,25},{25,17},{2,10},{10... | collective-permute-start | bytes 24584 | tf_op jit(solution)/shard_map/ppermute | solution.py:21
  60.3 5.5 %collective-permute-start.18 = (f32[16,128]{1,0:T(8,128)S(1)}, f32[16,128]{1,0:T(8,128)S(1)}, u32[]{:S(2)}, u32[]{:S(2)}) collective-permute-start(f32[16,128]{1,0:T(8,128)S(1)} %row_pass.2.refs_3_), channel_id=1, source_target_pairs={{0,6},{1,7},{2,4},{3,5},{4,2},{5,3},{6,0},{7,1},{8,14},{9,15},{10,... | collective-permute-start | bytes 24584 | tf_op jit(solution)/shard_map/ppermute | solution.py:21
  60.4 5.4 %collective-permute-start.17 = (f32[16,128]{1,0:T(8,128)S(1)}, f32[16,128]{1,0:T(8,128)S(1)}, u32[]{:S(2)}, u32[]{:S(2)}) collective-permute-start(f32[16,128]{1,0:T(8,128)S(1)} %row_pass.2.refs_3_), channel_id=1, source_target_pairs={{0,4},{1,5},{2,6},{3,7},{4,0},{5,1},{6,2},{7,3},{8,12},{9,13},{10,... | collective-permute-start | bytes 24584 | tf_op jit(solution)/shard_map/ppermute | solution.py:21
  60.5 5.9 %collective-permute-start.16 = (f32[16,128]{1,0:T(8,128)S(1)}, f32[16,128]{1,0:T(8,128)S(1)}, u32[]{:S(2)}, u32[]{:S(2)}) collective-permute-start(f32[16,128]{1,0:T(8,128)S(1)} %row_pass.2.refs_3_), channel_id=1, source_target_pairs={{0,2},{1,3},{2,0},{3,1},{4,6},{5,7},{6,4},{7,5},{8,10},{9,11},{10,... | collective-permute-start | bytes 24584 | tf_op jit(solution)/shard_map/ppermute | solution.py:21
  69.2 5.2 %collective-permute-start.21 = (f32[16,128]{1,0:T(8,128)S(1)}, f32[16,128]{1,0:T(8,128)S(1)}, u32[]{:S(2)}, u32[]{:S(2)}) collective-permute-start(f32[16,128]{1,0:T(8,128)S(1)} %get-tuple-element.48.refs_3_), channel_id=1, source_target_pairs={{0,24},{8,16},{16,8},{24,0},{1,25},{9,17},{17,9},{25,1},{2,26},{10... | collective-permute-start | bytes 24584 | tf_op jit(solution)/shard_map/ppermute | solution.py:21
  72.5 3.7 %collective-permute-start.20 = (f32[16,128]{1,0:T(8,128)S(1)}, f32[16,128]{1,0:T(8,128)S(1)}, u32[]{:S(2)}, u32[]{:S(2)}) collective-permute-start(f32[16,128]{1,0:T(8,128)S(1)} %get-tuple-element.48.refs_3_), channel_id=1, source_target_pairs={{0,16},{8,24},{16,0},{24,8},{1,17},{9,25},{17,1},{25,9},{2,18},{10... | collective-permute-start | bytes 24584 | tf_op jit(solution)/shard_map/ppermute | solution.py:21
  73.0 3.7 %collective-permute-start.19 = (f32[16,128]{1,0:T(8,128)S(1)}, f32[16,128]{1,0:T(8,128)S(1)}, u32[]{:S(2)}, u32[]{:S(2)}) collective-permute-start(f32[16,128]{1,0:T(8,128)S(1)} %get-tuple-element.48.refs_3_), channel_id=1, source_target_pairs={{0,8},{8,0},{16,24},{24,16},{1,9},{9,1},{17,25},{25,17},{2,10},{10... | collective-permute-start | bytes 24584 | tf_op jit(solution)/shard_map/ppermute | solution.py:21
  82.9 5.5 %collective-permute-start.24 = (f32[16,128]{1,0:T(8,128)S(1)}, f32[16,128]{1,0:T(8,128)S(1)}, u32[]{:S(2)}, u32[]{:S(2)}) collective-permute-start(f32[16,128]{1,0:T(8,128)S(1)} %row_pass.3.refs_3_), channel_id=1, source_target_pairs={{0,6},{1,7},{2,4},{3,5},{4,2},{5,3},{6,0},{7,1},{8,14},{9,15},{10,... | collective-permute-start | bytes 24584 | tf_op jit(solution)/shard_map/ppermute | solution.py:21
  83.0 5.4 %collective-permute-start.23 = (f32[16,128]{1,0:T(8,128)S(1)}, f32[16,128]{1,0:T(8,128)S(1)}, u32[]{:S(2)}, u32[]{:S(2)}) collective-permute-start(f32[16,128]{1,0:T(8,128)S(1)} %row_pass.3.refs_3_), channel_id=1, source_target_pairs={{0,4},{1,5},{2,6},{3,7},{4,0},{5,1},{6,2},{7,3},{8,12},{9,13},{10,... | collective-permute-start | bytes 24584 | tf_op jit(solution)/shard_map/ppermute | solution.py:21
  83.1 5.9 %collective-permute-start.22 = (f32[16,128]{1,0:T(8,128)S(1)}, f32[16,128]{1,0:T(8,128)S(1)}, u32[]{:S(2)}, u32[]{:S(2)}) collective-permute-start(f32[16,128]{1,0:T(8,128)S(1)} %row_pass.3.refs_3_), channel_id=1, source_target_pairs={{0,2},{1,3},{2,0},{3,1},{4,6},{5,7},{6,4},{7,5},{8,10},{9,11},{10,... | collective-permute-start | bytes 24584 | tf_op jit(solution)/shard_map/ppermute | solution.py:21
  91.8 6.0 %collective-permute-start.27 = (f32[16,128]{1,0:T(8,128)S(1)}, f32[16,128]{1,0:T(8,128)S(1)}, u32[]{:S(2)}, u32[]{:S(2)}) collective-permute-start(f32[16,128]{1,0:T(8,128)S(1)} %get-tuple-element.51.refs_3_), channel_id=1, source_target_pairs={{0,24},{8,16},{16,8},{24,0},{1,25},{9,17},{17,9},{25,1},{2,26},{10... | collective-permute-start | bytes 24584 | tf_op jit(solution)/shard_map/ppermute | solution.py:21
  96.1 3.7 %collective-permute-start.26 = (f32[16,128]{1,0:T(8,128)S(1)}, f32[16,128]{1,0:T(8,128)S(1)}, u32[]{:S(2)}, u32[]{:S(2)}) collective-permute-start(f32[16,128]{1,0:T(8,128)S(1)} %get-tuple-element.51.refs_3_), channel_id=1, source_target_pairs={{0,16},{8,24},{16,0},{24,8},{1,17},{9,25},{17,1},{25,9},{2,18},{10... | collective-permute-start | bytes 24584 | tf_op jit(solution)/shard_map/ppermute | solution.py:21
  96.1 3.7 %collective-permute-start.25 = (f32[16,128]{1,0:T(8,128)S(1)}, f32[16,128]{1,0:T(8,128)S(1)}, u32[]{:S(2)}, u32[]{:S(2)}) collective-permute-start(f32[16,128]{1,0:T(8,128)S(1)} %get-tuple-element.51.refs_3_), channel_id=1, source_target_pairs={{0,8},{8,0},{16,24},{24,16},{1,9},{9,1},{17,25},{25,17},{2,10},{10... | collective-permute-start | bytes 24584 | tf_op jit(solution)/shard_map/ppermute | solution.py:21
  103.0 16.1 %collective-permute-start.29 = (bf16[2048,128]{1,0:T(8,128)(2,1)S(1)}, bf16[2048,128]{1,0:T(8,128)(2,1)S(1)}, u32[]{:S(2)}, u32[]{:S(2)}) collective-permute-start(bf16[2048,128]{1,0:T(8,128)(2,1)S(1)} %get-tuple-element.56), channel_id=1, source_target_pairs={{0,2},{1,3},{2,0},{3,1},{4,6},{5,7},{6,4},{7,5},{8,10},{9,11},{10,... | collective-permute-start | bytes 1572872 | tf_op jit(solution)/shard_map/ppermute | solution.py:21
  108.3 17.8 %collective-permute-start.28 = (bf16[2048,128]{1,0:T(8,128)(2,1)S(1)}, bf16[2048,128]{1,0:T(8,128)(2,1)S(1)}, u32[]{:S(2)}, u32[]{:S(2)}) collective-permute-start(bf16[2048,128]{1,0:T(8,128)(2,1)S(1)} %get-tuple-element.54), channel_id=1, source_target_pairs={{0,2},{1,3},{2,0},{3,1},{4,6},{5,7},{6,4},{7,5},{8,10},{9,11},{10,... | collective-permute-start | bytes 1572872 | tf_op jit(solution)/shard_map/ppermute | solution.py:21
  119.2 15.8 %collective-permute-start.30 = (bf16[2048,128]{1,0:T(8,128)(2,1)S(1)}, bf16[2048,128]{1,0:T(8,128)(2,1)S(1)}, u32[]{:S(2)}, u32[]{:S(2)}) collective-permute-start(bf16[2048,128]{1,0:T(8,128)(2,1)S(1)} %add_convert_fusion.1), channel_id=1, source_target_pairs={{0,4},{1,5},{2,6},{3,7},{4,0},{5,1},{6,2},{7,3},{8,12},{9,13},{10,... | collective-permute-start | bytes 1572872 | tf_op jit(solution)/shard_map/ppermute | solution.py:21

commit v14 on v13

--- a/solution.py
+++ b/solution.py
@@ -33,6 +33,8 @@
 
 
 class Table:
+    together = 4
+
     def __init__(self, row_tiles, columns):
         self.row_tiles, self.columns = row_tiles, columns
         self.line = max(row_tiles, columns) + 8
@@ -41,7 +43,8 @@
         self.mask_at = (self.pair_base + columns // 2) * self.line
         self.item_at = self.mask_at + row_tiles * columns
         self.items = (columns // 2) * -(-row_tiles // 4)
-        self.total_at = self.item_at + 2 * (self.items + 1)
+        self.slots = self.items + self.together - 1
+        self.total_at = self.item_at + 2 * self.slots
         self.dummy = row_tiles * columns
 
     def build(self, mask):
@@ -53,26 +56,27 @@
         at = jnp.arange(self.columns // 2, dtype=jnp.int32)
         first = jnp.sum(jnp.where(at[None, :] < at[:, None], steps[None, :], 0), axis=1)
         total = jnp.sum(steps)
-        item = jnp.minimum(jnp.arange(self.items + 1, dtype=jnp.int32), total - 1)
+        item = jnp.minimum(jnp.arange(self.slots, dtype=jnp.int32), total - 1)
         pair = jnp.sum(jnp.where(item[:, None] >= (first + steps)[None, :], 1, 0), axis=1)
         step = item - jnp.sum(jnp.where(pair[:, None] == at[None, :], first[None, :], 0), axis=1)
         flat += [(self.pair_base + pair) * self.line + 4 * step, pair]
-        return jnp.concatenate(flat + [jnp.stack([total, (total + 1) // 2])])
+        rounds = (total + self.together - 1) // self.together
+        return jnp.concatenate(flat + [jnp.stack([total, rounds])])
 
     def each_item(self, ref, visit):
-        def two(k, carry):
-            for i in range(2):
-                number = 2 * k + i
+        def several(k, carry):
+            for i in range(self.together):
+                number = self.together * k + i
                 at = ref[self.item_at + number]
                 visit(
                     number,
                     number < ref[self.total_at],
-                    ref[self.item_at + self.items + 1 + number],
+                    ref[self.item_at + self.slots + number],
                     [ref[at + n] for n in range(4)],
                 )
             return carry
 
-        lax.fori_loop(0, ref[self.total_at + 1], two, 0)
+        lax.fori_loop(0, ref[self.total_at + 1], several, 0)
 
     def empty_bits(self, ref, base, count):
         bits = jnp.int32(0)
@@ -603,7 +607,7 @@
         with_table(plan_kernel, table, log_column, lines),
         out_shape=[
             block,
-            pltpu.VMEM((table.items + 1, 4 * TILE, 2 * TILE), jnp.bfloat16),
+            pltpu.VMEM((table.slots, 4 * TILE, 2 * TILE), jnp.bfloat16),
             jax.ShapeDtypeStruct((half, TILE), jnp.float32),
         ],
         in_specs=[ANY] + [VMEM] * (3 + len(parts)),

time: 137 us -> 135 us (0.985); the launches traced: 136 us -> 136 us
  Pallas kernels: 38 us -> 30.3 us
  waiting for transfers between devices: 47.5 us -> 51.2 us
  starting transfers between devices: 39.6 us -> 43.3 us
    pallas_call x2, Pallas kernels: 12.7 us -> 3.63 us  [shards(): pl.pallas_call(with_table(row_kernel, table, log_column), out_shape=row_s...]
    ppermute x31, waiting for transfers between devices: 47.5 us -> 51.2 us  [swap(): return lax.ppermute(x, axis, [(i, i ^ offset) for i in range(size)])]
    ppermute x31, starting transfers between devices: 39.6 us -> 43.3 us  [swap(): return lax.ppermute(x, axis, [(i, i ^ offset) for i in range(size)])]
    pallas_call x3, Pallas kernels: 8.36 us -> 6.81 us  [shards(): pl.pallas_call(with_table(column_kernel, table), out_shape=(column_shape,...]
  transfers between devices with their start and end apart: 31 -> 31, of which waited for: 20 -> 21; matrix products, arithmetic and copies ran while one was open for 3% -> 3% of each run, Pallas kernels for 7% -> 8%
where the time goes in v14:
time: 135 us; the launch traced here: 136 us
  waiting for transfers between devices  51.2 us (38%)
  starting transfers between devices  43.3 us (32%)
  Pallas kernels  30.3 us (22%)
  local copies, waits for them, and re-layouts  4.41 us (3%)
  other arithmetic  4.4 us (3%)
  between operations  2.18 us (2%)
    ppermute x31, waiting for transfers between devices, swap(): return lax.ppermute(x, axis, [(i, i ^ offset) for i in range(size)])  51.2 us
    ppermute x31, starting transfers between devices, swap(): return lax.ppermute(x, axis, [(i, i ^ offset) for i in range(size)])  43.3 us
    pallas_call x2, Pallas kernels, early(): pl.pallas_call(with_table(early_panel_kernel, table, places, owners, bool...  7.1 us
    pallas_call x3, Pallas kernels, shards(): pl.pallas_call(with_table(column_kernel, table), out_shape=(column_shape,...  6.81 us
    pallas_call x1, Pallas kernels, late(): pl.pallas_call(with_table(panel_kernel, table, places, add), out_shape=(p...  5.01 us
    pallas_call x1, Pallas kernels, shards(): pl.pallas_call(with_table(rest_kernel, table, lines), out_shape=[block] *...  4.03 us
    pallas_call x1, Pallas kernels, shards(): pl.pallas_call(with_table(plan_kernel, table, log_column, lines), out_sha...  3.71 us
    pallas_call x2, Pallas kernels, shards(): pl.pallas_call(with_table(row_kernel, table, log_column), out_shape=row_s...  3.63 us
  transfers between devices with their start and end apart: 31, of which 21 were waited for; matrix products, arithmetic and copies ran while one was open for 3% of the time, Pallas kernels for 8%

profile of v14, /device:TPU:0, one launch (start us, length us, event | category | flops | bytes accessed | tf_op | source)
XLA Modules:
  0.0 135.8 jit_solution(15889066652111874963)
XLA Ops:
  0.6 3.0 %collective-permute-start.2 = (bf16[1024,256]{1,0:T(8,128)(2,1)}, bf16[1024,256]{1,0:T(8,128)(2,1)S(1)}, u32[]{:S(2)}, u32[]{:S(2)}) collective-permute-start(bf16[1024,256]{1,0:T(8,128)(2,1)} %refs_1_.1), channel_id=1, source_target_pairs={{0,16},{8,24},{16,0},{24,8},{1,17},{9,25},{17,1},{25,9},{2,18},{10... | collective-permute-start | bytes 1572872 | tf_op jit(solution)/shard_map/ppermute | solution.py:21
  3.7 1.5 %collective-permute-start.1 = (bf16[1024,256]{1,0:T(8,128)(2,1)}, bf16[1024,256]{1,0:T(8,128)(2,1)S(1)}, u32[]{:S(2)}, u32[]{:S(2)}) collective-permute-start(bf16[1024,256]{1,0:T(8,128)(2,1)} %refs_1_.1), channel_id=1, source_target_pairs={{0,8},{8,0},{16,24},{24,16},{1,9},{9,1},{17,25},{25,17},{2,10},{10... | collective-permute-start | bytes 1572872 | tf_op jit(solution)/shard_map/ppermute | solution.py:21
  5.7 0.7 compare_select_fusion.1
  6.4 0.9 collective-permute-done
  11.6 0.7 concatenate.25.hbm_ref
  12.4 2.2 %copy-done = bf16[2048,1024]{1,0:T(8,128)(2,1)S(1)} copy-done((bf16[2048,1024]{1,0:T(8,128)(2,1)S(1)}, bf16[2048,1024]{1,0:T(8,128)(2,1)}, u32[]{:S(2)}) %copy-start) | copy-done | bytes 4194328
  14.6 1.0 copy-done.2
  15.6 2.8 %early_panel.2 = (f32[257,128,128]{2,1,0:T(8,128)S(1)}, bf16[2048,1024]{1,0:T(8,128)(2,1)S(1)}) custom-call(s32[1288]{0:T(1024)S(1)} %concatenate.25.hbm_ref, bf16[2048,1024]{1,0:T(8,128)(2,1)S(1)} %copy-done, bf16[1024,256]{1,0:T(8,128)(2,1)S(1)} %copy-done.2, bf16[1024,256]{1,0:T(8,128)(2,1)S(1)} %collective-permute-done.3.refs_2_), custom_call_target="tpu_custom_call" | custom-call | flops 1073741824 | bytes 33554432 | tf_op jit(solution)/shard_map/early_panel/pallas_call | solution.py:501
  19.1 1.1 collective-permute-start.5
  20.2 0.7 collective-permute-start.4
  21.2 4.3 %early_panel.3 = (f32[257,128,128]{2,1,0:T(8,128)S(1)}, bf16[2048,1024]{1,0:T(8,128)(2,1)S(1)}) custom-call(s32[1288]{0:T(1024)S(1)} %concatenate.25.hbm_ref, bf16[2048,1024]{1,0:T(8,128)(2,1)S(1)} %copy-done.1, bf16[1024,256]{1,0:T(8,128)(2,1)S(1)} %collective-permute-done.1.refs_1_, ...), custom_call_target="tpu_custom_call", output_to_operand_aliasing={{0}: (6, {}), {1}: (7, {})} | custom-call | flops 2147483648 | bytes 33554432 | tf_op jit(solution)/shard_map/early_panel/pallas_call | solution.py:501
  25.5 2.0 %collective-permute-done.5.refs_2_ = bf16[512,256]{1,0:T(8,128)(2,1)S(1)} collective-permute-done((bf16[512,256]{1,0:T(8,128)(2,1)S(1)}, bf16[512,256]{1,0:T(8,128)(2,1)S(1)}, u32[]{:S(2)}, u32[]{:S(2)}) %collective-permute-start.5) | collective-permute-done | bytes 262176 | tf_op jit(solution)/shard_map/ppermute | solution.py:21
  27.5 0.8 collective-permute-done.4.refs_1_
  28.8 1.0 collective-permute-done.8.refs_3_
  30.2 5.0 %panel.1 = (f32[257,128,128]{2,1,0:T(8,128)S(1)}, bf16[2048,1024]{1,0:T(8,128)(2,1)S(1)}, bf16[257,128,128]{2,1,0:T(8,128)(2,1)S(1)}, f32[16,128]{1,0:T(8,128)S(1)}, f32[16,128]{1,0:T(8,128)S(1)}) custom-call(s32[1288]{0:T(1024)S(1)} %concatenate.25.hbm_ref, bf16[2048,1024]{1,0:T(8,128)(2,1)S(1)} %copy-done.1, ...), custom_call_target="tpu_custom_call", output_to_operand_aliasing={{0}: (6, {}), {1}: (7, {})} | custom-call | tf_op jit(solution)/shard_map/panel/pallas_call | solution.py:480
  35.2 3.0 %collective-permute-start.12 = (f32[16,128]{1,0:T(8,128)S(1)}, f32[16,128]{1,0:T(8,128)S(1)}, u32[]{:S(2)}, u32[]{:S(2)}) collective-permute-start(f32[16,128]{1,0:T(8,128)S(1)} %get-tuple-element.46.refs_3_), channel_id=1, source_target_pairs={{0,6},{1,7},{2,4},{3,5},{4,2},{5,3},{6,0},{7,1},{8,14},{9,15},{10,... | collective-permute-start | bytes 24584 | tf_op jit(solution)/shard_map/ppermute | solution.py:21
  38.2 1.5 %collective-permute-start.10 = (f32[16,128]{1,0:T(8,128)S(1)}, f32[16,128]{1,0:T(8,128)S(1)}, u32[]{:S(2)}, u32[]{:S(2)}) collective-permute-start(f32[16,128]{1,0:T(8,128)S(1)} %get-tuple-element.46.refs_3_), channel_id=1, source_target_pairs={{0,2},{1,3},{2,0},{3,1},{4,6},{5,7},{6,4},{7,5},{8,10},{9,11},{10,... | collective-permute-start | bytes 24584 | tf_op jit(solution)/shard_map/ppermute | solution.py:21
  39.7 1.1 collective-permute-done.12.refs_6_
  40.8 1.9 %collective-permute-done.11.refs_5_ = f32[16,128]{1,0:T(8,128)S(1)} collective-permute-done((f32[16,128]{1,0:T(8,128)S(1)}, f32[16,128]{1,0:T(8,128)S(1)}, u32[]{:S(2)}, u32[]{:S(2)}) %collective-permute-start.11) | collective-permute-done | bytes 8224 | tf_op jit(solution)/shard_map/ppermute | solution.py:21
  42.7 2.2 %column_pass.3 = (f32[16,128]{1,0:T(8,128)S(1)}, f32[16,128]{1,0:T(8,128)}, f32[16,128]{1,0:T(8,128)}) custom-call(s32[1288]{0:T(1024)S(1)} %concatenate.25.hbm_ref, f32[257,128,128]{2,1,0:T(8,128)S(1)} %get-tuple-element.43.refs_0_, bf16[257,128,128]{2,1,0:T(8,128)(2,1)S(1)} %get-tuple-element.44.refs_1_, f32[16,128]{1,0:T(8,128)S(1)} %get-tuple-element.45.refs_2_, ...), custom_call_target="tpu_custom_call" | custom-call | tf_op jit(solution)/shard_map/column_pass/pallas_call | solution.py:590
  44.9 3.0 %collective-permute-start.15 = (f32[16,128]{1,0:T(8,128)S(1)}, f32[16,128]{1,0:T(8,128)S(1)}, u32[]{:S(2)}, u32[]{:S(2)}) collective-permute-start(f32[16,128]{1,0:T(8,128)S(1)} %get-tuple-element.47.refs_3_), channel_id=1, source_target_pairs={{0,24},{8,16},{16,8},{24,0},{1,25},{9,17},{17,9},{25,1},{2,26},{10... | collective-permute-start | bytes 24584 | tf_op jit(solution)/shard_map/ppermute | solution.py:21
  48.0 1.1 collective-permute-start.13
  49.6 2.0 %collective-permute-done.14.refs_5_ = f32[16,128]{1,0:T(8,128)S(1)} collective-permute-done((f32[16,128]{1,0:T(8,128)S(1)}, f32[16,128]{1,0:T(8,128)S(1)}, u32[]{:S(2)}, u32[]{:S(2)}) %collective-permute-start.14) | collective-permute-done | bytes 8224 | tf_op jit(solution)/shard_map/ppermute | solution.py:21
  51.6 1.9 %row_pass.2.refs_3_ = f32[16,128]{1,0:T(8,128)S(1)} custom-call(s32[1288]{0:T(1024)S(1)} %concatenate.25.hbm_ref, f32[257,128,128]{2,1,0:T(8,128)S(1)} %get-tuple-element.43.refs_0_, bf16[257,128,128]{2,1,0:T(8,128)(2,1)S(1)} %get-tuple-element.44.refs_1_, f32[16,128]{1,0:T(8,128)S(1)} %get-tuple-element.45.refs_2_, ...), custom_call_target="tpu_custom_call" | custom-call | tf_op jit(solution)/shard_map/row_pass/pallas_call | solution.py:580
  53.5 6.3 %collective-permute-start.18 = (f32[16,128]{1,0:T(8,128)S(1)}, f32[16,128]{1,0:T(8,128)S(1)}, u32[]{:S(2)}, u32[]{:S(2)}) collective-permute-start(f32[16,128]{1,0:T(8,128)S(1)} %row_pass.2.refs_3_), channel_id=1, source_target_pairs={{0,6},{1,7},{2,4},{3,5},{4,2},{5,3},{6,0},{7,1},{8,14},{9,15},{10,... | collective-permute-start | bytes 24584 | tf_op jit(solution)/shard_map/ppermute | solution.py:21
  60.5 1.0 collective-permute-done.18.refs_6_
  61.5 2.9 %collective-permute-done.17.refs_5_ = f32[16,128]{1,0:T(8,128)S(1)} collective-permute-done((f32[16,128]{1,0:T(8,128)S(1)}, f32[16,128]{1,0:T(8,128)S(1)}, u32[]{:S(2)}, u32[]{:S(2)}) %collective-permute-start.17) | collective-permute-done | bytes 8224 | tf_op jit(solution)/shard_map/ppermute | solution.py:21
  64.4 2.2 %column_pass.4 = (f32[16,128]{1,0:T(8,128)S(1)}, f32[16,128]{1,0:T(8,128)}, f32[16,128]{1,0:T(8,128)}) custom-call(s32[1288]{0:T(1024)S(1)} %concatenate.25.hbm_ref, f32[257,128,128]{2,1,0:T(8,128)S(1)} %get-tuple-element.43.refs_0_, bf16[257,128,128]{2,1,0:T(8,128)(2,1)S(1)} %get-tuple-element.44.refs_1_, f32[16,128]{1,0:T(8,128)S(1)} %get-tuple-element.45.refs_2_, ...), custom_call_target="tpu_custom_call" | custom-call | tf_op jit(solution)/shard_map/column_pass/pallas_call | solution.py:590
  66.6 5.2 %collective-permute-start.21 = (f32[16,128]{1,0:T(8,128)S(1)}, f32[16,128]{1,0:T(8,128)S(1)}, u32[]{:S(2)}, u32[]{:S(2)}) collective-permute-start(f32[16,128]{1,0:T(8,128)S(1)} %get-tuple-element.48.refs_3_), channel_id=1, source_target_pairs={{0,24},{8,16},{16,8},{24,0},{1,25},{9,17},{17,9},{25,1},{2,26},{10... | collective-permute-start | bytes 24584 | tf_op jit(solution)/shard_map/ppermute | solution.py:21
  71.8 0.6 collective-permute-start.19
  72.5 1.0 collective-permute-done.21.refs_6_
  73.5 2.0 %collective-permute-done.20.refs_5_ = f32[16,128]{1,0:T(8,128)S(1)} collective-permute-done((f32[16,128]{1,0:T(8,128)S(1)}, f32[16,128]{1,0:T(8,128)S(1)}, u32[]{:S(2)}, u32[]{:S(2)}) %collective-permute-start.20) | collective-permute-done | bytes 8224 | tf_op jit(solution)/shard_map/ppermute | solution.py:21
  75.5 1.7 %row_pass.3.refs_3_ = f32[16,128]{1,0:T(8,128)S(1)} custom-call(s32[1288]{0:T(1024)S(1)} %concatenate.25.hbm_ref, f32[257,128,128]{2,1,0:T(8,128)S(1)} %get-tuple-element.43.refs_0_, bf16[257,128,128]{2,1,0:T(8,128)(2,1)S(1)} %get-tuple-element.44.refs_1_, f32[16,128]{1,0:T(8,128)S(1)} %get-tuple-element.45.refs_2_, ...), custom_call_target="tpu_custom_call" | custom-call | tf_op jit(solution)/shard_map/row_pass/pallas_call | solution.py:580
  77.2 6.1 %collective-permute-start.24 = (f32[16,128]{1,0:T(8,128)S(1)}, f32[16,128]{1,0:T(8,128)S(1)}, u32[]{:S(2)}, u32[]{:S(2)}) collective-permute-start(f32[16,128]{1,0:T(8,128)S(1)} %row_pass.3.refs_3_), channel_id=1, source_target_pairs={{0,6},{1,7},{2,4},{3,5},{4,2},{5,3},{6,0},{7,1},{8,14},{9,15},{10,... | collective-permute-start | bytes 24584 | tf_op jit(solution)/shard_map/ppermute | solution.py:21
  84.0 1.0 collective-permute-done.24.refs_6_
  85.0 2.9 %collective-permute-done.23.refs_5_ = f32[16,128]{1,0:T(8,128)S(1)} collective-permute-done((f32[16,128]{1,0:T(8,128)S(1)}, f32[16,128]{1,0:T(8,128)S(1)}, u32[]{:S(2)}, u32[]{:S(2)}) %collective-permute-start.23) | collective-permute-done | bytes 8224 | tf_op jit(solution)/shard_map/ppermute | solution.py:21
  87.9 2.4 %column_pass.5 = (f32[16,128]{1,0:T(8,128)S(1)}, f32[16,128]{1,0:T(8,128)S(1)}, f32[16,128]{1,0:T(8,128)}) custom-call(s32[1288]{0:T(1024)S(1)} %concatenate.25.hbm_ref, f32[257,128,128]{2,1,0:T(8,128)S(1)} %get-tuple-element.43.refs_0_, bf16[257,128,128]{2,1,0:T(8,128)(2,1)S(1)} %get-tuple-element.44.refs_1_, f32[16,128]{1,0:T(8,128)S(1)} %get-tuple-element.45.refs_2_, ...), custom_call_target="tpu_custom_call" | custom-call | tf_op jit(solution)/shard_map/column_pass/pallas_call | solution.py:590
  90.3 4.9 %collective-permute-start.27 = (f32[16,128]{1,0:T(8,128)S(1)}, f32[16,128]{1,0:T(8,128)S(1)}, u32[]{:S(2)}, u32[]{:S(2)}) collective-permute-start(f32[16,128]{1,0:T(8,128)S(1)} %get-tuple-element.51.refs_3_), channel_id=1, source_target_pairs={{0,24},{8,16},{16,8},{24,0},{1,25},{9,17},{17,9},{25,1},{2,26},{10... | collective-permute-start | bytes 24584 | tf_op jit(solution)/shard_map/ppermute | solution.py:21
  95.2 0.9 collective-permute-start.25
  96.1 0.7 collective-permute-done.27.refs_6_
  96.9 2.0 %collective-permute-done.26.refs_5_ = f32[16,128]{1,0:T(8,128)S(1)} collective-permute-done((f32[16,128]{1,0:T(8,128)S(1)}, f32[16,128]{1,0:T(8,128)S(1)}, u32[]{:S(2)}, u32[]{:S(2)}) %collective-permute-start.26) | collective-permute-done | bytes 8224 | tf_op jit(solution)/shard_map/ppermute | solution.py:21
  98.9 3.7 %plan.1 = (bf16[2048,128]{1,0:T(8,128)(2,1)S(1)}, bf16[35,512,256]{2,1,0:T(8,128)(2,1)S(1)}, f32[8,128]{1,0:T(8,128)}) custom-call(s32[1288]{0:T(1024)S(1)} %concatenate.25.hbm_ref, f32[257,128,128]{2,1,0:T(8,128)S(1)} %get-tuple-element.43.refs_0_, f32[16,128]{1,0:T(8,128)S(1)} %get-tuple-element.49.refs_1_, ...), custom_call_target="tpu_custom_call" | custom-call | tf_op jit(solution)/shard_map/plan/pallas_call | solution.py:606
  102.7 4.0 %rest_of_plan.1 = (bf16[2048,128]{1,0:T(8,128)(2,1)S(1)}, bf16[2048,128]{1,0:T(8,128)(2,1)S(1)}, bf16[2048,128]{1,0:T(8,128)(2,1)S(1)}) custom-call(s32[1288]{0:T(1024)S(1)} %concatenate.25.hbm_ref, bf16[35,512,256]{2,1,0:T(8,128)(2,1)S(1)} %get-tuple-element.52.refs_0_, bf16[2048,1024]{1,0:T(8,128)(2,1)S(1)} %get-tuple-element.50.refs_2_.refs_1_), custom_call_target="tpu_custom_call" | custom-call | flops 3221225472 | bytes 16777216 | tf_op jit(solution)/shard_map/rest_of_plan/pallas_call | solution.py:620
  106.7 1.3 collective-permute-start.28
  108.0 10.8 %collective-permute-done.29 = bf16[2048,128]{1,0:T(8,128)(2,1)S(1)} collective-permute-done((bf16[2048,128]{1,0:T(8,128)(2,1)S(1)}, bf16[2048,128]{1,0:T(8,128)(2,1)S(1)}, u32[]{:S(2)}, u32[]{:S(2)}) %collective-permute-start.29) | collective-permute-done | bytes 524320 | tf_op jit(solution)/shard_map/ppermute | solution.py:21
  119.1 6.9 %collective-permute-done.28 = bf16[2048,128]{1,0:T(8,128)(2,1)S(1)} collective-permute-done((bf16[2048,128]{1,0:T(8,128)(2,1)S(1)}, bf16[2048,128]{1,0:T(8,128)(2,1)S(1)}, u32[]{:S(2)}, u32[]{:S(2)}) %collective-permute-start.28) | collective-permute-done | bytes 524320 | tf_op jit(solution)/shard_map/ppermute | solution.py:21
  126.0 8.8 %collective-permute-done.30 = bf16[2048,128]{1,0:T(8,128)(2,1)S(1)} collective-permute-done((bf16[2048,128]{1,0:T(8,128)(2,1)S(1)}, bf16[2048,128]{1,0:T(8,128)(2,1)S(1)}, u32[]{:S(2)}, u32[]{:S(2)}) %collective-permute-start.30) | collective-permute-done | bytes 524320 | tf_op jit(solution)/shard_map/ppermute | solution.py:21
  134.8 1.0 add_convert_fusion
  (64 shorter events, 7.5 us)
Async XLA Ops:
  0.6 17.8 %collective-permute-start.2 = (bf16[1024,256]{1,0:T(8,128)(2,1)}, bf16[1024,256]{1,0:T(8,128)(2,1)S(1)}, u32[]{:S(2)}, u32[]{:S(2)}) collective-permute-start(bf16[1024,256]{1,0:T(8,128)(2,1)} %refs_1_.1), channel_id=1, source_target_pairs={{0,16},{8,24},{16,0},{24,8},{1,17},{9,25},{17,1},{25,9},{2,18},{10... | collective-permute-start | bytes 1572872 | tf_op jit(solution)/shard_map/ppermute | solution.py:21
  3.7 14.8 %collective-permute-start.1 = (bf16[1024,256]{1,0:T(8,128)(2,1)}, bf16[1024,256]{1,0:T(8,128)(2,1)S(1)}, u32[]{:S(2)}, u32[]{:S(2)}) collective-permute-start(bf16[1024,256]{1,0:T(8,128)(2,1)} %refs_1_.1), channel_id=1, source_target_pairs={{0,8},{8,0},{16,24},{24,16},{1,9},{9,1},{17,25},{25,17},{2,10},{10... | collective-permute-start | bytes 1572872 | tf_op jit(solution)/shard_map/ppermute | solution.py:21
  5.2 7.2 %collective-permute-start.3 = (bf16[1024,256]{1,0:T(8,128)(2,1)}, bf16[1024,256]{1,0:T(8,128)(2,1)S(1)}, u32[]{:S(2)}, u32[]{:S(2)}) collective-permute-start(bf16[1024,256]{1,0:T(8,128)(2,1)} %refs_1_.1), channel_id=1, source_target_pairs={{0,1},{1,0},{2,3},{3,2},{4,5},{5,4},{6,7},{7,6},{8,9},{9,8},{10,11... | collective-permute-start | bytes 1572872 | tf_op jit(solution)/shard_map/ppermute | solution.py:21
  5.2 2.1 %collective-permute-start = (s32[16,8]{0,1:T(8,128)}, s32[16,8]{0,1:T(8,128)S(1)}, u32[]{:S(2)}, u32[]{:S(2)}) collective-permute-start(s32[16,8]{0,1:T(8,128)} %param.5), channel_id=1, source_target_pairs={{0,1},{1,0},{2,3},{3,2},{4,5},{5,4},{6,7},{7,6},{8,9},{9,8},{10,11... | collective-permute-start | bytes 1544 | tf_op jit(solution)/shard_map/ppermute | solution.py:21
  12.4 2.2 %copy-start = (bf16[2048,1024]{1,0:T(8,128)(2,1)S(1)}, bf16[2048,1024]{1,0:T(8,128)(2,1)}, u32[]{:S(2)}) copy-start(bf16[2048,1024]{1,0:T(8,128)(2,1)} %refs_0_.5) | copy-start | bytes 12582916
  14.6 1.0 copy-start.2
  15.6 5.6 %copy-start.1 = (bf16[2048,1024]{1,0:T(8,128)(2,1)S(1)}, bf16[2048,1024]{1,0:T(8,128)(2,1)}, u32[]{:S(2)}) copy-start(bf16[2048,1024]{1,0:T(8,128)(2,1)} %refs_0_.5) | copy-start | bytes 12582916
  18.5 2.4 %collective-permute-start.7 = (bf16[1024,256]{1,0:T(8,128)(2,1)S(1)}, bf16[1024,256]{1,0:T(8,128)(2,1)S(1)}, u32[]{:S(2)}, u32[]{:S(2)}) collective-permute-start(bf16[1024,256]{1,0:T(8,128)(2,1)S(1)} %collective-permute-done.2.refs_2_), channel_id=1, source_target_pairs={{0,1},{1,0},{2,3},{3,2},{4,5},{5,4},{6,7},{7,6},{8,9},{9,8},{10,11... | collective-permute-start | bytes 1572872 | tf_op jit(solution)/shard_map/ppermute | solution.py:21
  18.7 2.5 %collective-permute-start.6 = (bf16[1024,256]{1,0:T(8,128)(2,1)S(1)}, bf16[1024,256]{1,0:T(8,128)(2,1)S(1)}, u32[]{:S(2)}, u32[]{:S(2)}) collective-permute-start(bf16[1024,256]{1,0:T(8,128)(2,1)S(1)} %collective-permute-done.1.refs_1_), channel_id=1, source_target_pairs={{0,1},{1,0},{2,3},{3,2},{4,5},{5,4},{6,7},{7,6},{8,9},{9,8},{10,11... | collective-permute-start | bytes 1572872 | tf_op jit(solution)/shard_map/ppermute | solution.py:21
  19.1 8.4 %collective-permute-start.5 = (bf16[512,256]{1,0:T(8,128)(2,1)S(1)}, bf16[512,256]{1,0:T(8,128)(2,1)S(1)}, u32[]{:S(2)}, u32[]{:S(2)}) collective-permute-start(bf16[512,256]{1,0:T(8,128)(2,1)S(1)} %slice.7), channel_id=1, source_target_pairs={{0,16},{8,24},{16,0},{24,8},{1,17},{9,25},{17,1},{25,9},{2,18},{10... | collective-permute-start | bytes 786440 | tf_op jit(solution)/shard_map/ppermute | solution.py:21
  20.2 8.1 %collective-permute-start.4 = (bf16[512,256]{1,0:T(8,128)(2,1)S(1)}, bf16[512,256]{1,0:T(8,128)(2,1)S(1)}, u32[]{:S(2)}, u32[]{:S(2)}) collective-permute-start(bf16[512,256]{1,0:T(8,128)(2,1)S(1)} %slice.6), channel_id=1, source_target_pairs={{0,8},{8,0},{16,24},{24,16},{1,9},{9,1},{17,25},{25,17},{2,10},{10... | collective-permute-start | bytes 786440 | tf_op jit(solution)/shard_map/ppermute | solution.py:21
  28.3 1.5 %collective-permute-start.8 = (bf16[512,256]{1,0:T(8,128)(2,1)S(1)}, bf16[512,256]{1,0:T(8,128)(2,1)S(1)}, u32[]{:S(2)}, u32[]{:S(2)}) collective-permute-start(bf16[512,256]{1,0:T(8,128)(2,1)S(1)} %collective-permute-done.4.refs_1_), channel_id=1, source_target_pairs={{0,1},{1,0},{2,3},{3,2},{4,5},{5,4},{6,7},{7,6},{8,9},{9,8},{10,11... | collective-permute-start | bytes 786440 | tf_op jit(solution)/shard_map/ppermute | solution.py:21
  28.3 1.9 %collective-permute-start.9 = (bf16[512,256]{1,0:T(8,128)(2,1)S(1)}, bf16[512,256]{1,0:T(8,128)(2,1)S(1)}, u32[]{:S(2)}, u32[]{:S(2)}) collective-permute-start(bf16[512,256]{1,0:T(8,128)(2,1)S(1)} %collective-permute-done.5.refs_2_), channel_id=1, source_target_pairs={{0,1},{1,0},{2,3},{3,2},{4,5},{5,4},{6,7},{7,6},{8,9},{9,8},{10,11... | collective-permute-start | bytes 786440 | tf_op jit(solution)/shard_map/ppermute | solution.py:21
  35.2 5.6 %collective-permute-start.12 = (f32[16,128]{1,0:T(8,128)S(1)}, f32[16,128]{1,0:T(8,128)S(1)}, u32[]{:S(2)}, u32[]{:S(2)}) collective-permute-start(f32[16,128]{1,0:T(8,128)S(1)} %get-tuple-element.46.refs_3_), channel_id=1, source_target_pairs={{0,6},{1,7},{2,4},{3,5},{4,2},{5,3},{6,0},{7,1},{8,14},{9,15},{10,... | collective-permute-start | bytes 24584 | tf_op jit(solution)/shard_map/ppermute | solution.py:21
  38.2 4.5 %collective-permute-start.11 = (f32[16,128]{1,0:T(8,128)S(1)}, f32[16,128]{1,0:T(8,128)S(1)}, u32[]{:S(2)}, u32[]{:S(2)}) collective-permute-start(f32[16,128]{1,0:T(8,128)S(1)} %get-tuple-element.46.refs_3_), channel_id=1, source_target_pairs={{0,4},{1,5},{2,6},{3,7},{4,0},{5,1},{6,2},{7,3},{8,12},{9,13},{10,... | collective-permute-start | bytes 24584 | tf_op jit(solution)/shard_map/ppermute | solution.py:21
  38.2 4.5 %collective-permute-start.10 = (f32[16,128]{1,0:T(8,128)S(1)}, f32[16,128]{1,0:T(8,128)S(1)}, u32[]{:S(2)}, u32[]{:S(2)}) collective-permute-start(f32[16,128]{1,0:T(8,128)S(1)} %get-tuple-element.46.refs_3_), channel_id=1, source_target_pairs={{0,2},{1,3},{2,0},{3,1},{4,6},{5,7},{6,4},{7,5},{8,10},{9,11},{10,... | collective-permute-start | bytes 24584 | tf_op jit(solution)/shard_map/ppermute | solution.py:21
  44.9 4.7 %collective-permute-start.15 = (f32[16,128]{1,0:T(8,128)S(1)}, f32[16,128]{1,0:T(8,128)S(1)}, u32[]{:S(2)}, u32[]{:S(2)}) collective-permute-start(f32[16,128]{1,0:T(8,128)S(1)} %get-tuple-element.47.refs_3_), channel_id=1, source_target_pairs={{0,24},{8,16},{16,8},{24,0},{1,25},{9,17},{17,9},{25,1},{2,26},{10... | collective-permute-start | bytes 24584 | tf_op jit(solution)/shard_map/ppermute | solution.py:21
  48.0 3.7 %collective-permute-start.14 = (f32[16,128]{1,0:T(8,128)S(1)}, f32[16,128]{1,0:T(8,128)S(1)}, u32[]{:S(2)}, u32[]{:S(2)}) collective-permute-start(f32[16,128]{1,0:T(8,128)S(1)} %get-tuple-element.47.refs_3_), channel_id=1, source_target_pairs={{0,16},{8,24},{16,0},{24,8},{1,17},{9,25},{17,1},{25,9},{2,18},{10... | collective-permute-start | bytes 24584 | tf_op jit(solution)/shard_map/ppermute | solution.py:21
  48.0 3.7 %collective-permute-start.13 = (f32[16,128]{1,0:T(8,128)S(1)}, f32[16,128]{1,0:T(8,128)S(1)}, u32[]{:S(2)}, u32[]{:S(2)}) collective-permute-start(f32[16,128]{1,0:T(8,128)S(1)} %get-tuple-element.47.refs_3_), channel_id=1, source_target_pairs={{0,8},{8,0},{16,24},{24,16},{1,9},{9,1},{17,25},{25,17},{2,10},{10... | collective-permute-start | bytes 24584 | tf_op jit(solution)/shard_map/ppermute | solution.py:21
  53.5 7.9 %collective-permute-start.18 = (f32[16,128]{1,0:T(8,128)S(1)}, f32[16,128]{1,0:T(8,128)S(1)}, u32[]{:S(2)}, u32[]{:S(2)}) collective-permute-start(f32[16,128]{1,0:T(8,128)S(1)} %row_pass.2.refs_3_), channel_id=1, source_target_pairs={{0,6},{1,7},{2,4},{3,5},{4,2},{5,3},{6,0},{7,1},{8,14},{9,15},{10,... | collective-permute-start | bytes 24584 | tf_op jit(solution)/shard_map/ppermute | solution.py:21
  59.8 4.5 %collective-permute-start.17 = (f32[16,128]{1,0:T(8,128)S(1)}, f32[16,128]{1,0:T(8,128)S(1)}, u32[]{:S(2)}, u32[]{:S(2)}) collective-permute-start(f32[16,128]{1,0:T(8,128)S(1)} %row_pass.2.refs_3_), channel_id=1, source_target_pairs={{0,4},{1,5},{2,6},{3,7},{4,0},{5,1},{6,2},{7,3},{8,12},{9,13},{10,... | collective-permute-start | bytes 24584 | tf_op jit(solution)/shard_map/ppermute | solution.py:21
  59.8 4.5 %collective-permute-start.16 = (f32[16,128]{1,0:T(8,128)S(1)}, f32[16,128]{1,0:T(8,128)S(1)}, u32[]{:S(2)}, u32[]{:S(2)}) collective-permute-start(f32[16,128]{1,0:T(8,128)S(1)} %row_pass.2.refs_3_), channel_id=1, source_target_pairs={{0,2},{1,3},{2,0},{3,1},{4,6},{5,7},{6,4},{7,5},{8,10},{9,11},{10,... | collective-permute-start | bytes 24584 | tf_op jit(solution)/shard_map/ppermute | solution.py:21
  66.6 6.9 %collective-permute-start.21 = (f32[16,128]{1,0:T(8,128)S(1)}, f32[16,128]{1,0:T(8,128)S(1)}, u32[]{:S(2)}, u32[]{:S(2)}) collective-permute-start(f32[16,128]{1,0:T(8,128)S(1)} %get-tuple-element.48.refs_3_), channel_id=1, source_target_pairs={{0,24},{8,16},{16,8},{24,0},{1,25},{9,17},{17,9},{25,1},{2,26},{10... | collective-permute-start | bytes 24584 | tf_op jit(solution)/shard_map/ppermute | solution.py:21
  71.8 3.7 %collective-permute-start.20 = (f32[16,128]{1,0:T(8,128)S(1)}, f32[16,128]{1,0:T(8,128)S(1)}, u32[]{:S(2)}, u32[]{:S(2)}) collective-permute-start(f32[16,128]{1,0:T(8,128)S(1)} %get-tuple-element.48.refs_3_), channel_id=1, source_target_pairs={{0,16},{8,24},{16,0},{24,8},{1,17},{9,25},{17,1},{25,9},{2,18},{10... | collective-permute-start | bytes 24584 | tf_op jit(solution)/shard_map/ppermute | solution.py:21
  71.8 3.7 %collective-permute-start.19 = (f32[16,128]{1,0:T(8,128)S(1)}, f32[16,128]{1,0:T(8,128)S(1)}, u32[]{:S(2)}, u32[]{:S(2)}) collective-permute-start(f32[16,128]{1,0:T(8,128)S(1)} %get-tuple-element.48.refs_3_), channel_id=1, source_target_pairs={{0,8},{8,0},{16,24},{24,16},{1,9},{9,1},{17,25},{25,17},{2,10},{10... | collective-permute-start | bytes 24584 | tf_op jit(solution)/shard_map/ppermute | solution.py:21
  77.2 7.8 %collective-permute-start.24 = (f32[16,128]{1,0:T(8,128)S(1)}, f32[16,128]{1,0:T(8,128)S(1)}, u32[]{:S(2)}, u32[]{:S(2)}) collective-permute-start(f32[16,128]{1,0:T(8,128)S(1)} %row_pass.3.refs_3_), channel_id=1, source_target_pairs={{0,6},{1,7},{2,4},{3,5},{4,2},{5,3},{6,0},{7,1},{8,14},{9,15},{10,... | collective-permute-start | bytes 24584 | tf_op jit(solution)/shard_map/ppermute | solution.py:21
  83.3 4.5 %collective-permute-start.23 = (f32[16,128]{1,0:T(8,128)S(1)}, f32[16,128]{1,0:T(8,128)S(1)}, u32[]{:S(2)}, u32[]{:S(2)}) collective-permute-start(f32[16,128]{1,0:T(8,128)S(1)} %row_pass.3.refs_3_), channel_id=1, source_target_pairs={{0,4},{1,5},{2,6},{3,7},{4,0},{5,1},{6,2},{7,3},{8,12},{9,13},{10,... | collective-permute-start | bytes 24584 | tf_op jit(solution)/shard_map/ppermute | solution.py:21
  83.4 4.5 %collective-permute-start.22 = (f32[16,128]{1,0:T(8,128)S(1)}, f32[16,128]{1,0:T(8,128)S(1)}, u32[]{:S(2)}, u32[]{:S(2)}) collective-permute-start(f32[16,128]{1,0:T(8,128)S(1)} %row_pass.3.refs_3_), channel_id=1, source_target_pairs={{0,2},{1,3},{2,0},{3,1},{4,6},{5,7},{6,4},{7,5},{8,10},{9,11},{10,... | collective-permute-start | bytes 24584 | tf_op jit(solution)/shard_map/ppermute | solution.py:21
  90.3 6.5 %collective-permute-start.27 = (f32[16,128]{1,0:T(8,128)S(1)}, f32[16,128]{1,0:T(8,128)S(1)}, u32[]{:S(2)}, u32[]{:S(2)}) collective-permute-start(f32[16,128]{1,0:T(8,128)S(1)} %get-tuple-element.51.refs_3_), channel_id=1, source_target_pairs={{0,24},{8,16},{16,8},{24,0},{1,25},{9,17},{17,9},{25,1},{2,26},{10... | collective-permute-start | bytes 24584 | tf_op jit(solution)/shard_map/ppermute | solution.py:21
  95.2 3.7 %collective-permute-start.26 = (f32[16,128]{1,0:T(8,128)S(1)}, f32[16,128]{1,0:T(8,128)S(1)}, u32[]{:S(2)}, u32[]{:S(2)}) collective-permute-start(f32[16,128]{1,0:T(8,128)S(1)} %get-tuple-element.51.refs_3_), channel_id=1, source_target_pairs={{0,16},{8,24},{16,0},{24,8},{1,17},{9,25},{17,1},{25,9},{2,18},{10... | collective-permute-start | bytes 24584 | tf_op jit(solution)/shard_map/ppermute | solution.py:21
  95.2 3.7 %collective-permute-start.25 = (f32[16,128]{1,0:T(8,128)S(1)}, f32[16,128]{1,0:T(8,128)S(1)}, u32[]{:S(2)}, u32[]{:S(2)}) collective-permute-start(f32[16,128]{1,0:T(8,128)S(1)} %get-tuple-element.51.refs_3_), channel_id=1, source_target_pairs={{0,8},{8,0},{16,24},{24,16},{1,9},{9,1},{17,25},{25,17},{2,10},{10... | collective-permute-start | bytes 24584 | tf_op jit(solution)/shard_map/ppermute | solution.py:21
  102.6 16.2 %collective-permute-start.29 = (bf16[2048,128]{1,0:T(8,128)(2,1)S(1)}, bf16[2048,128]{1,0:T(8,128)(2,1)S(1)}, u32[]{:S(2)}, u32[]{:S(2)}) collective-permute-start(bf16[2048,128]{1,0:T(8,128)(2,1)S(1)} %get-tuple-element.56), channel_id=1, source_target_pairs={{0,2},{1,3},{2,0},{3,1},{4,6},{5,7},{6,4},{7,5},{8,10},{9,11},{10,... | collective-permute-start | bytes 1572872 | tf_op jit(solution)/shard_map/ppermute | solution.py:21
  106.7 19.2 %collective-permute-start.28 = (bf16[2048,128]{1,0:T(8,128)(2,1)S(1)}, bf16[2048,128]{1,0:T(8,128)(2,1)S(1)}, u32[]{:S(2)}, u32[]{:S(2)}) collective-permute-start(bf16[2048,128]{1,0:T(8,128)(2,1)S(1)} %get-tuple-element.54), channel_id=1, source_target_pairs={{0,2},{1,3},{2,0},{3,1},{4,6},{5,7},{6,4},{7,5},{8,10},{9,11},{10,... | collective-permute-start | bytes 1572872 | tf_op jit(solution)/shard_map/ppermute | solution.py:21
  119.0 15.8 %collective-permute-start.30 = (bf16[2048,128]{1,0:T(8,128)(2,1)S(1)}, bf16[2048,128]{1,0:T(8,128)(2,1)S(1)}, u32[]{:S(2)}, u32[]{:S(2)}) collective-permute-start(bf16[2048,128]{1,0:T(8,128)(2,1)S(1)} %add_convert_fusion.1), channel_id=1, source_target_pairs={{0,4},{1,5},{2,6},{3,7},{4,0},{5,1},{6,2},{7,3},{8,12},{9,13},{10,... | collective-permute-start | bytes 1572872 | tf_op jit(solution)/shard_map/ppermute | solution.py:21

commit v15 on v14

--- a/solution.py
+++ b/solution.py
@@ -533,7 +533,10 @@
     blocks = list(blocks)
     distance = 1
     while distance < len(blocks):
+        got = None
         for j in range(len(blocks) - distance, 0, -2 * distance):
+            if j == distance and got is not None:
+                blocks[j], got = tied(blocks[j], got)
             got = swap(blocks[j].astype(jnp.bfloat16), "proto", 2 * distance).astype(jnp.float32)
             blocks[j ^ distance] = blocks[j ^ distance].astype(jnp.float32) + got
         distance *= 2

time: 135 us -> 136 us (level)
  Pallas kernels: 30.3 us -> 41.8 us
  starting transfers between devices: 43.3 us -> 36.5 us
  waiting for transfers between devices: 51.2 us -> 46.4 us
    pallas_call x2, Pallas kernels: 3.63 us -> 13.3 us  [shards(): pl.pallas_call(with_table(row_kernel, table, log_column), out_shape=row_s...]
    ppermute x31, starting transfers between devices: 43.3 us -> 36.5 us  [swap(): return lax.ppermute(x, axis, [(i, i ^ offset) for i in range(size)])]
    ppermute x31, waiting for transfers between devices: 51.2 us -> 46.4 us  [swap(): return lax.ppermute(x, axis, [(i, i ^ offset) for i in range(size)])]
    pallas_call x3, Pallas kernels: 6.81 us -> 8.59 us  [shards(): pl.pallas_call(with_table(column_kernel, table), out_shape=(column_shape,...]
  transfers between devices with their start and end apart: 31 -> 31, of which waited for: 21 -> 22; matrix products, arithmetic and copies ran while one was open for 3% -> 3% of each run, Pallas kernels for 8% -> 8%
where the time goes in v15:
time: 136 us
  waiting for transfers between devices  46.4 us (34%)
  Pallas kernels  41.8 us (31%)
  starting transfers between devices  36.5 us (27%)
  local copies, waits for them, and re-layouts  4.41 us (3%)
  other arithmetic  4.4 us (3%)
  between operations  2.21 us (2%)
    ppermute x31, waiting for transfers between devices, swap(): return lax.ppermute(x, axis, [(i, i ^ offset) for i in range(size)])  46.4 us
    ppermute x31, starting transfers between devices, swap(): return lax.ppermute(x, axis, [(i, i ^ offset) for i in range(size)])  36.5 us
    pallas_call x2, Pallas kernels, shards(): pl.pallas_call(with_table(row_kernel, table, log_column), out_shape=row_s...  13.3 us
    pallas_call x3, Pallas kernels, shards(): pl.pallas_call(with_table(column_kernel, table), out_shape=(column_shape,...  8.59 us
    pallas_call x2, Pallas kernels, early(): pl.pallas_call(with_table(early_panel_kernel, table, places, owners, bool...  7.1 us
    pallas_call x1, Pallas kernels, late(): pl.pallas_call(with_table(panel_kernel, table, places, add), out_shape=(p...  5.06 us
    pallas_call x1, Pallas kernels, shards(): pl.pallas_call(with_table(rest_kernel, table, lines), out_shape=[block] *...  4.03 us
    pallas_call x1, Pallas kernels, shards(): pl.pallas_call(with_table(plan_kernel, table, log_column, lines), out_sha...  3.7 us
  transfers between devices with their start and end apart: 31, of which 22 were waited for; matrix products, arithmetic and copies ran while one was open for 3% of the time, Pallas kernels for 8%

profile of v15, /device:TPU:0, one launch (start us, length us, event | category | flops | bytes accessed | tf_op | source)
XLA Modules:
  0.0 135.8 jit_solution(3955960474087461236)
XLA Ops:
  0.6 3.0 %collective-permute-start.2 = (bf16[1024,256]{1,0:T(8,128)(2,1)}, bf16[1024,256]{1,0:T(8,128)(2,1)S(1)}, u32[]{:S(2)}, u32[]{:S(2)}) collective-permute-start(bf16[1024,256]{1,0:T(8,128)(2,1)} %refs_1_.1), channel_id=1, source_target_pairs={{0,16},{8,24},{16,0},{24,8},{1,17},{9,25},{17,1},{25,9},{2,18},{10... | collective-permute-start | bytes 1572872 | tf_op jit(solution)/shard_map/ppermute | solution.py:21
  3.7 1.5 %collective-permute-start.1 = (bf16[1024,256]{1,0:T(8,128)(2,1)}, bf16[1024,256]{1,0:T(8,128)(2,1)S(1)}, u32[]{:S(2)}, u32[]{:S(2)}) collective-permute-start(bf16[1024,256]{1,0:T(8,128)(2,1)} %refs_1_.1), channel_id=1, source_target_pairs={{0,8},{8,0},{16,24},{24,16},{1,9},{9,1},{17,25},{25,17},{2,10},{10... | collective-permute-start | bytes 1572872 | tf_op jit(solution)/shard_map/ppermute | solution.py:21
  5.7 0.7 compare_select_fusion.1
  6.4 0.9 collective-permute-done
  7.6 0.6 fusion.4
  10.3 0.6 select_reduce_fusion.1
  11.6 0.7 concatenate.25.hbm_ref
  12.4 2.2 %copy-done = bf16[2048,1024]{1,0:T(8,128)(2,1)S(1)} copy-done((bf16[2048,1024]{1,0:T(8,128)(2,1)S(1)}, bf16[2048,1024]{1,0:T(8,128)(2,1)}, u32[]{:S(2)}) %copy-start) | copy-done | bytes 4194328
  14.6 1.0 copy-done.2
  15.6 2.8 %early_panel.2 = (f32[257,128,128]{2,1,0:T(8,128)S(1)}, bf16[2048,1024]{1,0:T(8,128)(2,1)S(1)}) custom-call(s32[1288]{0:T(1024)S(1)} %concatenate.25.hbm_ref, bf16[2048,1024]{1,0:T(8,128)(2,1)S(1)} %copy-done, bf16[1024,256]{1,0:T(8,128)(2,1)S(1)} %copy-done.2, bf16[1024,256]{1,0:T(8,128)(2,1)S(1)} %collective-permute-done.3.refs_2_), custom_call_target="tpu_custom_call" | custom-call | flops 1073741824 | bytes 33554432 | tf_op jit(solution)/shard_map/early_panel/pallas_call | solution.py:501
  19.1 0.6 collective-permute-start.5
  19.7 0.7 collective-permute-start.4
  20.4 0.7 collective-permute-done.6.refs_3_
  21.2 4.3 %early_panel.3 = (f32[257,128,128]{2,1,0:T(8,128)S(1)}, bf16[2048,1024]{1,0:T(8,128)(2,1)S(1)}) custom-call(s32[1288]{0:T(1024)S(1)} %concatenate.25.hbm_ref, bf16[2048,1024]{1,0:T(8,128)(2,1)S(1)} %copy-done.1, bf16[1024,256]{1,0:T(8,128)(2,1)S(1)} %collective-permute-done.1.refs_1_, ...), custom_call_target="tpu_custom_call", output_to_operand_aliasing={{0}: (6, {}), {1}: (7, {})} | custom-call | flops 2147483648 | bytes 33554432 | tf_op jit(solution)/shard_map/early_panel/pallas_call | solution.py:501
  25.5 2.0 %collective-permute-done.5.refs_2_ = bf16[512,256]{1,0:T(8,128)(2,1)S(1)} collective-permute-done((bf16[512,256]{1,0:T(8,128)(2,1)S(1)}, bf16[512,256]{1,0:T(8,128)(2,1)S(1)}, u32[]{:S(2)}, u32[]{:S(2)}) %collective-permute-start.5) | collective-permute-done | bytes 262176 | tf_op jit(solution)/shard_map/ppermute | solution.py:21
  28.2 1.0 collective-permute-done.8.refs_3_
  29.6 5.1 %panel.1 = (f32[257,128,128]{2,1,0:T(8,128)S(1)}, bf16[2048,1024]{1,0:T(8,128)(2,1)S(1)}, bf16[257,128,128]{2,1,0:T(8,128)(2,1)S(1)}, f32[16,128]{1,0:T(8,128)S(1)}, f32[16,128]{1,0:T(8,128)S(1)}) custom-call(s32[1288]{0:T(1024)S(1)} %concatenate.25.hbm_ref, bf16[2048,1024]{1,0:T(8,128)(2,1)S(1)} %copy-done.1, ...), custom_call_target="tpu_custom_call", output_to_operand_aliasing={{0}: (6, {}), {1}: (7, {})} | custom-call | tf_op jit(solution)/shard_map/panel/pallas_call | solution.py:480
  34.7 2.9 %collective-permute-start.12 = (f32[16,128]{1,0:T(8,128)S(1)}, f32[16,128]{1,0:T(8,128)S(1)}, u32[]{:S(2)}, u32[]{:S(2)}) collective-permute-start(f32[16,128]{1,0:T(8,128)S(1)} %get-tuple-element.47.refs_3_), channel_id=1, source_target_pairs={{0,6},{1,7},{2,4},{3,5},{4,2},{5,3},{6,0},{7,1},{8,14},{9,15},{10,... | collective-permute-start | bytes 24584 | tf_op jit(solution)/shard_map/ppermute | solution.py:21
  37.6 1.5 %collective-permute-start.10 = (f32[16,128]{1,0:T(8,128)S(1)}, f32[16,128]{1,0:T(8,128)S(1)}, u32[]{:S(2)}, u32[]{:S(2)}) collective-permute-start(f32[16,128]{1,0:T(8,128)S(1)} %get-tuple-element.47.refs_3_), channel_id=1, source_target_pairs={{0,2},{1,3},{2,0},{3,1},{4,6},{5,7},{6,4},{7,5},{8,10},{9,11},{10,... | collective-permute-start | bytes 24584 | tf_op jit(solution)/shard_map/ppermute | solution.py:21
  39.2 1.1 collective-permute-done.12.refs_6_
  40.2 1.9 %collective-permute-done.11.refs_5_ = f32[16,128]{1,0:T(8,128)S(1)} collective-permute-done((f32[16,128]{1,0:T(8,128)S(1)}, f32[16,128]{1,0:T(8,128)S(1)}, u32[]{:S(2)}, u32[]{:S(2)}) %collective-permute-start.11) | collective-permute-done | bytes 8224 | tf_op jit(solution)/shard_map/ppermute | solution.py:21
  42.2 2.8 %column_pass.3 = (f32[16,128]{1,0:T(8,128)S(1)}, f32[16,128]{1,0:T(8,128)}, f32[16,128]{1,0:T(8,128)}) custom-call(s32[1288]{0:T(1024)S(1)} %concatenate.25.hbm_ref, f32[257,128,128]{2,1,0:T(8,128)S(1)} %get-tuple-element.44.refs_0_, bf16[257,128,128]{2,1,0:T(8,128)(2,1)S(1)} %get-tuple-element.45.refs_1_, f32[16,128]{1,0:T(8,128)S(1)} %get-tuple-element.46.refs_2_, ...), custom_call_target="tpu_custom_call" | custom-call | tf_op jit(solution)/shard_map/column_pass/pallas_call | solution.py:593
  45.0 3.6 %collective-permute-start.15 = (f32[16,128]{1,0:T(8,128)S(1)}, f32[16,128]{1,0:T(8,128)S(1)}, u32[]{:S(2)}, u32[]{:S(2)}) collective-permute-start(f32[16,128]{1,0:T(8,128)S(1)} %get-tuple-element.48.refs_3_), channel_id=1, source_target_pairs={{0,24},{8,16},{16,8},{24,0},{1,25},{9,17},{17,9},{25,1},{2,26},{10... | collective-permute-start | bytes 24584 | tf_op jit(solution)/shard_map/ppermute | solution.py:21
  48.6 0.6 collective-permute-start.13
  49.2 1.0 collective-permute-done.15.refs_6_
  50.2 2.0 %collective-permute-done.14.refs_5_ = f32[16,128]{1,0:T(8,128)S(1)} collective-permute-done((f32[16,128]{1,0:T(8,128)S(1)}, f32[16,128]{1,0:T(8,128)S(1)}, u32[]{:S(2)}, u32[]{:S(2)}) %collective-permute-start.14) | collective-permute-done | bytes 8224 | tf_op jit(solution)/shard_map/ppermute | solution.py:21
  52.2 6.8 %row_pass.2.refs_3_ = f32[16,128]{1,0:T(8,128)S(1)} custom-call(s32[1288]{0:T(1024)S(1)} %concatenate.25.hbm_ref, f32[257,128,128]{2,1,0:T(8,128)S(1)} %get-tuple-element.44.refs_0_, bf16[257,128,128]{2,1,0:T(8,128)(2,1)S(1)} %get-tuple-element.45.refs_1_, f32[16,128]{1,0:T(8,128)S(1)} %get-tuple-element.46.refs_2_, ...), custom_call_target="tpu_custom_call" | custom-call | tf_op jit(solution)/shard_map/row_pass/pallas_call | solution.py:583
  59.1 4.3 %collective-permute-start.16 = (f32[16,128]{1,0:T(8,128)S(1)}, f32[16,128]{1,0:T(8,128)S(1)}, u32[]{:S(2)}, u32[]{:S(2)}) collective-permute-start(f32[16,128]{1,0:T(8,128)S(1)} %row_pass.2.refs_3_), channel_id=1, source_target_pairs={{0,2},{1,3},{2,0},{3,1},{4,6},{5,7},{6,4},{7,5},{8,10},{9,11},{10,... | collective-permute-start | bytes 24584 | tf_op jit(solution)/shard_map/ppermute | solution.py:21
  63.4 1.1 collective-permute-done.18.refs_6_
  65.1 2.8 %column_pass.4 = (f32[16,128]{1,0:T(8,128)S(1)}, f32[16,128]{1,0:T(8,128)}, f32[16,128]{1,0:T(8,128)}) custom-call(s32[1288]{0:T(1024)S(1)} %concatenate.25.hbm_ref, f32[257,128,128]{2,1,0:T(8,128)S(1)} %get-tuple-element.44.refs_0_, bf16[257,128,128]{2,1,0:T(8,128)(2,1)S(1)} %get-tuple-element.45.refs_1_, f32[16,128]{1,0:T(8,128)S(1)} %get-tuple-element.46.refs_2_, ...), custom_call_target="tpu_custom_call" | custom-call | tf_op jit(solution)/shard_map/column_pass/pallas_call | solution.py:593
  67.9 3.6 %collective-permute-start.21 = (f32[16,128]{1,0:T(8,128)S(1)}, f32[16,128]{1,0:T(8,128)S(1)}, u32[]{:S(2)}, u32[]{:S(2)}) collective-permute-start(f32[16,128]{1,0:T(8,128)S(1)} %get-tuple-element.49.refs_3_), channel_id=1, source_target_pairs={{0,24},{8,16},{16,8},{24,0},{1,25},{9,17},{17,9},{25,1},{2,26},{10... | collective-permute-start | bytes 24584 | tf_op jit(solution)/shard_map/ppermute | solution.py:21
  71.4 1.3 collective-permute-start.19
  73.1 2.0 %collective-permute-done.20.refs_5_ = f32[16,128]{1,0:T(8,128)S(1)} collective-permute-done((f32[16,128]{1,0:T(8,128)S(1)}, f32[16,128]{1,0:T(8,128)S(1)}, u32[]{:S(2)}, u32[]{:S(2)}) %collective-permute-start.20) | collective-permute-done | bytes 8224 | tf_op jit(solution)/shard_map/ppermute | solution.py:21
  75.1 6.6 %row_pass.3.refs_3_ = f32[16,128]{1,0:T(8,128)S(1)} custom-call(s32[1288]{0:T(1024)S(1)} %concatenate.25.hbm_ref, f32[257,128,128]{2,1,0:T(8,128)S(1)} %get-tuple-element.44.refs_0_, bf16[257,128,128]{2,1,0:T(8,128)(2,1)S(1)} %get-tuple-element.45.refs_1_, f32[16,128]{1,0:T(8,128)S(1)} %get-tuple-element.46.refs_2_, ...), custom_call_target="tpu_custom_call" | custom-call | tf_op jit(solution)/shard_map/row_pass/pallas_call | solution.py:583
  81.8 4.3 %collective-permute-start.22 = (f32[16,128]{1,0:T(8,128)S(1)}, f32[16,128]{1,0:T(8,128)S(1)}, u32[]{:S(2)}, u32[]{:S(2)}) collective-permute-start(f32[16,128]{1,0:T(8,128)S(1)} %row_pass.3.refs_3_), channel_id=1, source_target_pairs={{0,2},{1,3},{2,0},{3,1},{4,6},{5,7},{6,4},{7,5},{8,10},{9,11},{10,... | collective-permute-start | bytes 24584 | tf_op jit(solution)/shard_map/ppermute | solution.py:21
  86.1 1.1 collective-permute-done.24.refs_6_
  87.8 3.0 %column_pass.5 = (f32[16,128]{1,0:T(8,128)S(1)}, f32[16,128]{1,0:T(8,128)S(1)}, f32[16,128]{1,0:T(8,128)}) custom-call(s32[1288]{0:T(1024)S(1)} %concatenate.25.hbm_ref, f32[257,128,128]{2,1,0:T(8,128)S(1)} %get-tuple-element.44.refs_0_, bf16[257,128,128]{2,1,0:T(8,128)(2,1)S(1)} %get-tuple-element.45.refs_1_, f32[16,128]{1,0:T(8,128)S(1)} %get-tuple-element.46.refs_2_, ...), custom_call_target="tpu_custom_call" | custom-call | tf_op jit(solution)/shard_map/column_pass/pallas_call | solution.py:593
  90.8 4.6 %collective-permute-start.27 = (f32[16,128]{1,0:T(8,128)S(1)}, f32[16,128]{1,0:T(8,128)S(1)}, u32[]{:S(2)}, u32[]{:S(2)}) collective-permute-start(f32[16,128]{1,0:T(8,128)S(1)} %get-tuple-element.52.refs_3_), channel_id=1, source_target_pairs={{0,24},{8,16},{16,8},{24,0},{1,25},{9,17},{17,9},{25,1},{2,26},{10... | collective-permute-start | bytes 24584 | tf_op jit(solution)/shard_map/ppermute | solution.py:21
  95.4 0.6 collective-permute-start.25
  96.0 1.0 collective-permute-done.27.refs_6_
  97.0 2.0 %collective-permute-done.26.refs_5_ = f32[16,128]{1,0:T(8,128)S(1)} collective-permute-done((f32[16,128]{1,0:T(8,128)S(1)}, f32[16,128]{1,0:T(8,128)S(1)}, u32[]{:S(2)}, u32[]{:S(2)}) %collective-permute-start.26) | collective-permute-done | bytes 8224 | tf_op jit(solution)/shard_map/ppermute | solution.py:21
  99.1 3.7 %plan.1 = (bf16[2048,128]{1,0:T(8,128)(2,1)S(1)}, bf16[35,512,256]{2,1,0:T(8,128)(2,1)S(1)}, f32[8,128]{1,0:T(8,128)}) custom-call(s32[1288]{0:T(1024)S(1)} %concatenate.25.hbm_ref, f32[257,128,128]{2,1,0:T(8,128)S(1)} %get-tuple-element.44.refs_0_, f32[16,128]{1,0:T(8,128)S(1)} %get-tuple-element.50.refs_1_, ...), custom_call_target="tpu_custom_call" | custom-call | tf_op jit(solution)/shard_map/plan/pallas_call | solution.py:609
  103.3 4.0 %rest_of_plan.1 = (bf16[2048,128]{1,0:T(8,128)(2,1)S(1)}, bf16[2048,128]{1,0:T(8,128)(2,1)S(1)}, bf16[2048,128]{1,0:T(8,128)(2,1)S(1)}) custom-call(s32[1288]{0:T(1024)S(1)} %concatenate.25.hbm_ref, bf16[35,512,256]{2,1,0:T(8,128)(2,1)S(1)} %get-tuple-element.53.refs_0_, bf16[2048,1024]{1,0:T(8,128)(2,1)S(1)} %get-tuple-element.51.refs_2_.refs_1_), custom_call_target="tpu_custom_call" | custom-call | flops 3221225472 | bytes 16777216 | tf_op jit(solution)/shard_map/rest_of_plan/pallas_call | solution.py:623
  107.4 0.8 collective-permute-start.29
  108.2 10.7 %collective-permute-done.28 = bf16[2048,128]{1,0:T(8,128)(2,1)S(1)} collective-permute-done((bf16[2048,128]{1,0:T(8,128)(2,1)S(1)}, bf16[2048,128]{1,0:T(8,128)(2,1)S(1)}, u32[]{:S(2)}, u32[]{:S(2)}) %collective-permute-start.28) | collective-permute-done | bytes 524320 | tf_op jit(solution)/shard_map/ppermute | solution.py:21
  119.1 5.6 %collective-permute-done.29 = bf16[2048,128]{1,0:T(8,128)(2,1)S(1)} collective-permute-done((bf16[2048,128]{1,0:T(8,128)(2,1)S(1)}, bf16[2048,128]{1,0:T(8,128)(2,1)S(1)}, u32[]{:S(2)}, u32[]{:S(2)}) %collective-permute-start.29) | collective-permute-done | bytes 524320 | tf_op jit(solution)/shard_map/ppermute | solution.py:21
  124.7 10.1 %collective-permute-done.30 = bf16[2048,128]{1,0:T(8,128)(2,1)S(1)} collective-permute-done((bf16[2048,128]{1,0:T(8,128)(2,1)S(1)}, bf16[2048,128]{1,0:T(8,128)(2,1)S(1)}, u32[]{:S(2)}, u32[]{:S(2)}) %collective-permute-start.30) | collective-permute-done | bytes 524320 | tf_op jit(solution)/shard_map/ppermute | solution.py:21
  134.8 1.0 add_convert_fusion
  (64 shorter events, 6.6 us)
Async XLA Ops:
  0.6 17.8 %collective-permute-start.2 = (bf16[1024,256]{1,0:T(8,128)(2,1)}, bf16[1024,256]{1,0:T(8,128)(2,1)S(1)}, u32[]{:S(2)}, u32[]{:S(2)}) collective-permute-start(bf16[1024,256]{1,0:T(8,128)(2,1)} %refs_1_.1), channel_id=1, source_target_pairs={{0,16},{8,24},{16,0},{24,8},{1,17},{9,25},{17,1},{25,9},{2,18},{10... | collective-permute-start | bytes 1572872 | tf_op jit(solution)/shard_map/ppermute | solution.py:21
  3.7 14.8 %collective-permute-start.1 = (bf16[1024,256]{1,0:T(8,128)(2,1)}, bf16[1024,256]{1,0:T(8,128)(2,1)S(1)}, u32[]{:S(2)}, u32[]{:S(2)}) collective-permute-start(bf16[1024,256]{1,0:T(8,128)(2,1)} %refs_1_.1), channel_id=1, source_target_pairs={{0,8},{8,0},{16,24},{24,16},{1,9},{9,1},{17,25},{25,17},{2,10},{10... | collective-permute-start | bytes 1572872 | tf_op jit(solution)/shard_map/ppermute | solution.py:21
  5.2 7.2 %collective-permute-start.3 = (bf16[1024,256]{1,0:T(8,128)(2,1)}, bf16[1024,256]{1,0:T(8,128)(2,1)S(1)}, u32[]{:S(2)}, u32[]{:S(2)}) collective-permute-start(bf16[1024,256]{1,0:T(8,128)(2,1)} %refs_1_.1), channel_id=1, source_target_pairs={{0,1},{1,0},{2,3},{3,2},{4,5},{5,4},{6,7},{7,6},{8,9},{9,8},{10,11... | collective-permute-start | bytes 1572872 | tf_op jit(solution)/shard_map/ppermute | solution.py:21
  5.2 2.1 %collective-permute-start = (s32[16,8]{0,1:T(8,128)}, s32[16,8]{0,1:T(8,128)S(1)}, u32[]{:S(2)}, u32[]{:S(2)}) collective-permute-start(s32[16,8]{0,1:T(8,128)} %param.5), channel_id=1, source_target_pairs={{0,1},{1,0},{2,3},{3,2},{4,5},{5,4},{6,7},{7,6},{8,9},{9,8},{10,11... | collective-permute-start | bytes 1544 | tf_op jit(solution)/shard_map/ppermute | solution.py:21
  12.4 2.2 %copy-start = (bf16[2048,1024]{1,0:T(8,128)(2,1)S(1)}, bf16[2048,1024]{1,0:T(8,128)(2,1)}, u32[]{:S(2)}) copy-start(bf16[2048,1024]{1,0:T(8,128)(2,1)} %refs_0_.5) | copy-start | bytes 12582916
  14.6 1.0 copy-start.2
  15.6 5.6 %copy-start.1 = (bf16[2048,1024]{1,0:T(8,128)(2,1)S(1)}, bf16[2048,1024]{1,0:T(8,128)(2,1)}, u32[]{:S(2)}) copy-start(bf16[2048,1024]{1,0:T(8,128)(2,1)} %refs_0_.5) | copy-start | bytes 12582916
  18.5 2.0 %collective-permute-start.7 = (bf16[1024,256]{1,0:T(8,128)(2,1)S(1)}, bf16[1024,256]{1,0:T(8,128)(2,1)S(1)}, u32[]{:S(2)}, u32[]{:S(2)}) collective-permute-start(bf16[1024,256]{1,0:T(8,128)(2,1)S(1)} %collective-permute-done.2.refs_2_), channel_id=1, source_target_pairs={{0,1},{1,0},{2,3},{3,2},{4,5},{5,4},{6,7},{7,6},{8,9},{9,8},{10,11... | collective-permute-start | bytes 1572872 | tf_op jit(solution)/shard_map/ppermute | solution.py:21
  18.7 2.5 %collective-permute-start.6 = (bf16[1024,256]{1,0:T(8,128)(2,1)S(1)}, bf16[1024,256]{1,0:T(8,128)(2,1)S(1)}, u32[]{:S(2)}, u32[]{:S(2)}) collective-permute-start(bf16[1024,256]{1,0:T(8,128)(2,1)S(1)} %collective-permute-done.1.refs_1_), channel_id=1, source_target_pairs={{0,1},{1,0},{2,3},{3,2},{4,5},{5,4},{6,7},{7,6},{8,9},{9,8},{10,11... | collective-permute-start | bytes 1572872 | tf_op jit(solution)/shard_map/ppermute | solution.py:21
  19.1 8.4 %collective-permute-start.5 = (bf16[512,256]{1,0:T(8,128)(2,1)S(1)}, bf16[512,256]{1,0:T(8,128)(2,1)S(1)}, u32[]{:S(2)}, u32[]{:S(2)}) collective-permute-start(bf16[512,256]{1,0:T(8,128)(2,1)S(1)} %slice.7), channel_id=1, source_target_pairs={{0,16},{8,24},{16,0},{24,8},{1,17},{9,25},{17,1},{25,9},{2,18},{10... | collective-permute-start | bytes 786440 | tf_op jit(solution)/shard_map/ppermute | solution.py:21
  19.7 8.1 %collective-permute-start.4 = (bf16[512,256]{1,0:T(8,128)(2,1)S(1)}, bf16[512,256]{1,0:T(8,128)(2,1)S(1)}, u32[]{:S(2)}, u32[]{:S(2)}) collective-permute-start(bf16[512,256]{1,0:T(8,128)(2,1)S(1)} %slice.6), channel_id=1, source_target_pairs={{0,8},{8,0},{16,24},{24,16},{1,9},{9,1},{17,25},{25,17},{2,10},{10... | collective-permute-start | bytes 786440 | tf_op jit(solution)/shard_map/ppermute | solution.py:21
  27.7 1.5 %collective-permute-start.8 = (bf16[512,256]{1,0:T(8,128)(2,1)S(1)}, bf16[512,256]{1,0:T(8,128)(2,1)S(1)}, u32[]{:S(2)}, u32[]{:S(2)}) collective-permute-start(bf16[512,256]{1,0:T(8,128)(2,1)S(1)} %collective-permute-done.4.refs_1_), channel_id=1, source_target_pairs={{0,1},{1,0},{2,3},{3,2},{4,5},{5,4},{6,7},{7,6},{8,9},{9,8},{10,11... | collective-permute-start | bytes 786440 | tf_op jit(solution)/shard_map/ppermute | solution.py:21
  27.7 1.9 %collective-permute-start.9 = (bf16[512,256]{1,0:T(8,128)(2,1)S(1)}, bf16[512,256]{1,0:T(8,128)(2,1)S(1)}, u32[]{:S(2)}, u32[]{:S(2)}) collective-permute-start(bf16[512,256]{1,0:T(8,128)(2,1)S(1)} %collective-permute-done.5.refs_2_), channel_id=1, source_target_pairs={{0,1},{1,0},{2,3},{3,2},{4,5},{5,4},{6,7},{7,6},{8,9},{9,8},{10,11... | collective-permute-start | bytes 786440 | tf_op jit(solution)/shard_map/ppermute | solution.py:21
  34.7 5.5 %collective-permute-start.12 = (f32[16,128]{1,0:T(8,128)S(1)}, f32[16,128]{1,0:T(8,128)S(1)}, u32[]{:S(2)}, u32[]{:S(2)}) collective-permute-start(f32[16,128]{1,0:T(8,128)S(1)} %get-tuple-element.47.refs_3_), channel_id=1, source_target_pairs={{0,6},{1,7},{2,4},{3,5},{4,2},{5,3},{6,0},{7,1},{8,14},{9,15},{10,... | collective-permute-start | bytes 24584 | tf_op jit(solution)/shard_map/ppermute | solution.py:21
  37.6 4.5 %collective-permute-start.11 = (f32[16,128]{1,0:T(8,128)S(1)}, f32[16,128]{1,0:T(8,128)S(1)}, u32[]{:S(2)}, u32[]{:S(2)}) collective-permute-start(f32[16,128]{1,0:T(8,128)S(1)} %get-tuple-element.47.refs_3_), channel_id=1, source_target_pairs={{0,4},{1,5},{2,6},{3,7},{4,0},{5,1},{6,2},{7,3},{8,12},{9,13},{10,... | collective-permute-start | bytes 24584 | tf_op jit(solution)/shard_map/ppermute | solution.py:21
  37.6 4.5 %collective-permute-start.10 = (f32[16,128]{1,0:T(8,128)S(1)}, f32[16,128]{1,0:T(8,128)S(1)}, u32[]{:S(2)}, u32[]{:S(2)}) collective-permute-start(f32[16,128]{1,0:T(8,128)S(1)} %get-tuple-element.47.refs_3_), channel_id=1, source_target_pairs={{0,2},{1,3},{2,0},{3,1},{4,6},{5,7},{6,4},{7,5},{8,10},{9,11},{10,... | collective-permute-start | bytes 24584 | tf_op jit(solution)/shard_map/ppermute | solution.py:21
  45.0 5.2 %collective-permute-start.15 = (f32[16,128]{1,0:T(8,128)S(1)}, f32[16,128]{1,0:T(8,128)S(1)}, u32[]{:S(2)}, u32[]{:S(2)}) collective-permute-start(f32[16,128]{1,0:T(8,128)S(1)} %get-tuple-element.48.refs_3_), channel_id=1, source_target_pairs={{0,24},{8,16},{16,8},{24,0},{1,25},{9,17},{17,9},{25,1},{2,26},{10... | collective-permute-start | bytes 24584 | tf_op jit(solution)/shard_map/ppermute | solution.py:21
  48.6 3.7 %collective-permute-start.14 = (f32[16,128]{1,0:T(8,128)S(1)}, f32[16,128]{1,0:T(8,128)S(1)}, u32[]{:S(2)}, u32[]{:S(2)}) collective-permute-start(f32[16,128]{1,0:T(8,128)S(1)} %get-tuple-element.48.refs_3_), channel_id=1, source_target_pairs={{0,16},{8,24},{16,0},{24,8},{1,17},{9,25},{17,1},{25,9},{2,18},{10... | collective-permute-start | bytes 24584 | tf_op jit(solution)/shard_map/ppermute | solution.py:21
  48.6 3.7 %collective-permute-start.13 = (f32[16,128]{1,0:T(8,128)S(1)}, f32[16,128]{1,0:T(8,128)S(1)}, u32[]{:S(2)}, u32[]{:S(2)}) collective-permute-start(f32[16,128]{1,0:T(8,128)S(1)} %get-tuple-element.48.refs_3_), channel_id=1, source_target_pairs={{0,8},{8,0},{16,24},{24,16},{1,9},{9,1},{17,25},{25,17},{2,10},{10... | collective-permute-start | bytes 24584 | tf_op jit(solution)/shard_map/ppermute | solution.py:21
  59.0 5.5 %collective-permute-start.18 = (f32[16,128]{1,0:T(8,128)S(1)}, f32[16,128]{1,0:T(8,128)S(1)}, u32[]{:S(2)}, u32[]{:S(2)}) collective-permute-start(f32[16,128]{1,0:T(8,128)S(1)} %row_pass.2.refs_3_), channel_id=1, source_target_pairs={{0,6},{1,7},{2,4},{3,5},{4,2},{5,3},{6,0},{7,1},{8,14},{9,15},{10,... | collective-permute-start | bytes 24584 | tf_op jit(solution)/shard_map/ppermute | solution.py:21
  59.1 5.4 %collective-permute-start.17 = (f32[16,128]{1,0:T(8,128)S(1)}, f32[16,128]{1,0:T(8,128)S(1)}, u32[]{:S(2)}, u32[]{:S(2)}) collective-permute-start(f32[16,128]{1,0:T(8,128)S(1)} %row_pass.2.refs_3_), channel_id=1, source_target_pairs={{0,4},{1,5},{2,6},{3,7},{4,0},{5,1},{6,2},{7,3},{8,12},{9,13},{10,... | collective-permute-start | bytes 24584 | tf_op jit(solution)/shard_map/ppermute | solution.py:21
  59.1 5.9 %collective-permute-start.16 = (f32[16,128]{1,0:T(8,128)S(1)}, f32[16,128]{1,0:T(8,128)S(1)}, u32[]{:S(2)}, u32[]{:S(2)}) collective-permute-start(f32[16,128]{1,0:T(8,128)S(1)} %row_pass.2.refs_3_), channel_id=1, source_target_pairs={{0,2},{1,3},{2,0},{3,1},{4,6},{5,7},{6,4},{7,5},{8,10},{9,11},{10,... | collective-permute-start | bytes 24584 | tf_op jit(solution)/shard_map/ppermute | solution.py:21
  67.9 5.2 %collective-permute-start.21 = (f32[16,128]{1,0:T(8,128)S(1)}, f32[16,128]{1,0:T(8,128)S(1)}, u32[]{:S(2)}, u32[]{:S(2)}) collective-permute-start(f32[16,128]{1,0:T(8,128)S(1)} %get-tuple-element.49.refs_3_), channel_id=1, source_target_pairs={{0,24},{8,16},{16,8},{24,0},{1,25},{9,17},{17,9},{25,1},{2,26},{10... | collective-permute-start | bytes 24584 | tf_op jit(solution)/shard_map/ppermute | solution.py:21
  71.4 3.7 %collective-permute-start.20 = (f32[16,128]{1,0:T(8,128)S(1)}, f32[16,128]{1,0:T(8,128)S(1)}, u32[]{:S(2)}, u32[]{:S(2)}) collective-permute-start(f32[16,128]{1,0:T(8,128)S(1)} %get-tuple-element.49.refs_3_), channel_id=1, source_target_pairs={{0,16},{8,24},{16,0},{24,8},{1,17},{9,25},{17,1},{25,9},{2,18},{10... | collective-permute-start | bytes 24584 | tf_op jit(solution)/shard_map/ppermute | solution.py:21
  71.4 3.7 %collective-permute-start.19 = (f32[16,128]{1,0:T(8,128)S(1)}, f32[16,128]{1,0:T(8,128)S(1)}, u32[]{:S(2)}, u32[]{:S(2)}) collective-permute-start(f32[16,128]{1,0:T(8,128)S(1)} %get-tuple-element.49.refs_3_), channel_id=1, source_target_pairs={{0,8},{8,0},{16,24},{24,16},{1,9},{9,1},{17,25},{25,17},{2,10},{10... | collective-permute-start | bytes 24584 | tf_op jit(solution)/shard_map/ppermute | solution.py:21
  81.7 5.5 %collective-permute-start.24 = (f32[16,128]{1,0:T(8,128)S(1)}, f32[16,128]{1,0:T(8,128)S(1)}, u32[]{:S(2)}, u32[]{:S(2)}) collective-permute-start(f32[16,128]{1,0:T(8,128)S(1)} %row_pass.3.refs_3_), channel_id=1, source_target_pairs={{0,6},{1,7},{2,4},{3,5},{4,2},{5,3},{6,0},{7,1},{8,14},{9,15},{10,... | collective-permute-start | bytes 24584 | tf_op jit(solution)/shard_map/ppermute | solution.py:21
  81.8 5.4 %collective-permute-start.23 = (f32[16,128]{1,0:T(8,128)S(1)}, f32[16,128]{1,0:T(8,128)S(1)}, u32[]{:S(2)}, u32[]{:S(2)}) collective-permute-start(f32[16,128]{1,0:T(8,128)S(1)} %row_pass.3.refs_3_), channel_id=1, source_target_pairs={{0,4},{1,5},{2,6},{3,7},{4,0},{5,1},{6,2},{7,3},{8,12},{9,13},{10,... | collective-permute-start | bytes 24584 | tf_op jit(solution)/shard_map/ppermute | solution.py:21
  81.8 5.9 %collective-permute-start.22 = (f32[16,128]{1,0:T(8,128)S(1)}, f32[16,128]{1,0:T(8,128)S(1)}, u32[]{:S(2)}, u32[]{:S(2)}) collective-permute-start(f32[16,128]{1,0:T(8,128)S(1)} %row_pass.3.refs_3_), channel_id=1, source_target_pairs={{0,2},{1,3},{2,0},{3,1},{4,6},{5,7},{6,4},{7,5},{8,10},{9,11},{10,... | collective-permute-start | bytes 24584 | tf_op jit(solution)/shard_map/ppermute | solution.py:21
  90.8 6.3 %collective-permute-start.27 = (f32[16,128]{1,0:T(8,128)S(1)}, f32[16,128]{1,0:T(8,128)S(1)}, u32[]{:S(2)}, u32[]{:S(2)}) collective-permute-start(f32[16,128]{1,0:T(8,128)S(1)} %get-tuple-element.52.refs_3_), channel_id=1, source_target_pairs={{0,24},{8,16},{16,8},{24,0},{1,25},{9,17},{17,9},{25,1},{2,26},{10... | collective-permute-start | bytes 24584 | tf_op jit(solution)/shard_map/ppermute | solution.py:21
  95.4 3.7 %collective-permute-start.26 = (f32[16,128]{1,0:T(8,128)S(1)}, f32[16,128]{1,0:T(8,128)S(1)}, u32[]{:S(2)}, u32[]{:S(2)}) collective-permute-start(f32[16,128]{1,0:T(8,128)S(1)} %get-tuple-element.52.refs_3_), channel_id=1, source_target_pairs={{0,16},{8,24},{16,0},{24,8},{1,17},{9,25},{17,1},{25,9},{2,18},{10... | collective-permute-start | bytes 24584 | tf_op jit(solution)/shard_map/ppermute | solution.py:21
  95.4 3.7 %collective-permute-start.25 = (f32[16,128]{1,0:T(8,128)S(1)}, f32[16,128]{1,0:T(8,128)S(1)}, u32[]{:S(2)}, u32[]{:S(2)}) collective-permute-start(f32[16,128]{1,0:T(8,128)S(1)} %get-tuple-element.52.refs_3_), channel_id=1, source_target_pairs={{0,8},{8,0},{16,24},{24,16},{1,9},{9,1},{17,25},{25,17},{2,10},{10... | collective-permute-start | bytes 24584 | tf_op jit(solution)/shard_map/ppermute | solution.py:21
  102.8 16.1 %collective-permute-start.28 = (bf16[2048,128]{1,0:T(8,128)(2,1)S(1)}, bf16[2048,128]{1,0:T(8,128)(2,1)S(1)}, u32[]{:S(2)}, u32[]{:S(2)}) collective-permute-start(bf16[2048,128]{1,0:T(8,128)(2,1)S(1)} %get-tuple-element.56), channel_id=1, source_target_pairs={{0,2},{1,3},{2,0},{3,1},{4,6},{5,7},{6,4},{7,5},{8,10},{9,11},{10,... | collective-permute-start | bytes 1572872 | tf_op jit(solution)/shard_map/ppermute | solution.py:21
  107.4 17.3 %collective-permute-start.29 = (bf16[2048,128]{1,0:T(8,128)(2,1)S(1)}, bf16[2048,128]{1,0:T(8,128)(2,1)S(1)}, u32[]{:S(2)}, u32[]{:S(2)}) collective-permute-start(bf16[2048,128]{1,0:T(8,128)(2,1)S(1)} %get-tuple-element.57), channel_id=1, source_target_pairs={{0,2},{1,3},{2,0},{3,1},{4,6},{5,7},{6,4},{7,5},{8,10},{9,11},{10,... | collective-permute-start | bytes 1572872 | tf_op jit(solution)/shard_map/ppermute | solution.py:21
  119.0 15.8 %collective-permute-start.30 = (bf16[2048,128]{1,0:T(8,128)(2,1)S(1)}, bf16[2048,128]{1,0:T(8,128)(2,1)S(1)}, u32[]{:S(2)}, u32[]{:S(2)}) collective-permute-start(bf16[2048,128]{1,0:T(8,128)(2,1)S(1)} %add_convert_fusion.1), channel_id=1, source_target_pairs={{0,4},{1,5},{2,6},{3,7},{4,0},{5,1},{6,2},{7,3},{8,12},{9,13},{10,... | collective-permute-start | bytes 1572872 | tf_op jit(solution)/shard_map/ppermute | solution.py:21

commit v16 on v14

--- a/solution.py
+++ b/solution.py
@@ -534,8 +534,10 @@
     distance = 1
     while distance < len(blocks):
         for j in range(len(blocks) - distance, 0, -2 * distance):
-            got = swap(blocks[j].astype(jnp.bfloat16), "proto", 2 * distance).astype(jnp.float32)
-            blocks[j ^ distance] = blocks[j ^ distance].astype(jnp.float32) + got
+            got = swap(blocks[j].astype(jnp.bfloat16), "proto", 2 * distance)
+            if j == 3 * distance:
+                got, blocks[distance] = tied(got, blocks[distance])
+            blocks[j ^ distance] = blocks[j ^ distance].astype(jnp.float32) + got.astype(jnp.float32)
         distance *= 2
     return blocks[0].astype(jnp.bfloat16)
 

time: 135 us -> 138 us (1.022); the launches traced: 136 us -> 136 us
  starting transfers between devices: 43.3 us -> 41.7 us
  waiting for transfers between devices: 51.2 us -> 52.8 us
    ppermute x31, starting transfers between devices: 43.3 us -> 41.7 us  [swap(): return lax.ppermute(x, axis, [(i, i ^ offset) for i in range(size)])]
    ppermute x31, waiting for transfers between devices: 51.2 us -> 52.8 us  [swap(): return lax.ppermute(x, axis, [(i, i ^ offset) for i in range(size)])]
  transfers between devices with their start and end apart: 31 -> 31, of which waited for: 21 -> 22; matrix products, arithmetic and copies ran while one was open for 3% -> 3% of each run, Pallas kernels for 8% -> 8%
where the time goes in v16:
time: 138 us; the launch traced here: 136 us
  waiting for transfers between devices  52.8 us (38%)
  starting transfers between devices  41.7 us (30%)
  Pallas kernels  30.8 us (22%)
  local copies, waits for them, and re-layouts  4.41 us (3%)
  other arithmetic  4.4 us (3%)
  between operations  2.18 us (2%)
    ppermute x31, waiting for transfers between devices, swap(): return lax.ppermute(x, axis, [(i, i ^ offset) for i in range(size)])  52.8 us
    ppermute x31, starting transfers between devices, swap(): return lax.ppermute(x, axis, [(i, i ^ offset) for i in range(size)])  41.7 us
    pallas_call x2, Pallas kernels, early(): pl.pallas_call(with_table(early_panel_kernel, table, places, owners, bool...  7.1 us
    pallas_call x3, Pallas kernels, shards(): pl.pallas_call(with_table(column_kernel, table), out_shape=(column_shape,...  6.95 us
    pallas_call x1, Pallas kernels, late(): pl.pallas_call(with_table(panel_kernel, table, places, add), out_shape=(p...  5.18 us
    pallas_call x1, Pallas kernels, shards(): pl.pallas_call(with_table(rest_kernel, table, lines), out_shape=[block] *...  4.02 us
    pallas_call x2, Pallas kernels, shards(): pl.pallas_call(with_table(row_kernel, table, log_column), out_shape=row_s...  3.88 us
    pallas_call x1, Pallas kernels, shards(): pl.pallas_call(with_table(plan_kernel, table, log_column, lines), out_sha...  3.7 us
  transfers between devices with their start and end apart: 31, of which 22 were waited for; matrix products, arithmetic and copies ran while one was open for 3% of the time, Pallas kernels for 8%

profile of v16, /device:TPU:0, one launch (start us, length us, event | category | flops | bytes accessed | tf_op | source)
XLA Modules:
  0.0 136.3 jit_solution(11425029890444492122)
XLA Ops:
  0.6 3.0 %collective-permute-start.2 = (bf16[1024,256]{1,0:T(8,128)(2,1)}, bf16[1024,256]{1,0:T(8,128)(2,1)S(1)}, u32[]{:S(2)}, u32[]{:S(2)}) collective-permute-start(bf16[1024,256]{1,0:T(8,128)(2,1)} %refs_1_.1), channel_id=1, source_target_pairs={{0,16},{8,24},{16,0},{24,8},{1,17},{9,25},{17,1},{25,9},{2,18},{10... | collective-permute-start | bytes 1572872 | tf_op jit(solution)/shard_map/ppermute | solution.py:21
  3.7 1.5 %collective-permute-start.1 = (bf16[1024,256]{1,0:T(8,128)(2,1)}, bf16[1024,256]{1,0:T(8,128)(2,1)S(1)}, u32[]{:S(2)}, u32[]{:S(2)}) collective-permute-start(bf16[1024,256]{1,0:T(8,128)(2,1)} %refs_1_.1), channel_id=1, source_target_pairs={{0,8},{8,0},{16,24},{24,16},{1,9},{9,1},{17,25},{25,17},{2,10},{10... | collective-permute-start | bytes 1572872 | tf_op jit(solution)/shard_map/ppermute | solution.py:21
  5.7 0.7 compare_select_fusion.1
  6.4 0.9 collective-permute-done
  11.6 0.7 concatenate.25.hbm_ref
  12.4 2.2 %copy-done = bf16[2048,1024]{1,0:T(8,128)(2,1)S(1)} copy-done((bf16[2048,1024]{1,0:T(8,128)(2,1)S(1)}, bf16[2048,1024]{1,0:T(8,128)(2,1)}, u32[]{:S(2)}) %copy-start) | copy-done | bytes 4194328
  14.6 1.0 copy-done.2
  15.6 2.8 %early_panel.2 = (f32[257,128,128]{2,1,0:T(8,128)S(1)}, bf16[2048,1024]{1,0:T(8,128)(2,1)S(1)}) custom-call(s32[1288]{0:T(1024)S(1)} %concatenate.25.hbm_ref, bf16[2048,1024]{1,0:T(8,128)(2,1)S(1)} %copy-done, bf16[1024,256]{1,0:T(8,128)(2,1)S(1)} %copy-done.2, bf16[1024,256]{1,0:T(8,128)(2,1)S(1)} %collective-permute-done.3.refs_2_), custom_call_target="tpu_custom_call" | custom-call | flops 1073741824 | bytes 33554432 | tf_op jit(solution)/shard_map/early_panel/pallas_call | solution.py:501
  19.7 0.7 collective-permute-start.4
  20.4 0.7 collective-permute-done.6.refs_3_
  21.2 4.3 %early_panel.3 = (f32[257,128,128]{2,1,0:T(8,128)S(1)}, bf16[2048,1024]{1,0:T(8,128)(2,1)S(1)}) custom-call(s32[1288]{0:T(1024)S(1)} %concatenate.25.hbm_ref, bf16[2048,1024]{1,0:T(8,128)(2,1)S(1)} %copy-done.1, bf16[1024,256]{1,0:T(8,128)(2,1)S(1)} %collective-permute-done.1.refs_1_, ...), custom_call_target="tpu_custom_call", output_to_operand_aliasing={{0}: (6, {}), {1}: (7, {})} | custom-call | flops 2147483648 | bytes 33554432 | tf_op jit(solution)/shard_map/early_panel/pallas_call | solution.py:501
  25.5 2.0 %collective-permute-done.5.refs_2_ = bf16[512,256]{1,0:T(8,128)(2,1)S(1)} collective-permute-done((bf16[512,256]{1,0:T(8,128)(2,1)S(1)}, bf16[512,256]{1,0:T(8,128)(2,1)S(1)}, u32[]{:S(2)}, u32[]{:S(2)}) %collective-permute-start.5) | collective-permute-done | bytes 262176 | tf_op jit(solution)/shard_map/ppermute | solution.py:21
  28.2 1.0 collective-permute-done.8.refs_3_
  29.6 5.2 %panel.1 = (f32[257,128,128]{2,1,0:T(8,128)S(1)}, bf16[2048,1024]{1,0:T(8,128)(2,1)S(1)}, bf16[257,128,128]{2,1,0:T(8,128)(2,1)S(1)}, f32[16,128]{1,0:T(8,128)S(1)}, f32[16,128]{1,0:T(8,128)S(1)}) custom-call(s32[1288]{0:T(1024)S(1)} %concatenate.25.hbm_ref, bf16[2048,1024]{1,0:T(8,128)(2,1)S(1)} %copy-done.1, ...), custom_call_target="tpu_custom_call", output_to_operand_aliasing={{0}: (6, {}), {1}: (7, {})} | custom-call | tf_op jit(solution)/shard_map/panel/pallas_call | solution.py:480
  34.8 2.7 %collective-permute-start.12 = (f32[16,128]{1,0:T(8,128)S(1)}, f32[16,128]{1,0:T(8,128)S(1)}, u32[]{:S(2)}, u32[]{:S(2)}) collective-permute-start(f32[16,128]{1,0:T(8,128)S(1)} %get-tuple-element.48.refs_3_), channel_id=1, source_target_pairs={{0,6},{1,7},{2,4},{3,5},{4,2},{5,3},{6,0},{7,1},{8,14},{9,15},{10,... | collective-permute-start | bytes 24584 | tf_op jit(solution)/shard_map/ppermute | solution.py:21
  37.6 1.7 %collective-permute-start.10 = (f32[16,128]{1,0:T(8,128)S(1)}, f32[16,128]{1,0:T(8,128)S(1)}, u32[]{:S(2)}, u32[]{:S(2)}) collective-permute-start(f32[16,128]{1,0:T(8,128)S(1)} %get-tuple-element.48.refs_3_), channel_id=1, source_target_pairs={{0,2},{1,3},{2,0},{3,1},{4,6},{5,7},{6,4},{7,5},{8,10},{9,11},{10,... | collective-permute-start | bytes 24584 | tf_op jit(solution)/shard_map/ppermute | solution.py:21
  39.3 1.1 collective-permute-done.12.refs_6_
  40.3 1.8 %collective-permute-done.11.refs_5_ = f32[16,128]{1,0:T(8,128)S(1)} collective-permute-done((f32[16,128]{1,0:T(8,128)S(1)}, f32[16,128]{1,0:T(8,128)S(1)}, u32[]{:S(2)}, u32[]{:S(2)}) %collective-permute-start.11) | collective-permute-done | bytes 8224 | tf_op jit(solution)/shard_map/ppermute | solution.py:21
  42.1 2.2 %column_pass.3 = (f32[16,128]{1,0:T(8,128)S(1)}, f32[16,128]{1,0:T(8,128)}, f32[16,128]{1,0:T(8,128)}) custom-call(s32[1288]{0:T(1024)S(1)} %concatenate.25.hbm_ref, f32[257,128,128]{2,1,0:T(8,128)S(1)} %get-tuple-element.45.refs_0_, bf16[257,128,128]{2,1,0:T(8,128)(2,1)S(1)} %get-tuple-element.46.refs_1_, f32[16,128]{1,0:T(8,128)S(1)} %get-tuple-element.47.refs_2_, ...), custom_call_target="tpu_custom_call" | custom-call | tf_op jit(solution)/shard_map/column_pass/pallas_call | solution.py:592
  44.4 4.1 %collective-permute-start.15 = (f32[16,128]{1,0:T(8,128)S(1)}, f32[16,128]{1,0:T(8,128)S(1)}, u32[]{:S(2)}, u32[]{:S(2)}) collective-permute-start(f32[16,128]{1,0:T(8,128)S(1)} %get-tuple-element.49.refs_3_), channel_id=1, source_target_pairs={{0,24},{8,16},{16,8},{24,0},{1,25},{9,17},{17,9},{25,1},{2,26},{10... | collective-permute-start | bytes 24584 | tf_op jit(solution)/shard_map/ppermute | solution.py:21
  48.5 0.6 collective-permute-start.13
  49.1 1.0 collective-permute-done.15.refs_6_
  50.1 2.0 %collective-permute-done.14.refs_5_ = f32[16,128]{1,0:T(8,128)S(1)} collective-permute-done((f32[16,128]{1,0:T(8,128)S(1)}, f32[16,128]{1,0:T(8,128)S(1)}, u32[]{:S(2)}, u32[]{:S(2)}) %collective-permute-start.14) | collective-permute-done | bytes 8224 | tf_op jit(solution)/shard_map/ppermute | solution.py:21
  52.1 2.0 %row_pass.2.refs_3_ = f32[16,128]{1,0:T(8,128)S(1)} custom-call(s32[1288]{0:T(1024)S(1)} %concatenate.25.hbm_ref, f32[257,128,128]{2,1,0:T(8,128)S(1)} %get-tuple-element.45.refs_0_, bf16[257,128,128]{2,1,0:T(8,128)(2,1)S(1)} %get-tuple-element.46.refs_1_, f32[16,128]{1,0:T(8,128)S(1)} %get-tuple-element.47.refs_2_, ...), custom_call_target="tpu_custom_call" | custom-call | tf_op jit(solution)/shard_map/row_pass/pallas_call | solution.py:582
  54.2 1.2 collective-permute-start.18
  55.4 5.2 %collective-permute-start.17 = (f32[16,128]{1,0:T(8,128)S(1)}, f32[16,128]{1,0:T(8,128)S(1)}, u32[]{:S(2)}, u32[]{:S(2)}) collective-permute-start(f32[16,128]{1,0:T(8,128)S(1)} %row_pass.2.refs_3_), channel_id=1, source_target_pairs={{0,4},{1,5},{2,6},{3,7},{4,0},{5,1},{6,2},{7,3},{8,12},{9,13},{10,... | collective-permute-start | bytes 24584 | tf_op jit(solution)/shard_map/ppermute | solution.py:21
  60.6 1.7 %collective-permute-done.17.refs_5_ = f32[16,128]{1,0:T(8,128)S(1)} collective-permute-done((f32[16,128]{1,0:T(8,128)S(1)}, f32[16,128]{1,0:T(8,128)S(1)}, u32[]{:S(2)}, u32[]{:S(2)}) %collective-permute-start.17) | collective-permute-done | bytes 8224 | tf_op jit(solution)/shard_map/ppermute | solution.py:21
  62.3 1.9 %collective-permute-done.16.refs_4_ = f32[16,128]{1,0:T(8,128)S(1)} collective-permute-done((f32[16,128]{1,0:T(8,128)S(1)}, f32[16,128]{1,0:T(8,128)S(1)}, u32[]{:S(2)}, u32[]{:S(2)}) %collective-permute-start.16) | collective-permute-done | bytes 8224 | tf_op jit(solution)/shard_map/ppermute | solution.py:21
  64.3 2.2 %column_pass.4 = (f32[16,128]{1,0:T(8,128)S(1)}, f32[16,128]{1,0:T(8,128)}, f32[16,128]{1,0:T(8,128)}) custom-call(s32[1288]{0:T(1024)S(1)} %concatenate.25.hbm_ref, f32[257,128,128]{2,1,0:T(8,128)S(1)} %get-tuple-element.45.refs_0_, bf16[257,128,128]{2,1,0:T(8,128)(2,1)S(1)} %get-tuple-element.46.refs_1_, f32[16,128]{1,0:T(8,128)S(1)} %get-tuple-element.47.refs_2_, ...), custom_call_target="tpu_custom_call" | custom-call | tf_op jit(solution)/shard_map/column_pass/pallas_call | solution.py:592
  66.5 4.0 %collective-permute-start.21 = (f32[16,128]{1,0:T(8,128)S(1)}, f32[16,128]{1,0:T(8,128)S(1)}, u32[]{:S(2)}, u32[]{:S(2)}) collective-permute-start(f32[16,128]{1,0:T(8,128)S(1)} %get-tuple-element.50.refs_3_), channel_id=1, source_target_pairs={{0,24},{8,16},{16,8},{24,0},{1,25},{9,17},{17,9},{25,1},{2,26},{10... | collective-permute-start | bytes 24584 | tf_op jit(solution)/shard_map/ppermute | solution.py:21
  70.5 0.8 collective-permute-start.19
  71.3 0.8 collective-permute-done.21.refs_6_
  72.2 2.0 %collective-permute-done.20.refs_5_ = f32[16,128]{1,0:T(8,128)S(1)} collective-permute-done((f32[16,128]{1,0:T(8,128)S(1)}, f32[16,128]{1,0:T(8,128)S(1)}, u32[]{:S(2)}, u32[]{:S(2)}) %collective-permute-start.20) | collective-permute-done | bytes 8224 | tf_op jit(solution)/shard_map/ppermute | solution.py:21
  74.2 1.9 %row_pass.3.refs_3_ = f32[16,128]{1,0:T(8,128)S(1)} custom-call(s32[1288]{0:T(1024)S(1)} %concatenate.25.hbm_ref, f32[257,128,128]{2,1,0:T(8,128)S(1)} %get-tuple-element.45.refs_0_, bf16[257,128,128]{2,1,0:T(8,128)(2,1)S(1)} %get-tuple-element.46.refs_1_, f32[16,128]{1,0:T(8,128)S(1)} %get-tuple-element.47.refs_2_, ...), custom_call_target="tpu_custom_call" | custom-call | tf_op jit(solution)/shard_map/row_pass/pallas_call | solution.py:582
  76.0 0.7 collective-permute-start.24
  76.8 5.9 %collective-permute-start.23 = (f32[16,128]{1,0:T(8,128)S(1)}, f32[16,128]{1,0:T(8,128)S(1)}, u32[]{:S(2)}, u32[]{:S(2)}) collective-permute-start(f32[16,128]{1,0:T(8,128)S(1)} %row_pass.3.refs_3_), channel_id=1, source_target_pairs={{0,4},{1,5},{2,6},{3,7},{4,0},{5,1},{6,2},{7,3},{8,12},{9,13},{10,... | collective-permute-start | bytes 24584 | tf_op jit(solution)/shard_map/ppermute | solution.py:21
  82.7 1.7 %collective-permute-done.23.refs_5_ = f32[16,128]{1,0:T(8,128)S(1)} collective-permute-done((f32[16,128]{1,0:T(8,128)S(1)}, f32[16,128]{1,0:T(8,128)S(1)}, u32[]{:S(2)}, u32[]{:S(2)}) %collective-permute-start.23) | collective-permute-done | bytes 8224 | tf_op jit(solution)/shard_map/ppermute | solution.py:21
  84.4 1.9 %collective-permute-done.22.refs_4_ = f32[16,128]{1,0:T(8,128)S(1)} collective-permute-done((f32[16,128]{1,0:T(8,128)S(1)}, f32[16,128]{1,0:T(8,128)S(1)}, u32[]{:S(2)}, u32[]{:S(2)}) %collective-permute-start.22) | collective-permute-done | bytes 8224 | tf_op jit(solution)/shard_map/ppermute | solution.py:21
  86.3 2.5 %column_pass.5 = (f32[16,128]{1,0:T(8,128)S(1)}, f32[16,128]{1,0:T(8,128)S(1)}, f32[16,128]{1,0:T(8,128)}) custom-call(s32[1288]{0:T(1024)S(1)} %concatenate.25.hbm_ref, f32[257,128,128]{2,1,0:T(8,128)S(1)} %get-tuple-element.45.refs_0_, bf16[257,128,128]{2,1,0:T(8,128)(2,1)S(1)} %get-tuple-element.46.refs_1_, f32[16,128]{1,0:T(8,128)S(1)} %get-tuple-element.47.refs_2_, ...), custom_call_target="tpu_custom_call" | custom-call | tf_op jit(solution)/shard_map/column_pass/pallas_call | solution.py:592
  88.8 4.8 %collective-permute-start.27 = (f32[16,128]{1,0:T(8,128)S(1)}, f32[16,128]{1,0:T(8,128)S(1)}, u32[]{:S(2)}, u32[]{:S(2)}) collective-permute-start(f32[16,128]{1,0:T(8,128)S(1)} %get-tuple-element.53.refs_3_), channel_id=1, source_target_pairs={{0,24},{8,16},{16,8},{24,0},{1,25},{9,17},{17,9},{25,1},{2,26},{10... | collective-permute-start | bytes 24584 | tf_op jit(solution)/shard_map/ppermute | solution.py:21
  94.2 1.0 collective-permute-done.27.refs_6_
  95.2 2.0 %collective-permute-done.26.refs_5_ = f32[16,128]{1,0:T(8,128)S(1)} collective-permute-done((f32[16,128]{1,0:T(8,128)S(1)}, f32[16,128]{1,0:T(8,128)S(1)}, u32[]{:S(2)}, u32[]{:S(2)}) %collective-permute-start.26) | collective-permute-done | bytes 8224 | tf_op jit(solution)/shard_map/ppermute | solution.py:21
  97.2 3.7 %plan.1 = (bf16[2048,128]{1,0:T(8,128)(2,1)S(1)}, bf16[35,512,256]{2,1,0:T(8,128)(2,1)S(1)}, f32[8,128]{1,0:T(8,128)}) custom-call(s32[1288]{0:T(1024)S(1)} %concatenate.25.hbm_ref, f32[257,128,128]{2,1,0:T(8,128)S(1)} %get-tuple-element.45.refs_0_, f32[16,128]{1,0:T(8,128)S(1)} %get-tuple-element.51.refs_1_, ...), custom_call_target="tpu_custom_call" | custom-call | tf_op jit(solution)/shard_map/plan/pallas_call | solution.py:608
  101.0 4.0 %rest_of_plan.1 = (bf16[2048,128]{1,0:T(8,128)(2,1)S(1)}, bf16[2048,128]{1,0:T(8,128)(2,1)S(1)}, bf16[2048,128]{1,0:T(8,128)(2,1)S(1)}) custom-call(s32[1288]{0:T(1024)S(1)} %concatenate.25.hbm_ref, bf16[35,512,256]{2,1,0:T(8,128)(2,1)S(1)} %get-tuple-element.54.refs_0_, bf16[2048,1024]{1,0:T(8,128)(2,1)S(1)} %get-tuple-element.52.refs_2_.refs_1_), custom_call_target="tpu_custom_call" | custom-call | flops 3221225472 | bytes 16777216 | tf_op jit(solution)/shard_map/rest_of_plan/pallas_call | solution.py:622
  105.1 15.2 %collective-permute-done.28 = bf16[2048,128]{1,0:T(8,128)(2,1)S(1)} collective-permute-done((bf16[2048,128]{1,0:T(8,128)(2,1)S(1)}, bf16[2048,128]{1,0:T(8,128)(2,1)S(1)}, u32[]{:S(2)}, u32[]{:S(2)}) %collective-permute-start.28) | collective-permute-done | bytes 524320 | tf_op jit(solution)/shard_map/ppermute | solution.py:21
  120.5 1.7 %collective-permute-start.29 = (bf16[2048,128]{1,0:T(8,128)(2,1)S(1)}, bf16[2048,128]{1,0:T(8,128)(2,1)S(1)}, u32[]{:S(2)}, u32[]{:S(2)}) collective-permute-start(bf16[2048,128]{1,0:T(8,128)(2,1)S(1)} %get-tuple-element.58), channel_id=1, source_target_pairs={{0,2},{1,3},{2,0},{3,1},{4,6},{5,7},{6,4},{7,5},{8,10},{9,11},{10,... | collective-permute-start | bytes 1572872 | tf_op jit(solution)/shard_map/ppermute | solution.py:21
  122.1 13.1 %collective-permute-done.30 = bf16[2048,128]{1,0:T(8,128)(2,1)S(1)} collective-permute-done((bf16[2048,128]{1,0:T(8,128)(2,1)S(1)}, bf16[2048,128]{1,0:T(8,128)(2,1)S(1)}, u32[]{:S(2)}, u32[]{:S(2)}) %collective-permute-start.30) | collective-permute-done | bytes 524320 | tf_op jit(solution)/shard_map/ppermute | solution.py:21
  135.3 1.0 add_convert_fusion
  (64 shorter events, 7.0 us)
Async XLA Ops:
  0.6 17.8 %collective-permute-start.2 = (bf16[1024,256]{1,0:T(8,128)(2,1)}, bf16[1024,256]{1,0:T(8,128)(2,1)S(1)}, u32[]{:S(2)}, u32[]{:S(2)}) collective-permute-start(bf16[1024,256]{1,0:T(8,128)(2,1)} %refs_1_.1), channel_id=1, source_target_pairs={{0,16},{8,24},{16,0},{24,8},{1,17},{9,25},{17,1},{25,9},{2,18},{10... | collective-permute-start | bytes 1572872 | tf_op jit(solution)/shard_map/ppermute | solution.py:21
  3.7 14.8 %collective-permute-start.1 = (bf16[1024,256]{1,0:T(8,128)(2,1)}, bf16[1024,256]{1,0:T(8,128)(2,1)S(1)}, u32[]{:S(2)}, u32[]{:S(2)}) collective-permute-start(bf16[1024,256]{1,0:T(8,128)(2,1)} %refs_1_.1), channel_id=1, source_target_pairs={{0,8},{8,0},{16,24},{24,16},{1,9},{9,1},{17,25},{25,17},{2,10},{10... | collective-permute-start | bytes 1572872 | tf_op jit(solution)/shard_map/ppermute | solution.py:21
  5.2 7.2 %collective-permute-start.3 = (bf16[1024,256]{1,0:T(8,128)(2,1)}, bf16[1024,256]{1,0:T(8,128)(2,1)S(1)}, u32[]{:S(2)}, u32[]{:S(2)}) collective-permute-start(bf16[1024,256]{1,0:T(8,128)(2,1)} %refs_1_.1), channel_id=1, source_target_pairs={{0,1},{1,0},{2,3},{3,2},{4,5},{5,4},{6,7},{7,6},{8,9},{9,8},{10,11... | collective-permute-start | bytes 1572872 | tf_op jit(solution)/shard_map/ppermute | solution.py:21
  5.2 2.1 %collective-permute-start = (s32[16,8]{0,1:T(8,128)}, s32[16,8]{0,1:T(8,128)S(1)}, u32[]{:S(2)}, u32[]{:S(2)}) collective-permute-start(s32[16,8]{0,1:T(8,128)} %param.5), channel_id=1, source_target_pairs={{0,1},{1,0},{2,3},{3,2},{4,5},{5,4},{6,7},{7,6},{8,9},{9,8},{10,11... | collective-permute-start | bytes 1544 | tf_op jit(solution)/shard_map/ppermute | solution.py:21
  12.4 2.2 %copy-start = (bf16[2048,1024]{1,0:T(8,128)(2,1)S(1)}, bf16[2048,1024]{1,0:T(8,128)(2,1)}, u32[]{:S(2)}) copy-start(bf16[2048,1024]{1,0:T(8,128)(2,1)} %refs_0_.5) | copy-start | bytes 12582916
  14.6 1.0 copy-start.2
  15.6 5.6 %copy-start.1 = (bf16[2048,1024]{1,0:T(8,128)(2,1)S(1)}, bf16[2048,1024]{1,0:T(8,128)(2,1)}, u32[]{:S(2)}) copy-start(bf16[2048,1024]{1,0:T(8,128)(2,1)} %refs_0_.5) | copy-start | bytes 12582916
  18.5 2.0 %collective-permute-start.7 = (bf16[1024,256]{1,0:T(8,128)(2,1)S(1)}, bf16[1024,256]{1,0:T(8,128)(2,1)S(1)}, u32[]{:S(2)}, u32[]{:S(2)}) collective-permute-start(bf16[1024,256]{1,0:T(8,128)(2,1)S(1)} %collective-permute-done.2.refs_2_), channel_id=1, source_target_pairs={{0,1},{1,0},{2,3},{3,2},{4,5},{5,4},{6,7},{7,6},{8,9},{9,8},{10,11... | collective-permute-start | bytes 1572872 | tf_op jit(solution)/shard_map/ppermute | solution.py:21
  18.7 2.5 %collective-permute-start.6 = (bf16[1024,256]{1,0:T(8,128)(2,1)S(1)}, bf16[1024,256]{1,0:T(8,128)(2,1)S(1)}, u32[]{:S(2)}, u32[]{:S(2)}) collective-permute-start(bf16[1024,256]{1,0:T(8,128)(2,1)S(1)} %collective-permute-done.1.refs_1_), channel_id=1, source_target_pairs={{0,1},{1,0},{2,3},{3,2},{4,5},{5,4},{6,7},{7,6},{8,9},{9,8},{10,11... | collective-permute-start | bytes 1572872 | tf_op jit(solution)/shard_map/ppermute | solution.py:21
  19.1 8.4 %collective-permute-start.5 = (bf16[512,256]{1,0:T(8,128)(2,1)S(1)}, bf16[512,256]{1,0:T(8,128)(2,1)S(1)}, u32[]{:S(2)}, u32[]{:S(2)}) collective-permute-start(bf16[512,256]{1,0:T(8,128)(2,1)S(1)} %slice.7), channel_id=1, source_target_pairs={{0,16},{8,24},{16,0},{24,8},{1,17},{9,25},{17,1},{25,9},{2,18},{10... | collective-permute-start | bytes 786440 | tf_op jit(solution)/shard_map/ppermute | solution.py:21
  19.7 8.1 %collective-permute-start.4 = (bf16[512,256]{1,0:T(8,128)(2,1)S(1)}, bf16[512,256]{1,0:T(8,128)(2,1)S(1)}, u32[]{:S(2)}, u32[]{:S(2)}) collective-permute-start(bf16[512,256]{1,0:T(8,128)(2,1)S(1)} %slice.6), channel_id=1, source_target_pairs={{0,8},{8,0},{16,24},{24,16},{1,9},{9,1},{17,25},{25,17},{2,10},{10... | collective-permute-start | bytes 786440 | tf_op jit(solution)/shard_map/ppermute | solution.py:21
  27.7 1.5 %collective-permute-start.8 = (bf16[512,256]{1,0:T(8,128)(2,1)S(1)}, bf16[512,256]{1,0:T(8,128)(2,1)S(1)}, u32[]{:S(2)}, u32[]{:S(2)}) collective-permute-start(bf16[512,256]{1,0:T(8,128)(2,1)S(1)} %collective-permute-done.4.refs_1_), channel_id=1, source_target_pairs={{0,1},{1,0},{2,3},{3,2},{4,5},{5,4},{6,7},{7,6},{8,9},{9,8},{10,11... | collective-permute-start | bytes 786440 | tf_op jit(solution)/shard_map/ppermute | solution.py:21
  27.7 1.9 %collective-permute-start.9 = (bf16[512,256]{1,0:T(8,128)(2,1)S(1)}, bf16[512,256]{1,0:T(8,128)(2,1)S(1)}, u32[]{:S(2)}, u32[]{:S(2)}) collective-permute-start(bf16[512,256]{1,0:T(8,128)(2,1)S(1)} %collective-permute-done.5.refs_2_), channel_id=1, source_target_pairs={{0,1},{1,0},{2,3},{3,2},{4,5},{5,4},{6,7},{7,6},{8,9},{9,8},{10,11... | collective-permute-start | bytes 786440 | tf_op jit(solution)/shard_map/ppermute | solution.py:21
  34.8 5.5 %collective-permute-start.12 = (f32[16,128]{1,0:T(8,128)S(1)}, f32[16,128]{1,0:T(8,128)S(1)}, u32[]{:S(2)}, u32[]{:S(2)}) collective-permute-start(f32[16,128]{1,0:T(8,128)S(1)} %get-tuple-element.48.refs_3_), channel_id=1, source_target_pairs={{0,6},{1,7},{2,4},{3,5},{4,2},{5,3},{6,0},{7,1},{8,14},{9,15},{10,... | collective-permute-start | bytes 24584 | tf_op jit(solution)/shard_map/ppermute | solution.py:21
  37.6 4.5 %collective-permute-start.11 = (f32[16,128]{1,0:T(8,128)S(1)}, f32[16,128]{1,0:T(8,128)S(1)}, u32[]{:S(2)}, u32[]{:S(2)}) collective-permute-start(f32[16,128]{1,0:T(8,128)S(1)} %get-tuple-element.48.refs_3_), channel_id=1, source_target_pairs={{0,4},{1,5},{2,6},{3,7},{4,0},{5,1},{6,2},{7,3},{8,12},{9,13},{10,... | collective-permute-start | bytes 24584 | tf_op jit(solution)/shard_map/ppermute | solution.py:21
  37.6 4.5 %collective-permute-start.10 = (f32[16,128]{1,0:T(8,128)S(1)}, f32[16,128]{1,0:T(8,128)S(1)}, u32[]{:S(2)}, u32[]{:S(2)}) collective-permute-start(f32[16,128]{1,0:T(8,128)S(1)} %get-tuple-element.48.refs_3_), channel_id=1, source_target_pairs={{0,2},{1,3},{2,0},{3,1},{4,6},{5,7},{6,4},{7,5},{8,10},{9,11},{10,... | collective-permute-start | bytes 24584 | tf_op jit(solution)/shard_map/ppermute | solution.py:21
  44.4 5.8 %collective-permute-start.15 = (f32[16,128]{1,0:T(8,128)S(1)}, f32[16,128]{1,0:T(8,128)S(1)}, u32[]{:S(2)}, u32[]{:S(2)}) collective-permute-start(f32[16,128]{1,0:T(8,128)S(1)} %get-tuple-element.49.refs_3_), channel_id=1, source_target_pairs={{0,24},{8,16},{16,8},{24,0},{1,25},{9,17},{17,9},{25,1},{2,26},{10... | collective-permute-start | bytes 24584 | tf_op jit(solution)/shard_map/ppermute | solution.py:21
  48.5 3.7 %collective-permute-start.14 = (f32[16,128]{1,0:T(8,128)S(1)}, f32[16,128]{1,0:T(8,128)S(1)}, u32[]{:S(2)}, u32[]{:S(2)}) collective-permute-start(f32[16,128]{1,0:T(8,128)S(1)} %get-tuple-element.49.refs_3_), channel_id=1, source_target_pairs={{0,16},{8,24},{16,0},{24,8},{1,17},{9,25},{17,1},{25,9},{2,18},{10... | collective-permute-start | bytes 24584 | tf_op jit(solution)/shard_map/ppermute | solution.py:21
  48.5 3.7 %collective-permute-start.13 = (f32[16,128]{1,0:T(8,128)S(1)}, f32[16,128]{1,0:T(8,128)S(1)}, u32[]{:S(2)}, u32[]{:S(2)}) collective-permute-start(f32[16,128]{1,0:T(8,128)S(1)} %get-tuple-element.49.refs_3_), channel_id=1, source_target_pairs={{0,8},{8,0},{16,24},{24,16},{1,9},{9,1},{17,25},{25,17},{2,10},{10... | collective-permute-start | bytes 24584 | tf_op jit(solution)/shard_map/ppermute | solution.py:21
  54.2 6.5 %collective-permute-start.18 = (f32[16,128]{1,0:T(8,128)S(1)}, f32[16,128]{1,0:T(8,128)S(1)}, u32[]{:S(2)}, u32[]{:S(2)}) collective-permute-start(f32[16,128]{1,0:T(8,128)S(1)} %row_pass.2.refs_3_), channel_id=1, source_target_pairs={{0,6},{1,7},{2,4},{3,5},{4,2},{5,3},{6,0},{7,1},{8,14},{9,15},{10,... | collective-permute-start | bytes 24584 | tf_op jit(solution)/shard_map/ppermute | solution.py:21
  55.4 6.9 %collective-permute-start.17 = (f32[16,128]{1,0:T(8,128)S(1)}, f32[16,128]{1,0:T(8,128)S(1)}, u32[]{:S(2)}, u32[]{:S(2)}) collective-permute-start(f32[16,128]{1,0:T(8,128)S(1)} %row_pass.2.refs_3_), channel_id=1, source_target_pairs={{0,4},{1,5},{2,6},{3,7},{4,0},{5,1},{6,2},{7,3},{8,12},{9,13},{10,... | collective-permute-start | bytes 24584 | tf_op jit(solution)/shard_map/ppermute | solution.py:21
  60.6 3.7 %collective-permute-start.16 = (f32[16,128]{1,0:T(8,128)S(1)}, f32[16,128]{1,0:T(8,128)S(1)}, u32[]{:S(2)}, u32[]{:S(2)}) collective-permute-start(f32[16,128]{1,0:T(8,128)S(1)} %row_pass.2.refs_3_), channel_id=1, source_target_pairs={{0,2},{1,3},{2,0},{3,1},{4,6},{5,7},{6,4},{7,5},{8,10},{9,11},{10,... | collective-permute-start | bytes 24584 | tf_op jit(solution)/shard_map/ppermute | solution.py:21
  66.5 5.6 %collective-permute-start.21 = (f32[16,128]{1,0:T(8,128)S(1)}, f32[16,128]{1,0:T(8,128)S(1)}, u32[]{:S(2)}, u32[]{:S(2)}) collective-permute-start(f32[16,128]{1,0:T(8,128)S(1)} %get-tuple-element.50.refs_3_), channel_id=1, source_target_pairs={{0,24},{8,16},{16,8},{24,0},{1,25},{9,17},{17,9},{25,1},{2,26},{10... | collective-permute-start | bytes 24584 | tf_op jit(solution)/shard_map/ppermute | solution.py:21
  70.5 3.7 %collective-permute-start.20 = (f32[16,128]{1,0:T(8,128)S(1)}, f32[16,128]{1,0:T(8,128)S(1)}, u32[]{:S(2)}, u32[]{:S(2)}) collective-permute-start(f32[16,128]{1,0:T(8,128)S(1)} %get-tuple-element.50.refs_3_), channel_id=1, source_target_pairs={{0,16},{8,24},{16,0},{24,8},{1,17},{9,25},{17,1},{25,9},{2,18},{10... | collective-permute-start | bytes 24584 | tf_op jit(solution)/shard_map/ppermute | solution.py:21
  70.5 3.7 %collective-permute-start.19 = (f32[16,128]{1,0:T(8,128)S(1)}, f32[16,128]{1,0:T(8,128)S(1)}, u32[]{:S(2)}, u32[]{:S(2)}) collective-permute-start(f32[16,128]{1,0:T(8,128)S(1)} %get-tuple-element.50.refs_3_), channel_id=1, source_target_pairs={{0,8},{8,0},{16,24},{24,16},{1,9},{9,1},{17,25},{25,17},{2,10},{10... | collective-permute-start | bytes 24584 | tf_op jit(solution)/shard_map/ppermute | solution.py:21
  76.0 6.7 %collective-permute-start.24 = (f32[16,128]{1,0:T(8,128)S(1)}, f32[16,128]{1,0:T(8,128)S(1)}, u32[]{:S(2)}, u32[]{:S(2)}) collective-permute-start(f32[16,128]{1,0:T(8,128)S(1)} %row_pass.3.refs_3_), channel_id=1, source_target_pairs={{0,6},{1,7},{2,4},{3,5},{4,2},{5,3},{6,0},{7,1},{8,14},{9,15},{10,... | collective-permute-start | bytes 24584 | tf_op jit(solution)/shard_map/ppermute | solution.py:21
  76.8 7.6 %collective-permute-start.23 = (f32[16,128]{1,0:T(8,128)S(1)}, f32[16,128]{1,0:T(8,128)S(1)}, u32[]{:S(2)}, u32[]{:S(2)}) collective-permute-start(f32[16,128]{1,0:T(8,128)S(1)} %row_pass.3.refs_3_), channel_id=1, source_target_pairs={{0,4},{1,5},{2,6},{3,7},{4,0},{5,1},{6,2},{7,3},{8,12},{9,13},{10,... | collective-permute-start | bytes 24584 | tf_op jit(solution)/shard_map/ppermute | solution.py:21
  82.7 3.7 %collective-permute-start.22 = (f32[16,128]{1,0:T(8,128)S(1)}, f32[16,128]{1,0:T(8,128)S(1)}, u32[]{:S(2)}, u32[]{:S(2)}) collective-permute-start(f32[16,128]{1,0:T(8,128)S(1)} %row_pass.3.refs_3_), channel_id=1, source_target_pairs={{0,2},{1,3},{2,0},{3,1},{4,6},{5,7},{6,4},{7,5},{8,10},{9,11},{10,... | collective-permute-start | bytes 24584 | tf_op jit(solution)/shard_map/ppermute | solution.py:21
  88.8 6.4 %collective-permute-start.27 = (f32[16,128]{1,0:T(8,128)S(1)}, f32[16,128]{1,0:T(8,128)S(1)}, u32[]{:S(2)}, u32[]{:S(2)}) collective-permute-start(f32[16,128]{1,0:T(8,128)S(1)} %get-tuple-element.53.refs_3_), channel_id=1, source_target_pairs={{0,24},{8,16},{16,8},{24,0},{1,25},{9,17},{17,9},{25,1},{2,26},{10... | collective-permute-start | bytes 24584 | tf_op jit(solution)/shard_map/ppermute | solution.py:21
  93.6 3.7 %collective-permute-start.26 = (f32[16,128]{1,0:T(8,128)S(1)}, f32[16,128]{1,0:T(8,128)S(1)}, u32[]{:S(2)}, u32[]{:S(2)}) collective-permute-start(f32[16,128]{1,0:T(8,128)S(1)} %get-tuple-element.53.refs_3_), channel_id=1, source_target_pairs={{0,16},{8,24},{16,0},{24,8},{1,17},{9,25},{17,1},{25,9},{2,18},{10... | collective-permute-start | bytes 24584 | tf_op jit(solution)/shard_map/ppermute | solution.py:21
  93.6 3.7 %collective-permute-start.25 = (f32[16,128]{1,0:T(8,128)S(1)}, f32[16,128]{1,0:T(8,128)S(1)}, u32[]{:S(2)}, u32[]{:S(2)}) collective-permute-start(f32[16,128]{1,0:T(8,128)S(1)} %get-tuple-element.53.refs_3_), channel_id=1, source_target_pairs={{0,8},{8,0},{16,24},{24,16},{1,9},{9,1},{17,25},{25,17},{2,10},{10... | collective-permute-start | bytes 24584 | tf_op jit(solution)/shard_map/ppermute | solution.py:21
  100.9 19.3 %collective-permute-start.28 = (bf16[2048,128]{1,0:T(8,128)(2,1)S(1)}, bf16[2048,128]{1,0:T(8,128)(2,1)S(1)}, u32[]{:S(2)}, u32[]{:S(2)}) collective-permute-start(bf16[2048,128]{1,0:T(8,128)(2,1)S(1)} %get-tuple-element.56), channel_id=1, source_target_pairs={{0,2},{1,3},{2,0},{3,1},{4,6},{5,7},{6,4},{7,5},{8,10},{9,11},{10,... | collective-permute-start | bytes 1572872 | tf_op jit(solution)/shard_map/ppermute | solution.py:21
  120.4 14.8 %collective-permute-start.30 = (bf16[2048,128]{1,0:T(8,128)(2,1)S(1)}, bf16[2048,128]{1,0:T(8,128)(2,1)S(1)}, u32[]{:S(2)}, u32[]{:S(2)}) collective-permute-start(bf16[2048,128]{1,0:T(8,128)(2,1)S(1)} %add_convert_fusion.1), channel_id=1, source_target_pairs={{0,4},{1,5},{2,6},{3,7},{4,0},{5,1},{6,2},{7,3},{8,12},{9,13},{10,... | collective-permute-start | bytes 1572872 | tf_op jit(solution)/shard_map/ppermute | solution.py:21
  120.5 14.9 %collective-permute-start.29 = (bf16[2048,128]{1,0:T(8,128)(2,1)S(1)}, bf16[2048,128]{1,0:T(8,128)(2,1)S(1)}, u32[]{:S(2)}, u32[]{:S(2)}) collective-permute-start(bf16[2048,128]{1,0:T(8,128)(2,1)S(1)} %get-tuple-element.58), channel_id=1, source_target_pairs={{0,2},{1,3},{2,0},{3,1},{4,6},{5,7},{6,4},{7,5},{8,10},{9,11},{10,... | collective-permute-start | bytes 1572872 | tf_op jit(solution)/shard_map/ppermute | solution.py:21

commit v17 on v16

--- a/solution.py
+++ b/solution.py
@@ -10,6 +10,7 @@
 
 ITERS = 3
 TILE = 128
+PARTS = 2
 NEGATIVE = -1e30
 
 VMEM = pl.BlockSpec(memory_space=pltpu.VMEM)
@@ -406,20 +407,23 @@
     table.each_item(table_ref, visit)
     for t in range(row_tiles):
         total = total_ref[t].astype(jnp.bfloat16)
-        rows = slice(t * TILE, (t + 1) * TILE)
+        part, at = divmod(t * TILE, outs[0].shape[0])
+        rows = slice(at, at + TILE)
         for n, j in enumerate(wanted):
+            out_ref = outs[PARTS * n + part]
             if fits:
-                outs[n][rows, :] = total[:, n * width : (n + 1) * width]
+                out_ref[rows, :] = total[:, n * width : (n + 1) * width]
                 continue
             for k in range(lines):
 
                 @pl.when(jnp.bitwise_xor(z, j) == k)
                 def _():
-                    outs[n][rows, :] = total[:, k * width : (k + 1) * width]
+                    out_ref[rows, :] = total[:, k * width : (k + 1) * width]
 
 
 def plan_kernel(table, log_column, lines, arrived, s_ref, r_ref, p_ref, *refs):
-    parts, (out_ref, kept_ref, own_ref, c_ref, wide_ref, total_ref) = refs[:-6], refs[-6:]
+    *refs, kept_ref, own_ref, c_ref, wide_ref, total_ref = refs
+    parts, outs = refs[:-PARTS], refs[-PARTS:]
     row_tiles, columns = table.row_tiles, table.columns
     core = lax.rem(lax.axis_index("proto"), 2)
     c_ref[...] = log_column - combine([part[...] for part in parts])
@@ -443,8 +447,8 @@
         kept_ref[number] = strips
         return strips
 
-    width = out_ref.shape[1]
-    plan_blocks(table, table_ref, p_ref, lines, [lines - 1], width, strip, [out_ref], total_ref)
+    width = outs[0].shape[1]
+    plan_blocks(table, table_ref, p_ref, lines, [lines - 1], width, strip, outs, total_ref)
 
 
 def rest_kernel(table, lines, arrived, kept_ref, p_ref, *refs):
@@ -530,16 +534,20 @@
 
 
 def scatter_partials(blocks):
-    blocks = list(blocks)
+    blocks = [blocks[at : at + PARTS] for at in range(0, len(blocks), PARTS)]
     distance = 1
     while distance < len(blocks):
         for j in range(len(blocks) - distance, 0, -2 * distance):
-            got = swap(blocks[j].astype(jnp.bfloat16), "proto", 2 * distance)
+            got = [swap(part.astype(jnp.bfloat16), "proto", 2 * distance) for part in blocks[j]]
             if j == 3 * distance:
-                got, blocks[distance] = tied(got, blocks[distance])
-            blocks[j ^ distance] = blocks[j ^ distance].astype(jnp.float32) + got.astype(jnp.float32)
+                tie = tied(*got, *blocks[distance])
+                got, blocks[distance] = tie[:PARTS], tie[PARTS:]
+            blocks[j ^ distance] = [
+                part.astype(jnp.float32) + other.astype(jnp.float32)
+                for part, other in zip(blocks[j ^ distance], got)
+            ]
         distance *= 2
-    return blocks[0].astype(jnp.bfloat16)
+    return jnp.concatenate([part.astype(jnp.bfloat16) for part in blocks[0]], axis=0)
 
 
 def shards(embeddings, prototypes, block_mask):
@@ -599,21 +607,21 @@
             name="column_pass",
         )(lists, similar, kept, first, *parts)
     parts = column_exchange(column_part)
-    block = jax.ShapeDtypeStruct((rows, width), jnp.bfloat16)
+    block = jax.ShapeDtypeStruct((rows // PARTS, width), jnp.bfloat16)
 
     def sums(blocks):
         taken = blocks if width % TILE == 0 else lines
         return pltpu.VMEM((row_tiles, TILE, taken * width), jnp.float32)
 
-    last, plan, column_potential = pl.pallas_call(
+    *last, plan, column_potential = pl.pallas_call(
         with_table(plan_kernel, table, log_column, lines),
-        out_shape=[
-            block,
+        out_shape=[block] * PARTS
+        + [
             pltpu.VMEM((table.slots, 4 * TILE, 2 * TILE), jnp.bfloat16),
             jax.ShapeDtypeStruct((half, TILE), jnp.float32),
         ],
         in_specs=[ANY] + [VMEM] * (3 + len(parts)),
-        out_specs=[VMEM] * 3,
+        out_specs=[VMEM] * (PARTS + 2),
         scratch_shapes=[pltpu.VMEM((columns, TILE), jnp.float32), wide, sums(1)] + table_scratch(lists),
         compiler_params=params(12),
         name="plan",
@@ -621,9 +629,9 @@
     visits = table.dummy * TILE * TILE
     blocks = pl.pallas_call(
         with_table(rest_kernel, table, lines),
-        out_shape=[block] * (lines - 1),
+        out_shape=[block] * (PARTS * (lines - 1)),
         in_specs=[ANY] + [VMEM] * 2,
-        out_specs=[VMEM] * (lines - 1),
+        out_specs=[VMEM] * (PARTS * (lines - 1)),
         scratch_shapes=[sums(lines - 1)] + table_scratch(lists),
         compiler_params=params(12),
         cost_estimate=pl.CostEstimate(
@@ -631,7 +639,7 @@
         ),
         name="rest_of_plan",
     )(lists, plan, whole)
-    blocks = list(blocks) + [last]
+    blocks = list(blocks) + last
     targets = scatter_partials(blocks)
     return (targets, row_out.reshape(rows), column_potential.reshape(protos // 2))
 

time: 138 us -> 138 us (level)
  starting transfers between devices: 41.7 us -> 49.6 us
  Pallas kernels: 30.8 us -> 26.6 us
  waiting for transfers between devices: 52.8 us -> 50 us
    ppermute x31 -> x34, starting transfers between devices: 41.7 us -> 49.6 us  [swap(): return lax.ppermute(x, axis, [(i, i ^ offset) for i in range(size)])]
    ppermute x31 -> x34, waiting for transfers between devices: 52.8 us -> 50 us  [swap(): return lax.ppermute(x, axis, [(i, i ^ offset) for i in range(size)])]
    pallas_call x2, Pallas kernels: 7.1 us -> 5.66 us  [early(): pl.pallas_call(with_table(early_panel_kernel, table, places, owners, bool...]
  transfers between devices with their start and end apart: 31 -> 34, of which waited for: 22 -> 22; matrix products, arithmetic and copies ran while one was open for 3% -> 3% of each run, Pallas kernels for 8% -> 7%
where the time goes in v17:
time: 138 us; the launch traced here: 137 us
  waiting for transfers between devices  50 us (36%)
  starting transfers between devices  49.6 us (36%)
  Pallas kernels  26.6 us (19%)
  other arithmetic  4.44 us (3%)
  local copies, waits for them, and re-layouts  4.41 us (3%)
  between operations  2.2 us (2%)
    ppermute x34, waiting for transfers between devices, swap(): return lax.ppermute(x, axis, [(i, i ^ offset) for i in range(size)])  50 us
    ppermute x34, starting transfers between devices, swap(): return lax.ppermute(x, axis, [(i, i ^ offset) for i in range(size)])  49.6 us
    pallas_call x3, Pallas kernels, shards(): pl.pallas_call(with_table(column_kernel, table), out_shape=(column_shape,...  6.68 us
    pallas_call x2, Pallas kernels, early(): pl.pallas_call(with_table(early_panel_kernel, table, places, owners, bool...  5.66 us
    pallas_call x1, Pallas kernels, late(): pl.pallas_call(with_table(panel_kernel, table, places, add), out_shape=(p...  4.24 us
    pallas_call x2, Pallas kernels, shards(): pl.pallas_call(with_table(row_kernel, table, log_column), out_shape=row_s...  3.63 us
    pallas_call x1, Pallas kernels, shards(): pl.pallas_call(with_table(rest_kernel, table, lines), out_shape=[block] *...  3.27 us
    unnamed x6, local copies, waits for them, and re-layouts  3.23 us
  transfers between devices with their start and end apart: 34, of which 22 were waited for; matrix products, arithmetic and copies ran while one was open for 3% of the time, Pallas kernels for 7%

profile of v17, /device:TPU:0, one launch (start us, length us, event | category | flops | bytes accessed | tf_op | source)
XLA Modules:
  0.0 137.2 jit_solution(5930396120818612253)
XLA Ops:
  0.6 3.0 %collective-permute-start.2 = (bf16[1024,256]{1,0:T(8,128)(2,1)}, bf16[1024,256]{1,0:T(8,128)(2,1)S(1)}, u32[]{:S(2)}, u32[]{:S(2)}) collective-permute-start(bf16[1024,256]{1,0:T(8,128)(2,1)} %refs_1_.1), channel_id=1, source_target_pairs={{0,16},{8,24},{16,0},{24,8},{1,17},{9,25},{17,1},{25,9},{2,18},{10... | collective-permute-start | bytes 1572872 | tf_op jit(solution)/shard_map/ppermute | solution.py:22
  3.7 1.5 %collective-permute-start.1 = (bf16[1024,256]{1,0:T(8,128)(2,1)}, bf16[1024,256]{1,0:T(8,128)(2,1)S(1)}, u32[]{:S(2)}, u32[]{:S(2)}) collective-permute-start(bf16[1024,256]{1,0:T(8,128)(2,1)} %refs_1_.1), channel_id=1, source_target_pairs={{0,8},{8,0},{16,24},{24,16},{1,9},{9,1},{17,25},{25,17},{2,10},{10... | collective-permute-start | bytes 1572872 | tf_op jit(solution)/shard_map/ppermute | solution.py:22
  5.7 0.7 compare_select_fusion.1
  6.4 0.9 collective-permute-done
  11.6 0.7 concatenate.28.hbm_ref
  12.4 2.2 %copy-done = bf16[2048,1024]{1,0:T(8,128)(2,1)S(1)} copy-done((bf16[2048,1024]{1,0:T(8,128)(2,1)S(1)}, bf16[2048,1024]{1,0:T(8,128)(2,1)}, u32[]{:S(2)}) %copy-start) | copy-done | bytes 4194328
  14.6 1.0 copy-done.2
  15.6 2.3 %early_panel.2 = (f32[257,128,128]{2,1,0:T(8,128)S(1)}, bf16[2048,1024]{1,0:T(8,128)(2,1)S(1)}) custom-call(s32[1288]{0:T(1024)S(1)} %concatenate.28.hbm_ref, bf16[2048,1024]{1,0:T(8,128)(2,1)S(1)} %copy-done, bf16[1024,256]{1,0:T(8,128)(2,1)S(1)} %copy-done.2, bf16[1024,256]{1,0:T(8,128)(2,1)S(1)} %collective-permute-done.3.refs_2_), custom_call_target="tpu_custom_call" | custom-call | flops 1073741824 | bytes 33554432 | tf_op jit(solution)/shard_map/early_panel/pallas_call | solution.py:505
  19.1 1.8 %collective-permute-start.4 = (bf16[512,256]{1,0:T(8,128)(2,1)S(1)}, bf16[512,256]{1,0:T(8,128)(2,1)S(1)}, u32[]{:S(2)}, u32[]{:S(2)}) collective-permute-start(bf16[512,256]{1,0:T(8,128)(2,1)S(1)} %slice.6), channel_id=1, source_target_pairs={{0,8},{8,0},{16,24},{24,16},{1,9},{9,1},{17,25},{25,17},{2,10},{10... | collective-permute-start | bytes 786440 | tf_op jit(solution)/shard_map/ppermute | solution.py:22
  20.9 3.4 %early_panel.3 = (f32[257,128,128]{2,1,0:T(8,128)S(1)}, bf16[2048,1024]{1,0:T(8,128)(2,1)S(1)}) custom-call(s32[1288]{0:T(1024)S(1)} %concatenate.28.hbm_ref, bf16[2048,1024]{1,0:T(8,128)(2,1)S(1)} %copy-done.1, bf16[1024,256]{1,0:T(8,128)(2,1)S(1)} %collective-permute-done.1.refs_1_, ...), custom_call_target="tpu_custom_call", output_to_operand_aliasing={{0}: (6, {}), {1}: (7, {})} | custom-call | flops 2147483648 | bytes 33554432 | tf_op jit(solution)/shard_map/early_panel/pallas_call | solution.py:505
  24.3 2.7 %collective-permute-done.5.refs_2_ = bf16[512,256]{1,0:T(8,128)(2,1)S(1)} collective-permute-done((bf16[512,256]{1,0:T(8,128)(2,1)S(1)}, bf16[512,256]{1,0:T(8,128)(2,1)S(1)}, u32[]{:S(2)}, u32[]{:S(2)}) %collective-permute-start.5) | collective-permute-done | bytes 262176 | tf_op jit(solution)/shard_map/ppermute | solution.py:22
  27.7 1.0 collective-permute-done.8.refs_3_
  29.1 4.2 %panel.1 = (f32[257,128,128]{2,1,0:T(8,128)S(1)}, bf16[2048,1024]{1,0:T(8,128)(2,1)S(1)}, bf16[257,128,128]{2,1,0:T(8,128)(2,1)S(1)}, f32[16,128]{1,0:T(8,128)S(1)}, f32[16,128]{1,0:T(8,128)S(1)}) custom-call(s32[1288]{0:T(1024)S(1)} %concatenate.28.hbm_ref, bf16[2048,1024]{1,0:T(8,128)(2,1)S(1)} %copy-done.1, ...), custom_call_target="tpu_custom_call", output_to_operand_aliasing={{0}: (6, {}), {1}: (7, {})} | custom-call | tf_op jit(solution)/shard_map/panel/pallas_call | solution.py:484
  33.3 4.2 %collective-permute-start.12 = (f32[16,128]{1,0:T(8,128)S(1)}, f32[16,128]{1,0:T(8,128)S(1)}, u32[]{:S(2)}, u32[]{:S(2)}) collective-permute-start(f32[16,128]{1,0:T(8,128)S(1)} %get-tuple-element.54.refs_3_), channel_id=1, source_target_pairs={{0,6},{1,7},{2,4},{3,5},{4,2},{5,3},{6,0},{7,1},{8,14},{9,15},{10,... | collective-permute-start | bytes 24584 | tf_op jit(solution)/shard_map/ppermute | solution.py:22
  37.6 0.6 collective-permute-start.10
  38.2 1.0 collective-permute-done.12.refs_6_
  39.2 2.9 %collective-permute-done.11.refs_5_ = f32[16,128]{1,0:T(8,128)S(1)} collective-permute-done((f32[16,128]{1,0:T(8,128)S(1)}, f32[16,128]{1,0:T(8,128)S(1)}, u32[]{:S(2)}, u32[]{:S(2)}) %collective-permute-start.11) | collective-permute-done | bytes 8224 | tf_op jit(solution)/shard_map/ppermute | solution.py:22
  42.1 2.2 %column_pass.3 = (f32[16,128]{1,0:T(8,128)S(1)}, f32[16,128]{1,0:T(8,128)}, f32[16,128]{1,0:T(8,128)}) custom-call(s32[1288]{0:T(1024)S(1)} %concatenate.28.hbm_ref, f32[257,128,128]{2,1,0:T(8,128)S(1)} %get-tuple-element.51.refs_0_, bf16[257,128,128]{2,1,0:T(8,128)(2,1)S(1)} %get-tuple-element.52.refs_1_, f32[16,128]{1,0:T(8,128)S(1)} %get-tuple-element.53.refs_2_, ...), custom_call_target="tpu_custom_call" | custom-call | tf_op jit(solution)/shard_map/column_pass/pallas_call | solution.py:600
  44.3 3.9 %collective-permute-start.15 = (f32[16,128]{1,0:T(8,128)S(1)}, f32[16,128]{1,0:T(8,128)S(1)}, u32[]{:S(2)}, u32[]{:S(2)}) collective-permute-start(f32[16,128]{1,0:T(8,128)S(1)} %get-tuple-element.55.refs_3_), channel_id=1, source_target_pairs={{0,24},{8,16},{16,8},{24,0},{1,25},{9,17},{17,9},{25,1},{2,26},{10... | collective-permute-start | bytes 24584 | tf_op jit(solution)/shard_map/ppermute | solution.py:22
  48.8 1.0 collective-permute-done.15.refs_6_
  49.8 2.0 %collective-permute-done.14.refs_5_ = f32[16,128]{1,0:T(8,128)S(1)} collective-permute-done((f32[16,128]{1,0:T(8,128)S(1)}, f32[16,128]{1,0:T(8,128)S(1)}, u32[]{:S(2)}, u32[]{:S(2)}) %collective-permute-start.14) | collective-permute-done | bytes 8224 | tf_op jit(solution)/shard_map/ppermute | solution.py:22
  51.8 1.9 %row_pass.2.refs_3_ = f32[16,128]{1,0:T(8,128)S(1)} custom-call(s32[1288]{0:T(1024)S(1)} %concatenate.28.hbm_ref, f32[257,128,128]{2,1,0:T(8,128)S(1)} %get-tuple-element.51.refs_0_, bf16[257,128,128]{2,1,0:T(8,128)(2,1)S(1)} %get-tuple-element.52.refs_1_, f32[16,128]{1,0:T(8,128)S(1)} %get-tuple-element.53.refs_2_, ...), custom_call_target="tpu_custom_call" | custom-call | tf_op jit(solution)/shard_map/row_pass/pallas_call | solution.py:590
  53.7 6.2 %collective-permute-start.18 = (f32[16,128]{1,0:T(8,128)S(1)}, f32[16,128]{1,0:T(8,128)S(1)}, u32[]{:S(2)}, u32[]{:S(2)}) collective-permute-start(f32[16,128]{1,0:T(8,128)S(1)} %row_pass.2.refs_3_), channel_id=1, source_target_pairs={{0,6},{1,7},{2,4},{3,5},{4,2},{5,3},{6,0},{7,1},{8,14},{9,15},{10,... | collective-permute-start | bytes 24584 | tf_op jit(solution)/shard_map/ppermute | solution.py:22
  60.5 1.0 collective-permute-done.18.refs_6_
  61.5 2.9 %collective-permute-done.17.refs_5_ = f32[16,128]{1,0:T(8,128)S(1)} collective-permute-done((f32[16,128]{1,0:T(8,128)S(1)}, f32[16,128]{1,0:T(8,128)S(1)}, u32[]{:S(2)}, u32[]{:S(2)}) %collective-permute-start.17) | collective-permute-done | bytes 8224 | tf_op jit(solution)/shard_map/ppermute | solution.py:22
  64.4 2.2 %column_pass.4 = (f32[16,128]{1,0:T(8,128)S(1)}, f32[16,128]{1,0:T(8,128)}, f32[16,128]{1,0:T(8,128)}) custom-call(s32[1288]{0:T(1024)S(1)} %concatenate.28.hbm_ref, f32[257,128,128]{2,1,0:T(8,128)S(1)} %get-tuple-element.51.refs_0_, bf16[257,128,128]{2,1,0:T(8,128)(2,1)S(1)} %get-tuple-element.52.refs_1_, f32[16,128]{1,0:T(8,128)S(1)} %get-tuple-element.53.refs_2_, ...), custom_call_target="tpu_custom_call" | custom-call | tf_op jit(solution)/shard_map/column_pass/pallas_call | solution.py:600
  66.6 4.0 %collective-permute-start.21 = (f32[16,128]{1,0:T(8,128)S(1)}, f32[16,128]{1,0:T(8,128)S(1)}, u32[]{:S(2)}, u32[]{:S(2)}) collective-permute-start(f32[16,128]{1,0:T(8,128)S(1)} %get-tuple-element.56.refs_3_), channel_id=1, source_target_pairs={{0,24},{8,16},{16,8},{24,0},{1,25},{9,17},{17,9},{25,1},{2,26},{10... | collective-permute-start | bytes 24584 | tf_op jit(solution)/shard_map/ppermute | solution.py:22
  70.6 1.3 collective-permute-start.19
  72.2 2.0 %collective-permute-done.20.refs_5_ = f32[16,128]{1,0:T(8,128)S(1)} collective-permute-done((f32[16,128]{1,0:T(8,128)S(1)}, f32[16,128]{1,0:T(8,128)S(1)}, u32[]{:S(2)}, u32[]{:S(2)}) %collective-permute-start.20) | collective-permute-done | bytes 8224 | tf_op jit(solution)/shard_map/ppermute | solution.py:22
  74.2 1.7 %row_pass.3.refs_3_ = f32[16,128]{1,0:T(8,128)S(1)} custom-call(s32[1288]{0:T(1024)S(1)} %concatenate.28.hbm_ref, f32[257,128,128]{2,1,0:T(8,128)S(1)} %get-tuple-element.51.refs_0_, bf16[257,128,128]{2,1,0:T(8,128)(2,1)S(1)} %get-tuple-element.52.refs_1_, f32[16,128]{1,0:T(8,128)S(1)} %get-tuple-element.53.refs_2_, ...), custom_call_target="tpu_custom_call" | custom-call | tf_op jit(solution)/shard_map/row_pass/pallas_call | solution.py:590
  76.0 6.2 %collective-permute-start.24 = (f32[16,128]{1,0:T(8,128)S(1)}, f32[16,128]{1,0:T(8,128)S(1)}, u32[]{:S(2)}, u32[]{:S(2)}) collective-permute-start(f32[16,128]{1,0:T(8,128)S(1)} %row_pass.3.refs_3_), channel_id=1, source_target_pairs={{0,6},{1,7},{2,4},{3,5},{4,2},{5,3},{6,0},{7,1},{8,14},{9,15},{10,... | collective-permute-start | bytes 24584 | tf_op jit(solution)/shard_map/ppermute | solution.py:22
  82.8 1.0 collective-permute-done.24.refs_6_
  83.8 2.9 %collective-permute-done.23.refs_5_ = f32[16,128]{1,0:T(8,128)S(1)} collective-permute-done((f32[16,128]{1,0:T(8,128)S(1)}, f32[16,128]{1,0:T(8,128)S(1)}, u32[]{:S(2)}, u32[]{:S(2)}) %collective-permute-start.23) | collective-permute-done | bytes 8224 | tf_op jit(solution)/shard_map/ppermute | solution.py:22
  86.7 2.4 %column_pass.5 = (f32[16,128]{1,0:T(8,128)S(1)}, f32[16,128]{1,0:T(8,128)S(1)}, f32[16,128]{1,0:T(8,128)}) custom-call(s32[1288]{0:T(1024)S(1)} %concatenate.28.hbm_ref, f32[257,128,128]{2,1,0:T(8,128)S(1)} %get-tuple-element.51.refs_0_, bf16[257,128,128]{2,1,0:T(8,128)(2,1)S(1)} %get-tuple-element.52.refs_1_, f32[16,128]{1,0:T(8,128)S(1)} %get-tuple-element.53.refs_2_, ...), custom_call_target="tpu_custom_call" | custom-call | tf_op jit(solution)/shard_map/column_pass/pallas_call | solution.py:600
  89.1 5.1 %collective-permute-start.27 = (f32[16,128]{1,0:T(8,128)S(1)}, f32[16,128]{1,0:T(8,128)S(1)}, u32[]{:S(2)}, u32[]{:S(2)}) collective-permute-start(f32[16,128]{1,0:T(8,128)S(1)} %get-tuple-element.59.refs_3_), channel_id=1, source_target_pairs={{0,24},{8,16},{16,8},{24,0},{1,25},{9,17},{17,9},{25,1},{2,26},{10... | collective-permute-start | bytes 24584 | tf_op jit(solution)/shard_map/ppermute | solution.py:22
  94.8 1.0 collective-permute-done.27.refs_6_
  95.8 2.0 %collective-permute-done.26.refs_5_ = f32[16,128]{1,0:T(8,128)S(1)} collective-permute-done((f32[16,128]{1,0:T(8,128)S(1)}, f32[16,128]{1,0:T(8,128)S(1)}, u32[]{:S(2)}, u32[]{:S(2)}) %collective-permute-start.26) | collective-permute-done | bytes 8224 | tf_op jit(solution)/shard_map/ppermute | solution.py:22
  97.9 3.1 %plan.1 = (bf16[1024,128]{1,0:T(8,128)(2,1)S(1)}, bf16[1024,128]{1,0:T(8,128)(2,1)S(1)}, bf16[35,512,256]{2,1,0:T(8,128)(2,1)S(1)}, f32[8,128]{1,0:T(8,128)}) custom-call(s32[1288]{0:T(1024)S(1)} %concatenate.28.hbm_ref, f32[257,128,128]{2,1,0:T(8,128)S(1)} %get-tuple-element.51.refs_0_, f32[16,128]{1,0:T(8,128)S(1)} %get-tuple-element.57.refs_1_, ...), custom_call_target="tpu_custom_call" | custom-call | tf_op jit(solution)/shard_map/plan/pallas_call | solution.py:616
  101.0 2.0 %collective-permute-start.29 = (bf16[1024,128]{1,0:T(8,128)(2,1)S(1)}, bf16[1024,128]{1,0:T(8,128)(2,1)S(1)}, u32[]{:S(2)}, u32[]{:S(2)}) collective-permute-start(bf16[1024,128]{1,0:T(8,128)(2,1)S(1)} %get-tuple-element.63), channel_id=1, source_target_pairs={{0,2},{1,3},{2,0},{3,1},{4,6},{5,7},{6,4},{7,5},{8,10},{9,11},{10,... | collective-permute-start | bytes 786440 | tf_op jit(solution)/shard_map/ppermute | solution.py:22
  103.1 3.3 %rest_of_plan.1 = (bf16[1024,128]{1,0:T(8,128)(2,1)S(1)}, bf16[1024,128]{1,0:T(8,128)(2,1)S(1)}, bf16[1024,128]{1,0:T(8,128)(2,1)S(1)}, bf16[1024,128]{1,0:T(8,1...) custom-call(s32[1288]{0:T(1024)S(1)} %concatenate.28.hbm_ref, ...), custom_call_target="tpu_custom_call" | custom-call | flops 3221225472 | bytes 16777216 | tf_op jit(solution)/shard_map/rest_of_plan/pallas_call | solution.py:630
  106.3 9.3 %collective-permute-done.28 = bf16[1024,128]{1,0:T(8,128)(2,1)S(1)} collective-permute-done((bf16[1024,128]{1,0:T(8,128)(2,1)S(1)}, bf16[1024,128]{1,0:T(8,128)(2,1)S(1)}, u32[]{:S(2)}, u32[]{:S(2)}) %collective-permute-start.28) | collective-permute-done | bytes 262176 | tf_op jit(solution)/shard_map/ppermute | solution.py:22
  115.6 5.6 %collective-permute-done.29 = bf16[1024,128]{1,0:T(8,128)(2,1)S(1)} collective-permute-done((bf16[1024,128]{1,0:T(8,128)(2,1)S(1)}, bf16[1024,128]{1,0:T(8,128)(2,1)S(1)}, u32[]{:S(2)}, u32[]{:S(2)}) %collective-permute-start.29) | collective-permute-done | bytes 262176 | tf_op jit(solution)/shard_map/ppermute | solution.py:22
  121.4 1.9 %collective-permute-start.30 = (bf16[1024,128]{1,0:T(8,128)(2,1)S(1)}, bf16[1024,128]{1,0:T(8,128)(2,1)S(1)}, u32[]{:S(2)}, u32[]{:S(2)}) collective-permute-start(bf16[1024,128]{1,0:T(8,128)(2,1)S(1)} %get-tuple-element.66), channel_id=1, source_target_pairs={{0,2},{1,3},{2,0},{3,1},{4,6},{5,7},{6,4},{7,5},{8,10},{9,11},{10,... | collective-permute-start | bytes 786440 | tf_op jit(solution)/shard_map/ppermute | solution.py:22
  123.6 2.9 %collective-permute-start.33 = (bf16[1024,128]{1,0:T(8,128)(2,1)S(1)}, bf16[1024,128]{1,0:T(8,128)(2,1)S(1)}, u32[]{:S(2)}, u32[]{:S(2)}) collective-permute-start(bf16[1024,128]{1,0:T(8,128)(2,1)S(1)} %add_convert_fusion.1), channel_id=1, source_target_pairs={{0,4},{1,5},{2,6},{3,7},{4,0},{5,1},{6,2},{7,3},{8,12},{9,13},{10,... | collective-permute-start | bytes 786440 | tf_op jit(solution)/shard_map/ppermute | solution.py:22
  126.5 4.1 %collective-permute-done.31 = bf16[1024,128]{1,0:T(8,128)(2,1)S(1)} collective-permute-done((bf16[1024,128]{1,0:T(8,128)(2,1)S(1)}, bf16[1024,128]{1,0:T(8,128)(2,1)S(1)}, u32[]{:S(2)}, u32[]{:S(2)}) %collective-permute-start.31) | collective-permute-done | bytes 262176 | tf_op jit(solution)/shard_map/ppermute | solution.py:22
  130.6 2.9 %collective-permute-done.30 = bf16[1024,128]{1,0:T(8,128)(2,1)S(1)} collective-permute-done((bf16[1024,128]{1,0:T(8,128)(2,1)S(1)}, bf16[1024,128]{1,0:T(8,128)(2,1)S(1)}, u32[]{:S(2)}, u32[]{:S(2)}) %collective-permute-start.30) | collective-permute-done | bytes 262176 | tf_op jit(solution)/shard_map/ppermute | solution.py:22
  133.6 2.7 %collective-permute-done.32 = bf16[1024,128]{1,0:T(8,128)(2,1)S(1)} collective-permute-done((bf16[1024,128]{1,0:T(8,128)(2,1)S(1)}, bf16[1024,128]{1,0:T(8,128)(2,1)S(1)}, u32[]{:S(2)}, u32[]{:S(2)}) %collective-permute-start.32) | collective-permute-done | bytes 262176 | tf_op jit(solution)/shard_map/ppermute | solution.py:22
  136.4 0.8 pad_maximum_fusion
  (73 shorter events, 9.4 us)
Async XLA Ops:
  0.6 17.3 %collective-permute-start.2 = (bf16[1024,256]{1,0:T(8,128)(2,1)}, bf16[1024,256]{1,0:T(8,128)(2,1)S(1)}, u32[]{:S(2)}, u32[]{:S(2)}) collective-permute-start(bf16[1024,256]{1,0:T(8,128)(2,1)} %refs_1_.1), channel_id=1, source_target_pairs={{0,16},{8,24},{16,0},{24,8},{1,17},{9,25},{17,1},{25,9},{2,18},{10... | collective-permute-start | bytes 1572872 | tf_op jit(solution)/shard_map/ppermute | solution.py:22
  3.7 14.2 %collective-permute-start.1 = (bf16[1024,256]{1,0:T(8,128)(2,1)}, bf16[1024,256]{1,0:T(8,128)(2,1)S(1)}, u32[]{:S(2)}, u32[]{:S(2)}) collective-permute-start(bf16[1024,256]{1,0:T(8,128)(2,1)} %refs_1_.1), channel_id=1, source_target_pairs={{0,8},{8,0},{16,24},{24,16},{1,9},{9,1},{17,25},{25,17},{2,10},{10... | collective-permute-start | bytes 1572872 | tf_op jit(solution)/shard_map/ppermute | solution.py:22
  5.2 7.2 %collective-permute-start.3 = (bf16[1024,256]{1,0:T(8,128)(2,1)}, bf16[1024,256]{1,0:T(8,128)(2,1)S(1)}, u32[]{:S(2)}, u32[]{:S(2)}) collective-permute-start(bf16[1024,256]{1,0:T(8,128)(2,1)} %refs_1_.1), channel_id=1, source_target_pairs={{0,1},{1,0},{2,3},{3,2},{4,5},{5,4},{6,7},{7,6},{8,9},{9,8},{10,11... | collective-permute-start | bytes 1572872 | tf_op jit(solution)/shard_map/ppermute | solution.py:22
  5.2 2.1 %collective-permute-start = (s32[16,8]{0,1:T(8,128)}, s32[16,8]{0,1:T(8,128)S(1)}, u32[]{:S(2)}, u32[]{:S(2)}) collective-permute-start(s32[16,8]{0,1:T(8,128)} %param.5), channel_id=1, source_target_pairs={{0,1},{1,0},{2,3},{3,2},{4,5},{5,4},{6,7},{7,6},{8,9},{9,8},{10,11... | collective-permute-start | bytes 1544 | tf_op jit(solution)/shard_map/ppermute | solution.py:22
  12.4 2.2 %copy-start = (bf16[2048,1024]{1,0:T(8,128)(2,1)S(1)}, bf16[2048,1024]{1,0:T(8,128)(2,1)}, u32[]{:S(2)}) copy-start(bf16[2048,1024]{1,0:T(8,128)(2,1)} %refs_0_.5) | copy-start | bytes 12582916
  14.6 1.0 copy-start.2
  15.6 5.3 %copy-start.1 = (bf16[2048,1024]{1,0:T(8,128)(2,1)S(1)}, bf16[2048,1024]{1,0:T(8,128)(2,1)}, u32[]{:S(2)}) copy-start(bf16[2048,1024]{1,0:T(8,128)(2,1)} %refs_0_.5) | copy-start | bytes 12582916
  17.9 3.0 %collective-permute-start.7 = (bf16[1024,256]{1,0:T(8,128)(2,1)S(1)}, bf16[1024,256]{1,0:T(8,128)(2,1)S(1)}, u32[]{:S(2)}, u32[]{:S(2)}) collective-permute-start(bf16[1024,256]{1,0:T(8,128)(2,1)S(1)} %collective-permute-done.2.refs_2_), channel_id=1, source_target_pairs={{0,1},{1,0},{2,3},{3,2},{4,5},{5,4},{6,7},{7,6},{8,9},{9,8},{10,11... | collective-permute-start | bytes 1572872 | tf_op jit(solution)/shard_map/ppermute | solution.py:22
  18.1 2.7 %collective-permute-start.6 = (bf16[1024,256]{1,0:T(8,128)(2,1)S(1)}, bf16[1024,256]{1,0:T(8,128)(2,1)S(1)}, u32[]{:S(2)}, u32[]{:S(2)}) collective-permute-start(bf16[1024,256]{1,0:T(8,128)(2,1)S(1)} %collective-permute-done.1.refs_1_), channel_id=1, source_target_pairs={{0,1},{1,0},{2,3},{3,2},{4,5},{5,4},{6,7},{7,6},{8,9},{9,8},{10,11... | collective-permute-start | bytes 1572872 | tf_op jit(solution)/shard_map/ppermute | solution.py:22
  18.5 8.4 %collective-permute-start.5 = (bf16[512,256]{1,0:T(8,128)(2,1)S(1)}, bf16[512,256]{1,0:T(8,128)(2,1)S(1)}, u32[]{:S(2)}, u32[]{:S(2)}) collective-permute-start(bf16[512,256]{1,0:T(8,128)(2,1)S(1)} %slice.7), channel_id=1, source_target_pairs={{0,16},{8,24},{16,0},{24,8},{1,17},{9,25},{17,1},{25,9},{2,18},{10... | collective-permute-start | bytes 786440 | tf_op jit(solution)/shard_map/ppermute | solution.py:22
  19.1 8.1 %collective-permute-start.4 = (bf16[512,256]{1,0:T(8,128)(2,1)S(1)}, bf16[512,256]{1,0:T(8,128)(2,1)S(1)}, u32[]{:S(2)}, u32[]{:S(2)}) collective-permute-start(bf16[512,256]{1,0:T(8,128)(2,1)S(1)} %slice.6), channel_id=1, source_target_pairs={{0,8},{8,0},{16,24},{24,16},{1,9},{9,1},{17,25},{25,17},{2,10},{10... | collective-permute-start | bytes 786440 | tf_op jit(solution)/shard_map/ppermute | solution.py:22
  27.2 1.5 %collective-permute-start.8 = (bf16[512,256]{1,0:T(8,128)(2,1)S(1)}, bf16[512,256]{1,0:T(8,128)(2,1)S(1)}, u32[]{:S(2)}, u32[]{:S(2)}) collective-permute-start(bf16[512,256]{1,0:T(8,128)(2,1)S(1)} %collective-permute-done.4.refs_1_), channel_id=1, source_target_pairs={{0,1},{1,0},{2,3},{3,2},{4,5},{5,4},{6,7},{7,6},{8,9},{9,8},{10,11... | collective-permute-start | bytes 786440 | tf_op jit(solution)/shard_map/ppermute | solution.py:22
  27.2 1.9 %collective-permute-start.9 = (bf16[512,256]{1,0:T(8,128)(2,1)S(1)}, bf16[512,256]{1,0:T(8,128)(2,1)S(1)}, u32[]{:S(2)}, u32[]{:S(2)}) collective-permute-start(bf16[512,256]{1,0:T(8,128)(2,1)S(1)} %collective-permute-done.5.refs_2_), channel_id=1, source_target_pairs={{0,1},{1,0},{2,3},{3,2},{4,5},{5,4},{6,7},{7,6},{8,9},{9,8},{10,11... | collective-permute-start | bytes 786440 | tf_op jit(solution)/shard_map/ppermute | solution.py:22
  33.3 5.8 %collective-permute-start.12 = (f32[16,128]{1,0:T(8,128)S(1)}, f32[16,128]{1,0:T(8,128)S(1)}, u32[]{:S(2)}, u32[]{:S(2)}) collective-permute-start(f32[16,128]{1,0:T(8,128)S(1)} %get-tuple-element.54.refs_3_), channel_id=1, source_target_pairs={{0,6},{1,7},{2,4},{3,5},{4,2},{5,3},{6,0},{7,1},{8,14},{9,15},{10,... | collective-permute-start | bytes 24584 | tf_op jit(solution)/shard_map/ppermute | solution.py:22
  37.6 4.5 %collective-permute-start.11 = (f32[16,128]{1,0:T(8,128)S(1)}, f32[16,128]{1,0:T(8,128)S(1)}, u32[]{:S(2)}, u32[]{:S(2)}) collective-permute-start(f32[16,128]{1,0:T(8,128)S(1)} %get-tuple-element.54.refs_3_), channel_id=1, source_target_pairs={{0,4},{1,5},{2,6},{3,7},{4,0},{5,1},{6,2},{7,3},{8,12},{9,13},{10,... | collective-permute-start | bytes 24584 | tf_op jit(solution)/shard_map/ppermute | solution.py:22
  37.6 4.5 %collective-permute-start.10 = (f32[16,128]{1,0:T(8,128)S(1)}, f32[16,128]{1,0:T(8,128)S(1)}, u32[]{:S(2)}, u32[]{:S(2)}) collective-permute-start(f32[16,128]{1,0:T(8,128)S(1)} %get-tuple-element.54.refs_3_), channel_id=1, source_target_pairs={{0,2},{1,3},{2,0},{3,1},{4,6},{5,7},{6,4},{7,5},{8,10},{9,11},{10,... | collective-permute-start | bytes 24584 | tf_op jit(solution)/shard_map/ppermute | solution.py:22
  44.3 5.5 %collective-permute-start.15 = (f32[16,128]{1,0:T(8,128)S(1)}, f32[16,128]{1,0:T(8,128)S(1)}, u32[]{:S(2)}, u32[]{:S(2)}) collective-permute-start(f32[16,128]{1,0:T(8,128)S(1)} %get-tuple-element.55.refs_3_), channel_id=1, source_target_pairs={{0,24},{8,16},{16,8},{24,0},{1,25},{9,17},{17,9},{25,1},{2,26},{10... | collective-permute-start | bytes 24584 | tf_op jit(solution)/shard_map/ppermute | solution.py:22
  48.1 3.7 %collective-permute-start.14 = (f32[16,128]{1,0:T(8,128)S(1)}, f32[16,128]{1,0:T(8,128)S(1)}, u32[]{:S(2)}, u32[]{:S(2)}) collective-permute-start(f32[16,128]{1,0:T(8,128)S(1)} %get-tuple-element.55.refs_3_), channel_id=1, source_target_pairs={{0,16},{8,24},{16,0},{24,8},{1,17},{9,25},{17,1},{25,9},{2,18},{10... | collective-permute-start | bytes 24584 | tf_op jit(solution)/shard_map/ppermute | solution.py:22
  48.1 3.7 %collective-permute-start.13 = (f32[16,128]{1,0:T(8,128)S(1)}, f32[16,128]{1,0:T(8,128)S(1)}, u32[]{:S(2)}, u32[]{:S(2)}) collective-permute-start(f32[16,128]{1,0:T(8,128)S(1)} %get-tuple-element.55.refs_3_), channel_id=1, source_target_pairs={{0,8},{8,0},{16,24},{24,16},{1,9},{9,1},{17,25},{25,17},{2,10},{10... | collective-permute-start | bytes 24584 | tf_op jit(solution)/shard_map/ppermute | solution.py:22
  53.7 7.8 %collective-permute-start.18 = (f32[16,128]{1,0:T(8,128)S(1)}, f32[16,128]{1,0:T(8,128)S(1)}, u32[]{:S(2)}, u32[]{:S(2)}) collective-permute-start(f32[16,128]{1,0:T(8,128)S(1)} %row_pass.2.refs_3_), channel_id=1, source_target_pairs={{0,6},{1,7},{2,4},{3,5},{4,2},{5,3},{6,0},{7,1},{8,14},{9,15},{10,... | collective-permute-start | bytes 24584 | tf_op jit(solution)/shard_map/ppermute | solution.py:22
  59.9 4.5 %collective-permute-start.17 = (f32[16,128]{1,0:T(8,128)S(1)}, f32[16,128]{1,0:T(8,128)S(1)}, u32[]{:S(2)}, u32[]{:S(2)}) collective-permute-start(f32[16,128]{1,0:T(8,128)S(1)} %row_pass.2.refs_3_), channel_id=1, source_target_pairs={{0,4},{1,5},{2,6},{3,7},{4,0},{5,1},{6,2},{7,3},{8,12},{9,13},{10,... | collective-permute-start | bytes 24584 | tf_op jit(solution)/shard_map/ppermute | solution.py:22
  59.9 4.5 %collective-permute-start.16 = (f32[16,128]{1,0:T(8,128)S(1)}, f32[16,128]{1,0:T(8,128)S(1)}, u32[]{:S(2)}, u32[]{:S(2)}) collective-permute-start(f32[16,128]{1,0:T(8,128)S(1)} %row_pass.2.refs_3_), channel_id=1, source_target_pairs={{0,2},{1,3},{2,0},{3,1},{4,6},{5,7},{6,4},{7,5},{8,10},{9,11},{10,... | collective-permute-start | bytes 24584 | tf_op jit(solution)/shard_map/ppermute | solution.py:22
  66.6 5.7 %collective-permute-start.21 = (f32[16,128]{1,0:T(8,128)S(1)}, f32[16,128]{1,0:T(8,128)S(1)}, u32[]{:S(2)}, u32[]{:S(2)}) collective-permute-start(f32[16,128]{1,0:T(8,128)S(1)} %get-tuple-element.56.refs_3_), channel_id=1, source_target_pairs={{0,24},{8,16},{16,8},{24,0},{1,25},{9,17},{17,9},{25,1},{2,26},{10... | collective-permute-start | bytes 24584 | tf_op jit(solution)/shard_map/ppermute | solution.py:22
  70.6 3.7 %collective-permute-start.20 = (f32[16,128]{1,0:T(8,128)S(1)}, f32[16,128]{1,0:T(8,128)S(1)}, u32[]{:S(2)}, u32[]{:S(2)}) collective-permute-start(f32[16,128]{1,0:T(8,128)S(1)} %get-tuple-element.56.refs_3_), channel_id=1, source_target_pairs={{0,16},{8,24},{16,0},{24,8},{1,17},{9,25},{17,1},{25,9},{2,18},{10... | collective-permute-start | bytes 24584 | tf_op jit(solution)/shard_map/ppermute | solution.py:22
  70.6 3.7 %collective-permute-start.19 = (f32[16,128]{1,0:T(8,128)S(1)}, f32[16,128]{1,0:T(8,128)S(1)}, u32[]{:S(2)}, u32[]{:S(2)}) collective-permute-start(f32[16,128]{1,0:T(8,128)S(1)} %get-tuple-element.56.refs_3_), channel_id=1, source_target_pairs={{0,8},{8,0},{16,24},{24,16},{1,9},{9,1},{17,25},{25,17},{2,10},{10... | collective-permute-start | bytes 24584 | tf_op jit(solution)/shard_map/ppermute | solution.py:22
  76.0 7.8 %collective-permute-start.24 = (f32[16,128]{1,0:T(8,128)S(1)}, f32[16,128]{1,0:T(8,128)S(1)}, u32[]{:S(2)}, u32[]{:S(2)}) collective-permute-start(f32[16,128]{1,0:T(8,128)S(1)} %row_pass.3.refs_3_), channel_id=1, source_target_pairs={{0,6},{1,7},{2,4},{3,5},{4,2},{5,3},{6,0},{7,1},{8,14},{9,15},{10,... | collective-permute-start | bytes 24584 | tf_op jit(solution)/shard_map/ppermute | solution.py:22
  82.1 4.5 %collective-permute-start.23 = (f32[16,128]{1,0:T(8,128)S(1)}, f32[16,128]{1,0:T(8,128)S(1)}, u32[]{:S(2)}, u32[]{:S(2)}) collective-permute-start(f32[16,128]{1,0:T(8,128)S(1)} %row_pass.3.refs_3_), channel_id=1, source_target_pairs={{0,4},{1,5},{2,6},{3,7},{4,0},{5,1},{6,2},{7,3},{8,12},{9,13},{10,... | collective-permute-start | bytes 24584 | tf_op jit(solution)/shard_map/ppermute | solution.py:22
  82.1 4.5 %collective-permute-start.22 = (f32[16,128]{1,0:T(8,128)S(1)}, f32[16,128]{1,0:T(8,128)S(1)}, u32[]{:S(2)}, u32[]{:S(2)}) collective-permute-start(f32[16,128]{1,0:T(8,128)S(1)} %row_pass.3.refs_3_), channel_id=1, source_target_pairs={{0,2},{1,3},{2,0},{3,1},{4,6},{5,7},{6,4},{7,5},{8,10},{9,11},{10,... | collective-permute-start | bytes 24584 | tf_op jit(solution)/shard_map/ppermute | solution.py:22
  89.1 6.8 %collective-permute-start.27 = (f32[16,128]{1,0:T(8,128)S(1)}, f32[16,128]{1,0:T(8,128)S(1)}, u32[]{:S(2)}, u32[]{:S(2)}) collective-permute-start(f32[16,128]{1,0:T(8,128)S(1)} %get-tuple-element.59.refs_3_), channel_id=1, source_target_pairs={{0,24},{8,16},{16,8},{24,0},{1,25},{9,17},{17,9},{25,1},{2,26},{10... | collective-permute-start | bytes 24584 | tf_op jit(solution)/shard_map/ppermute | solution.py:22
  94.2 3.7 %collective-permute-start.26 = (f32[16,128]{1,0:T(8,128)S(1)}, f32[16,128]{1,0:T(8,128)S(1)}, u32[]{:S(2)}, u32[]{:S(2)}) collective-permute-start(f32[16,128]{1,0:T(8,128)S(1)} %get-tuple-element.59.refs_3_), channel_id=1, source_target_pairs={{0,16},{8,24},{16,0},{24,8},{1,17},{9,25},{17,1},{25,9},{2,18},{10... | collective-permute-start | bytes 24584 | tf_op jit(solution)/shard_map/ppermute | solution.py:22
  94.2 3.7 %collective-permute-start.25 = (f32[16,128]{1,0:T(8,128)S(1)}, f32[16,128]{1,0:T(8,128)S(1)}, u32[]{:S(2)}, u32[]{:S(2)}) collective-permute-start(f32[16,128]{1,0:T(8,128)S(1)} %get-tuple-element.59.refs_3_), channel_id=1, source_target_pairs={{0,8},{8,0},{16,24},{24,16},{1,9},{9,1},{17,25},{25,17},{2,10},{10... | collective-permute-start | bytes 24584 | tf_op jit(solution)/shard_map/ppermute | solution.py:22
  101.0 14.7 %collective-permute-start.28 = (bf16[1024,128]{1,0:T(8,128)(2,1)S(1)}, bf16[1024,128]{1,0:T(8,128)(2,1)S(1)}, u32[]{:S(2)}, u32[]{:S(2)}) collective-permute-start(bf16[1024,128]{1,0:T(8,128)(2,1)S(1)} %get-tuple-element.62), channel_id=1, source_target_pairs={{0,2},{1,3},{2,0},{3,1},{4,6},{5,7},{6,4},{7,5},{8,10},{9,11},{10,... | collective-permute-start | bytes 786440 | tf_op jit(solution)/shard_map/ppermute | solution.py:22
  101.0 20.2 %collective-permute-start.29 = (bf16[1024,128]{1,0:T(8,128)(2,1)S(1)}, bf16[1024,128]{1,0:T(8,128)(2,1)S(1)}, u32[]{:S(2)}, u32[]{:S(2)}) collective-permute-start(bf16[1024,128]{1,0:T(8,128)(2,1)S(1)} %get-tuple-element.63), channel_id=1, source_target_pairs={{0,2},{1,3},{2,0},{3,1},{4,6},{5,7},{6,4},{7,5},{8,10},{9,11},{10,... | collective-permute-start | bytes 786440 | tf_op jit(solution)/shard_map/ppermute | solution.py:22
  121.3 9.2 %collective-permute-start.31 = (bf16[1024,128]{1,0:T(8,128)(2,1)S(1)}, bf16[1024,128]{1,0:T(8,128)(2,1)S(1)}, u32[]{:S(2)}, u32[]{:S(2)}) collective-permute-start(bf16[1024,128]{1,0:T(8,128)(2,1)S(1)} %add_convert_fusion.3), channel_id=1, source_target_pairs={{0,4},{1,5},{2,6},{3,7},{4,0},{5,1},{6,2},{7,3},{8,12},{9,13},{10,... | collective-permute-start | bytes 786440 | tf_op jit(solution)/shard_map/ppermute | solution.py:22
  121.4 12.1 %collective-permute-start.30 = (bf16[1024,128]{1,0:T(8,128)(2,1)S(1)}, bf16[1024,128]{1,0:T(8,128)(2,1)S(1)}, u32[]{:S(2)}, u32[]{:S(2)}) collective-permute-start(bf16[1024,128]{1,0:T(8,128)(2,1)S(1)} %get-tuple-element.66), channel_id=1, source_target_pairs={{0,2},{1,3},{2,0},{3,1},{4,6},{5,7},{6,4},{7,5},{8,10},{9,11},{10,... | collective-permute-start | bytes 786440 | tf_op jit(solution)/shard_map/ppermute | solution.py:22
  123.3 13.0 %collective-permute-start.32 = (bf16[1024,128]{1,0:T(8,128)(2,1)S(1)}, bf16[1024,128]{1,0:T(8,128)(2,1)S(1)}, u32[]{:S(2)}, u32[]{:S(2)}) collective-permute-start(bf16[1024,128]{1,0:T(8,128)(2,1)S(1)} %get-tuple-element.70), channel_id=1, source_target_pairs={{0,2},{1,3},{2,0},{3,1},{4,6},{5,7},{6,4},{7,5},{8,10},{9,11},{10,... | collective-permute-start | bytes 786440 | tf_op jit(solution)/shard_map/ppermute | solution.py:22
  123.6 12.7 %collective-permute-start.33 = (bf16[1024,128]{1,0:T(8,128)(2,1)S(1)}, bf16[1024,128]{1,0:T(8,128)(2,1)S(1)}, u32[]{:S(2)}, u32[]{:S(2)}) collective-permute-start(bf16[1024,128]{1,0:T(8,128)(2,1)S(1)} %add_convert_fusion.1), channel_id=1, source_target_pairs={{0,4},{1,5},{2,6},{3,7},{4,0},{5,1},{6,2},{7,3},{8,12},{9,13},{10,... | collective-permute-start | bytes 786440 | tf_op jit(solution)/shard_map/ppermute | solution.py:22

commit v18 on v14

--- a/solution.py
+++ b/solution.py
@@ -530,14 +530,10 @@
 
 
 def scatter_partials(blocks):
-    blocks = list(blocks)
-    distance = 1
-    while distance < len(blocks):
-        for j in range(len(blocks) - distance, 0, -2 * distance):
-            got = swap(blocks[j].astype(jnp.bfloat16), "proto", 2 * distance).astype(jnp.float32)
-            blocks[j ^ distance] = blocks[j ^ distance].astype(jnp.float32) + got
-        distance *= 2
-    return blocks[0].astype(jnp.bfloat16)
+    total = blocks[0].astype(jnp.float32)
+    for j in range(len(blocks) - 1, 0, -1):
+        total = total + swap(blocks[j].astype(jnp.bfloat16), "proto", 2 * j).astype(jnp.float32)
+    return total.astype(jnp.bfloat16)
 
 
 def shards(embeddings, prototypes, block_mask):

time: 135 us -> 145 us (1.074)
  the two profiles are of different devices: /device:TPU:0 before, /device:TPU:12 now
where the time goes in v18:
time: 145 us
  waiting for transfers between devices  57.2 us (39%)
  starting transfers between devices  45.6 us (31%)
  Pallas kernels  31 us (21%)
  local copies, waits for them, and re-layouts  4.41 us (3%)
  other arithmetic  4.33 us (3%)
  between operations  2.19 us (2%)
    ppermute x31, waiting for transfers between devices, swap(): return lax.ppermute(x, axis, [(i, i ^ offset) for i in range(size)])  57.2 us
    ppermute x31, starting transfers between devices, swap(): return lax.ppermute(x, axis, [(i, i ^ offset) for i in range(size)])  45.6 us
    pallas_call x2, Pallas kernels, early(): pl.pallas_call(with_table(early_panel_kernel, table, places, owners, bool...  7.17 us
    pallas_call x3, Pallas kernels, shards(): pl.pallas_call(with_table(column_kernel, table), out_shape=(column_shape,...  7.08 us
    pallas_call x1, Pallas kernels, late(): pl.pallas_call(with_table(panel_kernel, table, places, add), out_shape=(p...  5.2 us
    pallas_call x1, Pallas kernels, shards(): pl.pallas_call(with_table(rest_kernel, table, lines), out_shape=[block] *...  4.03 us
    pallas_call x2, Pallas kernels, shards(): pl.pallas_call(with_table(row_kernel, table, log_column), out_shape=row_s...  3.88 us
    pallas_call x1, Pallas kernels, shards(): pl.pallas_call(with_table(plan_kernel, table, log_column, lines), out_sha...  3.69 us
  transfers between devices with their start and end apart: 31, of which 20 were waited for; matrix products, arithmetic and copies ran while one was open for 3% of the time, Pallas kernels for 5%

profile of v18, /device:TPU:12, one launch (start us, length us, event | category | flops | bytes accessed | tf_op | source)
XLA Modules:
  0.0 144.8 jit_solution(8279374929477467183)
XLA Ops:
  1.2 1.5 %collective-permute-start.1 = (bf16[1024,256]{1,0:T(8,128)(2,1)}, bf16[1024,256]{1,0:T(8,128)(2,1)S(1)}, u32[]{:S(2)}, u32[]{:S(2)}) collective-permute-start(bf16[1024,256]{1,0:T(8,128)(2,1)} %refs_1_.1), channel_id=1, source_target_pairs={{0,8},{8,0},{16,24},{24,16},{1,9},{9,1},{17,25},{25,17},{2,10},{10... | collective-permute-start | bytes 1572872 | tf_op jit(solution)/shard_map/ppermute | solution.py:21
  3.2 0.7 compare_select_fusion.1
  3.9 0.9 collective-permute-done
  5.1 0.6 fusion.4
  9.2 0.7 concatenate.25.hbm_ref
  9.9 2.2 %copy-done = bf16[2048,1024]{1,0:T(8,128)(2,1)S(1)} copy-done((bf16[2048,1024]{1,0:T(8,128)(2,1)S(1)}, bf16[2048,1024]{1,0:T(8,128)(2,1)}, u32[]{:S(2)}) %copy-start) | copy-done | bytes 4194328
  12.1 1.0 copy-done.2
  13.1 2.8 %early_panel.2 = (f32[257,128,128]{2,1,0:T(8,128)S(1)}, bf16[2048,1024]{1,0:T(8,128)(2,1)S(1)}) custom-call(s32[1288]{0:T(1024)S(1)} %concatenate.25.hbm_ref, bf16[2048,1024]{1,0:T(8,128)(2,1)S(1)} %copy-done, bf16[1024,256]{1,0:T(8,128)(2,1)S(1)} %copy-done.2, bf16[1024,256]{1,0:T(8,128)(2,1)S(1)} %collective-permute-done.3.refs_2_), custom_call_target="tpu_custom_call" | custom-call | flops 1073741824 | bytes 33554432 | tf_op jit(solution)/shard_map/early_panel/pallas_call | solution.py:501
  16.6 1.0 collective-permute-start.5
  17.7 1.1 collective-permute-start.4
  18.8 4.3 %early_panel.3 = (f32[257,128,128]{2,1,0:T(8,128)S(1)}, bf16[2048,1024]{1,0:T(8,128)(2,1)S(1)}) custom-call(s32[1288]{0:T(1024)S(1)} %concatenate.25.hbm_ref, bf16[2048,1024]{1,0:T(8,128)(2,1)S(1)} %copy-done.1, bf16[1024,256]{1,0:T(8,128)(2,1)S(1)} %collective-permute-done.1.refs_1_, ...), custom_call_target="tpu_custom_call", output_to_operand_aliasing={{0}: (6, {}), {1}: (7, {})} | custom-call | flops 2147483648 | bytes 33554432 | tf_op jit(solution)/shard_map/early_panel/pallas_call | solution.py:501
  23.1 1.9 %collective-permute-done.5.refs_2_ = bf16[512,256]{1,0:T(8,128)(2,1)S(1)} collective-permute-done((bf16[512,256]{1,0:T(8,128)(2,1)S(1)}, bf16[512,256]{1,0:T(8,128)(2,1)S(1)}, u32[]{:S(2)}, u32[]{:S(2)}) %collective-permute-start.5) | collective-permute-done | bytes 262176 | tf_op jit(solution)/shard_map/ppermute | solution.py:21
  25.0 0.7 collective-permute-done.4.refs_1_
  26.2 1.0 collective-permute-done.8.refs_3_
  27.6 5.2 %panel.1 = (f32[257,128,128]{2,1,0:T(8,128)S(1)}, bf16[2048,1024]{1,0:T(8,128)(2,1)S(1)}, bf16[257,128,128]{2,1,0:T(8,128)(2,1)S(1)}, f32[16,128]{1,0:T(8,128)S(1)}, f32[16,128]{1,0:T(8,128)S(1)}) custom-call(s32[1288]{0:T(1024)S(1)} %concatenate.25.hbm_ref, bf16[2048,1024]{1,0:T(8,128)(2,1)S(1)} %copy-done.1, ...), custom_call_target="tpu_custom_call", output_to_operand_aliasing={{0}: (6, {}), {1}: (7, {})} | custom-call | tf_op jit(solution)/shard_map/panel/pallas_call | solution.py:480
  32.8 2.6 %collective-permute-start.12 = (f32[16,128]{1,0:T(8,128)S(1)}, f32[16,128]{1,0:T(8,128)S(1)}, u32[]{:S(2)}, u32[]{:S(2)}) collective-permute-start(f32[16,128]{1,0:T(8,128)S(1)} %get-tuple-element.46.refs_3_), channel_id=1, source_target_pairs={{0,6},{1,7},{2,4},{3,5},{4,2},{5,3},{6,0},{7,1},{8,14},{9,15},{10,... | collective-permute-start | bytes 24584 | tf_op jit(solution)/shard_map/ppermute | solution.py:21
  35.4 1.2 collective-permute-start.11
  36.7 0.8 collective-permute-start.10
  37.5 2.5 %collective-permute-done.11.refs_5_ = f32[16,128]{1,0:T(8,128)S(1)} collective-permute-done((f32[16,128]{1,0:T(8,128)S(1)}, f32[16,128]{1,0:T(8,128)S(1)}, u32[]{:S(2)}, u32[]{:S(2)}) %collective-permute-start.11) | collective-permute-done | bytes 8224 | tf_op jit(solution)/shard_map/ppermute | solution.py:21
  40.3 2.3 %column_pass.3 = (f32[16,128]{1,0:T(8,128)S(1)}, f32[16,128]{1,0:T(8,128)}, f32[16,128]{1,0:T(8,128)}) custom-call(s32[1288]{0:T(1024)S(1)} %concatenate.25.hbm_ref, f32[257,128,128]{2,1,0:T(8,128)S(1)} %get-tuple-element.43.refs_0_, bf16[257,128,128]{2,1,0:T(8,128)(2,1)S(1)} %get-tuple-element.44.refs_1_, f32[16,128]{1,0:T(8,128)S(1)} %get-tuple-element.45.refs_2_, ...), custom_call_target="tpu_custom_call" | custom-call | tf_op jit(solution)/shard_map/column_pass/pallas_call | solution.py:586
  42.7 2.5 %collective-permute-start.14 = (f32[16,128]{1,0:T(8,128)S(1)}, f32[16,128]{1,0:T(8,128)S(1)}, u32[]{:S(2)}, u32[]{:S(2)}) collective-permute-start(f32[16,128]{1,0:T(8,128)S(1)} %get-tuple-element.47.refs_3_), channel_id=1, source_target_pairs={{0,16},{8,24},{16,0},{24,8},{1,17},{9,25},{17,1},{25,9},{2,18},{10... | collective-permute-start | bytes 24584 | tf_op jit(solution)/shard_map/ppermute | solution.py:21
  45.3 0.9 collective-permute-start.13
  46.2 1.1 collective-permute-done.15.refs_6_
  47.2 1.7 %collective-permute-done.13.refs_4_ = f32[16,128]{1,0:T(8,128)S(1)} collective-permute-done((f32[16,128]{1,0:T(8,128)S(1)}, f32[16,128]{1,0:T(8,128)S(1)}, u32[]{:S(2)}, u32[]{:S(2)}) %collective-permute-start.13) | collective-permute-done | bytes 8224 | tf_op jit(solution)/shard_map/ppermute | solution.py:21
  48.9 2.0 %row_pass.2.refs_3_ = f32[16,128]{1,0:T(8,128)S(1)} custom-call(s32[1288]{0:T(1024)S(1)} %concatenate.25.hbm_ref, f32[257,128,128]{2,1,0:T(8,128)S(1)} %get-tuple-element.43.refs_0_, bf16[257,128,128]{2,1,0:T(8,128)(2,1)S(1)} %get-tuple-element.44.refs_1_, f32[16,128]{1,0:T(8,128)S(1)} %get-tuple-element.45.refs_2_, ...), custom_call_target="tpu_custom_call" | custom-call | tf_op jit(solution)/shard_map/row_pass/pallas_call | solution.py:576
  50.9 9.6 %collective-permute-start.18 = (f32[16,128]{1,0:T(8,128)S(1)}, f32[16,128]{1,0:T(8,128)S(1)}, u32[]{:S(2)}, u32[]{:S(2)}) collective-permute-start(f32[16,128]{1,0:T(8,128)S(1)} %row_pass.2.refs_3_), channel_id=1, source_target_pairs={{0,6},{1,7},{2,4},{3,5},{4,2},{5,3},{6,0},{7,1},{8,14},{9,15},{10,... | collective-permute-start | bytes 24584 | tf_op jit(solution)/shard_map/ppermute | solution.py:21
  60.6 1.5 %collective-permute-start.16 = (f32[16,128]{1,0:T(8,128)S(1)}, f32[16,128]{1,0:T(8,128)S(1)}, u32[]{:S(2)}, u32[]{:S(2)}) collective-permute-start(f32[16,128]{1,0:T(8,128)S(1)} %row_pass.2.refs_3_), channel_id=1, source_target_pairs={{0,2},{1,3},{2,0},{3,1},{4,6},{5,7},{6,4},{7,5},{8,10},{9,11},{10,... | collective-permute-start | bytes 24584 | tf_op jit(solution)/shard_map/ppermute | solution.py:21
  62.2 2.9 %collective-permute-done.17.refs_5_ = f32[16,128]{1,0:T(8,128)S(1)} collective-permute-done((f32[16,128]{1,0:T(8,128)S(1)}, f32[16,128]{1,0:T(8,128)S(1)}, u32[]{:S(2)}, u32[]{:S(2)}) %collective-permute-start.17) | collective-permute-done | bytes 8224 | tf_op jit(solution)/shard_map/ppermute | solution.py:21
  65.1 2.3 %column_pass.4 = (f32[16,128]{1,0:T(8,128)S(1)}, f32[16,128]{1,0:T(8,128)}, f32[16,128]{1,0:T(8,128)}) custom-call(s32[1288]{0:T(1024)S(1)} %concatenate.25.hbm_ref, f32[257,128,128]{2,1,0:T(8,128)S(1)} %get-tuple-element.43.refs_0_, bf16[257,128,128]{2,1,0:T(8,128)(2,1)S(1)} %get-tuple-element.44.refs_1_, f32[16,128]{1,0:T(8,128)S(1)} %get-tuple-element.45.refs_2_, ...), custom_call_target="tpu_custom_call" | custom-call | tf_op jit(solution)/shard_map/column_pass/pallas_call | solution.py:586
  67.5 2.4 %collective-permute-start.20 = (f32[16,128]{1,0:T(8,128)S(1)}, f32[16,128]{1,0:T(8,128)S(1)}, u32[]{:S(2)}, u32[]{:S(2)}) collective-permute-start(f32[16,128]{1,0:T(8,128)S(1)} %get-tuple-element.48.refs_3_), channel_id=1, source_target_pairs={{0,16},{8,24},{16,0},{24,8},{1,17},{9,25},{17,1},{25,9},{2,18},{10... | collective-permute-start | bytes 24584 | tf_op jit(solution)/shard_map/ppermute | solution.py:21
  69.9 1.1 collective-permute-start.19
  71.0 1.1 collective-permute-done.21.refs_6_
  72.0 1.5 %collective-permute-done.19.refs_4_ = f32[16,128]{1,0:T(8,128)S(1)} collective-permute-done((f32[16,128]{1,0:T(8,128)S(1)}, f32[16,128]{1,0:T(8,128)S(1)}, u32[]{:S(2)}, u32[]{:S(2)}) %collective-permute-start.19) | collective-permute-done | bytes 8224 | tf_op jit(solution)/shard_map/ppermute | solution.py:21
  73.5 1.9 %row_pass.3.refs_3_ = f32[16,128]{1,0:T(8,128)S(1)} custom-call(s32[1288]{0:T(1024)S(1)} %concatenate.25.hbm_ref, f32[257,128,128]{2,1,0:T(8,128)S(1)} %get-tuple-element.43.refs_0_, bf16[257,128,128]{2,1,0:T(8,128)(2,1)S(1)} %get-tuple-element.44.refs_1_, f32[16,128]{1,0:T(8,128)S(1)} %get-tuple-element.45.refs_2_, ...), custom_call_target="tpu_custom_call" | custom-call | tf_op jit(solution)/shard_map/row_pass/pallas_call | solution.py:576
  75.4 7.4 %collective-permute-start.24 = (f32[16,128]{1,0:T(8,128)S(1)}, f32[16,128]{1,0:T(8,128)S(1)}, u32[]{:S(2)}, u32[]{:S(2)}) collective-permute-start(f32[16,128]{1,0:T(8,128)S(1)} %row_pass.3.refs_3_), channel_id=1, source_target_pairs={{0,6},{1,7},{2,4},{3,5},{4,2},{5,3},{6,0},{7,1},{8,14},{9,15},{10,... | collective-permute-start | bytes 24584 | tf_op jit(solution)/shard_map/ppermute | solution.py:21
  82.8 1.5 %collective-permute-start.22 = (f32[16,128]{1,0:T(8,128)S(1)}, f32[16,128]{1,0:T(8,128)S(1)}, u32[]{:S(2)}, u32[]{:S(2)}) collective-permute-start(f32[16,128]{1,0:T(8,128)S(1)} %row_pass.3.refs_3_), channel_id=1, source_target_pairs={{0,2},{1,3},{2,0},{3,1},{4,6},{5,7},{6,4},{7,5},{8,10},{9,11},{10,... | collective-permute-start | bytes 24584 | tf_op jit(solution)/shard_map/ppermute | solution.py:21
  84.4 2.9 %collective-permute-done.23.refs_5_ = f32[16,128]{1,0:T(8,128)S(1)} collective-permute-done((f32[16,128]{1,0:T(8,128)S(1)}, f32[16,128]{1,0:T(8,128)S(1)}, u32[]{:S(2)}, u32[]{:S(2)}) %collective-permute-start.23) | collective-permute-done | bytes 8224 | tf_op jit(solution)/shard_map/ppermute | solution.py:21
  87.3 2.5 %column_pass.5 = (f32[16,128]{1,0:T(8,128)S(1)}, f32[16,128]{1,0:T(8,128)S(1)}, f32[16,128]{1,0:T(8,128)}) custom-call(s32[1288]{0:T(1024)S(1)} %concatenate.25.hbm_ref, f32[257,128,128]{2,1,0:T(8,128)S(1)} %get-tuple-element.43.refs_0_, bf16[257,128,128]{2,1,0:T(8,128)(2,1)S(1)} %get-tuple-element.44.refs_1_, f32[16,128]{1,0:T(8,128)S(1)} %get-tuple-element.45.refs_2_, ...), custom_call_target="tpu_custom_call" | custom-call | tf_op jit(solution)/shard_map/column_pass/pallas_call | solution.py:586
  89.9 3.1 %collective-permute-start.26 = (f32[16,128]{1,0:T(8,128)S(1)}, f32[16,128]{1,0:T(8,128)S(1)}, u32[]{:S(2)}, u32[]{:S(2)}) collective-permute-start(f32[16,128]{1,0:T(8,128)S(1)} %get-tuple-element.51.refs_3_), channel_id=1, source_target_pairs={{0,16},{8,24},{16,0},{24,8},{1,17},{9,25},{17,1},{25,9},{2,18},{10... | collective-permute-start | bytes 24584 | tf_op jit(solution)/shard_map/ppermute | solution.py:21
  93.4 1.1 collective-permute-done.27.refs_6_
  94.7 2.0 %collective-permute-done.25.refs_4_ = f32[16,128]{1,0:T(8,128)S(1)} collective-permute-done((f32[16,128]{1,0:T(8,128)S(1)}, f32[16,128]{1,0:T(8,128)S(1)}, u32[]{:S(2)}, u32[]{:S(2)}) %collective-permute-start.25) | collective-permute-done | bytes 8224 | tf_op jit(solution)/shard_map/ppermute | solution.py:21
  96.7 3.7 %plan.1 = (bf16[2048,128]{1,0:T(8,128)(2,1)S(1)}, bf16[35,512,256]{2,1,0:T(8,128)(2,1)S(1)}, f32[8,128]{1,0:T(8,128)}) custom-call(s32[1288]{0:T(1024)S(1)} %concatenate.25.hbm_ref, f32[257,128,128]{2,1,0:T(8,128)S(1)} %get-tuple-element.43.refs_0_, f32[16,128]{1,0:T(8,128)S(1)} %get-tuple-element.49.refs_1_, ...), custom_call_target="tpu_custom_call" | custom-call | tf_op jit(solution)/shard_map/plan/pallas_call | solution.py:602
  100.4 4.0 %rest_of_plan.1 = (bf16[2048,128]{1,0:T(8,128)(2,1)S(1)}, bf16[2048,128]{1,0:T(8,128)(2,1)S(1)}, bf16[2048,128]{1,0:T(8,128)(2,1)S(1)}) custom-call(s32[1288]{0:T(1024)S(1)} %concatenate.25.hbm_ref, bf16[35,512,256]{2,1,0:T(8,128)(2,1)S(1)} %get-tuple-element.52.refs_0_, bf16[2048,1024]{1,0:T(8,128)(2,1)S(1)} %get-tuple-element.50.refs_2_.refs_1_), custom_call_target="tpu_custom_call" | custom-call | flops 3221225472 | bytes 16777216 | tf_op jit(solution)/shard_map/rest_of_plan/pallas_call | solution.py:616
  104.4 2.2 %collective-permute-start.29 = (bf16[2048,128]{1,0:T(8,128)(2,1)S(1)}, bf16[2048,128]{1,0:T(8,128)(2,1)S(1)}, u32[]{:S(2)}, u32[]{:S(2)}) collective-permute-start(bf16[2048,128]{1,0:T(8,128)(2,1)S(1)} %get-tuple-element.55), channel_id=1, source_target_pairs={{0,4},{1,5},{2,6},{3,7},{4,0},{5,1},{6,2},{7,3},{8,12},{9,13},{10,... | collective-permute-start | bytes 1572872 | tf_op jit(solution)/shard_map/ppermute | solution.py:21
  106.6 2.2 %collective-permute-start.30 = (bf16[2048,128]{1,0:T(8,128)(2,1)S(1)}, bf16[2048,128]{1,0:T(8,128)(2,1)S(1)}, u32[]{:S(2)}, u32[]{:S(2)}) collective-permute-start(bf16[2048,128]{1,0:T(8,128)(2,1)S(1)} %get-tuple-element.56), channel_id=1, source_target_pairs={{0,2},{1,3},{2,0},{3,1},{4,6},{5,7},{6,4},{7,5},{8,10},{9,11},{10,... | collective-permute-start | bytes 1572872 | tf_op jit(solution)/shard_map/ppermute | solution.py:21
  108.8 27.0 %collective-permute-done.29 = bf16[2048,128]{1,0:T(8,128)(2,1)S(1)} collective-permute-done((bf16[2048,128]{1,0:T(8,128)(2,1)S(1)}, bf16[2048,128]{1,0:T(8,128)(2,1)S(1)}, u32[]{:S(2)}, u32[]{:S(2)}) %collective-permute-start.29) | collective-permute-done | bytes 524320 | tf_op jit(solution)/shard_map/ppermute | solution.py:21
  135.8 7.9 %collective-permute-done.28 = bf16[2048,128]{1,0:T(8,128)(2,1)S(1)} collective-permute-done((bf16[2048,128]{1,0:T(8,128)(2,1)S(1)}, bf16[2048,128]{1,0:T(8,128)(2,1)S(1)}, u32[]{:S(2)}, u32[]{:S(2)}) %collective-permute-start.28) | collective-permute-done | bytes 524320 | tf_op jit(solution)/shard_map/ppermute | solution.py:21
  143.7 1.1 add_convert_fusion
  (63 shorter events, 6.3 us)
Async XLA Ops:
  0.6 15.4 %collective-permute-start.2 = (bf16[1024,256]{1,0:T(8,128)(2,1)}, bf16[1024,256]{1,0:T(8,128)(2,1)S(1)}, u32[]{:S(2)}, u32[]{:S(2)}) collective-permute-start(bf16[1024,256]{1,0:T(8,128)(2,1)} %refs_1_.1), channel_id=1, source_target_pairs={{0,16},{8,24},{16,0},{24,8},{1,17},{9,25},{17,1},{25,9},{2,18},{10... | collective-permute-start | bytes 1572872 | tf_op jit(solution)/shard_map/ppermute | solution.py:21
  1.2 14.8 %collective-permute-start.1 = (bf16[1024,256]{1,0:T(8,128)(2,1)}, bf16[1024,256]{1,0:T(8,128)(2,1)S(1)}, u32[]{:S(2)}, u32[]{:S(2)}) collective-permute-start(bf16[1024,256]{1,0:T(8,128)(2,1)} %refs_1_.1), channel_id=1, source_target_pairs={{0,8},{8,0},{16,24},{24,16},{1,9},{9,1},{17,25},{25,17},{2,10},{10... | collective-permute-start | bytes 1572872 | tf_op jit(solution)/shard_map/ppermute | solution.py:21
  2.7 7.2 %collective-permute-start.3 = (bf16[1024,256]{1,0:T(8,128)(2,1)}, bf16[1024,256]{1,0:T(8,128)(2,1)S(1)}, u32[]{:S(2)}, u32[]{:S(2)}) collective-permute-start(bf16[1024,256]{1,0:T(8,128)(2,1)} %refs_1_.1), channel_id=1, source_target_pairs={{0,1},{1,0},{2,3},{3,2},{4,5},{5,4},{6,7},{7,6},{8,9},{9,8},{10,11... | collective-permute-start | bytes 1572872 | tf_op jit(solution)/shard_map/ppermute | solution.py:21
  2.7 2.1 %collective-permute-start = (s32[16,8]{0,1:T(8,128)}, s32[16,8]{0,1:T(8,128)S(1)}, u32[]{:S(2)}, u32[]{:S(2)}) collective-permute-start(s32[16,8]{0,1:T(8,128)} %param.5), channel_id=1, source_target_pairs={{0,1},{1,0},{2,3},{3,2},{4,5},{5,4},{6,7},{7,6},{8,9},{9,8},{10,11... | collective-permute-start | bytes 1544 | tf_op jit(solution)/shard_map/ppermute | solution.py:21
  9.9 2.2 %copy-start = (bf16[2048,1024]{1,0:T(8,128)(2,1)S(1)}, bf16[2048,1024]{1,0:T(8,128)(2,1)}, u32[]{:S(2)}) copy-start(bf16[2048,1024]{1,0:T(8,128)(2,1)} %refs_0_.5) | copy-start | bytes 12582916
  12.1 1.0 copy-start.2
  13.1 5.6 %copy-start.1 = (bf16[2048,1024]{1,0:T(8,128)(2,1)S(1)}, bf16[2048,1024]{1,0:T(8,128)(2,1)}, u32[]{:S(2)}) copy-start(bf16[2048,1024]{1,0:T(8,128)(2,1)} %refs_0_.5) | copy-start | bytes 12582916
  16.0 2.7 %collective-permute-start.7 = (bf16[1024,256]{1,0:T(8,128)(2,1)S(1)}, bf16[1024,256]{1,0:T(8,128)(2,1)S(1)}, u32[]{:S(2)}, u32[]{:S(2)}) collective-permute-start(bf16[1024,256]{1,0:T(8,128)(2,1)S(1)} %collective-permute-done.2.refs_2_), channel_id=1, source_target_pairs={{0,1},{1,0},{2,3},{3,2},{4,5},{5,4},{6,7},{7,6},{8,9},{9,8},{10,11... | collective-permute-start | bytes 1572872 | tf_op jit(solution)/shard_map/ppermute | solution.py:21
  16.2 2.5 %collective-permute-start.6 = (bf16[1024,256]{1,0:T(8,128)(2,1)S(1)}, bf16[1024,256]{1,0:T(8,128)(2,1)S(1)}, u32[]{:S(2)}, u32[]{:S(2)}) collective-permute-start(bf16[1024,256]{1,0:T(8,128)(2,1)S(1)} %collective-permute-done.1.refs_1_), channel_id=1, source_target_pairs={{0,1},{1,0},{2,3},{3,2},{4,5},{5,4},{6,7},{7,6},{8,9},{9,8},{10,11... | collective-permute-start | bytes 1572872 | tf_op jit(solution)/shard_map/ppermute | solution.py:21
  16.6 8.4 %collective-permute-start.5 = (bf16[512,256]{1,0:T(8,128)(2,1)S(1)}, bf16[512,256]{1,0:T(8,128)(2,1)S(1)}, u32[]{:S(2)}, u32[]{:S(2)}) collective-permute-start(bf16[512,256]{1,0:T(8,128)(2,1)S(1)} %slice.7), channel_id=1, source_target_pairs={{0,16},{8,24},{16,0},{24,8},{1,17},{9,25},{17,1},{25,9},{2,18},{10... | collective-permute-start | bytes 786440 | tf_op jit(solution)/shard_map/ppermute | solution.py:21
  17.7 8.1 %collective-permute-start.4 = (bf16[512,256]{1,0:T(8,128)(2,1)S(1)}, bf16[512,256]{1,0:T(8,128)(2,1)S(1)}, u32[]{:S(2)}, u32[]{:S(2)}) collective-permute-start(bf16[512,256]{1,0:T(8,128)(2,1)S(1)} %slice.6), channel_id=1, source_target_pairs={{0,8},{8,0},{16,24},{24,16},{1,9},{9,1},{17,25},{25,17},{2,10},{10... | collective-permute-start | bytes 786440 | tf_op jit(solution)/shard_map/ppermute | solution.py:21
  25.7 1.5 %collective-permute-start.8 = (bf16[512,256]{1,0:T(8,128)(2,1)S(1)}, bf16[512,256]{1,0:T(8,128)(2,1)S(1)}, u32[]{:S(2)}, u32[]{:S(2)}) collective-permute-start(bf16[512,256]{1,0:T(8,128)(2,1)S(1)} %collective-permute-done.4.refs_1_), channel_id=1, source_target_pairs={{0,1},{1,0},{2,3},{3,2},{4,5},{5,4},{6,7},{7,6},{8,9},{9,8},{10,11... | collective-permute-start | bytes 786440 | tf_op jit(solution)/shard_map/ppermute | solution.py:21
  25.7 1.9 %collective-permute-start.9 = (bf16[512,256]{1,0:T(8,128)(2,1)S(1)}, bf16[512,256]{1,0:T(8,128)(2,1)S(1)}, u32[]{:S(2)}, u32[]{:S(2)}) collective-permute-start(bf16[512,256]{1,0:T(8,128)(2,1)S(1)} %collective-permute-done.5.refs_2_), channel_id=1, source_target_pairs={{0,1},{1,0},{2,3},{3,2},{4,5},{5,4},{6,7},{7,6},{8,9},{9,8},{10,11... | collective-permute-start | bytes 786440 | tf_op jit(solution)/shard_map/ppermute | solution.py:21
  32.8 4.7 %collective-permute-start.12 = (f32[16,128]{1,0:T(8,128)S(1)}, f32[16,128]{1,0:T(8,128)S(1)}, u32[]{:S(2)}, u32[]{:S(2)}) collective-permute-start(f32[16,128]{1,0:T(8,128)S(1)} %get-tuple-element.46.refs_3_), channel_id=1, source_target_pairs={{0,6},{1,7},{2,4},{3,5},{4,2},{5,3},{6,0},{7,1},{8,14},{9,15},{10,... | collective-permute-start | bytes 24584 | tf_op jit(solution)/shard_map/ppermute | solution.py:21
  35.4 4.5 %collective-permute-start.11 = (f32[16,128]{1,0:T(8,128)S(1)}, f32[16,128]{1,0:T(8,128)S(1)}, u32[]{:S(2)}, u32[]{:S(2)}) collective-permute-start(f32[16,128]{1,0:T(8,128)S(1)} %get-tuple-element.46.refs_3_), channel_id=1, source_target_pairs={{0,4},{1,5},{2,6},{3,7},{4,0},{5,1},{6,2},{7,3},{8,12},{9,13},{10,... | collective-permute-start | bytes 24584 | tf_op jit(solution)/shard_map/ppermute | solution.py:21
  36.7 3.7 %collective-permute-start.10 = (f32[16,128]{1,0:T(8,128)S(1)}, f32[16,128]{1,0:T(8,128)S(1)}, u32[]{:S(2)}, u32[]{:S(2)}) collective-permute-start(f32[16,128]{1,0:T(8,128)S(1)} %get-tuple-element.46.refs_3_), channel_id=1, source_target_pairs={{0,2},{1,3},{2,0},{3,1},{4,6},{5,7},{6,4},{7,5},{8,10},{9,11},{10,... | collective-permute-start | bytes 24584 | tf_op jit(solution)/shard_map/ppermute | solution.py:21
  42.6 4.6 %collective-permute-start.15 = (f32[16,128]{1,0:T(8,128)S(1)}, f32[16,128]{1,0:T(8,128)S(1)}, u32[]{:S(2)}, u32[]{:S(2)}) collective-permute-start(f32[16,128]{1,0:T(8,128)S(1)} %get-tuple-element.47.refs_3_), channel_id=1, source_target_pairs={{0,24},{8,16},{16,8},{24,0},{1,25},{9,17},{17,9},{25,1},{2,26},{10... | collective-permute-start | bytes 24584 | tf_op jit(solution)/shard_map/ppermute | solution.py:21
  42.7 4.5 %collective-permute-start.14 = (f32[16,128]{1,0:T(8,128)S(1)}, f32[16,128]{1,0:T(8,128)S(1)}, u32[]{:S(2)}, u32[]{:S(2)}) collective-permute-start(f32[16,128]{1,0:T(8,128)S(1)} %get-tuple-element.47.refs_3_), channel_id=1, source_target_pairs={{0,16},{8,24},{16,0},{24,8},{1,17},{9,25},{17,1},{25,9},{2,18},{10... | collective-permute-start | bytes 24584 | tf_op jit(solution)/shard_map/ppermute | solution.py:21
  45.3 3.7 %collective-permute-start.13 = (f32[16,128]{1,0:T(8,128)S(1)}, f32[16,128]{1,0:T(8,128)S(1)}, u32[]{:S(2)}, u32[]{:S(2)}) collective-permute-start(f32[16,128]{1,0:T(8,128)S(1)} %get-tuple-element.47.refs_3_), channel_id=1, source_target_pairs={{0,8},{8,0},{16,24},{24,16},{1,9},{9,1},{17,25},{25,17},{2,10},{10... | collective-permute-start | bytes 24584 | tf_op jit(solution)/shard_map/ppermute | solution.py:21
  50.9 11.3 %collective-permute-start.18 = (f32[16,128]{1,0:T(8,128)S(1)}, f32[16,128]{1,0:T(8,128)S(1)}, u32[]{:S(2)}, u32[]{:S(2)}) collective-permute-start(f32[16,128]{1,0:T(8,128)S(1)} %row_pass.2.refs_3_), channel_id=1, source_target_pairs={{0,6},{1,7},{2,4},{3,5},{4,2},{5,3},{6,0},{7,1},{8,14},{9,15},{10,... | collective-permute-start | bytes 24584 | tf_op jit(solution)/shard_map/ppermute | solution.py:21
  60.6 4.5 %collective-permute-start.17 = (f32[16,128]{1,0:T(8,128)S(1)}, f32[16,128]{1,0:T(8,128)S(1)}, u32[]{:S(2)}, u32[]{:S(2)}) collective-permute-start(f32[16,128]{1,0:T(8,128)S(1)} %row_pass.2.refs_3_), channel_id=1, source_target_pairs={{0,4},{1,5},{2,6},{3,7},{4,0},{5,1},{6,2},{7,3},{8,12},{9,13},{10,... | collective-permute-start | bytes 24584 | tf_op jit(solution)/shard_map/ppermute | solution.py:21
  60.6 4.5 %collective-permute-start.16 = (f32[16,128]{1,0:T(8,128)S(1)}, f32[16,128]{1,0:T(8,128)S(1)}, u32[]{:S(2)}, u32[]{:S(2)}) collective-permute-start(f32[16,128]{1,0:T(8,128)S(1)} %row_pass.2.refs_3_), channel_id=1, source_target_pairs={{0,2},{1,3},{2,0},{3,1},{4,6},{5,7},{6,4},{7,5},{8,10},{9,11},{10,... | collective-permute-start | bytes 24584 | tf_op jit(solution)/shard_map/ppermute | solution.py:21
  67.4 4.6 %collective-permute-start.21 = (f32[16,128]{1,0:T(8,128)S(1)}, f32[16,128]{1,0:T(8,128)S(1)}, u32[]{:S(2)}, u32[]{:S(2)}) collective-permute-start(f32[16,128]{1,0:T(8,128)S(1)} %get-tuple-element.48.refs_3_), channel_id=1, source_target_pairs={{0,24},{8,16},{16,8},{24,0},{1,25},{9,17},{17,9},{25,1},{2,26},{10... | collective-permute-start | bytes 24584 | tf_op jit(solution)/shard_map/ppermute | solution.py:21
  67.5 4.5 %collective-permute-start.20 = (f32[16,128]{1,0:T(8,128)S(1)}, f32[16,128]{1,0:T(8,128)S(1)}, u32[]{:S(2)}, u32[]{:S(2)}) collective-permute-start(f32[16,128]{1,0:T(8,128)S(1)} %get-tuple-element.48.refs_3_), channel_id=1, source_target_pairs={{0,16},{8,24},{16,0},{24,8},{1,17},{9,25},{17,1},{25,9},{2,18},{10... | collective-permute-start | bytes 24584 | tf_op jit(solution)/shard_map/ppermute | solution.py:21
  69.9 3.7 %collective-permute-start.19 = (f32[16,128]{1,0:T(8,128)S(1)}, f32[16,128]{1,0:T(8,128)S(1)}, u32[]{:S(2)}, u32[]{:S(2)}) collective-permute-start(f32[16,128]{1,0:T(8,128)S(1)} %get-tuple-element.48.refs_3_), channel_id=1, source_target_pairs={{0,8},{8,0},{16,24},{24,16},{1,9},{9,1},{17,25},{25,17},{2,10},{10... | collective-permute-start | bytes 24584 | tf_op jit(solution)/shard_map/ppermute | solution.py:21
  75.4 9.1 %collective-permute-start.24 = (f32[16,128]{1,0:T(8,128)S(1)}, f32[16,128]{1,0:T(8,128)S(1)}, u32[]{:S(2)}, u32[]{:S(2)}) collective-permute-start(f32[16,128]{1,0:T(8,128)S(1)} %row_pass.3.refs_3_), channel_id=1, source_target_pairs={{0,6},{1,7},{2,4},{3,5},{4,2},{5,3},{6,0},{7,1},{8,14},{9,15},{10,... | collective-permute-start | bytes 24584 | tf_op jit(solution)/shard_map/ppermute | solution.py:21
  82.8 4.5 %collective-permute-start.23 = (f32[16,128]{1,0:T(8,128)S(1)}, f32[16,128]{1,0:T(8,128)S(1)}, u32[]{:S(2)}, u32[]{:S(2)}) collective-permute-start(f32[16,128]{1,0:T(8,128)S(1)} %row_pass.3.refs_3_), channel_id=1, source_target_pairs={{0,4},{1,5},{2,6},{3,7},{4,0},{5,1},{6,2},{7,3},{8,12},{9,13},{10,... | collective-permute-start | bytes 24584 | tf_op jit(solution)/shard_map/ppermute | solution.py:21
  82.8 4.5 %collective-permute-start.22 = (f32[16,128]{1,0:T(8,128)S(1)}, f32[16,128]{1,0:T(8,128)S(1)}, u32[]{:S(2)}, u32[]{:S(2)}) collective-permute-start(f32[16,128]{1,0:T(8,128)S(1)} %row_pass.3.refs_3_), channel_id=1, source_target_pairs={{0,2},{1,3},{2,0},{3,1},{4,6},{5,7},{6,4},{7,5},{8,10},{9,11},{10,... | collective-permute-start | bytes 24584 | tf_op jit(solution)/shard_map/ppermute | solution.py:21
  89.9 4.6 %collective-permute-start.27 = (f32[16,128]{1,0:T(8,128)S(1)}, f32[16,128]{1,0:T(8,128)S(1)}, u32[]{:S(2)}, u32[]{:S(2)}) collective-permute-start(f32[16,128]{1,0:T(8,128)S(1)} %get-tuple-element.51.refs_3_), channel_id=1, source_target_pairs={{0,24},{8,16},{16,8},{24,0},{1,25},{9,17},{17,9},{25,1},{2,26},{10... | collective-permute-start | bytes 24584 | tf_op jit(solution)/shard_map/ppermute | solution.py:21
  89.9 4.7 %collective-permute-start.26 = (f32[16,128]{1,0:T(8,128)S(1)}, f32[16,128]{1,0:T(8,128)S(1)}, u32[]{:S(2)}, u32[]{:S(2)}) collective-permute-start(f32[16,128]{1,0:T(8,128)S(1)} %get-tuple-element.51.refs_3_), channel_id=1, source_target_pairs={{0,16},{8,24},{16,0},{24,8},{1,17},{9,25},{17,1},{25,9},{2,18},{10... | collective-permute-start | bytes 24584 | tf_op jit(solution)/shard_map/ppermute | solution.py:21
  93.0 3.7 %collective-permute-start.25 = (f32[16,128]{1,0:T(8,128)S(1)}, f32[16,128]{1,0:T(8,128)S(1)}, u32[]{:S(2)}, u32[]{:S(2)}) collective-permute-start(f32[16,128]{1,0:T(8,128)S(1)} %get-tuple-element.51.refs_3_), channel_id=1, source_target_pairs={{0,8},{8,0},{16,24},{24,16},{1,9},{9,1},{17,25},{25,17},{2,10},{10... | collective-permute-start | bytes 24584 | tf_op jit(solution)/shard_map/ppermute | solution.py:21
  104.4 31.4 %collective-permute-start.29 = (bf16[2048,128]{1,0:T(8,128)(2,1)S(1)}, bf16[2048,128]{1,0:T(8,128)(2,1)S(1)}, u32[]{:S(2)}, u32[]{:S(2)}) collective-permute-start(bf16[2048,128]{1,0:T(8,128)(2,1)S(1)} %get-tuple-element.55), channel_id=1, source_target_pairs={{0,4},{1,5},{2,6},{3,7},{4,0},{5,1},{6,2},{7,3},{8,12},{9,13},{10,... | collective-permute-start | bytes 1572872 | tf_op jit(solution)/shard_map/ppermute | solution.py:21
  106.6 29.2 %collective-permute-start.30 = (bf16[2048,128]{1,0:T(8,128)(2,1)S(1)}, bf16[2048,128]{1,0:T(8,128)(2,1)S(1)}, u32[]{:S(2)}, u32[]{:S(2)}) collective-permute-start(bf16[2048,128]{1,0:T(8,128)(2,1)S(1)} %get-tuple-element.56), channel_id=1, source_target_pairs={{0,2},{1,3},{2,0},{3,1},{4,6},{5,7},{6,4},{7,5},{8,10},{9,11},{10,... | collective-permute-start | bytes 1572872 | tf_op jit(solution)/shard_map/ppermute | solution.py:21
  108.8 34.9 %collective-permute-start.28 = (bf16[2048,128]{1,0:T(8,128)(2,1)S(1)}, bf16[2048,128]{1,0:T(8,128)(2,1)S(1)}, u32[]{:S(2)}, u32[]{:S(2)}) collective-permute-start(bf16[2048,128]{1,0:T(8,128)(2,1)S(1)} %get-tuple-element.54), channel_id=1, source_target_pairs={{0,6},{1,7},{2,4},{3,5},{4,2},{5,3},{6,0},{7,1},{8,14},{9,15},{10,... | collective-permute-start | bytes 1572872 | tf_op jit(solution)/shard_map/ppermute | solution.py:21

commit v19 on v14

--- a/solution.py
+++ b/solution.py
@@ -33,7 +33,7 @@
 
 
 class Table:
-    together = 4
+    together = 6
 
     def __init__(self, row_tiles, columns):
         self.row_tiles, self.columns = row_tiles, columns

time: 135 us -> 135 us (level); the launches traced: 136 us -> 134 us
  Pallas kernels: 30.3 us -> 41.9 us
  starting transfers between devices: 43.3 us -> 35.5 us
  waiting for transfers between devices: 51.2 us -> 45.9 us
    pallas_call x2, Pallas kernels: 3.63 us -> 12.5 us  [shards(): pl.pallas_call(with_table(row_kernel, table, log_column), out_shape=row_s...]
    ppermute x31, starting transfers between devices: 43.3 us -> 35.5 us  [swap(): return lax.ppermute(x, axis, [(i, i ^ offset) for i in range(size)])]
    ppermute x31, waiting for transfers between devices: 51.2 us -> 45.9 us  [swap(): return lax.ppermute(x, axis, [(i, i ^ offset) for i in range(size)])]
    pallas_call x3, Pallas kernels: 6.81 us -> 8.87 us  [shards(): pl.pallas_call(with_table(column_kernel, table), out_shape=(column_shape,...]
  transfers between devices with their start and end apart: 31 -> 31, of which waited for: 21 -> 22; matrix products, arithmetic and copies ran while one was open for 3% -> 3% of each run, Pallas kernels for 8% -> 9%
where the time goes in v19:
time: 135 us; the launch traced here: 134 us
  waiting for transfers between devices  45.9 us (34%)
  Pallas kernels  41.9 us (31%)
  starting transfers between devices  35.5 us (26%)
  local copies, waits for them, and re-layouts  4.41 us (3%)
  other arithmetic  4.4 us (3%)
  between operations  2.22 us (2%)
    ppermute x31, waiting for transfers between devices, swap(): return lax.ppermute(x, axis, [(i, i ^ offset) for i in range(size)])  45.9 us
    ppermute x31, starting transfers between devices, swap(): return lax.ppermute(x, axis, [(i, i ^ offset) for i in range(size)])  35.5 us
    pallas_call x2, Pallas kernels, shards(): pl.pallas_call(with_table(row_kernel, table, log_column), out_shape=row_s...  12.5 us
    pallas_call x3, Pallas kernels, shards(): pl.pallas_call(with_table(column_kernel, table), out_shape=(column_shape,...  8.87 us
    pallas_call x2, Pallas kernels, early(): pl.pallas_call(with_table(early_panel_kernel, table, places, owners, bool...  7.33 us
    pallas_call x1, Pallas kernels, late(): pl.pallas_call(with_table(panel_kernel, table, places, add), out_shape=(p...  5.34 us
    pallas_call x1, Pallas kernels, shards(): pl.pallas_call(with_table(rest_kernel, table, lines), out_shape=[block] *...  4.12 us
    pallas_call x1, Pallas kernels, shards(): pl.pallas_call(with_table(plan_kernel, table, log_column, lines), out_sha...  3.79 us
  transfers between devices with their start and end apart: 31, of which 22 were waited for; matrix products, arithmetic and copies ran while one was open for 3% of the time, Pallas kernels for 9%

profile of v19, /device:TPU:0, one launch (start us, length us, event | category | flops | bytes accessed | tf_op | source)
XLA Modules:
  0.0 134.3 jit_solution(14011239217784319990)
XLA Ops:
  0.6 3.0 %collective-permute-start.2 = (bf16[1024,256]{1,0:T(8,128)(2,1)}, bf16[1024,256]{1,0:T(8,128)(2,1)S(1)}, u32[]{:S(2)}, u32[]{:S(2)}) collective-permute-start(bf16[1024,256]{1,0:T(8,128)(2,1)} %refs_1_.1), channel_id=1, source_target_pairs={{0,16},{8,24},{16,0},{24,8},{1,17},{9,25},{17,1},{25,9},{2,18},{10... | collective-permute-start | bytes 1572872 | tf_op jit(solution)/shard_map/ppermute | solution.py:21
  3.7 1.5 %collective-permute-start.1 = (bf16[1024,256]{1,0:T(8,128)(2,1)}, bf16[1024,256]{1,0:T(8,128)(2,1)S(1)}, u32[]{:S(2)}, u32[]{:S(2)}) collective-permute-start(bf16[1024,256]{1,0:T(8,128)(2,1)} %refs_1_.1), channel_id=1, source_target_pairs={{0,8},{8,0},{16,24},{24,16},{1,9},{9,1},{17,25},{25,17},{2,10},{10... | collective-permute-start | bytes 1572872 | tf_op jit(solution)/shard_map/ppermute | solution.py:21
  5.7 0.7 compare_select_fusion.1
  6.4 0.9 collective-permute-done
  7.6 0.6 fusion.4
  10.3 0.6 select_reduce_fusion.1
  11.6 0.7 concatenate.25.hbm_ref
  12.4 2.2 %copy-done = bf16[2048,1024]{1,0:T(8,128)(2,1)S(1)} copy-done((bf16[2048,1024]{1,0:T(8,128)(2,1)S(1)}, bf16[2048,1024]{1,0:T(8,128)(2,1)}, u32[]{:S(2)}) %copy-start) | copy-done | bytes 4194328
  14.6 1.0 copy-done.2
  15.6 2.9 %early_panel.2 = (f32[257,128,128]{2,1,0:T(8,128)S(1)}, bf16[2048,1024]{1,0:T(8,128)(2,1)S(1)}) custom-call(s32[1292]{0:T(1024)S(1)} %concatenate.25.hbm_ref, bf16[2048,1024]{1,0:T(8,128)(2,1)S(1)} %copy-done, bf16[1024,256]{1,0:T(8,128)(2,1)S(1)} %copy-done.2, bf16[1024,256]{1,0:T(8,128)(2,1)S(1)} %collective-permute-done.3.refs_2_), custom_call_target="tpu_custom_call" | custom-call | flops 1073741824 | bytes 33554432 | tf_op jit(solution)/shard_map/early_panel/pallas_call | solution.py:501
  19.7 0.9 collective-permute-start.4
  20.6 0.7 collective-permute-done.6.refs_3_
  21.2 4.5 %early_panel.3 = (f32[257,128,128]{2,1,0:T(8,128)S(1)}, bf16[2048,1024]{1,0:T(8,128)(2,1)S(1)}) custom-call(s32[1292]{0:T(1024)S(1)} %concatenate.25.hbm_ref, bf16[2048,1024]{1,0:T(8,128)(2,1)S(1)} %copy-done.1, bf16[1024,256]{1,0:T(8,128)(2,1)S(1)} %collective-permute-done.1.refs_1_, ...), custom_call_target="tpu_custom_call", output_to_operand_aliasing={{0}: (6, {}), {1}: (7, {})} | custom-call | flops 2147483648 | bytes 33554432 | tf_op jit(solution)/shard_map/early_panel/pallas_call | solution.py:501
  25.7 1.8 %collective-permute-done.5.refs_2_ = bf16[512,256]{1,0:T(8,128)(2,1)S(1)} collective-permute-done((bf16[512,256]{1,0:T(8,128)(2,1)S(1)}, bf16[512,256]{1,0:T(8,128)(2,1)S(1)}, u32[]{:S(2)}, u32[]{:S(2)}) %collective-permute-start.5) | collective-permute-done | bytes 262176 | tf_op jit(solution)/shard_map/ppermute | solution.py:21
  28.3 1.0 collective-permute-done.8.refs_3_
  29.7 5.3 %panel.1 = (f32[257,128,128]{2,1,0:T(8,128)S(1)}, bf16[2048,1024]{1,0:T(8,128)(2,1)S(1)}, bf16[257,128,128]{2,1,0:T(8,128)(2,1)S(1)}, f32[16,128]{1,0:T(8,128)S(1)}, f32[16,128]{1,0:T(8,128)S(1)}) custom-call(s32[1292]{0:T(1024)S(1)} %concatenate.25.hbm_ref, bf16[2048,1024]{1,0:T(8,128)(2,1)S(1)} %copy-done.1, ...), custom_call_target="tpu_custom_call", output_to_operand_aliasing={{0}: (6, {}), {1}: (7, {})} | custom-call | tf_op jit(solution)/shard_map/panel/pallas_call | solution.py:480
  35.0 2.6 %collective-permute-start.12 = (f32[16,128]{1,0:T(8,128)S(1)}, f32[16,128]{1,0:T(8,128)S(1)}, u32[]{:S(2)}, u32[]{:S(2)}) collective-permute-start(f32[16,128]{1,0:T(8,128)S(1)} %get-tuple-element.46.refs_3_), channel_id=1, source_target_pairs={{0,6},{1,7},{2,4},{3,5},{4,2},{5,3},{6,0},{7,1},{8,14},{9,15},{10,... | collective-permute-start | bytes 24584 | tf_op jit(solution)/shard_map/ppermute | solution.py:21
  38.1 1.4 %collective-permute-start.10 = (f32[16,128]{1,0:T(8,128)S(1)}, f32[16,128]{1,0:T(8,128)S(1)}, u32[]{:S(2)}, u32[]{:S(2)}) collective-permute-start(f32[16,128]{1,0:T(8,128)S(1)} %get-tuple-element.46.refs_3_), channel_id=1, source_target_pairs={{0,2},{1,3},{2,0},{3,1},{4,6},{5,7},{6,4},{7,5},{8,10},{9,11},{10,... | collective-permute-start | bytes 24584 | tf_op jit(solution)/shard_map/ppermute | solution.py:21
  39.5 1.1 collective-permute-done.12.refs_6_
  40.5 1.6 %collective-permute-done.11.refs_5_ = f32[16,128]{1,0:T(8,128)S(1)} collective-permute-done((f32[16,128]{1,0:T(8,128)S(1)}, f32[16,128]{1,0:T(8,128)S(1)}, u32[]{:S(2)}, u32[]{:S(2)}) %collective-permute-start.11) | collective-permute-done | bytes 8224 | tf_op jit(solution)/shard_map/ppermute | solution.py:21
  42.2 3.0 %column_pass.3 = (f32[16,128]{1,0:T(8,128)S(1)}, f32[16,128]{1,0:T(8,128)}, f32[16,128]{1,0:T(8,128)}) custom-call(s32[1292]{0:T(1024)S(1)} %concatenate.25.hbm_ref, f32[257,128,128]{2,1,0:T(8,128)S(1)} %get-tuple-element.43.refs_0_, bf16[257,128,128]{2,1,0:T(8,128)(2,1)S(1)} %get-tuple-element.44.refs_1_, f32[16,128]{1,0:T(8,128)S(1)} %get-tuple-element.45.refs_2_, ...), custom_call_target="tpu_custom_call" | custom-call | tf_op jit(solution)/shard_map/column_pass/pallas_call | solution.py:590
  45.2 3.2 %collective-permute-start.15 = (f32[16,128]{1,0:T(8,128)S(1)}, f32[16,128]{1,0:T(8,128)S(1)}, u32[]{:S(2)}, u32[]{:S(2)}) collective-permute-start(f32[16,128]{1,0:T(8,128)S(1)} %get-tuple-element.47.refs_3_), channel_id=1, source_target_pairs={{0,24},{8,16},{16,8},{24,0},{1,25},{9,17},{17,9},{25,1},{2,26},{10... | collective-permute-start | bytes 24584 | tf_op jit(solution)/shard_map/ppermute | solution.py:21
  49.1 1.0 collective-permute-done.15.refs_6_
  50.1 2.0 %collective-permute-done.14.refs_5_ = f32[16,128]{1,0:T(8,128)S(1)} collective-permute-done((f32[16,128]{1,0:T(8,128)S(1)}, f32[16,128]{1,0:T(8,128)S(1)}, u32[]{:S(2)}, u32[]{:S(2)}) %collective-permute-start.14) | collective-permute-done | bytes 8224 | tf_op jit(solution)/shard_map/ppermute | solution.py:21
  52.1 6.2 %row_pass.2.refs_3_ = f32[16,128]{1,0:T(8,128)S(1)} custom-call(s32[1292]{0:T(1024)S(1)} %concatenate.25.hbm_ref, f32[257,128,128]{2,1,0:T(8,128)S(1)} %get-tuple-element.43.refs_0_, bf16[257,128,128]{2,1,0:T(8,128)(2,1)S(1)} %get-tuple-element.44.refs_1_, f32[16,128]{1,0:T(8,128)S(1)} %get-tuple-element.45.refs_2_, ...), custom_call_target="tpu_custom_call" | custom-call | tf_op jit(solution)/shard_map/row_pass/pallas_call | solution.py:580
  58.5 4.3 %collective-permute-start.16 = (f32[16,128]{1,0:T(8,128)S(1)}, f32[16,128]{1,0:T(8,128)S(1)}, u32[]{:S(2)}, u32[]{:S(2)}) collective-permute-start(f32[16,128]{1,0:T(8,128)S(1)} %row_pass.2.refs_3_), channel_id=1, source_target_pairs={{0,2},{1,3},{2,0},{3,1},{4,6},{5,7},{6,4},{7,5},{8,10},{9,11},{10,... | collective-permute-start | bytes 24584 | tf_op jit(solution)/shard_map/ppermute | solution.py:21
  62.8 1.1 collective-permute-done.18.refs_6_
  64.5 2.8 %column_pass.4 = (f32[16,128]{1,0:T(8,128)S(1)}, f32[16,128]{1,0:T(8,128)}, f32[16,128]{1,0:T(8,128)}) custom-call(s32[1292]{0:T(1024)S(1)} %concatenate.25.hbm_ref, f32[257,128,128]{2,1,0:T(8,128)S(1)} %get-tuple-element.43.refs_0_, bf16[257,128,128]{2,1,0:T(8,128)(2,1)S(1)} %get-tuple-element.44.refs_1_, f32[16,128]{1,0:T(8,128)S(1)} %get-tuple-element.45.refs_2_, ...), custom_call_target="tpu_custom_call" | custom-call | tf_op jit(solution)/shard_map/column_pass/pallas_call | solution.py:590
  67.3 3.2 %collective-permute-start.21 = (f32[16,128]{1,0:T(8,128)S(1)}, f32[16,128]{1,0:T(8,128)S(1)}, u32[]{:S(2)}, u32[]{:S(2)}) collective-permute-start(f32[16,128]{1,0:T(8,128)S(1)} %get-tuple-element.48.refs_3_), channel_id=1, source_target_pairs={{0,24},{8,16},{16,8},{24,0},{1,25},{9,17},{17,9},{25,1},{2,26},{10... | collective-permute-start | bytes 24584 | tf_op jit(solution)/shard_map/ppermute | solution.py:21
  70.5 0.7 collective-permute-start.19
  71.2 0.9 collective-permute-done.21.refs_6_
  72.2 2.0 %collective-permute-done.20.refs_5_ = f32[16,128]{1,0:T(8,128)S(1)} collective-permute-done((f32[16,128]{1,0:T(8,128)S(1)}, f32[16,128]{1,0:T(8,128)S(1)}, u32[]{:S(2)}, u32[]{:S(2)}) %collective-permute-start.20) | collective-permute-done | bytes 8224 | tf_op jit(solution)/shard_map/ppermute | solution.py:21
  74.2 6.2 %row_pass.3.refs_3_ = f32[16,128]{1,0:T(8,128)S(1)} custom-call(s32[1292]{0:T(1024)S(1)} %concatenate.25.hbm_ref, f32[257,128,128]{2,1,0:T(8,128)S(1)} %get-tuple-element.43.refs_0_, bf16[257,128,128]{2,1,0:T(8,128)(2,1)S(1)} %get-tuple-element.44.refs_1_, f32[16,128]{1,0:T(8,128)S(1)} %get-tuple-element.45.refs_2_, ...), custom_call_target="tpu_custom_call" | custom-call | tf_op jit(solution)/shard_map/row_pass/pallas_call | solution.py:580
  80.6 4.3 %collective-permute-start.22 = (f32[16,128]{1,0:T(8,128)S(1)}, f32[16,128]{1,0:T(8,128)S(1)}, u32[]{:S(2)}, u32[]{:S(2)}) collective-permute-start(f32[16,128]{1,0:T(8,128)S(1)} %row_pass.3.refs_3_), channel_id=1, source_target_pairs={{0,2},{1,3},{2,0},{3,1},{4,6},{5,7},{6,4},{7,5},{8,10},{9,11},{10,... | collective-permute-start | bytes 24584 | tf_op jit(solution)/shard_map/ppermute | solution.py:21
  84.9 1.1 collective-permute-done.24.refs_6_
  86.5 3.0 %column_pass.5 = (f32[16,128]{1,0:T(8,128)S(1)}, f32[16,128]{1,0:T(8,128)S(1)}, f32[16,128]{1,0:T(8,128)}) custom-call(s32[1292]{0:T(1024)S(1)} %concatenate.25.hbm_ref, f32[257,128,128]{2,1,0:T(8,128)S(1)} %get-tuple-element.43.refs_0_, bf16[257,128,128]{2,1,0:T(8,128)(2,1)S(1)} %get-tuple-element.44.refs_1_, f32[16,128]{1,0:T(8,128)S(1)} %get-tuple-element.45.refs_2_, ...), custom_call_target="tpu_custom_call" | custom-call | tf_op jit(solution)/shard_map/column_pass/pallas_call | solution.py:590
  89.6 4.0 %collective-permute-start.27 = (f32[16,128]{1,0:T(8,128)S(1)}, f32[16,128]{1,0:T(8,128)S(1)}, u32[]{:S(2)}, u32[]{:S(2)}) collective-permute-start(f32[16,128]{1,0:T(8,128)S(1)} %get-tuple-element.51.refs_3_), channel_id=1, source_target_pairs={{0,24},{8,16},{16,8},{24,0},{1,25},{9,17},{17,9},{25,1},{2,26},{10... | collective-permute-start | bytes 24584 | tf_op jit(solution)/shard_map/ppermute | solution.py:21
  93.5 0.6 collective-permute-start.25
  94.2 1.0 collective-permute-done.27.refs_6_
  95.2 2.0 %collective-permute-done.26.refs_5_ = f32[16,128]{1,0:T(8,128)S(1)} collective-permute-done((f32[16,128]{1,0:T(8,128)S(1)}, f32[16,128]{1,0:T(8,128)S(1)}, u32[]{:S(2)}, u32[]{:S(2)}) %collective-permute-start.26) | collective-permute-done | bytes 8224 | tf_op jit(solution)/shard_map/ppermute | solution.py:21
  97.2 3.8 %plan.1 = (bf16[2048,128]{1,0:T(8,128)(2,1)S(1)}, bf16[37,512,256]{2,1,0:T(8,128)(2,1)S(1)}, f32[8,128]{1,0:T(8,128)}) custom-call(s32[1292]{0:T(1024)S(1)} %concatenate.25.hbm_ref, f32[257,128,128]{2,1,0:T(8,128)S(1)} %get-tuple-element.43.refs_0_, f32[16,128]{1,0:T(8,128)S(1)} %get-tuple-element.49.refs_1_, ...), custom_call_target="tpu_custom_call" | custom-call | tf_op jit(solution)/shard_map/plan/pallas_call | solution.py:606
  101.0 1.4 %collective-permute-start.29 = (bf16[2048,128]{1,0:T(8,128)(2,1)S(1)}, bf16[2048,128]{1,0:T(8,128)(2,1)S(1)}, u32[]{:S(2)}, u32[]{:S(2)}) collective-permute-start(bf16[2048,128]{1,0:T(8,128)(2,1)S(1)} %get-tuple-element.56), channel_id=1, source_target_pairs={{0,2},{1,3},{2,0},{3,1},{4,6},{5,7},{6,4},{7,5},{8,10},{9,11},{10,... | collective-permute-start | bytes 1572872 | tf_op jit(solution)/shard_map/ppermute | solution.py:21
  102.4 4.1 %rest_of_plan.1 = (bf16[2048,128]{1,0:T(8,128)(2,1)S(1)}, bf16[2048,128]{1,0:T(8,128)(2,1)S(1)}, bf16[2048,128]{1,0:T(8,128)(2,1)S(1)}) custom-call(s32[1292]{0:T(1024)S(1)} %concatenate.25.hbm_ref, bf16[37,512,256]{2,1,0:T(8,128)(2,1)S(1)} %get-tuple-element.52.refs_0_, bf16[2048,1024]{1,0:T(8,128)(2,1)S(1)} %get-tuple-element.50.refs_2_.refs_1_), custom_call_target="tpu_custom_call" | custom-call | flops 3221225472 | bytes 16777216 | tf_op jit(solution)/shard_map/rest_of_plan/pallas_call | solution.py:620
  106.5 0.7 collective-permute-start.28
  107.3 10.1 %collective-permute-done.29 = bf16[2048,128]{1,0:T(8,128)(2,1)S(1)} collective-permute-done((bf16[2048,128]{1,0:T(8,128)(2,1)S(1)}, bf16[2048,128]{1,0:T(8,128)(2,1)S(1)}, u32[]{:S(2)}, u32[]{:S(2)}) %collective-permute-start.29) | collective-permute-done | bytes 524320 | tf_op jit(solution)/shard_map/ppermute | solution.py:21
  117.6 5.6 %collective-permute-done.28 = bf16[2048,128]{1,0:T(8,128)(2,1)S(1)} collective-permute-done((bf16[2048,128]{1,0:T(8,128)(2,1)S(1)}, bf16[2048,128]{1,0:T(8,128)(2,1)S(1)}, u32[]{:S(2)}, u32[]{:S(2)}) %collective-permute-start.28) | collective-permute-done | bytes 524320 | tf_op jit(solution)/shard_map/ppermute | solution.py:21
  123.2 10.1 %collective-permute-done.30 = bf16[2048,128]{1,0:T(8,128)(2,1)S(1)} collective-permute-done((bf16[2048,128]{1,0:T(8,128)(2,1)S(1)}, bf16[2048,128]{1,0:T(8,128)(2,1)S(1)}, u32[]{:S(2)}, u32[]{:S(2)}) %collective-permute-start.30) | collective-permute-done | bytes 524320 | tf_op jit(solution)/shard_map/ppermute | solution.py:21
  133.3 1.0 add_convert_fusion
  (64 shorter events, 7.4 us)
Async XLA Ops:
  0.6 17.9 %collective-permute-start.2 = (bf16[1024,256]{1,0:T(8,128)(2,1)}, bf16[1024,256]{1,0:T(8,128)(2,1)S(1)}, u32[]{:S(2)}, u32[]{:S(2)}) collective-permute-start(bf16[1024,256]{1,0:T(8,128)(2,1)} %refs_1_.1), channel_id=1, source_target_pairs={{0,16},{8,24},{16,0},{24,8},{1,17},{9,25},{17,1},{25,9},{2,18},{10... | collective-permute-start | bytes 1572872 | tf_op jit(solution)/shard_map/ppermute | solution.py:21
  3.7 14.8 %collective-permute-start.1 = (bf16[1024,256]{1,0:T(8,128)(2,1)}, bf16[1024,256]{1,0:T(8,128)(2,1)S(1)}, u32[]{:S(2)}, u32[]{:S(2)}) collective-permute-start(bf16[1024,256]{1,0:T(8,128)(2,1)} %refs_1_.1), channel_id=1, source_target_pairs={{0,8},{8,0},{16,24},{24,16},{1,9},{9,1},{17,25},{25,17},{2,10},{10... | collective-permute-start | bytes 1572872 | tf_op jit(solution)/shard_map/ppermute | solution.py:21
  5.2 7.2 %collective-permute-start.3 = (bf16[1024,256]{1,0:T(8,128)(2,1)}, bf16[1024,256]{1,0:T(8,128)(2,1)S(1)}, u32[]{:S(2)}, u32[]{:S(2)}) collective-permute-start(bf16[1024,256]{1,0:T(8,128)(2,1)} %refs_1_.1), channel_id=1, source_target_pairs={{0,1},{1,0},{2,3},{3,2},{4,5},{5,4},{6,7},{7,6},{8,9},{9,8},{10,11... | collective-permute-start | bytes 1572872 | tf_op jit(solution)/shard_map/ppermute | solution.py:21
  5.2 2.1 %collective-permute-start = (s32[16,8]{0,1:T(8,128)}, s32[16,8]{0,1:T(8,128)S(1)}, u32[]{:S(2)}, u32[]{:S(2)}) collective-permute-start(s32[16,8]{0,1:T(8,128)} %param.5), channel_id=1, source_target_pairs={{0,1},{1,0},{2,3},{3,2},{4,5},{5,4},{6,7},{7,6},{8,9},{9,8},{10,11... | collective-permute-start | bytes 1544 | tf_op jit(solution)/shard_map/ppermute | solution.py:21
  12.4 2.2 %copy-start = (bf16[2048,1024]{1,0:T(8,128)(2,1)S(1)}, bf16[2048,1024]{1,0:T(8,128)(2,1)}, u32[]{:S(2)}) copy-start(bf16[2048,1024]{1,0:T(8,128)(2,1)} %refs_0_.5) | copy-start | bytes 12582916
  14.6 1.0 copy-start.2
  15.6 5.6 %copy-start.1 = (bf16[2048,1024]{1,0:T(8,128)(2,1)S(1)}, bf16[2048,1024]{1,0:T(8,128)(2,1)}, u32[]{:S(2)}) copy-start(bf16[2048,1024]{1,0:T(8,128)(2,1)} %refs_0_.5) | copy-start | bytes 12582916
  18.5 2.1 %collective-permute-start.7 = (bf16[1024,256]{1,0:T(8,128)(2,1)S(1)}, bf16[1024,256]{1,0:T(8,128)(2,1)S(1)}, u32[]{:S(2)}, u32[]{:S(2)}) collective-permute-start(bf16[1024,256]{1,0:T(8,128)(2,1)S(1)} %collective-permute-done.2.refs_2_), channel_id=1, source_target_pairs={{0,1},{1,0},{2,3},{3,2},{4,5},{5,4},{6,7},{7,6},{8,9},{9,8},{10,11... | collective-permute-start | bytes 1572872 | tf_op jit(solution)/shard_map/ppermute | solution.py:21
  18.7 2.5 %collective-permute-start.6 = (bf16[1024,256]{1,0:T(8,128)(2,1)S(1)}, bf16[1024,256]{1,0:T(8,128)(2,1)S(1)}, u32[]{:S(2)}, u32[]{:S(2)}) collective-permute-start(bf16[1024,256]{1,0:T(8,128)(2,1)S(1)} %collective-permute-done.1.refs_1_), channel_id=1, source_target_pairs={{0,1},{1,0},{2,3},{3,2},{4,5},{5,4},{6,7},{7,6},{8,9},{9,8},{10,11... | collective-permute-start | bytes 1572872 | tf_op jit(solution)/shard_map/ppermute | solution.py:21
  19.1 8.4 %collective-permute-start.5 = (bf16[512,256]{1,0:T(8,128)(2,1)S(1)}, bf16[512,256]{1,0:T(8,128)(2,1)S(1)}, u32[]{:S(2)}, u32[]{:S(2)}) collective-permute-start(bf16[512,256]{1,0:T(8,128)(2,1)S(1)} %slice.7), channel_id=1, source_target_pairs={{0,16},{8,24},{16,0},{24,8},{1,17},{9,25},{17,1},{25,9},{2,18},{10... | collective-permute-start | bytes 786440 | tf_op jit(solution)/shard_map/ppermute | solution.py:21
  19.7 8.1 %collective-permute-start.4 = (bf16[512,256]{1,0:T(8,128)(2,1)S(1)}, bf16[512,256]{1,0:T(8,128)(2,1)S(1)}, u32[]{:S(2)}, u32[]{:S(2)}) collective-permute-start(bf16[512,256]{1,0:T(8,128)(2,1)S(1)} %slice.6), channel_id=1, source_target_pairs={{0,8},{8,0},{16,24},{24,16},{1,9},{9,1},{17,25},{25,17},{2,10},{10... | collective-permute-start | bytes 786440 | tf_op jit(solution)/shard_map/ppermute | solution.py:21
  27.8 1.5 %collective-permute-start.8 = (bf16[512,256]{1,0:T(8,128)(2,1)S(1)}, bf16[512,256]{1,0:T(8,128)(2,1)S(1)}, u32[]{:S(2)}, u32[]{:S(2)}) collective-permute-start(bf16[512,256]{1,0:T(8,128)(2,1)S(1)} %collective-permute-done.4.refs_1_), channel_id=1, source_target_pairs={{0,1},{1,0},{2,3},{3,2},{4,5},{5,4},{6,7},{7,6},{8,9},{9,8},{10,11... | collective-permute-start | bytes 786440 | tf_op jit(solution)/shard_map/ppermute | solution.py:21
  27.8 1.9 %collective-permute-start.9 = (bf16[512,256]{1,0:T(8,128)(2,1)S(1)}, bf16[512,256]{1,0:T(8,128)(2,1)S(1)}, u32[]{:S(2)}, u32[]{:S(2)}) collective-permute-start(bf16[512,256]{1,0:T(8,128)(2,1)S(1)} %collective-permute-done.5.refs_2_), channel_id=1, source_target_pairs={{0,1},{1,0},{2,3},{3,2},{4,5},{5,4},{6,7},{7,6},{8,9},{9,8},{10,11... | collective-permute-start | bytes 786440 | tf_op jit(solution)/shard_map/ppermute | solution.py:21
  35.0 5.5 %collective-permute-start.12 = (f32[16,128]{1,0:T(8,128)S(1)}, f32[16,128]{1,0:T(8,128)S(1)}, u32[]{:S(2)}, u32[]{:S(2)}) collective-permute-start(f32[16,128]{1,0:T(8,128)S(1)} %get-tuple-element.46.refs_3_), channel_id=1, source_target_pairs={{0,6},{1,7},{2,4},{3,5},{4,2},{5,3},{6,0},{7,1},{8,14},{9,15},{10,... | collective-permute-start | bytes 24584 | tf_op jit(solution)/shard_map/ppermute | solution.py:21
  37.6 4.5 %collective-permute-start.11 = (f32[16,128]{1,0:T(8,128)S(1)}, f32[16,128]{1,0:T(8,128)S(1)}, u32[]{:S(2)}, u32[]{:S(2)}) collective-permute-start(f32[16,128]{1,0:T(8,128)S(1)} %get-tuple-element.46.refs_3_), channel_id=1, source_target_pairs={{0,4},{1,5},{2,6},{3,7},{4,0},{5,1},{6,2},{7,3},{8,12},{9,13},{10,... | collective-permute-start | bytes 24584 | tf_op jit(solution)/shard_map/ppermute | solution.py:21
  38.1 4.1 %collective-permute-start.10 = (f32[16,128]{1,0:T(8,128)S(1)}, f32[16,128]{1,0:T(8,128)S(1)}, u32[]{:S(2)}, u32[]{:S(2)}) collective-permute-start(f32[16,128]{1,0:T(8,128)S(1)} %get-tuple-element.46.refs_3_), channel_id=1, source_target_pairs={{0,2},{1,3},{2,0},{3,1},{4,6},{5,7},{6,4},{7,5},{8,10},{9,11},{10,... | collective-permute-start | bytes 24584 | tf_op jit(solution)/shard_map/ppermute | solution.py:21
  45.2 4.8 %collective-permute-start.15 = (f32[16,128]{1,0:T(8,128)S(1)}, f32[16,128]{1,0:T(8,128)S(1)}, u32[]{:S(2)}, u32[]{:S(2)}) collective-permute-start(f32[16,128]{1,0:T(8,128)S(1)} %get-tuple-element.47.refs_3_), channel_id=1, source_target_pairs={{0,24},{8,16},{16,8},{24,0},{1,25},{9,17},{17,9},{25,1},{2,26},{10... | collective-permute-start | bytes 24584 | tf_op jit(solution)/shard_map/ppermute | solution.py:21
  48.4 3.7 %collective-permute-start.14 = (f32[16,128]{1,0:T(8,128)S(1)}, f32[16,128]{1,0:T(8,128)S(1)}, u32[]{:S(2)}, u32[]{:S(2)}) collective-permute-start(f32[16,128]{1,0:T(8,128)S(1)} %get-tuple-element.47.refs_3_), channel_id=1, source_target_pairs={{0,16},{8,24},{16,0},{24,8},{1,17},{9,25},{17,1},{25,9},{2,18},{10... | collective-permute-start | bytes 24584 | tf_op jit(solution)/shard_map/ppermute | solution.py:21
  48.5 3.7 %collective-permute-start.13 = (f32[16,128]{1,0:T(8,128)S(1)}, f32[16,128]{1,0:T(8,128)S(1)}, u32[]{:S(2)}, u32[]{:S(2)}) collective-permute-start(f32[16,128]{1,0:T(8,128)S(1)} %get-tuple-element.47.refs_3_), channel_id=1, source_target_pairs={{0,8},{8,0},{16,24},{24,16},{1,9},{9,1},{17,25},{25,17},{2,10},{10... | collective-permute-start | bytes 24584 | tf_op jit(solution)/shard_map/ppermute | solution.py:21
  58.4 5.5 %collective-permute-start.18 = (f32[16,128]{1,0:T(8,128)S(1)}, f32[16,128]{1,0:T(8,128)S(1)}, u32[]{:S(2)}, u32[]{:S(2)}) collective-permute-start(f32[16,128]{1,0:T(8,128)S(1)} %row_pass.2.refs_3_), channel_id=1, source_target_pairs={{0,6},{1,7},{2,4},{3,5},{4,2},{5,3},{6,0},{7,1},{8,14},{9,15},{10,... | collective-permute-start | bytes 24584 | tf_op jit(solution)/shard_map/ppermute | solution.py:21
  58.5 5.4 %collective-permute-start.17 = (f32[16,128]{1,0:T(8,128)S(1)}, f32[16,128]{1,0:T(8,128)S(1)}, u32[]{:S(2)}, u32[]{:S(2)}) collective-permute-start(f32[16,128]{1,0:T(8,128)S(1)} %row_pass.2.refs_3_), channel_id=1, source_target_pairs={{0,4},{1,5},{2,6},{3,7},{4,0},{5,1},{6,2},{7,3},{8,12},{9,13},{10,... | collective-permute-start | bytes 24584 | tf_op jit(solution)/shard_map/ppermute | solution.py:21
  58.5 5.9 %collective-permute-start.16 = (f32[16,128]{1,0:T(8,128)S(1)}, f32[16,128]{1,0:T(8,128)S(1)}, u32[]{:S(2)}, u32[]{:S(2)}) collective-permute-start(f32[16,128]{1,0:T(8,128)S(1)} %row_pass.2.refs_3_), channel_id=1, source_target_pairs={{0,2},{1,3},{2,0},{3,1},{4,6},{5,7},{6,4},{7,5},{8,10},{9,11},{10,... | collective-permute-start | bytes 24584 | tf_op jit(solution)/shard_map/ppermute | solution.py:21
  67.3 4.9 %collective-permute-start.21 = (f32[16,128]{1,0:T(8,128)S(1)}, f32[16,128]{1,0:T(8,128)S(1)}, u32[]{:S(2)}, u32[]{:S(2)}) collective-permute-start(f32[16,128]{1,0:T(8,128)S(1)} %get-tuple-element.48.refs_3_), channel_id=1, source_target_pairs={{0,24},{8,16},{16,8},{24,0},{1,25},{9,17},{17,9},{25,1},{2,26},{10... | collective-permute-start | bytes 24584 | tf_op jit(solution)/shard_map/ppermute | solution.py:21
  70.5 3.7 %collective-permute-start.20 = (f32[16,128]{1,0:T(8,128)S(1)}, f32[16,128]{1,0:T(8,128)S(1)}, u32[]{:S(2)}, u32[]{:S(2)}) collective-permute-start(f32[16,128]{1,0:T(8,128)S(1)} %get-tuple-element.48.refs_3_), channel_id=1, source_target_pairs={{0,16},{8,24},{16,0},{24,8},{1,17},{9,25},{17,1},{25,9},{2,18},{10... | collective-permute-start | bytes 24584 | tf_op jit(solution)/shard_map/ppermute | solution.py:21
  70.5 3.7 %collective-permute-start.19 = (f32[16,128]{1,0:T(8,128)S(1)}, f32[16,128]{1,0:T(8,128)S(1)}, u32[]{:S(2)}, u32[]{:S(2)}) collective-permute-start(f32[16,128]{1,0:T(8,128)S(1)} %get-tuple-element.48.refs_3_), channel_id=1, source_target_pairs={{0,8},{8,0},{16,24},{24,16},{1,9},{9,1},{17,25},{25,17},{2,10},{10... | collective-permute-start | bytes 24584 | tf_op jit(solution)/shard_map/ppermute | solution.py:21
  80.4 5.5 %collective-permute-start.24 = (f32[16,128]{1,0:T(8,128)S(1)}, f32[16,128]{1,0:T(8,128)S(1)}, u32[]{:S(2)}, u32[]{:S(2)}) collective-permute-start(f32[16,128]{1,0:T(8,128)S(1)} %row_pass.3.refs_3_), channel_id=1, source_target_pairs={{0,6},{1,7},{2,4},{3,5},{4,2},{5,3},{6,0},{7,1},{8,14},{9,15},{10,... | collective-permute-start | bytes 24584 | tf_op jit(solution)/shard_map/ppermute | solution.py:21
  80.5 5.4 %collective-permute-start.23 = (f32[16,128]{1,0:T(8,128)S(1)}, f32[16,128]{1,0:T(8,128)S(1)}, u32[]{:S(2)}, u32[]{:S(2)}) collective-permute-start(f32[16,128]{1,0:T(8,128)S(1)} %row_pass.3.refs_3_), channel_id=1, source_target_pairs={{0,4},{1,5},{2,6},{3,7},{4,0},{5,1},{6,2},{7,3},{8,12},{9,13},{10,... | collective-permute-start | bytes 24584 | tf_op jit(solution)/shard_map/ppermute | solution.py:21
  80.6 5.9 %collective-permute-start.22 = (f32[16,128]{1,0:T(8,128)S(1)}, f32[16,128]{1,0:T(8,128)S(1)}, u32[]{:S(2)}, u32[]{:S(2)}) collective-permute-start(f32[16,128]{1,0:T(8,128)S(1)} %row_pass.3.refs_3_), channel_id=1, source_target_pairs={{0,2},{1,3},{2,0},{3,1},{4,6},{5,7},{6,4},{7,5},{8,10},{9,11},{10,... | collective-permute-start | bytes 24584 | tf_op jit(solution)/shard_map/ppermute | solution.py:21
  89.6 5.6 %collective-permute-start.27 = (f32[16,128]{1,0:T(8,128)S(1)}, f32[16,128]{1,0:T(8,128)S(1)}, u32[]{:S(2)}, u32[]{:S(2)}) collective-permute-start(f32[16,128]{1,0:T(8,128)S(1)} %get-tuple-element.51.refs_3_), channel_id=1, source_target_pairs={{0,24},{8,16},{16,8},{24,0},{1,25},{9,17},{17,9},{25,1},{2,26},{10... | collective-permute-start | bytes 24584 | tf_op jit(solution)/shard_map/ppermute | solution.py:21
  93.5 3.7 %collective-permute-start.26 = (f32[16,128]{1,0:T(8,128)S(1)}, f32[16,128]{1,0:T(8,128)S(1)}, u32[]{:S(2)}, u32[]{:S(2)}) collective-permute-start(f32[16,128]{1,0:T(8,128)S(1)} %get-tuple-element.51.refs_3_), channel_id=1, source_target_pairs={{0,16},{8,24},{16,0},{24,8},{1,17},{9,25},{17,1},{25,9},{2,18},{10... | collective-permute-start | bytes 24584 | tf_op jit(solution)/shard_map/ppermute | solution.py:21
  93.5 3.7 %collective-permute-start.25 = (f32[16,128]{1,0:T(8,128)S(1)}, f32[16,128]{1,0:T(8,128)S(1)}, u32[]{:S(2)}, u32[]{:S(2)}) collective-permute-start(f32[16,128]{1,0:T(8,128)S(1)} %get-tuple-element.51.refs_3_), channel_id=1, source_target_pairs={{0,8},{8,0},{16,24},{24,16},{1,9},{9,1},{17,25},{25,17},{2,10},{10... | collective-permute-start | bytes 24584 | tf_op jit(solution)/shard_map/ppermute | solution.py:21
  101.0 16.4 %collective-permute-start.29 = (bf16[2048,128]{1,0:T(8,128)(2,1)S(1)}, bf16[2048,128]{1,0:T(8,128)(2,1)S(1)}, u32[]{:S(2)}, u32[]{:S(2)}) collective-permute-start(bf16[2048,128]{1,0:T(8,128)(2,1)S(1)} %get-tuple-element.56), channel_id=1, source_target_pairs={{0,2},{1,3},{2,0},{3,1},{4,6},{5,7},{6,4},{7,5},{8,10},{9,11},{10,... | collective-permute-start | bytes 1572872 | tf_op jit(solution)/shard_map/ppermute | solution.py:21
  106.5 16.7 %collective-permute-start.28 = (bf16[2048,128]{1,0:T(8,128)(2,1)S(1)}, bf16[2048,128]{1,0:T(8,128)(2,1)S(1)}, u32[]{:S(2)}, u32[]{:S(2)}) collective-permute-start(bf16[2048,128]{1,0:T(8,128)(2,1)S(1)} %get-tuple-element.54), channel_id=1, source_target_pairs={{0,2},{1,3},{2,0},{3,1},{4,6},{5,7},{6,4},{7,5},{8,10},{9,11},{10,... | collective-permute-start | bytes 1572872 | tf_op jit(solution)/shard_map/ppermute | solution.py:21
  117.5 15.8 %collective-permute-start.30 = (bf16[2048,128]{1,0:T(8,128)(2,1)S(1)}, bf16[2048,128]{1,0:T(8,128)(2,1)S(1)}, u32[]{:S(2)}, u32[]{:S(2)}) collective-permute-start(bf16[2048,128]{1,0:T(8,128)(2,1)S(1)} %add_convert_fusion.1), channel_id=1, source_target_pairs={{0,4},{1,5},{2,6},{3,7},{4,0},{5,1},{6,2},{7,3},{8,12},{9,13},{10,... | collective-permute-start | bytes 1572872 | tf_op jit(solution)/shard_map/ppermute | solution.py:21
